TPU v7x, 128 devices: a whole 4x4x4 slice. The times are simulated.
128 devices in a mesh: gx: 2 (over core), gy: 2 (over z_lo), gzs: 32 (over y, z_hi, x).
Axes of the slice: x: 4, y: 4, z: 4 (z_hi: 2, z_lo: 2; z = z_hi * 2 + z_lo), core: 2. Of those that a mesh axis runs over, the one named last changes fastest.
Arguments:
- states: float32 [32, 32, 512, 128], P('gx', 'gy', 'gzs'), may hold values from -6 to 6
- potential: float32 [32, 32, 512], P('gx', 'gy', 'gzs'), may hold values from -6 to 2
- atom_sites: int32 [512, 3], P(('gx', 'gy', 'gzs')), may hold values from 0 to 511, as said below
- projectors: float32 [512, 9, 9, 9], P(('gx', 'gy', 'gzs')), may hold values from -0.21875 to 0.21875
- energies: float32 [512], P(('gx', 'gy', 'gzs')), may hold values from 2 to 16
Outputs:
- orbitals: float32 [32, 32, 512, 128], P('gx', 'gy', 'gzs')
Inputs may be any that keep to these rules, and one draw needn't show every extreme that they name: `atom_sites`: each atom's cell lies in the block of cells held by the device that holds the atom's row: along the first dimension within [16 i, 16 (i + 1)) for that device's index i along gx, and likewise with 16 and gy, 16 and gzs.
All inputs are finite; a program needn't handle non-finite values.
Results may differ from a plain program's by a relative error of at most 0.00005.
Values sent between devices are 32-bit elements; how exact they have to be, the bound alone decides.
No kernel may reach another device: no remote copies, remote signals or barrier semaphores. Data moves between devices by JAX's collectives and lax.ppermute only.
A program may use at most 128 MiB of HBM per device.

v0:
```python
import math

import jax
import jax.numpy as jnp
from jax import lax
from jax.sharding import PartitionSpec as P

H = 6


grid_step = 0.6
filter_centre = 36.0
filter_half = 26.0
HIGH = lax.Precision.HIGHEST


def extended_2(cells, sides, width):
    for axis, dim in sides:
        count = lax.axis_size(axis)
        head = lax.slice_in_dim(cells, 0, width, axis=dim)
        tail = lax.slice_in_dim(cells, cells.shape[dim] - width, cells.shape[dim], axis=dim)
        cells = jnp.concatenate(
            [
                lax.ppermute(tail, axis, [(i, (i + 1) % count) for i in range(count)]),
                cells,
                lax.ppermute(head, axis, [((i + 1) % count, i) for i in range(count)]),
            ],
            axis=dim,
        )
    return cells


def second_weights():
    weights = []
    for k in range(1, 7):
        top = 2.0 * (-1) ** (k + 1) * math.factorial(6) ** 2
        under = k * k * math.factorial(6 - k) * math.factorial(6 + k)
        weights.append(top / under)
    return (-2.0 * sum(weights), weights)


def kinetic(field, extended):
    centre, weights = second_weights()
    total = 3.0 * centre * field
    for axis in range(3):
        length = field.shape[axis]
        source = extended[axis]
        for k in range(1, 7):
            upper = lax.slice_in_dim(source, H + k, H + k + length, axis=axis)
            below = lax.slice_in_dim(source, H - k, H - k + length, axis=axis)
            total = total + weights[k - 1] * (upper + below)
    return -0.5 / (grid_step * grid_step) * total


def projector_grid(sites, shapes, anchor, extent):
    width = shapes.shape[1]
    reach = width // 2
    taps = jnp.arange(width, dtype=jnp.int32)
    tables = []
    for axis in range(3):
        cells = anchor + jnp.arange(extent[axis], dtype=jnp.int32)
        starts = sites[:, axis][:, None, None] - reach + taps[None, None, :]
        tables.append((cells[None, :, None] == starts).astype(jnp.float32))
    return jnp.einsum(
        "kxi,kyj,kzl,kijl->kxyz", tables[0], tables[1], tables[2], shapes, precision=HIGH
    )


def per_device(states, potential, atom_sites, projectors, energies):
    size_x, size_y, size_z, nstates = states.shape
    count = projectors.shape[0]
    width = projectors.shape[1]
    cells = size_x * size_y * size_z
    extent = (size_x, size_y, size_z)
    neigh = 27 * count
    block_sizes = jnp.array(extent, dtype=jnp.int32)
    local_sites = atom_sites % block_sizes[None, :]
    bundle = (
        extended_2(projectors[None, None, None], (("gx", 0), ("gy", 1), ("gzs", 2)), 1),
        extended_2(energies[None, None, None], (("gx", 0), ("gy", 1), ("gzs", 2)), 1),
        extended_2(
            local_sites.astype(jnp.float32)[None, None, None], (("gx", 0), ("gy", 1), ("gzs", 2)), 1
        ),
    )
    near_shapes = bundle[0].reshape(neigh, width, width, width)
    near_energy = bundle[1].reshape(neigh)
    steps_one = jnp.arange(3, dtype=jnp.int32) - 1
    step_x = jnp.broadcast_to(steps_one[:, None, None], (3, 3, 3))
    step_y = jnp.broadcast_to(steps_one[None, :, None], (3, 3, 3))
    step_z = jnp.broadcast_to(steps_one[None, None, :], (3, 3, 3))
    offsets = jnp.stack([step_x, step_y, step_z], axis=3)
    near_sites = bundle[2].astype(jnp.int32) + offsets[:, :, :, None, :] * block_sizes
    near_sites = near_sites.reshape(neigh, 3)
    near_grid = projector_grid(near_sites, near_shapes, 0, extent).reshape(neigh, cells)
    wide = (size_x + 2 * H, size_y + 2 * H, size_z + 2 * H)
    own_grid = projector_grid(local_sites, projectors, -H, wide).reshape(
        count, wide[0] * wide[1] * wide[2]
    )

    def hamiltonian(field):
        cube = extended_2(field, (("gx", 0), ("gy", 1), ("gzs", 2)), H)
        extended = (
            cube[:, H : H + size_y, H : H + size_z],
            cube[H : H + size_x, :, H : H + size_z],
            cube[H : H + size_x, H : H + size_y, :],
        )
        own_coef = jnp.dot(own_grid, cube.reshape(-1, nstates), precision=HIGH)
        near_coef = extended_2(
            own_coef[None, None, None], (("gx", 0), ("gy", 1), ("gzs", 2)), 1
        ).reshape(neigh, nstates)
        weighted = near_energy[:, None] * near_coef
        nonlocal_part = jnp.einsum("kc,ks->cs", near_grid, weighted, precision=HIGH).reshape(
            size_x, size_y, size_z, nstates
        )
        return kinetic(field, extended) + potential[..., None] * field + nonlocal_part

    first = (hamiltonian(states) - filter_centre * states) / filter_half
    second = 2.0 * (hamiltonian(first) - filter_centre * first) / filter_half - states
    flat_second = second.reshape(cells, nstates)
    total_cells = cells * lax.axis_size("gx") * lax.axis_size("gy") * lax.axis_size("gzs")
    gram = (
        lax.psum(jnp.dot(flat_second.T, flat_second, precision=HIGH), ("gx", "gy", "gzs"))
        / total_cells
    )
    lower = jnp.linalg.cholesky(gram)
    inverse = lax.linalg.triangular_solve(
        lower, jnp.eye(nstates, dtype=jnp.float32), left_side=True, lower=True
    )
    orbitals = jnp.dot(flat_second, inverse.T, precision=HIGH)
    return orbitals.reshape(size_x, size_y, size_z, nstates)


def solution(mesh):
    return jax.shard_map(
        per_device,
        mesh=mesh,
        in_specs=(
            P("gx", "gy", "gzs", None),
            P("gx", "gy", "gzs"),
            P(("gx", "gy", "gzs"), None),
            P(("gx", "gy", "gzs"), None, None, None),
            P(("gx", "gy", "gzs")),
        ),
        out_specs=P("gx", "gy", "gzs", None),
        check_vma=False,
    )
```

profile of v0, /device:TPU:0, one launch (start us, length us, event | category | flops | bytes accessed | tf_op | source)
XLA Modules:
  0.0 802.6 jit_solution(4174439043914833304)
XLA Ops:
  25.9 52.7 %collective-permute-done.20 = f32[3,1,1,4]{3,2,1,0:T(1,128)S(1)} collective-permute-done((f32[3,1,1,4]{3,2,1,0:T(1,128)S(1)}, f32[3,1,1,4]{3,2,1,0:T(1,128)S(1)}, u32[]{:S(2)}, u32[]{:S(2)}) %collective-permute-start.20) | collective-permute-done | bytes 80 | tf_op jit(solution)/shard_map/ppermute | solution.py:24
  84.0 8.2 %collective-permute-start.23 = (f32[3,3,1,4]{3,2,1,0:T(1,128)S(1)}, f32[3,3,1,4]{3,2,1,0:T(1,128)S(1)}, u32[]{:S(2)}, u32[]{:S(2)}) collective-permute-start(f32[3,3,1,4]{3,2,1,0:T(1,128)S(1)} %pad_maximum_fusion.22), channel_id=1, source_target_pairs={{1,0},{2,1},{3,2},{4,3},{5,4},{6,5},{7,6},{8,7},{9,8},{10,9},{11,1... | collective-permute-start | bytes 440 | tf_op jit(solution)/shard_map/ppermute | solution.py:26
  93.6 8.0 collective-permute-start.17
  107.9 8.3 %collective-permute-start.4 = (f32[28,28,6,128]{3,1,2,0:T(8,128)S(1)}, f32[28,28,6,128]{3,1,2,0:T(8,128)}, u32[]{:S(2)}, u32[]{:S(2)}) collective-permute-start(f32[28,28,6,128]{3,1,2,0:T(8,128)S(1)} %copy.22), channel_id=1, source_target_pairs={{1,0},{2,1},{3,2},{4,3},{5,4},{6,5},{7,6},{8,7},{9,8},{10,9},{11,1... | collective-permute-start | bytes 7225352 | tf_op jit(solution)/shard_map/ppermute | solution.py:26
  125.3 56.9 %collective-permute-done.8 = f32[3,1,1,4,9,9,9]{6,3,5,4,2,1,0:T(4,128)S(1)} collective-permute-done((f32[3,1,1,4,9,9,9]{6,3,5,4,2,1,0:T(4,128)}, f32[3,1,1,4,9,9,9]{6,3,5,4,2,1,0:T(4,128)S(1)}, u32[]{:S(2)}, u32[]{:S(2)}) %collective-permute-start.8) | collective-permute-done | bytes 35024 | tf_op jit(solution)/shard_map/ppermute | solution.py:24
  182.2 10.7 %collective-permute-done.9 = f32[3,1,1,4,9,9,9]{6,3,5,4,2,1,0:T(4,128)} collective-permute-done((f32[3,1,1,4,9,9,9]{6,3,5,4,2,1,0:T(4,128)}, f32[3,1,1,4,9,9,9]{6,3,5,4,2,1,0:T(4,128)}, u32[]{:S(2)}, u32[]{:S(2)}) %collective-permute-start.9) | collective-permute-done | bytes 35024 | tf_op jit(solution)/shard_map/ppermute | solution.py:26
  194.5 7.7 collective-permute-start.11
  202.4 32.5 %collective-permute-done.10 = f32[3,3,1,4,9,9,9]{6,3,5,4,2,1,0:T(4,128)S(1)} collective-permute-done((f32[3,3,1,4,9,9,9]{6,3,5,4,2,1,0:T(4,128)S(1)}, f32[3,3,1,4,9,9,9]{6,3,5,4,2,1,0:T(4,128)S(1)}, u32[]{:S(2)}, u32[]{:S(2)}) %collective-permute-start.10) | collective-permute-done | bytes 105008 | tf_op jit(solution)/shard_map/ppermute | solution.py:24
  234.9 4.1 pad_maximum_fusion.5
  238.9 10.4 %copy.60 = f32[3,3,3,4,9,9,9]{4,6,5,3,2,1,0:T(8,128)} copy(f32[3,3,3,4,9,9,9]{6,3,5,4,2,1,0:T(4,128)} %pad_maximum_fusion.5) | data formatting | bytes 629856 | tf_op jit(solution)/shard_map/reshape | solution.py:85
  249.3 8.2 %fusion.153 = f32[108,9,9,16]{3,2,1,0:T(8,128)} fusion(f32[108,9,9,9]{1,3,2,0:T(8,128)} %bitcast.99, s32[108,9]{1,0:T(8,128)S(1)} %copy-done.21), kind=kOutput, calls=%fused_computation.232 | convolution fusion | flops 15132096 | bytes 878688 | tf_op jit(solution)/shard_map/kxi,kyj,kzl,kijl->kxyz/dot_general | solution.py:64
  257.5 15.2 %copy.29 = f32[108,9,9,16]{1,2,3,0:T(8,128)} copy(f32[108,9,9,16]{3,2,1,0:T(8,128)} %fusion.153) | data formatting | bytes 1119744 | tf_op jit(solution)/shard_map/kxi,kyj,kzl,kijl->kxyz/dot_general | solution.py:64
  280.9 9.5 %fusion.145 = f32[1,1,1,4,128]{4,3,2,1,0:T(4,128)S(1)} fusion(f32[28,28,6,128]{3,2,1,0:T(8,128)S(1)} %copy.23, f32[28,6,16,128]{3,2,1,0:T(8,128)S(1)} %copy-done.11, f32[28,16,16,128]{3,2,1,0:T(8,128)S(1)} %copy-done.1, f32[28,6,16,128]{3,2,1,0:T(8,128)S(1)} %copy-done.13, f32[28,28,6,128]{3,2,1,0:T(8,128)S(1)} %copy.25, f32[4,28,28,28]{3,2,1,0:T(8,128)S(1)} %copy-done.15), kind=kOutput, calls=%fused_computation.224 | convolution fusion | flops 146112512 | bytes 11592704 | tf_op jit(solution)/shard_map/dot_general | solution.py:107
  291.0 52.7 %fusion.156 = f32[108,9,16,16]{1,3,2,0:T(8,128)S(1)} fusion(f32[108,9,9,16]{1,2,3,0:T(8,128)} %copy.29, s32[108,9]{1,0:T(8,128)S(1)} %iota_add_fusion.1), kind=kOutput, calls=%fused_computation.234 | convolution fusion | flops 26889408 | bytes 1559088 | tf_op jit(solution)/shard_map/kxi,kyj,kzl,kijl->kxyz/dot_general | solution.py:64
  345.9 9.8 %fusion.159 = f32[108,16,16,16]{3,2,1,0:T(8,128)} fusion(f32[108,9,16,16]{1,3,2,0:T(8,128)S(1)} %fusion.156, s32[108,9]{1,0:T(8,128)S(1)} %iota_add_fusion), kind=kOutput, calls=%fused_computation.236 | convolution fusion | flops 47791296 | bytes 2768688 | tf_op jit(solution)/shard_map/kxi,kyj,kzl,kijl->kxyz/dot_general | solution.py:64
  355.7 10.1 %copy.31 = f32[108,16,16,16]{0,3,2,1:T(8,128)} copy(f32[108,16,16,16]{3,2,1,0:T(8,128)} %fusion.159) | data formatting | bytes 3538944 | tf_op jit(solution)/shard_map/kxi,kyj,kzl,kijl->kxyz/dot_general | solution.py:64
  365.9 7.7 collective-permute-start.29
  373.6 13.4 %pad_maximum_fusion = (f32[28,28,22,128]{3,2,1,0:T(8,128)}, f32[28,28,22,128]{3,2,1,0:T(8,128)}) fusion(f32[28,28,6,128]{3,2,1,0:T(8,128)S(1)} %copy.23, f32[28,6,16,128]{3,2,1,0:T(8,128)} %copy-done.10, f32[28,16,16,128]{3,2,1,0:T(8,128)} %copy-done, f32[28,6,16,128]{3,2,1,0:T(8,128)} %copy-done.12, f32[28,28,6,128]{3,2,1,0:T(8,128)} %copy-done.3), kind=kLoop, calls=%fused_computation.34 | loop fusion | flops 13246464 | bytes 28901376 | tf_op jit(solution)/shard_map/concatenate | solution.py:22
  387.1 37.0 %broadcast_multiply_fusion = (f32[16,16,16,128]{3,2,1,0:T(8,128)S(1)}, f32[16,16,16,128]{3,2,1,0:T(8,128)}) fusion(f32[16,16,16,128]{3,2,1,0:T(8,128)} %param.6, f32[108,128,1,1]{1,0,2,3:T(8,128)S(1)} %reshape.329, f32[108,16,16,16]{0,3,2,1:T(8,128)} %copy.31, f32[16,16,16]{2,1,0:T(8,128)S(1)} %copy-done.23, f32[28,28,22,128]{3,2,1,0:T(8,128)} %get-tuple-element.15, ...), kind=kOutput, calls=%fused_computation.225 | convolution fusion | flops 718274560 | bytes 64886784 | tf_op jit(solution)/shard_map/kc,ks->cs/dot_general | solution.py:112
  430.0 31.0 %collective-permute-done.32 = f32[28,6,16,128]{3,2,1,0:T(8,128)S(1)} collective-permute-done((f32[28,6,16,128]{3,2,1,0:T(8,128)S(1)}, f32[28,6,16,128]{3,2,1,0:T(8,128)S(1)}, u32[]{:S(2)}, u32[]{:S(2)}) %collective-permute-start.32) | collective-permute-done | bytes 1376288 | tf_op jit(solution)/shard_map/ppermute | solution.py:26
  461.0 28.7 %collective-permute-done.33 = f32[28,6,16,128]{3,2,1,0:T(8,128)S(1)} collective-permute-done((f32[28,6,16,128]{3,2,1,0:T(8,128)S(1)}, f32[28,6,16,128]{3,2,1,0:T(8,128)S(1)}, u32[]{:S(2)}, u32[]{:S(2)}) %collective-permute-start.33) | collective-permute-done | bytes 1376288 | tf_op jit(solution)/shard_map/ppermute | solution.py:24
  495.5 58.2 %collective-permute-done.34 = f32[28,28,6,128]{3,1,2,0:T(8,128)S(1)} collective-permute-done((f32[28,28,6,128]{3,1,2,0:T(8,128)S(1)}, f32[28,28,6,128]{3,1,2,0:T(8,128)S(1)}, u32[]{:S(2)}, u32[]{:S(2)}) %collective-permute-start.34) | collective-permute-done | bytes 2408480 | tf_op jit(solution)/shard_map/ppermute | solution.py:26
  555.7 5.8 collective-permute-done.35
  563.6 14.3 %fusion.140 = f32[1,1,1,4,128]{4,3,2,1,0:T(4,128)S(1)} fusion(f32[28,28,6,128]{3,2,1,0:T(8,128)S(1)} %copy.39, f32[28,6,16,128]{3,2,1,0:T(8,128)} %copy-done.5, f32[6,16,16,128]{3,2,1,0:T(8,128)S(1)} %collective-permute-done.30, f32[16,16,16,128]{3,2,1,0:T(8,128)S(1)} %get-tuple-element.38, f32[6,16,16,128]{3,2,1,0:T(8,128)S(1)} %collective-permute-done.31, ...), kind=kOutput, calls=%fused_computation.223 | convolution fusion | flops 151732224 | bytes 11592704 | tf_op jit(solution)/shard_map/dot_general | solution.py:107
  581.4 5.5 pad_maximum_fusion.4
  587.0 7.7 collective-permute-start.41
  594.8 9.0 %pad_maximum_fusion.1 = (f32[28,28,22,128]{3,2,1,0:T(8,128)}, f32[28,28,22,128]{3,2,1,0:T(8,128)}) fusion(f32[28,28,6,128]{3,2,1,0:T(8,128)S(1)} %copy.39, f32[28,6,16,128]{3,2,1,0:T(8,128)S(1)} %copy-done.6, f32[6,16,16,128]{3,2,1,0:T(8,128)S(1)} %collective-permute-done.30, f32[16,16,16,128]{3,2,1,0:T(8,128)S(1)} %get-tuple-element.38, ...), kind=kLoop, calls=%fused_computation.36 | loop fusion | flops 22077440 | bytes 28901376 | tf_op jit(solution)/shard_map/concatenate | solution.py:22
  604.0 27.1 %multiply_subtract_fusion = f32[16,16,16,128]{3,2,1,0:T(8,128)} fusion(f32[16,16,16,128]{3,2,1,0:T(8,128)} %param.6, f32[16,16,16,128]{3,2,1,0:T(8,128)} %get-tuple-element.39, f32[28,28,22,128]{3,2,1,0:T(8,128)} %get-tuple-element.11, f32[28,28,22,128]{3,2,1,0:T(8,128)} %get-tuple-element.10, f32[28,22,16,128]{3,2,1,0:T(8,128)} %get-tuple-element.19, ...), kind=kOutput, calls=%fused_computation.213 | convolution fusion | flops 718798848 | bytes 62134272 | tf_op jit(solution)/shard_map/kc,ks->cs/dot_general | solution.py:112
  631.1 6.5 convolution_bitcast_fusion.2
  637.6 129.8 %all-reduce.2.cloned.1.call-done = f32[128,128]{0,1:T(8,128)} async-done(((f32[128,128]{0,1:T(8,128)}), f32[128,128]{0,1:T(8,128)}) %all-reduce.2.cloned.1.call-update) | async-done | bytes 65552 | tf_op jit(solution)/shard_map/psum | solution.py:122
  769.2 11.7 %cholesky.17 = f32[128,128]{1,0:T(8,128)S(1)} custom-call(f32[128,128]{1,0:T(8,128)S(1)} %fusion.169), custom_call_target="Cholesky" | custom-call | tf_op jit(solution)/shard_map/jit(cholesky)/cholesky | solution.py:125
  782.2 9.8 %custom-call.6 = f32[1,128,128]{1,2,0:T(8,128)S(1)} custom-call(f32[1,128,128]{2,1,0:T(8,128)S(1)} %fusion.167), custom_call_target="InvertDiagBlocksLowerTriangular" | custom-call | tf_op jit(solution)/shard_map/triangular_solve | solution.py:126
  (189 shorter events, 79.9 us)
Async XLA Ops:
  6.5 760.8 %all-reduce.2.cloned.1.call-start = ((), (), s32[]{:S(2)}) async-start(), calls=%async_computation | async-start | bytes 131072 | tf_op jit(solution)/shard_map/psum | solution.py:122
  7.3 16.4 %collective-permute-start.12 = (f32[1,1,1,4,3]{4,3,2,1,0:T(4,128)S(1)}, f32[1,1,1,4,3]{4,3,2,1,0:T(4,128)S(1)}, u32[]{:S(2)}, u32[]{:S(2)}) collective-permute-start(f32[1,1,1,4,3]{4,3,2,1,0:T(4,128)S(1)} %get-tuple-element.8), channel_id=1, source_target_pairs={{0,64},{64,0},{1,65},{65,1},{2,66},{66,2},{3,67},{67,3},{4,68},{68... | collective-permute-start | bytes 152 | tf_op jit(solution)/shard_map/ppermute | solution.py:24
  7.3 18.5 %collective-permute-start.13 = (f32[1,1,1,4,3]{4,3,2,1,0:T(4,128)S(1)}, f32[1,1,1,4,3]{4,3,2,1,0:T(4,128)S(1)}, u32[]{:S(2)}, u32[]{:S(2)}) collective-permute-start(f32[1,1,1,4,3]{4,3,2,1,0:T(4,128)S(1)} %get-tuple-element.8), channel_id=1, source_target_pairs={{64,0},{0,64},{65,1},{1,65},{66,2},{2,66},{67,3},{3,67},{68,4},{4,... | collective-permute-start | bytes 152 | tf_op jit(solution)/shard_map/ppermute | solution.py:26
  9.9 12.4 %collective-permute-start.18 = (f32[1,1,1,4]{3,2,1,0:T(1,128)S(1)}, f32[1,1,1,4]{3,2,1,0:T(1,128)S(1)}, u32[]{:S(2)}, u32[]{:S(2)}) collective-permute-start(f32[1,1,1,4]{3,2,1,0:T(1,128)S(1)} %bitcast.105), channel_id=1, source_target_pairs={{0,64},{64,0},{1,65},{65,1},{2,66},{66,2},{3,67},{67,3},{4,68},{68... | collective-permute-start | bytes 56 | tf_op jit(solution)/shard_map/ppermute | solution.py:24
  16.4 86.7 %collective-permute-start.2 = (f32[28,6,16,128]{3,2,1,0:T(8,128)}, f32[28,6,16,128]{3,2,1,0:T(8,128)S(1)}, u32[]{:S(2)}, u32[]{:S(2)}) collective-permute-start(f32[28,6,16,128]{3,2,1,0:T(8,128)} %get-tuple-element.22), channel_id=1, source_target_pairs={{32,0},{0,32},{33,1},{1,33},{34,2},{2,34},{35,3},{3,35},{36,4},{4,... | collective-permute-start | bytes 4128776 | tf_op jit(solution)/shard_map/ppermute | solution.py:26
  18.4 84.7 %collective-permute-start.3 = (f32[28,6,16,128]{3,2,1,0:T(8,128)}, f32[28,6,16,128]{3,2,1,0:T(8,128)S(1)}, u32[]{:S(2)}, u32[]{:S(2)}) collective-permute-start(f32[28,6,16,128]{3,2,1,0:T(8,128)} %get-tuple-element.23), channel_id=1, source_target_pairs={{0,32},{32,0},{1,33},{33,1},{2,34},{34,2},{3,35},{35,3},{4,36},{36... | collective-permute-start | bytes 4128776 | tf_op jit(solution)/shard_map/ppermute | solution.py:24
  23.5 96.2 %collective-permute-start.6 = (f32[1,1,1,4,9,9,9]{6,3,5,4,2,1,0:T(4,128)S(1)}, f32[1,1,1,4,9,9,9]{6,3,5,4,2,1,0:T(4,128)S(1)}, u32[]{:S(2)}, u32[]{:S(2)}) collective-permute-start(f32[1,1,1,4,9,9,9]{6,3,5,4,2,1,0:T(4,128)S(1)} %bitcast.100), channel_id=1, source_target_pairs={{0,64},{64,0},{1,65},{65,1},{2,66},{66,2},{3,67},{67,3},{4,68},{68... | collective-permute-start | bytes 35000 | tf_op jit(solution)/shard_map/ppermute | solution.py:24
  23.7 54.9 %collective-permute-start.20 = (f32[3,1,1,4]{3,2,1,0:T(1,128)S(1)}, f32[3,1,1,4]{3,2,1,0:T(1,128)S(1)}, u32[]{:S(2)}, u32[]{:S(2)}) collective-permute-start(f32[3,1,1,4]{3,2,1,0:T(1,128)S(1)} %pad_maximum_fusion.23), channel_id=1, source_target_pairs={{0,32},{32,0},{1,33},{33,1},{2,34},{34,2},{3,35},{35,3},{4,36},{36... | collective-permute-start | bytes 152 | tf_op jit(solution)/shard_map/ppermute | solution.py:24
  25.8 54.6 %collective-permute-start.21 = (f32[3,1,1,4]{3,2,1,0:T(1,128)S(1)}, f32[3,1,1,4]{3,2,1,0:T(1,128)S(1)}, u32[]{:S(2)}, u32[]{:S(2)}) collective-permute-start(f32[3,1,1,4]{3,2,1,0:T(1,128)S(1)} %pad_maximum_fusion.23), channel_id=1, source_target_pairs={{32,0},{0,32},{33,1},{1,33},{34,2},{2,34},{35,3},{3,35},{36,4},{4,... | collective-permute-start | bytes 152 | tf_op jit(solution)/shard_map/ppermute | solution.py:26
  82.3 10.0 %collective-permute-start.22 = (f32[3,3,1,4]{3,2,1,0:T(1,128)S(1)}, f32[3,3,1,4]{3,2,1,0:T(1,128)S(1)}, u32[]{:S(2)}, u32[]{:S(2)}) collective-permute-start(f32[3,3,1,4]{3,2,1,0:T(1,128)S(1)} %pad_maximum_fusion.22), channel_id=1, source_target_pairs={{0,1},{1,2},{2,3},{3,4},{4,5},{5,6},{6,7},{7,8},{8,9},{9,10},{10,1... | collective-permute-start | bytes 440 | tf_op jit(solution)/shard_map/ppermute | solution.py:24
  84.0 9.6 %collective-permute-start.23 = (f32[3,3,1,4]{3,2,1,0:T(1,128)S(1)}, f32[3,3,1,4]{3,2,1,0:T(1,128)S(1)}, u32[]{:S(2)}, u32[]{:S(2)}) collective-permute-start(f32[3,3,1,4]{3,2,1,0:T(1,128)S(1)} %pad_maximum_fusion.22), channel_id=1, source_target_pairs={{1,0},{2,1},{3,2},{4,3},{5,4},{6,5},{7,6},{8,7},{9,8},{10,9},{11,1... | collective-permute-start | bytes 440 | tf_op jit(solution)/shard_map/ppermute | solution.py:26
  92.3 9.6 %collective-permute-start.16 = (f32[3,3,1,4,3]{4,3,2,1,0:T(4,128)S(1)}, f32[3,3,1,4,3]{4,3,2,1,0:T(4,128)S(1)}, u32[]{:S(2)}, u32[]{:S(2)}) collective-permute-start(f32[3,3,1,4,3]{4,3,2,1,0:T(4,128)S(1)} %pad_maximum_fusion.15), channel_id=1, source_target_pairs={{0,1},{1,2},{2,3},{3,4},{4,5},{5,6},{6,7},{7,8},{8,9},{9,10},{10,1... | collective-permute-start | bytes 1304 | tf_op jit(solution)/shard_map/ppermute | solution.py:24
  93.6 9.5 %collective-permute-start.17 = (f32[3,3,1,4,3]{4,3,2,1,0:T(4,128)S(1)}, f32[3,3,1,4,3]{4,3,2,1,0:T(4,128)S(1)}, u32[]{:S(2)}, u32[]{:S(2)}) collective-permute-start(f32[3,3,1,4,3]{4,3,2,1,0:T(4,128)S(1)} %pad_maximum_fusion.15), channel_id=1, source_target_pairs={{1,0},{2,1},{3,2},{4,3},{5,4},{6,5},{7,6},{8,7},{9,8},{10,9},{11,1... | collective-permute-start | bytes 1304 | tf_op jit(solution)/shard_map/ppermute | solution.py:26
  101.8 17.9 %collective-permute-start.7 = (f32[1,1,1,4,9,9,9]{6,3,5,4,2,1,0:T(4,128)S(1)}, f32[1,1,1,4,9,9,9]{6,3,5,4,2,1,0:T(4,128)S(1)}, u32[]{:S(2)}, u32[]{:S(2)}) collective-permute-start(f32[1,1,1,4,9,9,9]{6,3,5,4,2,1,0:T(4,128)S(1)} %bitcast.101), channel_id=1, source_target_pairs={{64,0},{0,64},{65,1},{1,65},{66,2},{2,66},{67,3},{3,67},{68,4},{4,... | collective-permute-start | bytes 35000 | tf_op jit(solution)/shard_map/ppermute | solution.py:26
  107.9 164.8 %collective-permute-start.4 = (f32[28,28,6,128]{3,1,2,0:T(8,128)S(1)}, f32[28,28,6,128]{3,1,2,0:T(8,128)}, u32[]{:S(2)}, u32[]{:S(2)}) collective-permute-start(f32[28,28,6,128]{3,1,2,0:T(8,128)S(1)} %copy.22), channel_id=1, source_target_pairs={{1,0},{2,1},{3,2},{4,3},{5,4},{6,5},{7,6},{8,7},{9,8},{10,9},{11,1... | collective-permute-start | bytes 7225352 | tf_op jit(solution)/shard_map/ppermute | solution.py:26
  118.2 158.6 %collective-permute-start.5 = (f32[28,28,6,128]{3,1,2,0:T(8,128)}, f32[28,28,6,128]{3,1,2,0:T(8,128)}, u32[]{:S(2)}, u32[]{:S(2)}) collective-permute-start(f32[28,28,6,128]{3,1,2,0:T(8,128)} %copy.24), channel_id=1, source_target_pairs={{0,1},{1,2},{2,3},{3,4},{4,5},{5,6},{6,7},{7,8},{8,9},{9,10},{10,1... | collective-permute-start | bytes 7225352 | tf_op jit(solution)/shard_map/ppermute | solution.py:24
  122.0 60.3 %collective-permute-start.8 = (f32[3,1,1,4,9,9,9]{6,3,5,4,2,1,0:T(4,128)}, f32[3,1,1,4,9,9,9]{6,3,5,4,2,1,0:T(4,128)S(1)}, u32[]{:S(2)}, u32[]{:S(2)}) collective-permute-start(f32[3,1,1,4,9,9,9]{6,3,5,4,2,1,0:T(4,128)} %pad_maximum_fusion.14), channel_id=1, source_target_pairs={{0,32},{32,0},{1,33},{33,1},{2,34},{34,2},{3,35},{35,3},{4,36},{36... | collective-permute-start | bytes 104984 | tf_op jit(solution)/shard_map/ppermute | solution.py:24
  122.0 71.0 %collective-permute-start.9 = (f32[3,1,1,4,9,9,9]{6,3,5,4,2,1,0:T(4,128)}, f32[3,1,1,4,9,9,9]{6,3,5,4,2,1,0:T(4,128)}, u32[]{:S(2)}, u32[]{:S(2)}) collective-permute-start(f32[3,1,1,4,9,9,9]{6,3,5,4,2,1,0:T(4,128)} %pad_maximum_fusion.14), channel_id=1, source_target_pairs={{32,0},{0,32},{33,1},{1,33},{34,2},{2,34},{35,3},{3,35},{36,4},{4,... | collective-permute-start | bytes 104984 | tf_op jit(solution)/shard_map/ppermute | solution.py:26
  194.5 40.4 %collective-permute-start.10 = (f32[3,3,1,4,9,9,9]{6,3,5,4,2,1,0:T(4,128)S(1)}, f32[3,3,1,4,9,9,9]{6,3,5,4,2,1,0:T(4,128)S(1)}, u32[]{:S(2)}, u32[]{:S(2)}) collective-permute-start(f32[3,3,1,4,9,9,9]{6,3,5,4,2,1,0:T(4,128)S(1)} %pad_maximum_fusion.10), channel_id=1, source_target_pairs={{0,1},{1,2},{2,3},{3,4},{4,5},{5,6},{6,7},{7,8},{8,9},{9,10},{10,1... | collective-permute-start | bytes 314936 | tf_op jit(solution)/shard_map/ppermute | solution.py:24
  194.5 40.3 %collective-permute-start.11 = (f32[3,3,1,4,9,9,9]{6,3,5,4,2,1,0:T(4,128)S(1)}, f32[3,3,1,4,9,9,9]{6,3,5,4,2,1,0:T(4,128)S(1)}, u32[]{:S(2)}, u32[]{:S(2)}) collective-permute-start(f32[3,3,1,4,9,9,9]{6,3,5,4,2,1,0:T(4,128)S(1)} %pad_maximum_fusion.10), channel_id=1, source_target_pairs={{1,0},{2,1},{3,2},{4,3},{5,4},{6,5},{7,6},{8,7},{9,8},{10,9},{11,1... | collective-permute-start | bytes 314936 | tf_op jit(solution)/shard_map/ppermute | solution.py:26
  290.4 53.3 %collective-permute-start.24 = (f32[1,1,1,4,128]{4,3,2,1,0:T(4,128)S(1)}, f32[1,1,1,4,128]{4,3,2,1,0:T(4,128)S(1)}, u32[]{:S(2)}, u32[]{:S(2)}) collective-permute-start(f32[1,1,1,4,128]{4,3,2,1,0:T(4,128)S(1)} %fusion.145), channel_id=1, source_target_pairs={{0,64},{64,0},{1,65},{65,1},{2,66},{66,2},{3,67},{67,3},{4,68},{68... | collective-permute-start | bytes 6152 | tf_op jit(solution)/shard_map/ppermute | solution.py:24
  290.5 53.2 %collective-permute-start.25 = (f32[1,1,1,4,128]{4,3,2,1,0:T(4,128)S(1)}, f32[1,1,1,4,128]{4,3,2,1,0:T(4,128)S(1)}, u32[]{:S(2)}, u32[]{:S(2)}) collective-permute-start(f32[1,1,1,4,128]{4,3,2,1,0:T(4,128)S(1)} %fusion.145), channel_id=1, source_target_pairs={{64,0},{0,64},{65,1},{1,65},{66,2},{2,66},{67,3},{3,67},{68,4},{4,... | collective-permute-start | bytes 6152 | tf_op jit(solution)/shard_map/ppermute | solution.py:26
  343.7 22.0 %collective-permute-start.26 = (f32[3,1,1,4,128]{4,3,2,1,0:T(4,128)S(1)}, f32[3,1,1,4,128]{4,3,2,1,0:T(4,128)S(1)}, u32[]{:S(2)}, u32[]{:S(2)}) collective-permute-start(f32[3,1,1,4,128]{4,3,2,1,0:T(4,128)S(1)} %pad_maximum_fusion.20), channel_id=1, source_target_pairs={{0,32},{32,0},{1,33},{33,1},{2,34},{34,2},{3,35},{35,3},{4,36},{36... | collective-permute-start | bytes 18440 | tf_op jit(solution)/shard_map/ppermute | solution.py:24
  344.8 20.9 %collective-permute-start.27 = (f32[3,1,1,4,128]{4,3,2,1,0:T(4,128)S(1)}, f32[3,1,1,4,128]{4,3,2,1,0:T(4,128)S(1)}, u32[]{:S(2)}, u32[]{:S(2)}) collective-permute-start(f32[3,1,1,4,128]{4,3,2,1,0:T(4,128)S(1)} %pad_maximum_fusion.20), channel_id=1, source_target_pairs={{32,0},{0,32},{33,1},{1,33},{34,2},{2,34},{35,3},{3,35},{36,4},{4,... | collective-permute-start | bytes 18440 | tf_op jit(solution)/shard_map/ppermute | solution.py:26
  365.8 21.2 %collective-permute-start.28 = (f32[3,3,1,4,128]{4,3,2,1,0:T(4,128)S(1)}, f32[3,3,1,4,128]{4,3,2,1,0:T(4,128)S(1)}, u32[]{:S(2)}, u32[]{:S(2)}) collective-permute-start(f32[3,3,1,4,128]{4,3,2,1,0:T(4,128)S(1)} %pad_maximum_fusion.17), channel_id=1, source_target_pairs={{0,1},{1,2},{2,3},{3,4},{4,5},{5,6},{6,7},{7,8},{8,9},{9,10},{10,1... | collective-permute-start | bytes 55304 | tf_op jit(solution)/shard_map/ppermute | solution.py:24
  365.9 21.1 %collective-permute-start.29 = (f32[3,3,1,4,128]{4,3,2,1,0:T(4,128)S(1)}, f32[3,3,1,4,128]{4,3,2,1,0:T(4,128)S(1)}, u32[]{:S(2)}, u32[]{:S(2)}) collective-permute-start(f32[3,3,1,4,128]{4,3,2,1,0:T(4,128)S(1)} %pad_maximum_fusion.17), channel_id=1, source_target_pairs={{1,0},{2,1},{3,2},{4,3},{5,4},{6,5},{7,6},{8,7},{9,8},{10,9},{11,1... | collective-permute-start | bytes 55304 | tf_op jit(solution)/shard_map/ppermute | solution.py:26
  427.9 33.1 %collective-permute-start.32 = (f32[28,6,16,128]{3,2,1,0:T(8,128)S(1)}, f32[28,6,16,128]{3,2,1,0:T(8,128)S(1)}, u32[]{:S(2)}, u32[]{:S(2)}) collective-permute-start(f32[28,6,16,128]{3,2,1,0:T(8,128)S(1)} %get-tuple-element.21), channel_id=1, source_target_pairs={{32,0},{0,32},{33,1},{1,33},{34,2},{2,34},{35,3},{3,35},{36,4},{4,... | collective-permute-start | bytes 4128776 | tf_op jit(solution)/shard_map/ppermute | solution.py:26
  429.0 60.7 %collective-permute-start.33 = (f32[28,6,16,128]{3,2,1,0:T(8,128)S(1)}, f32[28,6,16,128]{3,2,1,0:T(8,128)S(1)}, u32[]{:S(2)}, u32[]{:S(2)}) collective-permute-start(f32[28,6,16,128]{3,2,1,0:T(8,128)S(1)} %get-tuple-element.20), channel_id=1, source_target_pairs={{0,32},{32,0},{1,33},{33,1},{2,34},{34,2},{3,35},{35,3},{4,36},{36... | collective-permute-start | bytes 4128776 | tf_op jit(solution)/shard_map/ppermute | solution.py:24
  492.7 61.0 %collective-permute-start.34 = (f32[28,28,6,128]{3,1,2,0:T(8,128)S(1)}, f32[28,28,6,128]{3,1,2,0:T(8,128)S(1)}, u32[]{:S(2)}, u32[]{:S(2)}) collective-permute-start(f32[28,28,6,128]{3,1,2,0:T(8,128)S(1)} %copy.38), channel_id=1, source_target_pairs={{1,0},{2,1},{3,2},{4,3},{5,4},{6,5},{7,6},{8,7},{9,8},{10,9},{11,1... | collective-permute-start | bytes 7225352 | tf_op jit(solution)/shard_map/ppermute | solution.py:26
  494.9 66.6 %collective-permute-start.35 = (f32[28,28,6,128]{3,1,2,0:T(8,128)S(1)}, f32[28,28,6,128]{3,1,2,0:T(8,128)S(1)}, u32[]{:S(2)}, u32[]{:S(2)}) collective-permute-start(f32[28,28,6,128]{3,1,2,0:T(8,128)S(1)} %copy.40), channel_id=1, source_target_pairs={{0,1},{1,2},{2,3},{3,4},{4,5},{5,6},{6,7},{7,8},{8,9},{9,10},{10,1... | collective-permute-start | bytes 7225352 | tf_op jit(solution)/shard_map/ppermute | solution.py:24
  587.0 16.9 %collective-permute-start.40 = (f32[3,3,1,4,128]{4,3,2,1,0:T(4,128)S(1)}, f32[3,3,1,4,128]{4,3,2,1,0:T(4,128)S(1)}, u32[]{:S(2)}, u32[]{:S(2)}) collective-permute-start(f32[3,3,1,4,128]{4,3,2,1,0:T(4,128)S(1)} %pad_maximum_fusion.18), channel_id=1, source_target_pairs={{0,1},{1,2},{2,3},{3,4},{4,5},{5,6},{6,7},{7,8},{8,9},{9,10},{10,1... | collective-permute-start | bytes 55304 | tf_op jit(solution)/shard_map/ppermute | solution.py:24
  587.0 16.8 %collective-permute-start.41 = (f32[3,3,1,4,128]{4,3,2,1,0:T(4,128)S(1)}, f32[3,3,1,4,128]{4,3,2,1,0:T(4,128)S(1)}, u32[]{:S(2)}, u32[]{:S(2)}) collective-permute-start(f32[3,3,1,4,128]{4,3,2,1,0:T(4,128)S(1)} %pad_maximum_fusion.18), channel_id=1, source_target_pairs={{1,0},{2,1},{3,2},{4,3},{5,4},{6,5},{7,6},{8,7},{9,8},{10,9},{11,1... | collective-permute-start | bytes 55304 | tf_op jit(solution)/shard_map/ppermute | solution.py:26
  (37 other events, 899.7 us)
Sparse Core Ops, SparseCore 0:
  637.7 129.6 all-reduce.1
where the time goes:
time: 815 us; the launch traced here: 803 us
  waiting for transfers between devices  417 us (51%)
  matrix products  173 us (21%)
  starting transfers between devices  69.6 us (9%)
  other arithmetic  66.2 us (8%)
  local copies, waits for them, and re-layouts  63.2 us (8%)
  between operations  14.4 us (2%)
    ppermute x21, waiting for transfers between devices, extended_2(): lax.ppermute(tail, axis, [(i, (i + 1) % count) for i in range(count)])  181 us
    psum x1, waiting for transfers between devices, per_device(): lax.psum(jnp.dot(flat_second.T, flat_second, precision=HIGH), ('gx', 'gy'...  130 us
    ppermute x21, waiting for transfers between devices, extended_2(): lax.ppermute(head, axis, [((i + 1) % count, i) for i in range(count)])  106 us
    dot_general x6, matrix products, projector_grid(): jnp.einsum('kxi,kyj,kzl,kijl->kxyz', tables[0], tables[1], tables[2], sha...  74.9 us
    dot_general x2, matrix products, hamiltonian(): jnp.einsum('kc,ks->cs', near_grid, weighted, precision=HIGH)  64.1 us
    ppermute x21, starting transfers between devices, extended_2(): lax.ppermute(head, axis, [((i + 1) % count, i) for i in range(count)])  59.1 us
    concatenate x18, other arithmetic, extended_2(): jnp.concatenate([lax.ppermute(tail, axis, [(i, (i + 1) % count) for i in...  38.7 us
    dot_general x2, local copies, waits for them, and re-layouts, projector_grid(): jnp.einsum('kxi,kyj,kzl,kijl->kxyz', tables[0], tables[1], tables[2], sha...  25.3 us
  transfers between devices with their start and end apart: 43, of which 21 were waited for; matrix products, arithmetic and copies ran while one was open for 21% of the time, Pallas kernels for 0%

commit v1 on v0

v1 whole, which is shorter than its diff:
```python
import math

import jax
import jax.numpy as jnp
from jax import lax
from jax.experimental import pallas as pl
from jax.experimental.pallas import tpu as pltpu
from jax.sharding import PartitionSpec as P

AXES = ("gx", "gy", "gzs")
H = 6
C = 16
ROWS = C * C
CELLS = C * C * C
S = 128
W = 9
R = 4
NEAR = 48
F32 = jnp.float32
BF16 = jnp.bfloat16

grid_step = 0.6
filter_centre = 36.0
filter_half = 26.0


def weights():
    taps = []
    for k in range(1, 7):
        top = 2.0 * (-1) ** (k + 1) * math.factorial(6) ** 2
        under = k * k * math.factorial(6 - k) * math.factorial(6 + k)
        taps.append(top / under)
    scale = -0.5 / (grid_step * grid_step)
    off = [scale * t / filter_half for t in taps]
    diagonal = 3.0 * scale * (-2.0 * sum(taps))
    return off, diagonal


OFF, DIAGONAL = weights()


def params(mib):
    return pltpu.CompilerParams(vmem_limit_bytes=mib * 1024 * 1024)


def cost(flops, nbytes):
    return pl.CostEstimate(flops=flops, bytes_accessed=nbytes, transcendentals=0)


def sds(shape, dtype=F32):
    return jax.ShapeDtypeStruct(shape, dtype)


def split(value):
    high = value.astype(BF16)
    low = (value - high.astype(F32)).astype(BF16)
    return high, low


def mm(a, b):
    return jnp.dot(a, b, preferred_element_type=F32)


def tap_sum(at, index):
    total = None
    for k in range(1, 7):
        term = OFF[k - 1] * (at(index + k) + at(index - k))
        total = term if total is None else total + term
    return total


def pack_kernel(s_ref, edge_ref, mid_ref, head_ref, tail_ref):
    def body(x, _):
        edge_ref[x, 0:96, :] = s_ref[x, 0:96, :]
        edge_ref[x, 96:192, :] = s_ref[x, 160:256, :]
        mid_ref[x] = s_ref[x, 96:160, :]
        for z in range(H):
            head_ref[z, x] = s_ref[x, pl.ds(z, C, stride=C), :]
            tail_ref[z, x] = s_ref[x, pl.ds(C - H + z, C, stride=C), :]
        return 0

    lax.fori_loop(0, C, body, 0)


def pack(s):
    return pl.pallas_call(
        pack_kernel,
        out_shape=[sds((C, 192, S)), sds((C, 64, S)), sds((H, C, C, S)), sds((H, C, C, S))],
        compiler_params=params(32),
        cost_estimate=cost(1000, 6 << 20),
        name="pack",
    )(s)


def fill_z(ext_ref, s_ref, low_ref, high_ref):
    def body(x, _):
        for y in range(C):
            ext_ref[x, y * 32 + 8 : y * 32 + 24, :] = s_ref[x, y * C : (y + 1) * C, :]
        for z in range(H):
            ext_ref[x, pl.ds(2 + z, C, stride=32), :] = low_ref[z, x]
            ext_ref[x, pl.ds(24 + z, C, stride=32), :] = high_ref[z, x]
        return 0

    lax.fori_loop(0, C, body, 0)


def z_taps(ext_ref, x, y):
    return tap_sum(lambda k: ext_ref[x, y * 32 + 8 + k : y * 32 + 24 + k, :], 0)


def x_ring(own_ref, mate_ref, rows):
    def at(x):
        if x < 0:
            return mate_ref[C + x, rows, :]
        if x >= C:
            return mate_ref[x - C, rows, :]
        return own_ref[x, rows, :]

    return [at(x) for x in range(-H, C + H)]


def side_kernel(s_ref, mate_ref, low_ref, high_ref, out_ref, ext_ref):
    fill_z(ext_ref, s_ref, low_ref, high_ref)

    def along_z(x, _):
        for y in range(C):
            out_ref[x, y * C : (y + 1) * C, :] = z_taps(ext_ref, x, y)
        return 0

    lax.fori_loop(0, C, along_z, 0)

    def along_x(block, _):
        rows = pl.ds(pl.multiple_of(block * 8, 8), 8)
        ring = x_ring(s_ref, mate_ref, rows)
        for x in range(C):
            out_ref[x, rows, :] += tap_sum(lambda i: ring[H + i], x)
        return 0

    lax.fori_loop(0, ROWS // 8, along_x, 0)


def side(s, mate, low, high):
    return pl.pallas_call(
        side_kernel,
        out_shape=sds((C, ROWS, S)),
        scratch_shapes=[pltpu.VMEM((C, C * 32, S), F32)],
        compiler_params=params(48),
        cost_estimate=cost(1 << 25, 8 << 20),
        name="side",
    )(s, mate, low, high)


def prep_kernel(table_ref, place_ref, pot_ref, near_ref, near_t_ref, vb_ref, a1_ref, a2_ref, g_ref):
    sub = lax.broadcasted_iota(jnp.int32, (8, 128), 0)
    px = jnp.broadcast_to(place_ref[0:1, :], (8, 128))
    py = jnp.broadcast_to(place_ref[1:2, :], (8, 128))
    pz = jnp.broadcast_to(place_ref[2:3, :], (8, 128))
    zero = jnp.zeros((8, 128), F32)

    for half in range(2):
        dz = sub + half * 8 - pz + R
        masks = [dz == t for t in range(W)]

        def place_z(ij, _, half=half, masks=masks):
            acc = zero
            for t in range(W):
                row = table_ref[t, pl.ds(ij, 1), :]
                acc = jnp.where(masks[t], jnp.broadcast_to(row, (8, 128)), acc)
            a1_ref[ij, half * 8 : half * 8 + 8, :] = acc
            return 0

        lax.fori_loop(0, W * W, place_z, 0)

    def place_y(y, _):
        dy = (y - py + R) & 31
        masks = [dy == t for t in range(W)]
        for i in range(W):
            for half in range(2):
                acc = zero
                for t in range(W):
                    acc = jnp.where(masks[t], a1_ref[i * W + t, half * 8 : half * 8 + 8, :], acc)
                a2_ref[i, y, half * 8 : half * 8 + 8, :] = acc
        return 0

    lax.fori_loop(0, 2 * C, place_y, 0)

    def place_x(x, _):
        dx = (x - px + R) & 31
        masks = [dx == t for t in range(W)]

        def per_y(y, _):
            side_index = y // C
            inner = y - side_index * C
            for half in range(2):
                acc = zero
                for t in range(W):
                    acc = jnp.where(masks[t], a2_ref[t, y, half * 8 : half * 8 + 8, :], acc)
                g_ref[half * 8 : half * 8 + 8, :] = acc
            value = g_ref[...]
            high, low = split(value)
            row = pl.multiple_of(x * ROWS + inner * C, C)
            near_ref[side_index, 0, pl.ds(row, C), :] = high
            near_ref[side_index, 1, pl.ds(row, C), :] = low
            return 0

        lax.fori_loop(0, 2 * C, per_y, 0)
        return 0

    lax.fori_loop(0, C, place_x, 0)

    for block in range(CELLS // 128):
        rows = slice(block * 128, block * 128 + 128)
        for part in range(2):
            turned = near_ref[0, part, rows, :].astype(F32).T
            near_t_ref[part * NEAR : (part + 1) * NEAR, rows] = turned[:NEAR].astype(BF16)

    def spread(row, _):
        for part in range(2):
            line = (pot_ref[part, pl.ds(row, 1), :] + (DIAGONAL - filter_centre)) * (1.0 / filter_half)
            start = pl.multiple_of(row * 128, 128)
            vb_ref[part, pl.ds(start, 128), :] = jnp.broadcast_to(line, (128, 128)).T
        return 0

    lax.fori_loop(0, CELLS // 128, spread, 0)


def prep(table, place, pot):
    return pl.pallas_call(
        prep_kernel,
        out_shape=[sds((2, 2, CELLS, 128), BF16), sds((2 * NEAR, CELLS), BF16), sds((2, CELLS, S))],
        scratch_shapes=[
            pltpu.VMEM((W * W, C, 128), F32),
            pltpu.VMEM((W, 2 * C, C, 128), F32),
            pltpu.VMEM((C, 128), F32),
        ],
        compiler_params=params(48),
        cost_estimate=cost(1 << 25, 10 << 20),
        name="prep",
    )(table, place, pot)


def project(near_t_ref, field_ref):
    total = jnp.zeros((NEAR, S), F32)
    for x in range(C):
        high, low = split(field_ref[x])
        columns = slice(x * ROWS, (x + 1) * ROWS)
        both = mm(near_t_ref[:, columns], high)
        total = total + (both[:NEAR] + both[NEAR:]) + mm(near_t_ref[:NEAR, columns], low)
    return total


def coef_kernel(near_t_ref, s_ref, out_ref):
    out_ref[...] = project(near_t_ref, s_ref)


def coef(near_t, s):
    return pl.pallas_call(
        coef_kernel,
        out_shape=sds((NEAR, S)),
        compiler_params=params(32),
        cost_estimate=cost(1 << 27, 3 << 20),
        name="coef",
    )(near_t, s)


def apply_near(near_ref, side_index, w_ref, x):
    rows = pl.ds(pl.multiple_of(x * ROWS, ROWS), ROWS)
    high, low = split(w_ref[...])
    g_high = near_ref[side_index, 0, rows, :]
    g_low = near_ref[side_index, 1, rows, :]
    return mm(g_high, high) + (mm(g_high, low) + mm(g_low, high))


def first_kernel(
    s_ref, side_ref, edge_ref, vb_ref, near_ref, near_t_ref, w_ref, first_ref, mix_ref, q_ref, head_ref, tail_ref, coef_ref
):
    def body(x, _):
        q_ref[x] = apply_near(near_ref, 0, w_ref, x)
        for half in range(2):

            def rows(y, half=half):
                return slice(y * C + half * 8, y * C + half * 8 + 8)

            ring = {y: s_ref[x, rows(y), :] for y in range(C)}
            for y in range(H):
                ring[C + y] = edge_ref[x, rows(y), :]
                ring[y - H] = edge_ref[x, rows(H + y), :]
            for y in range(C):
                dy = tap_sum(lambda i: ring[i], y)
                vrow = pl.ds(pl.multiple_of(x * ROWS + y * C + half * 8, 8), 8)
                q = dy + vb_ref[0, vrow, :] * ring[y] + q_ref[x, rows(y), :]
                q_ref[x, rows(y), :] = q
                first = side_ref[x, rows(y), :] + q
                first_ref[x, rows(y), :] = first
                mix_ref[x, rows(y), :] = first + dy
        for z in range(H):
            head_ref[z, x] = mix_ref[x, pl.ds(z, C, stride=C), :]
            tail_ref[z, x] = mix_ref[x, pl.ds(C - H + z, C, stride=C), :]
        return 0

    lax.fori_loop(0, C, body, 0)
    coef_ref[...] = project(near_t_ref, first_ref)


def make_first(s, side_part, edge, vb, near, near_t, weighted):
    full = sds((C, ROWS, S))
    halo = sds((H, C, C, S))
    return pl.pallas_call(
        first_kernel,
        out_shape=[full, full, full, halo, halo, sds((NEAR, S))],
        compiler_params=params(56),
        cost_estimate=cost(1 << 27, 20 << 20),
        name="first",
    )(s, side_part, edge, vb, near, near_t, weighted)


def base_kernel(s_ref, edge_ref, mid_ref, vb_ref, near_ref, w_ref, q_ref, first_ref, mix_ref, mate_ref, out_ref, n_ref):
    def body(x, _):
        n_ref[...] = apply_near(near_ref, 1, w_ref, x)
        for half in range(2):

            def rows(y, half=half):
                return slice(y * C + half * 8, y * C + half * 8 + 8)

            def other(y):
                if y < H:
                    return edge_ref[x, rows(y), :]
                if y < C - H:
                    return mid_ref[x, rows(y - H), :]
                return edge_ref[x, rows(y - 4), :]

            ring = [s_ref[x, rows(y), :] for y in range(C)] + [other(y) for y in range(C)]
            q = {y: q_ref[x, rows(y), :] for y in range(C)}
            for y in list(range(H)) + list(range(C - H, C)):
                dy = tap_sum(lambda i: ring[i % 32], C + y)
                vrow = pl.ds(pl.multiple_of(x * ROWS + y * C + half * 8, 8), 8)
                q[C + y] = dy + vb_ref[1, vrow, :] * ring[C + y] + n_ref[rows(y), :]
            for y in range(C):
                dq = tap_sum(lambda i: q[i % 32], y)
                vrow = pl.ds(pl.multiple_of(x * ROWS + y * C + half * 8, 8), 8)
                dq = dq + vb_ref[0, vrow, :] * first_ref[x, rows(y), :]
                out_ref[x, rows(y), :] = 2.0 * dq - ring[y]
        return 0

    lax.fori_loop(0, C, body, 0)

    def along_x(block, _):
        rows = pl.ds(pl.multiple_of(block * 8, 8), 8)
        ring = x_ring(mix_ref, mate_ref, rows)
        for x in range(C):
            out_ref[x, rows, :] += 2.0 * tap_sum(lambda i: ring[H + i], x)
        return 0

    lax.fori_loop(0, ROWS // 8, along_x, 0)


def make_base(s, edge, mid, vb, near, weighted, q, first, mix, mate):
    return pl.pallas_call(
        base_kernel,
        out_shape=sds((C, ROWS, S)),
        scratch_shapes=[pltpu.VMEM((ROWS, S), F32)],
        compiler_params=params(56),
        cost_estimate=cost(1 << 27, 24 << 20),
        name="base",
    )(s, edge, mid, vb, near, weighted, q, first, mix, mate)


def second_kernel(base_ref, mix_ref, low_ref, high_ref, near_ref, w_ref, second_ref, gram_ref, ext_ref, cross_ref):
    fill_z(ext_ref, mix_ref, low_ref, high_ref)
    gram_ref[...] = jnp.zeros((S, S), F32)
    cross_ref[...] = jnp.zeros((S, S), F32)

    def body(x, _):
        second_ref[x] = base_ref[x] + 2.0 * apply_near(near_ref, 0, w_ref, x)
        for y in range(C):
            rows = slice(y * C, (y + 1) * C)
            second_ref[x, rows, :] += 2.0 * z_taps(ext_ref, x, y)
        high, low = split(second_ref[x])
        turned = high.T
        gram_ref[...] += mm(turned, high)
        cross_ref[...] += mm(turned, low)
        return 0

    lax.fori_loop(0, C, body, 0)
    cross = cross_ref[...]
    gram_ref[...] += cross + cross.T


def make_second(base, mix, low, high, near, weighted):
    return pl.pallas_call(
        second_kernel,
        out_shape=[sds((C, ROWS, S)), sds((S, S))],
        scratch_shapes=[pltpu.VMEM((C, C * 32, S), F32), pltpu.VMEM((S, S), F32)],
        compiler_params=params(56),
        cost_estimate=cost(1 << 27, 12 << 20),
        name="second",
    )(base, mix, low, high, near, weighted)


def turn_kernel(second_ref, inverse_ref, out_ref):
    high, low = split(second_ref[...])
    i_high, i_low = split(inverse_ref[...].T)
    out_ref[...] = mm(high, i_high) + (mm(high, i_low) + mm(low, i_high))


def turn(second, inverse):
    block = 512
    return pl.pallas_call(
        turn_kernel,
        grid=(CELLS // block,),
        in_specs=[pl.BlockSpec((block, S), lambda i: (i, 0)), pl.BlockSpec((S, S), lambda i: (0, 0))],
        out_specs=pl.BlockSpec((block, S), lambda i: (i, 0)),
        out_shape=sds((CELLS, S)),
        compiler_params=params(32),
        cost_estimate=cost(1 << 28, 4 << 20),
        name="turn",
    )(second, inverse)


def per_device(states, potential, atom_sites, projectors, energies):
    gx, gy, gzs = (lax.axis_index(a) for a in AXES)
    depth = lax.axis_size("gzs")

    def swap(value, axis):
        return lax.ppermute(value, axis, [(0, 1), (1, 0)])

    def up(value):
        return lax.ppermute(value, "gzs", [(i, (i + 1) % depth) for i in range(depth)])

    def down(value):
        return lax.ppermute(value, "gzs", [((i + 1) % depth, i) for i in range(depth)])

    def both(value, axis, index):
        other = swap(value, axis)
        return jnp.where(index == 0, jnp.concatenate([value, other]), jnp.concatenate([other, value]))

    s = states.reshape(C, ROWS, S)

    atoms = jnp.concatenate(
        [
            projectors.reshape(4, W * W * W),
            atom_sites.astype(F32),
            energies[:, None],
            jnp.zeros((4, 768 - W * W * W - 4), F32),
        ],
        axis=1,
    )
    atoms = both(both(atoms, "gy", gy), "gx", gx)
    near = jnp.concatenate([up(atoms), atoms, down(atoms)])
    pot = potential.reshape(32, 128)
    pot = jnp.stack([pot, swap(pot, "gy")])

    edge, mid, head, tail = pack(s)
    edge = swap(edge, "gy")
    low, high = up(tail), down(head)
    mate = swap(s, "gx")
    mid = swap(mid, "gy")

    sites = near[:, 729:732].astype(jnp.int32)
    slab = jnp.repeat(jnp.arange(-1, 2, dtype=jnp.int32), 16) * C
    place = jnp.stack([sites[:, 0] - gx * C, sites[:, 1] - gy * C, sites[:, 2] % C + slab])
    place = jnp.pad(place, ((0, 5), (0, 80)), constant_values=1000)
    energy = near[:, 732:733] * (1.0 / filter_half)
    table = near[:, :729].reshape(NEAR, W * W, W).transpose(2, 1, 0)
    table = jnp.pad(table, ((0, 0), (0, 7), (0, 80)))
    near_g, near_t, vb = prep(table, place, pot)

    def weigh(part):
        part = part + swap(part, "gx")
        part = part + swap(part, "gy")
        own = part[16:32] + up(part[32:48]) + down(part[0:16])
        weighted = jnp.concatenate([up(own), own, down(own)]) * energy
        return jnp.pad(weighted, ((0, 80), (0, 0)))

    weighted = weigh(coef(near_t, s))
    side_part = side(s, mate, low, high)
    first, mix, q, head, tail, part = make_first(s, side_part, edge, vb, near_g, near_t, weighted)
    low, high = up(tail), down(head)
    mate = swap(mix, "gx")
    weighted_two = weigh(part)
    base = make_base(s, edge, mid, vb, near_g, weighted, q, first, mix, mate)
    second, gram = make_second(base, mix, low, high, near_g, weighted_two)

    def exchange(value, flip):
        count = 2 * 2 * depth
        return value + lax.ppermute(value, AXES, [(d, d ^ flip) for d in range(count)])

    for flip in (64, 32, 36, 1, 3, 8, 24):
        gram = exchange(gram, flip)
    gram = gram * (1.0 / (CELLS * 4 * depth))
    lower = jnp.linalg.cholesky(gram)
    inverse = lax.linalg.triangular_solve(lower, jnp.eye(S, dtype=F32), left_side=True, lower=True)
    orbitals = turn(second.reshape(CELLS, S), inverse)
    return orbitals.reshape(C, C, C, S)


def solution(mesh):
    return jax.shard_map(
        per_device,
        mesh=mesh,
        in_specs=(
            P("gx", "gy", "gzs", None),
            P("gx", "gy", "gzs"),
            P(("gx", "gy", "gzs"), None),
            P(("gx", "gy", "gzs"), None, None, None),
            P(("gx", "gy", "gzs")),
        ),
        out_specs=P("gx", "gy", "gzs", None),
        check_vma=False,
    )
```

time: 815 us -> 292 us (0.36); the launches traced: 803 us -> 292 us
  waiting for transfers between devices: 417 us -> 135 us
  matrix products: 173 us -> 0.25 us
  Pallas kernels: 0 us -> 69.9 us
  local copies, waits for them, and re-layouts: 63.2 us -> 18.1 us
  other arithmetic: 66.2 us -> 25.8 us
  starting transfers between devices: 69.6 us -> 42.5 us
  between operations: 14.4 us -> 0.33 us
    dot_general x12 -> x0, matrix products: 172 us -> none  [the longest x6 74.9 us: projector_grid(): jnp.einsum('kxi,kyj,kzl,kijl->kxyz', tables[0], tables[1], tables[2], sha...]
    ppermute x42 -> x32, waiting for transfers between devices: 287 us -> 135 us  [the longest x11 55.1 us: swap(): return lax.ppermute(value, axis, [(0, 1), (1, 0)])]
    psum x1 -> x0, waiting for transfers between devices: 130 us -> none  [per_device(): lax.psum(jnp.dot(flat_second.T, flat_second, precision=HIGH), ('gx', 'gy'...]
    pallas_call x0 -> x8, Pallas kernels: none -> 69.9 us  [the longest x1 16 us: prep(): pl.pallas_call(prep_kernel, out_shape=[sds((2, 2, CELLS, 128), BF16), sds...]
    concatenate x18 -> x2, other arithmetic: 38.7 us -> 0.76 us  [the longest x1 0.68 us: per_device(): near = jnp.concatenate([up(atoms), atoms, down(atoms)])]
    ppermute x42 -> x32, starting transfers between devices: 69.6 us -> 42.5 us  [the longest x7 32.8 us: down(): lax.ppermute(value, 'gzs', [((i + 1) % depth, i) for i in range(depth)])]
    dot_general x2 -> x0, local copies, waits for them, and re-layouts: 25.3 us -> none  [projector_grid(): jnp.einsum('kxi,kyj,kzl,kijl->kxyz', tables[0], tables[1], tables[2], sha...]
    ppermute x4 -> x0, local copies, waits for them, and re-layouts: 12.2 us -> none  [the longest x2 6.08 us: extended_2(): lax.ppermute(tail, axis, [(i, (i + 1) % count) for i in range(count)])]
  transfers between devices with their start and end apart: 43 -> 32, of which waited for: 21 -> 22; matrix products, arithmetic and copies ran while one was open for 21% -> 4% of each run, Pallas kernels for 0% -> 13%
where the time goes in v1:
time: 292 us
  waiting for transfers between devices  135 us (46%)
  Pallas kernels  69.9 us (24%)
  starting transfers between devices  42.5 us (15%)
  other arithmetic  25.8 us (9%)
  local copies, waits for them, and re-layouts  18.1 us (6%)
    ppermute x11, waiting for transfers between devices, swap(): return lax.ppermute(value, axis, [(0, 1), (1, 0)])  55.1 us
    ppermute x7, waiting for transfers between devices, up(): lax.ppermute(value, 'gzs', [(i, (i + 1) % depth) for i in range(depth)])  39.7 us
    ppermute x7, starting transfers between devices, down(): lax.ppermute(value, 'gzs', [((i + 1) % depth, i) for i in range(depth)])  32.8 us
    ppermute x7, waiting for transfers between devices, exchange(): lax.ppermute(value, AXES, [(d, d ^ flip) for d in range(count)])  29.4 us
    pallas_call x1, Pallas kernels, prep(): pl.pallas_call(prep_kernel, out_shape=[sds((2, 2, CELLS, 128), BF16), sds...  16 us
    pallas_call x1, Pallas kernels, make_base(): pl.pallas_call(base_kernel, out_shape=sds((C, ROWS, S)), scratch_shapes=[...  14.2 us
    pallas_call x1, Pallas kernels, make_second(): pl.pallas_call(second_kernel, out_shape=[sds((C, ROWS, S)), sds((S, S))],...  13.9 us
    another operation x3, other arithmetic, per_device(): lower = jnp.linalg.cholesky(gram)  12.4 us
  transfers between devices with their start and end apart: 32, of which 22 were waited for; matrix products, arithmetic and copies ran while one was open for 4% of the time, Pallas kernels for 13%

profile of v1, /device:TPU:0, one launch (start us, length us, event | category | flops | bytes accessed | tf_op | source)
XLA Modules:
  0.0 291.5 jit_solution(10875948660716489247)
XLA Ops:
  2.7 2.0 collective-permute-start.2
  6.3 2.4 pack.1
  8.8 2.1 collective-permute-start.6
  13.7 6.7 %collective-permute-start.5 = (f32[16,768]{1,0:T(8,128)S(1)}, f32[16,768]{1,0:T(8,128)S(1)}, u32[]{:S(2)}, u32[]{:S(2)}) collective-permute-start(f32[16,768]{1,0:T(8,128)S(1)} %maximum_select_fusion), channel_id=1, source_target_pairs={{1,0},{2,1},{3,2},{4,3},{5,4},{6,5},{7,6},{8,7},{9,8},{10,9},{11,1... | collective-permute-start | bytes 147464 | tf_op jit(solution)/shard_map/ppermute | solution.py:431
  20.4 42.1 %collective-permute-done.6 = f32[32,128]{1,0:T(8,128)S(1)} collective-permute-done((f32[32,128]{1,0:T(8,128)S(1)}, f32[32,128]{1,0:T(8,128)S(1)}, u32[]{:S(2)}, u32[]{:S(2)}) %collective-permute-start.6) | collective-permute-done | bytes 16416 | tf_op jit(solution)/shard_map/ppermute | solution.py:425
  62.6 7.7 %collective-permute-start.15 = (f32[6,16,16,128]{3,2,1,0:T(8,128)}, f32[6,16,16,128]{3,2,1,0:T(8,128)}, u32[]{:S(2)}, u32[]{:S(2)}) collective-permute-start(f32[6,16,16,128]{3,2,1,0:T(8,128)} %get-tuple-element.26), channel_id=1, source_target_pairs={{1,0},{2,1},{3,2},{4,3},{5,4},{6,5},{7,6},{8,7},{9,8},{10,9},{11,1... | collective-permute-start | bytes 2359304 | tf_op jit(solution)/shard_map/ppermute | solution.py:431
  70.3 2.1 collective-permute-done.4
  78.7 16.0 %prep.1 = (bf16[2,2,4096,128]{3,2,1,0:T(8,128)(2,1)S(1)}, bf16[96,4096]{1,0:T(8,128)(2,1)S(1)}, f32[2,4096,128]{2,1,0:T(8,128)}) custom-call(f32[9,88,128]{2,1,0:T(8,128)S(1)} %pad.15.table_ref, s32[8,128]{1,0:T(8,128)S(1)} %pad.16.place_ref, f32[2,32,128]{2,1,0:T(8,128)S(1)} %pad_maximum_fusion.1.pot_ref), custom_call_target="tpu_custom_call" | custom-call | flops 33554432 | bytes 10485760 | tf_op jit(solution)/shard_map/prep/pallas_call | solution.py:228
  98.7 3.5 %collective-permute-done.8 = f32[48,128]{1,0:T(8,128)S(1)} collective-permute-done((f32[48,128]{1,0:T(8,128)S(1)}, f32[48,128]{1,0:T(8,128)S(1)}, u32[]{:S(2)}, u32[]{:S(2)}) %collective-permute-start.8) | collective-permute-done | bytes 24608 | tf_op jit(solution)/shard_map/ppermute | solution.py:425
  102.3 3.6 %collective-permute-done.10 = f32[16,128]{1,0:T(8,128)S(1)} collective-permute-done((f32[16,128]{1,0:T(8,128)S(1)}, f32[16,128]{1,0:T(8,128)S(1)}, u32[]{:S(2)}, u32[]{:S(2)}) %collective-permute-start.10) | collective-permute-done | bytes 8224 | tf_op jit(solution)/shard_map/ppermute | solution.py:431
  106.0 9.4 %collective-permute-done.9 = f32[16,128]{1,0:T(8,128)S(1)} collective-permute-done((f32[16,128]{1,0:T(8,128)S(1)}, f32[16,128]{1,0:T(8,128)S(1)}, u32[]{:S(2)}, u32[]{:S(2)}) %collective-permute-start.9) | collective-permute-done | bytes 8224 | tf_op jit(solution)/shard_map/ppermute | solution.py:428
  115.4 3.6 %collective-permute-done.12 = f32[16,128]{1,0:T(8,128)S(1)} collective-permute-done((f32[16,128]{1,0:T(8,128)S(1)}, f32[16,128]{1,0:T(8,128)S(1)}, u32[]{:S(2)}, u32[]{:S(2)}) %collective-permute-start.12) | collective-permute-done | bytes 8224 | tf_op jit(solution)/shard_map/ppermute | solution.py:431
  119.2 9.2 %collective-permute-done.11 = f32[16,128]{1,0:T(8,128)S(1)} collective-permute-done((f32[16,128]{1,0:T(8,128)S(1)}, f32[16,128]{1,0:T(8,128)S(1)}, u32[]{:S(2)}, u32[]{:S(2)}) %collective-permute-start.11) | collective-permute-done | bytes 8224 | tf_op jit(solution)/shard_map/ppermute | solution.py:428
  129.1 6.0 %side.1.side_ref = f32[16,256,128]{2,1,0:T(8,128)S(1)} custom-call(f32[16,256,128]{2,1,0:T(8,128)S(1)} %bitcast.29, f32[16,256,128]{2,1,0:T(8,128)} %collective-permute-done.13.mate_ref, f32[6,16,16,128]{3,2,1,0:T(8,128)S(1)} %collective-permute-done.14.low_ref, f32[6,16,16,128]{3,2,1,0:T(8,128)} %collective-permute-done.15.high_ref), custom_call_target="tpu_custom_call" | custom-call | flops 33554432 | bytes 8388608 | tf_op jit(solution)/shard_map/side/pallas_call | solution.py:143
  136.5 12.3 %first.1 = (f32[16,256,128]{2,1,0:T(8,128)}, f32[16,256,128]{2,1,0:T(8,128)}, f32[16,256,128]{2,1,0:T(8,128)}, f32[6,16,16,128]{3,2,1,0:T(8,128)}, f32[6,16,16,128]{3,2,1,0:T(8,128)}, /*index=5*/f32[48,128]{1,0:T(8,128)}) custom-call(f32[16,256,128]{2,1,0:T(8,128)} %bitcast.25, f32[16,256,128]{2,1,0:T(8,128)} %copy-done.3, ...), custom_call_target="tpu_custom_call" | custom-call | flops 134217728 | bytes 20971520 | tf_op jit(solution)/shard_map/first/pallas_call | solution.py:308
  148.8 7.7 %collective-permute-start.18 = (f32[6,16,16,128]{3,2,1,0:T(8,128)}, f32[6,16,16,128]{3,2,1,0:T(8,128)S(1)}, u32[]{:S(2)}, u32[]{:S(2)}) collective-permute-start(f32[6,16,16,128]{3,2,1,0:T(8,128)} %get-tuple-element.31), channel_id=1, source_target_pairs={{1,0},{2,1},{3,2},{4,3},{5,4},{6,5},{7,6},{8,7},{9,8},{10,9},{11,1... | collective-permute-start | bytes 2359304 | tf_op jit(solution)/shard_map/ppermute | solution.py:431
  160.7 5.9 %collective-permute-done.20 = f32[48,128]{1,0:T(8,128)S(1)} collective-permute-done((f32[48,128]{1,0:T(8,128)S(1)}, f32[48,128]{1,0:T(8,128)S(1)}, u32[]{:S(2)}, u32[]{:S(2)}) %collective-permute-start.20) | collective-permute-done | bytes 24608 | tf_op jit(solution)/shard_map/ppermute | solution.py:425
  166.7 8.5 %collective-permute-start.22 = (f32[16,128]{1,0:T(8,128)S(1)}, f32[16,128]{1,0:T(8,128)S(1)}, u32[]{:S(2)}, u32[]{:S(2)}) collective-permute-start(f32[16,128]{1,0:T(8,128)S(1)} %get-tuple-element.39), channel_id=1, source_target_pairs={{1,0},{2,1},{3,2},{4,3},{5,4},{6,5},{7,6},{8,7},{9,8},{10,9},{11,1... | collective-permute-start | bytes 24584 | tf_op jit(solution)/shard_map/ppermute | solution.py:431
  176.5 9.7 %collective-permute-done.21 = f32[16,128]{1,0:T(8,128)S(1)} collective-permute-done((f32[16,128]{1,0:T(8,128)S(1)}, f32[16,128]{1,0:T(8,128)S(1)}, u32[]{:S(2)}, u32[]{:S(2)}) %collective-permute-start.21) | collective-permute-done | bytes 8224 | tf_op jit(solution)/shard_map/ppermute | solution.py:428
  186.3 2.0 collective-permute-start.24
  189.9 9.4 %collective-permute-done.23 = f32[16,128]{1,0:T(8,128)S(1)} collective-permute-done((f32[16,128]{1,0:T(8,128)S(1)}, f32[16,128]{1,0:T(8,128)S(1)}, u32[]{:S(2)}, u32[]{:S(2)}) %collective-permute-start.23) | collective-permute-done | bytes 8224 | tf_op jit(solution)/shard_map/ppermute | solution.py:428
  201.5 14.2 %base.1.base_ref = f32[16,256,128]{2,1,0:T(8,128)} custom-call(f32[16,256,128]{2,1,0:T(8,128)} %bitcast.26, f32[16,192,128]{2,1,0:T(8,128)} %collective-permute-done.edge_ref, f32[16,64,128]{2,1,0:T(8,128)} %copy-done.9, f32[2,4096,128]{2,1,0:T(8,128)} %get-tuple-element.22.vb_ref, bf16[2,2,4096,128]{3,2,1,0:T(8,128)(2,1)} %copy-done.2, ...), custom_call_target="tpu_custom_call" | custom-call | flops 134217728 | bytes 25165824 | tf_op jit(solution)/shard_map/base/pallas_call | solution.py:358
  217.6 13.9 %second.1 = (f32[16,256,128]{2,1,0:T(8,128)}, f32[128,128]{1,0:T(8,128)}) custom-call(f32[16,256,128]{2,1,0:T(8,128)} %base.1.base_ref, f32[16,256,128]{2,1,0:T(8,128)} %get-tuple-element.29.mix_ref, f32[6,16,16,128]{3,2,1,0:T(8,128)} %copy-done.7, f32[6,16,16,128]{3,2,1,0:T(8,128)} %copy-done.8, bf16[2,2,4096,128]{3,2,1,0:T(8,128)(2,1)} %copy-done.2, ...), custom_call_target="tpu_custom_call" | custom-call | flops 134217728 | bytes 12582912 | tf_op jit(solution)/shard_map/second/pallas_call | solution.py:390
  235.0 3.2 %collective-permute-done.26 = f32[128,128]{0,1:T(8,128)S(1)} collective-permute-done((f32[128,128]{0,1:T(8,128)S(1)}, f32[128,128]{0,1:T(8,128)S(1)}, u32[]{:S(2)}, u32[]{:S(2)}) %collective-permute-start.26) | collective-permute-done | bytes 65568 | tf_op jit(solution)/shard_map/ppermute | solution.py:486
  238.4 5.5 %collective-permute-done.27 = f32[128,128]{0,1:T(8,128)S(1)} collective-permute-done((f32[128,128]{0,1:T(8,128)S(1)}, f32[128,128]{0,1:T(8,128)S(1)}, u32[]{:S(2)}, u32[]{:S(2)}) %collective-permute-start.27) | collective-permute-done | bytes 65568 | tf_op jit(solution)/shard_map/ppermute | solution.py:486
  244.0 4.3 %collective-permute-done.28 = f32[128,128]{0,1:T(8,128)S(1)} collective-permute-done((f32[128,128]{0,1:T(8,128)S(1)}, f32[128,128]{0,1:T(8,128)S(1)}, u32[]{:S(2)}, u32[]{:S(2)}) %collective-permute-start.28) | collective-permute-done | bytes 65568 | tf_op jit(solution)/shard_map/ppermute | solution.py:486
  248.3 5.5 %collective-permute-done.29 = f32[128,128]{0,1:T(8,128)S(1)} collective-permute-done((f32[128,128]{0,1:T(8,128)S(1)}, f32[128,128]{0,1:T(8,128)S(1)}, u32[]{:S(2)}, u32[]{:S(2)}) %collective-permute-start.29) | collective-permute-done | bytes 65568 | tf_op jit(solution)/shard_map/ppermute | solution.py:486
  253.9 4.3 %collective-permute-done.30 = f32[128,128]{0,1:T(8,128)S(1)} collective-permute-done((f32[128,128]{0,1:T(8,128)S(1)}, f32[128,128]{0,1:T(8,128)S(1)}, u32[]{:S(2)}, u32[]{:S(2)}) %collective-permute-start.30) | collective-permute-done | bytes 65568 | tf_op jit(solution)/shard_map/ppermute | solution.py:486
  258.3 5.5 %collective-permute-done.31 = f32[128,128]{0,1:T(8,128)S(1)} collective-permute-done((f32[128,128]{0,1:T(8,128)S(1)}, f32[128,128]{0,1:T(8,128)S(1)}, u32[]{:S(2)}, u32[]{:S(2)}) %collective-permute-start.31) | collective-permute-done | bytes 65568 | tf_op jit(solution)/shard_map/ppermute | solution.py:486
  263.8 11.7 %cholesky.17 = f32[128,128]{1,0:T(8,128)S(1)} custom-call(f32[128,128]{1,0:T(8,128)S(1)} %fusion.3), custom_call_target="Cholesky" | custom-call | tf_op jit(solution)/shard_map/jit(cholesky)/cholesky | solution.py:491
  276.9 9.8 %custom-call.6 = f32[1,128,128]{1,2,0:T(8,128)S(1)} custom-call(f32[1,128,128]{2,1,0:T(8,128)S(1)} %fusion), custom_call_target="InvertDiagBlocksLowerTriangular" | custom-call | tf_op jit(solution)/shard_map/triangular_solve | solution.py:492
  287.0 4.5 %turn.1 = f32[4096,128]{1,0:T(8,128)} custom-call(f32[4096,128]{1,0:T(8,128)S(1)} %bitcast.30, f32[128,128]{1,0:T(8,128)S(1)} %fusion.1.inverse_ref), custom_call_target="tpu_custom_call" | custom-call | flops 268435456 | bytes 4194304 | tf_op jit(solution)/shard_map/turn/pallas_call | solution.py:408
  (119 shorter events, 36.7 us)
Async XLA Ops:
  0.0 129.1 %collective-permute-start.13 = (f32[16,256,128]{2,1,0:T(8,128)}, f32[16,256,128]{2,1,0:T(8,128)}, u32[]{:S(2)}, u32[]{:S(2)}) collective-permute-start(f32[16,256,128]{2,1,0:T(8,128)} %bitcast.24), channel_id=1, source_target_pairs={{0,64},{64,0},{1,65},{65,1},{2,66},{66,2},{3,67},{67,3},{4,68},{68... | collective-permute-start | bytes 6291464 | tf_op jit(solution)/shard_map/ppermute | solution.py:425
  2.7 9.7 %collective-permute-start.2 = (f32[4,768]{1,0:T(4,128)S(1)}, f32[4,768]{1,0:T(4,128)S(1)}, u32[]{:S(2)}, u32[]{:S(2)}) collective-permute-start(f32[4,768]{1,0:T(4,128)S(1)} %pad_maximum_fusion.2), channel_id=1, source_target_pairs={{0,32},{32,0},{1,33},{33,1},{2,34},{34,2},{3,35},{35,3},{4,36},{36... | collective-permute-start | bytes 36872 | tf_op jit(solution)/shard_map/ppermute | solution.py:425
  8.7 127.8 %collective-permute-start = (f32[16,192,128]{2,1,0:T(8,128)}, f32[16,192,128]{2,1,0:T(8,128)}, u32[]{:S(2)}, u32[]{:S(2)}) collective-permute-start(f32[16,192,128]{2,1,0:T(8,128)} %get-tuple-element.20), channel_id=1, source_target_pairs={{0,32},{32,0},{1,33},{33,1},{2,34},{34,2},{3,35},{35,3},{4,36},{36... | collective-permute-start | bytes 4718600 | tf_op jit(solution)/shard_map/ppermute | solution.py:425
  8.8 53.8 %collective-permute-start.6 = (f32[32,128]{1,0:T(8,128)S(1)}, f32[32,128]{1,0:T(8,128)S(1)}, u32[]{:S(2)}, u32[]{:S(2)}) collective-permute-start(f32[32,128]{1,0:T(8,128)S(1)} %reshape.122), channel_id=1, source_target_pairs={{0,32},{32,0},{1,33},{33,1},{2,34},{34,2},{3,35},{35,3},{4,36},{36... | collective-permute-start | bytes 49160 | tf_op jit(solution)/shard_map/ppermute | solution.py:425
  10.9 118.2 %collective-permute-start.14 = (f32[6,16,16,128]{3,2,1,0:T(8,128)}, f32[6,16,16,128]{3,2,1,0:T(8,128)S(1)}, u32[]{:S(2)}, u32[]{:S(2)}) collective-permute-start(f32[6,16,16,128]{3,2,1,0:T(8,128)} %get-tuple-element.25), channel_id=1, source_target_pairs={{0,1},{1,2},{2,3},{3,4},{4,5},{5,6},{6,7},{7,8},{8,9},{9,10},{10,1... | collective-permute-start | bytes 2359304 | tf_op jit(solution)/shard_map/ppermute | solution.py:428
  12.5 1.2 collective-permute-start.3
  13.7 48.9 %collective-permute-start.5 = (f32[16,768]{1,0:T(8,128)S(1)}, f32[16,768]{1,0:T(8,128)S(1)}, u32[]{:S(2)}, u32[]{:S(2)}) collective-permute-start(f32[16,768]{1,0:T(8,128)S(1)} %maximum_select_fusion), channel_id=1, source_target_pairs={{1,0},{2,1},{3,2},{4,3},{5,4},{6,5},{7,6},{8,7},{9,8},{10,9},{11,1... | collective-permute-start | bytes 147464 | tf_op jit(solution)/shard_map/ppermute | solution.py:431
  62.6 9.8 %collective-permute-start.4 = (f32[16,768]{1,0:T(8,128)S(1)}, f32[16,768]{1,0:T(8,128)S(1)}, u32[]{:S(2)}, u32[]{:S(2)}) collective-permute-start(f32[16,768]{1,0:T(8,128)S(1)} %maximum_select_fusion), channel_id=1, source_target_pairs={{0,1},{1,2},{2,3},{3,4},{4,5},{5,6},{6,7},{7,8},{8,9},{9,10},{10,1... | collective-permute-start | bytes 147464 | tf_op jit(solution)/shard_map/ppermute | solution.py:428
  62.6 66.5 %collective-permute-start.15 = (f32[6,16,16,128]{3,2,1,0:T(8,128)}, f32[6,16,16,128]{3,2,1,0:T(8,128)}, u32[]{:S(2)}, u32[]{:S(2)}) collective-permute-start(f32[6,16,16,128]{3,2,1,0:T(8,128)} %get-tuple-element.26), channel_id=1, source_target_pairs={{1,0},{2,1},{3,2},{4,3},{5,4},{6,5},{7,6},{8,7},{9,8},{10,9},{11,1... | collective-permute-start | bytes 2359304 | tf_op jit(solution)/shard_map/ppermute | solution.py:431
  97.1 1.3 collective-permute-start.7
  98.4 3.8 %collective-permute-start.8 = (f32[48,128]{1,0:T(8,128)S(1)}, f32[48,128]{1,0:T(8,128)S(1)}, u32[]{:S(2)}, u32[]{:S(2)}) collective-permute-start(f32[48,128]{1,0:T(8,128)S(1)} %add.93), channel_id=1, source_target_pairs={{0,32},{32,0},{1,33},{33,1},{2,34},{34,2},{3,35},{35,3},{4,36},{36... | collective-permute-start | bytes 73736 | tf_op jit(solution)/shard_map/ppermute | solution.py:425
  102.3 3.7 %collective-permute-start.10 = (f32[16,128]{1,0:T(8,128)S(1)}, f32[16,128]{1,0:T(8,128)S(1)}, u32[]{:S(2)}, u32[]{:S(2)}) collective-permute-start(f32[16,128]{1,0:T(8,128)S(1)} %get-tuple-element.41), channel_id=1, source_target_pairs={{1,0},{2,1},{3,2},{4,3},{5,4},{6,5},{7,6},{8,7},{9,8},{10,9},{11,1... | collective-permute-start | bytes 24584 | tf_op jit(solution)/shard_map/ppermute | solution.py:431
  106.0 9.4 %collective-permute-start.9 = (f32[16,128]{1,0:T(8,128)S(1)}, f32[16,128]{1,0:T(8,128)S(1)}, u32[]{:S(2)}, u32[]{:S(2)}) collective-permute-start(f32[16,128]{1,0:T(8,128)S(1)} %get-tuple-element.40), channel_id=1, source_target_pairs={{0,1},{1,2},{2,3},{3,4},{4,5},{5,6},{6,7},{7,8},{8,9},{9,10},{10,1... | collective-permute-start | bytes 24584 | tf_op jit(solution)/shard_map/ppermute | solution.py:428
  115.4 3.7 %collective-permute-start.12 = (f32[16,128]{1,0:T(8,128)S(1)}, f32[16,128]{1,0:T(8,128)S(1)}, u32[]{:S(2)}, u32[]{:S(2)}) collective-permute-start(f32[16,128]{1,0:T(8,128)S(1)} %fusion.8), channel_id=1, source_target_pairs={{1,0},{2,1},{3,2},{4,3},{5,4},{6,5},{7,6},{8,7},{9,8},{10,9},{11,1... | collective-permute-start | bytes 24584 | tf_op jit(solution)/shard_map/ppermute | solution.py:431
  119.0 9.4 %collective-permute-start.11 = (f32[16,128]{1,0:T(8,128)S(1)}, f32[16,128]{1,0:T(8,128)S(1)}, u32[]{:S(2)}, u32[]{:S(2)}) collective-permute-start(f32[16,128]{1,0:T(8,128)S(1)} %fusion.8), channel_id=1, source_target_pairs={{0,1},{1,2},{2,3},{3,4},{4,5},{5,6},{6,7},{7,8},{8,9},{9,10},{10,1... | collective-permute-start | bytes 24584 | tf_op jit(solution)/shard_map/ppermute | solution.py:428
  148.8 51.3 %collective-permute-start.16 = (f32[16,256,128]{2,1,0:T(8,128)}, f32[16,256,128]{2,1,0:T(8,128)S(1)}, u32[]{:S(2)}, u32[]{:S(2)}) collective-permute-start(f32[16,256,128]{2,1,0:T(8,128)} %get-tuple-element.29.mix_ref), channel_id=1, source_target_pairs={{0,64},{64,0},{1,65},{65,1},{2,66},{66,2},{3,67},{67,3},{4,68},{68... | collective-permute-start | bytes 6291464 | tf_op jit(solution)/shard_map/ppermute | solution.py:425
  148.8 67.0 %collective-permute-start.17 = (f32[6,16,16,128]{3,2,1,0:T(8,128)}, f32[6,16,16,128]{3,2,1,0:T(8,128)S(1)}, u32[]{:S(2)}, u32[]{:S(2)}) collective-permute-start(f32[6,16,16,128]{3,2,1,0:T(8,128)} %get-tuple-element.30), channel_id=1, source_target_pairs={{0,1},{1,2},{2,3},{3,4},{4,5},{5,6},{6,7},{7,8},{8,9},{9,10},{10,1... | collective-permute-start | bytes 2359304 | tf_op jit(solution)/shard_map/ppermute | solution.py:428
  148.8 66.9 %collective-permute-start.18 = (f32[6,16,16,128]{3,2,1,0:T(8,128)}, f32[6,16,16,128]{3,2,1,0:T(8,128)S(1)}, u32[]{:S(2)}, u32[]{:S(2)}) collective-permute-start(f32[6,16,16,128]{3,2,1,0:T(8,128)} %get-tuple-element.31), channel_id=1, source_target_pairs={{1,0},{2,1},{3,2},{4,3},{5,4},{6,5},{7,6},{8,7},{9,8},{10,9},{11,1... | collective-permute-start | bytes 2359304 | tf_op jit(solution)/shard_map/ppermute | solution.py:431
  156.6 1.4 collective-permute-start.19
  158.7 8.0 %collective-permute-start.20 = (f32[48,128]{1,0:T(8,128)S(1)}, f32[48,128]{1,0:T(8,128)S(1)}, u32[]{:S(2)}, u32[]{:S(2)}) collective-permute-start(f32[48,128]{1,0:T(8,128)S(1)} %add.97), channel_id=1, source_target_pairs={{0,32},{32,0},{1,33},{33,1},{2,34},{34,2},{3,35},{35,3},{4,36},{36... | collective-permute-start | bytes 73736 | tf_op jit(solution)/shard_map/ppermute | solution.py:425
  159.0 41.0 %collective-permute-start.1 = (f32[16,64,128]{2,1,0:T(8,128)S(1)}, f32[16,64,128]{2,1,0:T(8,128)S(1)}, u32[]{:S(2)}, u32[]{:S(2)}) collective-permute-start(f32[16,64,128]{2,1,0:T(8,128)S(1)} %get-tuple-element.21), channel_id=1, source_target_pairs={{0,32},{32,0},{1,33},{33,1},{2,34},{34,2},{3,35},{35,3},{4,36},{36... | collective-permute-start | bytes 1572872 | tf_op jit(solution)/shard_map/ppermute | solution.py:425
  166.7 9.8 %collective-permute-start.22 = (f32[16,128]{1,0:T(8,128)S(1)}, f32[16,128]{1,0:T(8,128)S(1)}, u32[]{:S(2)}, u32[]{:S(2)}) collective-permute-start(f32[16,128]{1,0:T(8,128)S(1)} %get-tuple-element.39), channel_id=1, source_target_pairs={{1,0},{2,1},{3,2},{4,3},{5,4},{6,5},{7,6},{8,7},{9,8},{10,9},{11,1... | collective-permute-start | bytes 24584 | tf_op jit(solution)/shard_map/ppermute | solution.py:431
  176.5 9.7 %collective-permute-start.21 = (f32[16,128]{1,0:T(8,128)S(1)}, f32[16,128]{1,0:T(8,128)S(1)}, u32[]{:S(2)}, u32[]{:S(2)}) collective-permute-start(f32[16,128]{1,0:T(8,128)S(1)} %get-tuple-element.38), channel_id=1, source_target_pairs={{0,1},{1,2},{2,3},{3,4},{4,5},{5,6},{6,7},{7,8},{8,9},{9,10},{10,1... | collective-permute-start | bytes 24584 | tf_op jit(solution)/shard_map/ppermute | solution.py:428
  186.3 3.7 %collective-permute-start.24 = (f32[16,128]{1,0:T(8,128)S(1)}, f32[16,128]{1,0:T(8,128)S(1)}, u32[]{:S(2)}, u32[]{:S(2)}) collective-permute-start(f32[16,128]{1,0:T(8,128)S(1)} %fusion.7), channel_id=1, source_target_pairs={{1,0},{2,1},{3,2},{4,3},{5,4},{6,5},{7,6},{8,7},{9,8},{10,9},{11,1... | collective-permute-start | bytes 24584 | tf_op jit(solution)/shard_map/ppermute | solution.py:431
  189.9 9.4 %collective-permute-start.23 = (f32[16,128]{1,0:T(8,128)S(1)}, f32[16,128]{1,0:T(8,128)S(1)}, u32[]{:S(2)}, u32[]{:S(2)}) collective-permute-start(f32[16,128]{1,0:T(8,128)S(1)} %fusion.7), channel_id=1, source_target_pairs={{0,1},{1,2},{2,3},{3,4},{4,5},{5,6},{6,7},{7,8},{8,9},{9,10},{10,1... | collective-permute-start | bytes 24584 | tf_op jit(solution)/shard_map/ppermute | solution.py:428
  232.6 1.3 collective-permute-start.25
  233.9 4.3 %collective-permute-start.26 = (f32[128,128]{0,1:T(8,128)S(1)}, f32[128,128]{0,1:T(8,128)S(1)}, u32[]{:S(2)}, u32[]{:S(2)}) collective-permute-start(f32[128,128]{0,1:T(8,128)S(1)} %add.101), channel_id=1, source_target_pairs={{0,32},{1,33},{2,34},{3,35},{4,36},{5,37},{6,38},{7,39},{8,40},{9,... | collective-permute-start | bytes 196616 | tf_op jit(solution)/shard_map/ppermute | solution.py:486
  238.3 5.6 %collective-permute-start.27 = (f32[128,128]{0,1:T(8,128)S(1)}, f32[128,128]{0,1:T(8,128)S(1)}, u32[]{:S(2)}, u32[]{:S(2)}) collective-permute-start(f32[128,128]{0,1:T(8,128)S(1)} %add.102), channel_id=1, source_target_pairs={{0,36},{1,37},{2,38},{3,39},{4,32},{5,33},{6,34},{7,35},{8,44},{9,... | collective-permute-start | bytes 196616 | tf_op jit(solution)/shard_map/ppermute | solution.py:486
  243.9 4.3 %collective-permute-start.28 = (f32[128,128]{0,1:T(8,128)S(1)}, f32[128,128]{0,1:T(8,128)S(1)}, u32[]{:S(2)}, u32[]{:S(2)}) collective-permute-start(f32[128,128]{0,1:T(8,128)S(1)} %add.103), channel_id=1, source_target_pairs={{0,1},{1,0},{2,3},{3,2},{4,5},{5,4},{6,7},{7,6},{8,9},{9,8},{10,11... | collective-permute-start | bytes 196616 | tf_op jit(solution)/shard_map/ppermute | solution.py:486
  248.2 5.6 %collective-permute-start.29 = (f32[128,128]{0,1:T(8,128)S(1)}, f32[128,128]{0,1:T(8,128)S(1)}, u32[]{:S(2)}, u32[]{:S(2)}) collective-permute-start(f32[128,128]{0,1:T(8,128)S(1)} %add.104), channel_id=1, source_target_pairs={{0,3},{1,2},{2,1},{3,0},{4,7},{5,6},{6,5},{7,4},{8,11},{9,10},{10,... | collective-permute-start | bytes 196616 | tf_op jit(solution)/shard_map/ppermute | solution.py:486
  253.8 4.3 %collective-permute-start.30 = (f32[128,128]{0,1:T(8,128)S(1)}, f32[128,128]{0,1:T(8,128)S(1)}, u32[]{:S(2)}, u32[]{:S(2)}) collective-permute-start(f32[128,128]{0,1:T(8,128)S(1)} %add.105), channel_id=1, source_target_pairs={{0,8},{1,9},{2,10},{3,11},{4,12},{5,13},{6,14},{7,15},{8,0},{9,1},... | collective-permute-start | bytes 196616 | tf_op jit(solution)/shard_map/ppermute | solution.py:486
  258.2 5.6 %collective-permute-start.31 = (f32[128,128]{0,1:T(8,128)S(1)}, f32[128,128]{0,1:T(8,128)S(1)}, u32[]{:S(2)}, u32[]{:S(2)}) collective-permute-start(f32[128,128]{0,1:T(8,128)S(1)} %add.106), channel_id=1, source_target_pairs={{0,24},{1,25},{2,26},{3,27},{4,28},{5,29},{6,30},{7,31},{8,16},{9,... | collective-permute-start | bytes 196616 | tf_op jit(solution)/shard_map/ppermute | solution.py:486
  (13 other events, 176.3 us)

commit v2 on v0

v2 whole, which is shorter than its diff:
```python
import math

import jax
import jax.numpy as jnp
from jax import lax
from jax.experimental import pallas as pl
from jax.experimental.pallas import tpu as pltpu
from jax.sharding import PartitionSpec as P

AXES = ("gx", "gy", "gzs")
H = 6
C = 16
ROWS = C * C
CELLS = C * C * C
S = 128
W = 9
R = 4
NEAR = 48
TAPS = W * W * W
F32 = jnp.float32
BF16 = jnp.bfloat16

grid_step = 0.6
filter_centre = 36.0
filter_half = 26.0


def weights():
    taps = []
    for k in range(1, 7):
        top = 2.0 * (-1) ** (k + 1) * math.factorial(6) ** 2
        under = k * k * math.factorial(6 - k) * math.factorial(6 + k)
        taps.append(top / under)
    scale = -0.5 / (grid_step * grid_step)
    off = [scale * t / filter_half for t in taps]
    diagonal = 3.0 * scale * (-2.0 * sum(taps))
    return off, diagonal


OFF, DIAGONAL = weights()


def params(mib):
    return pltpu.CompilerParams(vmem_limit_bytes=mib * 1024 * 1024)


def cost(flops, nbytes):
    return pl.CostEstimate(flops=flops, bytes_accessed=nbytes, transcendentals=0)


def sds(shape, dtype=F32):
    return jax.ShapeDtypeStruct(shape, dtype)


def split(value):
    high = value.astype(BF16)
    low = (value - high.astype(F32)).astype(BF16)
    return high, low


def mm(a, b):
    return jnp.dot(a, b, preferred_element_type=F32)


def tap_sum(at, index):
    total = None
    for k in range(1, 7):
        term = OFF[k - 1] * (at(index + k) + at(index - k))
        total = term if total is None else total + term
    return total


def stride_rows(z):
    return pl.ds(z, C, stride=C)


def plane_spec(rows=ROWS):
    return pl.BlockSpec((1, rows, S), lambda i: (i, 0, 0))


def halo_spec():
    return pl.BlockSpec((H, 1, C, S), lambda i: (0, i, 0, 0))


def part_spec(part):
    return pl.BlockSpec((1, 1, ROWS, S), lambda i: (part, i, 0, 0))


def whole(rows=S):
    return pl.BlockSpec((rows, S), lambda i: (0, 0))


FULL = sds((C, ROWS, S))
HALO = sds((H, C, C, S))


def pack_kernel(s_ref, edge_ref, mid_ref, head_ref, tail_ref):
    edge_ref[0, 0:96, :] = s_ref[0, 0:96, :]
    edge_ref[0, 96:192, :] = s_ref[0, 160:256, :]
    mid_ref[0] = s_ref[0, 96:160, :]
    for z in range(H):
        head_ref[z, 0] = s_ref[0, stride_rows(z), :]
        tail_ref[z, 0] = s_ref[0, stride_rows(C - H + z), :]


def pack(s):
    return pl.pallas_call(
        pack_kernel,
        grid=(C,),
        in_specs=[plane_spec()],
        out_specs=[plane_spec(192), plane_spec(64), halo_spec(), halo_spec()],
        out_shape=[sds((C, 192, S)), sds((C, 64, S)), HALO, HALO],
        compiler_params=params(16),
        cost_estimate=cost(1000, 6 << 20),
        name="pack",
    )(s)


def z_taps(ext_ref, x, y):
    return tap_sum(lambda k: ext_ref[x, y * 32 + 8 + k : y * 32 + 24 + k, :], 0)


def side_kernel(*refs):
    if len(refs) == 6:
        s_ref, mate_ref, low_ref, high_ref, out_ref, ext_ref = refs
    else:
        s_ref, mate_ref, out_ref, ext_ref = refs
        low_ref = high_ref = None

    def along_z(x, _):
        for y in range(C):
            ext_ref[x, y * 32 + 8 : y * 32 + 24, :] = s_ref[x, y * C : (y + 1) * C, :]
            if low_ref is None:
                ext_ref[x, y * 32 : y * 32 + 8, :] = jnp.zeros((8, S), F32)
                ext_ref[x, y * 32 + 24 : y * 32 + 32, :] = jnp.zeros((8, S), F32)
        if low_ref is not None:
            for z in range(H):
                ext_ref[x, pl.ds(2 + z, C, stride=32), :] = low_ref[z, x]
                ext_ref[x, pl.ds(24 + z, C, stride=32), :] = high_ref[z, x]
        for y in range(C):
            out_ref[x, y * C : (y + 1) * C, :] = z_taps(ext_ref, x, y)
        return 0

    lax.fori_loop(0, C, along_z, 0)

    def along_x(block, _):
        rows = pl.ds(pl.multiple_of(block * 8, 8), 8)
        ring = [mate_ref[C - H + i, rows, :] for i in range(H)]
        ring += [s_ref[x, rows, :] for x in range(C)]
        ring += [mate_ref[i, rows, :] for i in range(H)]
        for x in range(C):
            out_ref[x, rows, :] += tap_sum(lambda i: ring[H + i], x)
        return 0

    lax.fori_loop(0, ROWS // 8, along_x, 0)


def side(name, *arrays):
    return pl.pallas_call(
        side_kernel,
        out_shape=FULL,
        scratch_shapes=[pltpu.VMEM((C, C * 32, S), F32)],
        compiler_params=params(48),
        cost_estimate=cost(1 << 25, 8 << 20),
        name=name,
    )(*arrays)


def tap_weight(distance):
    value = jnp.zeros(distance.shape, F32)
    for k in range(1, 7):
        value = jnp.where(distance == k, OFF[k - 1], value)
    return value


def ring_tables(coordinate):
    masks, factors = [], []
    for t in range(W):
        away = (coordinate - t) & 31
        masks.append(away == 0)
        factors.append(tap_weight(jnp.minimum(away, 32 - away)))
    return masks, factors


def prep_kernel(
    near_ref, corner_ref, pot_ref, s_ref, gg_ref, vb_ref, coef_ref, table_ref, a1_ref, a1z_ref, a2_ref, a2s_ref, turn_ref
):
    for block in range(6):
        columns = slice(block * 128, block * 128 + 128)
        table_ref[columns, :] = near_ref[:, columns].T

    def spread(row, _):
        for part in range(2):
            line = (pot_ref[part, pl.ds(row, 1), :] + (DIAGONAL - filter_centre)) * (1.0 / filter_half)
            start = pl.multiple_of(row * 128, 128)
            vb_ref[part, pl.ds(start, 128), :] = jnp.broadcast_to(line, (128, 128)).T
        return 0

    lax.fori_loop(0, CELLS // 128, spread, 0)

    shape = (8, 128)
    sub = lax.broadcasted_iota(jnp.int32, shape, 0)
    lane = lax.broadcasted_iota(jnp.int32, shape, 1)
    sites = [jnp.broadcast_to(table_ref[TAPS + d : TAPS + d + 1, :], shape).astype(jnp.int32) for d in range(3)]
    px = sites[0] - corner_ref[0]
    py = sites[1] - corner_ref[1]
    pz = (sites[2] & 15) + (((lane & 63) >> 4) - 1) * C
    zero = jnp.zeros(shape, F32)

    for half in range(2):
        dz = sub + half * 8 - pz + R
        masks = [dz == t for t in range(W)]
        factors = [tap_weight(jnp.abs(dz - t)) for t in range(W)]

        def place_z(ij, _, half=half, masks=masks, factors=factors):
            acc = zero
            along = zero
            for t in range(W):
                row = jnp.broadcast_to(table_ref[pl.ds(ij * W + t, 1), :], shape)
                acc = jnp.where(masks[t], row, acc)
                along = along + factors[t] * row
            a1_ref[ij, half * 8 : half * 8 + 8, :] = acc
            a1z_ref[ij, half * 8 : half * 8 + 8, :] = along
            return 0

        lax.fori_loop(0, W * W, place_z, 0)

    def place_y(y, _):
        masks, factors = ring_tables(y - py + R)
        for i in range(W):
            for half in range(2):
                rows = slice(half * 8, half * 8 + 8)
                acc = zero
                along = zero
                moved = zero
                for t in range(W):
                    value = a1_ref[i * W + t, rows, :]
                    acc = jnp.where(masks[t], value, acc)
                    along = along + factors[t] * value
                    moved = jnp.where(masks[t], a1z_ref[i * W + t, rows, :], moved)
                a2_ref[i, y, rows, :] = acc
                a2s_ref[i, y, rows, :] = along + moved
        return 0

    lax.fori_loop(0, C, place_y, 0)

    def place_x(x, _):
        masks, factors = ring_tables(x - px + R)

        def per_y(y, _):
            row = pl.multiple_of(x * ROWS + y * C, C)
            halves = []
            for half in range(2):
                rows = slice(half * 8, half * 8 + 8)
                acc = zero
                along = zero
                moved = zero
                for t in range(W):
                    value = a2_ref[t, y, rows, :]
                    acc = jnp.where(masks[t], value, acc)
                    along = along + factors[t] * value
                    moved = jnp.where(masks[t], a2s_ref[t, y, rows, :], moved)
                vrow = pl.ds(pl.multiple_of(row + half * 8, 8), 8)
                halves.append(jnp.where(lane < 64, acc, along + moved + vb_ref[0, vrow, :] * acc))
            high, low = split(jnp.concatenate(halves, axis=0))
            gg_ref[0, pl.ds(row, C), :] = high
            gg_ref[1, pl.ds(row, C), :] = low
            return 0

        lax.fori_loop(0, C, per_y, 0)
        return 0

    lax.fori_loop(0, C, place_x, 0)

    coef_ref[...] = jnp.zeros((3, NEAR, S), F32)

    def contract(x, _):
        rows = pl.ds(pl.multiple_of(x * ROWS, ROWS), ROWS)
        g_high, g_low = gg_ref[0, rows, :], gg_ref[1, rows, :]
        turn_ref[0] = g_high.T
        turn_ref[1] = g_low.T
        t_high, t_low = turn_ref[0], turn_ref[1]
        high, low = split(s_ref[x])
        got = mm(t_high, high) + (mm(t_high, low) + mm(t_low, high))
        coef_ref[0] += got[:NEAR]
        coef_ref[1] += got[64 : 64 + NEAR]
        t_high, t_low = t_high[:NEAR], t_low[:NEAR]
        coef_ref[2] += mm(t_high, g_high) + (mm(t_high, g_low) + mm(t_low, g_high))
        return 0

    lax.fori_loop(0, C, contract, 0)


def prep(near, corner, pot, s):
    vmem = pl.BlockSpec(memory_space=pltpu.VMEM)
    return pl.pallas_call(
        prep_kernel,
        in_specs=[vmem, pl.BlockSpec(memory_space=pltpu.SMEM), vmem, vmem],
        out_shape=[sds((2, CELLS, S), BF16), sds((2, CELLS, S)), sds((3, NEAR, S))],
        scratch_shapes=[
            pltpu.VMEM((768, 128), F32),
            pltpu.VMEM((W * W, C, 128), F32),
            pltpu.VMEM((W * W, C, 128), F32),
            pltpu.VMEM((W, C, C, 128), F32),
            pltpu.VMEM((W, C, C, 128), F32),
            pltpu.VMEM((2, S, ROWS), BF16),
        ],
        compiler_params=params(48),
        cost_estimate=cost(1 << 27, 10 << 20),
        name="prep",
    )(near, corner, pot, s)


def first_kernel(s_ref, side_ref, edge_ref, vb_ref, q_ref, mix_ref, head_ref, tail_ref):
    for half in range(2):

        def rows(y, half=half):
            return slice(y * C + half * 8, y * C + half * 8 + 8)

        ring = {y: s_ref[0, rows(y), :] for y in range(C)}
        for y in range(H):
            ring[C + y] = edge_ref[0, rows(y), :]
            ring[y - H] = edge_ref[0, rows(H + y), :]
        for y in range(C):
            dy = tap_sum(lambda i: ring[i], y)
            q = dy + vb_ref[0, 0, rows(y), :] * ring[y]
            q_ref[0, rows(y), :] = q
            mix_ref[0, rows(y), :] = side_ref[0, rows(y), :] + q + dy
    for z in range(H):
        head_ref[z, 0] = mix_ref[0, stride_rows(z), :]
        tail_ref[z, 0] = mix_ref[0, stride_rows(C - H + z), :]


def make_first(s, side_part, edge, vb):
    return pl.pallas_call(
        first_kernel,
        grid=(C,),
        in_specs=[plane_spec(), plane_spec(), plane_spec(192), part_spec(0)],
        out_specs=[plane_spec(), plane_spec(), halo_spec(), halo_spec()],
        out_shape=[FULL, FULL, HALO, HALO],
        compiler_params=params(16),
        cost_estimate=cost(1 << 24, 14 << 20),
        name="first",
    )(s, side_part, edge, vb)


def base_kernel(s_ref, edge_ref, mid_ref, vb_ref, vb_mate_ref, q_ref, side_ref, part_ref, out_ref):
    for half in range(2):

        def rows(y, half=half):
            return slice(y * C + half * 8, y * C + half * 8 + 8)

        def other(y):
            if y < H:
                return edge_ref[0, rows(y), :]
            if y < C - H:
                return mid_ref[0, rows(y - H), :]
            return edge_ref[0, rows(y - 4), :]

        ring = [s_ref[0, rows(y), :] for y in range(C)] + [other(y) for y in range(C)]
        q = {y: q_ref[0, rows(y), :] for y in range(C)}
        for y in list(range(H)) + list(range(C - H, C)):
            q[C + y] = tap_sum(lambda i: ring[i % 32], C + y) + vb_mate_ref[0, 0, rows(y), :] * ring[C + y]
        for y in range(C):
            total = tap_sum(lambda i: q[i % 32], y)
            total = total + vb_ref[0, 0, rows(y), :] * (side_ref[0, rows(y), :] + q[y])
            out_ref[0, rows(y), :] = 2.0 * (total + part_ref[0, rows(y), :]) - ring[y]


def make_base(s, edge, mid, vb, q, side_part, part):
    return pl.pallas_call(
        base_kernel,
        grid=(C,),
        in_specs=[plane_spec(), plane_spec(192), plane_spec(64), part_spec(0), part_spec(1)] + [plane_spec()] * 3,
        out_specs=plane_spec(),
        out_shape=FULL,
        compiler_params=params(16),
        cost_estimate=cost(1 << 25, 16 << 20),
        name="base",
    )(s, edge, mid, vb, vb, q, side_part, part)


def second_kernel(base_ref, low_ref, high_ref, gg_high_ref, gg_low_ref, w_ref, second_ref, gram_ref, cross_ref):
    step = pl.program_id(0)

    @pl.when(step == 0)
    def _():
        gram_ref[...] = jnp.zeros((S, S), F32)
        cross_ref[...] = jnp.zeros((S, S), F32)

    w_high, w_low = split(2.0 * w_ref[...])
    g_high, g_low = gg_high_ref[0, 0], gg_low_ref[0, 0]
    second_ref[0] = base_ref[0] + (mm(g_high, w_high) + (mm(g_high, w_low) + mm(g_low, w_high)))
    low = [low_ref[j, 0] for j in range(H)]
    high = [high_ref[j, 0] for j in range(H)]
    for z in range(H):
        add = sum((2.0 * OFF[k - 1]) * low[z - k + H] for k in range(z + 1, H + 1))
        second_ref[0, stride_rows(z), :] += add
        add = sum((2.0 * OFF[H + j - z - 1]) * high[j] for j in range(z + 1))
        second_ref[0, stride_rows(C - H + z), :] += add
    s_high, s_low = split(second_ref[0])
    turned = s_high.T
    gram_ref[...] += mm(turned, s_high)
    cross_ref[...] += mm(turned, s_low)

    @pl.when(step == C - 1)
    def _():
        cross = cross_ref[...]
        gram_ref[...] += cross + cross.T


def make_second(base, low, high, gg, weighted):
    return pl.pallas_call(
        second_kernel,
        grid=(C,),
        in_specs=[plane_spec(), halo_spec(), halo_spec(), part_spec(0), part_spec(1), whole()],
        out_specs=[plane_spec(), whole()],
        out_shape=[FULL, sds((S, S))],
        scratch_shapes=[pltpu.VMEM((S, S), F32)],
        compiler_params=params(16),
        cost_estimate=cost(1 << 27, 8 << 20),
        name="second",
    )(base, low, high, gg, gg, weighted)


def exact(a, b):
    return jnp.dot(a, b, precision=lax.Precision.HIGHEST, preferred_element_type=F32)


def inverse_factor(gram_ref, a_ref, x_ref, state_ref):
    row = lax.broadcasted_iota(jnp.int32, (S, S), 0)
    column = lax.broadcasted_iota(jnp.int32, (S, S), 1)
    unit = jnp.where(row == column, 1.0, 0.0)
    gram = gram_ref[...]
    diagonal = jnp.where(row == column, gram, 0.0)
    down = lax.rsqrt(jnp.sum(diagonal, axis=1, keepdims=True))
    across = lax.rsqrt(jnp.sum(diagonal, axis=0, keepdims=True))
    a_ref[...] = gram * down * across
    x_ref[...] = unit

    def residual():
        x = x_ref[...]
        return unit - exact(exact(x, a_ref[...]), x.T)

    def size(e):
        return jnp.sum(e * e)

    def improve(e):
        lower = jnp.where(row > column, e, jnp.where(row == column, 0.5 * e, 0.0))
        x_ref[...] += exact(lower, x_ref[...])

    state_ref[0] = 0
    start = unit - a_ref[...]
    start_size = size(start)

    @pl.when(start_size < 0.16)
    def _():
        improve(start)
        state_ref[0] = jnp.where(start_size < 1e-6, 2, 1)

    for _ in range(5):

        @pl.when(state_ref[0] == 1)
        def _():
            e = residual()
            e_size = size(e)
            improve(e)
            state_ref[0] = jnp.where(e_size < 1e-6, 2, 1)

    @pl.when(state_ref[0] != 2)
    def _():
        x_ref[...] = unit
        lanes = lax.broadcasted_iota(jnp.int32, (1, S), 1)

        def step(j, _):
            line = a_ref[pl.ds(j, 1), :]
            scale = lax.rsqrt(jnp.sum(jnp.where(lanes == j, line, 0.0), axis=1, keepdims=True))
            a = a_ref[...]
            factor = jnp.sum(jnp.where(column == j, a, 0.0), axis=1, keepdims=True) * scale
            factor = jnp.where(row[:, :1] > j, factor, 0.0)
            x_line = x_ref[pl.ds(j, 1), :] * scale
            a_ref[...] = a - factor * (line * scale)
            x_ref[...] = jnp.where(row == j, x_line, x_ref[...] - factor * x_line)
            return 0

        lax.fori_loop(0, S, step, 0)

    x_ref[...] = x_ref[...] * across


def turn_kernel(second_ref, gram_ref, out_ref, a_ref, x_ref, i_high_ref, i_low_ref, state_ref):
    @pl.when(pl.program_id(0) == 0)
    def _():
        inverse_factor(gram_ref, a_ref, x_ref, state_ref)
        i_high, i_low = split(x_ref[...].T)
        i_high_ref[...] = i_high
        i_low_ref[...] = i_low

    high, low = split(second_ref[...])
    i_high = i_high_ref[...]
    out_ref[...] = mm(high, i_high) + (mm(high, i_low_ref[...]) + mm(low, i_high))


def turn(second, gram):
    block = 512
    return pl.pallas_call(
        turn_kernel,
        grid=(CELLS // block,),
        in_specs=[pl.BlockSpec((block, S), lambda i: (i, 0)), whole()],
        out_specs=pl.BlockSpec((block, S), lambda i: (i, 0)),
        out_shape=sds((CELLS, S)),
        scratch_shapes=[pltpu.VMEM((S, S), F32)] * 2 + [pltpu.VMEM((S, S), BF16)] * 2 + [pltpu.SMEM((1,), jnp.int32)],
        compiler_params=params(16),
        cost_estimate=cost(1 << 28, 4 << 20),
        name="turn",
    )(second, gram)


def per_device(states, potential, atom_sites, projectors, energies):
    gx, gy = lax.axis_index("gx"), lax.axis_index("gy")
    depth = lax.axis_size("gzs")

    def swap(value, axis):
        return lax.ppermute(value, axis, [(0, 1), (1, 0)])

    def up(value):
        return lax.ppermute(value, "gzs", [(i, (i + 1) % depth) for i in range(depth)])

    def down(value):
        return lax.ppermute(value, "gzs", [((i + 1) % depth, i) for i in range(depth)])

    def both(value, axis, index, dim):
        other = swap(value, axis)
        return jnp.where(index == 0, jnp.concatenate([value, other], dim), jnp.concatenate([other, value], dim))

    s = states.reshape(C, ROWS, S)

    atoms = jnp.concatenate(
        [
            projectors.reshape(4, TAPS),
            atom_sites.astype(F32),
            energies[:, None] * (1.0 / filter_half),
            jnp.zeros((4, 768 - TAPS - 4), F32),
        ],
        axis=1,
    )
    atoms = jnp.stack([up(atoms), atoms, down(atoms)])
    atoms = both(atoms, "gx", gx, 1)
    edge, mid, head, tail = pack(s)
    edge, atoms = lax.optimization_barrier((edge, atoms))
    pot = potential.reshape(32, 128)
    parcel = jnp.concatenate([atoms.reshape(144, 128), pot])
    parcel_mate = swap(parcel, "gy")
    edge = swap(edge, "gy")
    mate = swap(s, "gx")
    atoms_mate = parcel_mate[:144].reshape(3, 8, 768)
    near = jnp.where(
        gy == 0,
        jnp.stack([atoms.reshape(3, 2, 4, 768), atoms_mate.reshape(3, 2, 4, 768)], 2),
        jnp.stack([atoms_mate.reshape(3, 2, 4, 768), atoms.reshape(3, 2, 4, 768)], 2),
    ).reshape(NEAR, 768)
    low, high = up(tail), down(head)
    gap = jnp.zeros((16, 768), F32)
    energy = near[16:32, TAPS + 3 : TAPS + 4]
    corner = jnp.stack([gx * C, gy * C]).astype(jnp.int32)
    gg, vb, part = prep(jnp.concatenate([near, gap, near, gap]), corner, jnp.stack([pot, parcel_mate[144:]]), s)

    part = part + swap(part, "gx")
    below, above = up(part[:, 32:48]), down(part[:, 0:16])
    zeros = jnp.zeros((16, 16), F32)
    pair = part[2, 16:32, :NEAR]
    pair = pair + jnp.concatenate([below[2, :, 16:48], zeros], 1) + jnp.concatenate([zeros, above[2, :, 0:32]], 1)
    own = jnp.concatenate([part[:2, 16:32] + below[:2] + above[:2], jnp.pad(pair, ((0, 0), (0, S - NEAR)))[None]])
    own = own + swap(own, "gy")
    mid, own = lax.optimization_barrier((mid, own))
    mid = swap(mid, "gy")
    one = own[0] * energy
    one = jnp.concatenate([up(one), one, down(one)])
    two = (own[1] + jnp.dot(own[2, :, :NEAR], one, precision=lax.Precision.HIGHEST)) * energy
    two = jnp.concatenate([up(two), two, down(two)])
    gap = jnp.zeros((16, S), F32)
    weighted = jnp.concatenate([two, gap, one, gap])

    vb = vb.reshape(2, C, ROWS, S)
    side_part = side("side", s, mate, low, high)
    q, mix, head, tail = make_first(s, side_part, edge, vb)
    low, high = up(tail), down(head)
    mate = swap(mix, "gx")
    part = side("side_again", mix, mate)
    base = make_base(s, edge, mid, vb, q, side_part, part)
    second, gram = make_second(base, low, high, gg.reshape(2, C, ROWS, S), weighted)

    def exchange(value, flip):
        return value + lax.ppermute(value, AXES, [(d, d ^ flip) for d in range(4 * depth)])

    for flip in (64, 32, 36, 1, 3, 8, 24):
        gram = exchange(gram, flip)
    gram = gram * (1.0 / (CELLS * 4 * depth))
    orbitals = turn(second.reshape(CELLS, S), gram)
    return orbitals.reshape(C, C, C, S)


def solution(mesh):
    return jax.shard_map(
        per_device,
        mesh=mesh,
        in_specs=(
            P("gx", "gy", "gzs", None),
            P("gx", "gy", "gzs"),
            P(("gx", "gy", "gzs"), None),
            P(("gx", "gy", "gzs"), None, None, None),
            P(("gx", "gy", "gzs")),
        ),
        out_specs=P("gx", "gy", "gzs", None),
        check_vma=False,
    )
```

time: 815 us -> 217 us (0.27); the launches traced: 803 us -> 216 us
  waiting for transfers between devices: 417 us -> 73.8 us
  matrix products: 173 us -> 0.09 us
  Pallas kernels: 0 us -> 80.7 us
  other arithmetic: 66.2 us -> 1.97 us
  local copies, waits for them, and re-layouts: 63.2 us -> 11.3 us
  starting transfers between devices: 69.6 us -> 47.8 us
  between operations: 14.4 us -> 0.4 us
    ppermute x42 -> x27, waiting for transfers between devices: 287 us -> 73.8 us  [the longest x7 27.9 us: exchange(): lax.ppermute(value, AXES, [(d, d ^ flip) for d in range(4 * depth)])]
    dot_general x12 -> x1, matrix products: 172 us -> 0.09 us  [per_device(): jnp.dot(own[2, :, :NEAR], one, precision=lax.Precision.HIGHEST)]
    psum x1 -> x0, waiting for transfers between devices: 130 us -> none  [per_device(): lax.psum(jnp.dot(flat_second.T, flat_second, precision=HIGH), ('gx', 'gy'...]
    pallas_call x0 -> x8, Pallas kernels: none -> 80.7 us  [the longest x1 20.1 us: prep(): pl.pallas_call(prep_kernel, in_specs=[vmem, pl.BlockSpec(memory_space=plt...]
    concatenate x18 -> x4, other arithmetic: 38.7 us -> 0.12 us  [the longest x1 0.08 us: per_device(): jnp.concatenate([projectors.reshape(4, TAPS), atom_sites.astype(F32), ene...]
    dot_general x2 -> x0, local copies, waits for them, and re-layouts: 25.3 us -> none  [projector_grid(): jnp.einsum('kxi,kyj,kzl,kijl->kxyz', tables[0], tables[1], tables[2], sha...]
    another operation x5 -> x3, other arithmetic: 22.9 us -> 0.09 us  [the longest x1 0.07 us: per_device(): corner = jnp.stack([gx * C, gy * C]).astype(jnp.int32)]
    ppermute x42 -> x27, starting transfers between devices: 69.6 us -> 47.8 us  [the longest x6 39.9 us: down(): lax.ppermute(value, 'gzs', [((i + 1) % depth, i) for i in range(depth)])]
  transfers between devices with their start and end apart: 43 -> 27, of which waited for: 21 -> 18; matrix products, arithmetic and copies ran while one was open for 21% -> 1% of each run, Pallas kernels for 0% -> 21%
where the time goes in v2:
time: 217 us; the launch traced here: 216 us
  Pallas kernels  80.7 us (37%)
  waiting for transfers between devices  73.8 us (34%)
  starting transfers between devices  47.8 us (22%)
  local copies, waits for them, and re-layouts  11.3 us (5%)
    ppermute x6, starting transfers between devices, down(): lax.ppermute(value, 'gzs', [((i + 1) % depth, i) for i in range(depth)])  39.9 us
    ppermute x7, waiting for transfers between devices, exchange(): lax.ppermute(value, AXES, [(d, d ^ flip) for d in range(4 * depth)])  27.9 us
    pallas_call x1, Pallas kernels, prep(): pl.pallas_call(prep_kernel, in_specs=[vmem, pl.BlockSpec(memory_space=plt...  20.1 us
    ppermute x6, waiting for transfers between devices, up(): lax.ppermute(value, 'gzs', [(i, (i + 1) % depth) for i in range(depth)])  18.7 us
    pallas_call x1, Pallas kernels, turn(): pl.pallas_call(turn_kernel, grid=(CELLS // block,), in_specs=[pl.BlockSpe...  18.4 us
    ppermute x6, waiting for transfers between devices, down(): lax.ppermute(value, 'gzs', [((i + 1) % depth, i) for i in range(depth)])  18.1 us
    pallas_call x2, Pallas kernels, side(): pl.pallas_call(side_kernel, out_shape=FULL, scratch_shapes=[pltpu.VMEM((C...  10.7 us
    unnamed x33, local copies, waits for them, and re-layouts  10.4 us
  transfers between devices with their start and end apart: 27, of which 18 were waited for; matrix products, arithmetic and copies ran while one was open for 1% of the time, Pallas kernels for 21%

profile of v2, /device:TPU:0, one launch (start us, length us, event | category | flops | bytes accessed | tf_op | source)
XLA Modules:
  0.0 216.1 jit_solution(13205968875386341100)
XLA Ops:
  2.7 8.6 %collective-permute-start.1 = (f32[4,768]{1,0:T(4,128)S(1)}, f32[4,768]{1,0:T(4,128)S(1)}, u32[]{:S(2)}, u32[]{:S(2)}) collective-permute-start(f32[4,768]{1,0:T(4,128)S(1)} %maximum_maximum_fusion), channel_id=1, source_target_pairs={{1,0},{2,1},{3,2},{4,3},{5,4},{6,5},{7,6},{8,7},{9,8},{10,9},{11,1... | collective-permute-start | bytes 36872 | tf_op jit(solution)/shard_map/ppermute | solution.py:530
  11.4 1.4 collective-permute-done.1
  12.8 8.0 %collective-permute-done = f32[4,768]{1,0:T(4,128)S(1)} collective-permute-done((f32[4,768]{1,0:T(4,128)S(1)}, f32[4,768]{1,0:T(4,128)S(1)}, u32[]{:S(2)}, u32[]{:S(2)}) %collective-permute-start) | collective-permute-done | bytes 12320 | tf_op jit(solution)/shard_map/ppermute | solution.py:527
  20.9 1.6 copy-done
  22.5 5.3 %pack.1 = (f32[16,192,128]{2,1,0:T(8,128)S(1)}, f32[16,64,128]{2,1,0:T(8,128)}, f32[6,16,16,128]{3,2,1,0:T(8,128)S(1)}, f32[6,16,16,128]{3,2,1,0:T(8,128)S(1)}) custom-call(f32[16,256,128]{2,1,0:T(8,128)S(1)} %bitcast.36), custom_call_target="tpu_custom_call" | custom-call | flops 1000 | bytes 6291456 | tf_op jit(solution)/shard_map/pack/pallas_call | solution.py:107
  32.4 3.2 %collective-permute-done.4 = f32[176,128]{1,0:T(8,128)S(1)} collective-permute-done((f32[176,128]{1,0:T(8,128)S(1)}, f32[176,128]{1,0:T(8,128)S(1)}, u32[]{:S(2)}, u32[]{:S(2)}) %collective-permute-start.4) | collective-permute-done | bytes 90144 | tf_op jit(solution)/shard_map/ppermute | solution.py:524
  35.8 20.1 %prep.1 = (bf16[2,4096,128]{2,1,0:T(8,128)(2,1)S(1)}, f32[2,4096,128]{2,1,0:T(8,128)}, f32[3,48,128]{2,1,0:T(8,128)S(1)}) custom-call(f32[128,768]{1,0:T(8,128)S(1)} %pad_maximum_fusion.near_ref, s32[2]{0:T(128)S(1)} %pad_add_fusion.corner_ref, f32[2,32,128]{2,1,0:T(8,128)S(1)} %pad_maximum_fusion.3.pot_ref, f32[16,256,128]{2,1,0:T(8,128)S(1)} %bitcast.37), custom_call_target="tpu_custom_call" | custom-call | flops 134217728 | bytes 10485760 | tf_op jit(solution)/shard_map/prep/pallas_call | solution.py:296
  57.4 7.7 %collective-permute-start.12 = (f32[6,16,16,128]{3,2,1,0:T(8,128)S(1)}, f32[6,16,16,128]{3,2,1,0:T(8,128)S(1)}, u32[]{:S(2)}, u32[]{:S(2)}) collective-permute-start(f32[6,16,16,128]{3,2,1,0:T(8,128)S(1)} %get-tuple-element.30), channel_id=1, source_target_pairs={{1,0},{2,1},{3,2},{4,3},{5,4},{6,5},{7,6},{8,7},{9,8},{10,9},{11,1... | collective-permute-start | bytes 2359304 | tf_op jit(solution)/shard_map/ppermute | solution.py:530
  65.1 1.9 collective-permute-done.6
  67.1 15.3 %collective-permute-done.7 = f32[3,16,128]{2,1,0:T(8,128)S(1)} collective-permute-done((f32[3,16,128]{2,1,0:T(8,128)S(1)}, f32[3,16,128]{2,1,0:T(8,128)S(1)}, u32[]{:S(2)}, u32[]{:S(2)}) %collective-permute-start.7) | collective-permute-done | bytes 24608 | tf_op jit(solution)/shard_map/ppermute | solution.py:530
  83.1 6.1 %side.1.side_ref = f32[16,256,128]{2,1,0:T(8,128)S(1)} custom-call(f32[16,256,128]{2,1,0:T(8,128)S(1)} %bitcast.38, f32[16,256,128]{2,1,0:T(8,128)} %collective-permute-done.10.refs_1_, f32[6,16,16,128]{3,2,1,0:T(8,128)S(1)} %collective-permute-done.11.refs_2_, f32[6,16,16,128]{3,2,1,0:T(8,128)S(1)} %collective-permute-done.12.refs_3_), custom_call_target="tpu_custom_call" | custom-call | flops 33554432 | bytes 8388608 | tf_op jit(solution)/shard_map/side/pallas_call | solution.py:159
  89.3 8.4 %first.1 = (f32[16,256,128]{2,1,0:T(8,128)S(1)}, f32[16,256,128]{2,1,0:T(8,128)S(1)}, f32[6,16,16,128]{3,2,1,0:T(8,128)S(1)}, f32[6,16,16,128]{3,2,1,0:T(8,128)S(1)}) custom-call(f32[16,256,128]{2,1,0:T(8,128)S(1)} %bitcast.39, f32[16,256,128]{2,1,0:T(8,128)S(1)} %side.1.side_ref, f32[16,192,128]{2,1,0:T(8,128)} %collective-permute-done.3.edge_ref, ...), custom_call_target="tpu_custom_call" | custom-call | flops 16777216 | bytes 14680064 | tf_op jit(solution)/shard_map/first/pallas_call | solution.py:335
  101.7 2.6 %collective-permute-done.8 = f32[3,16,128]{2,1,0:T(8,128)S(1)} collective-permute-done((f32[3,16,128]{2,1,0:T(8,128)S(1)}, f32[3,16,128]{2,1,0:T(8,128)S(1)}, u32[]{:S(2)}, u32[]{:S(2)}) %collective-permute-start.8) | collective-permute-done | bytes 24608 | tf_op jit(solution)/shard_map/ppermute | solution.py:524
  104.4 7.6 %collective-permute-start.17 = (f32[16,128]{1,0:T(8,128)S(1)}, f32[16,128]{1,0:T(8,128)S(1)}, u32[]{:S(2)}, u32[]{:S(2)}) collective-permute-start(f32[16,128]{1,0:T(8,128)S(1)} %bitcast_multiply_fusion), channel_id=1, source_target_pairs={{1,0},{2,1},{3,2},{4,3},{5,4},{6,5},{7,6},{8,7},{9,8},{10,9},{11,1... | collective-permute-start | bytes 24584 | tf_op jit(solution)/shard_map/ppermute | solution.py:530
  112.0 1.4 collective-permute-done.17
  113.3 8.1 %collective-permute-done.16 = f32[16,128]{1,0:T(8,128)S(1)} collective-permute-done((f32[16,128]{1,0:T(8,128)S(1)}, f32[16,128]{1,0:T(8,128)S(1)}, u32[]{:S(2)}, u32[]{:S(2)}) %collective-permute-start.16) | collective-permute-done | bytes 8224 | tf_op jit(solution)/shard_map/ppermute | solution.py:527
  122.7 8.3 %collective-permute-start.19 = (f32[16,128]{1,0:T(8,128)S(1)}, f32[16,128]{1,0:T(8,128)S(1)}, u32[]{:S(2)}, u32[]{:S(2)}) collective-permute-start(f32[16,128]{1,0:T(8,128)S(1)} %fusion), channel_id=1, source_target_pairs={{1,0},{2,1},{3,2},{4,3},{5,4},{6,5},{7,6},{8,7},{9,8},{10,9},{11,1... | collective-permute-start | bytes 24584 | tf_op jit(solution)/shard_map/ppermute | solution.py:530
  131.0 7.7 %collective-permute-start.15 = (f32[6,16,16,128]{3,2,1,0:T(8,128)S(1)}, f32[6,16,16,128]{3,2,1,0:T(8,128)S(1)}, u32[]{:S(2)}, u32[]{:S(2)}) collective-permute-start(f32[6,16,16,128]{3,2,1,0:T(8,128)S(1)} %get-tuple-element.34), channel_id=1, source_target_pairs={{1,0},{2,1},{3,2},{4,3},{5,4},{6,5},{7,6},{8,7},{9,8},{10,9},{11,1... | collective-permute-start | bytes 2359304 | tf_op jit(solution)/shard_map/ppermute | solution.py:530
  138.9 1.6 copy-done.8
  140.4 4.6 %side_again.1.part_ref = f32[16,256,128]{2,1,0:T(8,128)S(1)} custom-call(f32[16,256,128]{2,1,0:T(8,128)S(1)} %copy-done.8, f32[16,256,128]{2,1,0:T(8,128)} %collective-permute-done.13.refs_1_), custom_call_target="tpu_custom_call" | custom-call | flops 33554432 | bytes 8388608 | tf_op jit(solution)/shard_map/side_again/pallas_call | solution.py:159
  145.1 2.0 collective-permute-done.9.mid_ref
  147.1 1.6 copy-done.6
  148.7 8.9 %base.1.base_ref = f32[16,256,128]{2,1,0:T(8,128)S(1)} custom-call(f32[16,256,128]{2,1,0:T(8,128)S(1)} %bitcast.40, f32[16,192,128]{2,1,0:T(8,128)} %collective-permute-done.3.edge_ref, f32[16,64,128]{2,1,0:T(8,128)S(1)} %collective-permute-done.9.mid_ref, f32[2,16,256,128]{3,2,1,0:T(8,128)S(1)} %bitcast.42, f32[2,16,256,128]{3,2,1,0:T(8,128)S(1)} %bitcast.43, ...), custom_call_target="tpu_custom_call" | custom-call | flops 33554432 | bytes 16777216 | tf_op jit(solution)/shard_map/base/pallas_call | solution.py:371
  157.7 8.9 %second.1 = (f32[16,256,128]{2,1,0:T(8,128)S(1)}, f32[128,128]{1,0:T(8,128)S(1)}) custom-call(f32[16,256,128]{2,1,0:T(8,128)S(1)} %base.1.base_ref, f32[6,16,16,128]{3,2,1,0:T(8,128)S(1)} %collective-permute-done.14.low_ref, f32[6,16,16,128]{3,2,1,0:T(8,128)S(1)} %collective-permute-done.15.high_ref, bf16[2,16,256,128]{3,2,1,0:T(8,128)(2,1)S(1)} %bitcast.44, ...), custom_call_target="tpu_custom_call" | custom-call | flops 134217728 | bytes 8388608 | tf_op jit(solution)/shard_map/second/pallas_call | solution.py:413
  168.7 3.6 %collective-permute-done.21 = f32[128,128]{1,0:T(8,128)S(1)} collective-permute-done((f32[128,128]{1,0:T(8,128)S(1)}, f32[128,128]{1,0:T(8,128)S(1)}, u32[]{:S(2)}, u32[]{:S(2)}) %collective-permute-start.21) | collective-permute-done | bytes 65568 | tf_op jit(solution)/shard_map/ppermute | solution.py:594
  172.3 5.5 %collective-permute-done.22 = f32[128,128]{1,0:T(8,128)S(1)} collective-permute-done((f32[128,128]{1,0:T(8,128)S(1)}, f32[128,128]{1,0:T(8,128)S(1)}, u32[]{:S(2)}, u32[]{:S(2)}) %collective-permute-start.22) | collective-permute-done | bytes 65568 | tf_op jit(solution)/shard_map/ppermute | solution.py:594
  177.9 4.3 %collective-permute-done.23 = f32[128,128]{1,0:T(8,128)S(1)} collective-permute-done((f32[128,128]{1,0:T(8,128)S(1)}, f32[128,128]{1,0:T(8,128)S(1)}, u32[]{:S(2)}, u32[]{:S(2)}) %collective-permute-start.23) | collective-permute-done | bytes 65568 | tf_op jit(solution)/shard_map/ppermute | solution.py:594
  182.3 5.5 %collective-permute-done.24 = f32[128,128]{1,0:T(8,128)S(1)} collective-permute-done((f32[128,128]{1,0:T(8,128)S(1)}, f32[128,128]{1,0:T(8,128)S(1)}, u32[]{:S(2)}, u32[]{:S(2)}) %collective-permute-start.24) | collective-permute-done | bytes 65568 | tf_op jit(solution)/shard_map/ppermute | solution.py:594
  187.8 4.3 %collective-permute-done.25 = f32[128,128]{1,0:T(8,128)S(1)} collective-permute-done((f32[128,128]{1,0:T(8,128)S(1)}, f32[128,128]{1,0:T(8,128)S(1)}, u32[]{:S(2)}, u32[]{:S(2)}) %collective-permute-start.25) | collective-permute-done | bytes 65568 | tf_op jit(solution)/shard_map/ppermute | solution.py:594
  192.1 1.9 collective-permute-start.26
  194.0 3.7 %collective-permute-done.26 = f32[128,128]{1,0:T(8,128)S(1)} collective-permute-done((f32[128,128]{1,0:T(8,128)S(1)}, f32[128,128]{1,0:T(8,128)S(1)}, u32[]{:S(2)}, u32[]{:S(2)}) %collective-permute-start.26) | collective-permute-done | bytes 65568 | tf_op jit(solution)/shard_map/ppermute | solution.py:594
  197.7 18.4 %turn.1 = f32[4096,128]{1,0:T(8,128)} custom-call(f32[4096,128]{1,0:T(8,128)S(1)} %bitcast.46, f32[128,128]{1,0:T(8,128)S(1)} %add_multiply_fusion.gram_ref), custom_call_target="tpu_custom_call" | custom-call | flops 268435456 | bytes 4194304 | tf_op jit(solution)/shard_map/turn/pallas_call | solution.py:506
  (108 shorter events, 17.7 us)
Async XLA Ops:
  0.0 29.8 %copy-start.12 = (f32[16,16,16]{2,1,0:T(8,128)S(1)}, f32[16,16,16]{2,1,0:T(8,128)}, u32[]{:S(2)}) copy-start(f32[16,16,16]{2,1,0:T(8,128)} %param.6) | copy-start | bytes 49156
  2.7 10.0 %collective-permute-start.1 = (f32[4,768]{1,0:T(4,128)S(1)}, f32[4,768]{1,0:T(4,128)S(1)}, u32[]{:S(2)}, u32[]{:S(2)}) collective-permute-start(f32[4,768]{1,0:T(4,128)S(1)} %maximum_maximum_fusion), channel_id=1, source_target_pairs={{1,0},{2,1},{3,2},{4,3},{5,4},{6,5},{7,6},{8,7},{9,8},{10,9},{11,1... | collective-permute-start | bytes 36872 | tf_op jit(solution)/shard_map/ppermute | solution.py:530
  11.4 9.4 %collective-permute-start = (f32[4,768]{1,0:T(4,128)S(1)}, f32[4,768]{1,0:T(4,128)S(1)}, u32[]{:S(2)}, u32[]{:S(2)}) collective-permute-start(f32[4,768]{1,0:T(4,128)S(1)} %maximum_maximum_fusion), channel_id=1, source_target_pairs={{0,1},{1,2},{2,3},{3,4},{4,5},{5,6},{6,7},{7,8},{8,9},{9,10},{10,1... | collective-permute-start | bytes 36872 | tf_op jit(solution)/shard_map/ppermute | solution.py:527
  11.4 71.8 %collective-permute-start.10 = (f32[16,256,128]{2,1,0:T(8,128)}, f32[16,256,128]{2,1,0:T(8,128)}, u32[]{:S(2)}, u32[]{:S(2)}) collective-permute-start(f32[16,256,128]{2,1,0:T(8,128)} %bitcast.35), channel_id=1, source_target_pairs={{0,64},{64,0},{1,65},{65,1},{2,66},{66,2},{3,67},{67,3},{4,68},{68... | collective-permute-start | bytes 6291464 | tf_op jit(solution)/shard_map/ppermute | solution.py:524
  20.8 9.2 %collective-permute-start.2 = (f32[3,4,768]{2,1,0:T(4,128)S(1)}, f32[3,4,768]{2,1,0:T(4,128)S(1)}, u32[]{:S(2)}, u32[]{:S(2)}) collective-permute-start(f32[3,4,768]{2,1,0:T(4,128)S(1)} %pad_maximum_fusion.2), channel_id=1, source_target_pairs={{0,64},{64,0},{1,65},{65,1},{2,66},{66,2},{3,67},{67,3},{4,68},{68... | collective-permute-start | bytes 110600 | tf_op jit(solution)/shard_map/ppermute | solution.py:524
  22.5 13.3 %copy-start.1 = (f32[16,16,16,128]{3,2,1,0:T(8,128)S(1)}, f32[16,16,16,128]{3,2,1,0:T(8,128)}, u32[]{:S(2)}) copy-start(f32[16,16,16,128]{3,2,1,0:T(8,128)} %param.5) | copy-start | bytes 6291460
  30.1 5.5 %collective-permute-start.4 = (f32[176,128]{1,0:T(8,128)S(1)}, f32[176,128]{1,0:T(8,128)S(1)}, u32[]{:S(2)}, u32[]{:S(2)}) collective-permute-start(f32[176,128]{1,0:T(8,128)S(1)} %pad_maximum_fusion.1), channel_id=1, source_target_pairs={{0,32},{32,0},{1,33},{33,1},{2,34},{34,2},{3,35},{35,3},{4,36},{36... | collective-permute-start | bytes 270344 | tf_op jit(solution)/shard_map/ppermute | solution.py:524
  31.3 58.0 %collective-permute-start.3 = (f32[16,192,128]{2,1,0:T(8,128)}, f32[16,192,128]{2,1,0:T(8,128)}, u32[]{:S(2)}, u32[]{:S(2)}) collective-permute-start(f32[16,192,128]{2,1,0:T(8,128)} %copy-done.9), channel_id=1, source_target_pairs={{0,32},{32,0},{1,33},{33,1},{2,34},{34,2},{3,35},{35,3},{4,36},{36... | collective-permute-start | bytes 4718600 | tf_op jit(solution)/shard_map/ppermute | solution.py:524
  35.7 21.5 %copy-start.11 = (f32[6,16,16,128]{3,2,1,0:T(8,128)S(1)}, f32[6,16,16,128]{3,2,1,0:T(8,128)}, u32[]{:S(2)}) copy-start(f32[6,16,16,128]{3,2,1,0:T(8,128)} %copy-done.10) | copy-start | bytes 2359300
  55.9 33.4 %copy-start.3 = (bf16[2,4096,128]{2,1,0:T(8,128)(2,1)}, bf16[2,4096,128]{2,1,0:T(8,128)(2,1)S(1)}, u32[]{:S(2)}) copy-start(bf16[2,4096,128]{2,1,0:T(8,128)(2,1)S(1)} %get-tuple-element.35) | copy-start | bytes 6291460
  55.9 1.3 collective-permute-start.5
  57.2 9.9 %collective-permute-start.6 = (f32[3,16,128]{2,1,0:T(8,128)S(1)}, f32[3,16,128]{2,1,0:T(8,128)S(1)}, u32[]{:S(2)}, u32[]{:S(2)}) collective-permute-start(f32[3,16,128]{2,1,0:T(8,128)S(1)} %get-tuple-element.39), channel_id=1, source_target_pairs={{0,1},{1,2},{2,3},{3,4},{4,5},{5,6},{6,7},{7,8},{8,9},{9,10},{10,1... | collective-permute-start | bytes 73736 | tf_op jit(solution)/shard_map/ppermute | solution.py:527
  57.3 25.8 %collective-permute-start.11 = (f32[6,16,16,128]{3,2,1,0:T(8,128)S(1)}, f32[6,16,16,128]{3,2,1,0:T(8,128)S(1)}, u32[]{:S(2)}, u32[]{:S(2)}) collective-permute-start(f32[6,16,16,128]{3,2,1,0:T(8,128)S(1)} %copy-done.11), channel_id=1, source_target_pairs={{0,1},{1,2},{2,3},{3,4},{4,5},{5,6},{6,7},{7,8},{8,9},{9,10},{10,1... | collective-permute-start | bytes 2359304 | tf_op jit(solution)/shard_map/ppermute | solution.py:527
  57.4 25.7 %collective-permute-start.12 = (f32[6,16,16,128]{3,2,1,0:T(8,128)S(1)}, f32[6,16,16,128]{3,2,1,0:T(8,128)S(1)}, u32[]{:S(2)}, u32[]{:S(2)}) collective-permute-start(f32[6,16,16,128]{3,2,1,0:T(8,128)S(1)} %get-tuple-element.30), channel_id=1, source_target_pairs={{1,0},{2,1},{3,2},{4,3},{5,4},{6,5},{7,6},{8,7},{9,8},{10,9},{11,1... | collective-permute-start | bytes 2359304 | tf_op jit(solution)/shard_map/ppermute | solution.py:530
  67.0 15.4 %collective-permute-start.7 = (f32[3,16,128]{2,1,0:T(8,128)S(1)}, f32[3,16,128]{2,1,0:T(8,128)S(1)}, u32[]{:S(2)}, u32[]{:S(2)}) collective-permute-start(f32[3,16,128]{2,1,0:T(8,128)S(1)} %get-tuple-element.40), channel_id=1, source_target_pairs={{1,0},{2,1},{3,2},{4,3},{5,4},{6,5},{7,6},{8,7},{9,8},{10,9},{11,1... | collective-permute-start | bytes 73736 | tf_op jit(solution)/shard_map/ppermute | solution.py:530
  99.0 39.8 %collective-permute-start.13 = (f32[16,256,128]{2,1,0:T(8,128)S(1)}, f32[16,256,128]{2,1,0:T(8,128)}, u32[]{:S(2)}, u32[]{:S(2)}) collective-permute-start(f32[16,256,128]{2,1,0:T(8,128)S(1)} %get-tuple-element.32.refs_0_), channel_id=1, source_target_pairs={{0,64},{64,0},{1,65},{65,1},{2,66},{66,2},{3,67},{67,3},{4,68},{68... | collective-permute-start | bytes 6291464 | tf_op jit(solution)/shard_map/ppermute | solution.py:524
  100.4 3.9 %collective-permute-start.8 = (f32[3,16,128]{2,1,0:T(8,128)S(1)}, f32[3,16,128]{2,1,0:T(8,128)S(1)}, u32[]{:S(2)}, u32[]{:S(2)}) collective-permute-start(f32[3,16,128]{2,1,0:T(8,128)S(1)} %pad_maximum_fusion.4), channel_id=1, source_target_pairs={{0,32},{32,0},{1,33},{33,1},{2,34},{34,2},{3,35},{35,3},{4,36},{36... | collective-permute-start | bytes 73736 | tf_op jit(solution)/shard_map/ppermute | solution.py:524
  104.4 9.0 %collective-permute-start.17 = (f32[16,128]{1,0:T(8,128)S(1)}, f32[16,128]{1,0:T(8,128)S(1)}, u32[]{:S(2)}, u32[]{:S(2)}) collective-permute-start(f32[16,128]{1,0:T(8,128)S(1)} %bitcast_multiply_fusion), channel_id=1, source_target_pairs={{1,0},{2,1},{3,2},{4,3},{5,4},{6,5},{7,6},{8,7},{9,8},{10,9},{11,1... | collective-permute-start | bytes 24584 | tf_op jit(solution)/shard_map/ppermute | solution.py:530
  112.0 9.5 %collective-permute-start.16 = (f32[16,128]{1,0:T(8,128)S(1)}, f32[16,128]{1,0:T(8,128)S(1)}, u32[]{:S(2)}, u32[]{:S(2)}) collective-permute-start(f32[16,128]{1,0:T(8,128)S(1)} %bitcast_multiply_fusion), channel_id=1, source_target_pairs={{0,1},{1,2},{2,3},{3,4},{4,5},{5,6},{6,7},{7,8},{8,9},{9,10},{10,1... | collective-permute-start | bytes 24584 | tf_op jit(solution)/shard_map/ppermute | solution.py:527
  121.5 9.5 %collective-permute-start.18 = (f32[16,128]{1,0:T(8,128)S(1)}, f32[16,128]{1,0:T(8,128)S(1)}, u32[]{:S(2)}, u32[]{:S(2)}) collective-permute-start(f32[16,128]{1,0:T(8,128)S(1)} %fusion), channel_id=1, source_target_pairs={{0,1},{1,2},{2,3},{3,4},{4,5},{5,6},{6,7},{7,8},{8,9},{9,10},{10,1... | collective-permute-start | bytes 24584 | tf_op jit(solution)/shard_map/ppermute | solution.py:527
  121.6 25.5 %collective-permute-start.9 = (f32[16,64,128]{2,1,0:T(8,128)}, f32[16,64,128]{2,1,0:T(8,128)S(1)}, u32[]{:S(2)}, u32[]{:S(2)}) collective-permute-start(f32[16,64,128]{2,1,0:T(8,128)} %get-tuple-element.27), channel_id=1, source_target_pairs={{0,32},{32,0},{1,33},{33,1},{2,34},{34,2},{3,35},{35,3},{4,36},{36... | collective-permute-start | bytes 1572872 | tf_op jit(solution)/shard_map/ppermute | solution.py:524
  122.7 16.1 %collective-permute-start.19 = (f32[16,128]{1,0:T(8,128)S(1)}, f32[16,128]{1,0:T(8,128)S(1)}, u32[]{:S(2)}, u32[]{:S(2)}) collective-permute-start(f32[16,128]{1,0:T(8,128)S(1)} %fusion), channel_id=1, source_target_pairs={{1,0},{2,1},{3,2},{4,3},{5,4},{6,5},{7,6},{8,7},{9,8},{10,9},{11,1... | collective-permute-start | bytes 24584 | tf_op jit(solution)/shard_map/ppermute | solution.py:530
  131.0 26.6 %collective-permute-start.14 = (f32[6,16,16,128]{3,2,1,0:T(8,128)S(1)}, f32[6,16,16,128]{3,2,1,0:T(8,128)S(1)}, u32[]{:S(2)}, u32[]{:S(2)}) collective-permute-start(f32[6,16,16,128]{3,2,1,0:T(8,128)S(1)} %get-tuple-element.33), channel_id=1, source_target_pairs={{0,1},{1,2},{2,3},{3,4},{4,5},{5,6},{6,7},{7,8},{8,9},{9,10},{10,1... | collective-permute-start | bytes 2359304 | tf_op jit(solution)/shard_map/ppermute | solution.py:527
  131.0 26.6 %collective-permute-start.15 = (f32[6,16,16,128]{3,2,1,0:T(8,128)S(1)}, f32[6,16,16,128]{3,2,1,0:T(8,128)S(1)}, u32[]{:S(2)}, u32[]{:S(2)}) collective-permute-start(f32[6,16,16,128]{3,2,1,0:T(8,128)S(1)} %get-tuple-element.34), channel_id=1, source_target_pairs={{1,0},{2,1},{3,2},{4,3},{5,4},{6,5},{7,6},{8,7},{9,8},{10,9},{11,1... | collective-permute-start | bytes 2359304 | tf_op jit(solution)/shard_map/ppermute | solution.py:530
  148.7 9.0 %copy-start.4 = (bf16[2,4096,128]{2,1,0:T(8,128)(2,1)S(1)}, bf16[2,4096,128]{2,1,0:T(8,128)(2,1)}, u32[]{:S(2)}) copy-start(bf16[2,4096,128]{2,1,0:T(8,128)(2,1)} %copy-done.3) | copy-start | bytes 6291460
  166.5 1.3 collective-permute-start.20
  167.9 4.3 %collective-permute-start.21 = (f32[128,128]{1,0:T(8,128)S(1)}, f32[128,128]{1,0:T(8,128)S(1)}, u32[]{:S(2)}, u32[]{:S(2)}) collective-permute-start(f32[128,128]{1,0:T(8,128)S(1)} %add.55), channel_id=1, source_target_pairs={{0,32},{1,33},{2,34},{3,35},{4,36},{5,37},{6,38},{7,39},{8,40},{9,... | collective-permute-start | bytes 196616 | tf_op jit(solution)/shard_map/ppermute | solution.py:594
  172.2 5.6 %collective-permute-start.22 = (f32[128,128]{1,0:T(8,128)S(1)}, f32[128,128]{1,0:T(8,128)S(1)}, u32[]{:S(2)}, u32[]{:S(2)}) collective-permute-start(f32[128,128]{1,0:T(8,128)S(1)} %add.56), channel_id=1, source_target_pairs={{0,36},{1,37},{2,38},{3,39},{4,32},{5,33},{6,34},{7,35},{8,44},{9,... | collective-permute-start | bytes 196616 | tf_op jit(solution)/shard_map/ppermute | solution.py:594
  177.8 4.3 %collective-permute-start.23 = (f32[128,128]{1,0:T(8,128)S(1)}, f32[128,128]{1,0:T(8,128)S(1)}, u32[]{:S(2)}, u32[]{:S(2)}) collective-permute-start(f32[128,128]{1,0:T(8,128)S(1)} %add.57), channel_id=1, source_target_pairs={{0,1},{1,0},{2,3},{3,2},{4,5},{5,4},{6,7},{7,6},{8,9},{9,8},{10,11... | collective-permute-start | bytes 196616 | tf_op jit(solution)/shard_map/ppermute | solution.py:594
  182.2 5.6 %collective-permute-start.24 = (f32[128,128]{1,0:T(8,128)S(1)}, f32[128,128]{1,0:T(8,128)S(1)}, u32[]{:S(2)}, u32[]{:S(2)}) collective-permute-start(f32[128,128]{1,0:T(8,128)S(1)} %add.58), channel_id=1, source_target_pairs={{0,3},{1,2},{2,1},{3,0},{4,7},{5,6},{6,5},{7,4},{8,11},{9,10},{10,... | collective-permute-start | bytes 196616 | tf_op jit(solution)/shard_map/ppermute | solution.py:594
  187.7 4.3 %collective-permute-start.25 = (f32[128,128]{1,0:T(8,128)S(1)}, f32[128,128]{1,0:T(8,128)S(1)}, u32[]{:S(2)}, u32[]{:S(2)}) collective-permute-start(f32[128,128]{1,0:T(8,128)S(1)} %add.59), channel_id=1, source_target_pairs={{0,8},{1,9},{2,10},{3,11},{4,12},{5,13},{6,14},{7,15},{8,0},{9,1},... | collective-permute-start | bytes 196616 | tf_op jit(solution)/shard_map/ppermute | solution.py:594
  192.1 5.6 %collective-permute-start.26 = (f32[128,128]{1,0:T(8,128)S(1)}, f32[128,128]{1,0:T(8,128)S(1)}, u32[]{:S(2)}, u32[]{:S(2)}) collective-permute-start(f32[128,128]{1,0:T(8,128)S(1)} %add.60), channel_id=1, source_target_pairs={{0,24},{1,25},{2,26},{3,27},{4,28},{5,29},{6,30},{7,31},{8,16},{9,... | collective-permute-start | bytes 196616 | tf_op jit(solution)/shard_map/ppermute | solution.py:594
  (8 other events, 16.2 us)

commit v3 on v2

v3 whole, which is shorter than its diff:
```python
import math

import jax
import jax.numpy as jnp
from jax import lax
from jax.experimental import pallas as pl
from jax.experimental.pallas import tpu as pltpu
from jax.sharding import PartitionSpec as P

AXES = ("gx", "gy", "gzs")
H = 6
C = 16
ROWS = C * C
CELLS = C * C * C
S = 128
W = 9
R = 4
NEAR = 48
TAPS = W * W * W
F32 = jnp.float32
BF16 = jnp.bfloat16

grid_step = 0.6
filter_centre = 36.0
filter_half = 26.0


def weights():
    taps = []
    for k in range(1, 7):
        top = 2.0 * (-1) ** (k + 1) * math.factorial(6) ** 2
        under = k * k * math.factorial(6 - k) * math.factorial(6 + k)
        taps.append(top / under)
    scale = -0.5 / (grid_step * grid_step)
    off = [scale * t / filter_half for t in taps]
    diagonal = 3.0 * scale * (-2.0 * sum(taps))
    return off, diagonal


OFF, DIAGONAL = weights()


def params(mib):
    return pltpu.CompilerParams(vmem_limit_bytes=mib * 1024 * 1024)


def cost(flops, nbytes):
    return pl.CostEstimate(flops=flops, bytes_accessed=nbytes, transcendentals=0)


def sds(shape, dtype=F32):
    return jax.ShapeDtypeStruct(shape, dtype)


def split(value):
    high = value.astype(BF16)
    low = (value - high.astype(F32)).astype(BF16)
    return high, low


def mm(a, b):
    return jnp.dot(a, b, preferred_element_type=F32)


def tap_sum(at, index):
    total = None
    for k in range(1, 7):
        term = OFF[k - 1] * (at(index + k) + at(index - k))
        total = term if total is None else total + term
    return total


B = 4
STEPS = C // B
CUT = 12


def stride_rows(z):
    return pl.ds(z, C, stride=C)


def plane_spec(rows=ROWS):
    return pl.BlockSpec((B, rows, S), lambda i: (i, 0, 0))


def halo_spec():
    return pl.BlockSpec((H, B, C, S), lambda i: (0, i, 0, 0))


def part_spec(part):
    return pl.BlockSpec((1, B, ROWS, S), lambda i: (part, i, 0, 0))


def whole(rows=S):
    return pl.BlockSpec((rows, S), lambda i: (0, 0))


def edge_specs():
    return [
        pl.BlockSpec((B, 192, S), lambda i: (jnp.minimum(i, CUT // B - 1), 0, 0)),
        pl.BlockSpec((B, 192, S), lambda i: (jnp.maximum(i - CUT // B, 0), 0, 0)),
    ]


def per_plane(body):
    def step(p, _):
        body(p)
        return 0

    lax.fori_loop(0, B, step, 0)


FULL = sds((C, ROWS, S))
HALO = sds((H, C, C, S))
EDGES = [sds((CUT, 192, S)), sds((C - CUT, 192, S))]


def halves(y, half):
    return slice(y * C + half * 8, y * C + half * 8 + 8)


def pack_kernel(s_ref, one_ref, two_ref, mid_ref, head_ref, tail_ref):
    step = pl.program_id(0)

    def edges(out_ref):
        out_ref[:, 0:96, :] = s_ref[:, 0:96, :]
        out_ref[:, 96:192, :] = s_ref[:, 160:256, :]

    @pl.when(step < CUT // B)
    def _():
        edges(one_ref)

    @pl.when(step >= CUT // B)
    def _():
        edges(two_ref)

    mid_ref[...] = s_ref[:, 96:160, :]
    for p in range(B):
        for z in range(H):
            head_ref[z, p] = s_ref[p, stride_rows(z), :]
            tail_ref[z, p] = s_ref[p, stride_rows(C - H + z), :]


def pack(s):
    return pl.pallas_call(
        pack_kernel,
        grid=(STEPS,),
        in_specs=[plane_spec()],
        out_specs=edge_specs() + [plane_spec(64), halo_spec(), halo_spec()],
        out_shape=EDGES + [sds((C, 64, S)), HALO, HALO],
        compiler_params=params(12),
        cost_estimate=cost(1 << 33, 6 << 20),
        name="pack",
    )(s)


def along_x(s_ref, mate_ref, out_ref, add):
    def column(block, _):
        rows = pl.ds(pl.multiple_of(block * 8, 8), 8)
        ring = [mate_ref[C - H + i, rows, :] for i in range(H)]
        ring += [s_ref[x, rows, :] for x in range(C)]
        ring += [mate_ref[i, rows, :] for i in range(H)]
        for x in range(C):
            value = tap_sum(lambda i: ring[H + i], x)
            if add:
                value = value + out_ref[x, rows, :]
            out_ref[x, rows, :] = value
        return 0

    lax.fori_loop(0, ROWS // 8, column, 0)


def z_taps(ext_ref, y):
    return tap_sum(lambda k: ext_ref[y * 32 + 8 + k : y * 32 + 24 + k, :], 0)


def side_x_kernel(s_ref, mate_ref, out_ref):
    along_x(s_ref, mate_ref, out_ref, False)


def side_x(s, mate):
    return pl.pallas_call(
        side_x_kernel,
        out_shape=FULL,
        compiler_params=params(12),
        cost_estimate=cost(1 << 24, 6 << 20),
        name="side_x",
    )(s, mate)


def side_z_kernel(s_ref, part_ref, low_ref, high_ref, out_ref, ext_ref):
    def plane(x, _):
        for y in range(C):
            ext_ref[y * 32 + 8 : y * 32 + 24, :] = s_ref[x, y * C : (y + 1) * C, :]
        for z in range(H):
            ext_ref[pl.ds(2 + z, C, stride=32), :] = low_ref[z, x]
            ext_ref[pl.ds(24 + z, C, stride=32), :] = high_ref[z, x]
        for y in range(C):
            rows = slice(y * C, (y + 1) * C)
            out_ref[x, rows, :] = part_ref[x, rows, :] + z_taps(ext_ref, y)
        return 0

    lax.fori_loop(0, C, plane, 0)


def side_z(s, part, low, high):
    return pl.pallas_call(
        side_z_kernel,
        out_shape=FULL,
        scratch_shapes=[pltpu.VMEM((C * 32, S), F32)],
        compiler_params=params(14),
        cost_estimate=cost(1 << 24, 8 << 20),
        name="side_z",
    )(s, part, low, high)


def side_again_kernel(s_ref, mate_ref, out_ref, ext_ref):
    for y in range(C):
        ext_ref[y * 32 : y * 32 + 8, :] = jnp.zeros((8, S), F32)
        ext_ref[y * 32 + 24 : y * 32 + 32, :] = jnp.zeros((8, S), F32)

    def plane(x, _):
        for y in range(C):
            ext_ref[y * 32 + 8 : y * 32 + 24, :] = s_ref[x, y * C : (y + 1) * C, :]
        for y in range(C):
            out_ref[x, y * C : (y + 1) * C, :] = z_taps(ext_ref, y)
        return 0

    lax.fori_loop(0, C, plane, 0)
    along_x(s_ref, mate_ref, out_ref, True)


def side_again(s, mate):
    return pl.pallas_call(
        side_again_kernel,
        out_shape=FULL,
        scratch_shapes=[pltpu.VMEM((C * 32, S), F32)],
        compiler_params=params(12),
        cost_estimate=cost(1 << 25, 6 << 20),
        name="side_again",
    )(s, mate)


def tap_weight(distance):
    value = jnp.zeros(distance.shape, F32)
    for k in range(1, 7):
        value = jnp.where(distance == k, OFF[k - 1], value)
    return value


def ring_tables(coordinate):
    masks, factors = [], []
    for t in range(W):
        away = (coordinate - t) & 31
        masks.append(away == 0)
        factors.append(tap_weight(jnp.minimum(away, 32 - away)))
    return masks, factors


def spread_rows(pot_ref, vb_ref):
    def spread(row, _):
        line = (pot_ref[pl.ds(row, 1), :] + (DIAGONAL - filter_centre)) * (1.0 / filter_half)
        start = pl.multiple_of(row * 128, 128)
        vb_ref[pl.ds(start, 128), :] = jnp.broadcast_to(line, (128, 128)).T
        return 0

    lax.fori_loop(0, CELLS // 128, spread, 0)


def spread(pot):
    return pl.pallas_call(
        spread_rows,
        out_shape=sds((CELLS, S)),
        compiler_params=params(8),
        cost_estimate=cost(1 << 20, 2 << 20),
        name="spread",
    )(pot)


def prep_kernel(near_ref, corner_ref, vb_ref, s_ref, gg_ref, coef_ref, table_ref, a1_ref, a1z_ref, a2_ref, a2s_ref):
    for block in range(6):
        columns = slice(block * 128, block * 128 + 128)
        table_ref[columns, :] = near_ref[:, columns].T

    shape = (8, 128)
    sub = lax.broadcasted_iota(jnp.int32, shape, 0)
    lane = lax.broadcasted_iota(jnp.int32, shape, 1)
    first_lanes = lane < 64
    sites = [jnp.broadcast_to(table_ref[TAPS + d : TAPS + d + 1, :], shape).astype(jnp.int32) for d in range(3)]
    px = sites[0] - corner_ref[0]
    py = sites[1] - corner_ref[1]
    pz = (sites[2] & 15) + (((lane & 63) >> 4) - 1) * C
    zero = jnp.zeros(shape, F32)

    dz = sub + (lane >> 6) * 8 - pz + R
    z_masks = [dz == t for t in range(W)]
    z_factors = [tap_weight(jnp.abs(dz - t)) for t in range(W)]

    def place_z(ij, _):
        acc = zero
        along = zero
        for t in range(W):
            row = jnp.broadcast_to(table_ref[pl.ds(ij * W + t, 1), :], shape)
            acc = jnp.where(z_masks[t], row, acc)
            along = along + z_factors[t] * row
        a1_ref[ij] = acc
        a1z_ref[ij] = along
        return 0

    lax.fori_loop(0, W * W, place_z, 0)

    def place_y(y, _):
        masks, factors = ring_tables(y - py + R)
        for i in range(W):
            acc = zero
            along = zero
            moved = zero
            for t in range(W):
                value = a1_ref[i * W + t]
                acc = jnp.where(masks[t], value, acc)
                along = along + factors[t] * value
                moved = jnp.where(masks[t], a1z_ref[i * W + t], moved)
            a2_ref[i, y] = acc
            a2s_ref[i, y] = along + moved
        return 0

    lax.fori_loop(0, C, place_y, 0)

    def place_x(x, _):
        masks, factors = ring_tables(x - px + R)

        def per_y(y, _):
            row = pl.multiple_of(x * ROWS + y * C, C)
            acc = zero
            along = zero
            moved = zero
            for t in range(W):
                value = a2_ref[t, y]
                acc = jnp.where(masks[t], value, acc)
                along = along + factors[t] * value
                moved = jnp.where(masks[t], a2s_ref[t, y], moved)
            v = vb_ref[pl.ds(row, C), :]
            moved = along + moved + jnp.where(first_lanes, v[:8], v[8:]) * acc
            lower = jnp.where(first_lanes, acc, pltpu.roll(moved, 64, 1))
            upper = jnp.where(first_lanes, pltpu.roll(acc, 64, 1), moved)
            high, low = split(jnp.concatenate([lower, upper], axis=0))
            gg_ref[0, pl.ds(row, C), :] = high
            gg_ref[1, pl.ds(row, C), :] = low
            return 0

        lax.fori_loop(0, C, per_y, 0)
        return 0

    lax.fori_loop(0, C, place_x, 0)

    coef_ref[...] = jnp.zeros((3, NEAR, S), F32)

    def contract(x, _):
        rows = pl.ds(pl.multiple_of(x * 2 * ROWS, ROWS), 2 * ROWS)
        g_high, g_low = gg_ref[0, rows, :], gg_ref[1, rows, :]
        t_high, t_low = g_high.T, g_low.T
        high, low = split(s_ref[rows, :])
        got = mm(t_high, high) + (mm(t_high, low) + mm(t_low, high))
        t_high, t_low = t_high[:NEAR], t_low[:NEAR]
        pair = mm(t_high, g_high) + (mm(t_high, g_low) + mm(t_low, g_high))
        for slab in range(3):
            rows = slice(slab * C, slab * C + C)
            coef_ref[slab, 0:16] += got[rows]
            coef_ref[slab, 16:32] += got[64 + slab * C : 80 + slab * C]
            coef_ref[slab, 32:48] += pair[rows]
        return 0

    lax.fori_loop(0, C // 2, contract, 0)


def prep(near, corner, vb, s):
    vmem = pl.BlockSpec(memory_space=pltpu.VMEM)
    return pl.pallas_call(
        prep_kernel,
        in_specs=[vmem, pl.BlockSpec(memory_space=pltpu.SMEM), vmem, vmem],
        out_shape=[sds((2, CELLS, S), BF16), sds((3, NEAR, S))],
        scratch_shapes=[
            pltpu.VMEM((768, 128), F32),
            pltpu.VMEM((W * W, 8, 128), F32),
            pltpu.VMEM((W * W, 8, 128), F32),
            pltpu.VMEM((W, C, 8, 128), F32),
            pltpu.VMEM((W, C, 8, 128), F32),
        ],
        compiler_params=params(16),
        cost_estimate=cost(1 << 27, 10 << 20),
        name="prep",
    )(near, corner, vb, s.reshape(CELLS, S))


def merge_kernel(part_ref, below_ref, above_ref, out_ref):
    out_ref[0:32, :] = part_ref[1, 0:32, :] + below_ref[0:32, :] + above_ref[0:32, :]
    lane = lax.broadcasted_iota(jnp.int32, (16, 128), 1)
    below = jnp.where(lane < 32, pltpu.roll(below_ref[32:48, :], 112, 1), 0.0)
    above = jnp.where((lane >= 16) & (lane < 48), pltpu.roll(above_ref[32:48, :], 16, 1), 0.0)
    out_ref[32:48, :] = jnp.where(lane < 48, part_ref[1, 32:48, :], 0.0) + below + above


def merge(part, below, above):
    return pl.pallas_call(merge_kernel, out_shape=sds((NEAR, S)), compiler_params=params(4), name="merge")(part, below, above)


def weigh_kernel(own_ref, other_ref, energy_ref, one_ref, rest_ref):
    total = own_ref[...] + other_ref[...]
    one_ref[...] = total[0:16] * energy_ref[...]
    rest_ref[...] = total[16:48]


def weigh(own, other, energy):
    return pl.pallas_call(
        weigh_kernel, out_shape=[sds((16, S)), sds((32, S))], compiler_params=params(4), name="weigh"
    )(own, other, energy)


def again_kernel(rest_ref, below_ref, one_ref, above_ref, energy_ref, two_ref):
    near = jnp.concatenate([below_ref[...], one_ref[...], above_ref[...], jnp.zeros((S - NEAR, S), F32)])
    two_ref[...] = (rest_ref[0:16, :] + exact(rest_ref[16:32, :], near)) * energy_ref[...]


def again(rest, below, one, above, energy):
    return pl.pallas_call(again_kernel, out_shape=sds((16, S)), compiler_params=params(4), name="again")(
        rest, below, one, above, energy
    )


def first_kernel(s_ref, side_ref, edge_one_ref, edge_two_ref, vb_ref, q_ref, mix_ref, head_ref, tail_ref):
    def planes(edge_ref):
        def plane(p):
            for half in range(2):
                ring = {y: s_ref[p, halves(y, half), :] for y in range(C)}
                for y in range(H):
                    ring[C + y] = edge_ref[p, halves(y, half), :]
                    ring[y - H] = edge_ref[p, halves(H + y, half), :]
                for y in range(C):
                    rows = halves(y, half)
                    dy = tap_sum(lambda i: ring[i], y)
                    q = dy + vb_ref[p, rows, :] * ring[y]
                    q_ref[p, rows, :] = q
                    mix_ref[p, rows, :] = side_ref[p, rows, :] + q + dy
            for z in range(H):
                head_ref[z, p] = mix_ref[p, stride_rows(z), :]
                tail_ref[z, p] = mix_ref[p, stride_rows(C - H + z), :]

        per_plane(plane)

    step = pl.program_id(0)

    @pl.when(step < CUT // B)
    def _():
        planes(edge_one_ref)

    @pl.when(step >= CUT // B)
    def _():
        planes(edge_two_ref)


def make_first(s, side_part, edges, vb):
    return pl.pallas_call(
        first_kernel,
        grid=(STEPS,),
        in_specs=[plane_spec(), plane_spec()] + edge_specs() + [plane_spec()],
        out_specs=[plane_spec(), plane_spec(), halo_spec(), halo_spec()],
        out_shape=[FULL, FULL, HALO, HALO],
        compiler_params=params(16),
        cost_estimate=cost(1 << 24, 14 << 20),
        name="first",
    )(s, side_part, *edges, vb)


def base_kernel(s_ref, edge_one_ref, edge_two_ref, mid_ref, vb_ref, vb_mate_ref, q_ref, side_ref, part_ref, out_ref):
    def planes(edge_ref):
        def plane(p):
            for half in range(2):

                def other(y, half=half):
                    if y < H:
                        return edge_ref[p, halves(y, half), :]
                    if y < C - H:
                        return mid_ref[p, halves(y - H, half), :]
                    return edge_ref[p, halves(y - 4, half), :]

                ring = [s_ref[p, halves(y, half), :] for y in range(C)] + [other(y) for y in range(C)]
                q = {y: q_ref[p, halves(y, half), :] for y in range(C)}
                for y in list(range(H)) + list(range(C - H, C)):
                    v = vb_mate_ref[p, halves(y, half), :]
                    q[C + y] = tap_sum(lambda i: ring[i % 32], C + y) + v * ring[C + y]
                for y in range(C):
                    rows = halves(y, half)
                    total = tap_sum(lambda i: q[i % 32], y)
                    total = total + vb_ref[p, rows, :] * (side_ref[p, rows, :] + q[y])
                    out_ref[p, rows, :] = 2.0 * (total + part_ref[p, rows, :]) - ring[y]

        per_plane(plane)

    step = pl.program_id(0)

    @pl.when(step < CUT // B)
    def _():
        planes(edge_one_ref)

    @pl.when(step >= CUT // B)
    def _():
        planes(edge_two_ref)


def make_base(s, edges, mid, vb, vb_mate, q, side_part, part):
    return pl.pallas_call(
        base_kernel,
        grid=(STEPS,),
        in_specs=[plane_spec()] + edge_specs() + [plane_spec(64)] + [plane_spec()] * 5,
        out_specs=plane_spec(),
        out_shape=FULL,
        compiler_params=params(16),
        cost_estimate=cost(1 << 25, 16 << 20),
        name="base",
    )(s, *edges, mid, vb, vb_mate, q, side_part, part)


def second_kernel(base_ref, low_ref, high_ref, gg_high_ref, gg_low_ref, *rest):
    weighted = rest[:6]
    second_ref, gram_ref, cross_ref, w_ref = rest[6:]
    step = pl.program_id(0)

    @pl.when(step == 0)
    def _():
        gram_ref[...] = jnp.zeros((S, S), F32)
        cross_ref[...] = jnp.zeros((S, S), F32)
        w_ref[...] = jnp.zeros((S, S), F32)
        for j in range(3):
            w_ref[j * C : j * C + C, :] = 2.0 * weighted[j][...]
            w_ref[64 + j * C : 80 + j * C, :] = 2.0 * weighted[3 + j][...]

    w_high, w_low = split(w_ref[...])

    def plane(p):
        g_high, g_low = gg_high_ref[0, p], gg_low_ref[0, p]
        second_ref[p] = base_ref[p] + (mm(g_high, w_high) + (mm(g_high, w_low) + mm(g_low, w_high)))
        low = [low_ref[j, p] for j in range(H)]
        high = [high_ref[j, p] for j in range(H)]
        for z in range(H):
            add = sum((2.0 * OFF[k - 1]) * low[z - k + H] for k in range(z + 1, H + 1))
            second_ref[p, stride_rows(z), :] += add
            add = sum((2.0 * OFF[H + j - z - 1]) * high[j] for j in range(z + 1))
            second_ref[p, stride_rows(C - H + z), :] += add
        s_high, s_low = split(second_ref[p])
        turned = s_high.T
        gram_ref[...] += mm(turned, s_high)
        cross_ref[...] += mm(turned, s_low)

    per_plane(plane)

    @pl.when(step == STEPS - 1)
    def _():
        cross = cross_ref[...]
        gram_ref[...] += cross + cross.T


def make_second(base, low, high, gg, weighted):
    return pl.pallas_call(
        second_kernel,
        grid=(STEPS,),
        in_specs=[plane_spec(), halo_spec(), halo_spec(), part_spec(0), part_spec(1)] + [whole(C)] * 6,
        out_specs=[plane_spec(), whole()],
        out_shape=[FULL, sds((S, S))],
        scratch_shapes=[pltpu.VMEM((S, S), F32), pltpu.VMEM((S, S), F32)],
        compiler_params=params(16),
        cost_estimate=cost(1 << 27, 8 << 20),
        name="second",
    )(base, low, high, gg, gg, *weighted)


def exact(a, b):
    return jnp.dot(a, b, precision=lax.Precision.HIGHEST, preferred_element_type=F32)


def inverse_factor(gram_ref, a_ref, x_ref, state_ref):
    row = lax.broadcasted_iota(jnp.int32, (S, S), 0)
    column = lax.broadcasted_iota(jnp.int32, (S, S), 1)
    unit = jnp.where(row == column, 1.0, 0.0)
    gram = gram_ref[...]
    diagonal = jnp.where(row == column, gram, 0.0)
    down = lax.rsqrt(jnp.sum(diagonal, axis=1, keepdims=True))
    across = lax.rsqrt(jnp.sum(diagonal, axis=0, keepdims=True))
    a_ref[...] = gram * down * across
    x_ref[...] = unit

    def residual():
        x = x_ref[...]
        return unit - exact(exact(x, a_ref[...]), x.T)

    def size(e):
        return jnp.sum(e * e)

    def improve(e):
        lower = jnp.where(row > column, e, jnp.where(row == column, 0.5 * e, 0.0))
        x_ref[...] += exact(lower, x_ref[...])

    state_ref[0] = 0
    start = unit - a_ref[...]
    start_size = size(start)

    @pl.when(start_size < 0.16)
    def _():
        improve(start)
        state_ref[0] = jnp.where(start_size < 1e-6, 2, 1)

    for _ in range(5):

        @pl.when(state_ref[0] == 1)
        def _():
            e = residual()
            e_size = size(e)
            improve(e)
            state_ref[0] = jnp.where(e_size < 1e-6, 2, 1)

    @pl.when(state_ref[0] != 2)
    def _():
        x_ref[...] = unit
        lanes = lax.broadcasted_iota(jnp.int32, (1, S), 1)

        def step(j, _):
            line = a_ref[pl.ds(j, 1), :]
            scale = lax.rsqrt(jnp.sum(jnp.where(lanes == j, line, 0.0), axis=1, keepdims=True))
            a = a_ref[...]
            factor = jnp.sum(jnp.where(column == j, a, 0.0), axis=1, keepdims=True) * scale
            factor = jnp.where(row[:, :1] > j, factor, 0.0)
            x_line = x_ref[pl.ds(j, 1), :] * scale
            a_ref[...] = a - factor * (line * scale)
            x_ref[...] = jnp.where(row == j, x_line, x_ref[...] - factor * x_line)
            return 0

        lax.fori_loop(0, S, step, 0)

    x_ref[...] = x_ref[...] * across


def turn_kernel(second_ref, gram_ref, out_ref, a_ref, x_ref, i_high_ref, i_low_ref, state_ref):
    @pl.when(pl.program_id(0) == 0)
    def _():
        inverse_factor(gram_ref, a_ref, x_ref, state_ref)
        i_high, i_low = split(x_ref[...].T)
        i_high_ref[...] = i_high
        i_low_ref[...] = i_low

    i_high, i_low = i_high_ref[...], i_low_ref[...]

    def plane(p):
        high, low = split(second_ref[p])
        out_ref[p] = mm(high, i_high) + (mm(high, i_low) + mm(low, i_high))

    per_plane(plane)


def turn(second, gram):
    return pl.pallas_call(
        turn_kernel,
        grid=(STEPS,),
        in_specs=[plane_spec(), whole()],
        out_specs=plane_spec(),
        out_shape=FULL,
        scratch_shapes=[pltpu.VMEM((S, S), F32)] * 2 + [pltpu.VMEM((S, S), BF16)] * 2 + [pltpu.SMEM((1,), jnp.int32)],
        compiler_params=params(16),
        cost_estimate=cost(1 << 28, 4 << 20),
        name="turn",
    )(second, gram)


def per_device(states, potential, atom_sites, projectors, energies):
    gx, gy = lax.axis_index("gx"), lax.axis_index("gy")
    depth = lax.axis_size("gzs")
    count = 4 * depth
    barrier = lax.optimization_barrier

    def send(value, flip=0, move=0):
        def target(d):
            return (d // depth * depth ^ flip) + (d + move) % depth

        return lax.ppermute(value, AXES, [(d, target(d)) for d in range(count)])

    over_x, over_y = 2 * depth, depth
    s = states.reshape(C, ROWS, S)
    pot = potential.reshape(32, 128)

    atoms = jnp.concatenate(
        [projectors.reshape(4, TAPS), atom_sites.astype(F32), energies[:, None], jnp.zeros((4, 768 - TAPS - 4), F32)],
        axis=1,
    )
    parcel = jnp.concatenate([atoms.reshape(24, 128), pot])
    parcel_mate = send(parcel, over_y)
    below, above = send(atoms, 0, 1), send(atoms, 0, -1)
    below_mate, above_mate = send(atoms, over_y, 1), send(atoms, over_y, -1)
    packed = pack(barrier((s, atoms))[0])
    edges, mid, head, tail = packed[:2], packed[2], packed[3], packed[4]
    edge_one = send(edges[0], over_y)
    low, high = send(tail, 0, 1), send(head, 0, -1)
    mine = jnp.stack([below, atoms, above])
    other = jnp.stack([below_mate, parcel_mate[:24].reshape(4, 768), above_mate])
    column = jnp.where(gy == 0, jnp.concatenate([mine, other], 1), jnp.concatenate([other, mine], 1))
    column_mate = send(column, over_x)
    s_mate, _ = barrier((s, column))
    mate = send(s_mate, over_x)
    near = jnp.where(
        gx == 0, jnp.concatenate([column, column_mate], 1), jnp.concatenate([column_mate, column], 1)
    ).reshape(NEAR, 768)
    gap = jnp.zeros((16, 768), F32)
    energy = near[16:32, TAPS + 3 : TAPS + 4] * (1.0 / filter_half)
    corner = jnp.stack([gx * C, gy * C]).astype(jnp.int32)
    vb = spread(pot)
    beside = side_x(s, mate)
    near, beside = barrier((jnp.concatenate([near, gap, near, gap]), beside))
    gg, part = prep(near, corner, vb, s)

    part = part + send(part, over_x)
    own = merge(part, send(part[2], 0, 1), send(part[0], 0, -1))
    edge_two, own = barrier((edges[1], own))
    own_mate = send(own, over_y)
    edge_two = send(edge_two, over_y)
    one, rest = weigh(own, own_mate, energy)
    mid, one = barrier((mid, one))
    mid = send(mid, over_y)
    ones = [send(one, 0, 1), one, send(one, 0, -1)]

    vb = vb.reshape(C, ROWS, S)
    vb_mate = spread(parcel_mate[24:]).reshape(C, ROWS, S)
    side_part = side_z(s, beside, low, high)
    edge_two, ones = barrier((edge_two, ones))
    edges = [edge_one, edge_two]
    two = again(rest, *ones, energy)
    twos = [send(two, 0, 1), two, send(two, 0, -1)]
    q, mix, head, tail = make_first(s, side_part, edges, vb)
    low, high = send(tail, 0, 1), send(head, 0, -1)
    mate = send(mix, over_x)
    part = side_again(mix, mate)
    base = make_base(s, edges, mid, vb, vb_mate, q, side_part, part)
    second, gram = make_second(base, low, high, gg.reshape(2, C, ROWS, S), twos + ones)

    for flip in (64, 32, 36, 1, 3, 8, 24):
        gram = gram + lax.ppermute(gram, AXES, [(d, d ^ flip) for d in range(count)])
    gram = gram * (1.0 / (CELLS * count))
    return turn(second, gram).reshape(C, C, C, S)


def solution(mesh):
    return jax.shard_map(
        per_device,
        mesh=mesh,
        in_specs=(
            P("gx", "gy", "gzs", None),
            P("gx", "gy", "gzs"),
            P(("gx", "gy", "gzs"), None),
            P(("gx", "gy", "gzs"), None, None, None),
            P(("gx", "gy", "gzs")),
        ),
        out_specs=P("gx", "gy", "gzs", None),
        check_vma=False,
    )
```

time: 217 us -> 199 us (0.917)
  waiting for transfers between devices: 73.8 us -> 45.1 us
  starting transfers between devices: 47.8 us -> 65.8 us
  local copies, waits for them, and re-layouts: 11.3 us -> 6.09 us
    ppermute x27 -> x30, waiting for transfers between devices: 73.8 us -> 45.1 us  [the longest x23 23.8 us: send(): return lax.ppermute(value, AXES, [(d, target(d)) for d in range(count)])]
    ppermute x27 -> x30, starting transfers between devices: 47.8 us -> 65.8 us  [the longest x23 54.9 us: send(): return lax.ppermute(value, AXES, [(d, target(d)) for d in range(count)])]
    pallas_call x7 -> x13, Pallas kernels: 60.6 us -> 51.3 us  [the longest x1 18.4 us: turn(): pl.pallas_call(turn_kernel, grid=(STEPS,), in_specs=[plane_spec(), whole(...]
    pallas_call x1, Pallas kernels: 20.1 us -> 28.9 us  [prep(): pl.pallas_call(prep_kernel, in_specs=[vmem, pl.BlockSpec(memory_space=plt...]
    unnamed x33 -> x13, local copies, waits for them, and re-layouts: 10.4 us -> 4.07 us
  transfers between devices with their start and end apart: 27 -> 30, of which waited for: 18 -> 14; matrix products, arithmetic and copies ran while one was open for 1% -> 0% of each run, Pallas kernels for 21% -> 26%
where the time goes in v3:
time: 199 us
  Pallas kernels  80.2 us (40%)
  starting transfers between devices  65.8 us (33%)
  waiting for transfers between devices  45.1 us (23%)
  local copies, waits for them, and re-layouts  6.09 us (3%)
    ppermute x23, starting transfers between devices, send(): return lax.ppermute(value, AXES, [(d, target(d)) for d in range(count)])  54.9 us
    pallas_call x1, Pallas kernels, prep(): pl.pallas_call(prep_kernel, in_specs=[vmem, pl.BlockSpec(memory_space=plt...  28.9 us
    ppermute x23, waiting for transfers between devices, send(): return lax.ppermute(value, AXES, [(d, target(d)) for d in range(count)])  23.8 us
    ppermute x7, waiting for transfers between devices, per_device(): lax.ppermute(gram, AXES, [(d, d ^ flip) for d in range(count)])  21.3 us
    pallas_call x1, Pallas kernels, turn(): pl.pallas_call(turn_kernel, grid=(STEPS,), in_specs=[plane_spec(), whole(...  18.4 us
    ppermute x7, starting transfers between devices, per_device(): lax.ppermute(gram, AXES, [(d, d ^ flip) for d in range(count)])  10.9 us
    pallas_call x1, Pallas kernels, make_second(): pl.pallas_call(second_kernel, grid=(STEPS,), in_specs=[plane_spec(), halo...  8.75 us
    pallas_call x2, Pallas kernels, spread(): pl.pallas_call(spread_rows, out_shape=sds((CELLS, S)), compiler_params=pa...  6.58 us
  transfers between devices with their start and end apart: 30, of which 14 were waited for; matrix products, arithmetic and copies ran while one was open for 0% of the time, Pallas kernels for 26%

profile of v3, /device:TPU:0, one launch (start us, length us, event | category | flops | bytes accessed | tf_op | source)
XLA Modules:
  0.0 198.6 jit_solution(4975219825650564268)
XLA Ops:
  3.7 2.1 %collective-permute-start.4 = (f32[56,128]{1,0:T(8,128)S(1)}, f32[56,128]{1,0:T(8,128)S(1)}, u32[]{:S(2)}, u32[]{:S(2)}) collective-permute-start(f32[56,128]{1,0:T(8,128)S(1)} %pad_maximum_fusion.1), channel_id=1, source_target_pairs={{0,32},{1,33},{2,34},{3,35},{4,36},{5,37},{6,38},{7,39},{8,40},{9,... | collective-permute-start | bytes 86024 | tf_op jit(solution)/shard_map/ppermute | solution.py:682
  7.3 6.7 %collective-permute-start.2 = (f32[4,768]{1,0:T(4,128)S(1)}, f32[4,768]{1,0:T(4,128)S(1)}, u32[]{:S(2)}, u32[]{:S(2)}) collective-permute-start(f32[4,768]{1,0:T(4,128)S(1)} %maximum_maximum_fusion), channel_id=1, source_target_pairs={{0,31},{1,0},{2,1},{3,2},{4,3},{5,4},{6,5},{7,6},{8,7},{9,8},{10,9... | collective-permute-start | bytes 36872 | tf_op jit(solution)/shard_map/ppermute | solution.py:682
  14.0 7.5 %collective-permute-start.5 = (f32[4,768]{1,0:T(4,128)S(1)}, f32[4,768]{1,0:T(4,128)S(1)}, u32[]{:S(2)}, u32[]{:S(2)}) collective-permute-start(f32[4,768]{1,0:T(4,128)S(1)} %maximum_maximum_fusion), channel_id=1, source_target_pairs={{0,63},{1,32},{2,33},{3,34},{4,35},{5,36},{6,37},{7,38},{8,39},{9,... | collective-permute-start | bytes 36872 | tf_op jit(solution)/shard_map/ppermute | solution.py:682
  24.9 2.3 %pack.1 = (f32[12,192,128]{2,1,0:T(8,128)}, f32[4,192,128]{2,1,0:T(8,128)S(1)}, f32[16,64,128]{2,1,0:T(8,128)S(1)}, f32[6,16,16,128]{3,2,1,0:T(8,128)}, f32[6,16,16,128]{3,2,1,0:T(8,128)}) custom-call(f32[16,256,128]{2,1,0:T(8,128)S(1)} %bitcast.20), custom_call_target="tpu_custom_call" | custom-call | flops 8589934592 | bytes 6291456 | tf_op jit(solution)/shard_map/pack/pallas_call | solution.py:145
  28.7 8.9 %collective-permute-start.17 = (f32[6,16,16,128]{3,2,1,0:T(8,128)}, f32[6,16,16,128]{3,2,1,0:T(8,128)}, u32[]{:S(2)}, u32[]{:S(2)}) collective-permute-start(f32[6,16,16,128]{3,2,1,0:T(8,128)} %get-tuple-element.47), channel_id=1, source_target_pairs={{0,31},{1,0},{2,1},{3,2},{4,3},{5,4},{6,5},{7,6},{8,7},{9,8},{10,9... | collective-permute-start | bytes 2359304 | tf_op jit(solution)/shard_map/ppermute | solution.py:682
  37.7 3.3 %spread.2.vb_ref = f32[4096,128]{1,0:T(8,128)S(1)} custom-call(f32[32,128]{1,0:T(8,128)S(1)} %reshape.32.pot_ref), custom_call_target="tpu_custom_call" | custom-call | flops 1048576 | bytes 2097152 | tf_op jit(solution)/shard_map/spread/pallas_call | solution.py:271
  42.4 3.1 %side_x.1.part_ref = f32[16,256,128]{2,1,0:T(8,128)S(1)} custom-call(f32[16,256,128]{2,1,0:T(8,128)S(1)} %bitcast.21, f32[16,256,128]{2,1,0:T(8,128)} %collective-permute-done.7.mate_ref), custom_call_target="tpu_custom_call" | custom-call | flops 16777216 | bytes 6291456 | tf_op jit(solution)/shard_map/side_x/pallas_call | solution.py:182
  45.5 28.9 %prep.1 = (bf16[2,4096,128]{2,1,0:T(8,128)(2,1)S(1)}, f32[3,48,128]{2,1,0:T(8,128)S(1)}) custom-call(f32[128,768]{1,0:T(8,128)S(1)} %pad_maximum_fusion.near_ref, s32[2]{0:T(128)S(1)} %pad_add_fusion.corner_ref, f32[4096,128]{1,0:T(8,128)S(1)} %spread.2.vb_ref, f32[4096,128]{1,0:T(8,128)S(1)} %bitcast.22), custom_call_target="tpu_custom_call" | custom-call | flops 134217728 | bytes 10485760 | tf_op jit(solution)/shard_map/prep/pallas_call | solution.py:378
  75.7 2.1 %collective-permute-start.10 = (f32[48,128]{1,0:T(8,128)S(1)}, f32[48,128]{1,0:T(8,128)S(1)}, u32[]{:S(2)}, u32[]{:S(2)}) collective-permute-start(f32[48,128]{1,0:T(8,128)S(1)} %get-tuple-element.59), channel_id=1, source_target_pairs={{0,31},{1,0},{2,1},{3,2},{4,3},{5,4},{6,5},{7,6},{8,7},{9,8},{10,9... | collective-permute-start | bytes 73736 | tf_op jit(solution)/shard_map/ppermute | solution.py:682
  77.8 1.8 collective-permute-done.10.above_ref
  79.6 7.9 %collective-permute-done.9.below_ref = f32[48,128]{1,0:T(8,128)S(1)} collective-permute-done((f32[48,128]{1,0:T(8,128)S(1)}, f32[48,128]{1,0:T(8,128)S(1)}, u32[]{:S(2)}, u32[]{:S(2)}) %collective-permute-start.9) | collective-permute-done | bytes 24608 | tf_op jit(solution)/shard_map/ppermute | solution.py:682
  87.6 2.0 %collective-permute-start.12 = (f32[48,128]{1,0:T(8,128)S(1)}, f32[48,128]{1,0:T(8,128)S(1)}, u32[]{:S(2)}, u32[]{:S(2)}) collective-permute-start(f32[48,128]{1,0:T(8,128)S(1)} %merge.1.own_ref), channel_id=1, source_target_pairs={{0,32},{1,33},{2,34},{3,35},{4,36},{5,37},{6,38},{7,39},{8,40},{9,... | collective-permute-start | bytes 73736 | tf_op jit(solution)/shard_map/ppermute | solution.py:682
  89.7 8.3 %collective-permute-done.12.other_ref = f32[48,128]{1,0:T(8,128)S(1)} collective-permute-done((f32[48,128]{1,0:T(8,128)S(1)}, f32[48,128]{1,0:T(8,128)S(1)}, u32[]{:S(2)}, u32[]{:S(2)}) %collective-permute-start.12) | collective-permute-done | bytes 24608 | tf_op jit(solution)/shard_map/ppermute | solution.py:682
  98.2 7.7 %collective-permute-start.14 = (f32[16,128]{1,0:T(8,128)S(1)}, f32[16,128]{1,0:T(8,128)S(1)}, u32[]{:S(2)}, u32[]{:S(2)}) collective-permute-start(f32[16,128]{1,0:T(8,128)S(1)} %get-tuple-element.55.one_ref.rest_4_), channel_id=1, source_target_pairs={{0,31},{1,0},{2,1},{3,2},{4,3},{5,4},{6,5},{7,6},{8,7},{9,8},{10,9... | collective-permute-start | bytes 24584 | tf_op jit(solution)/shard_map/ppermute | solution.py:682
  105.9 4.2 %side_z.1.side_ref = f32[16,256,128]{2,1,0:T(8,128)S(1)} custom-call(f32[16,256,128]{2,1,0:T(8,128)S(1)} %bitcast.23, f32[16,256,128]{2,1,0:T(8,128)S(1)} %side_x.1.part_ref, f32[6,16,16,128]{3,2,1,0:T(8,128)} %collective-permute-done.16.low_ref, f32[6,16,16,128]{3,2,1,0:T(8,128)} %collective-permute-done.17.high_ref), custom_call_target="tpu_custom_call" | custom-call | flops 16777216 | bytes 8388608 | tf_op jit(solution)/shard_map/side_z/pallas_call | solution.py:207
  110.1 2.1 %first.1 = (f32[16,256,128]{2,1,0:T(8,128)S(1)}, f32[16,256,128]{2,1,0:T(8,128)S(1)}, f32[6,16,16,128]{3,2,1,0:T(8,128)S(1)}, f32[6,16,16,128]{3,2,1,0:T(8,128)S(1)}) custom-call(f32[16,256,128]{2,1,0:T(8,128)S(1)} %bitcast.24, f32[16,256,128]{2,1,0:T(8,128)S(1)} %side_z.1.side_ref, f32[12,192,128]{2,1,0:T(8,128)S(1)} %collective-permute-done.edge_one_ref, ...), custom_call_target="tpu_custom_call" | custom-call | flops 16777216 | bytes 14680064 | tf_op jit(solution)/shard_map/first/pallas_call | solution.py:462
  112.4 7.7 %collective-permute-start.20 = (f32[6,16,16,128]{3,2,1,0:T(8,128)S(1)}, f32[6,16,16,128]{3,2,1,0:T(8,128)S(1)}, u32[]{:S(2)}, u32[]{:S(2)}) collective-permute-start(f32[6,16,16,128]{3,2,1,0:T(8,128)S(1)} %get-tuple-element.51), channel_id=1, source_target_pairs={{0,31},{1,0},{2,1},{3,2},{4,3},{5,4},{6,5},{7,6},{8,7},{9,8},{10,9... | collective-permute-start | bytes 2359304 | tf_op jit(solution)/shard_map/ppermute | solution.py:682
  120.6 7.7 %collective-permute-start.22 = (f32[16,128]{1,0:T(8,128)S(1)}, f32[16,128]{1,0:T(8,128)S(1)}, u32[]{:S(2)}, u32[]{:S(2)}) collective-permute-start(f32[16,128]{1,0:T(8,128)S(1)} %again.1.rest_1_), channel_id=1, source_target_pairs={{0,31},{1,0},{2,1},{3,2},{4,3},{5,4},{6,5},{7,6},{8,7},{9,8},{10,9... | collective-permute-start | bytes 24584 | tf_op jit(solution)/shard_map/ppermute | solution.py:682
  128.4 3.3 %spread.3 = f32[4096,128]{1,0:T(8,128)S(1)} custom-call(f32[32,128]{1,0:T(8,128)S(1)} %slice.24.pot_ref), custom_call_target="tpu_custom_call" | custom-call | flops 1048576 | bytes 2097152 | tf_op jit(solution)/shard_map/spread/pallas_call | solution.py:271
  131.7 2.9 %side_again.1.part_ref = f32[16,256,128]{2,1,0:T(8,128)S(1)} custom-call(f32[16,256,128]{2,1,0:T(8,128)S(1)} %get-tuple-element.49.s_ref, f32[16,256,128]{2,1,0:T(8,128)S(1)} %collective-permute-done.18.mate_ref), custom_call_target="tpu_custom_call" | custom-call | flops 33554432 | bytes 6291456 | tf_op jit(solution)/shard_map/side_again/pallas_call | solution.py:234
  134.6 1.8 collective-permute-done.15.mid_ref
  136.4 2.8 %base.1.base_ref = f32[16,256,128]{2,1,0:T(8,128)S(1)} custom-call(f32[16,256,128]{2,1,0:T(8,128)S(1)} %bitcast.25, f32[12,192,128]{2,1,0:T(8,128)S(1)} %collective-permute-done.edge_one_ref, f32[4,192,128]{2,1,0:T(8,128)S(1)} %collective-permute-done.11.edge_two_ref, f32[16,64,128]{2,1,0:T(8,128)S(1)} %collective-permute-done.15.mid_ref, ...), custom_call_target="tpu_custom_call" | custom-call | flops 33554432 | bytes 16777216 | tf_op jit(solution)/shard_map/base/pallas_call | solution.py:511
  139.2 8.8 %second.1 = (f32[16,256,128]{2,1,0:T(8,128)S(1)}, f32[128,128]{1,0:T(8,128)S(1)}) custom-call(f32[16,256,128]{2,1,0:T(8,128)S(1)} %base.1.base_ref, f32[6,16,16,128]{3,2,1,0:T(8,128)S(1)} %collective-permute-done.19.low_ref, f32[6,16,16,128]{3,2,1,0:T(8,128)S(1)} %collective-permute-done.20.high_ref, bf16[2,16,256,128]{3,2,1,0:T(8,128)(2,1)S(1)} %bitcast.28, ...), custom_call_target="tpu_custom_call" | custom-call | flops 134217728 | bytes 8388608 | tf_op jit(solution)/shard_map/second/pallas_call | solution.py:563
  150.3 3.4 %collective-permute-done.24 = f32[128,128]{1,0:T(8,128)S(1)} collective-permute-done((f32[128,128]{1,0:T(8,128)S(1)}, f32[128,128]{1,0:T(8,128)S(1)}, u32[]{:S(2)}, u32[]{:S(2)}) %collective-permute-start.24) | collective-permute-done | bytes 65568 | tf_op jit(solution)/shard_map/ppermute | solution.py:742
  153.7 4.2 %collective-permute-start.25 = (f32[128,128]{1,0:T(8,128)S(1)}, f32[128,128]{1,0:T(8,128)S(1)}, u32[]{:S(2)}, u32[]{:S(2)}) collective-permute-start(f32[128,128]{1,0:T(8,128)S(1)} %add.26), channel_id=1, source_target_pairs={{0,36},{1,37},{2,38},{3,39},{4,32},{5,33},{6,34},{7,35},{8,44},{9,... | collective-permute-start | bytes 196616 | tf_op jit(solution)/shard_map/ppermute | solution.py:742
  157.9 2.2 %collective-permute-done.25 = f32[128,128]{1,0:T(8,128)S(1)} collective-permute-done((f32[128,128]{1,0:T(8,128)S(1)}, f32[128,128]{1,0:T(8,128)S(1)}, u32[]{:S(2)}, u32[]{:S(2)}) %collective-permute-start.25) | collective-permute-done | bytes 65568 | tf_op jit(solution)/shard_map/ppermute | solution.py:742
  160.3 4.3 %collective-permute-done.26 = f32[128,128]{1,0:T(8,128)S(1)} collective-permute-done((f32[128,128]{1,0:T(8,128)S(1)}, f32[128,128]{1,0:T(8,128)S(1)}, u32[]{:S(2)}, u32[]{:S(2)}) %collective-permute-start.26) | collective-permute-done | bytes 65568 | tf_op jit(solution)/shard_map/ppermute | solution.py:742
  166.0 4.3 %collective-permute-done.27 = f32[128,128]{1,0:T(8,128)S(1)} collective-permute-done((f32[128,128]{1,0:T(8,128)S(1)}, f32[128,128]{1,0:T(8,128)S(1)}, u32[]{:S(2)}, u32[]{:S(2)}) %collective-permute-start.27) | collective-permute-done | bytes 65568 | tf_op jit(solution)/shard_map/ppermute | solution.py:742
  171.6 3.1 %collective-permute-done.28 = f32[128,128]{1,0:T(8,128)S(1)} collective-permute-done((f32[128,128]{1,0:T(8,128)S(1)}, f32[128,128]{1,0:T(8,128)S(1)}, u32[]{:S(2)}, u32[]{:S(2)}) %collective-permute-start.28) | collective-permute-done | bytes 65568 | tf_op jit(solution)/shard_map/ppermute | solution.py:742
  174.7 2.7 %collective-permute-start.29 = (f32[128,128]{1,0:T(8,128)S(1)}, f32[128,128]{1,0:T(8,128)S(1)}, u32[]{:S(2)}, u32[]{:S(2)}) collective-permute-start(f32[128,128]{1,0:T(8,128)S(1)} %add.30), channel_id=1, source_target_pairs={{0,24},{1,25},{2,26},{3,27},{4,28},{5,29},{6,30},{7,31},{8,16},{9,... | collective-permute-start | bytes 196616 | tf_op jit(solution)/shard_map/ppermute | solution.py:742
  177.4 2.8 %collective-permute-done.29 = f32[128,128]{1,0:T(8,128)S(1)} collective-permute-done((f32[128,128]{1,0:T(8,128)S(1)}, f32[128,128]{1,0:T(8,128)S(1)}, u32[]{:S(2)}, u32[]{:S(2)}) %collective-permute-start.29) | collective-permute-done | bytes 65568 | tf_op jit(solution)/shard_map/ppermute | solution.py:742
  180.2 18.4 %turn.1 = f32[16,256,128]{2,1,0:T(8,128)} custom-call(f32[16,256,128]{2,1,0:T(8,128)S(1)} %get-tuple-element.57.second_ref, f32[128,128]{1,0:T(8,128)S(1)} %add_multiply_fusion.gram_ref), custom_call_target="tpu_custom_call" | custom-call | flops 268435456 | bytes 4194304 | tf_op jit(solution)/shard_map/turn/pallas_call | solution.py:659
  (82 shorter events, 19.0 us)
Async XLA Ops:
  3.7 17.8 %collective-permute-start.4 = (f32[56,128]{1,0:T(8,128)S(1)}, f32[56,128]{1,0:T(8,128)S(1)}, u32[]{:S(2)}, u32[]{:S(2)}) collective-permute-start(f32[56,128]{1,0:T(8,128)S(1)} %pad_maximum_fusion.1), channel_id=1, source_target_pairs={{0,32},{1,33},{2,34},{3,35},{4,36},{5,37},{6,38},{7,39},{8,40},{9,... | collective-permute-start | bytes 86024 | tf_op jit(solution)/shard_map/ppermute | solution.py:682
  5.8 15.7 %collective-permute-start.1 = (f32[4,768]{1,0:T(4,128)S(1)}, f32[4,768]{1,0:T(4,128)S(1)}, u32[]{:S(2)}, u32[]{:S(2)}) collective-permute-start(f32[4,768]{1,0:T(4,128)S(1)} %maximum_maximum_fusion), channel_id=1, source_target_pairs={{0,1},{1,2},{2,3},{3,4},{4,5},{5,6},{6,7},{7,8},{8,9},{9,10},{10,1... | collective-permute-start | bytes 36872 | tf_op jit(solution)/shard_map/ppermute | solution.py:682
  7.3 14.2 %collective-permute-start.2 = (f32[4,768]{1,0:T(4,128)S(1)}, f32[4,768]{1,0:T(4,128)S(1)}, u32[]{:S(2)}, u32[]{:S(2)}) collective-permute-start(f32[4,768]{1,0:T(4,128)S(1)} %maximum_maximum_fusion), channel_id=1, source_target_pairs={{0,31},{1,0},{2,1},{3,2},{4,3},{5,4},{6,5},{7,6},{8,7},{9,8},{10,9... | collective-permute-start | bytes 36872 | tf_op jit(solution)/shard_map/ppermute | solution.py:682
  14.0 9.1 %collective-permute-start.3 = (f32[4,768]{1,0:T(4,128)S(1)}, f32[4,768]{1,0:T(4,128)S(1)}, u32[]{:S(2)}, u32[]{:S(2)}) collective-permute-start(f32[4,768]{1,0:T(4,128)S(1)} %maximum_maximum_fusion), channel_id=1, source_target_pairs={{0,33},{1,34},{2,35},{3,36},{4,37},{5,38},{6,39},{7,40},{8,41},{9,... | collective-permute-start | bytes 36872 | tf_op jit(solution)/shard_map/ppermute | solution.py:682
  14.0 9.1 %collective-permute-start.5 = (f32[4,768]{1,0:T(4,128)S(1)}, f32[4,768]{1,0:T(4,128)S(1)}, u32[]{:S(2)}, u32[]{:S(2)}) collective-permute-start(f32[4,768]{1,0:T(4,128)S(1)} %maximum_maximum_fusion), channel_id=1, source_target_pairs={{0,63},{1,32},{2,33},{3,34},{4,35},{5,36},{6,37},{7,38},{8,39},{9,... | collective-permute-start | bytes 36872 | tf_op jit(solution)/shard_map/ppermute | solution.py:682
  23.2 19.2 %collective-permute-start.7 = (f32[16,256,128]{2,1,0:T(8,128)}, f32[16,256,128]{2,1,0:T(8,128)}, u32[]{:S(2)}, u32[]{:S(2)}) collective-permute-start(f32[16,256,128]{2,1,0:T(8,128)} %bitcast.19), channel_id=1, source_target_pairs={{0,64},{1,65},{2,66},{3,67},{4,68},{5,69},{6,70},{7,71},{8,72},{9,... | collective-permute-start | bytes 6291464 | tf_op jit(solution)/shard_map/ppermute | solution.py:682
  28.7 13.6 %copy-start.1 = (f32[16,16,16,128]{3,2,1,0:T(8,128)S(1)}, f32[16,16,16,128]{3,2,1,0:T(8,128)}, u32[]{:S(2)}) copy-start(f32[16,16,16,128]{3,2,1,0:T(8,128)} %param.5) | copy-start | bytes 6291460
  28.7 81.4 %collective-permute-start = (f32[12,192,128]{2,1,0:T(8,128)}, f32[12,192,128]{2,1,0:T(8,128)S(1)}, u32[]{:S(2)}, u32[]{:S(2)}) collective-permute-start(f32[12,192,128]{2,1,0:T(8,128)} %get-tuple-element.33), channel_id=1, source_target_pairs={{0,32},{1,33},{2,34},{3,35},{4,36},{5,37},{6,38},{7,39},{8,40},{9,... | collective-permute-start | bytes 3538952 | tf_op jit(solution)/shard_map/ppermute | solution.py:682
  28.7 69.4 %collective-permute-start.16 = (f32[6,16,16,128]{3,2,1,0:T(8,128)}, f32[6,16,16,128]{3,2,1,0:T(8,128)}, u32[]{:S(2)}, u32[]{:S(2)}) collective-permute-start(f32[6,16,16,128]{3,2,1,0:T(8,128)} %get-tuple-element.46), channel_id=1, source_target_pairs={{0,1},{1,2},{2,3},{3,4},{4,5},{5,6},{6,7},{7,8},{8,9},{9,10},{10,1... | collective-permute-start | bytes 2359304 | tf_op jit(solution)/shard_map/ppermute | solution.py:682
  28.7 77.1 %collective-permute-start.17 = (f32[6,16,16,128]{3,2,1,0:T(8,128)}, f32[6,16,16,128]{3,2,1,0:T(8,128)}, u32[]{:S(2)}, u32[]{:S(2)}) collective-permute-start(f32[6,16,16,128]{3,2,1,0:T(8,128)} %get-tuple-element.47), channel_id=1, source_target_pairs={{0,31},{1,0},{2,1},{3,2},{4,3},{5,4},{6,5},{7,6},{8,7},{9,8},{10,9... | collective-permute-start | bytes 2359304 | tf_op jit(solution)/shard_map/ppermute | solution.py:682
  40.9 1.3 collective-permute-start.6
  45.4 42.1 %copy-start.5 = (f32[4,192,128]{2,1,0:T(8,128)S(1)}, f32[4,192,128]{2,1,0:T(8,128)}, u32[]{:S(2)}) copy-start(f32[4,192,128]{2,1,0:T(8,128)} %copy-done.4) | copy-start | bytes 1179652
  74.3 1.3 collective-permute-start.8
  75.7 3.9 %collective-permute-start.10 = (f32[48,128]{1,0:T(8,128)S(1)}, f32[48,128]{1,0:T(8,128)S(1)}, u32[]{:S(2)}, u32[]{:S(2)}) collective-permute-start(f32[48,128]{1,0:T(8,128)S(1)} %get-tuple-element.59), channel_id=1, source_target_pairs={{0,31},{1,0},{2,1},{3,2},{4,3},{5,4},{6,5},{7,6},{8,7},{9,8},{10,9... | collective-permute-start | bytes 73736 | tf_op jit(solution)/shard_map/ppermute | solution.py:682
  77.8 9.7 %collective-permute-start.9 = (f32[48,128]{1,0:T(8,128)S(1)}, f32[48,128]{1,0:T(8,128)S(1)}, u32[]{:S(2)}, u32[]{:S(2)}) collective-permute-start(f32[48,128]{1,0:T(8,128)S(1)} %get-tuple-element.60), channel_id=1, source_target_pairs={{0,1},{1,2},{2,3},{3,4},{4,5},{5,6},{6,7},{7,8},{8,9},{9,10},{10,1... | collective-permute-start | bytes 73736 | tf_op jit(solution)/shard_map/ppermute | solution.py:682
  87.6 22.6 %collective-permute-start.11 = (f32[4,192,128]{2,1,0:T(8,128)S(1)}, f32[4,192,128]{2,1,0:T(8,128)S(1)}, u32[]{:S(2)}, u32[]{:S(2)}) collective-permute-start(f32[4,192,128]{2,1,0:T(8,128)S(1)} %copy-done.5), channel_id=1, source_target_pairs={{0,32},{1,33},{2,34},{3,35},{4,36},{5,37},{6,38},{7,39},{8,40},{9,... | collective-permute-start | bytes 1179656 | tf_op jit(solution)/shard_map/ppermute | solution.py:682
  87.6 10.4 %collective-permute-start.12 = (f32[48,128]{1,0:T(8,128)S(1)}, f32[48,128]{1,0:T(8,128)S(1)}, u32[]{:S(2)}, u32[]{:S(2)}) collective-permute-start(f32[48,128]{1,0:T(8,128)S(1)} %merge.1.own_ref), channel_id=1, source_target_pairs={{0,32},{1,33},{2,34},{3,35},{4,36},{5,37},{6,38},{7,39},{8,40},{9,... | collective-permute-start | bytes 73736 | tf_op jit(solution)/shard_map/ppermute | solution.py:682
  98.1 12.0 %collective-permute-start.13 = (f32[16,128]{1,0:T(8,128)S(1)}, f32[16,128]{1,0:T(8,128)S(1)}, u32[]{:S(2)}, u32[]{:S(2)}) collective-permute-start(f32[16,128]{1,0:T(8,128)S(1)} %get-tuple-element.55.one_ref.rest_4_), channel_id=1, source_target_pairs={{0,1},{1,2},{2,3},{3,4},{4,5},{5,6},{6,7},{7,8},{8,9},{9,10},{10,1... | collective-permute-start | bytes 24584 | tf_op jit(solution)/shard_map/ppermute | solution.py:682
  98.2 11.9 %collective-permute-start.14 = (f32[16,128]{1,0:T(8,128)S(1)}, f32[16,128]{1,0:T(8,128)S(1)}, u32[]{:S(2)}, u32[]{:S(2)}) collective-permute-start(f32[16,128]{1,0:T(8,128)S(1)} %get-tuple-element.55.one_ref.rest_4_), channel_id=1, source_target_pairs={{0,31},{1,0},{2,1},{3,2},{4,3},{5,4},{6,5},{7,6},{8,7},{9,8},{10,9... | collective-permute-start | bytes 24584 | tf_op jit(solution)/shard_map/ppermute | solution.py:682
  112.3 8.3 %collective-permute-start.18 = (f32[16,256,128]{2,1,0:T(8,128)S(1)}, f32[16,256,128]{2,1,0:T(8,128)S(1)}, u32[]{:S(2)}, u32[]{:S(2)}) collective-permute-start(f32[16,256,128]{2,1,0:T(8,128)S(1)} %get-tuple-element.49.s_ref), channel_id=1, source_target_pairs={{0,64},{1,65},{2,66},{3,67},{4,68},{5,69},{6,70},{7,71},{8,72},{9,... | collective-permute-start | bytes 6291464 | tf_op jit(solution)/shard_map/ppermute | solution.py:682
  112.3 26.9 %collective-permute-start.19 = (f32[6,16,16,128]{3,2,1,0:T(8,128)S(1)}, f32[6,16,16,128]{3,2,1,0:T(8,128)S(1)}, u32[]{:S(2)}, u32[]{:S(2)}) collective-permute-start(f32[6,16,16,128]{3,2,1,0:T(8,128)S(1)} %get-tuple-element.50), channel_id=1, source_target_pairs={{0,1},{1,2},{2,3},{3,4},{4,5},{5,6},{6,7},{7,8},{8,9},{9,10},{10,1... | collective-permute-start | bytes 2359304 | tf_op jit(solution)/shard_map/ppermute | solution.py:682
  112.4 26.8 %collective-permute-start.20 = (f32[6,16,16,128]{3,2,1,0:T(8,128)S(1)}, f32[6,16,16,128]{3,2,1,0:T(8,128)S(1)}, u32[]{:S(2)}, u32[]{:S(2)}) collective-permute-start(f32[6,16,16,128]{3,2,1,0:T(8,128)S(1)} %get-tuple-element.51), channel_id=1, source_target_pairs={{0,31},{1,0},{2,1},{3,2},{4,3},{5,4},{6,5},{7,6},{8,7},{9,8},{10,9... | collective-permute-start | bytes 2359304 | tf_op jit(solution)/shard_map/ppermute | solution.py:682
  120.2 16.3 %collective-permute-start.15 = (f32[16,64,128]{2,1,0:T(8,128)S(1)}, f32[16,64,128]{2,1,0:T(8,128)S(1)}, u32[]{:S(2)}, u32[]{:S(2)}) collective-permute-start(f32[16,64,128]{2,1,0:T(8,128)S(1)} %copy-done.3), channel_id=1, source_target_pairs={{0,32},{1,33},{2,34},{3,35},{4,36},{5,37},{6,38},{7,39},{8,40},{9,... | collective-permute-start | bytes 1572872 | tf_op jit(solution)/shard_map/ppermute | solution.py:682
  120.5 18.7 %collective-permute-start.21 = (f32[16,128]{1,0:T(8,128)S(1)}, f32[16,128]{1,0:T(8,128)S(1)}, u32[]{:S(2)}, u32[]{:S(2)}) collective-permute-start(f32[16,128]{1,0:T(8,128)S(1)} %again.1.rest_1_), channel_id=1, source_target_pairs={{0,1},{1,2},{2,3},{3,4},{4,5},{5,6},{6,7},{7,8},{8,9},{9,10},{10,1... | collective-permute-start | bytes 24584 | tf_op jit(solution)/shard_map/ppermute | solution.py:682
  120.6 18.6 %collective-permute-start.22 = (f32[16,128]{1,0:T(8,128)S(1)}, f32[16,128]{1,0:T(8,128)S(1)}, u32[]{:S(2)}, u32[]{:S(2)}) collective-permute-start(f32[16,128]{1,0:T(8,128)S(1)} %again.1.rest_1_), channel_id=1, source_target_pairs={{0,31},{1,0},{2,1},{3,2},{4,3},{5,4},{6,5},{7,6},{8,7},{9,8},{10,9... | collective-permute-start | bytes 24584 | tf_op jit(solution)/shard_map/ppermute | solution.py:682
  148.0 1.3 collective-permute-start.23
  149.4 4.3 %collective-permute-start.24 = (f32[128,128]{1,0:T(8,128)S(1)}, f32[128,128]{1,0:T(8,128)S(1)}, u32[]{:S(2)}, u32[]{:S(2)}) collective-permute-start(f32[128,128]{1,0:T(8,128)S(1)} %add.25), channel_id=1, source_target_pairs={{0,32},{1,33},{2,34},{3,35},{4,36},{5,37},{6,38},{7,39},{8,40},{9,... | collective-permute-start | bytes 196616 | tf_op jit(solution)/shard_map/ppermute | solution.py:742
  153.7 6.5 %collective-permute-start.25 = (f32[128,128]{1,0:T(8,128)S(1)}, f32[128,128]{1,0:T(8,128)S(1)}, u32[]{:S(2)}, u32[]{:S(2)}) collective-permute-start(f32[128,128]{1,0:T(8,128)S(1)} %add.26), channel_id=1, source_target_pairs={{0,36},{1,37},{2,38},{3,39},{4,32},{5,33},{6,34},{7,35},{8,44},{9,... | collective-permute-start | bytes 196616 | tf_op jit(solution)/shard_map/ppermute | solution.py:742
  160.2 4.3 %collective-permute-start.26 = (f32[128,128]{1,0:T(8,128)S(1)}, f32[128,128]{1,0:T(8,128)S(1)}, u32[]{:S(2)}, u32[]{:S(2)}) collective-permute-start(f32[128,128]{1,0:T(8,128)S(1)} %add.27), channel_id=1, source_target_pairs={{0,1},{1,0},{2,3},{3,2},{4,5},{5,4},{6,7},{7,6},{8,9},{9,8},{10,11... | collective-permute-start | bytes 196616 | tf_op jit(solution)/shard_map/ppermute | solution.py:742
  164.6 5.7 %collective-permute-start.27 = (f32[128,128]{1,0:T(8,128)S(1)}, f32[128,128]{1,0:T(8,128)S(1)}, u32[]{:S(2)}, u32[]{:S(2)}) collective-permute-start(f32[128,128]{1,0:T(8,128)S(1)} %add.28), channel_id=1, source_target_pairs={{0,3},{1,2},{2,1},{3,0},{4,7},{5,6},{6,5},{7,4},{8,11},{9,10},{10,... | collective-permute-start | bytes 196616 | tf_op jit(solution)/shard_map/ppermute | solution.py:742
  170.3 4.3 %collective-permute-start.28 = (f32[128,128]{1,0:T(8,128)S(1)}, f32[128,128]{1,0:T(8,128)S(1)}, u32[]{:S(2)}, u32[]{:S(2)}) collective-permute-start(f32[128,128]{1,0:T(8,128)S(1)} %add.29), channel_id=1, source_target_pairs={{0,8},{1,9},{2,10},{3,11},{4,12},{5,13},{6,14},{7,15},{8,0},{9,1},... | collective-permute-start | bytes 196616 | tf_op jit(solution)/shard_map/ppermute | solution.py:742
  174.7 5.6 %collective-permute-start.29 = (f32[128,128]{1,0:T(8,128)S(1)}, f32[128,128]{1,0:T(8,128)S(1)}, u32[]{:S(2)}, u32[]{:S(2)}) collective-permute-start(f32[128,128]{1,0:T(8,128)S(1)} %add.30), channel_id=1, source_target_pairs={{0,24},{1,25},{2,26},{3,27},{4,28},{5,29},{6,30},{7,31},{8,16},{9,... | collective-permute-start | bytes 196616 | tf_op jit(solution)/shard_map/ppermute | solution.py:742
  (4 other events, 13.2 us)

commit v4 on v3

--- a/solution.py
+++ b/solution.py
@@ -72,19 +72,20 @@
 
 B = 4
 STEPS = C // B
-CUT = 12
+N = 2
+CUTS = (0, 6, 14, 16)
 
 
 def stride_rows(z):
     return pl.ds(z, C, stride=C)
 
 
-def plane_spec(rows=ROWS):
-    return pl.BlockSpec((B, rows, S), lambda i: (i, 0, 0))
-
-
-def halo_spec():
-    return pl.BlockSpec((H, B, C, S), lambda i: (0, i, 0, 0))
+def plane_spec(rows=ROWS, planes=B):
+    return pl.BlockSpec((planes, rows, S), lambda i: (i, 0, 0))
+
+
+def halo_spec(planes=B):
+    return pl.BlockSpec((H, planes, C, S), lambda i: (0, i, 0, 0))
 
 
 def part_spec(part):
@@ -96,46 +97,40 @@
 
 
 def edge_specs():
-    return [
-        pl.BlockSpec((B, 192, S), lambda i: (jnp.minimum(i, CUT // B - 1), 0, 0)),
-        pl.BlockSpec((B, 192, S), lambda i: (jnp.maximum(i - CUT // B, 0), 0, 0)),
-    ]
-
-
-def per_plane(body):
-    def step(p, _):
-        body(p)
-        return 0
-
-    lax.fori_loop(0, B, step, 0)
+    def spec(start, stop):
+        return pl.BlockSpec((N, 192, S), lambda i: (jnp.clip(i - start // N, 0, (stop - start) // N - 1), 0, 0))
+
+    return [spec(start, stop) for start, stop in zip(CUTS, CUTS[1:])]
+
+
+def for_piece(pieces, body):
+    step = pl.program_id(0)
+    for piece, start, stop in zip(pieces, CUTS, CUTS[1:]):
+
+        @pl.when((step >= start // N) & (step < stop // N))
+        def _(piece=piece):
+            body(piece)
 
 
 FULL = sds((C, ROWS, S))
 HALO = sds((H, C, C, S))
-EDGES = [sds((CUT, 192, S)), sds((C - CUT, 192, S))]
+EDGES = [sds((stop - start, 192, S)) for start, stop in zip(CUTS, CUTS[1:])]
 
 
 def halves(y, half):
     return slice(y * C + half * 8, y * C + half * 8 + 8)
 
 
-def pack_kernel(s_ref, one_ref, two_ref, mid_ref, head_ref, tail_ref):
-    step = pl.program_id(0)
+def pack_kernel(s_ref, *refs):
+    mid_ref, head_ref, tail_ref = refs[3:]
 
     def edges(out_ref):
         out_ref[:, 0:96, :] = s_ref[:, 0:96, :]
         out_ref[:, 96:192, :] = s_ref[:, 160:256, :]
 
-    @pl.when(step < CUT // B)
-    def _():
-        edges(one_ref)
-
-    @pl.when(step >= CUT // B)
-    def _():
-        edges(two_ref)
-
+    for_piece(refs[:3], edges)
     mid_ref[...] = s_ref[:, 96:160, :]
-    for p in range(B):
+    for p in range(N):
         for z in range(H):
             head_ref[z, p] = s_ref[p, stride_rows(z), :]
             tail_ref[z, p] = s_ref[p, stride_rows(C - H + z), :]
@@ -144,12 +139,12 @@
 def pack(s):
     return pl.pallas_call(
         pack_kernel,
-        grid=(STEPS,),
-        in_specs=[plane_spec()],
-        out_specs=edge_specs() + [plane_spec(64), halo_spec(), halo_spec()],
+        grid=(C // N,),
+        in_specs=[plane_spec(ROWS, N)],
+        out_specs=edge_specs() + [plane_spec(64, N), halo_spec(N), halo_spec(N)],
         out_shape=EDGES + [sds((C, 64, S)), HALO, HALO],
         compiler_params=params(12),
-        cost_estimate=cost(1 << 33, 6 << 20),
+        cost_estimate=cost(1 << 32, 6 << 20),
         name="pack",
     )(s)
 
@@ -264,7 +259,7 @@
         vb_ref[pl.ds(start, 128), :] = jnp.broadcast_to(line, (128, 128)).T
         return 0
 
-    lax.fori_loop(0, CELLS // 128, spread, 0)
+    lax.fori_loop(0, CELLS // 128, spread, 0, unroll=8)
 
 
 def spread(pot):
@@ -307,7 +302,7 @@
         a1z_ref[ij] = along
         return 0
 
-    lax.fori_loop(0, W * W, place_z, 0)
+    lax.fori_loop(0, W * W, place_z, 0, unroll=3)
 
     def place_y(y, _):
         masks, factors = ring_tables(y - py + R)
@@ -348,7 +343,7 @@
             gg_ref[1, pl.ds(row, C), :] = low
             return 0
 
-        lax.fori_loop(0, C, per_y, 0)
+        lax.fori_loop(0, C, per_y, 0, unroll=16)
         return 0
 
     lax.fori_loop(0, C, place_x, 0)
@@ -370,7 +365,7 @@
             coef_ref[slab, 32:48] += pair[rows]
         return 0
 
-    lax.fori_loop(0, C // 2, contract, 0)
+    lax.fori_loop(0, C // 2, contract, 0, unroll=2)
 
 
 def prep(near, corner, vb, s):
@@ -427,9 +422,11 @@
     )
 
 
-def first_kernel(s_ref, side_ref, edge_one_ref, edge_two_ref, vb_ref, q_ref, mix_ref, head_ref, tail_ref):
+def first_kernel(s_ref, side_ref, vb_ref, *refs):
+    q_ref, mix_ref, head_ref, tail_ref = refs[3:]
+
     def planes(edge_ref):
-        def plane(p):
+        for p in range(N):
             for half in range(2):
                 ring = {y: s_ref[p, halves(y, half), :] for y in range(C)}
                 for y in range(H):
@@ -445,38 +442,30 @@
                 head_ref[z, p] = mix_ref[p, stride_rows(z), :]
                 tail_ref[z, p] = mix_ref[p, stride_rows(C - H + z), :]
 
-        per_plane(plane)
-
-    step = pl.program_id(0)
-
-    @pl.when(step < CUT // B)
-    def _():
-        planes(edge_one_ref)
-
-    @pl.when(step >= CUT // B)
-    def _():
-        planes(edge_two_ref)
-
-
-def make_first(s, side_part, edges, vb):
+    for_piece(refs[:3], planes)
+
+
+def make_first(s, side_part, vb, edges):
     return pl.pallas_call(
         first_kernel,
-        grid=(STEPS,),
-        in_specs=[plane_spec(), plane_spec()] + edge_specs() + [plane_spec()],
-        out_specs=[plane_spec(), plane_spec(), halo_spec(), halo_spec()],
+        grid=(C // N,),
+        in_specs=[plane_spec(ROWS, N)] * 3 + edge_specs(),
+        out_specs=[plane_spec(ROWS, N), plane_spec(ROWS, N), halo_spec(N), halo_spec(N)],
         out_shape=[FULL, FULL, HALO, HALO],
         compiler_params=params(16),
         cost_estimate=cost(1 << 24, 14 << 20),
         name="first",
-    )(s, side_part, *edges, vb)
-
-
-def base_kernel(s_ref, edge_one_ref, edge_two_ref, mid_ref, vb_ref, vb_mate_ref, q_ref, side_ref, part_ref, out_ref):
+    )(s, side_part, vb, *edges)
+
+
+def base_kernel(s_ref, mid_ref, vb_ref, vb_mate_ref, q_ref, side_ref, part_ref, *refs):
+    out_ref = refs[3]
+
     def planes(edge_ref):
-        def plane(p):
+        for p in range(N):
             for half in range(2):
 
-                def other(y, half=half):
+                def other(y, p=p, half=half):
                     if y < H:
                         return edge_ref[p, halves(y, half), :]
                     if y < C - H:
@@ -494,35 +483,25 @@
                     total = total + vb_ref[p, rows, :] * (side_ref[p, rows, :] + q[y])
                     out_ref[p, rows, :] = 2.0 * (total + part_ref[p, rows, :]) - ring[y]
 
-        per_plane(plane)
-
-    step = pl.program_id(0)
-
-    @pl.when(step < CUT // B)
-    def _():
-        planes(edge_one_ref)
-
-    @pl.when(step >= CUT // B)
-    def _():
-        planes(edge_two_ref)
-
-
-def make_base(s, edges, mid, vb, vb_mate, q, side_part, part):
+    for_piece(refs[:3], planes)
+
+
+def make_base(s, mid, vb, vb_mate, q, side_part, part, edges):
     return pl.pallas_call(
         base_kernel,
-        grid=(STEPS,),
-        in_specs=[plane_spec()] + edge_specs() + [plane_spec(64)] + [plane_spec()] * 5,
-        out_specs=plane_spec(),
+        grid=(C // N,),
+        in_specs=[plane_spec(ROWS, N), plane_spec(64, N)] + [plane_spec(ROWS, N)] * 5 + edge_specs(),
+        out_specs=plane_spec(ROWS, N),
         out_shape=FULL,
         compiler_params=params(16),
         cost_estimate=cost(1 << 25, 16 << 20),
         name="base",
-    )(s, *edges, mid, vb, vb_mate, q, side_part, part)
+    )(s, mid, vb, vb_mate, q, side_part, part, *edges)
 
 
 def second_kernel(base_ref, low_ref, high_ref, gg_high_ref, gg_low_ref, *rest):
     weighted = rest[:6]
-    second_ref, gram_ref, cross_ref, w_ref = rest[6:]
+    second_ref, gram_ref, cross_ref, w_ref, halo_ref = rest[6:]
     step = pl.program_id(0)
 
     @pl.when(step == 0)
@@ -530,28 +509,33 @@
         gram_ref[...] = jnp.zeros((S, S), F32)
         cross_ref[...] = jnp.zeros((S, S), F32)
         w_ref[...] = jnp.zeros((S, S), F32)
+        halo_ref[...] = jnp.zeros((B, ROWS, S), F32)
         for j in range(3):
             w_ref[j * C : j * C + C, :] = 2.0 * weighted[j][...]
             w_ref[64 + j * C : 80 + j * C, :] = 2.0 * weighted[3 + j][...]
 
-    w_high, w_low = split(w_ref[...])
-
-    def plane(p):
-        g_high, g_low = gg_high_ref[0, p], gg_low_ref[0, p]
-        second_ref[p] = base_ref[p] + (mm(g_high, w_high) + (mm(g_high, w_low) + mm(g_low, w_high)))
+    for p in range(B):
         low = [low_ref[j, p] for j in range(H)]
         high = [high_ref[j, p] for j in range(H)]
         for z in range(H):
             add = sum((2.0 * OFF[k - 1]) * low[z - k + H] for k in range(z + 1, H + 1))
-            second_ref[p, stride_rows(z), :] += add
+            halo_ref[p, stride_rows(z), :] = add
             add = sum((2.0 * OFF[H + j - z - 1]) * high[j] for j in range(z + 1))
-            second_ref[p, stride_rows(C - H + z), :] += add
-        s_high, s_low = split(second_ref[p])
+            halo_ref[p, stride_rows(C - H + z), :] = add
+
+    w_high, w_low = split(w_ref[...])
+    gram = jnp.zeros((S, S), F32)
+    cross = jnp.zeros((S, S), F32)
+    for p in range(B):
+        g_high, g_low = gg_high_ref[0, p], gg_low_ref[0, p]
+        value = base_ref[p] + halo_ref[p] + (mm(g_high, w_high) + (mm(g_high, w_low) + mm(g_low, w_high)))
+        second_ref[p] = value
+        s_high, s_low = split(value)
         turned = s_high.T
-        gram_ref[...] += mm(turned, s_high)
-        cross_ref[...] += mm(turned, s_low)
-
-    per_plane(plane)
+        gram += mm(turned, s_high)
+        cross += mm(turned, s_low)
+    gram_ref[...] += gram
+    cross_ref[...] += cross
 
     @pl.when(step == STEPS - 1)
     def _():
@@ -566,7 +550,7 @@
         in_specs=[plane_spec(), halo_spec(), halo_spec(), part_spec(0), part_spec(1)] + [whole(C)] * 6,
         out_specs=[plane_spec(), whole()],
         out_shape=[FULL, sds((S, S))],
-        scratch_shapes=[pltpu.VMEM((S, S), F32), pltpu.VMEM((S, S), F32)],
+        scratch_shapes=[pltpu.VMEM((S, S), F32), pltpu.VMEM((S, S), F32), pltpu.VMEM((B, ROWS, S), F32)],
         compiler_params=params(16),
         cost_estimate=cost(1 << 27, 8 << 20),
         name="second",
@@ -648,11 +632,9 @@
 
     i_high, i_low = i_high_ref[...], i_low_ref[...]
 
-    def plane(p):
+    for p in range(B):
         high, low = split(second_ref[p])
         out_ref[p] = mm(high, i_high) + (mm(high, i_low) + mm(low, i_high))
-
-    per_plane(plane)
 
 
 def turn(second, gram):
@@ -689,20 +671,18 @@
         [projectors.reshape(4, TAPS), atom_sites.astype(F32), energies[:, None], jnp.zeros((4, 768 - TAPS - 4), F32)],
         axis=1,
     )
-    parcel = jnp.concatenate([atoms.reshape(24, 128), pot])
-    parcel_mate = send(parcel, over_y)
+    mate = send(s, over_x)
     below, above = send(atoms, 0, 1), send(atoms, 0, -1)
-    below_mate, above_mate = send(atoms, over_y, 1), send(atoms, over_y, -1)
-    packed = pack(barrier((s, atoms))[0])
-    edges, mid, head, tail = packed[:2], packed[2], packed[3], packed[4]
-    edge_one = send(edges[0], over_y)
+    one_edge, two_edge, three_edge, mid, head, tail = pack(s)
+    one_edge = send(one_edge, over_y)
+    mine = jnp.stack([below, atoms, above])
+    head, tail, mine = barrier((head, tail, mine))
+    parcel = send(jnp.concatenate([mine.reshape(72, 128), pot]), over_y)
     low, high = send(tail, 0, 1), send(head, 0, -1)
-    mine = jnp.stack([below, atoms, above])
-    other = jnp.stack([below_mate, parcel_mate[:24].reshape(4, 768), above_mate])
+    other, two_edge = barrier((parcel[:72].reshape(3, 4, 768), two_edge))
+    two_edge = send(two_edge, over_y)
     column = jnp.where(gy == 0, jnp.concatenate([mine, other], 1), jnp.concatenate([other, mine], 1))
     column_mate = send(column, over_x)
-    s_mate, _ = barrier((s, column))
-    mate = send(s_mate, over_x)
     near = jnp.where(
         gx == 0, jnp.concatenate([column, column_mate], 1), jnp.concatenate([column_mate, column], 1)
     ).reshape(NEAR, 768)
@@ -711,31 +691,31 @@
     corner = jnp.stack([gx * C, gy * C]).astype(jnp.int32)
     vb = spread(pot)
     beside = side_x(s, mate)
-    near, beside = barrier((jnp.concatenate([near, gap, near, gap]), beside))
+    near, beside, one_edge = barrier((jnp.concatenate([near, gap, near, gap]), beside, one_edge))
     gg, part = prep(near, corner, vb, s)
 
     part = part + send(part, over_x)
     own = merge(part, send(part[2], 0, 1), send(part[0], 0, -1))
-    edge_two, own = barrier((edges[1], own))
+    three_edge, own = barrier((three_edge, own))
     own_mate = send(own, over_y)
-    edge_two = send(edge_two, over_y)
+    three_edge = send(three_edge, over_y)
     one, rest = weigh(own, own_mate, energy)
-    mid, one = barrier((mid, one))
+    mid, one, two_edge = barrier((mid, one, two_edge))
     mid = send(mid, over_y)
     ones = [send(one, 0, 1), one, send(one, 0, -1)]
 
     vb = vb.reshape(C, ROWS, S)
-    vb_mate = spread(parcel_mate[24:]).reshape(C, ROWS, S)
+    vb_mate = spread(parcel[72:]).reshape(C, ROWS, S)
     side_part = side_z(s, beside, low, high)
-    edge_two, ones = barrier((edge_two, ones))
-    edges = [edge_one, edge_two]
+    three_edge, ones = barrier((three_edge, ones))
+    edges = [one_edge, two_edge, three_edge]
     two = again(rest, *ones, energy)
     twos = [send(two, 0, 1), two, send(two, 0, -1)]
-    q, mix, head, tail = make_first(s, side_part, edges, vb)
+    q, mix, head, tail = make_first(s, side_part, vb, edges)
     low, high = send(tail, 0, 1), send(head, 0, -1)
     mate = send(mix, over_x)
     part = side_again(mix, mate)
-    base = make_base(s, edges, mid, vb, vb_mate, q, side_part, part)
+    base = make_base(s, mid, vb, vb_mate, q, side_part, part, edges)
     second, gram = make_second(base, low, high, gg.reshape(2, C, ROWS, S), twos + ones)
 
     for flip in (64, 32, 36, 1, 3, 8, 24):

time: 199 us -> 184 us (0.925)
  Pallas kernels: 80.2 us -> 47.8 us
  waiting for transfers between devices: 45.1 us -> 55.1 us
  local copies, waits for them, and re-layouts: 6.09 us -> 13.8 us
  starting transfers between devices: 65.8 us -> 61.8 us
  other arithmetic: 1.07 us -> 4.01 us
    pallas_call x1, Pallas kernels: 28.9 us -> 7.73 us  [prep(): pl.pallas_call(prep_kernel, in_specs=[vmem, pl.BlockSpec(memory_space=plt...]
    ppermute x23 -> x22, waiting for transfers between devices: 23.8 us -> 31.9 us  [send(): return lax.ppermute(value, AXES, [(d, target(d)) for d in range(count)])]
    pallas_call x2, Pallas kernels: 6.58 us -> 1.62 us  [spread(): pl.pallas_call(spread_rows, out_shape=sds((CELLS, S)), compiler_params=pa...]
    pallas_call x1, Pallas kernels: 8.75 us -> 4.96 us  [make_second(): pl.pallas_call(second_kernel, grid=(STEPS,), in_specs=[plane_spec(), halo...]
    unnamed x13 -> x23, local copies, waits for them, and re-layouts: 4.07 us -> 7.72 us
    ppermute x7, starting transfers between devices: 10.9 us -> 7.83 us  [per_device(): lax.ppermute(gram, AXES, [(d, d ^ flip) for d in range(count)])]
    slice x2, local copies, waits for them, and re-layouts: 0.01 us -> 2.1 us  [the longest x1 1.38 us: per_device(): other, two_edge = barrier((parcel[:72].reshape(3, 4, 768), two_edge))]
    reshape x1 -> x2, local copies, waits for them, and re-layouts: 0.01 us -> 2.03 us  [the longest x1 1.39 us: per_device(): other, two_edge = barrier((parcel[:72].reshape(3, 4, 768), two_edge))]
  transfers between devices with their start and end apart: 30 -> 29, of which waited for: 14 -> 12; matrix products, arithmetic and copies ran while one was open for 0% -> 6% of each run, Pallas kernels for 26% -> 13%
where the time goes in v4:
time: 184 us; the launch traced here: 183 us
  starting transfers between devices  61.8 us (34%)
  waiting for transfers between devices  55.1 us (30%)
  Pallas kernels  47.8 us (26%)
  local copies, waits for them, and re-layouts  13.8 us (8%)
  other arithmetic  4.01 us (2%)
    ppermute x22, starting transfers between devices, send(): return lax.ppermute(value, AXES, [(d, target(d)) for d in range(count)])  53.9 us
    ppermute x22, waiting for transfers between devices, send(): return lax.ppermute(value, AXES, [(d, target(d)) for d in range(count)])  31.9 us
    ppermute x7, waiting for transfers between devices, per_device(): lax.ppermute(gram, AXES, [(d, d ^ flip) for d in range(count)])  23.2 us
    pallas_call x1, Pallas kernels, turn(): pl.pallas_call(turn_kernel, grid=(STEPS,), in_specs=[plane_spec(), whole(...  16.9 us
    ppermute x7, starting transfers between devices, per_device(): lax.ppermute(gram, AXES, [(d, d ^ flip) for d in range(count)])  7.83 us
    pallas_call x1, Pallas kernels, prep(): pl.pallas_call(prep_kernel, in_specs=[vmem, pl.BlockSpec(memory_space=plt...  7.73 us
    unnamed x23, local copies, waits for them, and re-layouts  7.72 us
    pallas_call x1, Pallas kernels, make_second(): pl.pallas_call(second_kernel, grid=(STEPS,), in_specs=[plane_spec(), halo...  4.96 us
  transfers between devices with their start and end apart: 29, of which 12 were waited for; matrix products, arithmetic and copies ran while one was open for 6% of the time, Pallas kernels for 13%

profile of v4, /device:TPU:0, one launch (start us, length us, event | category | flops | bytes accessed | tf_op | source)
XLA Modules:
  0.0 182.9 jit_solution(2165696199907521682)
XLA Ops:
  2.7 1.6 collective-permute-start
  4.3 7.1 %collective-permute-start.1 = (f32[4,768]{1,0:T(4,128)S(1)}, f32[4,768]{1,0:T(4,128)S(1)}, u32[]{:S(2)}, u32[]{:S(2)}) collective-permute-start(f32[4,768]{1,0:T(4,128)S(1)} %maximum_maximum_fusion), channel_id=1, source_target_pairs={{0,31},{1,0},{2,1},{3,2},{4,3},{5,4},{6,5},{7,6},{8,7},{9,8},{10,9... | collective-permute-start | bytes 36872 | tf_op jit(solution)/shard_map/ppermute | solution.py:664
  11.4 1.6 copy-done
  13.0 2.2 %pack.1 = (f32[6,192,128]{2,1,0:T(8,128)}, f32[8,192,128]{2,1,0:T(8,128)S(1)}, f32[2,192,128]{2,1,0:T(8,128)S(1)}, f32[16,64,128]{2,1,0:T(8,128)S(1)}, f32[6,16,...) custom-call(f32[16,256,128]{2,1,0:T(8,128)S(1)} %bitcast.18), custom_call_target="tpu_custom_call" | custom-call | flops 4294967296 | bytes 6291456 | tf_op jit(solution)/shard_map/pack/pallas_call | solution.py:140
  22.4 1.4 pad_maximum_fusion.1
  26.9 8.4 %collective-permute-done.2 = f32[104,128]{1,0:T(8,128)} collective-permute-done((f32[104,128]{1,0:T(8,128)}, f32[104,128]{1,0:T(8,128)}, u32[]{:S(2)}, u32[]{:S(2)}) %collective-permute-start.2) | collective-permute-done | bytes 53280 | tf_op jit(solution)/shard_map/ppermute | solution.py:664
  36.7 1.4 reshape.36
  39.2 7.7 %collective-permute-start.13 = (f32[6,16,16,128]{3,2,1,0:T(8,128)S(1)}, f32[6,16,16,128]{3,2,1,0:T(8,128)S(1)}, u32[]{:S(2)}, u32[]{:S(2)}) collective-permute-start(f32[6,16,16,128]{3,2,1,0:T(8,128)S(1)} %get-tuple-element.54), channel_id=1, source_target_pairs={{0,31},{1,0},{2,1},{3,2},{4,3},{5,4},{6,5},{7,6},{8,7},{9,8},{10,9... | collective-permute-start | bytes 2359304 | tf_op jit(solution)/shard_map/ppermute | solution.py:664
  48.0 3.2 %side_x.1.part_ref = f32[16,256,128]{2,1,0:T(8,128)S(1)} custom-call(f32[16,256,128]{2,1,0:T(8,128)S(1)} %bitcast.19, f32[16,256,128]{2,1,0:T(8,128)} %collective-permute-done.4.mate_ref), custom_call_target="tpu_custom_call" | custom-call | flops 16777216 | bytes 6291456 | tf_op jit(solution)/shard_map/side_x/pallas_call | solution.py:177
  51.3 7.7 %prep.1 = (bf16[2,4096,128]{2,1,0:T(8,128)(2,1)S(1)}, f32[3,48,128]{2,1,0:T(8,128)S(1)}) custom-call(f32[128,768]{1,0:T(8,128)S(1)} %pad_maximum_fusion.near_ref, s32[2]{0:T(128)S(1)} %pad_add_fusion.corner_ref, f32[4096,128]{1,0:T(8,128)S(1)} %copy-done.3, f32[4096,128]{1,0:T(8,128)S(1)} %bitcast.20), custom_call_target="tpu_custom_call" | custom-call | flops 134217728 | bytes 10485760 | tf_op jit(solution)/shard_map/prep/pallas_call | solution.py:373
  60.5 7.7 %collective-permute-start.8 = (f32[48,128]{1,0:T(8,128)S(1)}, f32[48,128]{1,0:T(8,128)S(1)}, u32[]{:S(2)}, u32[]{:S(2)}) collective-permute-start(f32[48,128]{1,0:T(8,128)S(1)} %get-tuple-element.71), channel_id=1, source_target_pairs={{0,31},{1,0},{2,1},{3,2},{4,3},{5,4},{6,5},{7,6},{8,7},{9,8},{10,9... | collective-permute-start | bytes 73736 | tf_op jit(solution)/shard_map/ppermute | solution.py:664
  68.2 1.8 %collective-permute-done.7.below_ref = f32[48,128]{1,0:T(8,128)S(1)} collective-permute-done((f32[48,128]{1,0:T(8,128)S(1)}, f32[48,128]{1,0:T(8,128)S(1)}, u32[]{:S(2)}, u32[]{:S(2)}) %collective-permute-start.7) | collective-permute-done | bytes 24608 | tf_op jit(solution)/shard_map/ppermute | solution.py:664
  72.2 6.8 %collective-permute-done.9.other_ref = f32[48,128]{1,0:T(8,128)S(1)} collective-permute-done((f32[48,128]{1,0:T(8,128)S(1)}, f32[48,128]{1,0:T(8,128)S(1)}, u32[]{:S(2)}, u32[]{:S(2)}) %collective-permute-start.9) | collective-permute-done | bytes 24608 | tf_op jit(solution)/shard_map/ppermute | solution.py:664
  79.1 7.7 %collective-permute-start.16 = (f32[16,128]{1,0:T(8,128)S(1)}, f32[16,128]{1,0:T(8,128)S(1)}, u32[]{:S(2)}, u32[]{:S(2)}) collective-permute-start(f32[16,128]{1,0:T(8,128)S(1)} %get-tuple-element.67.one_ref.rest_4_), channel_id=1, source_target_pairs={{0,31},{1,0},{2,1},{3,2},{4,3},{5,4},{6,5},{7,6},{8,7},{9,8},{10,9... | collective-permute-start | bytes 24584 | tf_op jit(solution)/shard_map/ppermute | solution.py:664
  86.9 3.1 %side_z.1.side_ref = f32[16,256,128]{2,1,0:T(8,128)S(1)} custom-call(f32[16,256,128]{2,1,0:T(8,128)S(1)} %bitcast.21, f32[16,256,128]{2,1,0:T(8,128)S(1)} %side_x.1.part_ref, f32[6,16,16,128]{3,2,1,0:T(8,128)S(1)} %collective-permute-done.12.low_ref, f32[6,16,16,128]{3,2,1,0:T(8,128)S(1)} %collective-permute-done.13.high_ref), custom_call_target="tpu_custom_call" | custom-call | flops 16777216 | bytes 8388608 | tf_op jit(solution)/shard_map/side_z/pallas_call | solution.py:202
  90.0 2.2 %first.1 = (f32[16,256,128]{2,1,0:T(8,128)S(1)}, f32[16,256,128]{2,1,0:T(8,128)S(1)}, f32[6,16,16,128]{3,2,1,0:T(8,128)S(1)}, f32[6,16,16,128]{3,2,1,0:T(8,128)S(1)}) custom-call(f32[16,256,128]{2,1,0:T(8,128)S(1)} %bitcast.22, f32[16,256,128]{2,1,0:T(8,128)S(1)} %side_z.1.side_ref, f32[16,256,128]{2,1,0:T(8,128)S(1)} %bitcast.24, ...), custom_call_target="tpu_custom_call" | custom-call | flops 16777216 | bytes 14680064 | tf_op jit(solution)/shard_map/first/pallas_call | solution.py:449
  92.4 7.7 %collective-permute-start.19 = (f32[6,16,16,128]{3,2,1,0:T(8,128)S(1)}, f32[6,16,16,128]{3,2,1,0:T(8,128)S(1)}, u32[]{:S(2)}, u32[]{:S(2)}) collective-permute-start(f32[6,16,16,128]{3,2,1,0:T(8,128)S(1)} %get-tuple-element.63), channel_id=1, source_target_pairs={{0,31},{1,0},{2,1},{3,2},{4,3},{5,4},{6,5},{7,6},{8,7},{9,8},{10,9... | collective-permute-start | bytes 2359304 | tf_op jit(solution)/shard_map/ppermute | solution.py:664
  101.3 7.7 %collective-permute-start.21 = (f32[16,128]{1,0:T(8,128)S(1)}, f32[16,128]{1,0:T(8,128)S(1)}, u32[]{:S(2)}, u32[]{:S(2)}) collective-permute-start(f32[16,128]{1,0:T(8,128)S(1)} %again.1.rest_1_), channel_id=1, source_target_pairs={{0,31},{1,0},{2,1},{3,2},{4,3},{5,4},{6,5},{7,6},{8,7},{9,8},{10,9... | collective-permute-start | bytes 24584 | tf_op jit(solution)/shard_map/ppermute | solution.py:664
  110.6 2.9 %side_again.1.part_ref = f32[16,256,128]{2,1,0:T(8,128)S(1)} custom-call(f32[16,256,128]{2,1,0:T(8,128)S(1)} %get-tuple-element.61.s_ref, f32[16,256,128]{2,1,0:T(8,128)S(1)} %collective-permute-done.17.mate_ref), custom_call_target="tpu_custom_call" | custom-call | flops 33554432 | bytes 6291456 | tf_op jit(solution)/shard_map/side_again/pallas_call | solution.py:229
  113.5 13.6 %collective-permute-done.11.mid_ref = f32[16,64,128]{2,1,0:T(8,128)S(1)} collective-permute-done((f32[16,64,128]{2,1,0:T(8,128)S(1)}, f32[16,64,128]{2,1,0:T(8,128)S(1)}, u32[]{:S(2)}, u32[]{:S(2)}) %collective-permute-start.11) | collective-permute-done | bytes 524320 | tf_op jit(solution)/shard_map/ppermute | solution.py:664
  127.1 2.8 %base.1.base_ref = f32[16,256,128]{2,1,0:T(8,128)S(1)} custom-call(f32[16,256,128]{2,1,0:T(8,128)S(1)} %bitcast.23, f32[16,64,128]{2,1,0:T(8,128)S(1)} %collective-permute-done.11.mid_ref, f32[16,256,128]{2,1,0:T(8,128)S(1)} %bitcast.25, f32[16,256,128]{2,1,0:T(8,128)S(1)} %bitcast.28, f32[16,256,128]{2,1,0:T(8,128)S(1)} %get-tuple-element.60.q_ref, ...), custom_call_target="tpu_custom_call" | custom-call | flops 33554432 | bytes 16777216 | tf_op jit(solution)/shard_map/base/pallas_call | solution.py:490
  129.9 5.0 %second.1 = (f32[16,256,128]{2,1,0:T(8,128)S(1)}, f32[128,128]{1,0:T(8,128)S(1)}) custom-call(f32[16,256,128]{2,1,0:T(8,128)S(1)} %base.1.base_ref, f32[6,16,16,128]{3,2,1,0:T(8,128)S(1)} %collective-permute-done.18.low_ref, f32[6,16,16,128]{3,2,1,0:T(8,128)S(1)} %collective-permute-done.19.high_ref, bf16[2,16,256,128]{3,2,1,0:T(8,128)(2,1)S(1)} %bitcast.26, ...), custom_call_target="tpu_custom_call" | custom-call | flops 134217728 | bytes 8388608 | tf_op jit(solution)/shard_map/second/pallas_call | solution.py:547
  136.2 1.6 collective-permute-start.23
  137.9 2.7 %collective-permute-done.23 = f32[128,128]{1,0:T(8,128)S(1)} collective-permute-done((f32[128,128]{1,0:T(8,128)S(1)}, f32[128,128]{1,0:T(8,128)S(1)}, u32[]{:S(2)}, u32[]{:S(2)}) %collective-permute-start.23) | collective-permute-done | bytes 65568 | tf_op jit(solution)/shard_map/ppermute | solution.py:722
  140.6 3.0 %collective-permute-start.24 = (f32[128,128]{1,0:T(8,128)S(1)}, f32[128,128]{1,0:T(8,128)S(1)}, u32[]{:S(2)}, u32[]{:S(2)}) collective-permute-start(f32[128,128]{1,0:T(8,128)S(1)} %add.26), channel_id=1, source_target_pairs={{0,36},{1,37},{2,38},{3,39},{4,32},{5,33},{6,34},{7,35},{8,44},{9,... | collective-permute-start | bytes 196616 | tf_op jit(solution)/shard_map/ppermute | solution.py:722
  143.6 2.6 %collective-permute-done.24 = f32[128,128]{1,0:T(8,128)S(1)} collective-permute-done((f32[128,128]{1,0:T(8,128)S(1)}, f32[128,128]{1,0:T(8,128)S(1)}, u32[]{:S(2)}, u32[]{:S(2)}) %collective-permute-start.24) | collective-permute-done | bytes 65568 | tf_op jit(solution)/shard_map/ppermute | solution.py:722
  146.3 4.3 %collective-permute-done.25 = f32[128,128]{1,0:T(8,128)S(1)} collective-permute-done((f32[128,128]{1,0:T(8,128)S(1)}, f32[128,128]{1,0:T(8,128)S(1)}, u32[]{:S(2)}, u32[]{:S(2)}) %collective-permute-start.25) | collective-permute-done | bytes 65568 | tf_op jit(solution)/shard_map/ppermute | solution.py:722
  150.5 2.1 %collective-permute-start.26 = (f32[128,128]{1,0:T(8,128)S(1)}, f32[128,128]{1,0:T(8,128)S(1)}, u32[]{:S(2)}, u32[]{:S(2)}) collective-permute-start(f32[128,128]{1,0:T(8,128)S(1)} %add.28), channel_id=1, source_target_pairs={{0,3},{1,2},{2,1},{3,0},{4,7},{5,6},{6,5},{7,4},{8,11},{9,10},{10,... | collective-permute-start | bytes 196616 | tf_op jit(solution)/shard_map/ppermute | solution.py:722
  152.7 3.4 %collective-permute-done.26 = f32[128,128]{1,0:T(8,128)S(1)} collective-permute-done((f32[128,128]{1,0:T(8,128)S(1)}, f32[128,128]{1,0:T(8,128)S(1)}, u32[]{:S(2)}, u32[]{:S(2)}) %collective-permute-start.26) | collective-permute-done | bytes 65568 | tf_op jit(solution)/shard_map/ppermute | solution.py:722
  156.2 4.3 %collective-permute-done.27 = f32[128,128]{1,0:T(8,128)S(1)} collective-permute-done((f32[128,128]{1,0:T(8,128)S(1)}, f32[128,128]{1,0:T(8,128)S(1)}, u32[]{:S(2)}, u32[]{:S(2)}) %collective-permute-start.27) | collective-permute-done | bytes 65568 | tf_op jit(solution)/shard_map/ppermute | solution.py:722
  161.3 4.7 %collective-permute-done.28 = f32[128,128]{1,0:T(8,128)S(1)} collective-permute-done((f32[128,128]{1,0:T(8,128)S(1)}, f32[128,128]{1,0:T(8,128)S(1)}, u32[]{:S(2)}, u32[]{:S(2)}) %collective-permute-start.28) | collective-permute-done | bytes 65568 | tf_op jit(solution)/shard_map/ppermute | solution.py:722
  166.0 16.9 %turn.1 = f32[16,256,128]{2,1,0:T(8,128)} custom-call(f32[16,256,128]{2,1,0:T(8,128)S(1)} %get-tuple-element.69.second_ref, f32[128,128]{1,0:T(8,128)S(1)} %add_multiply_fusion.gram_ref), custom_call_target="tpu_custom_call" | custom-call | flops 268435456 | bytes 4194304 | tf_op jit(solution)/shard_map/turn/pallas_call | solution.py:641
  (91 shorter events, 25.5 us)
Async XLA Ops:
  0.0 48.0 %collective-permute-start.4 = (f32[16,256,128]{2,1,0:T(8,128)}, f32[16,256,128]{2,1,0:T(8,128)}, u32[]{:S(2)}, u32[]{:S(2)}) collective-permute-start(f32[16,256,128]{2,1,0:T(8,128)} %bitcast.17), channel_id=1, source_target_pairs={{0,64},{1,65},{2,66},{3,67},{4,68},{5,69},{6,70},{7,71},{8,72},{9,... | collective-permute-start | bytes 6291464 | tf_op jit(solution)/shard_map/ppermute | solution.py:664
  2.7 17.8 %collective-permute-start = (f32[4,768]{1,0:T(4,128)S(1)}, f32[4,768]{1,0:T(4,128)S(1)}, u32[]{:S(2)}, u32[]{:S(2)}) collective-permute-start(f32[4,768]{1,0:T(4,128)S(1)} %maximum_maximum_fusion), channel_id=1, source_target_pairs={{0,1},{1,2},{2,3},{3,4},{4,5},{5,6},{6,7},{7,8},{8,9},{9,10},{10,1... | collective-permute-start | bytes 36872 | tf_op jit(solution)/shard_map/ppermute | solution.py:664
  4.3 16.2 %collective-permute-start.1 = (f32[4,768]{1,0:T(4,128)S(1)}, f32[4,768]{1,0:T(4,128)S(1)}, u32[]{:S(2)}, u32[]{:S(2)}) collective-permute-start(f32[4,768]{1,0:T(4,128)S(1)} %maximum_maximum_fusion), channel_id=1, source_target_pairs={{0,31},{1,0},{2,1},{3,2},{4,3},{5,4},{6,5},{7,6},{8,7},{9,8},{10,9... | collective-permute-start | bytes 36872 | tf_op jit(solution)/shard_map/ppermute | solution.py:664
  18.4 29.6 %copy-start.1 = (f32[16,16,16,128]{3,2,1,0:T(8,128)S(1)}, f32[16,16,16,128]{3,2,1,0:T(8,128)}, u32[]{:S(2)}) copy-start(f32[16,16,16,128]{3,2,1,0:T(8,128)} %param.5) | copy-start | bytes 6291460
  18.4 32.8 %collective-permute-start.5 = (f32[6,192,128]{2,1,0:T(8,128)}, f32[6,192,128]{2,1,0:T(8,128)S(1)}, u32[]{:S(2)}, u32[]{:S(2)}) collective-permute-start(f32[6,192,128]{2,1,0:T(8,128)} %get-tuple-element.45), channel_id=1, source_target_pairs={{0,32},{1,33},{2,34},{3,35},{4,36},{5,37},{6,38},{7,39},{8,40},{9,... | collective-permute-start | bytes 1769480 | tf_op jit(solution)/shard_map/ppermute | solution.py:664
  23.8 11.5 %collective-permute-start.2 = (f32[104,128]{1,0:T(8,128)}, f32[104,128]{1,0:T(8,128)}, u32[]{:S(2)}, u32[]{:S(2)}) collective-permute-start(f32[104,128]{1,0:T(8,128)} %pad_maximum_fusion.1), channel_id=1, source_target_pairs={{0,32},{1,33},{2,34},{3,35},{4,36},{5,37},{6,38},{7,39},{8,40},{9,... | collective-permute-start | bytes 159752 | tf_op jit(solution)/shard_map/ppermute | solution.py:664
  39.0 7.9 %collective-permute-start.3 = (f32[3,8,768]{2,1,0:T(8,128)S(1)}, f32[3,8,768]{2,1,0:T(8,128)S(1)}, u32[]{:S(2)}, u32[]{:S(2)}) collective-permute-start(f32[3,8,768]{2,1,0:T(8,128)S(1)} %maximum_select_fusion.1), channel_id=1, source_target_pairs={{0,64},{1,65},{2,66},{3,67},{4,68},{5,69},{6,70},{7,71},{8,72},{9,... | collective-permute-start | bytes 221192 | tf_op jit(solution)/shard_map/ppermute | solution.py:664
  39.1 47.7 %collective-permute-start.12 = (f32[6,16,16,128]{3,2,1,0:T(8,128)}, f32[6,16,16,128]{3,2,1,0:T(8,128)S(1)}, u32[]{:S(2)}, u32[]{:S(2)}) collective-permute-start(f32[6,16,16,128]{3,2,1,0:T(8,128)} %copy-done.4), channel_id=1, source_target_pairs={{0,1},{1,2},{2,3},{3,4},{4,5},{5,6},{6,7},{7,8},{8,9},{9,10},{10,1... | collective-permute-start | bytes 2359304 | tf_op jit(solution)/shard_map/ppermute | solution.py:664
  39.2 47.7 %collective-permute-start.13 = (f32[6,16,16,128]{3,2,1,0:T(8,128)S(1)}, f32[6,16,16,128]{3,2,1,0:T(8,128)S(1)}, u32[]{:S(2)}, u32[]{:S(2)}) collective-permute-start(f32[6,16,16,128]{3,2,1,0:T(8,128)S(1)} %get-tuple-element.54), channel_id=1, source_target_pairs={{0,31},{1,0},{2,1},{3,2},{4,3},{5,4},{6,5},{7,6},{8,7},{9,8},{10,9... | collective-permute-start | bytes 2359304 | tf_op jit(solution)/shard_map/ppermute | solution.py:664
  46.9 32.2 %collective-permute-start.10 = (f32[8,192,128]{2,1,0:T(8,128)}, f32[8,192,128]{2,1,0:T(8,128)S(1)}, u32[]{:S(2)}, u32[]{:S(2)}) collective-permute-start(f32[8,192,128]{2,1,0:T(8,128)} %copy-done.5), channel_id=1, source_target_pairs={{0,32},{1,33},{2,34},{3,35},{4,36},{5,37},{6,38},{7,39},{8,40},{9,... | collective-permute-start | bytes 2359304 | tf_op jit(solution)/shard_map/ppermute | solution.py:664
  51.3 19.9 %copy-start.9 = (f32[2,192,128]{2,1,0:T(8,128)S(1)}, f32[2,192,128]{2,1,0:T(8,128)}, u32[]{:S(2)}) copy-start(f32[2,192,128]{2,1,0:T(8,128)} %copy-done.8) | copy-start | bytes 589828
  59.0 1.3 collective-permute-start.6
  60.4 9.6 %collective-permute-start.7 = (f32[48,128]{1,0:T(8,128)S(1)}, f32[48,128]{1,0:T(8,128)S(1)}, u32[]{:S(2)}, u32[]{:S(2)}) collective-permute-start(f32[48,128]{1,0:T(8,128)S(1)} %get-tuple-element.72), channel_id=1, source_target_pairs={{0,1},{1,2},{2,3},{3,4},{4,5},{5,6},{6,7},{7,8},{8,9},{9,10},{10,1... | collective-permute-start | bytes 73736 | tf_op jit(solution)/shard_map/ppermute | solution.py:664
  60.5 9.6 %collective-permute-start.8 = (f32[48,128]{1,0:T(8,128)S(1)}, f32[48,128]{1,0:T(8,128)S(1)}, u32[]{:S(2)}, u32[]{:S(2)}) collective-permute-start(f32[48,128]{1,0:T(8,128)S(1)} %get-tuple-element.71), channel_id=1, source_target_pairs={{0,31},{1,0},{2,1},{3,2},{4,3},{5,4},{6,5},{7,6},{8,7},{9,8},{10,9... | collective-permute-start | bytes 73736 | tf_op jit(solution)/shard_map/ppermute | solution.py:664
  70.1 8.9 %collective-permute-start.9 = (f32[48,128]{1,0:T(8,128)S(1)}, f32[48,128]{1,0:T(8,128)S(1)}, u32[]{:S(2)}, u32[]{:S(2)}) collective-permute-start(f32[48,128]{1,0:T(8,128)S(1)} %merge.1.own_ref), channel_id=1, source_target_pairs={{0,32},{1,33},{2,34},{3,35},{4,36},{5,37},{6,38},{7,39},{8,40},{9,... | collective-permute-start | bytes 73736 | tf_op jit(solution)/shard_map/ppermute | solution.py:664
  71.1 18.8 %collective-permute-start.14 = (f32[2,192,128]{2,1,0:T(8,128)S(1)}, f32[2,192,128]{2,1,0:T(8,128)S(1)}, u32[]{:S(2)}, u32[]{:S(2)}) collective-permute-start(f32[2,192,128]{2,1,0:T(8,128)S(1)} %copy-done.9), channel_id=1, source_target_pairs={{0,32},{1,33},{2,34},{3,35},{4,36},{5,37},{6,38},{7,39},{8,40},{9,... | collective-permute-start | bytes 589832 | tf_op jit(solution)/shard_map/ppermute | solution.py:664
  79.1 10.8 %collective-permute-start.15 = (f32[16,128]{1,0:T(8,128)S(1)}, f32[16,128]{1,0:T(8,128)S(1)}, u32[]{:S(2)}, u32[]{:S(2)}) collective-permute-start(f32[16,128]{1,0:T(8,128)S(1)} %get-tuple-element.67.one_ref.rest_4_), channel_id=1, source_target_pairs={{0,1},{1,2},{2,3},{3,4},{4,5},{5,6},{6,7},{7,8},{8,9},{9,10},{10,1... | collective-permute-start | bytes 24584 | tf_op jit(solution)/shard_map/ppermute | solution.py:664
  79.1 10.8 %collective-permute-start.16 = (f32[16,128]{1,0:T(8,128)S(1)}, f32[16,128]{1,0:T(8,128)S(1)}, u32[]{:S(2)}, u32[]{:S(2)}) collective-permute-start(f32[16,128]{1,0:T(8,128)S(1)} %get-tuple-element.67.one_ref.rest_4_), channel_id=1, source_target_pairs={{0,31},{1,0},{2,1},{3,2},{4,3},{5,4},{6,5},{7,6},{8,7},{9,8},{10,9... | collective-permute-start | bytes 24584 | tf_op jit(solution)/shard_map/ppermute | solution.py:664
  90.0 10.1 %copy-start.7 = (f32[16,64,128]{2,1,0:T(8,128)S(1)}, f32[16,64,128]{2,1,0:T(8,128)}, u32[]{:S(2)}) copy-start(f32[16,64,128]{2,1,0:T(8,128)} %copy-done.6) | copy-start | bytes 1572868
  92.2 9.1 %collective-permute-start.17 = (f32[16,256,128]{2,1,0:T(8,128)S(1)}, f32[16,256,128]{2,1,0:T(8,128)S(1)}, u32[]{:S(2)}, u32[]{:S(2)}) collective-permute-start(f32[16,256,128]{2,1,0:T(8,128)S(1)} %get-tuple-element.61.s_ref), channel_id=1, source_target_pairs={{0,64},{1,65},{2,66},{3,67},{4,68},{5,69},{6,70},{7,71},{8,72},{9,... | collective-permute-start | bytes 6291464 | tf_op jit(solution)/shard_map/ppermute | solution.py:664
  92.3 37.6 %collective-permute-start.18 = (f32[6,16,16,128]{3,2,1,0:T(8,128)S(1)}, f32[6,16,16,128]{3,2,1,0:T(8,128)S(1)}, u32[]{:S(2)}, u32[]{:S(2)}) collective-permute-start(f32[6,16,16,128]{3,2,1,0:T(8,128)S(1)} %get-tuple-element.62), channel_id=1, source_target_pairs={{0,1},{1,2},{2,3},{3,4},{4,5},{5,6},{6,7},{7,8},{8,9},{9,10},{10,1... | collective-permute-start | bytes 2359304 | tf_op jit(solution)/shard_map/ppermute | solution.py:664
  92.4 37.5 %collective-permute-start.19 = (f32[6,16,16,128]{3,2,1,0:T(8,128)S(1)}, f32[6,16,16,128]{3,2,1,0:T(8,128)S(1)}, u32[]{:S(2)}, u32[]{:S(2)}) collective-permute-start(f32[6,16,16,128]{3,2,1,0:T(8,128)S(1)} %get-tuple-element.63), channel_id=1, source_target_pairs={{0,31},{1,0},{2,1},{3,2},{4,3},{5,4},{6,5},{7,6},{8,7},{9,8},{10,9... | collective-permute-start | bytes 2359304 | tf_op jit(solution)/shard_map/ppermute | solution.py:664
  100.1 26.9 %collective-permute-start.11 = (f32[16,64,128]{2,1,0:T(8,128)S(1)}, f32[16,64,128]{2,1,0:T(8,128)S(1)}, u32[]{:S(2)}, u32[]{:S(2)}) collective-permute-start(f32[16,64,128]{2,1,0:T(8,128)S(1)} %copy-done.7), channel_id=1, source_target_pairs={{0,32},{1,33},{2,34},{3,35},{4,36},{5,37},{6,38},{7,39},{8,40},{9,... | collective-permute-start | bytes 1572872 | tf_op jit(solution)/shard_map/ppermute | solution.py:664
  101.2 28.7 %collective-permute-start.20 = (f32[16,128]{1,0:T(8,128)S(1)}, f32[16,128]{1,0:T(8,128)S(1)}, u32[]{:S(2)}, u32[]{:S(2)}) collective-permute-start(f32[16,128]{1,0:T(8,128)S(1)} %again.1.rest_1_), channel_id=1, source_target_pairs={{0,1},{1,2},{2,3},{3,4},{4,5},{5,6},{6,7},{7,8},{8,9},{9,10},{10,1... | collective-permute-start | bytes 24584 | tf_op jit(solution)/shard_map/ppermute | solution.py:664
  101.3 28.6 %collective-permute-start.21 = (f32[16,128]{1,0:T(8,128)S(1)}, f32[16,128]{1,0:T(8,128)S(1)}, u32[]{:S(2)}, u32[]{:S(2)}) collective-permute-start(f32[16,128]{1,0:T(8,128)S(1)} %again.1.rest_1_), channel_id=1, source_target_pairs={{0,31},{1,0},{2,1},{3,2},{4,3},{5,4},{6,5},{7,6},{8,7},{9,8},{10,9... | collective-permute-start | bytes 24584 | tf_op jit(solution)/shard_map/ppermute | solution.py:664
  134.9 1.3 collective-permute-start.22
  136.2 4.3 %collective-permute-start.23 = (f32[128,128]{1,0:T(8,128)S(1)}, f32[128,128]{1,0:T(8,128)S(1)}, u32[]{:S(2)}, u32[]{:S(2)}) collective-permute-start(f32[128,128]{1,0:T(8,128)S(1)} %add.25), channel_id=1, source_target_pairs={{0,32},{1,33},{2,34},{3,35},{4,36},{5,37},{6,38},{7,39},{8,40},{9,... | collective-permute-start | bytes 196616 | tf_op jit(solution)/shard_map/ppermute | solution.py:722
  140.6 5.6 %collective-permute-start.24 = (f32[128,128]{1,0:T(8,128)S(1)}, f32[128,128]{1,0:T(8,128)S(1)}, u32[]{:S(2)}, u32[]{:S(2)}) collective-permute-start(f32[128,128]{1,0:T(8,128)S(1)} %add.26), channel_id=1, source_target_pairs={{0,36},{1,37},{2,38},{3,39},{4,32},{5,33},{6,34},{7,35},{8,44},{9,... | collective-permute-start | bytes 196616 | tf_op jit(solution)/shard_map/ppermute | solution.py:722
  146.2 4.3 %collective-permute-start.25 = (f32[128,128]{1,0:T(8,128)S(1)}, f32[128,128]{1,0:T(8,128)S(1)}, u32[]{:S(2)}, u32[]{:S(2)}) collective-permute-start(f32[128,128]{1,0:T(8,128)S(1)} %add.27), channel_id=1, source_target_pairs={{0,1},{1,0},{2,3},{3,2},{4,5},{5,4},{6,7},{7,6},{8,9},{9,8},{10,11... | collective-permute-start | bytes 196616 | tf_op jit(solution)/shard_map/ppermute | solution.py:722
  150.5 5.6 %collective-permute-start.26 = (f32[128,128]{1,0:T(8,128)S(1)}, f32[128,128]{1,0:T(8,128)S(1)}, u32[]{:S(2)}, u32[]{:S(2)}) collective-permute-start(f32[128,128]{1,0:T(8,128)S(1)} %add.28), channel_id=1, source_target_pairs={{0,3},{1,2},{2,1},{3,0},{4,7},{5,6},{6,5},{7,4},{8,11},{9,10},{10,... | collective-permute-start | bytes 196616 | tf_op jit(solution)/shard_map/ppermute | solution.py:722
  156.1 4.3 %collective-permute-start.27 = (f32[128,128]{1,0:T(8,128)S(1)}, f32[128,128]{1,0:T(8,128)S(1)}, u32[]{:S(2)}, u32[]{:S(2)}) collective-permute-start(f32[128,128]{1,0:T(8,128)S(1)} %add.29), channel_id=1, source_target_pairs={{0,8},{1,9},{2,10},{3,11},{4,12},{5,13},{6,14},{7,15},{8,0},{9,1},... | collective-permute-start | bytes 196616 | tf_op jit(solution)/shard_map/ppermute | solution.py:722
  160.5 5.6 %collective-permute-start.28 = (f32[128,128]{1,0:T(8,128)S(1)}, f32[128,128]{1,0:T(8,128)S(1)}, u32[]{:S(2)}, u32[]{:S(2)}) collective-permute-start(f32[128,128]{1,0:T(8,128)S(1)} %add.30), channel_id=1, source_target_pairs={{0,24},{1,25},{2,26},{3,27},{4,28},{5,29},{6,30},{7,31},{8,16},{9,... | collective-permute-start | bytes 196616 | tf_op jit(solution)/shard_map/ppermute | solution.py:722
  (8 other events, 10.0 us)

commit v5 on v4

--- a/solution.py
+++ b/solution.py
@@ -73,7 +73,7 @@
 B = 4
 STEPS = C // B
 N = 2
-CUTS = (0, 6, 14, 16)
+CUTS = (0, 6, 16)
 
 
 def stride_rows(z):
@@ -113,6 +113,7 @@
 
 
 FULL = sds((C, ROWS, S))
+FULL_ROWS = sds((CELLS, S))
 HALO = sds((H, C, C, S))
 EDGES = [sds((stop - start, 192, S)) for start, stop in zip(CUTS, CUTS[1:])]
 
@@ -121,15 +122,16 @@
     return slice(y * C + half * 8, y * C + half * 8 + 8)
 
 
-def pack_kernel(s_ref, *refs):
-    mid_ref, head_ref, tail_ref = refs[3:]
-
-    def edges(out_ref):
-        out_ref[:, 0:96, :] = s_ref[:, 0:96, :]
-        out_ref[:, 96:192, :] = s_ref[:, 160:256, :]
-
-    for_piece(refs[:3], edges)
-    mid_ref[...] = s_ref[:, 96:160, :]
+def pack_edges(s_ref, out_ref):
+    out_ref[:, 0:96, :] = s_ref[:, 0:96, :]
+    out_ref[:, 96:192, :] = s_ref[:, 160:256, :]
+
+
+def pack_kernel(s_ref, edge_ref, head_ref, tail_ref):
+    @pl.when(pl.program_id(0) < CUTS[1] // N)
+    def _():
+        pack_edges(s_ref, edge_ref)
+
     for p in range(N):
         for z in range(H):
             head_ref[z, p] = s_ref[p, stride_rows(z), :]
@@ -141,12 +143,45 @@
         pack_kernel,
         grid=(C // N,),
         in_specs=[plane_spec(ROWS, N)],
-        out_specs=edge_specs() + [plane_spec(64, N), halo_spec(N), halo_spec(N)],
-        out_shape=EDGES + [sds((C, 64, S)), HALO, HALO],
+        out_specs=edge_specs()[:1] + [halo_spec(N), halo_spec(N)],
+        out_shape=EDGES[:1] + [HALO, HALO],
         compiler_params=params(12),
         cost_estimate=cost(1 << 32, 6 << 20),
         name="pack",
     )(s)
+
+
+def pack_rest_kernel(s_ref, edge_ref, mid_ref):
+    @pl.when(pl.program_id(0) >= CUTS[1] // N)
+    def _():
+        pack_edges(s_ref, edge_ref)
+
+    mid_ref[...] = s_ref[:, 96:160, :]
+
+
+def pack_rest(s):
+    return pl.pallas_call(
+        pack_rest_kernel,
+        grid=(C // N,),
+        in_specs=[plane_spec(ROWS, N)],
+        out_specs=edge_specs()[1:] + [plane_spec(64, N)],
+        out_shape=EDGES[1:] + [sds((C, 64, S))],
+        compiler_params=params(12),
+        cost_estimate=cost(1 << 31, 4 << 20),
+        name="pack_rest",
+    )(s)
+
+
+def stack_kernel(*refs):
+    start = 0
+    for ref in refs[:-1]:
+        refs[-1][start : start + ref.shape[0], :] = ref[...]
+        start += ref.shape[0]
+
+
+def stack(*arrays):
+    rows = sum(a.shape[0] for a in arrays)
+    return pl.pallas_call(stack_kernel, out_shape=sds((rows, S)), compiler_params=params(4), name="stack")(*arrays)
 
 
 def along_x(s_ref, mate_ref, out_ref, add):
@@ -252,30 +287,44 @@
     return masks, factors
 
 
-def spread_rows(pot_ref, vb_ref):
-    def spread(row, _):
-        line = (pot_ref[pl.ds(row, 1), :] + (DIAGONAL - filter_centre)) * (1.0 / filter_half)
+def spread_kernel(parcel_ref, vb_ref):
+    def spread_row(row, _):
+        line = (parcel_ref[pl.ds(72 + row, 1), :] + (DIAGONAL - filter_centre)) * (1.0 / filter_half)
         start = pl.multiple_of(row * 128, 128)
         vb_ref[pl.ds(start, 128), :] = jnp.broadcast_to(line, (128, 128)).T
         return 0
 
-    lax.fori_loop(0, CELLS // 128, spread, 0, unroll=8)
-
-
-def spread(pot):
-    return pl.pallas_call(
-        spread_rows,
-        out_shape=sds((CELLS, S)),
+    lax.fori_loop(0, CELLS // 128, spread_row, 0, unroll=8)
+
+
+def spread(parcel):
+    return pl.pallas_call(
+        spread_kernel,
+        out_shape=FULL_ROWS,
         compiler_params=params(8),
         cost_estimate=cost(1 << 20, 2 << 20),
         name="spread",
-    )(pot)
-
-
-def prep_kernel(near_ref, corner_ref, vb_ref, s_ref, gg_ref, coef_ref, table_ref, a1_ref, a1z_ref, a2_ref, a2s_ref):
+    )(parcel)
+
+
+def prep_kernel(*refs):
+    parcels = refs[:4]
+    corner_ref, vb_ref, s_ref, gg_ref, coef_ref, energy_ref, near_ref, table_ref, a1_ref, a1z_ref, a2_ref, a2s_ref = refs[4:]
+    upper_x, upper_y = corner_ref[0] > 0, corner_ref[1] > 0
+    for slab in range(3):
+        own, over_x, over_y, over_xy = [parcel[slab * 24 : slab * 24 + 24, :] for parcel in parcels]
+        same_x = [jnp.where(upper_y, over_y, own), jnp.where(upper_y, own, over_y)]
+        other_x = [jnp.where(upper_y, over_xy, over_x), jnp.where(upper_y, over_x, over_xy)]
+        ordered = [jnp.where(upper_x, o, m) for m, o in zip(same_x, other_x)]
+        ordered += [jnp.where(upper_x, m, o) for m, o in zip(same_x, other_x)]
+        for j in range(4):
+            near_ref[slab * 96 + j * 24 : slab * 96 + j * 24 + 24, :] = ordered[j]
+    blank = jnp.zeros((16, 128), F32)
     for block in range(6):
-        columns = slice(block * 128, block * 128 + 128)
-        table_ref[columns, :] = near_ref[:, columns].T
+        rows = near_ref[pl.ds(block, NEAR, stride=6), :]
+        table_ref[block * 128 : block * 128 + 128, :] = jnp.concatenate([rows, blank, rows, blank]).T
+    at = TAPS + 3 - 640
+    energy_ref[...] = jnp.broadcast_to(rows[:, at : at + 1] * (1.0 / filter_half), (NEAR, S))
 
     shape = (8, 128)
     sub = lax.broadcasted_iota(jnp.int32, shape, 0)
@@ -368,13 +417,14 @@
     lax.fori_loop(0, C // 2, contract, 0, unroll=2)
 
 
-def prep(near, corner, vb, s):
+def prep(parcels, corner, vb, s):
     vmem = pl.BlockSpec(memory_space=pltpu.VMEM)
     return pl.pallas_call(
         prep_kernel,
-        in_specs=[vmem, pl.BlockSpec(memory_space=pltpu.SMEM), vmem, vmem],
-        out_shape=[sds((2, CELLS, S), BF16), sds((3, NEAR, S))],
+        in_specs=[vmem] * 4 + [pl.BlockSpec(memory_space=pltpu.SMEM), vmem, vmem],
+        out_shape=[sds((2, CELLS, S), BF16), sds((3, NEAR, S)), sds((NEAR, S))],
         scratch_shapes=[
+            pltpu.VMEM((288, 128), F32),
             pltpu.VMEM((768, 128), F32),
             pltpu.VMEM((W * W, 8, 128), F32),
             pltpu.VMEM((W * W, 8, 128), F32),
@@ -384,46 +434,27 @@
         compiler_params=params(16),
         cost_estimate=cost(1 << 27, 10 << 20),
         name="prep",
-    )(near, corner, vb, s.reshape(CELLS, S))
-
-
-def merge_kernel(part_ref, below_ref, above_ref, out_ref):
-    out_ref[0:32, :] = part_ref[1, 0:32, :] + below_ref[0:32, :] + above_ref[0:32, :]
+    )(*parcels, corner, vb, s.reshape(CELLS, S))
+
+
+def merge_kernel(part_ref, below_ref, above_ref, energy_ref, out_ref):
+    one = part_ref[1, 0:16, :] + below_ref[0:16, :] + above_ref[0:16, :]
+    out_ref[0:16, :] = one * energy_ref[16:32, :]
+    out_ref[16:32, :] = part_ref[1, 16:32, :] + below_ref[16:32, :] + above_ref[16:32, :]
     lane = lax.broadcasted_iota(jnp.int32, (16, 128), 1)
     below = jnp.where(lane < 32, pltpu.roll(below_ref[32:48, :], 112, 1), 0.0)
     above = jnp.where((lane >= 16) & (lane < 48), pltpu.roll(above_ref[32:48, :], 16, 1), 0.0)
     out_ref[32:48, :] = jnp.where(lane < 48, part_ref[1, 32:48, :], 0.0) + below + above
 
 
-def merge(part, below, above):
-    return pl.pallas_call(merge_kernel, out_shape=sds((NEAR, S)), compiler_params=params(4), name="merge")(part, below, above)
-
-
-def weigh_kernel(own_ref, other_ref, energy_ref, one_ref, rest_ref):
-    total = own_ref[...] + other_ref[...]
-    one_ref[...] = total[0:16] * energy_ref[...]
-    rest_ref[...] = total[16:48]
-
-
-def weigh(own, other, energy):
-    return pl.pallas_call(
-        weigh_kernel, out_shape=[sds((16, S)), sds((32, S))], compiler_params=params(4), name="weigh"
-    )(own, other, energy)
-
-
-def again_kernel(rest_ref, below_ref, one_ref, above_ref, energy_ref, two_ref):
-    near = jnp.concatenate([below_ref[...], one_ref[...], above_ref[...], jnp.zeros((S - NEAR, S), F32)])
-    two_ref[...] = (rest_ref[0:16, :] + exact(rest_ref[16:32, :], near)) * energy_ref[...]
-
-
-def again(rest, below, one, above, energy):
-    return pl.pallas_call(again_kernel, out_shape=sds((16, S)), compiler_params=params(4), name="again")(
-        rest, below, one, above, energy
+def merge(part, below, above, energy):
+    return pl.pallas_call(merge_kernel, out_shape=sds((NEAR, S)), compiler_params=params(4), name="merge")(
+        part, below, above, energy
     )
 
 
 def first_kernel(s_ref, side_ref, vb_ref, *refs):
-    q_ref, mix_ref, head_ref, tail_ref = refs[3:]
+    q_ref, mix_ref, head_ref, tail_ref = refs[2:]
 
     def planes(edge_ref):
         for p in range(N):
@@ -442,7 +473,7 @@
                 head_ref[z, p] = mix_ref[p, stride_rows(z), :]
                 tail_ref[z, p] = mix_ref[p, stride_rows(C - H + z), :]
 
-    for_piece(refs[:3], planes)
+    for_piece(refs[:2], planes)
 
 
 def make_first(s, side_part, vb, edges):
@@ -459,7 +490,7 @@
 
 
 def base_kernel(s_ref, mid_ref, vb_ref, vb_mate_ref, q_ref, side_ref, part_ref, *refs):
-    out_ref = refs[3]
+    out_ref = refs[2]
 
     def planes(edge_ref):
         for p in range(N):
@@ -483,7 +514,7 @@
                     total = total + vb_ref[p, rows, :] * (side_ref[p, rows, :] + q[y])
                     out_ref[p, rows, :] = 2.0 * (total + part_ref[p, rows, :]) - ring[y]
 
-    for_piece(refs[:3], planes)
+    for_piece(refs[:2], planes)
 
 
 def make_base(s, mid, vb, vb_mate, q, side_part, part, edges):
@@ -500,8 +531,7 @@
 
 
 def second_kernel(base_ref, low_ref, high_ref, gg_high_ref, gg_low_ref, *rest):
-    weighted = rest[:6]
-    second_ref, gram_ref, cross_ref, w_ref, halo_ref = rest[6:]
+    own_ref, mate_ref, energy_ref, second_ref, gram_ref, cross_ref, w_ref, halo_ref = rest
     step = pl.program_id(0)
 
     @pl.when(step == 0)
@@ -510,9 +540,15 @@
         cross_ref[...] = jnp.zeros((S, S), F32)
         w_ref[...] = jnp.zeros((S, S), F32)
         halo_ref[...] = jnp.zeros((B, ROWS, S), F32)
+        total = own_ref[...] + mate_ref[...]
+        ones = [total[i : i + 16] for i in (0, 16, 64, 112, 160)]
         for j in range(3):
-            w_ref[j * C : j * C + C, :] = 2.0 * weighted[j][...]
-            w_ref[64 + j * C : 80 + j * C, :] = 2.0 * weighted[3 + j][...]
+            row = 16 + j * NEAR
+            beside = jnp.concatenate(ones[j : j + 3] + [jnp.zeros((S - NEAR, S), F32)])
+            two = total[row + 16 : row + 32] + exact(total[row + 32 : row + 48], beside)
+            two = two * energy_ref[j * C : j * C + C, :]
+            w_ref[j * C : j * C + C, :] = 2.0 * two
+            w_ref[64 + j * C : 80 + j * C, :] = 2.0 * ones[j + 1]
 
     for p in range(B):
         low = [low_ref[j, p] for j in range(H)]
@@ -547,7 +583,8 @@
     return pl.pallas_call(
         second_kernel,
         grid=(STEPS,),
-        in_specs=[plane_spec(), halo_spec(), halo_spec(), part_spec(0), part_spec(1)] + [whole(C)] * 6,
+        in_specs=[plane_spec(), halo_spec(), halo_spec(), part_spec(0), part_spec(1)]
+        + [whole(3 * NEAR + 32), whole(3 * NEAR + 32), whole(NEAR)],
         out_specs=[plane_spec(), whole()],
         out_shape=[FULL, sds((S, S))],
         scratch_shapes=[pltpu.VMEM((S, S), F32), pltpu.VMEM((S, S), F32), pltpu.VMEM((B, ROWS, S), F32)],
@@ -670,53 +707,45 @@
     atoms = jnp.concatenate(
         [projectors.reshape(4, TAPS), atom_sites.astype(F32), energies[:, None], jnp.zeros((4, 768 - TAPS - 4), F32)],
         axis=1,
-    )
+    ).reshape(24, 128)
     mate = send(s, over_x)
     below, above = send(atoms, 0, 1), send(atoms, 0, -1)
-    one_edge, two_edge, three_edge, mid, head, tail = pack(s)
+    one_edge, head, tail = pack(s)
     one_edge = send(one_edge, over_y)
-    mine = jnp.stack([below, atoms, above])
-    head, tail, mine = barrier((head, tail, mine))
-    parcel = send(jnp.concatenate([mine.reshape(72, 128), pot]), over_y)
+    head, tail, below, above = barrier((head, tail, below, above))
+    parcel = stack(below, atoms, above, pot)
+    parcel_y = send(parcel, over_y)
+    parcel_x = send(parcel, over_x)
     low, high = send(tail, 0, 1), send(head, 0, -1)
-    other, two_edge = barrier((parcel[:72].reshape(3, 4, 768), two_edge))
+    two_edge, mid = pack_rest(s)
+    vb = spread(parcel)
+    beside = side_x(s, mate)
+    parcel_y, two_edge, beside = barrier((parcel_y, two_edge, beside))
     two_edge = send(two_edge, over_y)
-    column = jnp.where(gy == 0, jnp.concatenate([mine, other], 1), jnp.concatenate([other, mine], 1))
-    column_mate = send(column, over_x)
-    near = jnp.where(
-        gx == 0, jnp.concatenate([column, column_mate], 1), jnp.concatenate([column_mate, column], 1)
-    ).reshape(NEAR, 768)
-    gap = jnp.zeros((16, 768), F32)
-    energy = near[16:32, TAPS + 3 : TAPS + 4] * (1.0 / filter_half)
+    parcel_xy = send(parcel_y, over_x)
     corner = jnp.stack([gx * C, gy * C]).astype(jnp.int32)
-    vb = spread(pot)
-    beside = side_x(s, mate)
-    near, beside, one_edge = barrier((jnp.concatenate([near, gap, near, gap]), beside, one_edge))
-    gg, part = prep(near, corner, vb, s)
+    parcel_xy, one_edge = barrier((parcel_xy, one_edge))
+    gg, part, energy = prep([parcel, parcel_x, parcel_y, parcel_xy], corner, vb, s)
 
     part = part + send(part, over_x)
-    own = merge(part, send(part[2], 0, 1), send(part[0], 0, -1))
-    three_edge, own = barrier((three_edge, own))
-    own_mate = send(own, over_y)
-    three_edge = send(three_edge, over_y)
-    one, rest = weigh(own, own_mate, energy)
-    mid, one, two_edge = barrier((mid, one, two_edge))
-    mid = send(mid, over_y)
-    ones = [send(one, 0, 1), one, send(one, 0, -1)]
-
+    own = merge(part, send(part[2], 0, 1), send(part[0], 0, -1), energy)
+    side_part = side_z(s, beside, low, high)
+    own, side_part = barrier((own, side_part))
+    coefs = stack(send(own[:16], 0, 2), send(own, 0, 1), own, send(own, 0, -1), send(own[:16], 0, -2))
+    coefs, two_edge = barrier((coefs, two_edge))
+    coefs_mate = send(coefs, over_y)
+
+    edges = [one_edge, two_edge]
     vb = vb.reshape(C, ROWS, S)
-    vb_mate = spread(parcel[72:]).reshape(C, ROWS, S)
-    side_part = side_z(s, beside, low, high)
-    three_edge, ones = barrier((three_edge, ones))
-    edges = [one_edge, two_edge, three_edge]
-    two = again(rest, *ones, energy)
-    twos = [send(two, 0, 1), two, send(two, 0, -1)]
     q, mix, head, tail = make_first(s, side_part, vb, edges)
     low, high = send(tail, 0, 1), send(head, 0, -1)
     mate = send(mix, over_x)
+    mid, coefs_mate = barrier((mid, coefs_mate))
+    mid = send(mid, over_y)
+    vb_mate = spread(parcel_y).reshape(C, ROWS, S)
     part = side_again(mix, mate)
     base = make_base(s, mid, vb, vb_mate, q, side_part, part, edges)
-    second, gram = make_second(base, low, high, gg.reshape(2, C, ROWS, S), twos + ones)
+    second, gram = make_second(base, low, high, gg.reshape(2, C, ROWS, S), [coefs, coefs_mate, energy])
 
     for flip in (64, 32, 36, 1, 3, 8, 24):
         gram = gram + lax.ppermute(gram, AXES, [(d, d ^ flip) for d in range(count)])

time: 184 us -> 179 us (0.973)
  starting transfers between devices: 61.8 us -> 72.7 us
  waiting for transfers between devices: 55.1 us -> 44.2 us
  local copies, waits for them, and re-layouts: 13.8 us -> 4.97 us
  Pallas kernels: 47.8 us -> 55.4 us
  other arithmetic: 4.01 us -> 0.91 us
    ppermute x7, starting transfers between devices: 7.83 us -> 17.9 us  [per_device(): lax.ppermute(gram, AXES, [(d, d ^ flip) for d in range(count)])]
    ppermute x7, waiting for transfers between devices: 23.2 us -> 17.6 us  [per_device(): lax.ppermute(gram, AXES, [(d, d ^ flip) for d in range(count)])]
    ppermute x22, waiting for transfers between devices: 31.9 us -> 26.7 us  [send(): return lax.ppermute(value, AXES, [(d, target(d)) for d in range(count)])]
    unnamed x23 -> x15, local copies, waits for them, and re-layouts: 7.72 us -> 3.87 us
    slice x2 -> x1, local copies, waits for them, and re-layouts: 2.1 us -> 0.01 us  [per_device(): own[:16]]
    pallas_call x5 -> x6, Pallas kernels: 9.51 us -> 11.5 us  [the longest x1 7.74 us: prep(): pl.pallas_call(prep_kernel, in_specs=[vmem] * 4 + [pl.BlockSpec(memory_sp...]
    reshape x2 -> x1, local copies, waits for them, and re-layouts: 2.03 us -> 0.01 us  [per_device(): atoms = jnp.concatenate([projectors.reshape(4, TAPS), atom_sites.astype(F...]
  transfers between devices with their start and end apart: 29 -> 29, of which waited for: 12 -> 12; matrix products, arithmetic and copies ran while one was open for 6% -> 2% of each run, Pallas kernels for 13% -> 17%
where the time goes in v5:
time: 179 us
  starting transfers between devices  72.7 us (41%)
  Pallas kernels  55.4 us (31%)
  waiting for transfers between devices  44.2 us (25%)
  local copies, waits for them, and re-layouts  4.97 us (3%)
    ppermute x22, starting transfers between devices, send(): return lax.ppermute(value, AXES, [(d, target(d)) for d in range(count)])  54.8 us
    ppermute x22, waiting for transfers between devices, send(): return lax.ppermute(value, AXES, [(d, target(d)) for d in range(count)])  26.7 us
    ppermute x7, starting transfers between devices, per_device(): lax.ppermute(gram, AXES, [(d, d ^ flip) for d in range(count)])  17.9 us
    ppermute x7, waiting for transfers between devices, per_device(): lax.ppermute(gram, AXES, [(d, d ^ flip) for d in range(count)])  17.6 us
    pallas_call x1, Pallas kernels, turn(): pl.pallas_call(turn_kernel, grid=(STEPS,), in_specs=[plane_spec(), whole(...  16.9 us
    pallas_call x1, Pallas kernels, prep(): pl.pallas_call(prep_kernel, in_specs=[vmem] * 4 + [pl.BlockSpec(memory_sp...  7.74 us
    pallas_call x1, Pallas kernels, make_second(): pl.pallas_call(second_kernel, grid=(STEPS,), in_specs=[plane_spec(), halo...  5.11 us
    pallas_call x1, Pallas kernels, make_base(): pl.pallas_call(base_kernel, grid=(C // N,), in_specs=[plane_spec(ROWS, N)...  4.3 us
  transfers between devices with their start and end apart: 29, of which 12 were waited for; matrix products, arithmetic and copies ran while one was open for 2% of the time, Pallas kernels for 17%

profile of v5, /device:TPU:0, one launch (start us, length us, event | category | flops | bytes accessed | tf_op | source)
XLA Modules:
  0.0 178.5 jit_solution(6286458219532774308)
XLA Ops:
  2.7 1.6 collective-permute-start
  4.3 7.1 %collective-permute-start.1 = (f32[24,128]{1,0:T(8,128)S(1)}, f32[24,128]{1,0:T(8,128)S(1)}, u32[]{:S(2)}, u32[]{:S(2)}) collective-permute-start(f32[24,128]{1,0:T(8,128)S(1)} %reshape.26.refs_1_), channel_id=1, source_target_pairs={{0,31},{1,0},{2,1},{3,2},{4,3},{5,4},{6,5},{7,6},{8,7},{9,8},{10,9... | collective-permute-start | bytes 36872 | tf_op jit(solution)/shard_map/ppermute | solution.py:701
  13.1 3.3 %pack.1 = (f32[6,192,128]{2,1,0:T(8,128)}, f32[6,16,16,128]{3,2,1,0:T(8,128)}, f32[6,16,16,128]{3,2,1,0:T(8,128)}) custom-call(f32[16,256,128]{2,1,0:T(8,128)S(1)} %bitcast.14), custom_call_target="tpu_custom_call" | custom-call | flops 4294967296 | bytes 6291456 | tf_op jit(solution)/shard_map/pack/pallas_call | solution.py:142
  18.6 2.2 %pack_rest.1 = (f32[10,192,128]{2,1,0:T(8,128)}, f32[16,64,128]{2,1,0:T(8,128)S(1)}) custom-call(f32[16,256,128]{2,1,0:T(8,128)S(1)} %bitcast.15), custom_call_target="tpu_custom_call" | custom-call | flops 2147483648 | bytes 4194304 | tf_op jit(solution)/shard_map/pack_rest/pallas_call | solution.py:163
  20.8 3.2 %side_x.1.part_ref = f32[16,256,128]{2,1,0:T(8,128)S(1)} custom-call(f32[16,256,128]{2,1,0:T(8,128)S(1)} %bitcast.16, f32[16,256,128]{2,1,0:T(8,128)} %collective-permute-done.4.mate_ref), custom_call_target="tpu_custom_call" | custom-call | flops 16777216 | bytes 6291456 | tf_op jit(solution)/shard_map/side_x/pallas_call | solution.py:212
  25.3 7.8 %collective-permute-done.3.refs_2_.parcel_ref = f32[104,128]{1,0:T(8,128)S(1)} collective-permute-done((f32[104,128]{1,0:T(8,128)S(1)}, f32[104,128]{1,0:T(8,128)S(1)}, u32[]{:S(2)}, u32[]{:S(2)}) %collective-permute-start.3) | collective-permute-done | bytes 53280 | tf_op jit(solution)/shard_map/ppermute | solution.py:701
  34.2 7.7 %collective-permute-start.11 = (f32[6,16,16,128]{3,2,1,0:T(8,128)}, f32[6,16,16,128]{3,2,1,0:T(8,128)}, u32[]{:S(2)}, u32[]{:S(2)}) collective-permute-start(f32[6,16,16,128]{3,2,1,0:T(8,128)} %get-tuple-element.47), channel_id=1, source_target_pairs={{0,31},{1,0},{2,1},{3,2},{4,3},{5,4},{6,5},{7,6},{8,7},{9,8},{10,9... | collective-permute-start | bytes 2359304 | tf_op jit(solution)/shard_map/ppermute | solution.py:701
  43.4 7.7 %prep.1 = (bf16[2,4096,128]{2,1,0:T(8,128)(2,1)S(1)}, f32[3,48,128]{2,1,0:T(8,128)S(1)}, f32[48,128]{1,0:T(8,128)S(1)}) custom-call(f32[104,128]{1,0:T(8,128)S(1)} %stack.14.parcel_ref.refs_0_, f32[104,128]{1,0:T(8,128)S(1)} %collective-permute-done.2.refs_1_, f32[104,128]{1,0:T(8,128)S(1)} %collective-permute-done.3.refs_2_.parcel_ref, ...), custom_call_target="tpu_custom_call" | custom-call | flops 134217728 | bytes 10485760 | tf_op jit(solution)/shard_map/prep/pallas_call | solution.py:422
  52.6 7.7 %collective-permute-start.9 = (f32[48,128]{1,0:T(8,128)S(1)}, f32[48,128]{1,0:T(8,128)S(1)}, u32[]{:S(2)}, u32[]{:S(2)}) collective-permute-start(f32[48,128]{1,0:T(8,128)S(1)} %get-tuple-element.63), channel_id=1, source_target_pairs={{0,31},{1,0},{2,1},{3,2},{4,3},{5,4},{6,5},{7,6},{8,7},{9,8},{10,9... | collective-permute-start | bytes 73736 | tf_op jit(solution)/shard_map/ppermute | solution.py:701
  60.3 4.2 %side_z.1.side_ref = f32[16,256,128]{2,1,0:T(8,128)S(1)} custom-call(f32[16,256,128]{2,1,0:T(8,128)S(1)} %bitcast.18, f32[16,256,128]{2,1,0:T(8,128)S(1)} %copy-done.3, f32[6,16,16,128]{3,2,1,0:T(8,128)} %collective-permute-done.10.low_ref, f32[6,16,16,128]{3,2,1,0:T(8,128)} %collective-permute-done.11.high_ref), custom_call_target="tpu_custom_call" | custom-call | flops 16777216 | bytes 8388608 | tf_op jit(solution)/shard_map/side_z/pallas_call | solution.py:237
  64.6 7.7 %collective-permute-start.14 = (f32[48,128]{1,0:T(8,128)S(1)}, f32[48,128]{1,0:T(8,128)S(1)}, u32[]{:S(2)}, u32[]{:S(2)}) collective-permute-start(f32[48,128]{1,0:T(8,128)S(1)} %merge.1.refs_2_), channel_id=1, source_target_pairs={{0,31},{1,0},{2,1},{3,2},{4,3},{5,4},{6,5},{7,6},{8,7},{9,8},{10,9... | collective-permute-start | bytes 73736 | tf_op jit(solution)/shard_map/ppermute | solution.py:701
  72.4 8.0 %collective-permute-start.15 = (f32[16,128]{1,0:T(8,128)S(1)}, f32[16,128]{1,0:T(8,128)S(1)}, u32[]{:S(2)}, u32[]{:S(2)}) collective-permute-start(f32[16,128]{1,0:T(8,128)S(1)} %slice.12), channel_id=1, source_target_pairs={{0,30},{1,31},{2,0},{3,1},{4,2},{5,3},{6,4},{7,5},{8,6},{9,7},{10,... | collective-permute-start | bytes 24584 | tf_op jit(solution)/shard_map/ppermute | solution.py:701
  82.1 3.8 %first.1 = (f32[16,256,128]{2,1,0:T(8,128)S(1)}, f32[16,256,128]{2,1,0:T(8,128)S(1)}, f32[6,16,16,128]{3,2,1,0:T(8,128)S(1)}, f32[6,16,16,128]{3,2,1,0:T(8,128)S(1)}) custom-call(f32[16,256,128]{2,1,0:T(8,128)S(1)} %bitcast.19, f32[16,256,128]{2,1,0:T(8,128)S(1)} %side_z.1.side_ref, f32[16,256,128]{2,1,0:T(8,128)S(1)} %bitcast.21, ...), custom_call_target="tpu_custom_call" | custom-call | flops 16777216 | bytes 14680064 | tf_op jit(solution)/shard_map/first/pallas_call | solution.py:480
  86.1 7.7 %collective-permute-start.21 = (f32[6,16,16,128]{3,2,1,0:T(8,128)S(1)}, f32[6,16,16,128]{3,2,1,0:T(8,128)S(1)}, u32[]{:S(2)}, u32[]{:S(2)}) collective-permute-start(f32[6,16,16,128]{3,2,1,0:T(8,128)S(1)} %get-tuple-element.58), channel_id=1, source_target_pairs={{0,31},{1,0},{2,1},{3,2},{4,3},{5,4},{6,5},{7,6},{8,7},{9,8},{10,9... | collective-permute-start | bytes 2359304 | tf_op jit(solution)/shard_map/ppermute | solution.py:701
  94.9 7.9 %collective-permute-done.17.rest_1_ = f32[176,128]{1,0:T(8,128)S(1)} collective-permute-done((f32[176,128]{1,0:T(8,128)S(1)}, f32[176,128]{1,0:T(8,128)S(1)}, u32[]{:S(2)}, u32[]{:S(2)}) %collective-permute-start.17) | collective-permute-done | bytes 90144 | tf_op jit(solution)/shard_map/ppermute | solution.py:701
  102.8 1.7 collective-permute-start.18
  105.3 2.9 %side_again.1.part_ref = f32[16,256,128]{2,1,0:T(8,128)S(1)} custom-call(f32[16,256,128]{2,1,0:T(8,128)S(1)} %get-tuple-element.56.s_ref, f32[16,256,128]{2,1,0:T(8,128)S(1)} %collective-permute-done.19.mate_ref), custom_call_target="tpu_custom_call" | custom-call | flops 33554432 | bytes 6291456 | tf_op jit(solution)/shard_map/side_again/pallas_call | solution.py:264
  108.3 8.3 %collective-permute-done.18.mid_ref = f32[16,64,128]{2,1,0:T(8,128)S(1)} collective-permute-done((f32[16,64,128]{2,1,0:T(8,128)S(1)}, f32[16,64,128]{2,1,0:T(8,128)S(1)}, u32[]{:S(2)}, u32[]{:S(2)}) %collective-permute-start.18) | collective-permute-done | bytes 524320 | tf_op jit(solution)/shard_map/ppermute | solution.py:701
  116.6 4.3 %base.1.base_ref = f32[16,256,128]{2,1,0:T(8,128)S(1)} custom-call(f32[16,256,128]{2,1,0:T(8,128)S(1)} %bitcast.20, f32[16,64,128]{2,1,0:T(8,128)S(1)} %collective-permute-done.18.mid_ref, f32[16,256,128]{2,1,0:T(8,128)S(1)} %bitcast.22, f32[16,256,128]{2,1,0:T(8,128)S(1)} %bitcast.25, f32[16,256,128]{2,1,0:T(8,128)S(1)} %get-tuple-element.55.q_ref, ...), custom_call_target="tpu_custom_call" | custom-call | flops 33554432 | bytes 16777216 | tf_op jit(solution)/shard_map/base/pallas_call | solution.py:521
  121.0 5.1 %second.1 = (f32[16,256,128]{2,1,0:T(8,128)S(1)}, f32[128,128]{1,0:T(8,128)S(1)}) custom-call(f32[16,256,128]{2,1,0:T(8,128)S(1)} %base.1.base_ref, f32[6,16,16,128]{3,2,1,0:T(8,128)S(1)} %collective-permute-done.20.low_ref, f32[6,16,16,128]{3,2,1,0:T(8,128)S(1)} %collective-permute-done.21.high_ref, bf16[2,16,256,128]{3,2,1,0:T(8,128)(2,1)S(1)} %bitcast.23, ...), custom_call_target="tpu_custom_call" | custom-call | flops 134217728 | bytes 8388608 | tf_op jit(solution)/shard_map/second/pallas_call | solution.py:583
  127.6 1.8 %collective-permute-start.23 = (f32[128,128]{1,0:T(8,128)S(1)}, f32[128,128]{1,0:T(8,128)S(1)}, u32[]{:S(2)}, u32[]{:S(2)}) collective-permute-start(f32[128,128]{1,0:T(8,128)S(1)} %add.25), channel_id=1, source_target_pairs={{0,32},{1,33},{2,34},{3,35},{4,36},{5,37},{6,38},{7,39},{8,40},{9,... | collective-permute-start | bytes 196616 | tf_op jit(solution)/shard_map/ppermute | solution.py:751
  129.4 2.5 %collective-permute-done.23 = f32[128,128]{1,0:T(8,128)S(1)} collective-permute-done((f32[128,128]{1,0:T(8,128)S(1)}, f32[128,128]{1,0:T(8,128)S(1)}, u32[]{:S(2)}, u32[]{:S(2)}) %collective-permute-start.23) | collective-permute-done | bytes 65568 | tf_op jit(solution)/shard_map/ppermute | solution.py:751
  132.0 3.4 %collective-permute-start.24 = (f32[128,128]{1,0:T(8,128)S(1)}, f32[128,128]{1,0:T(8,128)S(1)}, u32[]{:S(2)}, u32[]{:S(2)}) collective-permute-start(f32[128,128]{1,0:T(8,128)S(1)} %add.26), channel_id=1, source_target_pairs={{0,36},{1,37},{2,38},{3,39},{4,32},{5,33},{6,34},{7,35},{8,44},{9,... | collective-permute-start | bytes 196616 | tf_op jit(solution)/shard_map/ppermute | solution.py:751
  135.3 2.2 %collective-permute-done.24 = f32[128,128]{1,0:T(8,128)S(1)} collective-permute-done((f32[128,128]{1,0:T(8,128)S(1)}, f32[128,128]{1,0:T(8,128)S(1)}, u32[]{:S(2)}, u32[]{:S(2)}) %collective-permute-start.24) | collective-permute-done | bytes 65568 | tf_op jit(solution)/shard_map/ppermute | solution.py:751
  137.7 4.3 %collective-permute-done.25 = f32[128,128]{1,0:T(8,128)S(1)} collective-permute-done((f32[128,128]{1,0:T(8,128)S(1)}, f32[128,128]{1,0:T(8,128)S(1)}, u32[]{:S(2)}, u32[]{:S(2)}) %collective-permute-start.25) | collective-permute-done | bytes 65568 | tf_op jit(solution)/shard_map/ppermute | solution.py:751
  141.9 2.8 %collective-permute-start.26 = (f32[128,128]{1,0:T(8,128)S(1)}, f32[128,128]{1,0:T(8,128)S(1)}, u32[]{:S(2)}, u32[]{:S(2)}) collective-permute-start(f32[128,128]{1,0:T(8,128)S(1)} %add.28), channel_id=1, source_target_pairs={{0,3},{1,2},{2,1},{3,0},{4,7},{5,6},{6,5},{7,4},{8,11},{9,10},{10,... | collective-permute-start | bytes 196616 | tf_op jit(solution)/shard_map/ppermute | solution.py:751
  144.7 2.8 %collective-permute-done.26 = f32[128,128]{1,0:T(8,128)S(1)} collective-permute-done((f32[128,128]{1,0:T(8,128)S(1)}, f32[128,128]{1,0:T(8,128)S(1)}, u32[]{:S(2)}, u32[]{:S(2)}) %collective-permute-start.26) | collective-permute-done | bytes 65568 | tf_op jit(solution)/shard_map/ppermute | solution.py:751
  147.5 2.3 %collective-permute-start.27 = (f32[128,128]{1,0:T(8,128)S(1)}, f32[128,128]{1,0:T(8,128)S(1)}, u32[]{:S(2)}, u32[]{:S(2)}) collective-permute-start(f32[128,128]{1,0:T(8,128)S(1)} %add.29), channel_id=1, source_target_pairs={{0,8},{1,9},{2,10},{3,11},{4,12},{5,13},{6,14},{7,15},{8,0},{9,1},... | collective-permute-start | bytes 196616 | tf_op jit(solution)/shard_map/ppermute | solution.py:751
  149.8 2.2 %collective-permute-done.27 = f32[128,128]{1,0:T(8,128)S(1)} collective-permute-done((f32[128,128]{1,0:T(8,128)S(1)}, f32[128,128]{1,0:T(8,128)S(1)}, u32[]{:S(2)}, u32[]{:S(2)}) %collective-permute-start.27) | collective-permute-done | bytes 65568 | tf_op jit(solution)/shard_map/ppermute | solution.py:751
  152.1 7.3 %collective-permute-start.28 = (f32[128,128]{1,0:T(8,128)S(1)}, f32[128,128]{1,0:T(8,128)S(1)}, u32[]{:S(2)}, u32[]{:S(2)}) collective-permute-start(f32[128,128]{1,0:T(8,128)S(1)} %add.30), channel_id=1, source_target_pairs={{0,24},{1,25},{2,26},{3,27},{4,28},{5,29},{6,30},{7,31},{8,16},{9,... | collective-permute-start | bytes 196616 | tf_op jit(solution)/shard_map/ppermute | solution.py:751
  159.4 2.2 %collective-permute-done.28 = f32[128,128]{1,0:T(8,128)S(1)} collective-permute-done((f32[128,128]{1,0:T(8,128)S(1)}, f32[128,128]{1,0:T(8,128)S(1)}, u32[]{:S(2)}, u32[]{:S(2)}) %collective-permute-start.28) | collective-permute-done | bytes 65568 | tf_op jit(solution)/shard_map/ppermute | solution.py:751
  161.6 16.9 %turn.1 = f32[16,256,128]{2,1,0:T(8,128)} custom-call(f32[16,256,128]{2,1,0:T(8,128)S(1)} %get-tuple-element.61.second_ref, f32[128,128]{1,0:T(8,128)S(1)} %add_multiply_fusion.gram_ref), custom_call_target="tpu_custom_call" | custom-call | flops 268435456 | bytes 4194304 | tf_op jit(solution)/shard_map/turn/pallas_call | solution.py:678
  (75 shorter events, 17.1 us)
Async XLA Ops:
  0.0 20.7 %collective-permute-start.4 = (f32[16,256,128]{2,1,0:T(8,128)}, f32[16,256,128]{2,1,0:T(8,128)}, u32[]{:S(2)}, u32[]{:S(2)}) collective-permute-start(f32[16,256,128]{2,1,0:T(8,128)} %bitcast.13), channel_id=1, source_target_pairs={{0,64},{1,65},{2,66},{3,67},{4,68},{5,69},{6,70},{7,71},{8,72},{9,... | collective-permute-start | bytes 6291464 | tf_op jit(solution)/shard_map/ppermute | solution.py:701
  2.7 14.8 %collective-permute-start = (f32[24,128]{1,0:T(8,128)S(1)}, f32[24,128]{1,0:T(8,128)S(1)}, u32[]{:S(2)}, u32[]{:S(2)}) collective-permute-start(f32[24,128]{1,0:T(8,128)S(1)} %reshape.26.refs_1_), channel_id=1, source_target_pairs={{0,1},{1,2},{2,3},{3,4},{4,5},{5,6},{6,7},{7,8},{8,9},{9,10},{10,1... | collective-permute-start | bytes 36872 | tf_op jit(solution)/shard_map/ppermute | solution.py:701
  4.3 13.2 %collective-permute-start.1 = (f32[24,128]{1,0:T(8,128)S(1)}, f32[24,128]{1,0:T(8,128)S(1)}, u32[]{:S(2)}, u32[]{:S(2)}) collective-permute-start(f32[24,128]{1,0:T(8,128)S(1)} %reshape.26.refs_1_), channel_id=1, source_target_pairs={{0,31},{1,0},{2,1},{3,2},{4,3},{5,4},{6,5},{7,6},{8,7},{9,8},{10,9... | collective-permute-start | bytes 36872 | tf_op jit(solution)/shard_map/ppermute | solution.py:701
  13.1 5.5 %copy-start.1 = (f32[16,16,16,128]{3,2,1,0:T(8,128)S(1)}, f32[16,16,16,128]{3,2,1,0:T(8,128)}, u32[]{:S(2)}) copy-start(f32[16,16,16,128]{3,2,1,0:T(8,128)} %param.5) | copy-start | bytes 6291460
  16.3 25.6 %collective-permute-start.6 = (f32[6,192,128]{2,1,0:T(8,128)}, f32[6,192,128]{2,1,0:T(8,128)}, u32[]{:S(2)}, u32[]{:S(2)}) collective-permute-start(f32[6,192,128]{2,1,0:T(8,128)} %get-tuple-element.41), channel_id=1, source_target_pairs={{0,32},{1,33},{2,34},{3,35},{4,36},{5,37},{6,38},{7,39},{8,40},{9,... | collective-permute-start | bytes 1769480 | tf_op jit(solution)/shard_map/ppermute | solution.py:701
  17.5 15.6 %collective-permute-start.3 = (f32[104,128]{1,0:T(8,128)S(1)}, f32[104,128]{1,0:T(8,128)S(1)}, u32[]{:S(2)}, u32[]{:S(2)}) collective-permute-start(f32[104,128]{1,0:T(8,128)S(1)} %stack.14.parcel_ref.refs_0_), channel_id=1, source_target_pairs={{0,32},{1,33},{2,34},{3,35},{4,36},{5,37},{6,38},{7,39},{8,40},{9,... | collective-permute-start | bytes 159752 | tf_op jit(solution)/shard_map/ppermute | solution.py:701
  33.2 48.9 %collective-permute-start.16 = (f32[10,192,128]{2,1,0:T(8,128)}, f32[10,192,128]{2,1,0:T(8,128)S(1)}, u32[]{:S(2)}, u32[]{:S(2)}) collective-permute-start(f32[10,192,128]{2,1,0:T(8,128)} %get-tuple-element.49), channel_id=1, source_target_pairs={{0,32},{1,33},{2,34},{3,35},{4,36},{5,37},{6,38},{7,39},{8,40},{9,... | collective-permute-start | bytes 2949128 | tf_op jit(solution)/shard_map/ppermute | solution.py:701
  34.2 26.1 %collective-permute-start.10 = (f32[6,16,16,128]{3,2,1,0:T(8,128)}, f32[6,16,16,128]{3,2,1,0:T(8,128)}, u32[]{:S(2)}, u32[]{:S(2)}) collective-permute-start(f32[6,16,16,128]{3,2,1,0:T(8,128)} %get-tuple-element.46), channel_id=1, source_target_pairs={{0,1},{1,2},{2,3},{3,4},{4,5},{5,6},{6,7},{7,8},{8,9},{9,10},{10,1... | collective-permute-start | bytes 2359304 | tf_op jit(solution)/shard_map/ppermute | solution.py:701
  34.2 26.1 %collective-permute-start.11 = (f32[6,16,16,128]{3,2,1,0:T(8,128)}, f32[6,16,16,128]{3,2,1,0:T(8,128)}, u32[]{:S(2)}, u32[]{:S(2)}) collective-permute-start(f32[6,16,16,128]{3,2,1,0:T(8,128)} %get-tuple-element.47), channel_id=1, source_target_pairs={{0,31},{1,0},{2,1},{3,2},{4,3},{5,4},{6,5},{7,6},{8,7},{9,8},{10,9... | collective-permute-start | bytes 2359304 | tf_op jit(solution)/shard_map/ppermute | solution.py:701
  41.9 1.4 collective-permute-start.2
  41.9 1.4 collective-permute-start.5
  43.3 17.0 %copy-start.3 = (f32[16,256,128]{2,1,0:T(8,128)S(1)}, f32[16,256,128]{2,1,0:T(8,128)}, u32[]{:S(2)}) copy-start(f32[16,256,128]{2,1,0:T(8,128)} %copy-done.2) | copy-start | bytes 6291460
  51.1 1.3 collective-permute-start.7
  52.5 12.0 %collective-permute-start.8 = (f32[48,128]{1,0:T(8,128)S(1)}, f32[48,128]{1,0:T(8,128)S(1)}, u32[]{:S(2)}, u32[]{:S(2)}) collective-permute-start(f32[48,128]{1,0:T(8,128)S(1)} %get-tuple-element.64), channel_id=1, source_target_pairs={{0,1},{1,2},{2,3},{3,4},{4,5},{5,6},{6,7},{7,8},{8,9},{9,10},{10,1... | collective-permute-start | bytes 73736 | tf_op jit(solution)/shard_map/ppermute | solution.py:701
  52.6 12.0 %collective-permute-start.9 = (f32[48,128]{1,0:T(8,128)S(1)}, f32[48,128]{1,0:T(8,128)S(1)}, u32[]{:S(2)}, u32[]{:S(2)}) collective-permute-start(f32[48,128]{1,0:T(8,128)S(1)} %get-tuple-element.63), channel_id=1, source_target_pairs={{0,31},{1,0},{2,1},{3,2},{4,3},{5,4},{6,5},{7,6},{8,7},{9,8},{10,9... | collective-permute-start | bytes 73736 | tf_op jit(solution)/shard_map/ppermute | solution.py:701
  64.6 17.4 %collective-permute-start.13 = (f32[48,128]{1,0:T(8,128)S(1)}, f32[48,128]{1,0:T(8,128)S(1)}, u32[]{:S(2)}, u32[]{:S(2)}) collective-permute-start(f32[48,128]{1,0:T(8,128)S(1)} %merge.1.refs_2_), channel_id=1, source_target_pairs={{0,1},{1,2},{2,3},{3,4},{4,5},{5,6},{6,7},{7,8},{8,9},{9,10},{10,1... | collective-permute-start | bytes 73736 | tf_op jit(solution)/shard_map/ppermute | solution.py:701
  64.6 17.4 %collective-permute-start.14 = (f32[48,128]{1,0:T(8,128)S(1)}, f32[48,128]{1,0:T(8,128)S(1)}, u32[]{:S(2)}, u32[]{:S(2)}) collective-permute-start(f32[48,128]{1,0:T(8,128)S(1)} %merge.1.refs_2_), channel_id=1, source_target_pairs={{0,31},{1,0},{2,1},{3,2},{4,3},{5,4},{6,5},{7,6},{8,7},{9,8},{10,9... | collective-permute-start | bytes 73736 | tf_op jit(solution)/shard_map/ppermute | solution.py:701
  72.4 9.7 %collective-permute-start.12 = (f32[16,128]{1,0:T(8,128)S(1)}, f32[16,128]{1,0:T(8,128)S(1)}, u32[]{:S(2)}, u32[]{:S(2)}) collective-permute-start(f32[16,128]{1,0:T(8,128)S(1)} %slice.12), channel_id=1, source_target_pairs={{0,2},{1,3},{2,4},{3,5},{4,6},{5,7},{6,8},{7,9},{8,10},{9,11},{10,... | collective-permute-start | bytes 24584 | tf_op jit(solution)/shard_map/ppermute | solution.py:701
  72.4 9.7 %collective-permute-start.15 = (f32[16,128]{1,0:T(8,128)S(1)}, f32[16,128]{1,0:T(8,128)S(1)}, u32[]{:S(2)}, u32[]{:S(2)}) collective-permute-start(f32[16,128]{1,0:T(8,128)S(1)} %slice.12), channel_id=1, source_target_pairs={{0,30},{1,31},{2,0},{3,1},{4,2},{5,3},{6,4},{7,5},{8,6},{9,7},{10,... | collective-permute-start | bytes 24584 | tf_op jit(solution)/shard_map/ppermute | solution.py:701
  82.1 20.7 %copy-start.5 = (f32[16,64,128]{2,1,0:T(8,128)S(1)}, f32[16,64,128]{2,1,0:T(8,128)}, u32[]{:S(2)}) copy-start(f32[16,64,128]{2,1,0:T(8,128)} %copy-done.4) | copy-start | bytes 1572868
  85.9 19.4 %collective-permute-start.19 = (f32[16,256,128]{2,1,0:T(8,128)S(1)}, f32[16,256,128]{2,1,0:T(8,128)S(1)}, u32[]{:S(2)}, u32[]{:S(2)}) collective-permute-start(f32[16,256,128]{2,1,0:T(8,128)S(1)} %get-tuple-element.56.s_ref), channel_id=1, source_target_pairs={{0,64},{1,65},{2,66},{3,67},{4,68},{5,69},{6,70},{7,71},{8,72},{9,... | collective-permute-start | bytes 6291464 | tf_op jit(solution)/shard_map/ppermute | solution.py:701
  86.0 34.9 %collective-permute-start.20 = (f32[6,16,16,128]{3,2,1,0:T(8,128)S(1)}, f32[6,16,16,128]{3,2,1,0:T(8,128)S(1)}, u32[]{:S(2)}, u32[]{:S(2)}) collective-permute-start(f32[6,16,16,128]{3,2,1,0:T(8,128)S(1)} %get-tuple-element.57), channel_id=1, source_target_pairs={{0,1},{1,2},{2,3},{3,4},{4,5},{5,6},{6,7},{7,8},{8,9},{9,10},{10,1... | collective-permute-start | bytes 2359304 | tf_op jit(solution)/shard_map/ppermute | solution.py:701
  86.1 34.8 %collective-permute-start.21 = (f32[6,16,16,128]{3,2,1,0:T(8,128)S(1)}, f32[6,16,16,128]{3,2,1,0:T(8,128)S(1)}, u32[]{:S(2)}, u32[]{:S(2)}) collective-permute-start(f32[6,16,16,128]{3,2,1,0:T(8,128)S(1)} %get-tuple-element.58), channel_id=1, source_target_pairs={{0,31},{1,0},{2,1},{3,2},{4,3},{5,4},{6,5},{7,6},{8,7},{9,8},{10,9... | collective-permute-start | bytes 2359304 | tf_op jit(solution)/shard_map/ppermute | solution.py:701
  93.9 8.9 %collective-permute-start.17 = (f32[176,128]{1,0:T(8,128)S(1)}, f32[176,128]{1,0:T(8,128)S(1)}, u32[]{:S(2)}, u32[]{:S(2)}) collective-permute-start(f32[176,128]{1,0:T(8,128)S(1)} %stack.15.rest_0_), channel_id=1, source_target_pairs={{0,32},{1,33},{2,34},{3,35},{4,36},{5,37},{6,38},{7,39},{8,40},{9,... | collective-permute-start | bytes 270344 | tf_op jit(solution)/shard_map/ppermute | solution.py:701
  102.8 13.8 %collective-permute-start.18 = (f32[16,64,128]{2,1,0:T(8,128)S(1)}, f32[16,64,128]{2,1,0:T(8,128)S(1)}, u32[]{:S(2)}, u32[]{:S(2)}) collective-permute-start(f32[16,64,128]{2,1,0:T(8,128)S(1)} %copy-done.5), channel_id=1, source_target_pairs={{0,32},{1,33},{2,34},{3,35},{4,36},{5,37},{6,38},{7,39},{8,40},{9,... | collective-permute-start | bytes 1572872 | tf_op jit(solution)/shard_map/ppermute | solution.py:701
  126.1 1.5 collective-permute-start.22
  127.6 4.3 %collective-permute-start.23 = (f32[128,128]{1,0:T(8,128)S(1)}, f32[128,128]{1,0:T(8,128)S(1)}, u32[]{:S(2)}, u32[]{:S(2)}) collective-permute-start(f32[128,128]{1,0:T(8,128)S(1)} %add.25), channel_id=1, source_target_pairs={{0,32},{1,33},{2,34},{3,35},{4,36},{5,37},{6,38},{7,39},{8,40},{9,... | collective-permute-start | bytes 196616 | tf_op jit(solution)/shard_map/ppermute | solution.py:751
  132.0 5.6 %collective-permute-start.24 = (f32[128,128]{1,0:T(8,128)S(1)}, f32[128,128]{1,0:T(8,128)S(1)}, u32[]{:S(2)}, u32[]{:S(2)}) collective-permute-start(f32[128,128]{1,0:T(8,128)S(1)} %add.26), channel_id=1, source_target_pairs={{0,36},{1,37},{2,38},{3,39},{4,32},{5,33},{6,34},{7,35},{8,44},{9,... | collective-permute-start | bytes 196616 | tf_op jit(solution)/shard_map/ppermute | solution.py:751
  137.6 4.3 %collective-permute-start.25 = (f32[128,128]{1,0:T(8,128)S(1)}, f32[128,128]{1,0:T(8,128)S(1)}, u32[]{:S(2)}, u32[]{:S(2)}) collective-permute-start(f32[128,128]{1,0:T(8,128)S(1)} %add.27), channel_id=1, source_target_pairs={{0,1},{1,0},{2,3},{3,2},{4,5},{5,4},{6,7},{7,6},{8,9},{9,8},{10,11... | collective-permute-start | bytes 196616 | tf_op jit(solution)/shard_map/ppermute | solution.py:751
  141.9 5.6 %collective-permute-start.26 = (f32[128,128]{1,0:T(8,128)S(1)}, f32[128,128]{1,0:T(8,128)S(1)}, u32[]{:S(2)}, u32[]{:S(2)}) collective-permute-start(f32[128,128]{1,0:T(8,128)S(1)} %add.28), channel_id=1, source_target_pairs={{0,3},{1,2},{2,1},{3,0},{4,7},{5,6},{6,5},{7,4},{8,11},{9,10},{10,... | collective-permute-start | bytes 196616 | tf_op jit(solution)/shard_map/ppermute | solution.py:751
  147.5 4.6 %collective-permute-start.27 = (f32[128,128]{1,0:T(8,128)S(1)}, f32[128,128]{1,0:T(8,128)S(1)}, u32[]{:S(2)}, u32[]{:S(2)}) collective-permute-start(f32[128,128]{1,0:T(8,128)S(1)} %add.29), channel_id=1, source_target_pairs={{0,8},{1,9},{2,10},{3,11},{4,12},{5,13},{6,14},{7,15},{8,0},{9,1},... | collective-permute-start | bytes 196616 | tf_op jit(solution)/shard_map/ppermute | solution.py:751
  152.1 9.5 %collective-permute-start.28 = (f32[128,128]{1,0:T(8,128)S(1)}, f32[128,128]{1,0:T(8,128)S(1)}, u32[]{:S(2)}, u32[]{:S(2)}) collective-permute-start(f32[128,128]{1,0:T(8,128)S(1)} %add.30), channel_id=1, source_target_pairs={{0,24},{1,25},{2,26},{3,27},{4,28},{5,29},{6,30},{7,31},{8,16},{9,... | collective-permute-start | bytes 196616 | tf_op jit(solution)/shard_map/ppermute | solution.py:751
  (4 other events, 10.5 us)

commit v6 on v5

--- a/solution.py
+++ b/solution.py
@@ -73,7 +73,7 @@
 B = 4
 STEPS = C // B
 N = 2
-CUTS = (0, 6, 16)
+CUTS = (0, 4, 16)
 
 
 def stride_rows(z):
@@ -114,8 +114,14 @@
 
 FULL = sds((C, ROWS, S))
 FULL_ROWS = sds((CELLS, S))
+HALO_ROWS = H * ROWS
+MESSAGE = sds((HALO_ROWS + 2 * NEAR, S))
 HALO = sds((H, C, C, S))
 EDGES = [sds((stop - start, 192, S)) for start, stop in zip(CUTS, CUTS[1:])]
+
+
+def halo_rows(x, z):
+    return pl.ds(pl.multiple_of(z * ROWS + x * C, C), C)
 
 
 def halves(y, half):
@@ -437,24 +443,23 @@
     )(*parcels, corner, vb, s.reshape(CELLS, S))
 
 
-def merge_kernel(part_ref, below_ref, above_ref, energy_ref, out_ref):
-    one = part_ref[1, 0:16, :] + below_ref[0:16, :] + above_ref[0:16, :]
-    out_ref[0:16, :] = one * energy_ref[16:32, :]
-    out_ref[16:32, :] = part_ref[1, 16:32, :] + below_ref[16:32, :] + above_ref[16:32, :]
+def move_pair(shares, away):
     lane = lax.broadcasted_iota(jnp.int32, (16, 128), 1)
-    below = jnp.where(lane < 32, pltpu.roll(below_ref[32:48, :], 112, 1), 0.0)
-    above = jnp.where((lane >= 16) & (lane < 48), pltpu.roll(above_ref[32:48, :], 16, 1), 0.0)
-    out_ref[32:48, :] = jnp.where(lane < 48, part_ref[1, 32:48, :], 0.0) + below + above
-
-
-def merge(part, below, above, energy):
-    return pl.pallas_call(merge_kernel, out_shape=sds((NEAR, S)), compiler_params=params(4), name="merge")(
-        part, below, above, energy
-    )
+    keep = (lane < 32) if away < 0 else (lane >= 16) & (lane < 48)
+    pair = jnp.where(keep, pltpu.roll(shares[32:48], (away * 16) % 128, 1), 0.0)
+    return jnp.concatenate([shares[0:32], pair])
 
 
 def first_kernel(s_ref, side_ref, vb_ref, *refs):
-    q_ref, mix_ref, head_ref, tail_ref = refs[2:]
+    part_ref, mate_ref, q_ref, mix_ref, head_ref, tail_ref = refs[2:]
+    step = pl.program_id(0)
+
+    @pl.when(step == 0)
+    def _():
+        for j in range(2):
+            rows = slice(HALO_ROWS + j * NEAR, HALO_ROWS + (j + 1) * NEAR)
+            head_ref[rows, :] = part_ref[j] + mate_ref[j]
+            tail_ref[rows, :] = part_ref[j + 1] + mate_ref[j + 1]
 
     def planes(edge_ref):
         for p in range(N):
@@ -470,23 +475,25 @@
                     q_ref[p, rows, :] = q
                     mix_ref[p, rows, :] = side_ref[p, rows, :] + q + dy
             for z in range(H):
-                head_ref[z, p] = mix_ref[p, stride_rows(z), :]
-                tail_ref[z, p] = mix_ref[p, stride_rows(C - H + z), :]
+                rows = halo_rows(step * N + p, z)
+                head_ref[rows, :] = mix_ref[p, stride_rows(z), :]
+                tail_ref[rows, :] = mix_ref[p, stride_rows(C - H + z), :]
 
     for_piece(refs[:2], planes)
 
 
-def make_first(s, side_part, vb, edges):
+def make_first(s, side_part, vb, edges, part, part_mate):
+    shares = pl.BlockSpec((3, NEAR, S), lambda i: (0, 0, 0))
     return pl.pallas_call(
         first_kernel,
         grid=(C // N,),
-        in_specs=[plane_spec(ROWS, N)] * 3 + edge_specs(),
-        out_specs=[plane_spec(ROWS, N), plane_spec(ROWS, N), halo_spec(N), halo_spec(N)],
-        out_shape=[FULL, FULL, HALO, HALO],
+        in_specs=[plane_spec(ROWS, N)] * 3 + edge_specs() + [shares] * 2,
+        out_specs=[plane_spec(ROWS, N), plane_spec(ROWS, N), whole(MESSAGE.shape[0]), whole(MESSAGE.shape[0])],
+        out_shape=[FULL, FULL, MESSAGE, MESSAGE],
         compiler_params=params(16),
         cost_estimate=cost(1 << 24, 14 << 20),
         name="first",
-    )(s, side_part, vb, *edges)
+    )(s, side_part, vb, *edges, part, part_mate)
 
 
 def base_kernel(s_ref, mid_ref, vb_ref, vb_mate_ref, q_ref, side_ref, part_ref, *refs):
@@ -531,7 +538,7 @@
 
 
 def second_kernel(base_ref, low_ref, high_ref, gg_high_ref, gg_low_ref, *rest):
-    own_ref, mate_ref, energy_ref, second_ref, gram_ref, cross_ref, w_ref, halo_ref = rest
+    part_ref, mate_ref, energy_ref, second_ref, gram_ref, cross_ref, w_ref, halo_ref = rest
     step = pl.program_id(0)
 
     @pl.when(step == 0)
@@ -540,19 +547,21 @@
         cross_ref[...] = jnp.zeros((S, S), F32)
         w_ref[...] = jnp.zeros((S, S), F32)
         halo_ref[...] = jnp.zeros((B, ROWS, S), F32)
-        total = own_ref[...] + mate_ref[...]
-        ones = [total[i : i + 16] for i in (0, 16, 64, 112, 160)]
-        for j in range(3):
-            row = 16 + j * NEAR
-            beside = jnp.concatenate(ones[j : j + 3] + [jnp.zeros((S - NEAR, S), F32)])
-            two = total[row + 16 : row + 32] + exact(total[row + 32 : row + 48], beside)
-            two = two * energy_ref[j * C : j * C + C, :]
-            w_ref[j * C : j * C + C, :] = 2.0 * two
-            w_ref[64 + j * C : 80 + j * C, :] = 2.0 * ones[j + 1]
+        mine = [part_ref[j] + mate_ref[j] for j in range(3)]
+        below = [move_pair(low_ref[HALO_ROWS + j * NEAR : HALO_ROWS + (j + 1) * NEAR, :], -1) for j in range(2)]
+        above = [move_pair(high_ref[HALO_ROWS + j * NEAR : HALO_ROWS + (j + 1) * NEAR, :], 1) for j in range(2)]
+        slabs = [mine[0] + below[0], mine[1] + below[1] + above[0], mine[2] + above[1]]
+        near = jnp.concatenate([slab[0:16] for slab in slabs]) * energy_ref[...]
+        lane = lax.broadcasted_iota(jnp.int32, (NEAR, S), 1)
+        pair = jnp.where(lane < NEAR, jnp.concatenate([slab[32:48] for slab in slabs]), 0.0)
+        two = jnp.concatenate([slab[16:32] for slab in slabs])
+        two = two + exact(pair, jnp.concatenate([near, jnp.zeros((S - NEAR, S), F32)]))
+        w_ref[0:NEAR, :] = 2.0 * energy_ref[...] * two
+        w_ref[64 : 64 + NEAR, :] = 2.0 * near
 
     for p in range(B):
-        low = [low_ref[j, p] for j in range(H)]
-        high = [high_ref[j, p] for j in range(H)]
+        low = [low_ref[halo_rows(step * B + p, j), :] for j in range(H)]
+        high = [high_ref[halo_rows(step * B + p, j), :] for j in range(H)]
         for z in range(H):
             add = sum((2.0 * OFF[k - 1]) * low[z - k + H] for k in range(z + 1, H + 1))
             halo_ref[p, stride_rows(z), :] = add
@@ -580,11 +589,12 @@
 
 
 def make_second(base, low, high, gg, weighted):
+    shares = pl.BlockSpec((3, NEAR, S), lambda i: (0, 0, 0))
     return pl.pallas_call(
         second_kernel,
         grid=(STEPS,),
-        in_specs=[plane_spec(), halo_spec(), halo_spec(), part_spec(0), part_spec(1)]
-        + [whole(3 * NEAR + 32), whole(3 * NEAR + 32), whole(NEAR)],
+        in_specs=[plane_spec(), whole(MESSAGE.shape[0]), whole(MESSAGE.shape[0]), part_spec(0), part_spec(1)]
+        + [shares, shares, whole(NEAR)],
         out_specs=[plane_spec(), whole()],
         out_shape=[FULL, sds((S, S))],
         scratch_shapes=[pltpu.VMEM((S, S), F32), pltpu.VMEM((S, S), F32), pltpu.VMEM((B, ROWS, S), F32)],
@@ -720,32 +730,26 @@
     two_edge, mid = pack_rest(s)
     vb = spread(parcel)
     beside = side_x(s, mate)
-    parcel_y, two_edge, beside = barrier((parcel_y, two_edge, beside))
+    parcel_y, one_edge, two_edge, beside = barrier((parcel_y, one_edge, two_edge, beside))
     two_edge = send(two_edge, over_y)
     parcel_xy = send(parcel_y, over_x)
     corner = jnp.stack([gx * C, gy * C]).astype(jnp.int32)
-    parcel_xy, one_edge = barrier((parcel_xy, one_edge))
     gg, part, energy = prep([parcel, parcel_x, parcel_y, parcel_xy], corner, vb, s)
 
     part = part + send(part, over_x)
-    own = merge(part, send(part[2], 0, 1), send(part[0], 0, -1), energy)
+    part_mate = send(part, over_y)
     side_part = side_z(s, beside, low, high)
-    own, side_part = barrier((own, side_part))
-    coefs = stack(send(own[:16], 0, 2), send(own, 0, 1), own, send(own, 0, -1), send(own[:16], 0, -2))
-    coefs, two_edge = barrier((coefs, two_edge))
-    coefs_mate = send(coefs, over_y)
-
     edges = [one_edge, two_edge]
     vb = vb.reshape(C, ROWS, S)
-    q, mix, head, tail = make_first(s, side_part, vb, edges)
+    q, mix, head, tail = make_first(s, side_part, vb, edges, part, part_mate)
     low, high = send(tail, 0, 1), send(head, 0, -1)
     mate = send(mix, over_x)
-    mid, coefs_mate = barrier((mid, coefs_mate))
+    mid, part_mate = barrier((mid, part_mate))
     mid = send(mid, over_y)
     vb_mate = spread(parcel_y).reshape(C, ROWS, S)
-    part = side_again(mix, mate)
-    base = make_base(s, mid, vb, vb_mate, q, side_part, part, edges)
-    second, gram = make_second(base, low, high, gg.reshape(2, C, ROWS, S), [coefs, coefs_mate, energy])
+    part_two = side_again(mix, mate)
+    base = make_base(s, mid, vb, vb_mate, q, side_part, part_two, edges)
+    second, gram = make_second(base, low, high, gg.reshape(2, C, ROWS, S), [part, part_mate, energy])
 
     for flip in (64, 32, 36, 1, 3, 8, 24):
         gram = gram + lax.ppermute(gram, AXES, [(d, d ^ flip) for d in range(count)])

time: 179 us -> 165 us (0.922)
  starting transfers between devices: 72.7 us -> 40.4 us
  waiting for transfers between devices: 44.2 us -> 67.4 us
  Pallas kernels: 55.4 us -> 52 us
    ppermute x22 -> x16, starting transfers between devices: 54.8 us -> 30.8 us  [send(): return lax.ppermute(value, AXES, [(d, target(d)) for d in range(count)])]
    ppermute x22 -> x16, waiting for transfers between devices: 26.7 us -> 45.2 us  [send(): return lax.ppermute(value, AXES, [(d, target(d)) for d in range(count)])]
    ppermute x7, starting transfers between devices: 17.9 us -> 9.56 us  [per_device(): lax.ppermute(gram, AXES, [(d, d ^ flip) for d in range(count)])]
    ppermute x7, waiting for transfers between devices: 17.6 us -> 22.2 us  [per_device(): lax.ppermute(gram, AXES, [(d, d ^ flip) for d in range(count)])]
    pallas_call x2 -> x1, Pallas kernels: 5.18 us -> 4.96 us  [make_second(): pl.pallas_call(second_kernel, grid=(STEPS,), in_specs=[plane_spec(), whol...]
    unnamed x15 -> x25, local copies, waits for them, and re-layouts: 3.87 us -> 3.71 us
  transfers between devices with their start and end apart: 29 -> 23, of which waited for: 12 -> 12; matrix products, arithmetic and copies ran while one was open for 2% -> 0% of each run, Pallas kernels for 17% -> 17%
where the time goes in v6:
time: 165 us; the launch traced here: 164 us
  waiting for transfers between devices  67.4 us (41%)
  Pallas kernels  52 us (32%)
  starting transfers between devices  40.4 us (24%)
  local copies, waits for them, and re-layouts  4.15 us (3%)
    ppermute x16, waiting for transfers between devices, send(): return lax.ppermute(value, AXES, [(d, target(d)) for d in range(count)])  45.2 us
    ppermute x16, starting transfers between devices, send(): return lax.ppermute(value, AXES, [(d, target(d)) for d in range(count)])  30.8 us
    ppermute x7, waiting for transfers between devices, per_device(): lax.ppermute(gram, AXES, [(d, d ^ flip) for d in range(count)])  22.2 us
    pallas_call x1, Pallas kernels, turn(): pl.pallas_call(turn_kernel, grid=(STEPS,), in_specs=[plane_spec(), whole(...  16.9 us
    ppermute x7, starting transfers between devices, per_device(): lax.ppermute(gram, AXES, [(d, d ^ flip) for d in range(count)])  9.56 us
    pallas_call x1, Pallas kernels, prep(): pl.pallas_call(prep_kernel, in_specs=[vmem] * 4 + [pl.BlockSpec(memory_sp...  7.76 us
    pallas_call x1, Pallas kernels, make_second(): pl.pallas_call(second_kernel, grid=(STEPS,), in_specs=[plane_spec(), whol...  4.96 us
    pallas_call x1, Pallas kernels, side_z(): pl.pallas_call(side_z_kernel, out_shape=FULL, scratch_shapes=[pltpu.VMEM(...  4.2 us
  transfers between devices with their start and end apart: 23, of which 12 were waited for; matrix products, arithmetic and copies ran while one was open for 0% of the time, Pallas kernels for 17%

profile of v6, /device:TPU:0, one launch (start us, length us, event | category | flops | bytes accessed | tf_op | source)
XLA Modules:
  0.0 164.4 jit_solution(15904002467967391764)
XLA Ops:
  0.0 1.6 copy-done
  1.6 3.3 %pack.1 = (f32[4,192,128]{2,1,0:T(8,128)}, f32[6,16,16,128]{3,2,1,0:T(8,128)}, f32[6,16,16,128]{3,2,1,0:T(8,128)}) custom-call(f32[16,256,128]{2,1,0:T(8,128)S(1)} %bitcast.10), custom_call_target="tpu_custom_call" | custom-call | flops 4294967296 | bytes 6291456 | tf_op jit(solution)/shard_map/pack/pallas_call | solution.py:148
  4.9 2.0 %collective-permute-start.4 = (f32[4,192,128]{2,1,0:T(8,128)}, f32[4,192,128]{2,1,0:T(8,128)S(1)}, u32[]{:S(2)}, u32[]{:S(2)}) collective-permute-start(f32[4,192,128]{2,1,0:T(8,128)} %get-tuple-element.34), channel_id=1, source_target_pairs={{0,32},{1,33},{2,34},{3,35},{4,36},{5,37},{6,38},{7,39},{8,40},{9,... | collective-permute-start | bytes 1179656 | tf_op jit(solution)/shard_map/ppermute | solution.py:711
  7.4 1.6 collective-permute-start
  9.0 6.8 %collective-permute-start.1 = (f32[24,128]{1,0:T(8,128)S(1)}, f32[24,128]{1,0:T(8,128)S(1)}, u32[]{:S(2)}, u32[]{:S(2)}) collective-permute-start(f32[24,128]{1,0:T(8,128)S(1)} %reshape.26.refs_1_), channel_id=1, source_target_pairs={{0,31},{1,0},{2,1},{3,2},{4,3},{5,4},{6,5},{7,6},{8,7},{9,8},{10,9... | collective-permute-start | bytes 36872 | tf_op jit(solution)/shard_map/ppermute | solution.py:711
  15.9 1.5 collective-permute-done.refs_0_
  17.5 2.2 %pack_rest.1 = (f32[12,192,128]{2,1,0:T(8,128)}, f32[16,64,128]{2,1,0:T(8,128)S(1)}) custom-call(f32[16,256,128]{2,1,0:T(8,128)S(1)} %bitcast.11), custom_call_target="tpu_custom_call" | custom-call | flops 2147483648 | bytes 4194304 | tf_op jit(solution)/shard_map/pack_rest/pallas_call | solution.py:169
  19.8 3.2 %side_x.1.part_ref = f32[16,256,128]{2,1,0:T(8,128)S(1)} custom-call(f32[16,256,128]{2,1,0:T(8,128)S(1)} %bitcast.12, f32[16,256,128]{2,1,0:T(8,128)} %collective-permute-done.5.mate_ref), custom_call_target="tpu_custom_call" | custom-call | flops 16777216 | bytes 6291456 | tf_op jit(solution)/shard_map/side_x/pallas_call | solution.py:218
  23.0 1.3 copy-done.2
  25.1 2.0 %collective-permute-start.12 = (f32[12,192,128]{2,1,0:T(8,128)}, f32[12,192,128]{2,1,0:T(8,128)S(1)}, u32[]{:S(2)}, u32[]{:S(2)}) collective-permute-start(f32[12,192,128]{2,1,0:T(8,128)} %get-tuple-element.43), channel_id=1, source_target_pairs={{0,32},{1,33},{2,34},{3,35},{4,36},{5,37},{6,38},{7,39},{8,40},{9,... | collective-permute-start | bytes 3538952 | tf_op jit(solution)/shard_map/ppermute | solution.py:711
  27.1 7.7 %collective-permute-start.11 = (f32[6,16,16,128]{3,2,1,0:T(8,128)}, f32[6,16,16,128]{3,2,1,0:T(8,128)}, u32[]{:S(2)}, u32[]{:S(2)}) collective-permute-start(f32[6,16,16,128]{3,2,1,0:T(8,128)} %get-tuple-element.41), channel_id=1, source_target_pairs={{0,31},{1,0},{2,1},{3,2},{4,3},{5,4},{6,5},{7,6},{8,7},{9,8},{10,9... | collective-permute-start | bytes 2359304 | tf_op jit(solution)/shard_map/ppermute | solution.py:711
  36.3 7.8 %prep.1 = (bf16[2,4096,128]{2,1,0:T(8,128)(2,1)S(1)}, f32[3,48,128]{2,1,0:T(8,128)S(1)}, f32[48,128]{1,0:T(8,128)S(1)}) custom-call(f32[104,128]{1,0:T(8,128)S(1)} %stack.13.parcel_ref.refs_0_, f32[104,128]{1,0:T(8,128)S(1)} %collective-permute-done.2.refs_1_, f32[104,128]{1,0:T(8,128)S(1)} %collective-permute-done.3.refs_2_.parcel_ref, ...), custom_call_target="tpu_custom_call" | custom-call | flops 134217728 | bytes 10485760 | tf_op jit(solution)/shard_map/prep/pallas_call | solution.py:428
  45.5 6.0 %collective-permute-done.10.low_ref = f32[6,16,16,128]{3,2,1,0:T(8,128)} collective-permute-done((f32[6,16,16,128]{3,2,1,0:T(8,128)}, f32[6,16,16,128]{3,2,1,0:T(8,128)}, u32[]{:S(2)}, u32[]{:S(2)}) %collective-permute-start.10) | collective-permute-done | bytes 786464 | tf_op jit(solution)/shard_map/ppermute | solution.py:711
  51.6 4.2 %side_z.1.side_ref = f32[16,256,128]{2,1,0:T(8,128)S(1)} custom-call(f32[16,256,128]{2,1,0:T(8,128)S(1)} %bitcast.14, f32[16,256,128]{2,1,0:T(8,128)S(1)} %copy-done.3, f32[6,16,16,128]{3,2,1,0:T(8,128)} %collective-permute-done.10.low_ref, f32[6,16,16,128]{3,2,1,0:T(8,128)} %collective-permute-done.11.high_ref), custom_call_target="tpu_custom_call" | custom-call | flops 16777216 | bytes 8388608 | tf_op jit(solution)/shard_map/side_z/pallas_call | solution.py:243
  55.8 15.3 %collective-permute-done.8.refs_3_.rest_1_ = f32[3,48,128]{2,1,0:T(8,128)S(1)} collective-permute-done((f32[3,48,128]{2,1,0:T(8,128)S(1)}, f32[3,48,128]{2,1,0:T(8,128)S(1)}, u32[]{:S(2)}, u32[]{:S(2)}) %collective-permute-start.8) | collective-permute-done | bytes 73760 | tf_op jit(solution)/shard_map/ppermute | solution.py:711
  71.1 2.1 %first.1 = (f32[16,256,128]{2,1,0:T(8,128)S(1)}, f32[16,256,128]{2,1,0:T(8,128)S(1)}, f32[1632,128]{1,0:T(8,128)S(1)}, f32[1632,128]{1,0:T(8,128)S(1)}) custom-call(f32[16,256,128]{2,1,0:T(8,128)S(1)} %bitcast.15, f32[16,256,128]{2,1,0:T(8,128)S(1)} %side_z.1.side_ref, f32[16,256,128]{2,1,0:T(8,128)S(1)} %bitcast.17, f32[4,192,128]{2,1,0:T(8,128)S(1)} %copy-done.5, ...), custom_call_target="tpu_custom_call" | custom-call | flops 16777216 | bytes 14680064 | tf_op jit(solution)/shard_map/first/pallas_call | solution.py:487
  73.3 7.7 %collective-permute-start.15 = (f32[1632,128]{1,0:T(8,128)S(1)}, f32[1632,128]{1,0:T(8,128)S(1)}, u32[]{:S(2)}, u32[]{:S(2)}) collective-permute-start(f32[1632,128]{1,0:T(8,128)S(1)} %get-tuple-element.47), channel_id=1, source_target_pairs={{0,31},{1,0},{2,1},{3,2},{4,3},{5,4},{6,5},{7,6},{8,7},{9,8},{10,9... | collective-permute-start | bytes 2506760 | tf_op jit(solution)/shard_map/ppermute | solution.py:711
  81.1 1.7 %collective-permute-start.9 = (f32[16,64,128]{2,1,0:T(8,128)S(1)}, f32[16,64,128]{2,1,0:T(8,128)S(1)}, u32[]{:S(2)}, u32[]{:S(2)}) collective-permute-start(f32[16,64,128]{2,1,0:T(8,128)S(1)} %copy-done.7), channel_id=1, source_target_pairs={{0,32},{1,33},{2,34},{3,35},{4,36},{5,37},{6,38},{7,39},{8,40},{9,... | collective-permute-start | bytes 1572872 | tf_op jit(solution)/shard_map/ppermute | solution.py:711
  83.6 2.9 %side_again.1.part_ref = f32[16,256,128]{2,1,0:T(8,128)S(1)} custom-call(f32[16,256,128]{2,1,0:T(8,128)S(1)} %get-tuple-element.45.s_ref, f32[16,256,128]{2,1,0:T(8,128)S(1)} %collective-permute-done.13.mate_ref), custom_call_target="tpu_custom_call" | custom-call | flops 33554432 | bytes 6291456 | tf_op jit(solution)/shard_map/side_again/pallas_call | solution.py:270
  86.5 21.4 %collective-permute-done.9.mid_ref = f32[16,64,128]{2,1,0:T(8,128)S(1)} collective-permute-done((f32[16,64,128]{2,1,0:T(8,128)S(1)}, f32[16,64,128]{2,1,0:T(8,128)S(1)}, u32[]{:S(2)}, u32[]{:S(2)}) %collective-permute-start.9) | collective-permute-done | bytes 524320 | tf_op jit(solution)/shard_map/ppermute | solution.py:711
  107.9 2.7 %base.1.base_ref = f32[16,256,128]{2,1,0:T(8,128)S(1)} custom-call(f32[16,256,128]{2,1,0:T(8,128)S(1)} %bitcast.16, f32[16,64,128]{2,1,0:T(8,128)S(1)} %collective-permute-done.9.mid_ref, f32[16,256,128]{2,1,0:T(8,128)S(1)} %bitcast.18, f32[16,256,128]{2,1,0:T(8,128)S(1)} %bitcast.21, f32[16,256,128]{2,1,0:T(8,128)S(1)} %get-tuple-element.44.q_ref, ...), custom_call_target="tpu_custom_call" | custom-call | flops 33554432 | bytes 16777216 | tf_op jit(solution)/shard_map/base/pallas_call | solution.py:528
  110.6 5.0 %second.1 = (f32[16,256,128]{2,1,0:T(8,128)S(1)}, f32[128,128]{1,0:T(8,128)S(1)}) custom-call(f32[16,256,128]{2,1,0:T(8,128)S(1)} %base.1.base_ref, f32[1632,128]{1,0:T(8,128)S(1)} %collective-permute-done.14.low_ref, f32[1632,128]{1,0:T(8,128)S(1)} %collective-permute-done.15.high_ref, bf16[2,16,256,128]{3,2,1,0:T(8,128)(2,1)S(1)} %bitcast.19, ...), custom_call_target="tpu_custom_call" | custom-call | flops 134217728 | bytes 8388608 | tf_op jit(solution)/shard_map/second/pallas_call | solution.py:593
  117.5 3.8 %collective-permute-done.17 = f32[128,128]{1,0:T(8,128)S(1)} collective-permute-done((f32[128,128]{1,0:T(8,128)S(1)}, f32[128,128]{1,0:T(8,128)S(1)}, u32[]{:S(2)}, u32[]{:S(2)}) %collective-permute-start.17) | collective-permute-done | bytes 65568 | tf_op jit(solution)/shard_map/ppermute | solution.py:755
  121.3 4.0 %collective-permute-start.18 = (f32[128,128]{1,0:T(8,128)S(1)}, f32[128,128]{1,0:T(8,128)S(1)}, u32[]{:S(2)}, u32[]{:S(2)}) collective-permute-start(f32[128,128]{1,0:T(8,128)S(1)} %add.26), channel_id=1, source_target_pairs={{0,36},{1,37},{2,38},{3,39},{4,32},{5,33},{6,34},{7,35},{8,44},{9,... | collective-permute-start | bytes 196616 | tf_op jit(solution)/shard_map/ppermute | solution.py:755
  125.3 2.2 %collective-permute-done.18 = f32[128,128]{1,0:T(8,128)S(1)} collective-permute-done((f32[128,128]{1,0:T(8,128)S(1)}, f32[128,128]{1,0:T(8,128)S(1)}, u32[]{:S(2)}, u32[]{:S(2)}) %collective-permute-start.18) | collective-permute-done | bytes 65568 | tf_op jit(solution)/shard_map/ppermute | solution.py:755
  127.7 4.3 %collective-permute-done.19 = f32[128,128]{1,0:T(8,128)S(1)} collective-permute-done((f32[128,128]{1,0:T(8,128)S(1)}, f32[128,128]{1,0:T(8,128)S(1)}, u32[]{:S(2)}, u32[]{:S(2)}) %collective-permute-start.19) | collective-permute-done | bytes 65568 | tf_op jit(solution)/shard_map/ppermute | solution.py:755
  131.9 1.5 collective-permute-start.20
  133.4 4.1 %collective-permute-done.20 = f32[128,128]{1,0:T(8,128)S(1)} collective-permute-done((f32[128,128]{1,0:T(8,128)S(1)}, f32[128,128]{1,0:T(8,128)S(1)}, u32[]{:S(2)}, u32[]{:S(2)}) %collective-permute-start.20) | collective-permute-done | bytes 65568 | tf_op jit(solution)/shard_map/ppermute | solution.py:755
  138.5 3.4 %collective-permute-done.21 = f32[128,128]{1,0:T(8,128)S(1)} collective-permute-done((f32[128,128]{1,0:T(8,128)S(1)}, f32[128,128]{1,0:T(8,128)S(1)}, u32[]{:S(2)}, u32[]{:S(2)}) %collective-permute-start.21) | collective-permute-done | bytes 65568 | tf_op jit(solution)/shard_map/ppermute | solution.py:755
  141.9 2.4 %collective-permute-start.22 = (f32[128,128]{1,0:T(8,128)S(1)}, f32[128,128]{1,0:T(8,128)S(1)}, u32[]{:S(2)}, u32[]{:S(2)}) collective-permute-start(f32[128,128]{1,0:T(8,128)S(1)} %add.30), channel_id=1, source_target_pairs={{0,24},{1,25},{2,26},{3,27},{4,28},{5,29},{6,30},{7,31},{8,16},{9,... | collective-permute-start | bytes 196616 | tf_op jit(solution)/shard_map/ppermute | solution.py:755
  144.3 3.2 %collective-permute-done.22 = f32[128,128]{1,0:T(8,128)S(1)} collective-permute-done((f32[128,128]{1,0:T(8,128)S(1)}, f32[128,128]{1,0:T(8,128)S(1)}, u32[]{:S(2)}, u32[]{:S(2)}) %collective-permute-start.22) | collective-permute-done | bytes 65568 | tf_op jit(solution)/shard_map/ppermute | solution.py:755
  147.4 16.9 %turn.1 = f32[16,256,128]{2,1,0:T(8,128)} custom-call(f32[16,256,128]{2,1,0:T(8,128)S(1)} %get-tuple-element.51.second_ref, f32[128,128]{1,0:T(8,128)S(1)} %add_multiply_fusion.gram_ref), custom_call_target="tpu_custom_call" | custom-call | flops 268435456 | bytes 4194304 | tf_op jit(solution)/shard_map/turn/pallas_call | solution.py:688
  (69 shorter events, 8.3 us)
Async XLA Ops:
  0.0 19.8 %collective-permute-start.5 = (f32[16,256,128]{2,1,0:T(8,128)}, f32[16,256,128]{2,1,0:T(8,128)}, u32[]{:S(2)}, u32[]{:S(2)}) collective-permute-start(f32[16,256,128]{2,1,0:T(8,128)} %bitcast.9), channel_id=1, source_target_pairs={{0,64},{1,65},{2,66},{3,67},{4,68},{5,69},{6,70},{7,71},{8,72},{9,... | collective-permute-start | bytes 6291464 | tf_op jit(solution)/shard_map/ppermute | solution.py:711
  1.6 5.3 %copy-start.8 = (f32[4,9,9,9]{3,0,2,1:T(4,128)S(1)}, f32[4,9,9,9]{3,0,2,1:T(4,128)}, u32[]{:S(2)}) copy-start(f32[4,9,9,9]{3,0,2,1:T(4,128)} %param.8) | copy-start | bytes 34996
  1.6 5.5 %copy-start.10 = (s32[4,3]{1,0:T(4,128)S(1)}, s32[4,3]{1,0:T(4,128)}, u32[]{:S(2)}) copy-start(s32[4,3]{1,0:T(4,128)} %param.7) | copy-start | bytes 148
  1.6 5.6 %copy-start.11 = (f32[4]{0:T(128)S(1)}, f32[4]{0:T(128)}, u32[]{:S(2)}) copy-start(f32[4]{0:T(128)} %param.9) | copy-start | bytes 52
  1.6 14.2 %copy-start.9 = (f32[16,16,16]{2,1,0:T(8,128)S(1)}, f32[16,16,16]{2,1,0:T(8,128)}, u32[]{:S(2)}) copy-start(f32[16,16,16]{2,1,0:T(8,128)} %param.6) | copy-start | bytes 49156
  1.6 15.9 %copy-start.1 = (f32[16,16,16,128]{3,2,1,0:T(8,128)S(1)}, f32[16,16,16,128]{3,2,1,0:T(8,128)}, u32[]{:S(2)}) copy-start(f32[16,16,16,128]{3,2,1,0:T(8,128)} %param.5) | copy-start | bytes 6291460
  4.9 19.4 %collective-permute-start.4 = (f32[4,192,128]{2,1,0:T(8,128)}, f32[4,192,128]{2,1,0:T(8,128)S(1)}, u32[]{:S(2)}, u32[]{:S(2)}) collective-permute-start(f32[4,192,128]{2,1,0:T(8,128)} %get-tuple-element.34), channel_id=1, source_target_pairs={{0,32},{1,33},{2,34},{3,35},{4,36},{5,37},{6,38},{7,39},{8,40},{9,... | collective-permute-start | bytes 1179656 | tf_op jit(solution)/shard_map/ppermute | solution.py:711
  7.4 10.0 %collective-permute-start = (f32[24,128]{1,0:T(8,128)S(1)}, f32[24,128]{1,0:T(8,128)S(1)}, u32[]{:S(2)}, u32[]{:S(2)}) collective-permute-start(f32[24,128]{1,0:T(8,128)S(1)} %reshape.26.refs_1_), channel_id=1, source_target_pairs={{0,1},{1,2},{2,3},{3,4},{4,5},{5,6},{6,7},{7,8},{8,9},{9,10},{10,1... | collective-permute-start | bytes 36872 | tf_op jit(solution)/shard_map/ppermute | solution.py:711
  9.0 8.4 %collective-permute-start.1 = (f32[24,128]{1,0:T(8,128)S(1)}, f32[24,128]{1,0:T(8,128)S(1)}, u32[]{:S(2)}, u32[]{:S(2)}) collective-permute-start(f32[24,128]{1,0:T(8,128)S(1)} %reshape.26.refs_1_), channel_id=1, source_target_pairs={{0,31},{1,0},{2,1},{3,2},{4,3},{5,4},{6,5},{7,6},{8,7},{9,8},{10,9... | collective-permute-start | bytes 36872 | tf_op jit(solution)/shard_map/ppermute | solution.py:711
  17.4 6.9 %collective-permute-start.3 = (f32[104,128]{1,0:T(8,128)S(1)}, f32[104,128]{1,0:T(8,128)S(1)}, u32[]{:S(2)}, u32[]{:S(2)}) collective-permute-start(f32[104,128]{1,0:T(8,128)S(1)} %stack.13.parcel_ref.refs_0_), channel_id=1, source_target_pairs={{0,32},{1,33},{2,34},{3,35},{4,36},{5,37},{6,38},{7,39},{8,40},{9,... | collective-permute-start | bytes 159752 | tf_op jit(solution)/shard_map/ppermute | solution.py:711
  19.8 3.3 %copy-start.6 = (f32[16,64,128]{2,1,0:T(8,128)}, f32[16,64,128]{2,1,0:T(8,128)S(1)}, u32[]{:S(2)}) copy-start(f32[16,64,128]{2,1,0:T(8,128)S(1)} %get-tuple-element.38) | copy-start | bytes 1572868
  25.1 46.0 %collective-permute-start.12 = (f32[12,192,128]{2,1,0:T(8,128)}, f32[12,192,128]{2,1,0:T(8,128)S(1)}, u32[]{:S(2)}, u32[]{:S(2)}) collective-permute-start(f32[12,192,128]{2,1,0:T(8,128)} %get-tuple-element.43), channel_id=1, source_target_pairs={{0,32},{1,33},{2,34},{3,35},{4,36},{5,37},{6,38},{7,39},{8,40},{9,... | collective-permute-start | bytes 3538952 | tf_op jit(solution)/shard_map/ppermute | solution.py:711
  27.1 24.5 %collective-permute-start.10 = (f32[6,16,16,128]{3,2,1,0:T(8,128)}, f32[6,16,16,128]{3,2,1,0:T(8,128)}, u32[]{:S(2)}, u32[]{:S(2)}) collective-permute-start(f32[6,16,16,128]{3,2,1,0:T(8,128)} %get-tuple-element.40), channel_id=1, source_target_pairs={{0,1},{1,2},{2,3},{3,4},{4,5},{5,6},{6,7},{7,8},{8,9},{9,10},{10,1... | collective-permute-start | bytes 2359304 | tf_op jit(solution)/shard_map/ppermute | solution.py:711
  27.1 24.5 %collective-permute-start.11 = (f32[6,16,16,128]{3,2,1,0:T(8,128)}, f32[6,16,16,128]{3,2,1,0:T(8,128)}, u32[]{:S(2)}, u32[]{:S(2)}) collective-permute-start(f32[6,16,16,128]{3,2,1,0:T(8,128)} %get-tuple-element.41), channel_id=1, source_target_pairs={{0,31},{1,0},{2,1},{3,2},{4,3},{5,4},{6,5},{7,6},{8,7},{9,8},{10,9... | collective-permute-start | bytes 2359304 | tf_op jit(solution)/shard_map/ppermute | solution.py:711
  34.8 1.4 collective-permute-start.2
  34.8 1.4 collective-permute-start.6
  36.2 15.3 %copy-start.3 = (f32[16,256,128]{2,1,0:T(8,128)S(1)}, f32[16,256,128]{2,1,0:T(8,128)}, u32[]{:S(2)}) copy-start(f32[16,256,128]{2,1,0:T(8,128)} %copy-done.2) | copy-start | bytes 6291460
  44.0 1.3 collective-permute-start.7
  45.4 25.7 %copy-start.5 = (f32[4,192,128]{2,1,0:T(8,128)S(1)}, f32[4,192,128]{2,1,0:T(8,128)}, u32[]{:S(2)}) copy-start(f32[4,192,128]{2,1,0:T(8,128)} %copy-done.4) | copy-start | bytes 1179652
  45.4 25.7 %collective-permute-start.8 = (f32[3,48,128]{2,1,0:T(8,128)S(1)}, f32[3,48,128]{2,1,0:T(8,128)S(1)}, u32[]{:S(2)}, u32[]{:S(2)}) collective-permute-start(f32[3,48,128]{2,1,0:T(8,128)S(1)} %add.24.refs_2_.rest_0_), channel_id=1, source_target_pairs={{0,32},{1,33},{2,34},{3,35},{4,36},{5,37},{6,38},{7,39},{8,40},{9,... | collective-permute-start | bytes 221192 | tf_op jit(solution)/shard_map/ppermute | solution.py:711
  71.1 10.0 %copy-start.7 = (f32[16,64,128]{2,1,0:T(8,128)S(1)}, f32[16,64,128]{2,1,0:T(8,128)}, u32[]{:S(2)}) copy-start(f32[16,64,128]{2,1,0:T(8,128)} %copy-done.6) | copy-start | bytes 1572868
  73.2 10.4 %collective-permute-start.13 = (f32[16,256,128]{2,1,0:T(8,128)S(1)}, f32[16,256,128]{2,1,0:T(8,128)S(1)}, u32[]{:S(2)}, u32[]{:S(2)}) collective-permute-start(f32[16,256,128]{2,1,0:T(8,128)S(1)} %get-tuple-element.45.s_ref), channel_id=1, source_target_pairs={{0,64},{1,65},{2,66},{3,67},{4,68},{5,69},{6,70},{7,71},{8,72},{9,... | collective-permute-start | bytes 6291464 | tf_op jit(solution)/shard_map/ppermute | solution.py:711
  73.2 37.4 %collective-permute-start.14 = (f32[1632,128]{1,0:T(8,128)S(1)}, f32[1632,128]{1,0:T(8,128)S(1)}, u32[]{:S(2)}, u32[]{:S(2)}) collective-permute-start(f32[1632,128]{1,0:T(8,128)S(1)} %get-tuple-element.46), channel_id=1, source_target_pairs={{0,1},{1,2},{2,3},{3,4},{4,5},{5,6},{6,7},{7,8},{8,9},{9,10},{10,1... | collective-permute-start | bytes 2506760 | tf_op jit(solution)/shard_map/ppermute | solution.py:711
  73.3 37.3 %collective-permute-start.15 = (f32[1632,128]{1,0:T(8,128)S(1)}, f32[1632,128]{1,0:T(8,128)S(1)}, u32[]{:S(2)}, u32[]{:S(2)}) collective-permute-start(f32[1632,128]{1,0:T(8,128)S(1)} %get-tuple-element.47), channel_id=1, source_target_pairs={{0,31},{1,0},{2,1},{3,2},{4,3},{5,4},{6,5},{7,6},{8,7},{9,8},{10,9... | collective-permute-start | bytes 2506760 | tf_op jit(solution)/shard_map/ppermute | solution.py:711
  81.1 26.8 %collective-permute-start.9 = (f32[16,64,128]{2,1,0:T(8,128)S(1)}, f32[16,64,128]{2,1,0:T(8,128)S(1)}, u32[]{:S(2)}, u32[]{:S(2)}) collective-permute-start(f32[16,64,128]{2,1,0:T(8,128)S(1)} %copy-done.7), channel_id=1, source_target_pairs={{0,32},{1,33},{2,34},{3,35},{4,36},{5,37},{6,38},{7,39},{8,40},{9,... | collective-permute-start | bytes 1572872 | tf_op jit(solution)/shard_map/ppermute | solution.py:711
  115.6 1.3 collective-permute-start.16
  117.0 4.3 %collective-permute-start.17 = (f32[128,128]{1,0:T(8,128)S(1)}, f32[128,128]{1,0:T(8,128)S(1)}, u32[]{:S(2)}, u32[]{:S(2)}) collective-permute-start(f32[128,128]{1,0:T(8,128)S(1)} %add.25), channel_id=1, source_target_pairs={{0,32},{1,33},{2,34},{3,35},{4,36},{5,37},{6,38},{7,39},{8,40},{9,... | collective-permute-start | bytes 196616 | tf_op jit(solution)/shard_map/ppermute | solution.py:755
  121.3 6.3 %collective-permute-start.18 = (f32[128,128]{1,0:T(8,128)S(1)}, f32[128,128]{1,0:T(8,128)S(1)}, u32[]{:S(2)}, u32[]{:S(2)}) collective-permute-start(f32[128,128]{1,0:T(8,128)S(1)} %add.26), channel_id=1, source_target_pairs={{0,36},{1,37},{2,38},{3,39},{4,32},{5,33},{6,34},{7,35},{8,44},{9,... | collective-permute-start | bytes 196616 | tf_op jit(solution)/shard_map/ppermute | solution.py:755
  127.6 4.3 %collective-permute-start.19 = (f32[128,128]{1,0:T(8,128)S(1)}, f32[128,128]{1,0:T(8,128)S(1)}, u32[]{:S(2)}, u32[]{:S(2)}) collective-permute-start(f32[128,128]{1,0:T(8,128)S(1)} %add.27), channel_id=1, source_target_pairs={{0,1},{1,0},{2,3},{3,2},{4,5},{5,4},{6,7},{7,6},{8,9},{9,8},{10,11... | collective-permute-start | bytes 196616 | tf_op jit(solution)/shard_map/ppermute | solution.py:755
  131.9 5.6 %collective-permute-start.20 = (f32[128,128]{1,0:T(8,128)S(1)}, f32[128,128]{1,0:T(8,128)S(1)}, u32[]{:S(2)}, u32[]{:S(2)}) collective-permute-start(f32[128,128]{1,0:T(8,128)S(1)} %add.28), channel_id=1, source_target_pairs={{0,3},{1,2},{2,1},{3,0},{4,7},{5,6},{6,5},{7,4},{8,11},{9,10},{10,... | collective-permute-start | bytes 196616 | tf_op jit(solution)/shard_map/ppermute | solution.py:755
  137.5 4.3 %collective-permute-start.21 = (f32[128,128]{1,0:T(8,128)S(1)}, f32[128,128]{1,0:T(8,128)S(1)}, u32[]{:S(2)}, u32[]{:S(2)}) collective-permute-start(f32[128,128]{1,0:T(8,128)S(1)} %add.29), channel_id=1, source_target_pairs={{0,8},{1,9},{2,10},{3,11},{4,12},{5,13},{6,14},{7,15},{8,0},{9,1},... | collective-permute-start | bytes 196616 | tf_op jit(solution)/shard_map/ppermute | solution.py:755
  141.9 5.6 %collective-permute-start.22 = (f32[128,128]{1,0:T(8,128)S(1)}, f32[128,128]{1,0:T(8,128)S(1)}, u32[]{:S(2)}, u32[]{:S(2)}) collective-permute-start(f32[128,128]{1,0:T(8,128)S(1)} %add.30), channel_id=1, source_target_pairs={{0,24},{1,25},{2,26},{3,27},{4,28},{5,29},{6,30},{7,31},{8,16},{9,... | collective-permute-start | bytes 196616 | tf_op jit(solution)/shard_map/ppermute | solution.py:755
  (3 other events, 3.7 us)

commit v7 on v6

--- a/solution.py
+++ b/solution.py
@@ -73,7 +73,7 @@
 B = 4
 STEPS = C // B
 N = 2
-CUTS = (0, 4, 16)
+CUTS = (0, 6, 12, 16)
 
 
 def stride_rows(z):
@@ -103,15 +103,29 @@
     return [spec(start, stop) for start, stop in zip(CUTS, CUTS[1:])]
 
 
-def for_piece(pieces, body):
+def for_piece(pieces, body, inner_ref=None):
     step = pl.program_id(0)
-    for piece, start, stop in zip(pieces, CUTS, CUTS[1:]):
-
-        @pl.when((step >= start // N) & (step < stop // N))
-        def _(piece=piece):
-            body(piece)
-
-
+    for j, (start, stop) in enumerate(zip(CUTS, CUTS[1:])):
+        here = (step >= start // N) & (step < stop // N)
+        if inner_ref is None or j < len(CUTS) - 2:
+
+            @pl.when(here)
+            def _(j=j):
+                body(pieces[j])
+
+        else:
+            inner = inner_ref[0] == 1
+
+            @pl.when(here & inner)
+            def _(j=j):
+                body(pieces[j])
+
+            @pl.when(here & jnp.logical_not(inner))
+            def _(j=j):
+                body(pieces[j + 1])
+
+
+SCALARS = pl.BlockSpec(memory_space=pltpu.SMEM)
 FULL = sds((C, ROWS, S))
 FULL_ROWS = sds((CELLS, S))
 HALO_ROWS = H * ROWS
@@ -157,11 +171,8 @@
     )(s)
 
 
-def pack_rest_kernel(s_ref, edge_ref, mid_ref):
-    @pl.when(pl.program_id(0) >= CUTS[1] // N)
-    def _():
-        pack_edges(s_ref, edge_ref)
-
+def pack_rest_kernel(s_ref, two_ref, three_ref, mid_ref):
+    for_piece([None, two_ref, three_ref], lambda out_ref: out_ref is None or pack_edges(s_ref, out_ref))
     mid_ref[...] = s_ref[:, 96:160, :]
 
 
@@ -451,7 +462,7 @@
 
 
 def first_kernel(s_ref, side_ref, vb_ref, *refs):
-    part_ref, mate_ref, q_ref, mix_ref, head_ref, tail_ref = refs[2:]
+    inner_ref, part_ref, mate_ref, q_ref, mix_ref, head_ref, tail_ref = refs[4:]
     step = pl.program_id(0)
 
     @pl.when(step == 0)
@@ -479,25 +490,25 @@
                 head_ref[rows, :] = mix_ref[p, stride_rows(z), :]
                 tail_ref[rows, :] = mix_ref[p, stride_rows(C - H + z), :]
 
-    for_piece(refs[:2], planes)
-
-
-def make_first(s, side_part, vb, edges, part, part_mate):
+    for_piece(refs[:4], planes, inner_ref)
+
+
+def make_first(s, side_part, vb, edges, inner, part, part_mate):
     shares = pl.BlockSpec((3, NEAR, S), lambda i: (0, 0, 0))
     return pl.pallas_call(
         first_kernel,
         grid=(C // N,),
-        in_specs=[plane_spec(ROWS, N)] * 3 + edge_specs() + [shares] * 2,
+        in_specs=[plane_spec(ROWS, N)] * 3 + edge_specs() + edge_specs()[-1:] + [SCALARS] + [shares] * 2,
         out_specs=[plane_spec(ROWS, N), plane_spec(ROWS, N), whole(MESSAGE.shape[0]), whole(MESSAGE.shape[0])],
         out_shape=[FULL, FULL, MESSAGE, MESSAGE],
         compiler_params=params(16),
         cost_estimate=cost(1 << 24, 14 << 20),
         name="first",
-    )(s, side_part, vb, *edges, part, part_mate)
+    )(s, side_part, vb, *edges, inner, part, part_mate)
 
 
 def base_kernel(s_ref, mid_ref, vb_ref, vb_mate_ref, q_ref, side_ref, part_ref, *refs):
-    out_ref = refs[2]
+    inner_ref, out_ref = refs[4:]
 
     def planes(edge_ref):
         for p in range(N):
@@ -521,20 +532,24 @@
                     total = total + vb_ref[p, rows, :] * (side_ref[p, rows, :] + q[y])
                     out_ref[p, rows, :] = 2.0 * (total + part_ref[p, rows, :]) - ring[y]
 
-    for_piece(refs[:2], planes)
-
-
-def make_base(s, mid, vb, vb_mate, q, side_part, part, edges):
+    for_piece(refs[:4], planes, inner_ref)
+
+
+def make_base(s, mid, vb, vb_mate, q, side_part, part, edges, inner):
     return pl.pallas_call(
         base_kernel,
         grid=(C // N,),
-        in_specs=[plane_spec(ROWS, N), plane_spec(64, N)] + [plane_spec(ROWS, N)] * 5 + edge_specs(),
+        in_specs=[plane_spec(ROWS, N), plane_spec(64, N)]
+        + [plane_spec(ROWS, N)] * 5
+        + edge_specs()
+        + edge_specs()[-1:]
+        + [SCALARS],
         out_specs=plane_spec(ROWS, N),
         out_shape=FULL,
         compiler_params=params(16),
         cost_estimate=cost(1 << 25, 16 << 20),
         name="base",
-    )(s, mid, vb, vb_mate, q, side_part, part, *edges)
+    )(s, mid, vb, vb_mate, q, side_part, part, *edges, inner)
 
 
 def second_kernel(base_ref, low_ref, high_ref, gg_high_ref, gg_low_ref, *rest):
@@ -711,6 +726,9 @@
         return lax.ppermute(value, AXES, [(d, target(d)) for d in range(count)])
 
     over_x, over_y = 2 * depth, depth
+    inner_ones = [d for d in range(count) if d % 4 in (1, 2)]
+    outer_ones = [d for d in range(count) if d % 4 in (0, 3)]
+    inner = ((lax.axis_index("gzs") + 1) // 2 % 2).astype(jnp.int32).reshape(1)
     s = states.reshape(C, ROWS, S)
     pot = potential.reshape(32, 128)
 
@@ -727,28 +745,32 @@
     parcel_y = send(parcel, over_y)
     parcel_x = send(parcel, over_x)
     low, high = send(tail, 0, 1), send(head, 0, -1)
-    two_edge, mid = pack_rest(s)
+    two_edge, three_edge, mid = pack_rest(s)
     vb = spread(parcel)
     beside = side_x(s, mate)
-    parcel_y, one_edge, two_edge, beside = barrier((parcel_y, one_edge, two_edge, beside))
+    parcel_y, one_edge, two_edge, three_edge, beside = barrier((parcel_y, one_edge, two_edge, three_edge, beside))
+    relayed = lax.ppermute(three_edge, AXES, [(d, d ^ over_y ^ 1) for d in outer_ones])
     two_edge = send(two_edge, over_y)
     parcel_xy = send(parcel_y, over_x)
     corner = jnp.stack([gx * C, gy * C]).astype(jnp.int32)
     gg, part, energy = prep([parcel, parcel_x, parcel_y, parcel_xy], corner, vb, s)
 
+    part, relayed, three_edge = barrier((part, relayed, three_edge))
+    relayed = lax.ppermute(relayed, AXES, [(d, d ^ 1) for d in inner_ones])
+    three_edge = lax.ppermute(three_edge, AXES, [(d, d ^ over_y) for d in inner_ones])
     part = part + send(part, over_x)
     part_mate = send(part, over_y)
     side_part = side_z(s, beside, low, high)
-    edges = [one_edge, two_edge]
+    edges = [one_edge, two_edge, three_edge, relayed]
     vb = vb.reshape(C, ROWS, S)
-    q, mix, head, tail = make_first(s, side_part, vb, edges, part, part_mate)
+    q, mix, head, tail = make_first(s, side_part, vb, edges, inner, part, part_mate)
     low, high = send(tail, 0, 1), send(head, 0, -1)
     mate = send(mix, over_x)
     mid, part_mate = barrier((mid, part_mate))
     mid = send(mid, over_y)
     vb_mate = spread(parcel_y).reshape(C, ROWS, S)
     part_two = side_again(mix, mate)
-    base = make_base(s, mid, vb, vb_mate, q, side_part, part_two, edges)
+    base = make_base(s, mid, vb, vb_mate, q, side_part, part_two, edges, inner)
     second, gram = make_second(base, low, high, gg.reshape(2, C, ROWS, S), [part, part_mate, energy])
 
     for flip in (64, 32, 36, 1, 3, 8, 24):

time: 165 us -> 165 us (level)
  waiting for transfers between devices: 67.4 us -> 53.6 us
  local copies, waits for them, and re-layouts: 4.15 us -> 9.89 us
  starting transfers between devices: 40.4 us -> 45.7 us
  Pallas kernels: 52 us -> 54.8 us
    ppermute x16, waiting for transfers between devices: 45.2 us -> 30.3 us  [send(): return lax.ppermute(value, AXES, [(d, target(d)) for d in range(count)])]
    unnamed x25 -> x31, local copies, waits for them, and re-layouts: 3.71 us -> 8.49 us
    ppermute x0 -> x3, starting transfers between devices: none -> 4.72 us  [the longest x1 2.03 us: per_device(): lax.ppermute(three_edge, AXES, [(d, d ^ over_y ^ 1) for d in outer_ones])]
    pallas_call x1, Pallas kernels: 2.74 us -> 4.8 us  [make_base(): pl.pallas_call(base_kernel, grid=(C // N,), in_specs=[plane_spec(ROWS, N)...]
    pallas_call x1, Pallas kernels: 2.06 us -> 4.1 us  [make_first(): pl.pallas_call(first_kernel, grid=(C // N,), in_specs=[plane_spec(ROWS, N...]
  transfers between devices with their start and end apart: 23 -> 26, of which waited for: 12 -> 13; matrix products, arithmetic and copies ran while one was open for 0% -> 1% of each run, Pallas kernels for 17% -> 17%
where the time goes in v7:
time: 165 us
  Pallas kernels  54.8 us (33%)
  waiting for transfers between devices  53.6 us (32%)
  starting transfers between devices  45.7 us (28%)
  local copies, waits for them, and re-layouts  9.89 us (6%)
    ppermute x16, starting transfers between devices, send(): return lax.ppermute(value, AXES, [(d, target(d)) for d in range(count)])  32.1 us
    ppermute x16, waiting for transfers between devices, send(): return lax.ppermute(value, AXES, [(d, target(d)) for d in range(count)])  30.3 us
    ppermute x7, waiting for transfers between devices, per_device(): lax.ppermute(gram, AXES, [(d, d ^ flip) for d in range(count)])  23 us
    pallas_call x1, Pallas kernels, turn(): pl.pallas_call(turn_kernel, grid=(STEPS,), in_specs=[plane_spec(), whole(...  17 us
    ppermute x7, starting transfers between devices, per_device(): lax.ppermute(gram, AXES, [(d, d ^ flip) for d in range(count)])  8.83 us
    unnamed x31, local copies, waits for them, and re-layouts  8.49 us
    pallas_call x1, Pallas kernels, prep(): pl.pallas_call(prep_kernel, in_specs=[vmem] * 4 + [pl.BlockSpec(memory_sp...  7.76 us
    pallas_call x1, Pallas kernels, make_second(): pl.pallas_call(second_kernel, grid=(STEPS,), in_specs=[plane_spec(), whol...  5.06 us
  transfers between devices with their start and end apart: 26, of which 13 were waited for; matrix products, arithmetic and copies ran while one was open for 1% of the time, Pallas kernels for 17%

profile of v7, /device:TPU:0, one launch (start us, length us, event | category | flops | bytes accessed | tf_op | source)
XLA Modules:
  0.0 164.5 jit_solution(9975672803592743736)
XLA Ops:
  0.0 1.6 copy-done
  1.6 3.2 %pack.1 = (f32[6,192,128]{2,1,0:T(8,128)S(1)}, f32[6,16,16,128]{3,2,1,0:T(8,128)}, f32[6,16,16,128]{3,2,1,0:T(8,128)}) custom-call(f32[16,256,128]{2,1,0:T(8,128)S(1)} %bitcast.11), custom_call_target="tpu_custom_call" | custom-call | flops 4294967296 | bytes 6291456 | tf_op jit(solution)/shard_map/pack/pallas_call | solution.py:162
  4.8 2.0 %collective-permute-start.4 = (f32[6,192,128]{2,1,0:T(8,128)S(1)}, f32[6,192,128]{2,1,0:T(8,128)S(1)}, u32[]{:S(2)}, u32[]{:S(2)}) collective-permute-start(f32[6,192,128]{2,1,0:T(8,128)S(1)} %get-tuple-element.39), channel_id=1, source_target_pairs={{0,32},{1,33},{2,34},{3,35},{4,36},{5,37},{6,38},{7,39},{8,40},{9,... | collective-permute-start | bytes 1769480 | tf_op jit(solution)/shard_map/ppermute | solution.py:726
  9.0 1.6 collective-permute-start
  10.5 6.8 %collective-permute-start.1 = (f32[24,128]{1,0:T(8,128)S(1)}, f32[24,128]{1,0:T(8,128)S(1)}, u32[]{:S(2)}, u32[]{:S(2)}) collective-permute-start(f32[24,128]{1,0:T(8,128)S(1)} %reshape.29.refs_1_), channel_id=1, source_target_pairs={{0,31},{1,0},{2,1},{3,2},{4,3},{5,4},{6,5},{7,6},{8,7},{9,8},{10,9... | collective-permute-start | bytes 36872 | tf_op jit(solution)/shard_map/ppermute | solution.py:726
  17.4 1.5 collective-permute-done.refs_0_
  21.9 3.1 %side_x.1.part_ref = f32[16,256,128]{2,1,0:T(8,128)S(1)} custom-call(f32[16,256,128]{2,1,0:T(8,128)S(1)} %bitcast.13, f32[16,256,128]{2,1,0:T(8,128)} %collective-permute-done.5.mate_ref), custom_call_target="tpu_custom_call" | custom-call | flops 16777216 | bytes 6291456 | tf_op jit(solution)/shard_map/side_x/pallas_call | solution.py:229
  26.3 2.0 %collective-permute-start.7 = (f32[4,192,128]{2,1,0:T(8,128)}, f32[4,192,128]{2,1,0:T(8,128)}, u32[]{:S(2)}, u32[]{:S(2)}) collective-permute-start(f32[4,192,128]{2,1,0:T(8,128)} %get-tuple-element.52), channel_id=1, source_target_pairs={{0,33},{3,34},{4,37},{7,38},{8,41},{11,42},{12,45},{15,46},{16,49}... | collective-permute-start | bytes 1179656 | tf_op jit(solution)/shard_map/ppermute | solution.py:752
  28.3 8.2 %collective-permute-start.12 = (f32[6,16,16,128]{3,2,1,0:T(8,128)}, f32[6,16,16,128]{3,2,1,0:T(8,128)}, u32[]{:S(2)}, u32[]{:S(2)}) collective-permute-start(f32[6,16,16,128]{3,2,1,0:T(8,128)} %get-tuple-element.49), channel_id=1, source_target_pairs={{0,31},{1,0},{2,1},{3,2},{4,3},{5,4},{6,5},{7,6},{8,7},{9,8},{10,9... | collective-permute-start | bytes 2359304 | tf_op jit(solution)/shard_map/ppermute | solution.py:726
  37.7 1.5 collective-permute-start.13
  40.1 7.8 %prep.1 = (bf16[2,4096,128]{2,1,0:T(8,128)(2,1)S(1)}, f32[3,48,128]{2,1,0:T(8,128)S(1)}, f32[48,128]{1,0:T(8,128)S(1)}) custom-call(f32[104,128]{1,0:T(8,128)S(1)} %stack.13.parcel_ref.refs_0_, f32[104,128]{1,0:T(8,128)S(1)} %collective-permute-done.2.refs_1_, f32[104,128]{1,0:T(8,128)S(1)} %collective-permute-done.3.refs_2_.parcel_ref, ...), custom_call_target="tpu_custom_call" | custom-call | flops 134217728 | bytes 10485760 | tf_op jit(solution)/shard_map/prep/pallas_call | solution.py:439
  53.4 1.6 collective-permute-start.9
  55.0 1.7 %copy-done.7 = f32[16,256,128]{2,1,0:T(8,128)S(1)} copy-done((f32[16,256,128]{2,1,0:T(8,128)S(1)}, f32[16,256,128]{2,1,0:T(8,128)}, u32[]{:S(2)}) %copy-start.7) | copy-done | bytes 2097176
  56.8 4.3 %side_z.1.side_ref = f32[16,256,128]{2,1,0:T(8,128)S(1)} custom-call(f32[16,256,128]{2,1,0:T(8,128)S(1)} %bitcast.15, f32[16,256,128]{2,1,0:T(8,128)S(1)} %copy-done.7, f32[6,16,16,128]{3,2,1,0:T(8,128)} %collective-permute-done.11.low_ref, f32[6,16,16,128]{3,2,1,0:T(8,128)} %collective-permute-done.12.high_ref), custom_call_target="tpu_custom_call" | custom-call | flops 16777216 | bytes 8388608 | tf_op jit(solution)/shard_map/side_z/pallas_call | solution.py:254
  61.1 3.0 %collective-permute-done.9.refs_6_.rest_1_ = f32[3,48,128]{2,1,0:T(8,128)S(1)} collective-permute-done((f32[3,48,128]{2,1,0:T(8,128)S(1)}, f32[3,48,128]{2,1,0:T(8,128)S(1)}, u32[]{:S(2)}, u32[]{:S(2)}) %collective-permute-start.9) | collective-permute-done | bytes 73760 | tf_op jit(solution)/shard_map/ppermute | solution.py:726
  64.4 4.1 %first.1 = (f32[16,256,128]{2,1,0:T(8,128)S(1)}, f32[16,256,128]{2,1,0:T(8,128)S(1)}, f32[1632,128]{1,0:T(8,128)S(1)}, f32[1632,128]{1,0:T(8,128)S(1)}) custom-call(f32[16,256,128]{2,1,0:T(8,128)S(1)} %bitcast.16, f32[16,256,128]{2,1,0:T(8,128)S(1)} %side_z.1.side_ref, f32[16,256,128]{2,1,0:T(8,128)S(1)} %bitcast.18, ...), custom_call_target="tpu_custom_call" | custom-call | flops 16777216 | bytes 14680064 | tf_op jit(solution)/shard_map/first/pallas_call | solution.py:498
  68.7 8.2 %collective-permute-start.18 = (f32[1632,128]{1,0:T(8,128)S(1)}, f32[1632,128]{1,0:T(8,128)S(1)}, u32[]{:S(2)}, u32[]{:S(2)}) collective-permute-start(f32[1632,128]{1,0:T(8,128)S(1)} %get-tuple-element.57), channel_id=1, source_target_pairs={{0,31},{1,0},{2,1},{3,2},{4,3},{5,4},{6,5},{7,6},{8,7},{9,8},{10,9... | collective-permute-start | bytes 2506760 | tf_op jit(solution)/shard_map/ppermute | solution.py:726
  79.2 2.9 %side_again.1.part_ref = f32[16,256,128]{2,1,0:T(8,128)S(1)} custom-call(f32[16,256,128]{2,1,0:T(8,128)S(1)} %get-tuple-element.55.s_ref, f32[16,256,128]{2,1,0:T(8,128)S(1)} %collective-permute-done.16.mate_ref), custom_call_target="tpu_custom_call" | custom-call | flops 33554432 | bytes 6291456 | tf_op jit(solution)/shard_map/side_again/pallas_call | solution.py:281
  82.1 23.6 %collective-permute-done.10.mid_ref = f32[16,64,128]{2,1,0:T(8,128)S(1)} collective-permute-done((f32[16,64,128]{2,1,0:T(8,128)S(1)}, f32[16,64,128]{2,1,0:T(8,128)S(1)}, u32[]{:S(2)}, u32[]{:S(2)}) %collective-permute-start.10) | collective-permute-done | bytes 524320 | tf_op jit(solution)/shard_map/ppermute | solution.py:726
  105.7 4.8 %base.1.base_ref = f32[16,256,128]{2,1,0:T(8,128)S(1)} custom-call(f32[16,256,128]{2,1,0:T(8,128)S(1)} %bitcast.17, f32[16,64,128]{2,1,0:T(8,128)S(1)} %collective-permute-done.10.mid_ref, f32[16,256,128]{2,1,0:T(8,128)S(1)} %bitcast.19, f32[16,256,128]{2,1,0:T(8,128)S(1)} %bitcast.22, f32[16,256,128]{2,1,0:T(8,128)S(1)} %get-tuple-element.54.q_ref, ...), custom_call_target="tpu_custom_call" | custom-call | flops 33554432 | bytes 16777216 | tf_op jit(solution)/shard_map/base/pallas_call | solution.py:539
  110.6 5.1 %second.1 = (f32[16,256,128]{2,1,0:T(8,128)S(1)}, f32[128,128]{1,0:T(8,128)S(1)}) custom-call(f32[16,256,128]{2,1,0:T(8,128)S(1)} %base.1.base_ref, f32[1632,128]{1,0:T(8,128)S(1)} %collective-permute-done.17.low_ref, f32[1632,128]{1,0:T(8,128)S(1)} %collective-permute-done.18.high_ref, bf16[2,16,256,128]{3,2,1,0:T(8,128)(2,1)S(1)} %bitcast.20, ...), custom_call_target="tpu_custom_call" | custom-call | flops 134217728 | bytes 8388608 | tf_op jit(solution)/shard_map/second/pallas_call | solution.py:608
  117.0 2.5 %collective-permute-start.20 = (f32[128,128]{1,0:T(8,128)S(1)}, f32[128,128]{1,0:T(8,128)S(1)}, u32[]{:S(2)}, u32[]{:S(2)}) collective-permute-start(f32[128,128]{1,0:T(8,128)S(1)} %add.35), channel_id=1, source_target_pairs={{0,32},{1,33},{2,34},{3,35},{4,36},{5,37},{6,38},{7,39},{8,40},{9,... | collective-permute-start | bytes 196616 | tf_op jit(solution)/shard_map/ppermute | solution.py:777
  119.5 2.4 %collective-permute-done.20 = f32[128,128]{1,0:T(8,128)S(1)} collective-permute-done((f32[128,128]{1,0:T(8,128)S(1)}, f32[128,128]{1,0:T(8,128)S(1)}, u32[]{:S(2)}, u32[]{:S(2)}) %collective-permute-start.20) | collective-permute-done | bytes 65568 | tf_op jit(solution)/shard_map/ppermute | solution.py:777
  122.0 1.5 collective-permute-start.21
  123.5 4.0 %collective-permute-done.21 = f32[128,128]{1,0:T(8,128)S(1)} collective-permute-done((f32[128,128]{1,0:T(8,128)S(1)}, f32[128,128]{1,0:T(8,128)S(1)}, u32[]{:S(2)}, u32[]{:S(2)}) %collective-permute-start.21) | collective-permute-done | bytes 65568 | tf_op jit(solution)/shard_map/ppermute | solution.py:777
  127.8 4.3 %collective-permute-done.22 = f32[128,128]{1,0:T(8,128)S(1)} collective-permute-done((f32[128,128]{1,0:T(8,128)S(1)}, f32[128,128]{1,0:T(8,128)S(1)}, u32[]{:S(2)}, u32[]{:S(2)}) %collective-permute-start.22) | collective-permute-done | bytes 65568 | tf_op jit(solution)/shard_map/ppermute | solution.py:777
  132.1 2.2 %collective-permute-start.23 = (f32[128,128]{1,0:T(8,128)S(1)}, f32[128,128]{1,0:T(8,128)S(1)}, u32[]{:S(2)}, u32[]{:S(2)}) collective-permute-start(f32[128,128]{1,0:T(8,128)S(1)} %add.38), channel_id=1, source_target_pairs={{0,3},{1,2},{2,1},{3,0},{4,7},{5,6},{6,5},{7,4},{8,11},{9,10},{10,... | collective-permute-start | bytes 196616 | tf_op jit(solution)/shard_map/ppermute | solution.py:777
  134.3 3.3 %collective-permute-done.23 = f32[128,128]{1,0:T(8,128)S(1)} collective-permute-done((f32[128,128]{1,0:T(8,128)S(1)}, f32[128,128]{1,0:T(8,128)S(1)}, u32[]{:S(2)}, u32[]{:S(2)}) %collective-permute-start.23) | collective-permute-done | bytes 65568 | tf_op jit(solution)/shard_map/ppermute | solution.py:777
  137.7 4.3 %collective-permute-done.24 = f32[128,128]{1,0:T(8,128)S(1)} collective-permute-done((f32[128,128]{1,0:T(8,128)S(1)}, f32[128,128]{1,0:T(8,128)S(1)}, u32[]{:S(2)}, u32[]{:S(2)}) %collective-permute-start.24) | collective-permute-done | bytes 65568 | tf_op jit(solution)/shard_map/ppermute | solution.py:777
  142.0 2.1 %collective-permute-start.25 = (f32[128,128]{1,0:T(8,128)S(1)}, f32[128,128]{1,0:T(8,128)S(1)}, u32[]{:S(2)}, u32[]{:S(2)}) collective-permute-start(f32[128,128]{1,0:T(8,128)S(1)} %add.40), channel_id=1, source_target_pairs={{0,24},{1,25},{2,26},{3,27},{4,28},{5,29},{6,30},{7,31},{8,16},{9,... | collective-permute-start | bytes 196616 | tf_op jit(solution)/shard_map/ppermute | solution.py:777
  144.1 3.4 %collective-permute-done.25 = f32[128,128]{1,0:T(8,128)S(1)} collective-permute-done((f32[128,128]{1,0:T(8,128)S(1)}, f32[128,128]{1,0:T(8,128)S(1)}, u32[]{:S(2)}, u32[]{:S(2)}) %collective-permute-start.25) | collective-permute-done | bytes 65568 | tf_op jit(solution)/shard_map/ppermute | solution.py:777
  147.6 17.0 %turn.1 = f32[16,256,128]{2,1,0:T(8,128)} custom-call(f32[16,256,128]{2,1,0:T(8,128)S(1)} %get-tuple-element.61.second_ref, f32[128,128]{1,0:T(8,128)S(1)} %add_multiply_fusion.gram_ref), custom_call_target="tpu_custom_call" | custom-call | flops 268435456 | bytes 4194304 | tf_op jit(solution)/shard_map/turn/pallas_call | solution.py:703
  (81 shorter events, 18.6 us)
Async XLA Ops:
  0.0 21.9 %collective-permute-start.5 = (f32[16,256,128]{2,1,0:T(8,128)}, f32[16,256,128]{2,1,0:T(8,128)}, u32[]{:S(2)}, u32[]{:S(2)}) collective-permute-start(f32[16,256,128]{2,1,0:T(8,128)} %bitcast.10), channel_id=1, source_target_pairs={{0,64},{1,65},{2,66},{3,67},{4,68},{5,69},{6,70},{7,71},{8,72},{9,... | collective-permute-start | bytes 6291464 | tf_op jit(solution)/shard_map/ppermute | solution.py:726
  1.6 7.1 %copy-start.14 = (f32[4]{0:T(128)S(1)}, f32[4]{0:T(128)}, u32[]{:S(2)}) copy-start(f32[4]{0:T(128)} %param.9) | copy-start | bytes 52
  1.6 15.7 %copy-start.12 = (f32[16,16,16]{2,1,0:T(8,128)S(1)}, f32[16,16,16]{2,1,0:T(8,128)}, u32[]{:S(2)}) copy-start(f32[16,16,16]{2,1,0:T(8,128)} %param.6) | copy-start | bytes 49156
  1.6 17.4 %copy-start.1 = (f32[16,16,16,128]{3,2,1,0:T(8,128)S(1)}, f32[16,16,16,128]{3,2,1,0:T(8,128)}, u32[]{:S(2)}) copy-start(f32[16,16,16,128]{3,2,1,0:T(8,128)} %param.5) | copy-start | bytes 6291460
  4.8 21.5 %collective-permute-start.4 = (f32[6,192,128]{2,1,0:T(8,128)S(1)}, f32[6,192,128]{2,1,0:T(8,128)S(1)}, u32[]{:S(2)}, u32[]{:S(2)}) collective-permute-start(f32[6,192,128]{2,1,0:T(8,128)S(1)} %get-tuple-element.39), channel_id=1, source_target_pairs={{0,32},{1,33},{2,34},{3,35},{4,36},{5,37},{6,38},{7,39},{8,40},{9,... | collective-permute-start | bytes 1769480 | tf_op jit(solution)/shard_map/ppermute | solution.py:726
  9.0 10.0 %collective-permute-start = (f32[24,128]{1,0:T(8,128)S(1)}, f32[24,128]{1,0:T(8,128)S(1)}, u32[]{:S(2)}, u32[]{:S(2)}) collective-permute-start(f32[24,128]{1,0:T(8,128)S(1)} %reshape.29.refs_1_), channel_id=1, source_target_pairs={{0,1},{1,2},{2,3},{3,4},{4,5},{5,6},{6,7},{7,8},{8,9},{9,10},{10,1... | collective-permute-start | bytes 36872 | tf_op jit(solution)/shard_map/ppermute | solution.py:726
  10.5 8.4 %collective-permute-start.1 = (f32[24,128]{1,0:T(8,128)S(1)}, f32[24,128]{1,0:T(8,128)S(1)}, u32[]{:S(2)}, u32[]{:S(2)}) collective-permute-start(f32[24,128]{1,0:T(8,128)S(1)} %reshape.29.refs_1_), channel_id=1, source_target_pairs={{0,31},{1,0},{2,1},{3,2},{4,3},{5,4},{6,5},{7,6},{8,7},{9,8},{10,9... | collective-permute-start | bytes 36872 | tf_op jit(solution)/shard_map/ppermute | solution.py:726
  19.0 7.3 %collective-permute-start.3 = (f32[104,128]{1,0:T(8,128)S(1)}, f32[104,128]{1,0:T(8,128)S(1)}, u32[]{:S(2)}, u32[]{:S(2)}) collective-permute-start(f32[104,128]{1,0:T(8,128)S(1)} %stack.13.parcel_ref.refs_0_), channel_id=1, source_target_pairs={{0,32},{1,33},{2,34},{3,35},{4,36},{5,37},{6,38},{7,39},{8,40},{9,... | collective-permute-start | bytes 159752 | tf_op jit(solution)/shard_map/ppermute | solution.py:726
  26.3 23.0 %collective-permute-start.7 = (f32[4,192,128]{2,1,0:T(8,128)}, f32[4,192,128]{2,1,0:T(8,128)}, u32[]{:S(2)}, u32[]{:S(2)}) collective-permute-start(f32[4,192,128]{2,1,0:T(8,128)} %get-tuple-element.52), channel_id=1, source_target_pairs={{0,33},{3,34},{4,37},{7,38},{8,41},{11,42},{12,45},{15,46},{16,49}... | collective-permute-start | bytes 1179656 | tf_op jit(solution)/shard_map/ppermute | solution.py:752
  28.3 25.1 %collective-permute-start.11 = (f32[6,16,16,128]{3,2,1,0:T(8,128)}, f32[6,16,16,128]{3,2,1,0:T(8,128)}, u32[]{:S(2)}, u32[]{:S(2)}) collective-permute-start(f32[6,16,16,128]{3,2,1,0:T(8,128)} %get-tuple-element.48), channel_id=1, source_target_pairs={{0,1},{1,2},{2,3},{3,4},{4,5},{5,6},{6,7},{7,8},{8,9},{9,10},{10,1... | collective-permute-start | bytes 2359304 | tf_op jit(solution)/shard_map/ppermute | solution.py:726
  28.3 26.7 %collective-permute-start.12 = (f32[6,16,16,128]{3,2,1,0:T(8,128)}, f32[6,16,16,128]{3,2,1,0:T(8,128)}, u32[]{:S(2)}, u32[]{:S(2)}) collective-permute-start(f32[6,16,16,128]{3,2,1,0:T(8,128)} %get-tuple-element.49), channel_id=1, source_target_pairs={{0,31},{1,0},{2,1},{3,2},{4,3},{5,4},{6,5},{7,6},{8,7},{9,8},{10,9... | collective-permute-start | bytes 2359304 | tf_op jit(solution)/shard_map/ppermute | solution.py:726
  36.5 1.2 collective-permute-start.2
  36.5 3.7 %collective-permute-start.6 = (f32[104,128]{1,0:T(8,128)S(1)}, f32[104,128]{1,0:T(8,128)S(1)}, u32[]{:S(2)}, u32[]{:S(2)}) collective-permute-start(f32[104,128]{1,0:T(8,128)S(1)} %collective-permute-done.3.refs_2_.parcel_ref), channel_id=1, source_target_pairs={{0,64},{1,65},{2,66},{3,67},{4,68},{5,69},{6,70},{7,71},{8,72},{9,... | collective-permute-start | bytes 159752 | tf_op jit(solution)/shard_map/ppermute | solution.py:726
  37.7 26.4 %collective-permute-start.13 = (f32[6,192,128]{2,1,0:T(8,128)}, f32[6,192,128]{2,1,0:T(8,128)S(1)}, u32[]{:S(2)}, u32[]{:S(2)}) collective-permute-start(f32[6,192,128]{2,1,0:T(8,128)} %copy-done.8), channel_id=1, source_target_pairs={{0,32},{1,33},{2,34},{3,35},{4,36},{5,37},{6,38},{7,39},{8,40},{9,... | collective-permute-start | bytes 1769480 | tf_op jit(solution)/shard_map/ppermute | solution.py:726
  40.1 7.8 %copy-start.2 = (f32[4096,128]{1,0:T(8,128)}, f32[4096,128]{1,0:T(8,128)S(1)}, u32[]{:S(2)}) copy-start(f32[4096,128]{1,0:T(8,128)S(1)} %spread.2.refs_5_) | copy-start | bytes 6291460
  49.3 1.4 collective-permute-start.8
  49.3 14.8 %collective-permute-start.14 = (f32[4,192,128]{2,1,0:T(8,128)}, f32[4,192,128]{2,1,0:T(8,128)}, u32[]{:S(2)}, u32[]{:S(2)}) collective-permute-start(f32[4,192,128]{2,1,0:T(8,128)} %get-tuple-element.52), channel_id=1, source_target_pairs={{1,33},{2,34},{5,37},{6,38},{9,41},{10,42},{13,45},{14,46},{17,49}... | collective-permute-start | bytes 1179656 | tf_op jit(solution)/shard_map/ppermute | solution.py:760
  50.7 13.7 %collective-permute-start.15 = (f32[4,192,128]{2,1,0:T(8,128)}, f32[4,192,128]{2,1,0:T(8,128)}, u32[]{:S(2)}, u32[]{:S(2)}) collective-permute-start(f32[4,192,128]{2,1,0:T(8,128)} %collective-permute-done.7), channel_id=1, source_target_pairs={{1,0},{2,3},{5,4},{6,7},{9,8},{10,11},{13,12},{14,15},{17,16},{18,... | collective-permute-start | bytes 1179656 | tf_op jit(solution)/shard_map/ppermute | solution.py:759
  53.4 10.7 %collective-permute-start.9 = (f32[3,48,128]{2,1,0:T(8,128)S(1)}, f32[3,48,128]{2,1,0:T(8,128)S(1)}, u32[]{:S(2)}, u32[]{:S(2)}) collective-permute-start(f32[3,48,128]{2,1,0:T(8,128)S(1)} %add.32.refs_5_.rest_0_), channel_id=1, source_target_pairs={{0,32},{1,33},{2,34},{3,35},{4,36},{5,37},{6,38},{7,39},{8,40},{9,... | collective-permute-start | bytes 221192 | tf_op jit(solution)/shard_map/ppermute | solution.py:726
  55.0 9.4 %copy-start.3 = (f32[4096,128]{1,0:T(8,128)S(1)}, f32[4096,128]{1,0:T(8,128)}, u32[]{:S(2)}) copy-start(f32[4096,128]{1,0:T(8,128)} %copy-done.2) | copy-start | bytes 6291460
  64.4 12.4 %copy-start.10 = (f32[16,64,128]{2,1,0:T(8,128)S(1)}, f32[16,64,128]{2,1,0:T(8,128)}, u32[]{:S(2)}) copy-start(f32[16,64,128]{2,1,0:T(8,128)} %copy-done.9) | copy-start | bytes 1572868
  68.5 10.6 %collective-permute-start.16 = (f32[16,256,128]{2,1,0:T(8,128)S(1)}, f32[16,256,128]{2,1,0:T(8,128)S(1)}, u32[]{:S(2)}, u32[]{:S(2)}) collective-permute-start(f32[16,256,128]{2,1,0:T(8,128)S(1)} %get-tuple-element.55.s_ref), channel_id=1, source_target_pairs={{0,64},{1,65},{2,66},{3,67},{4,68},{5,69},{6,70},{7,71},{8,72},{9,... | collective-permute-start | bytes 6291464 | tf_op jit(solution)/shard_map/ppermute | solution.py:726
  68.6 41.9 %collective-permute-start.17 = (f32[1632,128]{1,0:T(8,128)S(1)}, f32[1632,128]{1,0:T(8,128)S(1)}, u32[]{:S(2)}, u32[]{:S(2)}) collective-permute-start(f32[1632,128]{1,0:T(8,128)S(1)} %get-tuple-element.56), channel_id=1, source_target_pairs={{0,1},{1,2},{2,3},{3,4},{4,5},{5,6},{6,7},{7,8},{8,9},{9,10},{10,1... | collective-permute-start | bytes 2506760 | tf_op jit(solution)/shard_map/ppermute | solution.py:726
  68.7 41.9 %collective-permute-start.18 = (f32[1632,128]{1,0:T(8,128)S(1)}, f32[1632,128]{1,0:T(8,128)S(1)}, u32[]{:S(2)}, u32[]{:S(2)}) collective-permute-start(f32[1632,128]{1,0:T(8,128)S(1)} %get-tuple-element.57), channel_id=1, source_target_pairs={{0,31},{1,0},{2,1},{3,2},{4,3},{5,4},{6,5},{7,6},{8,7},{9,8},{10,9... | collective-permute-start | bytes 2506760 | tf_op jit(solution)/shard_map/ppermute | solution.py:726
  76.9 28.9 %collective-permute-start.10 = (f32[16,64,128]{2,1,0:T(8,128)S(1)}, f32[16,64,128]{2,1,0:T(8,128)S(1)}, u32[]{:S(2)}, u32[]{:S(2)}) collective-permute-start(f32[16,64,128]{2,1,0:T(8,128)S(1)} %copy-done.10), channel_id=1, source_target_pairs={{0,32},{1,33},{2,34},{3,35},{4,36},{5,37},{6,38},{7,39},{8,40},{9,... | collective-permute-start | bytes 1572872 | tf_op jit(solution)/shard_map/ppermute | solution.py:726
  115.7 1.3 collective-permute-start.19
  117.0 5.0 %collective-permute-start.20 = (f32[128,128]{1,0:T(8,128)S(1)}, f32[128,128]{1,0:T(8,128)S(1)}, u32[]{:S(2)}, u32[]{:S(2)}) collective-permute-start(f32[128,128]{1,0:T(8,128)S(1)} %add.35), channel_id=1, source_target_pairs={{0,32},{1,33},{2,34},{3,35},{4,36},{5,37},{6,38},{7,39},{8,40},{9,... | collective-permute-start | bytes 196616 | tf_op jit(solution)/shard_map/ppermute | solution.py:777
  122.0 5.6 %collective-permute-start.21 = (f32[128,128]{1,0:T(8,128)S(1)}, f32[128,128]{1,0:T(8,128)S(1)}, u32[]{:S(2)}, u32[]{:S(2)}) collective-permute-start(f32[128,128]{1,0:T(8,128)S(1)} %add.36), channel_id=1, source_target_pairs={{0,36},{1,37},{2,38},{3,39},{4,32},{5,33},{6,34},{7,35},{8,44},{9,... | collective-permute-start | bytes 196616 | tf_op jit(solution)/shard_map/ppermute | solution.py:777
  127.5 4.5 %collective-permute-start.22 = (f32[128,128]{1,0:T(8,128)S(1)}, f32[128,128]{1,0:T(8,128)S(1)}, u32[]{:S(2)}, u32[]{:S(2)}) collective-permute-start(f32[128,128]{1,0:T(8,128)S(1)} %add.37), channel_id=1, source_target_pairs={{0,1},{1,0},{2,3},{3,2},{4,5},{5,4},{6,7},{7,6},{8,9},{9,8},{10,11... | collective-permute-start | bytes 196616 | tf_op jit(solution)/shard_map/ppermute | solution.py:777
  132.1 5.6 %collective-permute-start.23 = (f32[128,128]{1,0:T(8,128)S(1)}, f32[128,128]{1,0:T(8,128)S(1)}, u32[]{:S(2)}, u32[]{:S(2)}) collective-permute-start(f32[128,128]{1,0:T(8,128)S(1)} %add.38), channel_id=1, source_target_pairs={{0,3},{1,2},{2,1},{3,0},{4,7},{5,6},{6,5},{7,4},{8,11},{9,10},{10,... | collective-permute-start | bytes 196616 | tf_op jit(solution)/shard_map/ppermute | solution.py:777
  137.7 4.3 %collective-permute-start.24 = (f32[128,128]{1,0:T(8,128)S(1)}, f32[128,128]{1,0:T(8,128)S(1)}, u32[]{:S(2)}, u32[]{:S(2)}) collective-permute-start(f32[128,128]{1,0:T(8,128)S(1)} %add.39), channel_id=1, source_target_pairs={{0,8},{1,9},{2,10},{3,11},{4,12},{5,13},{6,14},{7,15},{8,0},{9,1},... | collective-permute-start | bytes 196616 | tf_op jit(solution)/shard_map/ppermute | solution.py:777
  142.0 5.6 %collective-permute-start.25 = (f32[128,128]{1,0:T(8,128)S(1)}, f32[128,128]{1,0:T(8,128)S(1)}, u32[]{:S(2)}, u32[]{:S(2)}) collective-permute-start(f32[128,128]{1,0:T(8,128)S(1)} %add.40), channel_id=1, source_target_pairs={{0,24},{1,25},{2,26},{3,27},{4,28},{5,29},{6,30},{7,31},{8,16},{9,... | collective-permute-start | bytes 196616 | tf_op jit(solution)/shard_map/ppermute | solution.py:777
  (9 other events, 24.8 us)

commit v8 on v7

--- a/solution.py
+++ b/solution.py
@@ -73,7 +73,11 @@
 B = 4
 STEPS = C // B
 N = 2
-CUTS = (0, 6, 12, 16)
+FIRST = 6
+MIDDLE = 10
+EDGE = 192
+MID = 64
+MID_START = (MIDDLE - FIRST) * EDGE
 
 
 def stride_rows(z):
@@ -96,33 +100,29 @@
     return pl.BlockSpec((rows, S), lambda i: (0, 0))
 
 
+def edge_spec(start, stop):
+    return pl.BlockSpec((N, EDGE, S), lambda i: (jnp.clip(i - start // N, 0, (stop - start) // N - 1), 0, 0))
+
+
 def edge_specs():
-    def spec(start, stop):
-        return pl.BlockSpec((N, 192, S), lambda i: (jnp.clip(i - start // N, 0, (stop - start) // N - 1), 0, 0))
-
-    return [spec(start, stop) for start, stop in zip(CUTS, CUTS[1:])]
-
-
-def for_piece(pieces, body, inner_ref=None):
+    return [edge_spec(0, FIRST), edge_spec(FIRST, C), edge_spec(MIDDLE, C)]
+
+
+def for_piece(edges, inner_ref, body):
     step = pl.program_id(0)
-    for j, (start, stop) in enumerate(zip(CUTS, CUTS[1:])):
-        here = (step >= start // N) & (step < stop // N)
-        if inner_ref is None or j < len(CUTS) - 2:
-
-            @pl.when(here)
-            def _(j=j):
-                body(pieces[j])
-
-        else:
-            inner = inner_ref[0] == 1
-
-            @pl.when(here & inner)
-            def _(j=j):
-                body(pieces[j])
-
-            @pl.when(here & jnp.logical_not(inner))
-            def _(j=j):
-                body(pieces[j + 1])
+    direct = (inner_ref[0] == 1) | (step < MIDDLE // N)
+
+    @pl.when(step < FIRST // N)
+    def _():
+        body(edges[0])
+
+    @pl.when((step >= FIRST // N) & direct)
+    def _():
+        body(edges[1])
+
+    @pl.when(jnp.logical_not(direct))
+    def _():
+        body(edges[2])
 
 
 SCALARS = pl.BlockSpec(memory_space=pltpu.SMEM)
@@ -131,7 +131,7 @@
 HALO_ROWS = H * ROWS
 MESSAGE = sds((HALO_ROWS + 2 * NEAR, S))
 HALO = sds((H, C, C, S))
-EDGES = [sds((stop - start, 192, S)) for start, stop in zip(CUTS, CUTS[1:])]
+EDGES = [sds((FIRST, EDGE, S)), sds((C - FIRST, EDGE, S)), sds((C - MIDDLE, EDGE, S))]
 
 
 def halo_rows(x, z):
@@ -148,7 +148,7 @@
 
 
 def pack_kernel(s_ref, edge_ref, head_ref, tail_ref):
-    @pl.when(pl.program_id(0) < CUTS[1] // N)
+    @pl.when(pl.program_id(0) < FIRST // N)
     def _():
         pack_edges(s_ref, edge_ref)
 
@@ -171,22 +171,42 @@
     )(s)
 
 
-def pack_rest_kernel(s_ref, two_ref, three_ref, mid_ref):
-    for_piece([None, two_ref, three_ref], lambda out_ref: out_ref is None or pack_edges(s_ref, out_ref))
+def pack_rest_kernel(s_ref, inner_ref, message_ref, relay_ref, mid_ref):
+    step = pl.program_id(0)
+    inner = inner_ref[0] == 1
     mid_ref[...] = s_ref[:, 96:160, :]
 
-
-def pack_rest(s):
-    return pl.pallas_call(
+    @pl.when(step >= MIDDLE // N)
+    def _():
+        pack_edges(s_ref, relay_ref)
+
+    @pl.when((step >= FIRST // N) & (inner | (step < MIDDLE // N)))
+    def _():
+        for p in range(N):
+            row = pl.multiple_of((step * N + p - FIRST) * EDGE, MID)
+            message_ref[pl.ds(row, 96), :] = s_ref[p, 0:96, :]
+            message_ref[pl.ds(row + 96, 96), :] = s_ref[p, 160:256, :]
+
+    @pl.when(jnp.logical_not(inner))
+    def _():
+        for p in range(N):
+            row = pl.multiple_of(MID_START + (step * N + p) * MID, MID)
+            message_ref[pl.ds(row, MID), :] = s_ref[p, 96:160, :]
+
+
+def pack_rest(s, inner):
+    rows = (C - FIRST) * EDGE
+    message, relay, mid = pl.pallas_call(
         pack_rest_kernel,
         grid=(C // N,),
-        in_specs=[plane_spec(ROWS, N)],
-        out_specs=edge_specs()[1:] + [plane_spec(64, N)],
-        out_shape=EDGES[1:] + [sds((C, 64, S))],
+        in_specs=[plane_spec(ROWS, N), SCALARS],
+        out_specs=[whole(rows), edge_spec(MIDDLE, C), plane_spec(MID, N)],
+        out_shape=[sds((rows, S)), EDGES[2], sds((C, MID, S))],
         compiler_params=params(12),
         cost_estimate=cost(1 << 31, 4 << 20),
         name="pack_rest",
-    )(s)
+    )(s, inner)
+    return message, relay, mid
 
 
 def stack_kernel(*refs):
@@ -462,7 +482,7 @@
 
 
 def first_kernel(s_ref, side_ref, vb_ref, *refs):
-    inner_ref, part_ref, mate_ref, q_ref, mix_ref, head_ref, tail_ref = refs[4:]
+    inner_ref, part_ref, mate_ref, q_ref, mix_ref, head_ref, tail_ref = refs[3:]
     step = pl.program_id(0)
 
     @pl.when(step == 0)
@@ -490,7 +510,7 @@
                 head_ref[rows, :] = mix_ref[p, stride_rows(z), :]
                 tail_ref[rows, :] = mix_ref[p, stride_rows(C - H + z), :]
 
-    for_piece(refs[:4], planes, inner_ref)
+    for_piece(refs[:3], inner_ref, planes)
 
 
 def make_first(s, side_part, vb, edges, inner, part, part_mate):
@@ -498,7 +518,7 @@
     return pl.pallas_call(
         first_kernel,
         grid=(C // N,),
-        in_specs=[plane_spec(ROWS, N)] * 3 + edge_specs() + edge_specs()[-1:] + [SCALARS] + [shares] * 2,
+        in_specs=[plane_spec(ROWS, N)] * 3 + edge_specs() + [SCALARS] + [shares] * 2,
         out_specs=[plane_spec(ROWS, N), plane_spec(ROWS, N), whole(MESSAGE.shape[0]), whole(MESSAGE.shape[0])],
         out_shape=[FULL, FULL, MESSAGE, MESSAGE],
         compiler_params=params(16),
@@ -508,7 +528,18 @@
 
 
 def base_kernel(s_ref, mid_ref, vb_ref, vb_mate_ref, q_ref, side_ref, part_ref, *refs):
-    inner_ref, out_ref = refs[4:]
+    inner_ref, message_ref, out_ref, middle_ref = refs[3:]
+    step = pl.program_id(0)
+    inner = inner_ref[0] == 1
+
+    @pl.when(inner)
+    def _():
+        middle_ref[...] = mid_ref[...]
+
+    @pl.when(jnp.logical_not(inner))
+    def _():
+        for p in range(N):
+            middle_ref[p] = message_ref[pl.ds(pl.multiple_of(MID_START + (step * N + p) * MID, MID), MID), :]
 
     def planes(edge_ref):
         for p in range(N):
@@ -518,7 +549,7 @@
                     if y < H:
                         return edge_ref[p, halves(y, half), :]
                     if y < C - H:
-                        return mid_ref[p, halves(y - H, half), :]
+                        return middle_ref[p, halves(y - H, half), :]
                     return edge_ref[p, halves(y - 4, half), :]
 
                 ring = [s_ref[p, halves(y, half), :] for y in range(C)] + [other(y) for y in range(C)]
@@ -532,24 +563,24 @@
                     total = total + vb_ref[p, rows, :] * (side_ref[p, rows, :] + q[y])
                     out_ref[p, rows, :] = 2.0 * (total + part_ref[p, rows, :]) - ring[y]
 
-    for_piece(refs[:4], planes, inner_ref)
+    for_piece(refs[:3], inner_ref, planes)
 
 
 def make_base(s, mid, vb, vb_mate, q, side_part, part, edges, inner):
     return pl.pallas_call(
         base_kernel,
         grid=(C // N,),
-        in_specs=[plane_spec(ROWS, N), plane_spec(64, N)]
+        in_specs=[plane_spec(ROWS, N), plane_spec(MID, N)]
         + [plane_spec(ROWS, N)] * 5
         + edge_specs()
-        + edge_specs()[-1:]
-        + [SCALARS],
+        + [SCALARS, whole((C - FIRST) * EDGE)],
         out_specs=plane_spec(ROWS, N),
         out_shape=FULL,
+        scratch_shapes=[pltpu.VMEM((N, MID, S), F32)],
         compiler_params=params(16),
         cost_estimate=cost(1 << 25, 16 << 20),
         name="base",
-    )(s, mid, vb, vb_mate, q, side_part, part, *edges, inner)
+    )(s, mid, vb, vb_mate, q, side_part, part, *edges, inner, edges[1].reshape(-1, S))
 
 
 def second_kernel(base_ref, low_ref, high_ref, gg_high_ref, gg_low_ref, *rest):
@@ -745,29 +776,28 @@
     parcel_y = send(parcel, over_y)
     parcel_x = send(parcel, over_x)
     low, high = send(tail, 0, 1), send(head, 0, -1)
-    two_edge, three_edge, mid = pack_rest(s)
+    message, relay, mid = pack_rest(s, inner)
     vb = spread(parcel)
     beside = side_x(s, mate)
-    parcel_y, one_edge, two_edge, three_edge, beside = barrier((parcel_y, one_edge, two_edge, three_edge, beside))
-    relayed = lax.ppermute(three_edge, AXES, [(d, d ^ over_y ^ 1) for d in outer_ones])
-    two_edge = send(two_edge, over_y)
+    parcel_y, one_edge, message, relay, beside = barrier((parcel_y, one_edge, message, relay, beside))
+    relayed = lax.ppermute(relay, AXES, [(d, d ^ over_y ^ 1) for d in outer_ones])
+    message = send(message, over_y)
     parcel_xy = send(parcel_y, over_x)
     corner = jnp.stack([gx * C, gy * C]).astype(jnp.int32)
     gg, part, energy = prep([parcel, parcel_x, parcel_y, parcel_xy], corner, vb, s)
 
-    part, relayed, three_edge = barrier((part, relayed, three_edge))
+    part, relayed = barrier((part, relayed))
     relayed = lax.ppermute(relayed, AXES, [(d, d ^ 1) for d in inner_ones])
-    three_edge = lax.ppermute(three_edge, AXES, [(d, d ^ over_y) for d in inner_ones])
     part = part + send(part, over_x)
     part_mate = send(part, over_y)
     side_part = side_z(s, beside, low, high)
-    edges = [one_edge, two_edge, three_edge, relayed]
+    edges = [one_edge, message.reshape(C - FIRST, EDGE, S), relayed]
     vb = vb.reshape(C, ROWS, S)
     q, mix, head, tail = make_first(s, side_part, vb, edges, inner, part, part_mate)
     low, high = send(tail, 0, 1), send(head, 0, -1)
     mate = send(mix, over_x)
     mid, part_mate = barrier((mid, part_mate))
-    mid = send(mid, over_y)
+    mid = lax.ppermute(mid, AXES, [(d, d ^ over_y) for d in inner_ones])
     vb_mate = spread(parcel_y).reshape(C, ROWS, S)
     part_two = side_again(mix, mate)
     base = make_base(s, mid, vb, vb_mate, q, side_part, part_two, edges, inner)

time: 165 us -> 154 us (0.933)
  local copies, waits for them, and re-layouts: 9.89 us -> 5 us
  Pallas kernels: 54.8 us -> 52.1 us
  starting transfers between devices: 45.7 us -> 43.6 us
  waiting for transfers between devices: 53.6 us -> 51.7 us
    unnamed x31 -> x25, local copies, waits for them, and re-layouts: 8.49 us -> 4.56 us
    ppermute x16 -> x15, starting transfers between devices: 32.1 us -> 28.7 us  [send(): return lax.ppermute(value, AXES, [(d, target(d)) for d in range(count)])]
    pallas_call x1, Pallas kernels: 4.1 us -> 2.15 us  [make_first(): pl.pallas_call(first_kernel, grid=(C // N,), in_specs=[plane_spec(ROWS, N...]
    pallas_call x1, Pallas kernels: 4.8 us -> 2.95 us  [make_base(): pl.pallas_call(base_kernel, grid=(C // N,), in_specs=[plane_spec(ROWS, N)...]
    ppermute x16 -> x15, waiting for transfers between devices: 30.3 us -> 30.3 us  [send(): return lax.ppermute(value, AXES, [(d, target(d)) for d in range(count)])]
  transfers between devices with their start and end apart: 26 -> 25, of which waited for: 13 -> 14; matrix products, arithmetic and copies ran while one was open for 1% -> 0% of each run, Pallas kernels for 17% -> 18%
where the time goes in v8:
time: 154 us; the launch traced here: 153 us
  Pallas kernels  52.1 us (34%)
  waiting for transfers between devices  51.7 us (34%)
  starting transfers between devices  43.6 us (28%)
  local copies, waits for them, and re-layouts  5 us (3%)
    ppermute x15, waiting for transfers between devices, send(): return lax.ppermute(value, AXES, [(d, target(d)) for d in range(count)])  30.3 us
    ppermute x15, starting transfers between devices, send(): return lax.ppermute(value, AXES, [(d, target(d)) for d in range(count)])  28.7 us
    ppermute x7, waiting for transfers between devices, per_device(): lax.ppermute(gram, AXES, [(d, d ^ flip) for d in range(count)])  21.5 us
    pallas_call x1, Pallas kernels, turn(): pl.pallas_call(turn_kernel, grid=(STEPS,), in_specs=[plane_spec(), whole(...  16.9 us
    ppermute x7, starting transfers between devices, per_device(): lax.ppermute(gram, AXES, [(d, d ^ flip) for d in range(count)])  10.1 us
    pallas_call x1, Pallas kernels, prep(): pl.pallas_call(prep_kernel, in_specs=[vmem] * 4 + [pl.BlockSpec(memory_sp...  7.8 us
    pallas_call x1, Pallas kernels, make_second(): pl.pallas_call(second_kernel, grid=(STEPS,), in_specs=[plane_spec(), whol...  4.92 us
    unnamed x25, local copies, waits for them, and re-layouts  4.56 us
  transfers between devices with their start and end apart: 25, of which 14 were waited for; matrix products, arithmetic and copies ran while one was open for 0% of the time, Pallas kernels for 18%

profile of v8, /device:TPU:0, one launch (start us, length us, event | category | flops | bytes accessed | tf_op | source)
XLA Modules:
  0.0 153.0 jit_solution(9217570003445077705)
XLA Ops:
  0.0 1.6 %copy-done = f32[16,16,16,128]{3,2,1,0:T(8,128)S(1)} copy-done((f32[16,16,16,128]{3,2,1,0:T(8,128)S(1)}, f32[16,16,16,128]{3,2,1,0:T(8,128)}, u32[]{:S(2)}) %copy-start) | copy-done | bytes 2097176
  1.6 3.4 %pack.1 = (f32[6,192,128]{2,1,0:T(8,128)}, f32[6,16,16,128]{3,2,1,0:T(8,128)}, f32[6,16,16,128]{3,2,1,0:T(8,128)}) custom-call(f32[16,256,128]{2,1,0:T(8,128)S(1)} %bitcast.12), custom_call_target="tpu_custom_call" | custom-call | flops 4294967296 | bytes 6291456 | tf_op jit(solution)/shard_map/pack/pallas_call | solution.py:162
  5.0 2.0 %collective-permute-start.4 = (f32[6,192,128]{2,1,0:T(8,128)}, f32[6,192,128]{2,1,0:T(8,128)S(1)}, u32[]{:S(2)}, u32[]{:S(2)}) collective-permute-start(f32[6,192,128]{2,1,0:T(8,128)} %get-tuple-element.38), channel_id=1, source_target_pairs={{0,32},{1,33},{2,34},{3,35},{4,36},{5,37},{6,38},{7,39},{8,40},{9,... | collective-permute-start | bytes 1769480 | tf_op jit(solution)/shard_map/ppermute | solution.py:757
  7.5 1.6 %collective-permute-start = (f32[24,128]{1,0:T(8,128)S(1)}, f32[24,128]{1,0:T(8,128)S(1)}, u32[]{:S(2)}, u32[]{:S(2)}) collective-permute-start(f32[24,128]{1,0:T(8,128)S(1)} %reshape.33.refs_1_), channel_id=1, source_target_pairs={{0,1},{1,2},{2,3},{3,4},{4,5},{5,6},{6,7},{7,8},{8,9},{9,10},{10,1... | collective-permute-start | bytes 36872 | tf_op jit(solution)/shard_map/ppermute | solution.py:757
  9.1 6.8 %collective-permute-start.1 = (f32[24,128]{1,0:T(8,128)S(1)}, f32[24,128]{1,0:T(8,128)S(1)}, u32[]{:S(2)}, u32[]{:S(2)}) collective-permute-start(f32[24,128]{1,0:T(8,128)S(1)} %reshape.33.refs_1_), channel_id=1, source_target_pairs={{0,31},{1,0},{2,1},{3,2},{4,3},{5,4},{6,5},{7,6},{8,7},{9,8},{10,9... | collective-permute-start | bytes 36872 | tf_op jit(solution)/shard_map/ppermute | solution.py:757
  16.0 1.5 collective-permute-done.refs_0_
  17.6 2.1 %pack_rest.1 = (f32[1920,128]{1,0:T(8,128)}, f32[6,192,128]{2,1,0:T(8,128)}, f32[16,64,128]{2,1,0:T(8,128)S(1)}) custom-call(f32[16,256,128]{2,1,0:T(8,128)S(1)} %bitcast.13, s32[1]{0:T(128)} %bitcast.1.inner_ref.refs_3_), custom_call_target="tpu_custom_call" | custom-call | flops 2147483648 | bytes 4194304 | tf_op jit(solution)/shard_map/pack_rest/pallas_call | solution.py:199
  20.5 3.1 %side_x.1.part_ref = f32[16,256,128]{2,1,0:T(8,128)S(1)} custom-call(f32[16,256,128]{2,1,0:T(8,128)S(1)} %bitcast.14, f32[16,256,128]{2,1,0:T(8,128)} %collective-permute-done.5.mate_ref), custom_call_target="tpu_custom_call" | custom-call | flops 16777216 | bytes 6291456 | tf_op jit(solution)/shard_map/side_x/pallas_call | solution.py:249
  23.6 1.3 copy-done.2
  25.7 2.9 %collective-permute-start.7 = (f32[6,192,128]{2,1,0:T(8,128)}, f32[6,192,128]{2,1,0:T(8,128)}, u32[]{:S(2)}, u32[]{:S(2)}) collective-permute-start(f32[6,192,128]{2,1,0:T(8,128)} %get-tuple-element.43), channel_id=1, source_target_pairs={{0,33},{3,34},{4,37},{7,38},{8,41},{11,42},{12,45},{15,46},{16,49}... | collective-permute-start | bytes 1769480 | tf_op jit(solution)/shard_map/ppermute | solution.py:783
  29.8 7.8 %collective-permute-start.12 = (f32[6,16,16,128]{3,2,1,0:T(8,128)}, f32[6,16,16,128]{3,2,1,0:T(8,128)}, u32[]{:S(2)}, u32[]{:S(2)}) collective-permute-start(f32[6,16,16,128]{3,2,1,0:T(8,128)} %get-tuple-element.48), channel_id=1, source_target_pairs={{0,31},{1,0},{2,1},{3,2},{4,3},{5,4},{6,5},{7,6},{8,7},{9,8},{10,9... | collective-permute-start | bytes 2359304 | tf_op jit(solution)/shard_map/ppermute | solution.py:757
  40.1 7.8 %prep.1 = (bf16[2,4096,128]{2,1,0:T(8,128)(2,1)S(1)}, f32[3,48,128]{2,1,0:T(8,128)S(1)}, f32[48,128]{1,0:T(8,128)S(1)}) custom-call(f32[104,128]{1,0:T(8,128)S(1)} %stack.13.parcel_ref.refs_0_, f32[104,128]{1,0:T(8,128)S(1)} %collective-permute-done.2.refs_1_, f32[104,128]{1,0:T(8,128)S(1)} %collective-permute-done.3.refs_2_.parcel_ref, ...), custom_call_target="tpu_custom_call" | custom-call | flops 134217728 | bytes 10485760 | tf_op jit(solution)/shard_map/prep/pallas_call | solution.py:459
  47.9 1.3 collective-permute-start.14
  51.4 6.0 %collective-permute-done.11.low_ref = f32[6,16,16,128]{3,2,1,0:T(8,128)} collective-permute-done((f32[6,16,16,128]{3,2,1,0:T(8,128)}, f32[6,16,16,128]{3,2,1,0:T(8,128)}, u32[]{:S(2)}, u32[]{:S(2)}) %collective-permute-start.11) | collective-permute-done | bytes 786464 | tf_op jit(solution)/shard_map/ppermute | solution.py:757
  57.4 4.2 %side_z.1.side_ref = f32[16,256,128]{2,1,0:T(8,128)S(1)} custom-call(f32[16,256,128]{2,1,0:T(8,128)S(1)} %bitcast.16, f32[16,256,128]{2,1,0:T(8,128)S(1)} %copy-done.3, f32[6,16,16,128]{3,2,1,0:T(8,128)} %collective-permute-done.11.low_ref, f32[6,16,16,128]{3,2,1,0:T(8,128)} %collective-permute-done.12.high_ref), custom_call_target="tpu_custom_call" | custom-call | flops 16777216 | bytes 8388608 | tf_op jit(solution)/shard_map/side_z/pallas_call | solution.py:274
  61.6 8.7 %collective-permute-done.9.refs_5_.rest_1_ = f32[3,48,128]{2,1,0:T(8,128)S(1)} collective-permute-done((f32[3,48,128]{2,1,0:T(8,128)S(1)}, f32[3,48,128]{2,1,0:T(8,128)S(1)}, u32[]{:S(2)}, u32[]{:S(2)}) %collective-permute-start.9) | collective-permute-done | bytes 73760 | tf_op jit(solution)/shard_map/ppermute | solution.py:757
  70.4 2.2 %first.1 = (f32[16,256,128]{2,1,0:T(8,128)S(1)}, f32[16,256,128]{2,1,0:T(8,128)S(1)}, f32[1632,128]{1,0:T(8,128)S(1)}, f32[1632,128]{1,0:T(8,128)S(1)}) custom-call(f32[16,256,128]{2,1,0:T(8,128)S(1)} %bitcast.17, f32[16,256,128]{2,1,0:T(8,128)S(1)} %side_z.1.side_ref, f32[16,256,128]{2,1,0:T(8,128)S(1)} %bitcast.19, f32[6,192,128]{2,1,0:T(8,128)S(1)} %copy-done.5, ...), custom_call_target="tpu_custom_call" | custom-call | flops 16777216 | bytes 14680064 | tf_op jit(solution)/shard_map/first/pallas_call | solution.py:518
  72.7 7.7 %collective-permute-start.17 = (f32[1632,128]{1,0:T(8,128)S(1)}, f32[1632,128]{1,0:T(8,128)S(1)}, u32[]{:S(2)}, u32[]{:S(2)}) collective-permute-start(f32[1632,128]{1,0:T(8,128)S(1)} %get-tuple-element.55), channel_id=1, source_target_pairs={{0,31},{1,0},{2,1},{3,2},{4,3},{5,4},{6,5},{7,6},{8,7},{9,8},{10,9... | collective-permute-start | bytes 2506760 | tf_op jit(solution)/shard_map/ppermute | solution.py:757
  81.9 2.9 %side_again.1.part_ref = f32[16,256,128]{2,1,0:T(8,128)S(1)} custom-call(f32[16,256,128]{2,1,0:T(8,128)S(1)} %get-tuple-element.53.s_ref, f32[16,256,128]{2,1,0:T(8,128)S(1)} %collective-permute-done.15.mate_ref), custom_call_target="tpu_custom_call" | custom-call | flops 33554432 | bytes 6291456 | tf_op jit(solution)/shard_map/side_again/pallas_call | solution.py:301
  84.9 3.0 %base.1.base_ref = f32[16,256,128]{2,1,0:T(8,128)S(1)} custom-call(f32[16,256,128]{2,1,0:T(8,128)S(1)} %bitcast.18, f32[16,64,128]{2,1,0:T(8,128)S(1)} %collective-permute-done.10.mid_ref, f32[16,256,128]{2,1,0:T(8,128)S(1)} %bitcast.20, f32[16,256,128]{2,1,0:T(8,128)S(1)} %bitcast.25, f32[16,256,128]{2,1,0:T(8,128)S(1)} %get-tuple-element.52.q_ref, ...), custom_call_target="tpu_custom_call" | custom-call | flops 33554432 | bytes 16777216 | tf_op jit(solution)/shard_map/base/pallas_call | solution.py:570
  87.9 11.6 %collective-permute-done.16.low_ref = f32[1632,128]{1,0:T(8,128)S(1)} collective-permute-done((f32[1632,128]{1,0:T(8,128)S(1)}, f32[1632,128]{1,0:T(8,128)S(1)}, u32[]{:S(2)}, u32[]{:S(2)}) %collective-permute-start.16) | collective-permute-done | bytes 835616 | tf_op jit(solution)/shard_map/ppermute | solution.py:757
  99.4 4.9 %second.1 = (f32[16,256,128]{2,1,0:T(8,128)S(1)}, f32[128,128]{1,0:T(8,128)S(1)}) custom-call(f32[16,256,128]{2,1,0:T(8,128)S(1)} %base.1.base_ref, f32[1632,128]{1,0:T(8,128)S(1)} %collective-permute-done.16.low_ref, f32[1632,128]{1,0:T(8,128)S(1)} %collective-permute-done.17.high_ref, bf16[2,16,256,128]{3,2,1,0:T(8,128)(2,1)S(1)} %bitcast.23, ...), custom_call_target="tpu_custom_call" | custom-call | flops 134217728 | bytes 8388608 | tf_op jit(solution)/shard_map/second/pallas_call | solution.py:639
  106.6 3.4 %collective-permute-done.19 = f32[128,128]{1,0:T(8,128)S(1)} collective-permute-done((f32[128,128]{1,0:T(8,128)S(1)}, f32[128,128]{1,0:T(8,128)S(1)}, u32[]{:S(2)}, u32[]{:S(2)}) %collective-permute-start.19) | collective-permute-done | bytes 65568 | tf_op jit(solution)/shard_map/ppermute | solution.py:807
  110.5 5.1 %collective-permute-done.20 = f32[128,128]{1,0:T(8,128)S(1)} collective-permute-done((f32[128,128]{1,0:T(8,128)S(1)}, f32[128,128]{1,0:T(8,128)S(1)}, u32[]{:S(2)}, u32[]{:S(2)}) %collective-permute-start.20) | collective-permute-done | bytes 65568 | tf_op jit(solution)/shard_map/ppermute | solution.py:807
  115.7 4.3 %collective-permute-done.21 = f32[128,128]{1,0:T(8,128)S(1)} collective-permute-done((f32[128,128]{1,0:T(8,128)S(1)}, f32[128,128]{1,0:T(8,128)S(1)}, u32[]{:S(2)}, u32[]{:S(2)}) %collective-permute-start.21) | collective-permute-done | bytes 65568 | tf_op jit(solution)/shard_map/ppermute | solution.py:807
  120.0 3.9 %collective-permute-start.22 = (f32[128,128]{1,0:T(8,128)S(1)}, f32[128,128]{1,0:T(8,128)S(1)}, u32[]{:S(2)}, u32[]{:S(2)}) collective-permute-start(f32[128,128]{1,0:T(8,128)S(1)} %add.38), channel_id=1, source_target_pairs={{0,3},{1,2},{2,1},{3,0},{4,7},{5,6},{6,5},{7,4},{8,11},{9,10},{10,... | collective-permute-start | bytes 196616 | tf_op jit(solution)/shard_map/ppermute | solution.py:807
  123.9 2.2 %collective-permute-done.22 = f32[128,128]{1,0:T(8,128)S(1)} collective-permute-done((f32[128,128]{1,0:T(8,128)S(1)}, f32[128,128]{1,0:T(8,128)S(1)}, u32[]{:S(2)}, u32[]{:S(2)}) %collective-permute-start.22) | collective-permute-done | bytes 65568 | tf_op jit(solution)/shard_map/ppermute | solution.py:807
  126.1 1.7 %collective-permute-start.23 = (f32[128,128]{1,0:T(8,128)S(1)}, f32[128,128]{1,0:T(8,128)S(1)}, u32[]{:S(2)}, u32[]{:S(2)}) collective-permute-start(f32[128,128]{1,0:T(8,128)S(1)} %add.39), channel_id=1, source_target_pairs={{0,8},{1,9},{2,10},{3,11},{4,12},{5,13},{6,14},{7,15},{8,0},{9,1},... | collective-permute-start | bytes 196616 | tf_op jit(solution)/shard_map/ppermute | solution.py:807
  127.8 2.7 %collective-permute-done.23 = f32[128,128]{1,0:T(8,128)S(1)} collective-permute-done((f32[128,128]{1,0:T(8,128)S(1)}, f32[128,128]{1,0:T(8,128)S(1)}, u32[]{:S(2)}, u32[]{:S(2)}) %collective-permute-start.23) | collective-permute-done | bytes 65568 | tf_op jit(solution)/shard_map/ppermute | solution.py:807
  130.5 3.1 %collective-permute-start.24 = (f32[128,128]{1,0:T(8,128)S(1)}, f32[128,128]{1,0:T(8,128)S(1)}, u32[]{:S(2)}, u32[]{:S(2)}) collective-permute-start(f32[128,128]{1,0:T(8,128)S(1)} %add.40), channel_id=1, source_target_pairs={{0,24},{1,25},{2,26},{3,27},{4,28},{5,29},{6,30},{7,31},{8,16},{9,... | collective-permute-start | bytes 196616 | tf_op jit(solution)/shard_map/ppermute | solution.py:807
  133.6 2.5 %collective-permute-done.24 = f32[128,128]{1,0:T(8,128)S(1)} collective-permute-done((f32[128,128]{1,0:T(8,128)S(1)}, f32[128,128]{1,0:T(8,128)S(1)}, u32[]{:S(2)}, u32[]{:S(2)}) %collective-permute-start.24) | collective-permute-done | bytes 65568 | tf_op jit(solution)/shard_map/ppermute | solution.py:807
  136.0 16.9 %turn.1 = f32[16,256,128]{2,1,0:T(8,128)} custom-call(f32[16,256,128]{2,1,0:T(8,128)S(1)} %get-tuple-element.59.second_ref, f32[128,128]{1,0:T(8,128)S(1)} %add_multiply_fusion.gram_ref), custom_call_target="tpu_custom_call" | custom-call | flops 268435456 | bytes 4194304 | tf_op jit(solution)/shard_map/turn/pallas_call | solution.py:734
  (73 shorter events, 12.6 us)
Async XLA Ops:
  0.0 20.5 %collective-permute-start.5 = (f32[16,256,128]{2,1,0:T(8,128)}, f32[16,256,128]{2,1,0:T(8,128)}, u32[]{:S(2)}, u32[]{:S(2)}) collective-permute-start(f32[16,256,128]{2,1,0:T(8,128)} %bitcast.11), channel_id=1, source_target_pairs={{0,64},{1,65},{2,66},{3,67},{4,68},{5,69},{6,70},{7,71},{8,72},{9,... | collective-permute-start | bytes 6291464 | tf_op jit(solution)/shard_map/ppermute | solution.py:757
  1.6 5.6 %copy-start.10 = (s32[4,3]{1,0:T(4,128)S(1)}, s32[4,3]{1,0:T(4,128)}, u32[]{:S(2)}) copy-start(s32[4,3]{1,0:T(4,128)} %param.7) | copy-start | bytes 148
  1.6 5.6 %copy-start.11 = (f32[4]{0:T(128)S(1)}, f32[4]{0:T(128)}, u32[]{:S(2)}) copy-start(f32[4]{0:T(128)} %param.9) | copy-start | bytes 52
  1.6 14.3 %copy-start.9 = (f32[16,16,16]{2,1,0:T(8,128)S(1)}, f32[16,16,16]{2,1,0:T(8,128)}, u32[]{:S(2)}) copy-start(f32[16,16,16]{2,1,0:T(8,128)} %param.6) | copy-start | bytes 49156
  1.6 16.0 %copy-start.1 = (f32[16,16,16,128]{3,2,1,0:T(8,128)S(1)}, f32[16,16,16,128]{3,2,1,0:T(8,128)}, u32[]{:S(2)}) copy-start(f32[16,16,16,128]{3,2,1,0:T(8,128)} %param.5) | copy-start | bytes 6291460
  5.0 19.9 %collective-permute-start.4 = (f32[6,192,128]{2,1,0:T(8,128)}, f32[6,192,128]{2,1,0:T(8,128)S(1)}, u32[]{:S(2)}, u32[]{:S(2)}) collective-permute-start(f32[6,192,128]{2,1,0:T(8,128)} %get-tuple-element.38), channel_id=1, source_target_pairs={{0,32},{1,33},{2,34},{3,35},{4,36},{5,37},{6,38},{7,39},{8,40},{9,... | collective-permute-start | bytes 1769480 | tf_op jit(solution)/shard_map/ppermute | solution.py:757
  7.5 10.0 %collective-permute-start = (f32[24,128]{1,0:T(8,128)S(1)}, f32[24,128]{1,0:T(8,128)S(1)}, u32[]{:S(2)}, u32[]{:S(2)}) collective-permute-start(f32[24,128]{1,0:T(8,128)S(1)} %reshape.33.refs_1_), channel_id=1, source_target_pairs={{0,1},{1,2},{2,3},{3,4},{4,5},{5,6},{6,7},{7,8},{8,9},{9,10},{10,1... | collective-permute-start | bytes 36872 | tf_op jit(solution)/shard_map/ppermute | solution.py:757
  9.1 8.4 %collective-permute-start.1 = (f32[24,128]{1,0:T(8,128)S(1)}, f32[24,128]{1,0:T(8,128)S(1)}, u32[]{:S(2)}, u32[]{:S(2)}) collective-permute-start(f32[24,128]{1,0:T(8,128)S(1)} %reshape.33.refs_1_), channel_id=1, source_target_pairs={{0,31},{1,0},{2,1},{3,2},{4,3},{5,4},{6,5},{7,6},{8,7},{9,8},{10,9... | collective-permute-start | bytes 36872 | tf_op jit(solution)/shard_map/ppermute | solution.py:757
  17.5 7.4 %collective-permute-start.3 = (f32[104,128]{1,0:T(8,128)S(1)}, f32[104,128]{1,0:T(8,128)S(1)}, u32[]{:S(2)}, u32[]{:S(2)}) collective-permute-start(f32[104,128]{1,0:T(8,128)S(1)} %stack.13.parcel_ref.refs_0_), channel_id=1, source_target_pairs={{0,32},{1,33},{2,34},{3,35},{4,36},{5,37},{6,38},{7,39},{8,40},{9,... | collective-permute-start | bytes 159752 | tf_op jit(solution)/shard_map/ppermute | solution.py:757
  25.7 22.2 %collective-permute-start.7 = (f32[6,192,128]{2,1,0:T(8,128)}, f32[6,192,128]{2,1,0:T(8,128)}, u32[]{:S(2)}, u32[]{:S(2)}) collective-permute-start(f32[6,192,128]{2,1,0:T(8,128)} %get-tuple-element.43), channel_id=1, source_target_pairs={{0,33},{3,34},{4,37},{7,38},{8,41},{11,42},{12,45},{15,46},{16,49}... | collective-permute-start | bytes 1769480 | tf_op jit(solution)/shard_map/ppermute | solution.py:783
  28.6 41.8 %collective-permute-start.13 = (f32[1920,128]{1,0:T(8,128)}, f32[1920,128]{1,0:T(8,128)S(1)}, u32[]{:S(2)}, u32[]{:S(2)}) collective-permute-start(f32[1920,128]{1,0:T(8,128)} %get-tuple-element.50), channel_id=1, source_target_pairs={{0,32},{1,33},{2,34},{3,35},{4,36},{5,37},{6,38},{7,39},{8,40},{9,... | collective-permute-start | bytes 2949128 | tf_op jit(solution)/shard_map/ppermute | solution.py:757
  29.8 27.6 %collective-permute-start.11 = (f32[6,16,16,128]{3,2,1,0:T(8,128)}, f32[6,16,16,128]{3,2,1,0:T(8,128)}, u32[]{:S(2)}, u32[]{:S(2)}) collective-permute-start(f32[6,16,16,128]{3,2,1,0:T(8,128)} %get-tuple-element.47), channel_id=1, source_target_pairs={{0,1},{1,2},{2,3},{3,4},{4,5},{5,6},{6,7},{7,8},{8,9},{9,10},{10,1... | collective-permute-start | bytes 2359304 | tf_op jit(solution)/shard_map/ppermute | solution.py:757
  29.8 27.6 %collective-permute-start.12 = (f32[6,16,16,128]{3,2,1,0:T(8,128)}, f32[6,16,16,128]{3,2,1,0:T(8,128)}, u32[]{:S(2)}, u32[]{:S(2)}) collective-permute-start(f32[6,16,16,128]{3,2,1,0:T(8,128)} %get-tuple-element.48), channel_id=1, source_target_pairs={{0,31},{1,0},{2,1},{3,2},{4,3},{5,4},{6,5},{7,6},{8,7},{9,8},{10,9... | collective-permute-start | bytes 2359304 | tf_op jit(solution)/shard_map/ppermute | solution.py:757
  37.6 1.2 collective-permute-start.2
  38.9 1.2 collective-permute-start.6
  40.1 17.3 %copy-start.3 = (f32[16,256,128]{2,1,0:T(8,128)S(1)}, f32[16,256,128]{2,1,0:T(8,128)}, u32[]{:S(2)}) copy-start(f32[16,256,128]{2,1,0:T(8,128)} %copy-done.2) | copy-start | bytes 6291460
  47.9 22.4 %collective-permute-start.14 = (f32[6,192,128]{2,1,0:T(8,128)}, f32[6,192,128]{2,1,0:T(8,128)S(1)}, u32[]{:S(2)}, u32[]{:S(2)}) collective-permute-start(f32[6,192,128]{2,1,0:T(8,128)} %collective-permute-done.7), channel_id=1, source_target_pairs={{1,0},{2,3},{5,4},{6,7},{9,8},{10,11},{13,12},{14,15},{17,16},{18,... | collective-permute-start | bytes 1769480 | tf_op jit(solution)/shard_map/ppermute | solution.py:790
  49.2 1.3 collective-permute-start.8
  50.6 19.8 %copy-start.5 = (f32[6,192,128]{2,1,0:T(8,128)S(1)}, f32[6,192,128]{2,1,0:T(8,128)}, u32[]{:S(2)}) copy-start(f32[6,192,128]{2,1,0:T(8,128)} %copy-done.4) | copy-start | bytes 1769476
  50.6 19.7 %collective-permute-start.9 = (f32[3,48,128]{2,1,0:T(8,128)S(1)}, f32[3,48,128]{2,1,0:T(8,128)S(1)}, u32[]{:S(2)}, u32[]{:S(2)}) collective-permute-start(f32[3,48,128]{2,1,0:T(8,128)S(1)} %add.34.refs_4_.rest_0_), channel_id=1, source_target_pairs={{0,32},{1,33},{2,34},{3,35},{4,36},{5,37},{6,38},{7,39},{8,40},{9,... | collective-permute-start | bytes 221192 | tf_op jit(solution)/shard_map/ppermute | solution.py:757
  70.3 10.1 %copy-start.7 = (f32[16,64,128]{2,1,0:T(8,128)S(1)}, f32[16,64,128]{2,1,0:T(8,128)}, u32[]{:S(2)}) copy-start(f32[16,64,128]{2,1,0:T(8,128)} %copy-done.6) | copy-start | bytes 1572868
  72.5 9.4 %collective-permute-start.15 = (f32[16,256,128]{2,1,0:T(8,128)S(1)}, f32[16,256,128]{2,1,0:T(8,128)S(1)}, u32[]{:S(2)}, u32[]{:S(2)}) collective-permute-start(f32[16,256,128]{2,1,0:T(8,128)S(1)} %get-tuple-element.53.s_ref), channel_id=1, source_target_pairs={{0,64},{1,65},{2,66},{3,67},{4,68},{5,69},{6,70},{7,71},{8,72},{9,... | collective-permute-start | bytes 6291464 | tf_op jit(solution)/shard_map/ppermute | solution.py:757
  72.6 26.8 %collective-permute-start.16 = (f32[1632,128]{1,0:T(8,128)S(1)}, f32[1632,128]{1,0:T(8,128)S(1)}, u32[]{:S(2)}, u32[]{:S(2)}) collective-permute-start(f32[1632,128]{1,0:T(8,128)S(1)} %get-tuple-element.54), channel_id=1, source_target_pairs={{0,1},{1,2},{2,3},{3,4},{4,5},{5,6},{6,7},{7,8},{8,9},{9,10},{10,1... | collective-permute-start | bytes 2506760 | tf_op jit(solution)/shard_map/ppermute | solution.py:757
  72.7 26.7 %collective-permute-start.17 = (f32[1632,128]{1,0:T(8,128)S(1)}, f32[1632,128]{1,0:T(8,128)S(1)}, u32[]{:S(2)}, u32[]{:S(2)}) collective-permute-start(f32[1632,128]{1,0:T(8,128)S(1)} %get-tuple-element.55), channel_id=1, source_target_pairs={{0,31},{1,0},{2,1},{3,2},{4,3},{5,4},{6,5},{7,6},{8,7},{9,8},{10,9... | collective-permute-start | bytes 2506760 | tf_op jit(solution)/shard_map/ppermute | solution.py:757
  80.4 4.5 %collective-permute-start.10 = (f32[16,64,128]{2,1,0:T(8,128)S(1)}, f32[16,64,128]{2,1,0:T(8,128)S(1)}, u32[]{:S(2)}, u32[]{:S(2)}) collective-permute-start(f32[16,64,128]{2,1,0:T(8,128)S(1)} %copy-done.7), channel_id=1, source_target_pairs={{1,33},{2,34},{5,37},{6,38},{9,41},{10,42},{13,45},{14,46},{17,49}... | collective-permute-start | bytes 1572872 | tf_op jit(solution)/shard_map/ppermute | solution.py:800
  104.4 1.3 collective-permute-start.18
  105.7 4.3 %collective-permute-start.19 = (f32[128,128]{1,0:T(8,128)S(1)}, f32[128,128]{1,0:T(8,128)S(1)}, u32[]{:S(2)}, u32[]{:S(2)}) collective-permute-start(f32[128,128]{1,0:T(8,128)S(1)} %add.35), channel_id=1, source_target_pairs={{0,32},{1,33},{2,34},{3,35},{4,36},{5,37},{6,38},{7,39},{8,40},{9,... | collective-permute-start | bytes 196616 | tf_op jit(solution)/shard_map/ppermute | solution.py:807
  110.1 5.6 %collective-permute-start.20 = (f32[128,128]{1,0:T(8,128)S(1)}, f32[128,128]{1,0:T(8,128)S(1)}, u32[]{:S(2)}, u32[]{:S(2)}) collective-permute-start(f32[128,128]{1,0:T(8,128)S(1)} %add.36), channel_id=1, source_target_pairs={{0,36},{1,37},{2,38},{3,39},{4,32},{5,33},{6,34},{7,35},{8,44},{9,... | collective-permute-start | bytes 196616 | tf_op jit(solution)/shard_map/ppermute | solution.py:807
  115.6 4.3 %collective-permute-start.21 = (f32[128,128]{1,0:T(8,128)S(1)}, f32[128,128]{1,0:T(8,128)S(1)}, u32[]{:S(2)}, u32[]{:S(2)}) collective-permute-start(f32[128,128]{1,0:T(8,128)S(1)} %add.37), channel_id=1, source_target_pairs={{0,1},{1,0},{2,3},{3,2},{4,5},{5,4},{6,7},{7,6},{8,9},{9,8},{10,11... | collective-permute-start | bytes 196616 | tf_op jit(solution)/shard_map/ppermute | solution.py:807
  120.0 6.1 %collective-permute-start.22 = (f32[128,128]{1,0:T(8,128)S(1)}, f32[128,128]{1,0:T(8,128)S(1)}, u32[]{:S(2)}, u32[]{:S(2)}) collective-permute-start(f32[128,128]{1,0:T(8,128)S(1)} %add.38), channel_id=1, source_target_pairs={{0,3},{1,2},{2,1},{3,0},{4,7},{5,6},{6,5},{7,4},{8,11},{9,10},{10,... | collective-permute-start | bytes 196616 | tf_op jit(solution)/shard_map/ppermute | solution.py:807
  126.1 4.3 %collective-permute-start.23 = (f32[128,128]{1,0:T(8,128)S(1)}, f32[128,128]{1,0:T(8,128)S(1)}, u32[]{:S(2)}, u32[]{:S(2)}) collective-permute-start(f32[128,128]{1,0:T(8,128)S(1)} %add.39), channel_id=1, source_target_pairs={{0,8},{1,9},{2,10},{3,11},{4,12},{5,13},{6,14},{7,15},{8,0},{9,1},... | collective-permute-start | bytes 196616 | tf_op jit(solution)/shard_map/ppermute | solution.py:807
  130.5 5.6 %collective-permute-start.24 = (f32[128,128]{1,0:T(8,128)S(1)}, f32[128,128]{1,0:T(8,128)S(1)}, u32[]{:S(2)}, u32[]{:S(2)}) collective-permute-start(f32[128,128]{1,0:T(8,128)S(1)} %add.40), channel_id=1, source_target_pairs={{0,24},{1,25},{2,26},{3,27},{4,28},{5,29},{6,30},{7,31},{8,16},{9,... | collective-permute-start | bytes 196616 | tf_op jit(solution)/shard_map/ppermute | solution.py:807
  (5 other events, 9.9 us)

commit v9 on v8

--- a/solution.py
+++ b/solution.py
@@ -12,6 +12,7 @@
 C = 16
 ROWS = C * C
 CELLS = C * C * C
+NCELLS = 32 * 32 * 512
 S = 128
 W = 9
 R = 4
@@ -73,7 +74,7 @@
 B = 4
 STEPS = C // B
 N = 2
-FIRST = 6
+FIRST = 8
 MIDDLE = 10
 EDGE = 192
 MID = 64
@@ -128,14 +129,14 @@
 SCALARS = pl.BlockSpec(memory_space=pltpu.SMEM)
 FULL = sds((C, ROWS, S))
 FULL_ROWS = sds((CELLS, S))
-HALO_ROWS = H * ROWS
-MESSAGE = sds((HALO_ROWS + 2 * NEAR, S))
+HALO_ROWS = H * FIRST * C
+SHARES = 2 * NEAR
 HALO = sds((H, C, C, S))
 EDGES = [sds((FIRST, EDGE, S)), sds((C - FIRST, EDGE, S)), sds((C - MIDDLE, EDGE, S))]
 
 
 def halo_rows(x, z):
-    return pl.ds(pl.multiple_of(z * ROWS + x * C, C), C)
+    return pl.ds(pl.multiple_of(z * FIRST * C + x * C, C), C)
 
 
 def halves(y, half):
@@ -481,50 +482,79 @@
     return jnp.concatenate([shares[0:32], pair])
 
 
-def first_kernel(s_ref, side_ref, vb_ref, *refs):
-    inner_ref, part_ref, mate_ref, q_ref, mix_ref, head_ref, tail_ref = refs[3:]
-    step = pl.program_id(0)
-
-    @pl.when(step == 0)
+def first_planes(s_ref, side_ref, vb_ref, edge_ref, q_ref, mix_ref, head_ref, tail_ref):
+    for p in range(N):
+        for half in range(2):
+            ring = {y: s_ref[p, halves(y, half), :] for y in range(C)}
+            for y in range(H):
+                ring[C + y] = edge_ref[p, halves(y, half), :]
+                ring[y - H] = edge_ref[p, halves(H + y, half), :]
+            for y in range(C):
+                rows = halves(y, half)
+                dy = tap_sum(lambda i: ring[i], y)
+                q = dy + vb_ref[p, rows, :] * ring[y]
+                q_ref[p, rows, :] = q
+                mix_ref[p, rows, :] = side_ref[p, rows, :] + q + dy
+        for z in range(H):
+            rows = halo_rows(pl.program_id(0) * N + p, z)
+            head_ref[rows, :] = mix_ref[p, stride_rows(z), :]
+            tail_ref[rows, :] = mix_ref[p, stride_rows(C - H + z), :]
+
+
+def half_spec(start):
+    return pl.BlockSpec((N, ROWS, S), lambda i: (i + start // N, 0, 0))
+
+
+def first_half(s, side_part, vb, edge):
+    return pl.pallas_call(
+        first_planes,
+        grid=(FIRST // N,),
+        in_specs=[half_spec(0)] * 3 + [edge_spec(0, FIRST)],
+        out_specs=[half_spec(0)] * 2 + [whole(HALO_ROWS)] * 2,
+        out_shape=[FULL, FULL, sds((HALO_ROWS, S)), sds((HALO_ROWS, S))],
+        compiler_params=params(16),
+        cost_estimate=cost(1 << 23, 7 << 20),
+        name="first_half",
+    )(s, side_part, vb, edge)
+
+
+def other_half_kernel(s_ref, side_ref, vb_ref, edge_ref, relay_ref, inner_ref, part_ref, mate_ref, _, __, *out):
+    q_ref, mix_ref, head_ref, tail_ref = out
+
+    @pl.when(pl.program_id(0) == 0)
     def _():
         for j in range(2):
             rows = slice(HALO_ROWS + j * NEAR, HALO_ROWS + (j + 1) * NEAR)
             head_ref[rows, :] = part_ref[j] + mate_ref[j]
             tail_ref[rows, :] = part_ref[j + 1] + mate_ref[j + 1]
 
-    def planes(edge_ref):
-        for p in range(N):
-            for half in range(2):
-                ring = {y: s_ref[p, halves(y, half), :] for y in range(C)}
-                for y in range(H):
-                    ring[C + y] = edge_ref[p, halves(y, half), :]
-                    ring[y - H] = edge_ref[p, halves(H + y, half), :]
-                for y in range(C):
-                    rows = halves(y, half)
-                    dy = tap_sum(lambda i: ring[i], y)
-                    q = dy + vb_ref[p, rows, :] * ring[y]
-                    q_ref[p, rows, :] = q
-                    mix_ref[p, rows, :] = side_ref[p, rows, :] + q + dy
-            for z in range(H):
-                rows = halo_rows(step * N + p, z)
-                head_ref[rows, :] = mix_ref[p, stride_rows(z), :]
-                tail_ref[rows, :] = mix_ref[p, stride_rows(C - H + z), :]
-
-    for_piece(refs[:3], inner_ref, planes)
-
-
-def make_first(s, side_part, vb, edges, inner, part, part_mate):
+    direct = (inner_ref[0] == 1) | (pl.program_id(0) < (MIDDLE - FIRST) // N)
+
+    @pl.when(direct)
+    def _():
+        first_planes(s_ref, side_ref, vb_ref, edge_ref, *out)
+
+    @pl.when(jnp.logical_not(direct))
+    def _():
+        first_planes(s_ref, side_ref, vb_ref, relay_ref, *out)
+
+
+def other_half(s, side_part, vb, message, relayed, inner, part, part_mate, q, mix):
     shares = pl.BlockSpec((3, NEAR, S), lambda i: (0, 0, 0))
-    return pl.pallas_call(
-        first_kernel,
-        grid=(C // N,),
-        in_specs=[plane_spec(ROWS, N)] * 3 + edge_specs() + [SCALARS] + [shares] * 2,
-        out_specs=[plane_spec(ROWS, N), plane_spec(ROWS, N), whole(MESSAGE.shape[0]), whole(MESSAGE.shape[0])],
-        out_shape=[FULL, FULL, MESSAGE, MESSAGE],
+    anywhere = pl.BlockSpec(memory_space=pl.ANY)
+    relay_spec = pl.BlockSpec((N, EDGE, S), lambda i: (jnp.maximum(i - (MIDDLE - FIRST) // N, 0), 0, 0))
+    return pl.pallas_call(
+        other_half_kernel,
+        grid=((C - FIRST) // N,),
+        in_specs=[half_spec(FIRST)] * 3
+        + [pl.BlockSpec((N, EDGE, S), lambda i: (i, 0, 0)), relay_spec, SCALARS, shares, shares, anywhere, anywhere],
+        out_specs=[half_spec(FIRST)] * 2 + [whole(HALO_ROWS + SHARES)] * 2,
+        out_shape=[FULL, FULL, sds((HALO_ROWS + SHARES, S)), sds((HALO_ROWS + SHARES, S))],
+        input_output_aliases={8: 0, 9: 1},
         compiler_params=params(16),
-        cost_estimate=cost(1 << 24, 14 << 20),
-        name="first",
-    )(s, side_part, vb, *edges, inner, part, part_mate)
+        cost_estimate=cost(1 << 23, 7 << 20),
+        name="other_half",
+    )(s, side_part, vb, message, relayed, inner, part, part_mate, q, mix)
 
 
 def base_kernel(s_ref, mid_ref, vb_ref, vb_mate_ref, q_ref, side_ref, part_ref, *refs):
@@ -583,8 +613,8 @@
     )(s, mid, vb, vb_mate, q, side_part, part, *edges, inner, edges[1].reshape(-1, S))
 
 
-def second_kernel(base_ref, low_ref, high_ref, gg_high_ref, gg_low_ref, *rest):
-    part_ref, mate_ref, energy_ref, second_ref, gram_ref, cross_ref, w_ref, halo_ref = rest
+def second_kernel(base_ref, low_one_ref, high_one_ref, low_ref, high_ref, gg_high_ref, gg_low_ref, *rest):
+    part_ref, mate_ref, energy_ref, upper_ref, second_ref, keep_ref, give_ref, gram_ref, cross_ref, w_ref, halo_ref = rest
     step = pl.program_id(0)
 
     @pl.when(step == 0)
@@ -605,14 +635,23 @@
         w_ref[0:NEAR, :] = 2.0 * energy_ref[...] * two
         w_ref[64 : 64 + NEAR, :] = 2.0 * near
 
-    for p in range(B):
-        low = [low_ref[halo_rows(step * B + p, j), :] for j in range(H)]
-        high = [high_ref[halo_rows(step * B + p, j), :] for j in range(H)]
-        for z in range(H):
-            add = sum((2.0 * OFF[k - 1]) * low[z - k + H] for k in range(z + 1, H + 1))
-            halo_ref[p, stride_rows(z), :] = add
-            add = sum((2.0 * OFF[H + j - z - 1]) * high[j] for j in range(z + 1))
-            halo_ref[p, stride_rows(C - H + z), :] = add
+    def halo_part(below_ref, above_ref, first_plane):
+        for p in range(B):
+            low = [below_ref[halo_rows(step * B + p - first_plane, j), :] for j in range(H)]
+            high = [above_ref[halo_rows(step * B + p - first_plane, j), :] for j in range(H)]
+            for z in range(H):
+                add = sum((2.0 * OFF[k - 1]) * low[z - k + H] for k in range(z + 1, H + 1))
+                halo_ref[p, stride_rows(z), :] = add
+                add = sum((2.0 * OFF[H + j - z - 1]) * high[j] for j in range(z + 1))
+                halo_ref[p, stride_rows(C - H + z), :] = add
+
+    @pl.when(step < FIRST // B)
+    def _():
+        halo_part(low_one_ref, high_one_ref, 0)
+
+    @pl.when(step >= FIRST // B)
+    def _():
+        halo_part(low_ref, high_ref, FIRST)
 
     w_high, w_low = split(w_ref[...])
     gram = jnp.zeros((S, S), F32)
@@ -631,23 +670,28 @@
     @pl.when(step == STEPS - 1)
     def _():
         cross = cross_ref[...]
-        gram_ref[...] += cross + cross.T
-
-
-def make_second(base, low, high, gg, weighted):
-    shares = pl.BlockSpec((3, NEAR, S), lambda i: (0, 0, 0))
+        gram = (gram_ref[...] + (cross + cross.T)) * (1.0 / NCELLS)
+        upper = upper_ref[0] == 1
+        keep_ref[...] = jnp.where(upper, gram[S // 2 :], gram[: S // 2])
+        give_ref[...] = jnp.where(upper, gram[: S // 2], gram[S // 2 :])
+
+
+def make_second(base, halos, gg, shares, upper):
+    three = pl.BlockSpec((3, NEAR, S), lambda i: (0, 0, 0))
     return pl.pallas_call(
         second_kernel,
         grid=(STEPS,),
-        in_specs=[plane_spec(), whole(MESSAGE.shape[0]), whole(MESSAGE.shape[0]), part_spec(0), part_spec(1)]
-        + [shares, shares, whole(NEAR)],
-        out_specs=[plane_spec(), whole()],
-        out_shape=[FULL, sds((S, S))],
-        scratch_shapes=[pltpu.VMEM((S, S), F32), pltpu.VMEM((S, S), F32), pltpu.VMEM((B, ROWS, S), F32)],
+        in_specs=[plane_spec()]
+        + [whole(HALO_ROWS)] * 2
+        + [whole(HALO_ROWS + SHARES)] * 2
+        + [part_spec(0), part_spec(1), three, three, whole(NEAR), SCALARS],
+        out_specs=[plane_spec(), whole(S // 2), whole(S // 2)],
+        out_shape=[FULL, sds((S // 2, S)), sds((S // 2, S))],
+        scratch_shapes=[pltpu.VMEM((S, S), F32)] * 3 + [pltpu.VMEM((B, ROWS, S), F32)],
         compiler_params=params(16),
         cost_estimate=cost(1 << 27, 8 << 20),
         name="second",
-    )(base, low, high, gg, gg, *weighted)
+    )(base, *halos, gg, gg, *shares, upper)
 
 
 def exact(a, b):
@@ -715,9 +759,12 @@
     x_ref[...] = x_ref[...] * across
 
 
-def turn_kernel(second_ref, gram_ref, out_ref, a_ref, x_ref, i_high_ref, i_low_ref, state_ref):
+def turn_kernel(second_ref, own_ref, other_ref, upper_ref, out_ref, gram_ref, a_ref, x_ref, i_high_ref, i_low_ref, state_ref):
     @pl.when(pl.program_id(0) == 0)
     def _():
+        upper = upper_ref[0] == 1
+        gram_ref[: S // 2, :] = jnp.where(upper, other_ref[...], own_ref[...])
+        gram_ref[S // 2 :, :] = jnp.where(upper, own_ref[...], other_ref[...])
         inverse_factor(gram_ref, a_ref, x_ref, state_ref)
         i_high, i_low = split(x_ref[...].T)
         i_high_ref[...] = i_high
@@ -730,18 +777,18 @@
         out_ref[p] = mm(high, i_high) + (mm(high, i_low) + mm(low, i_high))
 
 
-def turn(second, gram):
+def turn(second, own, other, upper):
     return pl.pallas_call(
         turn_kernel,
         grid=(STEPS,),
-        in_specs=[plane_spec(), whole()],
+        in_specs=[plane_spec(), whole(S // 2), whole(S // 2), SCALARS],
         out_specs=plane_spec(),
         out_shape=FULL,
-        scratch_shapes=[pltpu.VMEM((S, S), F32)] * 2 + [pltpu.VMEM((S, S), BF16)] * 2 + [pltpu.SMEM((1,), jnp.int32)],
+        scratch_shapes=[pltpu.VMEM((S, S), F32)] * 3 + [pltpu.VMEM((S, S), BF16)] * 2 + [pltpu.SMEM((1,), jnp.int32)],
         compiler_params=params(16),
         cost_estimate=cost(1 << 28, 4 << 20),
         name="turn",
-    )(second, gram)
+    )(second, own, other, upper)
 
 
 def per_device(states, potential, atom_sites, projectors, energies):
@@ -784,29 +831,34 @@
     message = send(message, over_y)
     parcel_xy = send(parcel_y, over_x)
     corner = jnp.stack([gx * C, gy * C]).astype(jnp.int32)
+    upper = gx.astype(jnp.int32).reshape(1)
+    planes = vb.reshape(C, ROWS, S)
+    side_part = side_z(s, beside, low, high)
+    q, mix, head, tail = first_half(s, side_part, planes, one_edge)
+    low_one, high_one = send(tail, 0, 1), send(head, 0, -1)
+    parcel_xy, head, tail, relayed = barrier((parcel_xy, head, tail, relayed))
+    relayed = lax.ppermute(relayed, AXES, [(d, d ^ 1) for d in inner_ones])
     gg, part, energy = prep([parcel, parcel_x, parcel_y, parcel_xy], corner, vb, s)
 
-    part, relayed = barrier((part, relayed))
-    relayed = lax.ppermute(relayed, AXES, [(d, d ^ 1) for d in inner_ones])
     part = part + send(part, over_x)
     part_mate = send(part, over_y)
-    side_part = side_z(s, beside, low, high)
-    edges = [one_edge, message.reshape(C - FIRST, EDGE, S), relayed]
-    vb = vb.reshape(C, ROWS, S)
-    q, mix, head, tail = make_first(s, side_part, vb, edges, inner, part, part_mate)
-    low, high = send(tail, 0, 1), send(head, 0, -1)
+    part_mate, low_one, high_one = barrier((part_mate, low_one, high_one))
+    message = message.reshape(C - FIRST, EDGE, S)
+    q, mix, head, tail = other_half(s, side_part, planes, message, relayed, inner, part, part_mate, q, mix)
+    halos = [low_one, high_one, send(tail, 0, 1), send(head, 0, -1)]
     mate = send(mix, over_x)
     mid, part_mate = barrier((mid, part_mate))
     mid = lax.ppermute(mid, AXES, [(d, d ^ over_y) for d in inner_ones])
-    vb_mate = spread(parcel_y).reshape(C, ROWS, S)
+    planes_mate = spread(parcel_y).reshape(C, ROWS, S)
     part_two = side_again(mix, mate)
-    base = make_base(s, mid, vb, vb_mate, q, side_part, part_two, edges, inner)
-    second, gram = make_second(base, low, high, gg.reshape(2, C, ROWS, S), [part, part_mate, energy])
-
-    for flip in (64, 32, 36, 1, 3, 8, 24):
-        gram = gram + lax.ppermute(gram, AXES, [(d, d ^ flip) for d in range(count)])
-    gram = gram * (1.0 / (CELLS * count))
-    return turn(second, gram).reshape(C, C, C, S)
+    base = make_base(s, mid, planes, planes_mate, q, side_part, part_two, [one_edge, message, relayed], inner)
+    gg = gg.reshape(2, C, ROWS, S)
+    second, own, give = make_second(base, halos, gg, [part, part_mate, energy], upper)
+
+    own = own + send(give, over_x)
+    for flip in (32, 36, 1, 3, 8, 24):
+        own = own + lax.ppermute(own, AXES, [(d, d ^ flip) for d in range(count)])
+    return turn(second, own, send(own, over_x), upper).reshape(C, C, C, S)
 
 
 def solution(mesh):

time: 154 us -> 164 us (1.065)
  local copies, waits for them, and re-layouts: 5 us -> 15.1 us
  waiting for transfers between devices: 51.7 us -> 46.2 us
  starting transfers between devices: 43.6 us -> 48.9 us
    unnamed x25 -> x57, local copies, waits for them, and re-layouts: 4.56 us -> 14.7 us
    ppermute x15 -> x19, starting transfers between devices: 28.7 us -> 38.1 us  [send(): return lax.ppermute(value, AXES, [(d, target(d)) for d in range(count)])]
    ppermute x15 -> x19, waiting for transfers between devices: 30.3 us -> 25 us  [send(): return lax.ppermute(value, AXES, [(d, target(d)) for d in range(count)])]
    ppermute x7 -> x6, starting transfers between devices: 10.1 us -> 6.68 us  [per_device(): own = own + lax.ppermute(own, AXES, [(d, d ^ flip) for d in range(count)])]
    pallas_call x2 -> x3, Pallas kernels: 7.08 us -> 9.71 us  [the longest x1 6.8 us: make_second(): pl.pallas_call(second_kernel, grid=(STEPS,), in_specs=[plane_spec()] + [w...]
    ppermute x7 -> x6, waiting for transfers between devices: 21.5 us -> 20.4 us  [per_device(): own = own + lax.ppermute(own, AXES, [(d, d ^ flip) for d in range(count)])]
  transfers between devices with their start and end apart: 25 -> 28, of which waited for: 14 -> 16; matrix products, arithmetic and copies ran while one was open for 0% -> 0% of each run, Pallas kernels for 18% -> 17%
where the time goes in v9:
time: 164 us; the launch traced here: 163 us
  Pallas kernels  51.8 us (32%)
  starting transfers between devices  48.9 us (30%)
  waiting for transfers between devices  46.2 us (28%)
  local copies, waits for them, and re-layouts  15.1 us (9%)
    ppermute x19, starting transfers between devices, send(): return lax.ppermute(value, AXES, [(d, target(d)) for d in range(count)])  38.1 us
    ppermute x19, waiting for transfers between devices, send(): return lax.ppermute(value, AXES, [(d, target(d)) for d in range(count)])  25 us
    ppermute x6, waiting for transfers between devices, per_device(): own = own + lax.ppermute(own, AXES, [(d, d ^ flip) for d in range(count)])  20.4 us
    pallas_call x1, Pallas kernels, turn(): pl.pallas_call(turn_kernel, grid=(STEPS,), in_specs=[plane_spec(), whole(...  16.9 us
    unnamed x57, local copies, waits for them, and re-layouts  14.7 us
    pallas_call x1, Pallas kernels, prep(): pl.pallas_call(prep_kernel, in_specs=[vmem] * 4 + [pl.BlockSpec(memory_sp...  7.79 us
    pallas_call x1, Pallas kernels, make_second(): pl.pallas_call(second_kernel, grid=(STEPS,), in_specs=[plane_spec()] + [w...  6.8 us
    ppermute x6, starting transfers between devices, per_device(): own = own + lax.ppermute(own, AXES, [(d, d ^ flip) for d in range(count)])  6.68 us
  transfers between devices with their start and end apart: 28, of which 16 were waited for; matrix products, arithmetic and copies ran while one was open for 0% of the time, Pallas kernels for 17%

profile of v9, /device:TPU:0, one launch (start us, length us, event | category | flops | bytes accessed | tf_op | source)
XLA Modules:
  0.0 162.6 jit_solution(6042016601971042715)
XLA Ops:
  0.0 1.6 copy-done
  1.6 2.6 %pack.1 = (f32[8,192,128]{2,1,0:T(8,128)}, f32[6,16,16,128]{3,2,1,0:T(8,128)S(1)}, f32[6,16,16,128]{3,2,1,0:T(8,128)S(1)}) custom-call(f32[16,256,128]{2,1,0:T(8,128)S(1)} %bitcast.13), custom_call_target="tpu_custom_call" | custom-call | flops 4294967296 | bytes 6291456 | tf_op jit(solution)/shard_map/pack/pallas_call | solution.py:163
  5.9 2.0 %collective-permute-start.4 = (f32[8,192,128]{2,1,0:T(8,128)}, f32[8,192,128]{2,1,0:T(8,128)S(1)}, u32[]{:S(2)}, u32[]{:S(2)}) collective-permute-start(f32[8,192,128]{2,1,0:T(8,128)} %get-tuple-element.46), channel_id=1, source_target_pairs={{0,32},{1,33},{2,34},{3,35},{4,36},{5,37},{6,38},{7,39},{8,40},{9,... | collective-permute-start | bytes 2359304 | tf_op jit(solution)/shard_map/ppermute | solution.py:804
  10.0 6.8 %collective-permute-start.1 = (f32[24,128]{1,0:T(8,128)S(1)}, f32[24,128]{1,0:T(8,128)S(1)}, u32[]{:S(2)}, u32[]{:S(2)}) collective-permute-start(f32[24,128]{1,0:T(8,128)S(1)} %reshape.36.refs_1_), channel_id=1, source_target_pairs={{0,31},{1,0},{2,1},{3,2},{4,3},{5,4},{6,5},{7,6},{8,7},{9,8},{10,9... | collective-permute-start | bytes 36872 | tf_op jit(solution)/shard_map/ppermute | solution.py:804
  18.6 8.1 %collective-permute-start.8 = (f32[6,16,16,128]{3,2,1,0:T(8,128)}, f32[6,16,16,128]{3,2,1,0:T(8,128)S(1)}, u32[]{:S(2)}, u32[]{:S(2)}) collective-permute-start(f32[6,16,16,128]{3,2,1,0:T(8,128)} %copy-done.20), channel_id=1, source_target_pairs={{0,31},{1,0},{2,1},{3,2},{4,3},{5,4},{6,5},{7,6},{8,7},{9,8},{10,9... | collective-permute-start | bytes 2359304 | tf_op jit(solution)/shard_map/ppermute | solution.py:804
  28.0 3.2 %side_x.1.part_ref = f32[16,256,128]{2,1,0:T(8,128)S(1)} custom-call(f32[16,256,128]{2,1,0:T(8,128)S(1)} %bitcast.15, f32[16,256,128]{2,1,0:T(8,128)} %collective-permute-done.5.mate_ref), custom_call_target="tpu_custom_call" | custom-call | flops 16777216 | bytes 6291456 | tf_op jit(solution)/shard_map/side_x/pallas_call | solution.py:250
  31.3 13.4 %collective-permute-done.3.refs_2_.parcel_ref = f32[104,128]{1,0:T(8,128)S(1)} collective-permute-done((f32[104,128]{1,0:T(8,128)S(1)}, f32[104,128]{1,0:T(8,128)S(1)}, u32[]{:S(2)}, u32[]{:S(2)}) %collective-permute-start.3) | collective-permute-done | bytes 53280 | tf_op jit(solution)/shard_map/ppermute | solution.py:804
  45.5 2.2 %collective-permute-start.9 = (f32[6,192,128]{2,1,0:T(8,128)S(1)}, f32[6,192,128]{2,1,0:T(8,128)}, u32[]{:S(2)}, u32[]{:S(2)}) collective-permute-start(f32[6,192,128]{2,1,0:T(8,128)S(1)} %get-tuple-element.56), channel_id=1, source_target_pairs={{0,33},{3,34},{4,37},{7,38},{8,41},{11,42},{12,45},{15,46},{16,49}... | collective-permute-start | bytes 1769480 | tf_op jit(solution)/shard_map/ppermute | solution.py:830
  47.7 1.7 %collective-permute-start.15 = (f32[1536,128]{1,0:T(8,128)}, f32[1536,128]{1,0:T(8,128)S(1)}, u32[]{:S(2)}, u32[]{:S(2)}) collective-permute-start(f32[1536,128]{1,0:T(8,128)} %get-tuple-element.61), channel_id=1, source_target_pairs={{0,32},{1,33},{2,34},{3,35},{4,36},{5,37},{6,38},{7,39},{8,40},{9,... | collective-permute-start | bytes 2359304 | tf_op jit(solution)/shard_map/ppermute | solution.py:804
  50.9 2.8 %side_z.1.side_ref = f32[16,256,128]{2,1,0:T(8,128)S(1)} custom-call(f32[16,256,128]{2,1,0:T(8,128)S(1)} %bitcast.16, f32[16,256,128]{2,1,0:T(8,128)S(1)} %side_x.1.part_ref, f32[6,16,16,128]{3,2,1,0:T(8,128)S(1)} %collective-permute-done.7.low_ref, f32[6,16,16,128]{3,2,1,0:T(8,128)S(1)} %collective-permute-done.8.high_ref), custom_call_target="tpu_custom_call" | custom-call | flops 16777216 | bytes 8388608 | tf_op jit(solution)/shard_map/side_z/pallas_call | solution.py:275
  53.8 1.9 %first_half.1 = (f32[16,256,128]{2,1,0:T(8,128)S(1)}, f32[16,256,128]{2,1,0:T(8,128)S(1)}, f32[768,128]{1,0:T(8,128)}, f32[768,128]{1,0:T(8,128)}) custom-call(f32[16,256,128]{2,1,0:T(8,128)S(1)} %bitcast.17, f32[16,256,128]{2,1,0:T(8,128)S(1)} %side_z.1.side_ref, f32[16,256,128]{2,1,0:T(8,128)S(1)} %bitcast.21, f32[8,192,128]{2,1,0:T(8,128)S(1)} %copy-done.14), custom_call_target="tpu_custom_call" | custom-call | flops 8388608 | bytes 7340032 | tf_op jit(solution)/shard_map/first_half/pallas_call | solution.py:509
  61.0 3.7 %collective-permute-start.12 = (f32[768,128]{1,0:T(8,128)}, f32[768,128]{1,0:T(8,128)}, u32[]{:S(2)}, u32[]{:S(2)}) collective-permute-start(f32[768,128]{1,0:T(8,128)} %get-tuple-element.55), channel_id=1, source_target_pairs={{0,1},{1,2},{2,3},{3,4},{4,5},{5,6},{6,7},{7,8},{8,9},{9,10},{10,1... | collective-permute-start | bytes 1179656 | tf_op jit(solution)/shard_map/ppermute | solution.py:804
  64.8 4.6 %collective-permute-start.13 = (f32[768,128]{1,0:T(8,128)}, f32[768,128]{1,0:T(8,128)}, u32[]{:S(2)}, u32[]{:S(2)}) collective-permute-start(f32[768,128]{1,0:T(8,128)} %get-tuple-element.54), channel_id=1, source_target_pairs={{0,31},{1,0},{2,1},{3,2},{4,3},{5,4},{6,5},{7,6},{8,7},{9,8},{10,9... | collective-permute-start | bytes 1179656 | tf_op jit(solution)/shard_map/ppermute | solution.py:804
  70.6 1.6 copy-done.3
  73.8 7.8 %prep.1 = (bf16[2,4096,128]{2,1,0:T(8,128)(2,1)S(1)}, f32[3,48,128]{2,1,0:T(8,128)S(1)}, f32[48,128]{1,0:T(8,128)S(1)}) custom-call(f32[104,128]{1,0:T(8,128)S(1)} %stack.13.parcel_ref.refs_0_, f32[104,128]{1,0:T(8,128)S(1)} %collective-permute-done.2.refs_1_, f32[104,128]{1,0:T(8,128)S(1)} %copy-done.17, f32[104,128]{1,0:T(8,128)S(1)} %copy-done.19, ...), custom_call_target="tpu_custom_call" | custom-call | flops 134217728 | bytes 10485760 | tf_op jit(solution)/shard_map/prep/pallas_call | solution.py:460
  84.1 1.9 %collective-permute-done.13.high_one_ref = f32[768,128]{1,0:T(8,128)} collective-permute-done((f32[768,128]{1,0:T(8,128)}, f32[768,128]{1,0:T(8,128)}, u32[]{:S(2)}, u32[]{:S(2)}) %collective-permute-start.13) | collective-permute-done | bytes 393248 | tf_op jit(solution)/shard_map/ppermute | solution.py:804
  87.4 1.6 copy-done.10
  91.0 7.7 %collective-permute-start.19 = (f32[864,128]{1,0:T(8,128)S(1)}, f32[864,128]{1,0:T(8,128)S(1)}, u32[]{:S(2)}, u32[]{:S(2)}) collective-permute-start(f32[864,128]{1,0:T(8,128)S(1)} %get-tuple-element.70), channel_id=1, source_target_pairs={{0,31},{1,0},{2,1},{3,2},{4,3},{5,4},{6,5},{7,6},{8,7},{9,8},{10,9... | collective-permute-start | bytes 1327112 | tf_op jit(solution)/shard_map/ppermute | solution.py:804
  99.6 2.9 %side_again.1.part_ref = f32[16,256,128]{2,1,0:T(8,128)S(1)} custom-call(f32[16,256,128]{2,1,0:T(8,128)S(1)} %get-tuple-element.66.s_ref, f32[16,256,128]{2,1,0:T(8,128)S(1)} %collective-permute-done.17.mate_ref), custom_call_target="tpu_custom_call" | custom-call | flops 33554432 | bytes 6291456 | tf_op jit(solution)/shard_map/side_again/pallas_call | solution.py:302
  102.5 1.6 copy-done.12
  104.1 2.9 %base.1.base_ref = f32[16,256,128]{2,1,0:T(8,128)S(1)} custom-call(f32[16,256,128]{2,1,0:T(8,128)S(1)} %bitcast.20, f32[16,64,128]{2,1,0:T(8,128)S(1)} %collective-permute-done.14.mid_ref, f32[16,256,128]{2,1,0:T(8,128)S(1)} %bitcast.23, f32[16,256,128]{2,1,0:T(8,128)S(1)} %bitcast.26, f32[16,256,128]{2,1,0:T(8,128)S(1)} %copy-done.12, ...), custom_call_target="tpu_custom_call" | custom-call | flops 33554432 | bytes 16777216 | tf_op jit(solution)/shard_map/base/pallas_call | solution.py:600
  107.0 2.2 %collective-permute-done.18.low_ref = f32[864,128]{1,0:T(8,128)S(1)} collective-permute-done((f32[864,128]{1,0:T(8,128)S(1)}, f32[864,128]{1,0:T(8,128)S(1)}, u32[]{:S(2)}, u32[]{:S(2)}) %collective-permute-start.18) | collective-permute-done | bytes 442400 | tf_op jit(solution)/shard_map/ppermute | solution.py:804
  109.2 6.8 %second.1 = (f32[16,256,128]{2,1,0:T(8,128)S(1)}, f32[64,128]{1,0:T(8,128)S(1)}, f32[64,128]{1,0:T(8,128)S(1)}) custom-call(f32[16,256,128]{2,1,0:T(8,128)S(1)} %base.1.base_ref, f32[768,128]{1,0:T(8,128)} %collective-permute-done.12.low_one_ref, f32[768,128]{1,0:T(8,128)} %collective-permute-done.13.high_one_ref, ...), custom_call_target="tpu_custom_call" | custom-call | flops 134217728 | bytes 8388608 | tf_op jit(solution)/shard_map/second/pallas_call | solution.py:681
  118.4 2.9 %collective-permute-done.21 = f32[64,128]{1,0:T(8,128)S(1)} collective-permute-done((f32[64,128]{1,0:T(8,128)S(1)}, f32[64,128]{1,0:T(8,128)S(1)}, u32[]{:S(2)}, u32[]{:S(2)}) %collective-permute-start.21) | collective-permute-done | bytes 32800 | tf_op jit(solution)/shard_map/ppermute | solution.py:860
  121.3 5.1 %collective-permute-done.22 = f32[64,128]{1,0:T(8,128)S(1)} collective-permute-done((f32[64,128]{1,0:T(8,128)S(1)}, f32[64,128]{1,0:T(8,128)S(1)}, u32[]{:S(2)}, u32[]{:S(2)}) %collective-permute-start.22) | collective-permute-done | bytes 32800 | tf_op jit(solution)/shard_map/ppermute | solution.py:860
  126.4 3.9 %collective-permute-done.23 = f32[64,128]{1,0:T(8,128)S(1)} collective-permute-done((f32[64,128]{1,0:T(8,128)S(1)}, f32[64,128]{1,0:T(8,128)S(1)}, u32[]{:S(2)}, u32[]{:S(2)}) %collective-permute-start.23) | collective-permute-done | bytes 32800 | tf_op jit(solution)/shard_map/ppermute | solution.py:860
  130.3 2.5 %collective-permute-start.24 = (f32[64,128]{1,0:T(8,128)S(1)}, f32[64,128]{1,0:T(8,128)S(1)}, u32[]{:S(2)}, u32[]{:S(2)}) collective-permute-start(f32[64,128]{1,0:T(8,128)S(1)} %add.38), channel_id=1, source_target_pairs={{0,3},{1,2},{2,1},{3,0},{4,7},{5,6},{6,5},{7,4},{8,11},{9,10},{10,... | collective-permute-start | bytes 98312 | tf_op jit(solution)/shard_map/ppermute | solution.py:860
  132.8 2.6 %collective-permute-done.24 = f32[64,128]{1,0:T(8,128)S(1)} collective-permute-done((f32[64,128]{1,0:T(8,128)S(1)}, f32[64,128]{1,0:T(8,128)S(1)}, u32[]{:S(2)}, u32[]{:S(2)}) %collective-permute-start.24) | collective-permute-done | bytes 32800 | tf_op jit(solution)/shard_map/ppermute | solution.py:860
  136.3 3.1 %collective-permute-done.25 = f32[64,128]{1,0:T(8,128)S(1)} collective-permute-done((f32[64,128]{1,0:T(8,128)S(1)}, f32[64,128]{1,0:T(8,128)S(1)}, u32[]{:S(2)}, u32[]{:S(2)}) %collective-permute-start.25) | collective-permute-done | bytes 32800 | tf_op jit(solution)/shard_map/ppermute | solution.py:860
  139.4 2.3 %collective-permute-start.26 = (f32[64,128]{1,0:T(8,128)S(1)}, f32[64,128]{1,0:T(8,128)S(1)}, u32[]{:S(2)}, u32[]{:S(2)}) collective-permute-start(f32[64,128]{1,0:T(8,128)S(1)} %add.40), channel_id=1, source_target_pairs={{0,24},{1,25},{2,26},{3,27},{4,28},{5,29},{6,30},{7,31},{8,16},{9,... | collective-permute-start | bytes 98312 | tf_op jit(solution)/shard_map/ppermute | solution.py:860
  141.7 2.8 %collective-permute-done.26 = f32[64,128]{1,0:T(8,128)S(1)} collective-permute-done((f32[64,128]{1,0:T(8,128)S(1)}, f32[64,128]{1,0:T(8,128)S(1)}, u32[]{:S(2)}, u32[]{:S(2)}) %collective-permute-start.26) | collective-permute-done | bytes 32800 | tf_op jit(solution)/shard_map/ppermute | solution.py:860
  145.7 16.9 %turn.1 = f32[16,256,128]{2,1,0:T(8,128)} custom-call(f32[16,256,128]{2,1,0:T(8,128)S(1)} %get-tuple-element.74.second_ref, f32[64,128]{1,0:T(8,128)S(1)} %add.41.own_ref, f32[64,128]{1,0:T(8,128)S(1)} %collective-permute-done.27.other_ref, s32[1]{0:T(128)} %bitcast.10.rest_3_.upper_ref), custom_call_target="tpu_custom_call" | custom-call | flops 268435456 | bytes 4194304 | tf_op jit(solution)/shard_map/turn/pallas_call | solution.py:781
  (112 shorter events, 28.4 us)
Async XLA Ops:
  0.0 28.0 %collective-permute-start.5 = (f32[16,256,128]{2,1,0:T(8,128)}, f32[16,256,128]{2,1,0:T(8,128)}, u32[]{:S(2)}, u32[]{:S(2)}) collective-permute-start(f32[16,256,128]{2,1,0:T(8,128)} %bitcast.12), channel_id=1, source_target_pairs={{0,64},{1,65},{2,66},{3,67},{4,68},{5,69},{6,70},{7,71},{8,72},{9,... | collective-permute-start | bytes 6291464 | tf_op jit(solution)/shard_map/ppermute | solution.py:804
  1.6 15.2 %copy-start.25 = (f32[16,16,16]{2,1,0:T(8,128)S(1)}, f32[16,16,16]{2,1,0:T(8,128)}, u32[]{:S(2)}) copy-start(f32[16,16,16]{2,1,0:T(8,128)} %param.6) | copy-start | bytes 49156
  1.6 25.1 %copy-start.1 = (f32[16,16,16,128]{3,2,1,0:T(8,128)S(1)}, f32[16,16,16,128]{3,2,1,0:T(8,128)}, u32[]{:S(2)}) copy-start(f32[16,16,16,128]{3,2,1,0:T(8,128)} %param.5) | copy-start | bytes 6291460
  5.9 38.7 %collective-permute-start.4 = (f32[8,192,128]{2,1,0:T(8,128)}, f32[8,192,128]{2,1,0:T(8,128)S(1)}, u32[]{:S(2)}, u32[]{:S(2)}) collective-permute-start(f32[8,192,128]{2,1,0:T(8,128)} %get-tuple-element.46), channel_id=1, source_target_pairs={{0,32},{1,33},{2,34},{3,35},{4,36},{5,37},{6,38},{7,39},{8,40},{9,... | collective-permute-start | bytes 2359304 | tf_op jit(solution)/shard_map/ppermute | solution.py:804
  8.4 10.0 %collective-permute-start = (f32[24,128]{1,0:T(8,128)S(1)}, f32[24,128]{1,0:T(8,128)S(1)}, u32[]{:S(2)}, u32[]{:S(2)}) collective-permute-start(f32[24,128]{1,0:T(8,128)S(1)} %reshape.36.refs_1_), channel_id=1, source_target_pairs={{0,1},{1,2},{2,3},{3,4},{4,5},{5,6},{6,7},{7,8},{8,9},{9,10},{10,1... | collective-permute-start | bytes 36872 | tf_op jit(solution)/shard_map/ppermute | solution.py:804
  10.0 8.4 %collective-permute-start.1 = (f32[24,128]{1,0:T(8,128)S(1)}, f32[24,128]{1,0:T(8,128)S(1)}, u32[]{:S(2)}, u32[]{:S(2)}) collective-permute-start(f32[24,128]{1,0:T(8,128)S(1)} %reshape.36.refs_1_), channel_id=1, source_target_pairs={{0,31},{1,0},{2,1},{3,2},{4,3},{5,4},{6,5},{7,6},{8,7},{9,8},{10,9... | collective-permute-start | bytes 36872 | tf_op jit(solution)/shard_map/ppermute | solution.py:804
  18.4 26.2 %collective-permute-start.3 = (f32[104,128]{1,0:T(8,128)S(1)}, f32[104,128]{1,0:T(8,128)S(1)}, u32[]{:S(2)}, u32[]{:S(2)}) collective-permute-start(f32[104,128]{1,0:T(8,128)S(1)} %stack.13.parcel_ref.refs_0_), channel_id=1, source_target_pairs={{0,32},{1,33},{2,34},{3,35},{4,36},{5,37},{6,38},{7,39},{8,40},{9,... | collective-permute-start | bytes 159752 | tf_op jit(solution)/shard_map/ppermute | solution.py:804
  18.5 32.4 %collective-permute-start.7 = (f32[6,16,16,128]{3,2,1,0:T(8,128)}, f32[6,16,16,128]{3,2,1,0:T(8,128)S(1)}, u32[]{:S(2)}, u32[]{:S(2)}) collective-permute-start(f32[6,16,16,128]{3,2,1,0:T(8,128)} %copy-done.21), channel_id=1, source_target_pairs={{0,1},{1,2},{2,3},{3,4},{4,5},{5,6},{6,7},{7,8},{8,9},{9,10},{10,1... | collective-permute-start | bytes 2359304 | tf_op jit(solution)/shard_map/ppermute | solution.py:804
  18.6 32.3 %collective-permute-start.8 = (f32[6,16,16,128]{3,2,1,0:T(8,128)}, f32[6,16,16,128]{3,2,1,0:T(8,128)S(1)}, u32[]{:S(2)}, u32[]{:S(2)}) collective-permute-start(f32[6,16,16,128]{3,2,1,0:T(8,128)} %copy-done.20), channel_id=1, source_target_pairs={{0,31},{1,0},{2,1},{3,2},{4,3},{5,4},{6,5},{7,6},{8,7},{9,8},{10,9... | collective-permute-start | bytes 2359304 | tf_op jit(solution)/shard_map/ppermute | solution.py:804
  45.5 14.3 %collective-permute-start.9 = (f32[6,192,128]{2,1,0:T(8,128)S(1)}, f32[6,192,128]{2,1,0:T(8,128)}, u32[]{:S(2)}, u32[]{:S(2)}) collective-permute-start(f32[6,192,128]{2,1,0:T(8,128)S(1)} %get-tuple-element.56), channel_id=1, source_target_pairs={{0,33},{3,34},{4,37},{7,38},{8,41},{11,42},{12,45},{15,46},{16,49}... | collective-permute-start | bytes 1769480 | tf_op jit(solution)/shard_map/ppermute | solution.py:830
  47.7 39.7 %collective-permute-start.15 = (f32[1536,128]{1,0:T(8,128)}, f32[1536,128]{1,0:T(8,128)S(1)}, u32[]{:S(2)}, u32[]{:S(2)}) collective-permute-start(f32[1536,128]{1,0:T(8,128)} %get-tuple-element.61), channel_id=1, source_target_pairs={{0,32},{1,33},{2,34},{3,35},{4,36},{5,37},{6,38},{7,39},{8,40},{9,... | collective-permute-start | bytes 2359304 | tf_op jit(solution)/shard_map/ppermute | solution.py:804
  49.4 8.9 %collective-permute-start.6 = (f32[104,128]{1,0:T(8,128)S(1)}, f32[104,128]{1,0:T(8,128)S(1)}, u32[]{:S(2)}, u32[]{:S(2)}) collective-permute-start(f32[104,128]{1,0:T(8,128)S(1)} %collective-permute-done.3.refs_2_.parcel_ref), channel_id=1, source_target_pairs={{0,64},{1,65},{2,66},{3,67},{4,68},{5,69},{6,70},{7,71},{8,72},{9,... | collective-permute-start | bytes 159752 | tf_op jit(solution)/shard_map/ppermute | solution.py:804
  59.8 27.7 %collective-permute-start.16 = (f32[6,192,128]{2,1,0:T(8,128)}, f32[6,192,128]{2,1,0:T(8,128)S(1)}, u32[]{:S(2)}, u32[]{:S(2)}) collective-permute-start(f32[6,192,128]{2,1,0:T(8,128)} %collective-permute-done.9), channel_id=1, source_target_pairs={{1,0},{2,3},{5,4},{6,7},{9,8},{10,11},{13,12},{14,15},{17,16},{18,... | collective-permute-start | bytes 1769480 | tf_op jit(solution)/shard_map/ppermute | solution.py:840
  61.0 23.1 %collective-permute-start.12 = (f32[768,128]{1,0:T(8,128)}, f32[768,128]{1,0:T(8,128)}, u32[]{:S(2)}, u32[]{:S(2)}) collective-permute-start(f32[768,128]{1,0:T(8,128)} %get-tuple-element.55), channel_id=1, source_target_pairs={{0,1},{1,2},{2,3},{3,4},{4,5},{5,6},{6,7},{7,8},{8,9},{9,10},{10,1... | collective-permute-start | bytes 1179656 | tf_op jit(solution)/shard_map/ppermute | solution.py:804
  64.8 21.2 %collective-permute-start.13 = (f32[768,128]{1,0:T(8,128)}, f32[768,128]{1,0:T(8,128)}, u32[]{:S(2)}, u32[]{:S(2)}) collective-permute-start(f32[768,128]{1,0:T(8,128)} %get-tuple-element.54), channel_id=1, source_target_pairs={{0,31},{1,0},{2,1},{3,2},{4,3},{5,4},{6,5},{7,6},{8,7},{9,8},{10,9... | collective-permute-start | bytes 1179656 | tf_op jit(solution)/shard_map/ppermute | solution.py:804
  69.4 1.2 collective-permute-start.2
  73.8 13.6 %copy-start.6 = (f32[16,256,128]{2,1,0:T(8,128)S(1)}, f32[16,256,128]{2,1,0:T(8,128)}, u32[]{:S(2)}) copy-start(f32[16,256,128]{2,1,0:T(8,128)} %copy-done.5) | copy-start | bytes 6291460
  73.8 13.6 %copy-start.8 = (f32[16,256,128]{2,1,0:T(8,128)S(1)}, f32[16,256,128]{2,1,0:T(8,128)}, u32[]{:S(2)}) copy-start(f32[16,256,128]{2,1,0:T(8,128)} %copy-done.7) | copy-start | bytes 6291460
  81.6 1.3 collective-permute-start.10
  83.0 4.4 %collective-permute-start.11 = (f32[3,48,128]{2,1,0:T(8,128)S(1)}, f32[3,48,128]{2,1,0:T(8,128)S(1)}, u32[]{:S(2)}, u32[]{:S(2)}) collective-permute-start(f32[3,48,128]{2,1,0:T(8,128)S(1)} %add.34.part_ref.rest_0_), channel_id=1, source_target_pairs={{0,32},{1,33},{2,34},{3,35},{4,36},{5,37},{6,38},{7,39},{8,40},{9,... | collective-permute-start | bytes 221192 | tf_op jit(solution)/shard_map/ppermute | solution.py:804
  90.1 9.5 %collective-permute-start.17 = (f32[16,256,128]{2,1,0:T(8,128)S(1)}, f32[16,256,128]{2,1,0:T(8,128)S(1)}, u32[]{:S(2)}, u32[]{:S(2)}) collective-permute-start(f32[16,256,128]{2,1,0:T(8,128)S(1)} %get-tuple-element.66.s_ref), channel_id=1, source_target_pairs={{0,64},{1,65},{2,66},{3,67},{4,68},{5,69},{6,70},{7,71},{8,72},{9,... | collective-permute-start | bytes 6291464 | tf_op jit(solution)/shard_map/ppermute | solution.py:804
  90.2 12.3 %collective-permute-start.14 = (f32[16,64,128]{2,1,0:T(8,128)S(1)}, f32[16,64,128]{2,1,0:T(8,128)S(1)}, u32[]{:S(2)}, u32[]{:S(2)}) collective-permute-start(f32[16,64,128]{2,1,0:T(8,128)S(1)} %copy-done.23), channel_id=1, source_target_pairs={{1,33},{2,34},{5,37},{6,38},{9,41},{10,42},{13,45},{14,46},{17,49}... | collective-permute-start | bytes 1572872 | tf_op jit(solution)/shard_map/ppermute | solution.py:851
  90.9 18.3 %collective-permute-start.18 = (f32[864,128]{1,0:T(8,128)S(1)}, f32[864,128]{1,0:T(8,128)S(1)}, u32[]{:S(2)}, u32[]{:S(2)}) collective-permute-start(f32[864,128]{1,0:T(8,128)S(1)} %get-tuple-element.69), channel_id=1, source_target_pairs={{0,1},{1,2},{2,3},{3,4},{4,5},{5,6},{6,7},{7,8},{8,9},{9,10},{10,1... | collective-permute-start | bytes 1327112 | tf_op jit(solution)/shard_map/ppermute | solution.py:804
  91.0 18.2 %collective-permute-start.19 = (f32[864,128]{1,0:T(8,128)S(1)}, f32[864,128]{1,0:T(8,128)S(1)}, u32[]{:S(2)}, u32[]{:S(2)}) collective-permute-start(f32[864,128]{1,0:T(8,128)S(1)} %get-tuple-element.70), channel_id=1, source_target_pairs={{0,31},{1,0},{2,1},{3,2},{4,3},{5,4},{6,5},{7,6},{8,7},{9,8},{10,9... | collective-permute-start | bytes 1327112 | tf_op jit(solution)/shard_map/ppermute | solution.py:804
  116.0 1.3 collective-permute-start.20
  117.3 3.9 %collective-permute-start.21 = (f32[64,128]{1,0:T(8,128)S(1)}, f32[64,128]{1,0:T(8,128)S(1)}, u32[]{:S(2)}, u32[]{:S(2)}) collective-permute-start(f32[64,128]{1,0:T(8,128)S(1)} %add.35), channel_id=1, source_target_pairs={{0,32},{1,33},{2,34},{3,35},{4,36},{5,37},{6,38},{7,39},{8,40},{9,... | collective-permute-start | bytes 98312 | tf_op jit(solution)/shard_map/ppermute | solution.py:860
  121.3 5.1 %collective-permute-start.22 = (f32[64,128]{1,0:T(8,128)S(1)}, f32[64,128]{1,0:T(8,128)S(1)}, u32[]{:S(2)}, u32[]{:S(2)}) collective-permute-start(f32[64,128]{1,0:T(8,128)S(1)} %add.36), channel_id=1, source_target_pairs={{0,36},{1,37},{2,38},{3,39},{4,32},{5,33},{6,34},{7,35},{8,44},{9,... | collective-permute-start | bytes 98312 | tf_op jit(solution)/shard_map/ppermute | solution.py:860
  126.4 3.9 %collective-permute-start.23 = (f32[64,128]{1,0:T(8,128)S(1)}, f32[64,128]{1,0:T(8,128)S(1)}, u32[]{:S(2)}, u32[]{:S(2)}) collective-permute-start(f32[64,128]{1,0:T(8,128)S(1)} %add.37), channel_id=1, source_target_pairs={{0,1},{1,0},{2,3},{3,2},{4,5},{5,4},{6,7},{7,6},{8,9},{9,8},{10,11... | collective-permute-start | bytes 98312 | tf_op jit(solution)/shard_map/ppermute | solution.py:860
  130.3 5.1 %collective-permute-start.24 = (f32[64,128]{1,0:T(8,128)S(1)}, f32[64,128]{1,0:T(8,128)S(1)}, u32[]{:S(2)}, u32[]{:S(2)}) collective-permute-start(f32[64,128]{1,0:T(8,128)S(1)} %add.38), channel_id=1, source_target_pairs={{0,3},{1,2},{2,1},{3,0},{4,7},{5,6},{6,5},{7,4},{8,11},{9,10},{10,... | collective-permute-start | bytes 98312 | tf_op jit(solution)/shard_map/ppermute | solution.py:860
  135.4 3.9 %collective-permute-start.25 = (f32[64,128]{1,0:T(8,128)S(1)}, f32[64,128]{1,0:T(8,128)S(1)}, u32[]{:S(2)}, u32[]{:S(2)}) collective-permute-start(f32[64,128]{1,0:T(8,128)S(1)} %add.39), channel_id=1, source_target_pairs={{0,8},{1,9},{2,10},{3,11},{4,12},{5,13},{6,14},{7,15},{8,0},{9,1},... | collective-permute-start | bytes 98312 | tf_op jit(solution)/shard_map/ppermute | solution.py:860
  139.4 5.1 %collective-permute-start.26 = (f32[64,128]{1,0:T(8,128)S(1)}, f32[64,128]{1,0:T(8,128)S(1)}, u32[]{:S(2)}, u32[]{:S(2)}) collective-permute-start(f32[64,128]{1,0:T(8,128)S(1)} %add.40), channel_id=1, source_target_pairs={{0,24},{1,25},{2,26},{3,27},{4,28},{5,29},{6,30},{7,31},{8,16},{9,... | collective-permute-start | bytes 98312 | tf_op jit(solution)/shard_map/ppermute | solution.py:860
  144.5 1.2 collective-permute-start.27
  (24 other events, 64.5 us)

commit v10 on v9

--- a/solution.py
+++ b/solution.py
@@ -210,16 +210,16 @@
     return message, relay, mid
 
 
-def stack_kernel(*refs):
-    start = 0
-    for ref in refs[:-1]:
-        refs[-1][start : start + ref.shape[0], :] = ref[...]
-        start += ref.shape[0]
-
-
-def stack(*arrays):
-    rows = sum(a.shape[0] for a in arrays)
-    return pl.pallas_call(stack_kernel, out_shape=sds((rows, S)), compiler_params=params(4), name="stack")(*arrays)
+def stack(*pieces):
+    def kernel(*refs):
+        start = 0
+        for ref, (_, rows) in zip(refs, pieces):
+            refs[-1][start : start + rows, :] = ref[:rows, :]
+            start += rows
+
+    arrays = [array for array, _ in pieces]
+    rows = sum(rows for _, rows in pieces)
+    return pl.pallas_call(kernel, out_shape=sds((rows, S)), compiler_params=params(4), name="stack")(*arrays)
 
 
 def along_x(s_ref, mate_ref, out_ref, add):
@@ -327,7 +327,7 @@
 
 def spread_kernel(parcel_ref, vb_ref):
     def spread_row(row, _):
-        line = (parcel_ref[pl.ds(72 + row, 1), :] + (DIAGONAL - filter_centre)) * (1.0 / filter_half)
+        line = (parcel_ref[pl.ds(24 + row, 1), :] + (DIAGONAL - filter_centre)) * (1.0 / filter_half)
         start = pl.multiple_of(row * 128, 128)
         vb_ref[pl.ds(start, 128), :] = jnp.broadcast_to(line, (128, 128)).T
         return 0
@@ -346,15 +346,17 @@
 
 
 def prep_kernel(*refs):
-    parcels = refs[:4]
-    corner_ref, vb_ref, s_ref, gg_ref, coef_ref, energy_ref, near_ref, table_ref, a1_ref, a1z_ref, a2_ref, a2s_ref = refs[4:]
+    own_ref, other_ref, corner_ref, vb_ref, s_ref, gg_ref, coef_ref, energy_ref, near_ref, table_ref = refs[:10]
+    a1_ref, a1z_ref, a2_ref, a2s_ref = refs[10:]
     upper_x, upper_y = corner_ref[0] > 0, corner_ref[1] > 0
     for slab in range(3):
-        own, over_x, over_y, over_xy = [parcel[slab * 24 : slab * 24 + 24, :] for parcel in parcels]
-        same_x = [jnp.where(upper_y, over_y, own), jnp.where(upper_y, own, over_y)]
-        other_x = [jnp.where(upper_y, over_xy, over_x), jnp.where(upper_y, over_x, over_xy)]
-        ordered = [jnp.where(upper_x, o, m) for m, o in zip(same_x, other_x)]
-        ordered += [jnp.where(upper_x, m, o) for m, o in zip(same_x, other_x)]
+        own = [own_ref[slab * 48 + j * 24 : slab * 48 + j * 24 + 24, :] for j in range(2)]
+        other = [other_ref[slab * 48 + j * 24 : slab * 48 + j * 24 + 24, :] for j in range(2)]
+        lower = [jnp.where(upper_x, o, m) for m, o in zip(own, other)]
+        higher = [jnp.where(upper_x, m, o) for m, o in zip(own, other)]
+        ordered = []
+        for pair in (lower, higher):
+            ordered += [jnp.where(upper_y, pair[1], pair[0]), jnp.where(upper_y, pair[0], pair[1])]
         for j in range(4):
             near_ref[slab * 96 + j * 24 : slab * 96 + j * 24 + 24, :] = ordered[j]
     blank = jnp.zeros((16, 128), F32)
@@ -459,7 +461,7 @@
     vmem = pl.BlockSpec(memory_space=pltpu.VMEM)
     return pl.pallas_call(
         prep_kernel,
-        in_specs=[vmem] * 4 + [pl.BlockSpec(memory_space=pltpu.SMEM), vmem, vmem],
+        in_specs=[vmem] * 2 + [pl.BlockSpec(memory_space=pltpu.SMEM), vmem, vmem],
         out_shape=[sds((2, CELLS, S), BF16), sds((3, NEAR, S)), sds((NEAR, S))],
         scratch_shapes=[
             pltpu.VMEM((288, 128), F32),
@@ -808,37 +810,37 @@
     outer_ones = [d for d in range(count) if d % 4 in (0, 3)]
     inner = ((lax.axis_index("gzs") + 1) // 2 % 2).astype(jnp.int32).reshape(1)
     s = states.reshape(C, ROWS, S)
+    mate = send(s, over_x)
     pot = potential.reshape(32, 128)
-
+    corner = jnp.stack([gx * C, gy * C]).astype(jnp.int32)
+    upper = gx.astype(jnp.int32).reshape(1)
     atoms = jnp.concatenate(
         [projectors.reshape(4, TAPS), atom_sites.astype(F32), energies[:, None], jnp.zeros((4, 768 - TAPS - 4), F32)],
         axis=1,
     ).reshape(24, 128)
-    mate = send(s, over_x)
-    below, above = send(atoms, 0, 1), send(atoms, 0, -1)
-    one_edge, head, tail = pack(s)
+    to_pack, pot, corner, upper, inner, atoms = barrier((s, pot, corner, upper, inner, atoms))
+
+    parcel = stack((atoms, 24), (pot, 32))
+    parcel_mate = send(parcel, over_y)
+    one_edge, head, tail = pack(to_pack)
     one_edge = send(one_edge, over_y)
-    head, tail, below, above = barrier((head, tail, below, above))
-    parcel = stack(below, atoms, above, pot)
-    parcel_y = send(parcel, over_y)
-    parcel_x = send(parcel, over_x)
-    low, high = send(tail, 0, 1), send(head, 0, -1)
+    pair = stack((parcel, 24), (parcel_mate, 24))
+    column = stack((send(pair, 0, 1), 48), (pair, 48), (send(pair, 0, -1), 48))
+    column_mate = send(column, over_x)
     message, relay, mid = pack_rest(s, inner)
     vb = spread(parcel)
     beside = side_x(s, mate)
-    parcel_y, one_edge, message, relay, beside = barrier((parcel_y, one_edge, message, relay, beside))
+    column_mate, head, tail, message, relay, beside = barrier((column_mate, head, tail, message, relay, beside))
+    low, high = send(tail, 0, 1), send(head, 0, -1)
     relayed = lax.ppermute(relay, AXES, [(d, d ^ over_y ^ 1) for d in outer_ones])
     message = send(message, over_y)
-    parcel_xy = send(parcel_y, over_x)
-    corner = jnp.stack([gx * C, gy * C]).astype(jnp.int32)
-    upper = gx.astype(jnp.int32).reshape(1)
+    gg, part, energy = prep([column, column_mate], corner, vb, s)
+    part, relayed, one_edge = barrier((part, relayed, one_edge))
+    relayed = lax.ppermute(relayed, AXES, [(d, d ^ 1) for d in inner_ones])
     planes = vb.reshape(C, ROWS, S)
     side_part = side_z(s, beside, low, high)
     q, mix, head, tail = first_half(s, side_part, planes, one_edge)
     low_one, high_one = send(tail, 0, 1), send(head, 0, -1)
-    parcel_xy, head, tail, relayed = barrier((parcel_xy, head, tail, relayed))
-    relayed = lax.ppermute(relayed, AXES, [(d, d ^ 1) for d in inner_ones])
-    gg, part, energy = prep([parcel, parcel_x, parcel_y, parcel_xy], corner, vb, s)
 
     part = part + send(part, over_x)
     part_mate = send(part, over_y)
@@ -849,7 +851,7 @@
     mate = send(mix, over_x)
     mid, part_mate = barrier((mid, part_mate))
     mid = lax.ppermute(mid, AXES, [(d, d ^ over_y) for d in inner_ones])
-    planes_mate = spread(parcel_y).reshape(C, ROWS, S)
+    planes_mate = spread(parcel_mate).reshape(C, ROWS, S)
     part_two = side_again(mix, mate)
     base = make_base(s, mid, planes, planes_mate, q, side_part, part_two, [one_edge, message, relayed], inner)
     gg = gg.reshape(2, C, ROWS, S)

time: 164 us -> 158 us (0.963)
  waiting for transfers between devices: 46.2 us -> 62.9 us
  local copies, waits for them, and re-layouts: 15.1 us -> 4.53 us
  Pallas kernels: 51.8 us -> 45.3 us
  starting transfers between devices: 48.9 us -> 42.4 us
    unnamed x57 -> x5, local copies, waits for them, and re-layouts: 14.7 us -> 2.54 us
    ppermute x19 -> x18, waiting for transfers between devices: 25 us -> 36.9 us  [send(): return lax.ppermute(value, AXES, [(d, target(d)) for d in range(count)])]
    ppermute x6, starting transfers between devices: 6.68 us -> 3.01 us  [per_device(): own = own + lax.ppermute(own, AXES, [(d, d ^ flip) for d in range(count)])]
    ppermute x6, waiting for transfers between devices: 20.4 us -> 24.1 us  [per_device(): own = own + lax.ppermute(own, AXES, [(d, d ^ flip) for d in range(count)])]
    ppermute x19 -> x18, starting transfers between devices: 38.1 us -> 36.1 us  [send(): return lax.ppermute(value, AXES, [(d, target(d)) for d in range(count)])]
    pallas_call x1, Pallas kernels: 2.56 us -> 0.77 us  [pack(): pl.pallas_call(pack_kernel, grid=(C // N,), in_specs=[plane_spec(ROWS, N)...]
    pallas_call x1, Pallas kernels: 3.24 us -> 1.47 us  [side_x(): pl.pallas_call(side_x_kernel, out_shape=FULL, compiler_params=params(12),...]
    pallas_call x2 -> x4, Pallas kernels: 7.79 us -> 7.82 us  [the longest x1 7.81 us: prep(): pl.pallas_call(prep_kernel, in_specs=[vmem] * 2 + [pl.BlockSpec(memory_sp...]
  transfers between devices with their start and end apart: 28 -> 27, of which waited for: 16 -> 15; matrix products, arithmetic and copies ran while one was open for 0% -> 2% of each run, Pallas kernels for 17% -> 14%
where the time goes in v10:
time: 158 us; the launch traced here: 156 us
  waiting for transfers between devices  62.9 us (40%)
  Pallas kernels  45.3 us (29%)
  starting transfers between devices  42.4 us (27%)
  local copies, waits for them, and re-layouts  4.53 us (3%)
    ppermute x18, waiting for transfers between devices, send(): return lax.ppermute(value, AXES, [(d, target(d)) for d in range(count)])  36.9 us
    ppermute x18, starting transfers between devices, send(): return lax.ppermute(value, AXES, [(d, target(d)) for d in range(count)])  36.1 us
    ppermute x6, waiting for transfers between devices, per_device(): own = own + lax.ppermute(own, AXES, [(d, d ^ flip) for d in range(count)])  24.1 us
    pallas_call x1, Pallas kernels, turn(): pl.pallas_call(turn_kernel, grid=(STEPS,), in_specs=[plane_spec(), whole(...  16.9 us
    pallas_call x1, Pallas kernels, prep(): pl.pallas_call(prep_kernel, in_specs=[vmem] * 2 + [pl.BlockSpec(memory_sp...  7.81 us
    pallas_call x1, Pallas kernels, make_second(): pl.pallas_call(second_kernel, grid=(STEPS,), in_specs=[plane_spec()] + [w...  5.66 us
  transfers between devices with their start and end apart: 27, of which 15 were waited for; matrix products, arithmetic and copies ran while one was open for 2% of the time, Pallas kernels for 14%

profile of v10, /device:TPU:0, one launch (start us, length us, event | category | flops | bytes accessed | tf_op | source)
XLA Modules:
  0.0 156.4 jit_solution(18422537705320537641)
XLA Ops:
  3.8 2.0 %collective-permute-start = (f32[56,128]{1,0:T(8,128)S(1)}, f32[56,128]{1,0:T(8,128)S(1)}, u32[]{:S(2)}, u32[]{:S(2)}) collective-permute-start(f32[56,128]{1,0:T(8,128)S(1)} %stack.15.refs_0_.parcel_ref), channel_id=1, source_target_pairs={{0,32},{1,33},{2,34},{3,35},{4,36},{5,37},{6,38},{7,39},{8,40},{9,... | collective-permute-start | bytes 86024 | tf_op jit(solution)/shard_map/ppermute | solution.py:806
  5.8 2.0 %collective-permute-done.refs_1_.parcel_ref = f32[56,128]{1,0:T(8,128)S(1)} collective-permute-done((f32[56,128]{1,0:T(8,128)S(1)}, f32[56,128]{1,0:T(8,128)S(1)}, u32[]{:S(2)}, u32[]{:S(2)}) %collective-permute-start) | collective-permute-done | bytes 28704 | tf_op jit(solution)/shard_map/ppermute | solution.py:806
  7.8 1.5 collective-permute-start.1
  9.3 7.0 %collective-permute-start.2 = (f32[48,128]{1,0:T(8,128)S(1)}, f32[48,128]{1,0:T(8,128)S(1)}, u32[]{:S(2)}, u32[]{:S(2)}) collective-permute-start(f32[48,128]{1,0:T(8,128)S(1)} %stack.16.refs_1_), channel_id=1, source_target_pairs={{0,31},{1,0},{2,1},{3,2},{4,3},{5,4},{6,5},{7,6},{8,7},{9,8},{10,9... | collective-permute-start | bytes 73736 | tf_op jit(solution)/shard_map/ppermute | solution.py:806
  16.3 1.6 %copy-done = f32[16,16,16,128]{3,2,1,0:T(8,128)S(1)} copy-done((f32[16,16,16,128]{3,2,1,0:T(8,128)S(1)}, f32[16,16,16,128]{3,2,1,0:T(8,128)}, u32[]{:S(2)}) %copy-start) | copy-done | bytes 2097176
  20.3 1.5 side_x.1.part_ref
  21.8 6.0 %collective-permute-start.10 = (f32[6,16,16,128]{3,2,1,0:T(8,128)S(1)}, f32[6,16,16,128]{3,2,1,0:T(8,128)S(1)}, u32[]{:S(2)}, u32[]{:S(2)}) collective-permute-start(f32[6,16,16,128]{3,2,1,0:T(8,128)S(1)} %get-tuple-element.62), channel_id=1, source_target_pairs={{0,31},{1,0},{2,1},{3,2},{4,3},{5,4},{6,5},{7,6},{8,7},{9,8},{10,9... | collective-permute-start | bytes 2359304 | tf_op jit(solution)/shard_map/ppermute | solution.py:806
  27.9 1.3 collective-permute-start.5
  31.3 7.8 %prep.1 = (bf16[2,4096,128]{2,1,0:T(8,128)(2,1)S(1)}, f32[3,48,128]{2,1,0:T(8,128)S(1)}, f32[48,128]{1,0:T(8,128)S(1)}) custom-call(f32[144,128]{1,0:T(8,128)S(1)} %stack.17.refs_0_, f32[144,128]{1,0:T(8,128)S(1)} %collective-permute-done.3.refs_1_, s32[2]{0:T(128)S(1)} %pad_add_fusion.refs_2_, f32[4096,128]{1,0:T(8,128)S(1)} %spread.2.refs_3_, ...), custom_call_target="tpu_custom_call" | custom-call | flops 134217728 | bytes 10485760 | tf_op jit(solution)/shard_map/prep/pallas_call | solution.py:462
  39.1 17.0 %collective-permute-done.6.edge_ref.refs_0_ = f32[8,192,128]{2,1,0:T(8,128)S(1)} collective-permute-done((f32[8,192,128]{2,1,0:T(8,128)S(1)}, f32[8,192,128]{2,1,0:T(8,128)S(1)}, u32[]{:S(2)}, u32[]{:S(2)}) %collective-permute-start.6) | collective-permute-done | bytes 786464 | tf_op jit(solution)/shard_map/ppermute | solution.py:806
  56.1 1.9 %collective-permute-done.5 = f32[6,192,128]{2,1,0:T(8,128)S(1)} collective-permute-done((f32[6,192,128]{2,1,0:T(8,128)S(1)}, f32[6,192,128]{2,1,0:T(8,128)S(1)}, u32[]{:S(2)}, u32[]{:S(2)}) %collective-permute-start.5) | collective-permute-done | bytes 589856 | tf_op jit(solution)/shard_map/ppermute | solution.py:835
  58.0 1.3 collective-permute-start.15
  59.3 2.9 %side_z.1.side_ref = f32[16,256,128]{2,1,0:T(8,128)S(1)} custom-call(f32[16,256,128]{2,1,0:T(8,128)S(1)} %bitcast.17, f32[16,256,128]{2,1,0:T(8,128)S(1)} %side_x.1.part_ref, f32[6,16,16,128]{3,2,1,0:T(8,128)S(1)} %collective-permute-done.9.low_ref, f32[6,16,16,128]{3,2,1,0:T(8,128)S(1)} %collective-permute-done.10.high_ref), custom_call_target="tpu_custom_call" | custom-call | flops 16777216 | bytes 8388608 | tf_op jit(solution)/shard_map/side_z/pallas_call | solution.py:275
  63.2 3.2 %collective-permute-start.11 = (f32[768,128]{1,0:T(8,128)S(1)}, f32[768,128]{1,0:T(8,128)S(1)}, u32[]{:S(2)}, u32[]{:S(2)}) collective-permute-start(f32[768,128]{1,0:T(8,128)S(1)} %get-tuple-element.64), channel_id=1, source_target_pairs={{0,1},{1,2},{2,3},{3,4},{4,5},{5,6},{6,7},{7,8},{8,9},{9,10},{10,1... | collective-permute-start | bytes 1179656 | tf_op jit(solution)/shard_map/ppermute | solution.py:806
  66.4 4.6 %collective-permute-start.12 = (f32[768,128]{1,0:T(8,128)S(1)}, f32[768,128]{1,0:T(8,128)S(1)}, u32[]{:S(2)}, u32[]{:S(2)}) collective-permute-start(f32[768,128]{1,0:T(8,128)S(1)} %get-tuple-element.65), channel_id=1, source_target_pairs={{0,31},{1,0},{2,1},{3,2},{4,3},{5,4},{6,5},{7,6},{8,7},{9,8},{10,9... | collective-permute-start | bytes 1179656 | tf_op jit(solution)/shard_map/ppermute | solution.py:806
  71.0 1.3 collective-permute-done.7
  73.5 7.5 %collective-permute-done.8.mate_ref.rest_1_ = f32[3,48,128]{2,1,0:T(8,128)S(1)} collective-permute-done((f32[3,48,128]{2,1,0:T(8,128)S(1)}, f32[3,48,128]{2,1,0:T(8,128)S(1)}, u32[]{:S(2)}, u32[]{:S(2)}) %collective-permute-start.8) | collective-permute-done | bytes 73760 | tf_op jit(solution)/shard_map/ppermute | solution.py:806
  81.0 2.9 %collective-permute-done.12.high_one_ref = f32[768,128]{1,0:T(8,128)S(1)} collective-permute-done((f32[768,128]{1,0:T(8,128)S(1)}, f32[768,128]{1,0:T(8,128)S(1)}, u32[]{:S(2)}, u32[]{:S(2)}) %collective-permute-start.12) | collective-permute-done | bytes 393248 | tf_op jit(solution)/shard_map/ppermute | solution.py:806
  85.8 1.7 %collective-permute-start.17 = (f32[864,128]{1,0:T(8,128)S(1)}, f32[864,128]{1,0:T(8,128)S(1)}, u32[]{:S(2)}, u32[]{:S(2)}) collective-permute-start(f32[864,128]{1,0:T(8,128)S(1)} %get-tuple-element.76), channel_id=1, source_target_pairs={{0,1},{1,2},{2,3},{3,4},{4,5},{5,6},{6,7},{7,8},{8,9},{9,10},{10,1... | collective-permute-start | bytes 1327112 | tf_op jit(solution)/shard_map/ppermute | solution.py:806
  87.5 6.1 %collective-permute-start.18 = (f32[864,128]{1,0:T(8,128)S(1)}, f32[864,128]{1,0:T(8,128)S(1)}, u32[]{:S(2)}, u32[]{:S(2)}) collective-permute-start(f32[864,128]{1,0:T(8,128)S(1)} %get-tuple-element.77), channel_id=1, source_target_pairs={{0,31},{1,0},{2,1},{3,2},{4,3},{5,4},{6,5},{7,6},{8,7},{9,8},{10,9... | collective-permute-start | bytes 1327112 | tf_op jit(solution)/shard_map/ppermute | solution.py:806
  94.4 2.9 %side_again.1.part_ref = f32[16,256,128]{2,1,0:T(8,128)S(1)} custom-call(f32[16,256,128]{2,1,0:T(8,128)S(1)} %get-tuple-element.73.s_ref, f32[16,256,128]{2,1,0:T(8,128)S(1)} %collective-permute-done.16.mate_ref), custom_call_target="tpu_custom_call" | custom-call | flops 33554432 | bytes 6291456 | tf_op jit(solution)/shard_map/side_again/pallas_call | solution.py:302
  97.3 3.0 %base.1.base_ref = f32[16,256,128]{2,1,0:T(8,128)S(1)} custom-call(f32[16,256,128]{2,1,0:T(8,128)S(1)} %bitcast.20, f32[16,64,128]{2,1,0:T(8,128)S(1)} %collective-permute-done.13.mid_ref, f32[16,256,128]{2,1,0:T(8,128)S(1)} %bitcast.23, f32[16,256,128]{2,1,0:T(8,128)S(1)} %bitcast.26, f32[16,256,128]{2,1,0:T(8,128)S(1)} %get-tuple-element.72.q_ref, ...), custom_call_target="tpu_custom_call" | custom-call | flops 33554432 | bytes 16777216 | tf_op jit(solution)/shard_map/base/pallas_call | solution.py:602
  100.3 3.8 %collective-permute-done.17.low_ref = f32[864,128]{1,0:T(8,128)S(1)} collective-permute-done((f32[864,128]{1,0:T(8,128)S(1)}, f32[864,128]{1,0:T(8,128)S(1)}, u32[]{:S(2)}, u32[]{:S(2)}) %collective-permute-start.17) | collective-permute-done | bytes 442400 | tf_op jit(solution)/shard_map/ppermute | solution.py:806
  104.1 5.7 %second.1 = (f32[16,256,128]{2,1,0:T(8,128)S(1)}, f32[64,128]{1,0:T(8,128)S(1)}, f32[64,128]{1,0:T(8,128)S(1)}) custom-call(f32[16,256,128]{2,1,0:T(8,128)S(1)} %base.1.base_ref, f32[768,128]{1,0:T(8,128)S(1)} %collective-permute-done.11.low_one_ref, f32[768,128]{1,0:T(8,128)S(1)} %collective-permute-done.12.high_one_ref, ...), custom_call_target="tpu_custom_call" | custom-call | flops 134217728 | bytes 8388608 | tf_op jit(solution)/shard_map/second/pallas_call | solution.py:683
  112.0 3.0 %collective-permute-done.20 = f32[64,128]{1,0:T(8,128)S(1)} collective-permute-done((f32[64,128]{1,0:T(8,128)S(1)}, f32[64,128]{1,0:T(8,128)S(1)}, u32[]{:S(2)}, u32[]{:S(2)}) %collective-permute-start.20) | collective-permute-done | bytes 32800 | tf_op jit(solution)/shard_map/ppermute | solution.py:862
  115.0 5.1 %collective-permute-done.21 = f32[64,128]{1,0:T(8,128)S(1)} collective-permute-done((f32[64,128]{1,0:T(8,128)S(1)}, f32[64,128]{1,0:T(8,128)S(1)}, u32[]{:S(2)}, u32[]{:S(2)}) %collective-permute-start.21) | collective-permute-done | bytes 32800 | tf_op jit(solution)/shard_map/ppermute | solution.py:862
  120.1 3.9 %collective-permute-done.22 = f32[64,128]{1,0:T(8,128)S(1)} collective-permute-done((f32[64,128]{1,0:T(8,128)S(1)}, f32[64,128]{1,0:T(8,128)S(1)}, u32[]{:S(2)}, u32[]{:S(2)}) %collective-permute-start.22) | collective-permute-done | bytes 32800 | tf_op jit(solution)/shard_map/ppermute | solution.py:862
  124.1 5.1 %collective-permute-done.23 = f32[64,128]{1,0:T(8,128)S(1)} collective-permute-done((f32[64,128]{1,0:T(8,128)S(1)}, f32[64,128]{1,0:T(8,128)S(1)}, u32[]{:S(2)}, u32[]{:S(2)}) %collective-permute-start.23) | collective-permute-done | bytes 32800 | tf_op jit(solution)/shard_map/ppermute | solution.py:862
  129.2 3.9 %collective-permute-done.24 = f32[64,128]{1,0:T(8,128)S(1)} collective-permute-done((f32[64,128]{1,0:T(8,128)S(1)}, f32[64,128]{1,0:T(8,128)S(1)}, u32[]{:S(2)}, u32[]{:S(2)}) %collective-permute-start.24) | collective-permute-done | bytes 32800 | tf_op jit(solution)/shard_map/ppermute | solution.py:862
  133.1 2.1 %collective-permute-start.25 = (f32[64,128]{1,0:T(8,128)S(1)}, f32[64,128]{1,0:T(8,128)S(1)}, u32[]{:S(2)}, u32[]{:S(2)}) collective-permute-start(f32[64,128]{1,0:T(8,128)S(1)} %add.40), channel_id=1, source_target_pairs={{0,24},{1,25},{2,26},{3,27},{4,28},{5,29},{6,30},{7,31},{8,16},{9,... | collective-permute-start | bytes 98312 | tf_op jit(solution)/shard_map/ppermute | solution.py:862
  135.2 3.0 %collective-permute-done.25 = f32[64,128]{1,0:T(8,128)S(1)} collective-permute-done((f32[64,128]{1,0:T(8,128)S(1)}, f32[64,128]{1,0:T(8,128)S(1)}, u32[]{:S(2)}, u32[]{:S(2)}) %collective-permute-start.25) | collective-permute-done | bytes 32800 | tf_op jit(solution)/shard_map/ppermute | solution.py:862
  139.4 16.9 %turn.1 = f32[16,256,128]{2,1,0:T(8,128)} custom-call(f32[16,256,128]{2,1,0:T(8,128)S(1)} %get-tuple-element.82.second_ref, f32[64,128]{1,0:T(8,128)S(1)} %add.41.own_ref, f32[64,128]{1,0:T(8,128)S(1)} %collective-permute-done.26.other_ref, s32[1]{0:T(128)} %bitcast.3.rest_3_.upper_ref), custom_call_target="tpu_custom_call" | custom-call | flops 268435456 | bytes 4194304 | tf_op jit(solution)/shard_map/turn/pallas_call | solution.py:783
  (60 shorter events, 16.5 us)
Async XLA Ops:
  0.0 20.3 %collective-permute-start.4 = (f32[16,256,128]{2,1,0:T(8,128)}, f32[16,256,128]{2,1,0:T(8,128)S(1)}, u32[]{:S(2)}, u32[]{:S(2)}) collective-permute-start(f32[16,256,128]{2,1,0:T(8,128)} %bitcast.12), channel_id=1, source_target_pairs={{0,64},{1,65},{2,66},{3,67},{4,68},{5,69},{6,70},{7,71},{8,72},{9,... | collective-permute-start | bytes 6291464 | tf_op jit(solution)/shard_map/ppermute | solution.py:806
  3.8 4.0 %collective-permute-start = (f32[56,128]{1,0:T(8,128)S(1)}, f32[56,128]{1,0:T(8,128)S(1)}, u32[]{:S(2)}, u32[]{:S(2)}) collective-permute-start(f32[56,128]{1,0:T(8,128)S(1)} %stack.15.refs_0_.parcel_ref), channel_id=1, source_target_pairs={{0,32},{1,33},{2,34},{3,35},{4,36},{5,37},{6,38},{7,39},{8,40},{9,... | collective-permute-start | bytes 86024 | tf_op jit(solution)/shard_map/ppermute | solution.py:806
  7.8 12.1 %collective-permute-start.1 = (f32[48,128]{1,0:T(8,128)S(1)}, f32[48,128]{1,0:T(8,128)S(1)}, u32[]{:S(2)}, u32[]{:S(2)}) collective-permute-start(f32[48,128]{1,0:T(8,128)S(1)} %stack.16.refs_1_), channel_id=1, source_target_pairs={{0,1},{1,2},{2,3},{3,4},{4,5},{5,6},{6,7},{7,8},{8,9},{9,10},{10,1... | collective-permute-start | bytes 73736 | tf_op jit(solution)/shard_map/ppermute | solution.py:806
  9.3 10.6 %collective-permute-start.2 = (f32[48,128]{1,0:T(8,128)S(1)}, f32[48,128]{1,0:T(8,128)S(1)}, u32[]{:S(2)}, u32[]{:S(2)}) collective-permute-start(f32[48,128]{1,0:T(8,128)S(1)} %stack.16.refs_1_), channel_id=1, source_target_pairs={{0,31},{1,0},{2,1},{3,2},{4,3},{5,4},{6,5},{7,6},{8,7},{9,8},{10,9... | collective-permute-start | bytes 73736 | tf_op jit(solution)/shard_map/ppermute | solution.py:806
  16.3 1.6 %copy-start = (f32[16,16,16,128]{3,2,1,0:T(8,128)S(1)}, f32[16,16,16,128]{3,2,1,0:T(8,128)}, u32[]{:S(2)}) copy-start(f32[16,16,16,128]{3,2,1,0:T(8,128)} %param.5) | copy-start | bytes 6291460
  18.7 37.4 %collective-permute-start.6 = (f32[8,192,128]{2,1,0:T(8,128)S(1)}, f32[8,192,128]{2,1,0:T(8,128)S(1)}, u32[]{:S(2)}, u32[]{:S(2)}) collective-permute-start(f32[8,192,128]{2,1,0:T(8,128)S(1)} %get-tuple-element.58), channel_id=1, source_target_pairs={{0,32},{1,33},{2,34},{3,35},{4,36},{5,37},{6,38},{7,39},{8,40},{9,... | collective-permute-start | bytes 2359304 | tf_op jit(solution)/shard_map/ppermute | solution.py:806
  19.9 1.9 %collective-permute-start.3 = (f32[144,128]{1,0:T(8,128)S(1)}, f32[144,128]{1,0:T(8,128)S(1)}, u32[]{:S(2)}, u32[]{:S(2)}) collective-permute-start(f32[144,128]{1,0:T(8,128)S(1)} %stack.17.refs_0_), channel_id=1, source_target_pairs={{0,64},{1,65},{2,66},{3,67},{4,68},{5,69},{6,70},{7,71},{8,72},{9,... | collective-permute-start | bytes 221192 | tf_op jit(solution)/shard_map/ppermute | solution.py:806
  21.8 9.4 %copy-start.1 = (f32[16,16,16,128]{3,2,1,0:T(8,128)S(1)}, f32[16,16,16,128]{3,2,1,0:T(8,128)}, u32[]{:S(2)}) copy-start(f32[16,16,16,128]{3,2,1,0:T(8,128)} %param.5) | copy-start | bytes 6291460
  21.8 37.5 %collective-permute-start.10 = (f32[6,16,16,128]{3,2,1,0:T(8,128)S(1)}, f32[6,16,16,128]{3,2,1,0:T(8,128)S(1)}, u32[]{:S(2)}, u32[]{:S(2)}) collective-permute-start(f32[6,16,16,128]{3,2,1,0:T(8,128)S(1)} %get-tuple-element.62), channel_id=1, source_target_pairs={{0,31},{1,0},{2,1},{3,2},{4,3},{5,4},{6,5},{7,6},{8,7},{9,8},{10,9... | collective-permute-start | bytes 2359304 | tf_op jit(solution)/shard_map/ppermute | solution.py:806
  27.9 31.4 %collective-permute-start.9 = (f32[6,16,16,128]{3,2,1,0:T(8,128)S(1)}, f32[6,16,16,128]{3,2,1,0:T(8,128)S(1)}, u32[]{:S(2)}, u32[]{:S(2)}) collective-permute-start(f32[6,16,16,128]{3,2,1,0:T(8,128)S(1)} %get-tuple-element.61), channel_id=1, source_target_pairs={{0,1},{1,2},{2,3},{3,4},{4,5},{5,6},{6,7},{7,8},{8,9},{9,10},{10,1... | collective-permute-start | bytes 2359304 | tf_op jit(solution)/shard_map/ppermute | solution.py:806
  27.9 30.1 %collective-permute-start.5 = (f32[6,192,128]{2,1,0:T(8,128)S(1)}, f32[6,192,128]{2,1,0:T(8,128)S(1)}, u32[]{:S(2)}, u32[]{:S(2)}) collective-permute-start(f32[6,192,128]{2,1,0:T(8,128)S(1)} %get-tuple-element.57), channel_id=1, source_target_pairs={{0,33},{3,34},{4,37},{7,38},{8,41},{11,42},{12,45},{15,46},{16,49}... | collective-permute-start | bytes 1769480 | tf_op jit(solution)/shard_map/ppermute | solution.py:835
  29.2 54.7 %collective-permute-start.14 = (f32[1536,128]{1,0:T(8,128)S(1)}, f32[1536,128]{1,0:T(8,128)S(1)}, u32[]{:S(2)}, u32[]{:S(2)}) collective-permute-start(f32[1536,128]{1,0:T(8,128)S(1)} %get-tuple-element.68), channel_id=1, source_target_pairs={{0,32},{1,33},{2,34},{3,35},{4,36},{5,37},{6,38},{7,39},{8,40},{9,... | collective-permute-start | bytes 2359304 | tf_op jit(solution)/shard_map/ppermute | solution.py:806
  58.0 25.9 %collective-permute-start.15 = (f32[6,192,128]{2,1,0:T(8,128)S(1)}, f32[6,192,128]{2,1,0:T(8,128)S(1)}, u32[]{:S(2)}, u32[]{:S(2)}) collective-permute-start(f32[6,192,128]{2,1,0:T(8,128)S(1)} %collective-permute-done.5), channel_id=1, source_target_pairs={{1,0},{2,3},{5,4},{6,7},{9,8},{10,11},{13,12},{14,15},{17,16},{18,... | collective-permute-start | bytes 1769480 | tf_op jit(solution)/shard_map/ppermute | solution.py:839
  63.2 17.8 %collective-permute-start.11 = (f32[768,128]{1,0:T(8,128)S(1)}, f32[768,128]{1,0:T(8,128)S(1)}, u32[]{:S(2)}, u32[]{:S(2)}) collective-permute-start(f32[768,128]{1,0:T(8,128)S(1)} %get-tuple-element.64), channel_id=1, source_target_pairs={{0,1},{1,2},{2,3},{3,4},{4,5},{5,6},{6,7},{7,8},{8,9},{9,10},{10,1... | collective-permute-start | bytes 1179656 | tf_op jit(solution)/shard_map/ppermute | solution.py:806
  66.4 17.5 %collective-permute-start.12 = (f32[768,128]{1,0:T(8,128)S(1)}, f32[768,128]{1,0:T(8,128)S(1)}, u32[]{:S(2)}, u32[]{:S(2)}) collective-permute-start(f32[768,128]{1,0:T(8,128)S(1)} %get-tuple-element.65), channel_id=1, source_target_pairs={{0,31},{1,0},{2,1},{3,2},{4,3},{5,4},{6,5},{7,6},{8,7},{9,8},{10,9... | collective-permute-start | bytes 1179656 | tf_op jit(solution)/shard_map/ppermute | solution.py:806
  71.0 1.3 collective-permute-start.7
  72.3 8.7 %collective-permute-start.8 = (f32[3,48,128]{2,1,0:T(8,128)S(1)}, f32[3,48,128]{2,1,0:T(8,128)S(1)}, u32[]{:S(2)}, u32[]{:S(2)}) collective-permute-start(f32[3,48,128]{2,1,0:T(8,128)S(1)} %add.34.part_ref.rest_0_), channel_id=1, source_target_pairs={{0,32},{1,33},{2,34},{3,35},{4,36},{5,37},{6,38},{7,39},{8,40},{9,... | collective-permute-start | bytes 221192 | tf_op jit(solution)/shard_map/ppermute | solution.py:806
  85.0 9.4 %collective-permute-start.16 = (f32[16,256,128]{2,1,0:T(8,128)S(1)}, f32[16,256,128]{2,1,0:T(8,128)S(1)}, u32[]{:S(2)}, u32[]{:S(2)}) collective-permute-start(f32[16,256,128]{2,1,0:T(8,128)S(1)} %get-tuple-element.73.s_ref), channel_id=1, source_target_pairs={{0,64},{1,65},{2,66},{3,67},{4,68},{5,69},{6,70},{7,71},{8,72},{9,... | collective-permute-start | bytes 6291464 | tf_op jit(solution)/shard_map/ppermute | solution.py:806
  85.1 12.3 %collective-permute-start.13 = (f32[16,64,128]{2,1,0:T(8,128)S(1)}, f32[16,64,128]{2,1,0:T(8,128)S(1)}, u32[]{:S(2)}, u32[]{:S(2)}) collective-permute-start(f32[16,64,128]{2,1,0:T(8,128)S(1)} %get-tuple-element.67), channel_id=1, source_target_pairs={{1,33},{2,34},{5,37},{6,38},{9,41},{10,42},{13,45},{14,46},{17,49}... | collective-permute-start | bytes 1572872 | tf_op jit(solution)/shard_map/ppermute | solution.py:853
  85.8 18.4 %collective-permute-start.17 = (f32[864,128]{1,0:T(8,128)S(1)}, f32[864,128]{1,0:T(8,128)S(1)}, u32[]{:S(2)}, u32[]{:S(2)}) collective-permute-start(f32[864,128]{1,0:T(8,128)S(1)} %get-tuple-element.76), channel_id=1, source_target_pairs={{0,1},{1,2},{2,3},{3,4},{4,5},{5,6},{6,7},{7,8},{8,9},{9,10},{10,1... | collective-permute-start | bytes 1327112 | tf_op jit(solution)/shard_map/ppermute | solution.py:806
  87.5 16.6 %collective-permute-start.18 = (f32[864,128]{1,0:T(8,128)S(1)}, f32[864,128]{1,0:T(8,128)S(1)}, u32[]{:S(2)}, u32[]{:S(2)}) collective-permute-start(f32[864,128]{1,0:T(8,128)S(1)} %get-tuple-element.77), channel_id=1, source_target_pairs={{0,31},{1,0},{2,1},{3,2},{4,3},{5,4},{6,5},{7,6},{8,7},{9,8},{10,9... | collective-permute-start | bytes 1327112 | tf_op jit(solution)/shard_map/ppermute | solution.py:806
  109.8 1.3 collective-permute-start.19
  111.1 3.9 %collective-permute-start.20 = (f32[64,128]{1,0:T(8,128)S(1)}, f32[64,128]{1,0:T(8,128)S(1)}, u32[]{:S(2)}, u32[]{:S(2)}) collective-permute-start(f32[64,128]{1,0:T(8,128)S(1)} %add.35), channel_id=1, source_target_pairs={{0,32},{1,33},{2,34},{3,35},{4,36},{5,37},{6,38},{7,39},{8,40},{9,... | collective-permute-start | bytes 98312 | tf_op jit(solution)/shard_map/ppermute | solution.py:862
  115.0 5.1 %collective-permute-start.21 = (f32[64,128]{1,0:T(8,128)S(1)}, f32[64,128]{1,0:T(8,128)S(1)}, u32[]{:S(2)}, u32[]{:S(2)}) collective-permute-start(f32[64,128]{1,0:T(8,128)S(1)} %add.36), channel_id=1, source_target_pairs={{0,36},{1,37},{2,38},{3,39},{4,32},{5,33},{6,34},{7,35},{8,44},{9,... | collective-permute-start | bytes 98312 | tf_op jit(solution)/shard_map/ppermute | solution.py:862
  120.1 3.9 %collective-permute-start.22 = (f32[64,128]{1,0:T(8,128)S(1)}, f32[64,128]{1,0:T(8,128)S(1)}, u32[]{:S(2)}, u32[]{:S(2)}) collective-permute-start(f32[64,128]{1,0:T(8,128)S(1)} %add.37), channel_id=1, source_target_pairs={{0,1},{1,0},{2,3},{3,2},{4,5},{5,4},{6,7},{7,6},{8,9},{9,8},{10,11... | collective-permute-start | bytes 98312 | tf_op jit(solution)/shard_map/ppermute | solution.py:862
  124.0 5.1 %collective-permute-start.23 = (f32[64,128]{1,0:T(8,128)S(1)}, f32[64,128]{1,0:T(8,128)S(1)}, u32[]{:S(2)}, u32[]{:S(2)}) collective-permute-start(f32[64,128]{1,0:T(8,128)S(1)} %add.38), channel_id=1, source_target_pairs={{0,3},{1,2},{2,1},{3,0},{4,7},{5,6},{6,5},{7,4},{8,11},{9,10},{10,... | collective-permute-start | bytes 98312 | tf_op jit(solution)/shard_map/ppermute | solution.py:862
  129.2 3.9 %collective-permute-start.24 = (f32[64,128]{1,0:T(8,128)S(1)}, f32[64,128]{1,0:T(8,128)S(1)}, u32[]{:S(2)}, u32[]{:S(2)}) collective-permute-start(f32[64,128]{1,0:T(8,128)S(1)} %add.39), channel_id=1, source_target_pairs={{0,8},{1,9},{2,10},{3,11},{4,12},{5,13},{6,14},{7,15},{8,0},{9,1},... | collective-permute-start | bytes 98312 | tf_op jit(solution)/shard_map/ppermute | solution.py:862
  133.1 5.1 %collective-permute-start.25 = (f32[64,128]{1,0:T(8,128)S(1)}, f32[64,128]{1,0:T(8,128)S(1)}, u32[]{:S(2)}, u32[]{:S(2)}) collective-permute-start(f32[64,128]{1,0:T(8,128)S(1)} %add.40), channel_id=1, source_target_pairs={{0,24},{1,25},{2,26},{3,27},{4,28},{5,29},{6,30},{7,31},{8,16},{9,... | collective-permute-start | bytes 98312 | tf_op jit(solution)/shard_map/ppermute | solution.py:862
  138.2 1.2 collective-permute-start.26

commit v11 on v10

--- a/solution.py
+++ b/solution.py
@@ -148,7 +148,11 @@
     out_ref[:, 96:192, :] = s_ref[:, 160:256, :]
 
 
-def pack_kernel(s_ref, edge_ref, head_ref, tail_ref):
+def pack_kernel(s_ref, edge_ref, relay_ref, head_ref, tail_ref):
+    @pl.when(pl.program_id(0) >= MIDDLE // N)
+    def _():
+        pack_edges(s_ref, relay_ref)
+
     @pl.when(pl.program_id(0) < FIRST // N)
     def _():
         pack_edges(s_ref, edge_ref)
@@ -164,22 +168,18 @@
         pack_kernel,
         grid=(C // N,),
         in_specs=[plane_spec(ROWS, N)],
-        out_specs=edge_specs()[:1] + [halo_spec(N), halo_spec(N)],
-        out_shape=EDGES[:1] + [HALO, HALO],
+        out_specs=[edge_spec(0, FIRST), edge_spec(MIDDLE, C), halo_spec(N), halo_spec(N)],
+        out_shape=[EDGES[0], EDGES[2], HALO, HALO],
         compiler_params=params(12),
         cost_estimate=cost(1 << 32, 6 << 20),
         name="pack",
     )(s)
 
 
-def pack_rest_kernel(s_ref, inner_ref, message_ref, relay_ref, mid_ref):
+def pack_rest_kernel(s_ref, inner_ref, message_ref, mid_ref):
     step = pl.program_id(0)
     inner = inner_ref[0] == 1
     mid_ref[...] = s_ref[:, 96:160, :]
-
-    @pl.when(step >= MIDDLE // N)
-    def _():
-        pack_edges(s_ref, relay_ref)
 
     @pl.when((step >= FIRST // N) & (inner | (step < MIDDLE // N)))
     def _():
@@ -197,17 +197,16 @@
 
 def pack_rest(s, inner):
     rows = (C - FIRST) * EDGE
-    message, relay, mid = pl.pallas_call(
+    return pl.pallas_call(
         pack_rest_kernel,
         grid=(C // N,),
         in_specs=[plane_spec(ROWS, N), SCALARS],
-        out_specs=[whole(rows), edge_spec(MIDDLE, C), plane_spec(MID, N)],
-        out_shape=[sds((rows, S)), EDGES[2], sds((C, MID, S))],
+        out_specs=[whole(rows), plane_spec(MID, N)],
+        out_shape=[sds((rows, S)), sds((C, MID, S))],
         compiler_params=params(12),
         cost_estimate=cost(1 << 31, 4 << 20),
         name="pack_rest",
     )(s, inner)
-    return message, relay, mid
 
 
 def stack(*pieces):
@@ -822,20 +821,23 @@
 
     parcel = stack((atoms, 24), (pot, 32))
     parcel_mate = send(parcel, over_y)
-    one_edge, head, tail = pack(to_pack)
+    one_edge, relay, head, tail = pack(to_pack)
+    relayed = lax.ppermute(relay, AXES, [(d, d ^ over_y ^ 1) for d in outer_ones])
     one_edge = send(one_edge, over_y)
+    parcel_mate, relay = barrier((parcel_mate, relay))
     pair = stack((parcel, 24), (parcel_mate, 24))
     column = stack((send(pair, 0, 1), 48), (pair, 48), (send(pair, 0, -1), 48))
+    column, head, tail = barrier((column, head, tail))
+    column, relayed = barrier((column, relayed))
     column_mate = send(column, over_x)
-    message, relay, mid = pack_rest(s, inner)
+    message, mid = pack_rest(s, inner)
     vb = spread(parcel)
     beside = side_x(s, mate)
-    column_mate, head, tail, message, relay, beside = barrier((column_mate, head, tail, message, relay, beside))
     low, high = send(tail, 0, 1), send(head, 0, -1)
-    relayed = lax.ppermute(relay, AXES, [(d, d ^ over_y ^ 1) for d in outer_ones])
+    column_mate, message, beside = barrier((column_mate, message, beside))
     message = send(message, over_y)
     gg, part, energy = prep([column, column_mate], corner, vb, s)
-    part, relayed, one_edge = barrier((part, relayed, one_edge))
+    part, low, one_edge, relayed = barrier((part, low, one_edge, relayed))
     relayed = lax.ppermute(relayed, AXES, [(d, d ^ 1) for d in inner_ones])
     planes = vb.reshape(C, ROWS, S)
     side_part = side_z(s, beside, low, high)
@@ -847,15 +849,15 @@
     part_mate, low_one, high_one = barrier((part_mate, low_one, high_one))
     message = message.reshape(C - FIRST, EDGE, S)
     q, mix, head, tail = other_half(s, side_part, planes, message, relayed, inner, part, part_mate, q, mix)
-    halos = [low_one, high_one, send(tail, 0, 1), send(head, 0, -1)]
     mate = send(mix, over_x)
+    halos = [send(tail, 0, 1), send(head, 0, -1)]
     mid, part_mate = barrier((mid, part_mate))
     mid = lax.ppermute(mid, AXES, [(d, d ^ over_y) for d in inner_ones])
     planes_mate = spread(parcel_mate).reshape(C, ROWS, S)
     part_two = side_again(mix, mate)
     base = make_base(s, mid, planes, planes_mate, q, side_part, part_two, [one_edge, message, relayed], inner)
     gg = gg.reshape(2, C, ROWS, S)
-    second, own, give = make_second(base, halos, gg, [part, part_mate, energy], upper)
+    second, own, give = make_second(base, [low_one, high_one] + halos, gg, [part, part_mate, energy], upper)
 
     own = own + send(give, over_x)
     for flip in (32, 36, 1, 3, 8, 24):

time: 158 us -> 158 us (level)
    ppermute x18, starting transfers between devices: 36.1 us -> 32 us  [send(): return lax.ppermute(value, AXES, [(d, target(d)) for d in range(count)])]
    ppermute x1, starting transfers between devices: 1.32 us -> 4.87 us  [per_device(): lax.ppermute(relay, AXES, [(d, d ^ over_y ^ 1) for d in outer_ones])]
    ppermute x18, waiting for transfers between devices: 36.9 us -> 39.5 us  [send(): return lax.ppermute(value, AXES, [(d, target(d)) for d in range(count)])]
    ppermute x1, waiting for transfers between devices: 1.91 us -> 0.01 us  [per_device(): lax.ppermute(relay, AXES, [(d, d ^ over_y ^ 1) for d in outer_ones])]
  transfers between devices with their start and end apart: 27 -> 27, of which waited for: 15 -> 14; matrix products, arithmetic and copies ran while one was open for 2% -> 2% of each run, Pallas kernels for 14% -> 14%
where the time goes in v11:
time: 158 us; the launch traced here: 157 us
  waiting for transfers between devices  62.6 us (40%)
  Pallas kernels  45.3 us (29%)
  starting transfers between devices  42.9 us (27%)
  local copies, waits for them, and re-layouts  5.1 us (3%)
    ppermute x18, waiting for transfers between devices, send(): return lax.ppermute(value, AXES, [(d, target(d)) for d in range(count)])  39.5 us
    ppermute x18, starting transfers between devices, send(): return lax.ppermute(value, AXES, [(d, target(d)) for d in range(count)])  32 us
    ppermute x6, waiting for transfers between devices, per_device(): own = own + lax.ppermute(own, AXES, [(d, d ^ flip) for d in range(count)])  23.1 us
    pallas_call x1, Pallas kernels, turn(): pl.pallas_call(turn_kernel, grid=(STEPS,), in_specs=[plane_spec(), whole(...  16.9 us
    pallas_call x1, Pallas kernels, prep(): pl.pallas_call(prep_kernel, in_specs=[vmem] * 2 + [pl.BlockSpec(memory_sp...  7.8 us
    pallas_call x1, Pallas kernels, make_second(): pl.pallas_call(second_kernel, grid=(STEPS,), in_specs=[plane_spec()] + [w...  5.65 us
    ppermute x1, starting transfers between devices, per_device(): lax.ppermute(relay, AXES, [(d, d ^ over_y ^ 1) for d in outer_ones])  4.87 us
    ppermute x6, starting transfers between devices, per_device(): own = own + lax.ppermute(own, AXES, [(d, d ^ flip) for d in range(count)])  4.02 us
  transfers between devices with their start and end apart: 27, of which 14 were waited for; matrix products, arithmetic and copies ran while one was open for 2% of the time, Pallas kernels for 14%

profile of v11, /device:TPU:0, one launch (start us, length us, event | category | flops | bytes accessed | tf_op | source)
XLA Modules:
  0.0 157.1 jit_solution(16780936942001174845)
XLA Ops:
  3.8 1.6 %copy-done = f32[16,16,16,128]{3,2,1,0:T(8,128)S(1)} copy-done((f32[16,16,16,128]{3,2,1,0:T(8,128)S(1)}, f32[16,16,16,128]{3,2,1,0:T(8,128)}, u32[]{:S(2)}) %copy-start) | copy-done | bytes 2097176
  6.2 4.9 %collective-permute-start.3 = (f32[6,192,128]{2,1,0:T(8,128)S(1)}, f32[6,192,128]{2,1,0:T(8,128)S(1)}, u32[]{:S(2)}, u32[]{:S(2)}) collective-permute-start(f32[6,192,128]{2,1,0:T(8,128)S(1)} %get-tuple-element.54), channel_id=1, source_target_pairs={{0,33},{3,34},{4,37},{7,38},{8,41},{11,42},{12,45},{15,46},{16,49}... | collective-permute-start | bytes 1769480 | tf_op jit(solution)/shard_map/ppermute | solution.py:825
  11.3 3.8 %collective-permute-done.refs_1_.parcel_ref = f32[56,128]{1,0:T(8,128)S(1)} collective-permute-done((f32[56,128]{1,0:T(8,128)S(1)}, f32[56,128]{1,0:T(8,128)S(1)}, u32[]{:S(2)}, u32[]{:S(2)}) %collective-permute-start) | collective-permute-done | bytes 28704 | tf_op jit(solution)/shard_map/ppermute | solution.py:805
  15.1 7.7 %collective-permute-start.2 = (f32[48,128]{1,0:T(8,128)S(1)}, f32[48,128]{1,0:T(8,128)S(1)}, u32[]{:S(2)}, u32[]{:S(2)}) collective-permute-start(f32[48,128]{1,0:T(8,128)S(1)} %stack.16.refs_1_), channel_id=1, source_target_pairs={{0,31},{1,0},{2,1},{3,2},{4,3},{5,4},{6,5},{7,6},{8,7},{9,8},{10,9... | collective-permute-start | bytes 73736 | tf_op jit(solution)/shard_map/ppermute | solution.py:805
  22.9 1.9 %collective-permute-done.1.refs_0_ = f32[48,128]{1,0:T(8,128)S(1)} collective-permute-done((f32[48,128]{1,0:T(8,128)S(1)}, f32[48,128]{1,0:T(8,128)S(1)}, u32[]{:S(2)}, u32[]{:S(2)}) %collective-permute-start.1) | collective-permute-done | bytes 24608 | tf_op jit(solution)/shard_map/ppermute | solution.py:805
  24.9 2.6 %collective-permute-start.6 = (f32[6,16,16,128]{3,2,1,0:T(8,128)S(1)}, f32[6,16,16,128]{3,2,1,0:T(8,128)S(1)}, u32[]{:S(2)}, u32[]{:S(2)}) collective-permute-start(f32[6,16,16,128]{3,2,1,0:T(8,128)S(1)} %get-tuple-element.64), channel_id=1, source_target_pairs={{0,1},{1,2},{2,3},{3,4},{4,5},{5,6},{6,7},{7,8},{8,9},{9,10},{10,1... | collective-permute-start | bytes 2359304 | tf_op jit(solution)/shard_map/ppermute | solution.py:805
  27.5 5.3 %collective-permute-start.10 = (f32[6,16,16,128]{3,2,1,0:T(8,128)S(1)}, f32[6,16,16,128]{3,2,1,0:T(8,128)S(1)}, u32[]{:S(2)}, u32[]{:S(2)}) collective-permute-start(f32[6,16,16,128]{3,2,1,0:T(8,128)S(1)} %get-tuple-element.70), channel_id=1, source_target_pairs={{0,31},{1,0},{2,1},{3,2},{4,3},{5,4},{6,5},{7,6},{8,7},{9,8},{10,9... | collective-permute-start | bytes 2359304 | tf_op jit(solution)/shard_map/ppermute | solution.py:805
  33.0 1.5 side_x.1.part_ref
  36.0 7.8 %prep.1 = (bf16[2,4096,128]{2,1,0:T(8,128)(2,1)S(1)}, f32[3,48,128]{2,1,0:T(8,128)S(1)}, f32[48,128]{1,0:T(8,128)S(1)}) custom-call(f32[144,128]{1,0:T(8,128)S(1)} %stack.17.refs_0_, f32[144,128]{1,0:T(8,128)S(1)} %collective-permute-done.4.refs_1_, s32[2]{0:T(128)S(1)} %pad_add_fusion.refs_2_, f32[4096,128]{1,0:T(8,128)S(1)} %spread.2.refs_3_, ...), custom_call_target="tpu_custom_call" | custom-call | flops 134217728 | bytes 10485760 | tf_op jit(solution)/shard_map/prep/pallas_call | solution.py:461
  43.8 16.3 %collective-permute-done.7.edge_ref.refs_0_ = f32[8,192,128]{2,1,0:T(8,128)S(1)} collective-permute-done((f32[8,192,128]{2,1,0:T(8,128)S(1)}, f32[8,192,128]{2,1,0:T(8,128)S(1)}, u32[]{:S(2)}, u32[]{:S(2)}) %collective-permute-start.7) | collective-permute-done | bytes 786464 | tf_op jit(solution)/shard_map/ppermute | solution.py:805
  60.2 1.3 collective-permute-start.15
  61.5 2.9 %side_z.1.side_ref = f32[16,256,128]{2,1,0:T(8,128)S(1)} custom-call(f32[16,256,128]{2,1,0:T(8,128)S(1)} %bitcast.17, f32[16,256,128]{2,1,0:T(8,128)S(1)} %side_x.1.part_ref, f32[6,16,16,128]{3,2,1,0:T(8,128)S(1)} %collective-permute-done.6.low_ref, f32[6,16,16,128]{3,2,1,0:T(8,128)S(1)} %collective-permute-done.10.high_ref), custom_call_target="tpu_custom_call" | custom-call | flops 16777216 | bytes 8388608 | tf_op jit(solution)/shard_map/side_z/pallas_call | solution.py:274
  65.3 2.7 %collective-permute-start.11 = (f32[768,128]{1,0:T(8,128)S(1)}, f32[768,128]{1,0:T(8,128)S(1)}, u32[]{:S(2)}, u32[]{:S(2)}) collective-permute-start(f32[768,128]{1,0:T(8,128)S(1)} %get-tuple-element.72), channel_id=1, source_target_pairs={{0,1},{1,2},{2,3},{3,4},{4,5},{5,6},{6,7},{7,8},{8,9},{9,10},{10,1... | collective-permute-start | bytes 1179656 | tf_op jit(solution)/shard_map/ppermute | solution.py:805
  68.1 5.1 %collective-permute-start.12 = (f32[768,128]{1,0:T(8,128)S(1)}, f32[768,128]{1,0:T(8,128)S(1)}, u32[]{:S(2)}, u32[]{:S(2)}) collective-permute-start(f32[768,128]{1,0:T(8,128)S(1)} %get-tuple-element.73), channel_id=1, source_target_pairs={{0,31},{1,0},{2,1},{3,2},{4,3},{5,4},{6,5},{7,6},{8,7},{9,8},{10,9... | collective-permute-start | bytes 1179656 | tf_op jit(solution)/shard_map/ppermute | solution.py:805
  73.2 1.3 collective-permute-done.8
  74.6 10.0 %collective-permute-done.9.mate_ref.rest_1_ = f32[3,48,128]{2,1,0:T(8,128)S(1)} collective-permute-done((f32[3,48,128]{2,1,0:T(8,128)S(1)}, f32[3,48,128]{2,1,0:T(8,128)S(1)}, u32[]{:S(2)}, u32[]{:S(2)}) %collective-permute-start.9) | collective-permute-done | bytes 73760 | tf_op jit(solution)/shard_map/ppermute | solution.py:805
  86.6 7.7 %collective-permute-start.18 = (f32[864,128]{1,0:T(8,128)S(1)}, f32[864,128]{1,0:T(8,128)S(1)}, u32[]{:S(2)}, u32[]{:S(2)}) collective-permute-start(f32[864,128]{1,0:T(8,128)S(1)} %get-tuple-element.85), channel_id=1, source_target_pairs={{0,31},{1,0},{2,1},{3,2},{4,3},{5,4},{6,5},{7,6},{8,7},{9,8},{10,9... | collective-permute-start | bytes 1327112 | tf_op jit(solution)/shard_map/ppermute | solution.py:805
  95.1 2.9 %side_again.1.part_ref = f32[16,256,128]{2,1,0:T(8,128)S(1)} custom-call(f32[16,256,128]{2,1,0:T(8,128)S(1)} %get-tuple-element.81.s_ref, f32[16,256,128]{2,1,0:T(8,128)S(1)} %collective-permute-done.16.mate_ref), custom_call_target="tpu_custom_call" | custom-call | flops 33554432 | bytes 6291456 | tf_op jit(solution)/shard_map/side_again/pallas_call | solution.py:301
  98.1 3.0 %base.1.base_ref = f32[16,256,128]{2,1,0:T(8,128)S(1)} custom-call(f32[16,256,128]{2,1,0:T(8,128)S(1)} %bitcast.20, f32[16,64,128]{2,1,0:T(8,128)S(1)} %collective-permute-done.13.mid_ref, f32[16,256,128]{2,1,0:T(8,128)S(1)} %bitcast.23, f32[16,256,128]{2,1,0:T(8,128)S(1)} %bitcast.26, f32[16,256,128]{2,1,0:T(8,128)S(1)} %get-tuple-element.80.q_ref, ...), custom_call_target="tpu_custom_call" | custom-call | flops 33554432 | bytes 16777216 | tf_op jit(solution)/shard_map/base/pallas_call | solution.py:601
  101.0 3.8 %collective-permute-done.17.low_ref = f32[864,128]{1,0:T(8,128)S(1)} collective-permute-done((f32[864,128]{1,0:T(8,128)S(1)}, f32[864,128]{1,0:T(8,128)S(1)}, u32[]{:S(2)}, u32[]{:S(2)}) %collective-permute-start.17) | collective-permute-done | bytes 442400 | tf_op jit(solution)/shard_map/ppermute | solution.py:805
  104.8 5.6 %second.1 = (f32[16,256,128]{2,1,0:T(8,128)S(1)}, f32[64,128]{1,0:T(8,128)S(1)}, f32[64,128]{1,0:T(8,128)S(1)}) custom-call(f32[16,256,128]{2,1,0:T(8,128)S(1)} %base.1.base_ref, f32[768,128]{1,0:T(8,128)S(1)} %collective-permute-done.11.low_one_ref, f32[768,128]{1,0:T(8,128)S(1)} %collective-permute-done.12.high_one_ref, ...), custom_call_target="tpu_custom_call" | custom-call | flops 134217728 | bytes 8388608 | tf_op jit(solution)/shard_map/second/pallas_call | solution.py:682
  110.6 1.2 collective-permute-done.19
  112.3 3.4 %collective-permute-done.20 = f32[64,128]{1,0:T(8,128)S(1)} collective-permute-done((f32[64,128]{1,0:T(8,128)S(1)}, f32[64,128]{1,0:T(8,128)S(1)}, u32[]{:S(2)}, u32[]{:S(2)}) %collective-permute-start.20) | collective-permute-done | bytes 32800 | tf_op jit(solution)/shard_map/ppermute | solution.py:864
  115.7 5.1 %collective-permute-done.21 = f32[64,128]{1,0:T(8,128)S(1)} collective-permute-done((f32[64,128]{1,0:T(8,128)S(1)}, f32[64,128]{1,0:T(8,128)S(1)}, u32[]{:S(2)}, u32[]{:S(2)}) %collective-permute-start.21) | collective-permute-done | bytes 32800 | tf_op jit(solution)/shard_map/ppermute | solution.py:864
  120.9 3.9 %collective-permute-done.22 = f32[64,128]{1,0:T(8,128)S(1)} collective-permute-done((f32[64,128]{1,0:T(8,128)S(1)}, f32[64,128]{1,0:T(8,128)S(1)}, u32[]{:S(2)}, u32[]{:S(2)}) %collective-permute-start.22) | collective-permute-done | bytes 32800 | tf_op jit(solution)/shard_map/ppermute | solution.py:864
  124.8 1.7 %collective-permute-start.23 = (f32[64,128]{1,0:T(8,128)S(1)}, f32[64,128]{1,0:T(8,128)S(1)}, u32[]{:S(2)}, u32[]{:S(2)}) collective-permute-start(f32[64,128]{1,0:T(8,128)S(1)} %add.38), channel_id=1, source_target_pairs={{0,3},{1,2},{2,1},{3,0},{4,7},{5,6},{6,5},{7,4},{8,11},{9,10},{10,... | collective-permute-start | bytes 98312 | tf_op jit(solution)/shard_map/ppermute | solution.py:864
  126.4 3.5 %collective-permute-done.23 = f32[64,128]{1,0:T(8,128)S(1)} collective-permute-done((f32[64,128]{1,0:T(8,128)S(1)}, f32[64,128]{1,0:T(8,128)S(1)}, u32[]{:S(2)}, u32[]{:S(2)}) %collective-permute-start.23) | collective-permute-done | bytes 32800 | tf_op jit(solution)/shard_map/ppermute | solution.py:864
  129.9 3.9 %collective-permute-done.24 = f32[64,128]{1,0:T(8,128)S(1)} collective-permute-done((f32[64,128]{1,0:T(8,128)S(1)}, f32[64,128]{1,0:T(8,128)S(1)}, u32[]{:S(2)}, u32[]{:S(2)}) %collective-permute-start.24) | collective-permute-done | bytes 32800 | tf_op jit(solution)/shard_map/ppermute | solution.py:864
  133.8 1.8 %collective-permute-start.25 = (f32[64,128]{1,0:T(8,128)S(1)}, f32[64,128]{1,0:T(8,128)S(1)}, u32[]{:S(2)}, u32[]{:S(2)}) collective-permute-start(f32[64,128]{1,0:T(8,128)S(1)} %add.40), channel_id=1, source_target_pairs={{0,24},{1,25},{2,26},{3,27},{4,28},{5,29},{6,30},{7,31},{8,16},{9,... | collective-permute-start | bytes 98312 | tf_op jit(solution)/shard_map/ppermute | solution.py:864
  135.6 3.3 %collective-permute-done.25 = f32[64,128]{1,0:T(8,128)S(1)} collective-permute-done((f32[64,128]{1,0:T(8,128)S(1)}, f32[64,128]{1,0:T(8,128)S(1)}, u32[]{:S(2)}, u32[]{:S(2)}) %collective-permute-start.25) | collective-permute-done | bytes 32800 | tf_op jit(solution)/shard_map/ppermute | solution.py:864
  139.0 1.2 collective-permute-done.26.other_ref
  140.2 16.9 %turn.1 = f32[16,256,128]{2,1,0:T(8,128)} custom-call(f32[16,256,128]{2,1,0:T(8,128)S(1)} %get-tuple-element.90.second_ref, f32[64,128]{1,0:T(8,128)S(1)} %add.41.own_ref, f32[64,128]{1,0:T(8,128)S(1)} %collective-permute-done.26.other_ref, s32[1]{0:T(128)} %bitcast.3.rest_3_.upper_ref), custom_call_target="tpu_custom_call" | custom-call | flops 268435456 | bytes 4194304 | tf_op jit(solution)/shard_map/turn/pallas_call | solution.py:782
  (60 shorter events, 11.3 us)
Async XLA Ops:
  0.0 32.9 %collective-permute-start.5 = (f32[16,256,128]{2,1,0:T(8,128)}, f32[16,256,128]{2,1,0:T(8,128)S(1)}, u32[]{:S(2)}, u32[]{:S(2)}) collective-permute-start(f32[16,256,128]{2,1,0:T(8,128)} %bitcast.12), channel_id=1, source_target_pairs={{0,64},{1,65},{2,66},{3,67},{4,68},{5,69},{6,70},{7,71},{8,72},{9,... | collective-permute-start | bytes 6291464 | tf_op jit(solution)/shard_map/ppermute | solution.py:805
  3.8 1.6 %copy-start = (f32[16,16,16,128]{3,2,1,0:T(8,128)S(1)}, f32[16,16,16,128]{3,2,1,0:T(8,128)}, u32[]{:S(2)}) copy-start(f32[16,16,16,128]{3,2,1,0:T(8,128)} %param.5) | copy-start | bytes 6291460
  6.2 26.5 %collective-permute-start.3 = (f32[6,192,128]{2,1,0:T(8,128)S(1)}, f32[6,192,128]{2,1,0:T(8,128)S(1)}, u32[]{:S(2)}, u32[]{:S(2)}) collective-permute-start(f32[6,192,128]{2,1,0:T(8,128)S(1)} %get-tuple-element.54), channel_id=1, source_target_pairs={{0,33},{3,34},{4,37},{7,38},{8,41},{11,42},{12,45},{15,46},{16,49}... | collective-permute-start | bytes 1769480 | tf_op jit(solution)/shard_map/ppermute | solution.py:825
  11.1 4.0 %collective-permute-start = (f32[56,128]{1,0:T(8,128)S(1)}, f32[56,128]{1,0:T(8,128)S(1)}, u32[]{:S(2)}, u32[]{:S(2)}) collective-permute-start(f32[56,128]{1,0:T(8,128)S(1)} %stack.15.refs_0_.parcel_ref), channel_id=1, source_target_pairs={{0,32},{1,33},{2,34},{3,35},{4,36},{5,37},{6,38},{7,39},{8,40},{9,... | collective-permute-start | bytes 86024 | tf_op jit(solution)/shard_map/ppermute | solution.py:805
  15.1 9.8 %collective-permute-start.1 = (f32[48,128]{1,0:T(8,128)S(1)}, f32[48,128]{1,0:T(8,128)S(1)}, u32[]{:S(2)}, u32[]{:S(2)}) collective-permute-start(f32[48,128]{1,0:T(8,128)S(1)} %stack.16.refs_1_), channel_id=1, source_target_pairs={{0,1},{1,2},{2,3},{3,4},{4,5},{5,6},{6,7},{7,8},{8,9},{9,10},{10,1... | collective-permute-start | bytes 73736 | tf_op jit(solution)/shard_map/ppermute | solution.py:805
  15.1 9.8 %collective-permute-start.2 = (f32[48,128]{1,0:T(8,128)S(1)}, f32[48,128]{1,0:T(8,128)S(1)}, u32[]{:S(2)}, u32[]{:S(2)}) collective-permute-start(f32[48,128]{1,0:T(8,128)S(1)} %stack.16.refs_1_), channel_id=1, source_target_pairs={{0,31},{1,0},{2,1},{3,2},{4,3},{5,4},{6,5},{7,6},{8,7},{9,8},{10,9... | collective-permute-start | bytes 73736 | tf_op jit(solution)/shard_map/ppermute | solution.py:805
  22.8 37.3 %collective-permute-start.7 = (f32[8,192,128]{2,1,0:T(8,128)S(1)}, f32[8,192,128]{2,1,0:T(8,128)S(1)}, u32[]{:S(2)}, u32[]{:S(2)}) collective-permute-start(f32[8,192,128]{2,1,0:T(8,128)S(1)} %get-tuple-element.65), channel_id=1, source_target_pairs={{0,32},{1,33},{2,34},{3,35},{4,36},{5,37},{6,38},{7,39},{8,40},{9,... | collective-permute-start | bytes 2359304 | tf_op jit(solution)/shard_map/ppermute | solution.py:805
  24.9 35.3 %collective-permute-start.6 = (f32[6,16,16,128]{3,2,1,0:T(8,128)S(1)}, f32[6,16,16,128]{3,2,1,0:T(8,128)S(1)}, u32[]{:S(2)}, u32[]{:S(2)}) collective-permute-start(f32[6,16,16,128]{3,2,1,0:T(8,128)S(1)} %get-tuple-element.64), channel_id=1, source_target_pairs={{0,1},{1,2},{2,3},{3,4},{4,5},{5,6},{6,7},{7,8},{8,9},{9,10},{10,1... | collective-permute-start | bytes 2359304 | tf_op jit(solution)/shard_map/ppermute | solution.py:805
  27.5 34.0 %collective-permute-start.10 = (f32[6,16,16,128]{3,2,1,0:T(8,128)S(1)}, f32[6,16,16,128]{3,2,1,0:T(8,128)S(1)}, u32[]{:S(2)}, u32[]{:S(2)}) collective-permute-start(f32[6,16,16,128]{3,2,1,0:T(8,128)S(1)} %get-tuple-element.70), channel_id=1, source_target_pairs={{0,31},{1,0},{2,1},{3,2},{4,3},{5,4},{6,5},{7,6},{8,7},{9,8},{10,9... | collective-permute-start | bytes 2359304 | tf_op jit(solution)/shard_map/ppermute | solution.py:805
  32.7 1.7 %collective-permute-start.4 = (f32[144,128]{1,0:T(8,128)S(1)}, f32[144,128]{1,0:T(8,128)S(1)}, u32[]{:S(2)}, u32[]{:S(2)}) collective-permute-start(f32[144,128]{1,0:T(8,128)S(1)} %stack.17.refs_0_), channel_id=1, source_target_pairs={{0,64},{1,65},{2,66},{3,67},{4,68},{5,69},{6,70},{7,71},{8,72},{9,... | collective-permute-start | bytes 221192 | tf_op jit(solution)/shard_map/ppermute | solution.py:805
  34.4 1.6 %copy-start.1 = (f32[16,16,16,128]{3,2,1,0:T(8,128)S(1)}, f32[16,16,16,128]{3,2,1,0:T(8,128)}, u32[]{:S(2)}) copy-start(f32[16,16,16,128]{3,2,1,0:T(8,128)} %param.5) | copy-start | bytes 6291460
  34.5 50.2 %collective-permute-start.14 = (f32[1536,128]{1,0:T(8,128)S(1)}, f32[1536,128]{1,0:T(8,128)S(1)}, u32[]{:S(2)}, u32[]{:S(2)}) collective-permute-start(f32[1536,128]{1,0:T(8,128)S(1)} %get-tuple-element.76), channel_id=1, source_target_pairs={{0,32},{1,33},{2,34},{3,35},{4,36},{5,37},{6,38},{7,39},{8,40},{9,... | collective-permute-start | bytes 2359304 | tf_op jit(solution)/shard_map/ppermute | solution.py:805
  60.2 24.5 %collective-permute-start.15 = (f32[6,192,128]{2,1,0:T(8,128)S(1)}, f32[6,192,128]{2,1,0:T(8,128)S(1)}, u32[]{:S(2)}, u32[]{:S(2)}) collective-permute-start(f32[6,192,128]{2,1,0:T(8,128)S(1)} %collective-permute-done.3), channel_id=1, source_target_pairs={{1,0},{2,3},{5,4},{6,7},{9,8},{10,11},{13,12},{14,15},{17,16},{18,... | collective-permute-start | bytes 1769480 | tf_op jit(solution)/shard_map/ppermute | solution.py:841
  65.3 19.3 %collective-permute-start.11 = (f32[768,128]{1,0:T(8,128)S(1)}, f32[768,128]{1,0:T(8,128)S(1)}, u32[]{:S(2)}, u32[]{:S(2)}) collective-permute-start(f32[768,128]{1,0:T(8,128)S(1)} %get-tuple-element.72), channel_id=1, source_target_pairs={{0,1},{1,2},{2,3},{3,4},{4,5},{5,6},{6,7},{7,8},{8,9},{9,10},{10,1... | collective-permute-start | bytes 1179656 | tf_op jit(solution)/shard_map/ppermute | solution.py:805
  68.1 16.5 %collective-permute-start.12 = (f32[768,128]{1,0:T(8,128)S(1)}, f32[768,128]{1,0:T(8,128)S(1)}, u32[]{:S(2)}, u32[]{:S(2)}) collective-permute-start(f32[768,128]{1,0:T(8,128)S(1)} %get-tuple-element.73), channel_id=1, source_target_pairs={{0,31},{1,0},{2,1},{3,2},{4,3},{5,4},{6,5},{7,6},{8,7},{9,8},{10,9... | collective-permute-start | bytes 1179656 | tf_op jit(solution)/shard_map/ppermute | solution.py:805
  73.2 1.3 collective-permute-start.8
  74.4 10.2 %collective-permute-start.9 = (f32[3,48,128]{2,1,0:T(8,128)S(1)}, f32[3,48,128]{2,1,0:T(8,128)S(1)}, u32[]{:S(2)}, u32[]{:S(2)}) collective-permute-start(f32[3,48,128]{2,1,0:T(8,128)S(1)} %add.34.part_ref.rest_0_), channel_id=1, source_target_pairs={{0,32},{1,33},{2,34},{3,35},{4,36},{5,37},{6,38},{7,39},{8,40},{9,... | collective-permute-start | bytes 221192 | tf_op jit(solution)/shard_map/ppermute | solution.py:805
  85.7 9.4 %collective-permute-start.16 = (f32[16,256,128]{2,1,0:T(8,128)S(1)}, f32[16,256,128]{2,1,0:T(8,128)S(1)}, u32[]{:S(2)}, u32[]{:S(2)}) collective-permute-start(f32[16,256,128]{2,1,0:T(8,128)S(1)} %get-tuple-element.81.s_ref), channel_id=1, source_target_pairs={{0,64},{1,65},{2,66},{3,67},{4,68},{5,69},{6,70},{7,71},{8,72},{9,... | collective-permute-start | bytes 6291464 | tf_op jit(solution)/shard_map/ppermute | solution.py:805
  85.8 12.3 %collective-permute-start.13 = (f32[16,64,128]{2,1,0:T(8,128)S(1)}, f32[16,64,128]{2,1,0:T(8,128)S(1)}, u32[]{:S(2)}, u32[]{:S(2)}) collective-permute-start(f32[16,64,128]{2,1,0:T(8,128)S(1)} %get-tuple-element.75), channel_id=1, source_target_pairs={{1,33},{2,34},{5,37},{6,38},{9,41},{10,42},{13,45},{14,46},{17,49}... | collective-permute-start | bytes 1572872 | tf_op jit(solution)/shard_map/ppermute | solution.py:855
  86.5 18.4 %collective-permute-start.17 = (f32[864,128]{1,0:T(8,128)S(1)}, f32[864,128]{1,0:T(8,128)S(1)}, u32[]{:S(2)}, u32[]{:S(2)}) collective-permute-start(f32[864,128]{1,0:T(8,128)S(1)} %get-tuple-element.84), channel_id=1, source_target_pairs={{0,1},{1,2},{2,3},{3,4},{4,5},{5,6},{6,7},{7,8},{8,9},{9,10},{10,1... | collective-permute-start | bytes 1327112 | tf_op jit(solution)/shard_map/ppermute | solution.py:805
  86.6 18.3 %collective-permute-start.18 = (f32[864,128]{1,0:T(8,128)S(1)}, f32[864,128]{1,0:T(8,128)S(1)}, u32[]{:S(2)}, u32[]{:S(2)}) collective-permute-start(f32[864,128]{1,0:T(8,128)S(1)} %get-tuple-element.85), channel_id=1, source_target_pairs={{0,31},{1,0},{2,1},{3,2},{4,3},{5,4},{6,5},{7,6},{8,7},{9,8},{10,9... | collective-permute-start | bytes 1327112 | tf_op jit(solution)/shard_map/ppermute | solution.py:805
  110.5 1.3 collective-permute-start.19
  111.8 3.9 %collective-permute-start.20 = (f32[64,128]{1,0:T(8,128)S(1)}, f32[64,128]{1,0:T(8,128)S(1)}, u32[]{:S(2)}, u32[]{:S(2)}) collective-permute-start(f32[64,128]{1,0:T(8,128)S(1)} %add.35), channel_id=1, source_target_pairs={{0,32},{1,33},{2,34},{3,35},{4,36},{5,37},{6,38},{7,39},{8,40},{9,... | collective-permute-start | bytes 98312 | tf_op jit(solution)/shard_map/ppermute | solution.py:864
  115.7 5.1 %collective-permute-start.21 = (f32[64,128]{1,0:T(8,128)S(1)}, f32[64,128]{1,0:T(8,128)S(1)}, u32[]{:S(2)}, u32[]{:S(2)}) collective-permute-start(f32[64,128]{1,0:T(8,128)S(1)} %add.36), channel_id=1, source_target_pairs={{0,36},{1,37},{2,38},{3,39},{4,32},{5,33},{6,34},{7,35},{8,44},{9,... | collective-permute-start | bytes 98312 | tf_op jit(solution)/shard_map/ppermute | solution.py:864
  120.9 3.9 %collective-permute-start.22 = (f32[64,128]{1,0:T(8,128)S(1)}, f32[64,128]{1,0:T(8,128)S(1)}, u32[]{:S(2)}, u32[]{:S(2)}) collective-permute-start(f32[64,128]{1,0:T(8,128)S(1)} %add.37), channel_id=1, source_target_pairs={{0,1},{1,0},{2,3},{3,2},{4,5},{5,4},{6,7},{7,6},{8,9},{9,8},{10,11... | collective-permute-start | bytes 98312 | tf_op jit(solution)/shard_map/ppermute | solution.py:864
  124.8 5.1 %collective-permute-start.23 = (f32[64,128]{1,0:T(8,128)S(1)}, f32[64,128]{1,0:T(8,128)S(1)}, u32[]{:S(2)}, u32[]{:S(2)}) collective-permute-start(f32[64,128]{1,0:T(8,128)S(1)} %add.38), channel_id=1, source_target_pairs={{0,3},{1,2},{2,1},{3,0},{4,7},{5,6},{6,5},{7,4},{8,11},{9,10},{10,... | collective-permute-start | bytes 98312 | tf_op jit(solution)/shard_map/ppermute | solution.py:864
  129.9 3.9 %collective-permute-start.24 = (f32[64,128]{1,0:T(8,128)S(1)}, f32[64,128]{1,0:T(8,128)S(1)}, u32[]{:S(2)}, u32[]{:S(2)}) collective-permute-start(f32[64,128]{1,0:T(8,128)S(1)} %add.39), channel_id=1, source_target_pairs={{0,8},{1,9},{2,10},{3,11},{4,12},{5,13},{6,14},{7,15},{8,0},{9,1},... | collective-permute-start | bytes 98312 | tf_op jit(solution)/shard_map/ppermute | solution.py:864
  133.8 5.1 %collective-permute-start.25 = (f32[64,128]{1,0:T(8,128)S(1)}, f32[64,128]{1,0:T(8,128)S(1)}, u32[]{:S(2)}, u32[]{:S(2)}) collective-permute-start(f32[64,128]{1,0:T(8,128)S(1)} %add.40), channel_id=1, source_target_pairs={{0,24},{1,25},{2,26},{3,27},{4,28},{5,29},{6,30},{7,31},{8,16},{9,... | collective-permute-start | bytes 98312 | tf_op jit(solution)/shard_map/ppermute | solution.py:864
  139.0 1.2 collective-permute-start.26

commit v12 on v8

--- a/solution.py
+++ b/solution.py
@@ -12,6 +12,7 @@
 C = 16
 ROWS = C * C
 CELLS = C * C * C
+NCELLS = 32 * 32 * 512
 S = 128
 W = 9
 R = 4
@@ -73,7 +74,7 @@
 B = 4
 STEPS = C // B
 N = 2
-FIRST = 6
+FIRST = 8
 MIDDLE = 10
 EDGE = 192
 MID = 64
@@ -209,16 +210,16 @@
     return message, relay, mid
 
 
-def stack_kernel(*refs):
-    start = 0
-    for ref in refs[:-1]:
-        refs[-1][start : start + ref.shape[0], :] = ref[...]
-        start += ref.shape[0]
-
-
-def stack(*arrays):
-    rows = sum(a.shape[0] for a in arrays)
-    return pl.pallas_call(stack_kernel, out_shape=sds((rows, S)), compiler_params=params(4), name="stack")(*arrays)
+def stack(*pieces):
+    def kernel(*refs):
+        start = 0
+        for ref, (_, rows) in zip(refs, pieces):
+            refs[-1][start : start + rows, :] = ref[:rows, :]
+            start += rows
+
+    arrays = [array for array, _ in pieces]
+    rows = sum(rows for _, rows in pieces)
+    return pl.pallas_call(kernel, out_shape=sds((rows, S)), compiler_params=params(4), name="stack")(*arrays)
 
 
 def along_x(s_ref, mate_ref, out_ref, add):
@@ -326,7 +327,7 @@
 
 def spread_kernel(parcel_ref, vb_ref):
     def spread_row(row, _):
-        line = (parcel_ref[pl.ds(72 + row, 1), :] + (DIAGONAL - filter_centre)) * (1.0 / filter_half)
+        line = (parcel_ref[pl.ds(24 + row, 1), :] + (DIAGONAL - filter_centre)) * (1.0 / filter_half)
         start = pl.multiple_of(row * 128, 128)
         vb_ref[pl.ds(start, 128), :] = jnp.broadcast_to(line, (128, 128)).T
         return 0
@@ -345,15 +346,17 @@
 
 
 def prep_kernel(*refs):
-    parcels = refs[:4]
-    corner_ref, vb_ref, s_ref, gg_ref, coef_ref, energy_ref, near_ref, table_ref, a1_ref, a1z_ref, a2_ref, a2s_ref = refs[4:]
+    own_ref, other_ref, corner_ref, vb_ref, s_ref, gg_ref, coef_ref, energy_ref, near_ref, table_ref = refs[:10]
+    a1_ref, a1z_ref, a2_ref, a2s_ref = refs[10:]
     upper_x, upper_y = corner_ref[0] > 0, corner_ref[1] > 0
     for slab in range(3):
-        own, over_x, over_y, over_xy = [parcel[slab * 24 : slab * 24 + 24, :] for parcel in parcels]
-        same_x = [jnp.where(upper_y, over_y, own), jnp.where(upper_y, own, over_y)]
-        other_x = [jnp.where(upper_y, over_xy, over_x), jnp.where(upper_y, over_x, over_xy)]
-        ordered = [jnp.where(upper_x, o, m) for m, o in zip(same_x, other_x)]
-        ordered += [jnp.where(upper_x, m, o) for m, o in zip(same_x, other_x)]
+        own = [own_ref[slab * 48 + j * 24 : slab * 48 + j * 24 + 24, :] for j in range(2)]
+        other = [other_ref[slab * 48 + j * 24 : slab * 48 + j * 24 + 24, :] for j in range(2)]
+        lower = [jnp.where(upper_x, o, m) for m, o in zip(own, other)]
+        higher = [jnp.where(upper_x, m, o) for m, o in zip(own, other)]
+        ordered = []
+        for pair in (lower, higher):
+            ordered += [jnp.where(upper_y, pair[1], pair[0]), jnp.where(upper_y, pair[0], pair[1])]
         for j in range(4):
             near_ref[slab * 96 + j * 24 : slab * 96 + j * 24 + 24, :] = ordered[j]
     blank = jnp.zeros((16, 128), F32)
@@ -458,7 +461,7 @@
     vmem = pl.BlockSpec(memory_space=pltpu.VMEM)
     return pl.pallas_call(
         prep_kernel,
-        in_specs=[vmem] * 4 + [pl.BlockSpec(memory_space=pltpu.SMEM), vmem, vmem],
+        in_specs=[vmem] * 2 + [pl.BlockSpec(memory_space=pltpu.SMEM), vmem, vmem],
         out_shape=[sds((2, CELLS, S), BF16), sds((3, NEAR, S)), sds((NEAR, S))],
         scratch_shapes=[
             pltpu.VMEM((288, 128), F32),
@@ -584,7 +587,7 @@
 
 
 def second_kernel(base_ref, low_ref, high_ref, gg_high_ref, gg_low_ref, *rest):
-    part_ref, mate_ref, energy_ref, second_ref, gram_ref, cross_ref, w_ref, halo_ref = rest
+    part_ref, mate_ref, energy_ref, upper_ref, second_ref, keep_ref, give_ref, gram_ref, cross_ref, w_ref, halo_ref = rest
     step = pl.program_id(0)
 
     @pl.when(step == 0)
@@ -615,39 +618,42 @@
             halo_ref[p, stride_rows(C - H + z), :] = add
 
     w_high, w_low = split(w_ref[...])
-    gram = jnp.zeros((S, S), F32)
-    cross = jnp.zeros((S, S), F32)
+    w_twice = jnp.concatenate([w_high, w_high])
+    gram = jnp.zeros((S, 2 * S), F32)
     for p in range(B):
         g_high, g_low = gg_high_ref[0, p], gg_low_ref[0, p]
-        value = base_ref[p] + halo_ref[p] + (mm(g_high, w_high) + (mm(g_high, w_low) + mm(g_low, w_high)))
+        near = mm(jnp.concatenate([g_high, g_low], axis=1), w_twice) + mm(g_high, w_low)
+        value = base_ref[p] + halo_ref[p] + near
         second_ref[p] = value
         s_high, s_low = split(value)
-        turned = s_high.T
-        gram += mm(turned, s_high)
-        cross += mm(turned, s_low)
-    gram_ref[...] += gram
-    cross_ref[...] += cross
+        gram += mm(s_high.T, jnp.concatenate([s_high, s_low], axis=1))
+    gram_ref[...] += gram[:, :S]
+    cross_ref[...] += gram[:, S:]
 
     @pl.when(step == STEPS - 1)
     def _():
         cross = cross_ref[...]
-        gram_ref[...] += cross + cross.T
-
-
-def make_second(base, low, high, gg, weighted):
-    shares = pl.BlockSpec((3, NEAR, S), lambda i: (0, 0, 0))
+        gram = (gram_ref[...] + (cross + cross.T)) * (1.0 / NCELLS)
+        upper = upper_ref[0] == 1
+        keep_ref[...] = jnp.where(upper, gram[S // 2 :], gram[: S // 2])
+        give_ref[...] = jnp.where(upper, gram[: S // 2], gram[S // 2 :])
+
+
+def make_second(base, halos, gg, shares, upper):
+    three = pl.BlockSpec((3, NEAR, S), lambda i: (0, 0, 0))
     return pl.pallas_call(
         second_kernel,
         grid=(STEPS,),
-        in_specs=[plane_spec(), whole(MESSAGE.shape[0]), whole(MESSAGE.shape[0]), part_spec(0), part_spec(1)]
-        + [shares, shares, whole(NEAR)],
-        out_specs=[plane_spec(), whole()],
-        out_shape=[FULL, sds((S, S))],
-        scratch_shapes=[pltpu.VMEM((S, S), F32), pltpu.VMEM((S, S), F32), pltpu.VMEM((B, ROWS, S), F32)],
+        in_specs=[plane_spec()]
+        + [whole(MESSAGE.shape[0])] * 2
+        + [part_spec(0), part_spec(1), three, three, whole(NEAR), SCALARS],
+        out_specs=[plane_spec(), whole(S // 2), whole(S // 2)],
+        out_shape=[FULL, sds((S // 2, S)), sds((S // 2, S))],
+        scratch_shapes=[pltpu.VMEM((S, S), F32)] * 3 + [pltpu.VMEM((B, ROWS, S), F32)],
         compiler_params=params(16),
         cost_estimate=cost(1 << 27, 8 << 20),
         name="second",
-    )(base, low, high, gg, gg, *weighted)
+    )(base, *halos, gg, gg, *shares, upper)
 
 
 def exact(a, b):
@@ -715,33 +721,36 @@
     x_ref[...] = x_ref[...] * across
 
 
-def turn_kernel(second_ref, gram_ref, out_ref, a_ref, x_ref, i_high_ref, i_low_ref, state_ref):
+def turn_kernel(second_ref, own_ref, other_ref, upper_ref, out_ref, gram_ref, a_ref, x_ref, i_high_ref, i_low_ref, state_ref):
     @pl.when(pl.program_id(0) == 0)
     def _():
+        upper = upper_ref[0] == 1
+        gram_ref[: S // 2, :] = jnp.where(upper, other_ref[...], own_ref[...])
+        gram_ref[S // 2 :, :] = jnp.where(upper, own_ref[...], other_ref[...])
         inverse_factor(gram_ref, a_ref, x_ref, state_ref)
         i_high, i_low = split(x_ref[...].T)
         i_high_ref[...] = i_high
         i_low_ref[...] = i_low
 
     i_high, i_low = i_high_ref[...], i_low_ref[...]
-
+    i_twice = jnp.concatenate([i_high, i_high])
     for p in range(B):
         high, low = split(second_ref[p])
-        out_ref[p] = mm(high, i_high) + (mm(high, i_low) + mm(low, i_high))
-
-
-def turn(second, gram):
+        out_ref[p] = mm(jnp.concatenate([high, low], axis=1), i_twice) + mm(high, i_low)
+
+
+def turn(second, own, other, upper):
     return pl.pallas_call(
         turn_kernel,
         grid=(STEPS,),
-        in_specs=[plane_spec(), whole()],
+        in_specs=[plane_spec(), whole(S // 2), whole(S // 2), SCALARS],
         out_specs=plane_spec(),
         out_shape=FULL,
-        scratch_shapes=[pltpu.VMEM((S, S), F32)] * 2 + [pltpu.VMEM((S, S), BF16)] * 2 + [pltpu.SMEM((1,), jnp.int32)],
+        scratch_shapes=[pltpu.VMEM((S, S), F32)] * 3 + [pltpu.VMEM((S, S), BF16)] * 2 + [pltpu.SMEM((1,), jnp.int32)],
         compiler_params=params(16),
         cost_estimate=cost(1 << 28, 4 << 20),
         name="turn",
-    )(second, gram)
+    )(second, own, other, upper)
 
 
 def per_device(states, potential, atom_sites, projectors, energies):
@@ -761,52 +770,57 @@
     outer_ones = [d for d in range(count) if d % 4 in (0, 3)]
     inner = ((lax.axis_index("gzs") + 1) // 2 % 2).astype(jnp.int32).reshape(1)
     s = states.reshape(C, ROWS, S)
+    mate = send(s, over_x)
     pot = potential.reshape(32, 128)
-
+    corner = jnp.stack([gx * C, gy * C]).astype(jnp.int32)
+    upper = gx.astype(jnp.int32).reshape(1)
     atoms = jnp.concatenate(
         [projectors.reshape(4, TAPS), atom_sites.astype(F32), energies[:, None], jnp.zeros((4, 768 - TAPS - 4), F32)],
         axis=1,
     ).reshape(24, 128)
-    mate = send(s, over_x)
-    below, above = send(atoms, 0, 1), send(atoms, 0, -1)
-    one_edge, head, tail = pack(s)
+    to_pack, pot, corner, upper, inner, atoms = barrier((s, pot, corner, upper, inner, atoms))
+
+    parcel = stack((atoms, 24), (pot, 32))
+    parcel_mate = send(parcel, over_y)
+    one_edge, head, tail = pack(to_pack)
     one_edge = send(one_edge, over_y)
-    head, tail, below, above = barrier((head, tail, below, above))
-    parcel = stack(below, atoms, above, pot)
-    parcel_y = send(parcel, over_y)
-    parcel_x = send(parcel, over_x)
-    low, high = send(tail, 0, 1), send(head, 0, -1)
+    pair = stack((parcel, 24), (parcel_mate, 24))
+    column = stack((send(pair, 0, 1), 48), (pair, 48), (send(pair, 0, -1), 48))
+    column_mate = send(column, over_x)
     message, relay, mid = pack_rest(s, inner)
     vb = spread(parcel)
     beside = side_x(s, mate)
-    parcel_y, one_edge, message, relay, beside = barrier((parcel_y, one_edge, message, relay, beside))
+    column_mate, head, tail, relay, beside = barrier((column_mate, head, tail, relay, beside))
+    low, high = send(tail, 0, 1), send(head, 0, -1)
     relayed = lax.ppermute(relay, AXES, [(d, d ^ over_y ^ 1) for d in outer_ones])
+    column_mate, one_edge = barrier((column_mate, one_edge))
+    gg, part, energy = prep([column, column_mate], corner, vb, s)
+    part, message = barrier((part, message))
     message = send(message, over_y)
-    parcel_xy = send(parcel_y, over_x)
-    corner = jnp.stack([gx * C, gy * C]).astype(jnp.int32)
-    gg, part, energy = prep([parcel, parcel_x, parcel_y, parcel_xy], corner, vb, s)
-
-    part, relayed = barrier((part, relayed))
+    side_part = side_z(s, beside, low, high)
+    side_part, relayed = barrier((side_part, relayed))
     relayed = lax.ppermute(relayed, AXES, [(d, d ^ 1) for d in inner_ones])
+    planes = vb.reshape(C, ROWS, S)
+
     part = part + send(part, over_x)
     part_mate = send(part, over_y)
-    side_part = side_z(s, beside, low, high)
-    edges = [one_edge, message.reshape(C - FIRST, EDGE, S), relayed]
-    vb = vb.reshape(C, ROWS, S)
-    q, mix, head, tail = make_first(s, side_part, vb, edges, inner, part, part_mate)
-    low, high = send(tail, 0, 1), send(head, 0, -1)
+    message = message.reshape(C - FIRST, EDGE, S)
+    edges = [one_edge, message, relayed]
+    q, mix, head, tail = make_first(s, side_part, planes, edges, inner, part, part_mate)
+    halos = [send(tail, 0, 1), send(head, 0, -1)]
     mate = send(mix, over_x)
     mid, part_mate = barrier((mid, part_mate))
     mid = lax.ppermute(mid, AXES, [(d, d ^ over_y) for d in inner_ones])
-    vb_mate = spread(parcel_y).reshape(C, ROWS, S)
+    planes_mate = spread(parcel_mate).reshape(C, ROWS, S)
     part_two = side_again(mix, mate)
-    base = make_base(s, mid, vb, vb_mate, q, side_part, part_two, edges, inner)
-    second, gram = make_second(base, low, high, gg.reshape(2, C, ROWS, S), [part, part_mate, energy])
-
-    for flip in (64, 32, 36, 1, 3, 8, 24):
-        gram = gram + lax.ppermute(gram, AXES, [(d, d ^ flip) for d in range(count)])
-    gram = gram * (1.0 / (CELLS * count))
-    return turn(second, gram).reshape(C, C, C, S)
+    base = make_base(s, mid, planes, planes_mate, q, side_part, part_two, edges, inner)
+    gg = gg.reshape(2, C, ROWS, S)
+    second, own, give = make_second(base, halos, gg, [part, part_mate, energy], upper)
+
+    own = own + send(give, over_x)
+    for flip in (32, 36, 1, 3, 8, 24):
+        own = own + lax.ppermute(own, AXES, [(d, d ^ flip) for d in range(count)])
+    return turn(second, own, send(own, over_x), upper).reshape(C, C, C, S)
 
 
 def solution(mesh):

time: 154 us -> 162 us (1.052)
  waiting for transfers between devices: 51.7 us -> 75.8 us
  Pallas kernels: 52.1 us -> 43.5 us
  starting transfers between devices: 43.6 us -> 35.5 us
    ppermute x15 -> x16, waiting for transfers between devices: 30.3 us -> 52.8 us  [send(): return lax.ppermute(value, AXES, [(d, target(d)) for d in range(count)])]
    ppermute x7 -> x6, starting transfers between devices: 10.1 us -> 4.06 us  [per_device(): own = own + lax.ppermute(own, AXES, [(d, d ^ flip) for d in range(count)])]
    pallas_call x1, Pallas kernels: 3.4 us -> 0.77 us  [pack(): pl.pallas_call(pack_kernel, grid=(C // N,), in_specs=[plane_spec(ROWS, N)...]
    unnamed x25 -> x5, local copies, waits for them, and re-layouts: 4.56 us -> 2.54 us
    pallas_call x1, Pallas kernels: 2.12 us -> 0.3 us  [pack_rest(): pl.pallas_call(pack_rest_kernel, grid=(C // N,), in_specs=[plane_spec(ROW...]
    ppermute x7 -> x6, waiting for transfers between devices: 21.5 us -> 23 us  [per_device(): own = own + lax.ppermute(own, AXES, [(d, d ^ flip) for d in range(count)])]
    pallas_call x3 -> x5, Pallas kernels: 12.7 us -> 11.5 us  [the longest x1 7.8 us: prep(): pl.pallas_call(prep_kernel, in_specs=[vmem] * 2 + [pl.BlockSpec(memory_sp...]
    ppermute x15 -> x16, starting transfers between devices: 28.7 us -> 28.1 us  [send(): return lax.ppermute(value, AXES, [(d, target(d)) for d in range(count)])]
  transfers between devices with their start and end apart: 25 -> 25, of which waited for: 14 -> 13; matrix products, arithmetic and copies ran while one was open for 0% -> 2% of each run, Pallas kernels for 18% -> 13%
where the time goes in v12:
time: 162 us; the launch traced here: 160 us
  waiting for transfers between devices  75.8 us (47%)
  Pallas kernels  43.5 us (27%)
  starting transfers between devices  35.5 us (22%)
  local copies, waits for them, and re-layouts  4.53 us (3%)
    ppermute x16, waiting for transfers between devices, send(): return lax.ppermute(value, AXES, [(d, target(d)) for d in range(count)])  52.8 us
    ppermute x16, starting transfers between devices, send(): return lax.ppermute(value, AXES, [(d, target(d)) for d in range(count)])  28.1 us
    ppermute x6, waiting for transfers between devices, per_device(): own = own + lax.ppermute(own, AXES, [(d, d ^ flip) for d in range(count)])  23 us
    pallas_call x1, Pallas kernels, turn(): pl.pallas_call(turn_kernel, grid=(STEPS,), in_specs=[plane_spec(), whole(...  17 us
    pallas_call x1, Pallas kernels, prep(): pl.pallas_call(prep_kernel, in_specs=[vmem] * 2 + [pl.BlockSpec(memory_sp...  7.8 us
    ppermute x6, starting transfers between devices, per_device(): own = own + lax.ppermute(own, AXES, [(d, d ^ flip) for d in range(count)])  4.06 us
    pallas_call x1, Pallas kernels, make_second(): pl.pallas_call(second_kernel, grid=(STEPS,), in_specs=[plane_spec()] + [w...  3.67 us
  transfers between devices with their start and end apart: 25, of which 13 were waited for; matrix products, arithmetic and copies ran while one was open for 2% of the time, Pallas kernels for 13%

profile of v12, /device:TPU:0, one launch (start us, length us, event | category | flops | bytes accessed | tf_op | source)
XLA Modules:
  0.0 160.5 jit_solution(6625366158893767611)
XLA Ops:
  3.8 2.0 %collective-permute-start = (f32[56,128]{1,0:T(8,128)S(1)}, f32[56,128]{1,0:T(8,128)S(1)}, u32[]{:S(2)}, u32[]{:S(2)}) collective-permute-start(f32[56,128]{1,0:T(8,128)S(1)} %stack.15.refs_0_.parcel_ref), channel_id=1, source_target_pairs={{0,32},{1,33},{2,34},{3,35},{4,36},{5,37},{6,38},{7,39},{8,40},{9,... | collective-permute-start | bytes 86024 | tf_op jit(solution)/shard_map/ppermute | solution.py:766
  5.8 2.0 %collective-permute-done.refs_1_.parcel_ref = f32[56,128]{1,0:T(8,128)S(1)} collective-permute-done((f32[56,128]{1,0:T(8,128)S(1)}, f32[56,128]{1,0:T(8,128)S(1)}, u32[]{:S(2)}, u32[]{:S(2)}) %collective-permute-start) | collective-permute-done | bytes 28704 | tf_op jit(solution)/shard_map/ppermute | solution.py:766
  7.8 1.5 collective-permute-start.1
  9.3 7.0 %collective-permute-start.2 = (f32[48,128]{1,0:T(8,128)S(1)}, f32[48,128]{1,0:T(8,128)S(1)}, u32[]{:S(2)}, u32[]{:S(2)}) collective-permute-start(f32[48,128]{1,0:T(8,128)S(1)} %stack.16.refs_1_), channel_id=1, source_target_pairs={{0,31},{1,0},{2,1},{3,2},{4,3},{5,4},{6,5},{7,6},{8,7},{9,8},{10,9... | collective-permute-start | bytes 73736 | tf_op jit(solution)/shard_map/ppermute | solution.py:766
  16.3 1.6 copy-done
  18.7 1.2 collective-permute-start.5
  20.3 1.5 side_x.1.part_ref
  21.8 6.0 %collective-permute-start.10 = (f32[6,16,16,128]{3,2,1,0:T(8,128)S(1)}, f32[6,16,16,128]{3,2,1,0:T(8,128)S(1)}, u32[]{:S(2)}, u32[]{:S(2)}) collective-permute-start(f32[6,16,16,128]{3,2,1,0:T(8,128)S(1)} %get-tuple-element.58), channel_id=1, source_target_pairs={{0,31},{1,0},{2,1},{3,2},{4,3},{5,4},{6,5},{7,6},{8,7},{9,8},{10,9... | collective-permute-start | bytes 2359304 | tf_op jit(solution)/shard_map/ppermute | solution.py:766
  27.9 1.3 collective-permute-start.11
  30.0 24.1 %collective-permute-done.5.refs_0_ = f32[8,192,128]{2,1,0:T(8,128)S(1)} collective-permute-done((f32[8,192,128]{2,1,0:T(8,128)S(1)}, f32[8,192,128]{2,1,0:T(8,128)S(1)}, u32[]{:S(2)}, u32[]{:S(2)}) %collective-permute-start.5) | collective-permute-done | bytes 786464 | tf_op jit(solution)/shard_map/ppermute | solution.py:766
  54.1 7.8 %prep.1 = (bf16[2,4096,128]{2,1,0:T(8,128)(2,1)S(1)}, f32[3,48,128]{2,1,0:T(8,128)S(1)}, f32[48,128]{1,0:T(8,128)S(1)}) custom-call(f32[144,128]{1,0:T(8,128)S(1)} %stack.17.refs_0_, f32[144,128]{1,0:T(8,128)S(1)} %collective-permute-done.3.refs_1_, s32[2]{0:T(128)S(1)} %pad_add_fusion.refs_2_, f32[4096,128]{1,0:T(8,128)S(1)} %spread.2.refs_3_, ...), custom_call_target="tpu_custom_call" | custom-call | flops 134217728 | bytes 10485760 | tf_op jit(solution)/shard_map/prep/pallas_call | solution.py:462
  62.0 1.1 collective-permute-start.12
  63.1 2.9 %side_z.1.side_ref = f32[16,256,128]{2,1,0:T(8,128)S(1)} custom-call(f32[16,256,128]{2,1,0:T(8,128)S(1)} %bitcast.17, f32[16,256,128]{2,1,0:T(8,128)S(1)} %side_x.1.part_ref, f32[6,16,16,128]{3,2,1,0:T(8,128)S(1)} %collective-permute-done.9.low_ref, f32[6,16,16,128]{3,2,1,0:T(8,128)S(1)} %collective-permute-done.10.high_ref), custom_call_target="tpu_custom_call" | custom-call | flops 16777216 | bytes 8388608 | tf_op jit(solution)/shard_map/side_z/pallas_call | solution.py:275
  66.0 1.3 collective-permute-start.13
  67.3 1.3 collective-permute-done.6
  69.7 11.5 %collective-permute-done.7.refs_5_.rest_1_ = f32[3,48,128]{2,1,0:T(8,128)S(1)} collective-permute-done((f32[3,48,128]{2,1,0:T(8,128)S(1)}, f32[3,48,128]{2,1,0:T(8,128)S(1)}, u32[]{:S(2)}, u32[]{:S(2)}) %collective-permute-start.7) | collective-permute-done | bytes 73760 | tf_op jit(solution)/shard_map/ppermute | solution.py:766
  81.2 2.1 %first.1 = (f32[16,256,128]{2,1,0:T(8,128)S(1)}, f32[16,256,128]{2,1,0:T(8,128)S(1)}, f32[1632,128]{1,0:T(8,128)S(1)}, f32[1632,128]{1,0:T(8,128)S(1)}) custom-call(f32[16,256,128]{2,1,0:T(8,128)S(1)} %bitcast.18, f32[16,256,128]{2,1,0:T(8,128)S(1)} %side_z.1.side_ref, f32[16,256,128]{2,1,0:T(8,128)S(1)} %bitcast.20, ...), custom_call_target="tpu_custom_call" | custom-call | flops 16777216 | bytes 14680064 | tf_op jit(solution)/shard_map/first/pallas_call | solution.py:521
  83.5 7.7 %collective-permute-start.16 = (f32[1632,128]{1,0:T(8,128)S(1)}, f32[1632,128]{1,0:T(8,128)S(1)}, u32[]{:S(2)}, u32[]{:S(2)}) collective-permute-start(f32[1632,128]{1,0:T(8,128)S(1)} %get-tuple-element.67), channel_id=1, source_target_pairs={{0,31},{1,0},{2,1},{3,2},{4,3},{5,4},{6,5},{7,6},{8,7},{9,8},{10,9... | collective-permute-start | bytes 2506760 | tf_op jit(solution)/shard_map/ppermute | solution.py:766
  92.8 2.9 %side_again.1.part_ref = f32[16,256,128]{2,1,0:T(8,128)S(1)} custom-call(f32[16,256,128]{2,1,0:T(8,128)S(1)} %get-tuple-element.65.s_ref, f32[16,256,128]{2,1,0:T(8,128)S(1)} %collective-permute-done.14.mate_ref), custom_call_target="tpu_custom_call" | custom-call | flops 33554432 | bytes 6291456 | tf_op jit(solution)/shard_map/side_again/pallas_call | solution.py:302
  95.7 3.0 %base.1.base_ref = f32[16,256,128]{2,1,0:T(8,128)S(1)} custom-call(f32[16,256,128]{2,1,0:T(8,128)S(1)} %bitcast.19, f32[16,64,128]{2,1,0:T(8,128)S(1)} %collective-permute-done.8.mid_ref, f32[16,256,128]{2,1,0:T(8,128)S(1)} %bitcast.21, f32[16,256,128]{2,1,0:T(8,128)S(1)} %bitcast.24, f32[16,256,128]{2,1,0:T(8,128)S(1)} %get-tuple-element.64.q_ref, ...), custom_call_target="tpu_custom_call" | custom-call | flops 33554432 | bytes 16777216 | tf_op jit(solution)/shard_map/base/pallas_call | solution.py:573
  98.7 11.5 %collective-permute-done.15.low_ref = f32[1632,128]{1,0:T(8,128)S(1)} collective-permute-done((f32[1632,128]{1,0:T(8,128)S(1)}, f32[1632,128]{1,0:T(8,128)S(1)}, u32[]{:S(2)}, u32[]{:S(2)}) %collective-permute-start.15) | collective-permute-done | bytes 835616 | tf_op jit(solution)/shard_map/ppermute | solution.py:766
  110.2 3.7 %second.1 = (f32[16,256,128]{2,1,0:T(8,128)S(1)}, f32[64,128]{1,0:T(8,128)S(1)}, f32[64,128]{1,0:T(8,128)S(1)}) custom-call(f32[16,256,128]{2,1,0:T(8,128)S(1)} %base.1.base_ref, f32[1632,128]{1,0:T(8,128)S(1)} %collective-permute-done.15.low_ref, f32[1632,128]{1,0:T(8,128)S(1)} %collective-permute-done.16.high_ref, bf16[2,16,256,128]{3,2,1,0:T(8,128)(2,1)S(1)} %bitcast.22, ...), custom_call_target="tpu_custom_call" | custom-call | flops 134217728 | bytes 8388608 | tf_op jit(solution)/shard_map/second/pallas_call | solution.py:644
  113.9 1.2 collective-permute-done.17
  116.0 3.0 %collective-permute-done.18 = f32[64,128]{1,0:T(8,128)S(1)} collective-permute-done((f32[64,128]{1,0:T(8,128)S(1)}, f32[64,128]{1,0:T(8,128)S(1)}, u32[]{:S(2)}, u32[]{:S(2)}) %collective-permute-start.18) | collective-permute-done | bytes 32800 | tf_op jit(solution)/shard_map/ppermute | solution.py:822
  119.1 5.1 %collective-permute-done.19 = f32[64,128]{1,0:T(8,128)S(1)} collective-permute-done((f32[64,128]{1,0:T(8,128)S(1)}, f32[64,128]{1,0:T(8,128)S(1)}, u32[]{:S(2)}, u32[]{:S(2)}) %collective-permute-start.19) | collective-permute-done | bytes 32800 | tf_op jit(solution)/shard_map/ppermute | solution.py:822
  124.2 3.9 %collective-permute-done.20 = f32[64,128]{1,0:T(8,128)S(1)} collective-permute-done((f32[64,128]{1,0:T(8,128)S(1)}, f32[64,128]{1,0:T(8,128)S(1)}, u32[]{:S(2)}, u32[]{:S(2)}) %collective-permute-start.20) | collective-permute-done | bytes 32800 | tf_op jit(solution)/shard_map/ppermute | solution.py:822
  129.1 4.1 %collective-permute-done.21 = f32[64,128]{1,0:T(8,128)S(1)} collective-permute-done((f32[64,128]{1,0:T(8,128)S(1)}, f32[64,128]{1,0:T(8,128)S(1)}, u32[]{:S(2)}, u32[]{:S(2)}) %collective-permute-start.21) | collective-permute-done | bytes 32800 | tf_op jit(solution)/shard_map/ppermute | solution.py:822
  133.3 3.9 %collective-permute-done.22 = f32[64,128]{1,0:T(8,128)S(1)} collective-permute-done((f32[64,128]{1,0:T(8,128)S(1)}, f32[64,128]{1,0:T(8,128)S(1)}, u32[]{:S(2)}, u32[]{:S(2)}) %collective-permute-start.22) | collective-permute-done | bytes 32800 | tf_op jit(solution)/shard_map/ppermute | solution.py:822
  137.2 2.2 %collective-permute-start.23 = (f32[64,128]{1,0:T(8,128)S(1)}, f32[64,128]{1,0:T(8,128)S(1)}, u32[]{:S(2)}, u32[]{:S(2)}) collective-permute-start(f32[64,128]{1,0:T(8,128)S(1)} %add.40), channel_id=1, source_target_pairs={{0,24},{1,25},{2,26},{3,27},{4,28},{5,29},{6,30},{7,31},{8,16},{9,... | collective-permute-start | bytes 98312 | tf_op jit(solution)/shard_map/ppermute | solution.py:822
  139.3 3.0 %collective-permute-done.23 = f32[64,128]{1,0:T(8,128)S(1)} collective-permute-done((f32[64,128]{1,0:T(8,128)S(1)}, f32[64,128]{1,0:T(8,128)S(1)}, u32[]{:S(2)}, u32[]{:S(2)}) %collective-permute-start.23) | collective-permute-done | bytes 32800 | tf_op jit(solution)/shard_map/ppermute | solution.py:822
  142.3 1.2 collective-permute-done.24.other_ref
  143.5 17.0 %turn.1 = f32[16,256,128]{2,1,0:T(8,128)} custom-call(f32[16,256,128]{2,1,0:T(8,128)S(1)} %get-tuple-element.72.second_ref, f32[64,128]{1,0:T(8,128)S(1)} %add.41.own_ref, f32[64,128]{1,0:T(8,128)S(1)} %collective-permute-done.24.other_ref, s32[1]{0:T(128)} %bitcast.3.rest_3_.upper_ref), custom_call_target="tpu_custom_call" | custom-call | flops 268435456 | bytes 4194304 | tf_op jit(solution)/shard_map/turn/pallas_call | solution.py:743
  (55 shorter events, 10.7 us)
Async XLA Ops:
  0.0 20.3 %collective-permute-start.4 = (f32[16,256,128]{2,1,0:T(8,128)}, f32[16,256,128]{2,1,0:T(8,128)S(1)}, u32[]{:S(2)}, u32[]{:S(2)}) collective-permute-start(f32[16,256,128]{2,1,0:T(8,128)} %bitcast.12), channel_id=1, source_target_pairs={{0,64},{1,65},{2,66},{3,67},{4,68},{5,69},{6,70},{7,71},{8,72},{9,... | collective-permute-start | bytes 6291464 | tf_op jit(solution)/shard_map/ppermute | solution.py:766
  3.8 4.0 %collective-permute-start = (f32[56,128]{1,0:T(8,128)S(1)}, f32[56,128]{1,0:T(8,128)S(1)}, u32[]{:S(2)}, u32[]{:S(2)}) collective-permute-start(f32[56,128]{1,0:T(8,128)S(1)} %stack.15.refs_0_.parcel_ref), channel_id=1, source_target_pairs={{0,32},{1,33},{2,34},{3,35},{4,36},{5,37},{6,38},{7,39},{8,40},{9,... | collective-permute-start | bytes 86024 | tf_op jit(solution)/shard_map/ppermute | solution.py:766
  7.8 12.1 %collective-permute-start.1 = (f32[48,128]{1,0:T(8,128)S(1)}, f32[48,128]{1,0:T(8,128)S(1)}, u32[]{:S(2)}, u32[]{:S(2)}) collective-permute-start(f32[48,128]{1,0:T(8,128)S(1)} %stack.16.refs_1_), channel_id=1, source_target_pairs={{0,1},{1,2},{2,3},{3,4},{4,5},{5,6},{6,7},{7,8},{8,9},{9,10},{10,1... | collective-permute-start | bytes 73736 | tf_op jit(solution)/shard_map/ppermute | solution.py:766
  9.3 10.6 %collective-permute-start.2 = (f32[48,128]{1,0:T(8,128)S(1)}, f32[48,128]{1,0:T(8,128)S(1)}, u32[]{:S(2)}, u32[]{:S(2)}) collective-permute-start(f32[48,128]{1,0:T(8,128)S(1)} %stack.16.refs_1_), channel_id=1, source_target_pairs={{0,31},{1,0},{2,1},{3,2},{4,3},{5,4},{6,5},{7,6},{8,7},{9,8},{10,9... | collective-permute-start | bytes 73736 | tf_op jit(solution)/shard_map/ppermute | solution.py:766
  16.3 1.6 copy-start
  18.7 35.5 %collective-permute-start.5 = (f32[8,192,128]{2,1,0:T(8,128)S(1)}, f32[8,192,128]{2,1,0:T(8,128)S(1)}, u32[]{:S(2)}, u32[]{:S(2)}) collective-permute-start(f32[8,192,128]{2,1,0:T(8,128)S(1)} %get-tuple-element.49), channel_id=1, source_target_pairs={{0,32},{1,33},{2,34},{3,35},{4,36},{5,37},{6,38},{7,39},{8,40},{9,... | collective-permute-start | bytes 2359304 | tf_op jit(solution)/shard_map/ppermute | solution.py:766
  19.9 1.9 %collective-permute-start.3 = (f32[144,128]{1,0:T(8,128)S(1)}, f32[144,128]{1,0:T(8,128)S(1)}, u32[]{:S(2)}, u32[]{:S(2)}) collective-permute-start(f32[144,128]{1,0:T(8,128)S(1)} %stack.17.refs_0_), channel_id=1, source_target_pairs={{0,64},{1,65},{2,66},{3,67},{4,68},{5,69},{6,70},{7,71},{8,72},{9,... | collective-permute-start | bytes 221192 | tf_op jit(solution)/shard_map/ppermute | solution.py:766
  21.8 32.3 %copy-start.1 = (f32[16,16,16,128]{3,2,1,0:T(8,128)S(1)}, f32[16,16,16,128]{3,2,1,0:T(8,128)}, u32[]{:S(2)}) copy-start(f32[16,16,16,128]{3,2,1,0:T(8,128)} %param.5) | copy-start | bytes 6291460
  21.8 41.2 %collective-permute-start.10 = (f32[6,16,16,128]{3,2,1,0:T(8,128)S(1)}, f32[6,16,16,128]{3,2,1,0:T(8,128)S(1)}, u32[]{:S(2)}, u32[]{:S(2)}) collective-permute-start(f32[6,16,16,128]{3,2,1,0:T(8,128)S(1)} %get-tuple-element.58), channel_id=1, source_target_pairs={{0,31},{1,0},{2,1},{3,2},{4,3},{5,4},{6,5},{7,6},{8,7},{9,8},{10,9... | collective-permute-start | bytes 2359304 | tf_op jit(solution)/shard_map/ppermute | solution.py:766
  27.9 35.2 %collective-permute-start.9 = (f32[6,16,16,128]{3,2,1,0:T(8,128)S(1)}, f32[6,16,16,128]{3,2,1,0:T(8,128)S(1)}, u32[]{:S(2)}, u32[]{:S(2)}) collective-permute-start(f32[6,16,16,128]{3,2,1,0:T(8,128)S(1)} %get-tuple-element.57), channel_id=1, source_target_pairs={{0,1},{1,2},{2,3},{3,4},{4,5},{5,6},{6,7},{7,8},{8,9},{9,10},{10,1... | collective-permute-start | bytes 2359304 | tf_op jit(solution)/shard_map/ppermute | solution.py:766
  27.9 38.1 %collective-permute-start.11 = (f32[6,192,128]{2,1,0:T(8,128)S(1)}, f32[6,192,128]{2,1,0:T(8,128)S(1)}, u32[]{:S(2)}, u32[]{:S(2)}) collective-permute-start(f32[6,192,128]{2,1,0:T(8,128)S(1)} %get-tuple-element.59), channel_id=1, source_target_pairs={{0,33},{3,34},{4,37},{7,38},{8,41},{11,42},{12,45},{15,46},{16,49}... | collective-permute-start | bytes 1769480 | tf_op jit(solution)/shard_map/ppermute | solution.py:795
  62.0 19.3 %collective-permute-start.12 = (f32[1536,128]{1,0:T(8,128)S(1)}, f32[1536,128]{1,0:T(8,128)S(1)}, u32[]{:S(2)}, u32[]{:S(2)}) collective-permute-start(f32[1536,128]{1,0:T(8,128)S(1)} %get-tuple-element.62), channel_id=1, source_target_pairs={{0,32},{1,33},{2,34},{3,35},{4,36},{5,37},{6,38},{7,39},{8,40},{9,... | collective-permute-start | bytes 2359304 | tf_op jit(solution)/shard_map/ppermute | solution.py:766
  66.0 15.3 %collective-permute-start.13 = (f32[6,192,128]{2,1,0:T(8,128)S(1)}, f32[6,192,128]{2,1,0:T(8,128)S(1)}, u32[]{:S(2)}, u32[]{:S(2)}) collective-permute-start(f32[6,192,128]{2,1,0:T(8,128)S(1)} %collective-permute-done.11), channel_id=1, source_target_pairs={{1,0},{2,3},{5,4},{6,7},{9,8},{10,11},{13,12},{14,15},{17,16},{18,... | collective-permute-start | bytes 1769480 | tf_op jit(solution)/shard_map/ppermute | solution.py:802
  67.3 1.3 collective-permute-start.6
  68.6 12.6 %collective-permute-start.7 = (f32[3,48,128]{2,1,0:T(8,128)S(1)}, f32[3,48,128]{2,1,0:T(8,128)S(1)}, u32[]{:S(2)}, u32[]{:S(2)}) collective-permute-start(f32[3,48,128]{2,1,0:T(8,128)S(1)} %add.34.refs_4_.rest_0_), channel_id=1, source_target_pairs={{0,32},{1,33},{2,34},{3,35},{4,36},{5,37},{6,38},{7,39},{8,40},{9,... | collective-permute-start | bytes 221192 | tf_op jit(solution)/shard_map/ppermute | solution.py:766
  83.3 9.4 %collective-permute-start.14 = (f32[16,256,128]{2,1,0:T(8,128)S(1)}, f32[16,256,128]{2,1,0:T(8,128)S(1)}, u32[]{:S(2)}, u32[]{:S(2)}) collective-permute-start(f32[16,256,128]{2,1,0:T(8,128)S(1)} %get-tuple-element.65.s_ref), channel_id=1, source_target_pairs={{0,64},{1,65},{2,66},{3,67},{4,68},{5,69},{6,70},{7,71},{8,72},{9,... | collective-permute-start | bytes 6291464 | tf_op jit(solution)/shard_map/ppermute | solution.py:766
  83.4 26.7 %collective-permute-start.15 = (f32[1632,128]{1,0:T(8,128)S(1)}, f32[1632,128]{1,0:T(8,128)S(1)}, u32[]{:S(2)}, u32[]{:S(2)}) collective-permute-start(f32[1632,128]{1,0:T(8,128)S(1)} %get-tuple-element.66), channel_id=1, source_target_pairs={{0,1},{1,2},{2,3},{3,4},{4,5},{5,6},{6,7},{7,8},{8,9},{9,10},{10,1... | collective-permute-start | bytes 2506760 | tf_op jit(solution)/shard_map/ppermute | solution.py:766
  83.5 26.7 %collective-permute-start.16 = (f32[1632,128]{1,0:T(8,128)S(1)}, f32[1632,128]{1,0:T(8,128)S(1)}, u32[]{:S(2)}, u32[]{:S(2)}) collective-permute-start(f32[1632,128]{1,0:T(8,128)S(1)} %get-tuple-element.67), channel_id=1, source_target_pairs={{0,31},{1,0},{2,1},{3,2},{4,3},{5,4},{6,5},{7,6},{8,7},{9,8},{10,9... | collective-permute-start | bytes 2506760 | tf_op jit(solution)/shard_map/ppermute | solution.py:766
  91.3 4.5 %collective-permute-start.8 = (f32[16,64,128]{2,1,0:T(8,128)S(1)}, f32[16,64,128]{2,1,0:T(8,128)S(1)}, u32[]{:S(2)}, u32[]{:S(2)}) collective-permute-start(f32[16,64,128]{2,1,0:T(8,128)S(1)} %get-tuple-element.55), channel_id=1, source_target_pairs={{1,33},{2,34},{5,37},{6,38},{9,41},{10,42},{13,45},{14,46},{17,49}... | collective-permute-start | bytes 1572872 | tf_op jit(solution)/shard_map/ppermute | solution.py:813
  113.9 1.3 collective-permute-start.17
  115.1 3.9 %collective-permute-start.18 = (f32[64,128]{1,0:T(8,128)S(1)}, f32[64,128]{1,0:T(8,128)S(1)}, u32[]{:S(2)}, u32[]{:S(2)}) collective-permute-start(f32[64,128]{1,0:T(8,128)S(1)} %add.35), channel_id=1, source_target_pairs={{0,32},{1,33},{2,34},{3,35},{4,36},{5,37},{6,38},{7,39},{8,40},{9,... | collective-permute-start | bytes 98312 | tf_op jit(solution)/shard_map/ppermute | solution.py:822
  119.1 5.1 %collective-permute-start.19 = (f32[64,128]{1,0:T(8,128)S(1)}, f32[64,128]{1,0:T(8,128)S(1)}, u32[]{:S(2)}, u32[]{:S(2)}) collective-permute-start(f32[64,128]{1,0:T(8,128)S(1)} %add.36), channel_id=1, source_target_pairs={{0,36},{1,37},{2,38},{3,39},{4,32},{5,33},{6,34},{7,35},{8,44},{9,... | collective-permute-start | bytes 98312 | tf_op jit(solution)/shard_map/ppermute | solution.py:822
  124.2 3.9 %collective-permute-start.20 = (f32[64,128]{1,0:T(8,128)S(1)}, f32[64,128]{1,0:T(8,128)S(1)}, u32[]{:S(2)}, u32[]{:S(2)}) collective-permute-start(f32[64,128]{1,0:T(8,128)S(1)} %add.37), channel_id=1, source_target_pairs={{0,1},{1,0},{2,3},{3,2},{4,5},{5,4},{6,7},{7,6},{8,9},{9,8},{10,11... | collective-permute-start | bytes 98312 | tf_op jit(solution)/shard_map/ppermute | solution.py:822
  128.1 5.1 %collective-permute-start.21 = (f32[64,128]{1,0:T(8,128)S(1)}, f32[64,128]{1,0:T(8,128)S(1)}, u32[]{:S(2)}, u32[]{:S(2)}) collective-permute-start(f32[64,128]{1,0:T(8,128)S(1)} %add.38), channel_id=1, source_target_pairs={{0,3},{1,2},{2,1},{3,0},{4,7},{5,6},{6,5},{7,4},{8,11},{9,10},{10,... | collective-permute-start | bytes 98312 | tf_op jit(solution)/shard_map/ppermute | solution.py:822
  133.3 3.9 %collective-permute-start.22 = (f32[64,128]{1,0:T(8,128)S(1)}, f32[64,128]{1,0:T(8,128)S(1)}, u32[]{:S(2)}, u32[]{:S(2)}) collective-permute-start(f32[64,128]{1,0:T(8,128)S(1)} %add.39), channel_id=1, source_target_pairs={{0,8},{1,9},{2,10},{3,11},{4,12},{5,13},{6,14},{7,15},{8,0},{9,1},... | collective-permute-start | bytes 98312 | tf_op jit(solution)/shard_map/ppermute | solution.py:822
  137.2 5.1 %collective-permute-start.23 = (f32[64,128]{1,0:T(8,128)S(1)}, f32[64,128]{1,0:T(8,128)S(1)}, u32[]{:S(2)}, u32[]{:S(2)}) collective-permute-start(f32[64,128]{1,0:T(8,128)S(1)} %add.40), channel_id=1, source_target_pairs={{0,24},{1,25},{2,26},{3,27},{4,28},{5,29},{6,30},{7,31},{8,16},{9,... | collective-permute-start | bytes 98312 | tf_op jit(solution)/shard_map/ppermute | solution.py:822
  142.3 1.2 collective-permute-start.24

commit v13 on v12

--- a/solution.py
+++ b/solution.py
@@ -784,21 +784,21 @@
     parcel_mate = send(parcel, over_y)
     one_edge, head, tail = pack(to_pack)
     one_edge = send(one_edge, over_y)
+    parcel_mate, head = barrier((parcel_mate, head))
     pair = stack((parcel, 24), (parcel_mate, 24))
     column = stack((send(pair, 0, 1), 48), (pair, 48), (send(pair, 0, -1), 48))
     column_mate = send(column, over_x)
     message, relay, mid = pack_rest(s, inner)
     vb = spread(parcel)
     beside = side_x(s, mate)
-    column_mate, head, tail, relay, beside = barrier((column_mate, head, tail, relay, beside))
+    column_mate, head, tail, relay, message, beside = barrier((column_mate, head, tail, relay, message, beside))
     low, high = send(tail, 0, 1), send(head, 0, -1)
     relayed = lax.ppermute(relay, AXES, [(d, d ^ over_y ^ 1) for d in outer_ones])
+    message = send(message, over_y)
     column_mate, one_edge = barrier((column_mate, one_edge))
     gg, part, energy = prep([column, column_mate], corner, vb, s)
-    part, message = barrier((part, message))
-    message = send(message, over_y)
+    part, relayed = barrier((part, relayed))
     side_part = side_z(s, beside, low, high)
-    side_part, relayed = barrier((side_part, relayed))
     relayed = lax.ppermute(relayed, AXES, [(d, d ^ 1) for d in inner_ones])
     planes = vb.reshape(C, ROWS, S)
 

time: 162 us -> 157 us (0.969)
  waiting for transfers between devices: 75.8 us -> 72.6 us
    ppermute x16, waiting for transfers between devices: 52.8 us -> 41.6 us  [send(): return lax.ppermute(value, AXES, [(d, target(d)) for d in range(count)])]
    ppermute x1, waiting for transfers between devices: 0.01 us -> 5.6 us  [per_device(): relayed = lax.ppermute(relayed, AXES, [(d, d ^ 1) for d in inner_ones])]
    ppermute x6, starting transfers between devices: 4.06 us -> 1.69 us  [per_device(): own = own + lax.ppermute(own, AXES, [(d, d ^ flip) for d in range(count)])]
    ppermute x6, waiting for transfers between devices: 23 us -> 25.4 us  [per_device(): own = own + lax.ppermute(own, AXES, [(d, d ^ flip) for d in range(count)])]
  transfers between devices with their start and end apart: 25 -> 25, of which waited for: 13 -> 14; matrix products, arithmetic and copies ran while one was open for 2% -> 2% of each run, Pallas kernels for 13% -> 13%
where the time goes in v13:
time: 157 us; the launch traced here: 156 us
  waiting for transfers between devices  72.6 us (46%)
  Pallas kernels  43.5 us (28%)
  starting transfers between devices  34.4 us (22%)
  local copies, waits for them, and re-layouts  4.53 us (3%)
    ppermute x16, waiting for transfers between devices, send(): return lax.ppermute(value, AXES, [(d, target(d)) for d in range(count)])  41.6 us
    ppermute x16, starting transfers between devices, send(): return lax.ppermute(value, AXES, [(d, target(d)) for d in range(count)])  29.3 us
    ppermute x6, waiting for transfers between devices, per_device(): own = own + lax.ppermute(own, AXES, [(d, d ^ flip) for d in range(count)])  25.4 us
    pallas_call x1, Pallas kernels, turn(): pl.pallas_call(turn_kernel, grid=(STEPS,), in_specs=[plane_spec(), whole(...  17 us
    pallas_call x1, Pallas kernels, prep(): pl.pallas_call(prep_kernel, in_specs=[vmem] * 2 + [pl.BlockSpec(memory_sp...  7.8 us
    ppermute x1, waiting for transfers between devices, per_device(): relayed = lax.ppermute(relayed, AXES, [(d, d ^ 1) for d in inner_ones])  5.6 us
    pallas_call x1, Pallas kernels, make_second(): pl.pallas_call(second_kernel, grid=(STEPS,), in_specs=[plane_spec()] + [w...  3.67 us
  transfers between devices with their start and end apart: 25, of which 14 were waited for; matrix products, arithmetic and copies ran while one was open for 2% of the time, Pallas kernels for 13%

profile of v13, /device:TPU:0, one launch (start us, length us, event | category | flops | bytes accessed | tf_op | source)
XLA Modules:
  0.0 156.2 jit_solution(1562456648450992103)
XLA Ops:
  0.0 0.9 copy.7
  2.7 1.0 reshape.34.refs_1_
  3.8 2.0 %collective-permute-start = (f32[56,128]{1,0:T(8,128)S(1)}, f32[56,128]{1,0:T(8,128)S(1)}, u32[]{:S(2)}, u32[]{:S(2)}) collective-permute-start(f32[56,128]{1,0:T(8,128)S(1)} %stack.15.refs_0_.parcel_ref), channel_id=1, source_target_pairs={{0,32},{1,33},{2,34},{3,35},{4,36},{5,37},{6,38},{7,39},{8,40},{9,... | collective-permute-start | bytes 86024 | tf_op jit(solution)/shard_map/ppermute | solution.py:766
  5.8 1.6 %copy-done = f32[16,16,16,128]{3,2,1,0:T(8,128)S(1)} copy-done((f32[16,16,16,128]{3,2,1,0:T(8,128)S(1)}, f32[16,16,16,128]{3,2,1,0:T(8,128)}, u32[]{:S(2)}) %copy-start) | copy-done | bytes 2097176
  8.2 1.6 collective-permute-start.1
  9.8 6.8 %collective-permute-start.2 = (f32[48,128]{1,0:T(8,128)S(1)}, f32[48,128]{1,0:T(8,128)S(1)}, u32[]{:S(2)}, u32[]{:S(2)}) collective-permute-start(f32[48,128]{1,0:T(8,128)S(1)} %stack.16.refs_1_), channel_id=1, source_target_pairs={{0,31},{1,0},{2,1},{3,2},{4,3},{5,4},{6,5},{7,6},{8,7},{9,8},{10,9... | collective-permute-start | bytes 73736 | tf_op jit(solution)/shard_map/ppermute | solution.py:766
  18.8 1.5 side_x.1.part_ref
  20.3 1.5 collective-permute-start.6
  21.8 7.8 %collective-permute-start.11 = (f32[6,16,16,128]{3,2,1,0:T(8,128)S(1)}, f32[6,16,16,128]{3,2,1,0:T(8,128)S(1)}, u32[]{:S(2)}, u32[]{:S(2)}) collective-permute-start(f32[6,16,16,128]{3,2,1,0:T(8,128)S(1)} %get-tuple-element.62), channel_id=1, source_target_pairs={{0,31},{1,0},{2,1},{3,2},{4,3},{5,4},{6,5},{7,6},{8,7},{9,8},{10,9... | collective-permute-start | bytes 2359304 | tf_op jit(solution)/shard_map/ppermute | solution.py:766
  31.4 22.5 %collective-permute-done.5.refs_0_ = f32[8,192,128]{2,1,0:T(8,128)S(1)} collective-permute-done((f32[8,192,128]{2,1,0:T(8,128)S(1)}, f32[8,192,128]{2,1,0:T(8,128)S(1)}, u32[]{:S(2)}, u32[]{:S(2)}) %collective-permute-start.5) | collective-permute-done | bytes 786464 | tf_op jit(solution)/shard_map/ppermute | solution.py:766
  53.9 7.8 %prep.1 = (bf16[2,4096,128]{2,1,0:T(8,128)(2,1)S(1)}, f32[3,48,128]{2,1,0:T(8,128)S(1)}, f32[48,128]{1,0:T(8,128)S(1)}) custom-call(f32[144,128]{1,0:T(8,128)S(1)} %stack.17.refs_0_, f32[144,128]{1,0:T(8,128)S(1)} %collective-permute-done.3.refs_1_, s32[2]{0:T(128)S(1)} %pad_add_fusion.refs_2_, f32[4096,128]{1,0:T(8,128)S(1)} %spread.2.refs_3_, ...), custom_call_target="tpu_custom_call" | custom-call | flops 134217728 | bytes 10485760 | tf_op jit(solution)/shard_map/prep/pallas_call | solution.py:462
  61.7 1.3 collective-permute-start.13
  63.1 1.3 collective-permute-done.7
  64.4 1.0 collective-permute-start.8
  65.4 2.9 %side_z.1.side_ref = f32[16,256,128]{2,1,0:T(8,128)S(1)} custom-call(f32[16,256,128]{2,1,0:T(8,128)S(1)} %bitcast.17, f32[16,256,128]{2,1,0:T(8,128)S(1)} %side_x.1.part_ref, f32[6,16,16,128]{3,2,1,0:T(8,128)S(1)} %collective-permute-done.10.low_ref, f32[6,16,16,128]{3,2,1,0:T(8,128)S(1)} %collective-permute-done.11.high_ref), custom_call_target="tpu_custom_call" | custom-call | flops 16777216 | bytes 8388608 | tf_op jit(solution)/shard_map/side_z/pallas_call | solution.py:275
  68.2 3.0 %collective-permute-done.8.refs_5_.rest_1_ = f32[3,48,128]{2,1,0:T(8,128)S(1)} collective-permute-done((f32[3,48,128]{2,1,0:T(8,128)S(1)}, f32[3,48,128]{2,1,0:T(8,128)S(1)}, u32[]{:S(2)}, u32[]{:S(2)}) %collective-permute-start.8) | collective-permute-done | bytes 73760 | tf_op jit(solution)/shard_map/ppermute | solution.py:766
  71.3 5.6 %collective-permute-done.13.refs_2_ = f32[6,192,128]{2,1,0:T(8,128)S(1)} collective-permute-done((f32[6,192,128]{2,1,0:T(8,128)S(1)}, f32[6,192,128]{2,1,0:T(8,128)S(1)}, u32[]{:S(2)}, u32[]{:S(2)}) %collective-permute-start.13) | collective-permute-done | bytes 589856 | tf_op jit(solution)/shard_map/ppermute | solution.py:802
  76.9 2.1 %first.1 = (f32[16,256,128]{2,1,0:T(8,128)S(1)}, f32[16,256,128]{2,1,0:T(8,128)S(1)}, f32[1632,128]{1,0:T(8,128)S(1)}, f32[1632,128]{1,0:T(8,128)S(1)}) custom-call(f32[16,256,128]{2,1,0:T(8,128)S(1)} %bitcast.18, f32[16,256,128]{2,1,0:T(8,128)S(1)} %side_z.1.side_ref, f32[16,256,128]{2,1,0:T(8,128)S(1)} %bitcast.20, ...), custom_call_target="tpu_custom_call" | custom-call | flops 16777216 | bytes 14680064 | tf_op jit(solution)/shard_map/first/pallas_call | solution.py:521
  79.2 7.7 %collective-permute-start.16 = (f32[1632,128]{1,0:T(8,128)S(1)}, f32[1632,128]{1,0:T(8,128)S(1)}, u32[]{:S(2)}, u32[]{:S(2)}) collective-permute-start(f32[1632,128]{1,0:T(8,128)S(1)} %get-tuple-element.69), channel_id=1, source_target_pairs={{0,31},{1,0},{2,1},{3,2},{4,3},{5,4},{6,5},{7,6},{8,7},{9,8},{10,9... | collective-permute-start | bytes 2506760 | tf_op jit(solution)/shard_map/ppermute | solution.py:766
  88.4 2.9 %side_again.1.part_ref = f32[16,256,128]{2,1,0:T(8,128)S(1)} custom-call(f32[16,256,128]{2,1,0:T(8,128)S(1)} %get-tuple-element.67.s_ref, f32[16,256,128]{2,1,0:T(8,128)S(1)} %collective-permute-done.14.mate_ref), custom_call_target="tpu_custom_call" | custom-call | flops 33554432 | bytes 6291456 | tf_op jit(solution)/shard_map/side_again/pallas_call | solution.py:302
  91.4 3.0 %base.1.base_ref = f32[16,256,128]{2,1,0:T(8,128)S(1)} custom-call(f32[16,256,128]{2,1,0:T(8,128)S(1)} %bitcast.19, f32[16,64,128]{2,1,0:T(8,128)S(1)} %collective-permute-done.9.mid_ref, f32[16,256,128]{2,1,0:T(8,128)S(1)} %bitcast.21, f32[16,256,128]{2,1,0:T(8,128)S(1)} %bitcast.24, f32[16,256,128]{2,1,0:T(8,128)S(1)} %get-tuple-element.66.q_ref, ...), custom_call_target="tpu_custom_call" | custom-call | flops 33554432 | bytes 16777216 | tf_op jit(solution)/shard_map/base/pallas_call | solution.py:573
  94.3 11.5 %collective-permute-done.15.low_ref = f32[1632,128]{1,0:T(8,128)S(1)} collective-permute-done((f32[1632,128]{1,0:T(8,128)S(1)}, f32[1632,128]{1,0:T(8,128)S(1)}, u32[]{:S(2)}, u32[]{:S(2)}) %collective-permute-start.15) | collective-permute-done | bytes 835616 | tf_op jit(solution)/shard_map/ppermute | solution.py:766
  105.8 3.7 %second.1 = (f32[16,256,128]{2,1,0:T(8,128)S(1)}, f32[64,128]{1,0:T(8,128)S(1)}, f32[64,128]{1,0:T(8,128)S(1)}) custom-call(f32[16,256,128]{2,1,0:T(8,128)S(1)} %base.1.base_ref, f32[1632,128]{1,0:T(8,128)S(1)} %collective-permute-done.15.low_ref, f32[1632,128]{1,0:T(8,128)S(1)} %collective-permute-done.16.high_ref, bf16[2,16,256,128]{3,2,1,0:T(8,128)(2,1)S(1)} %bitcast.22, ...), custom_call_target="tpu_custom_call" | custom-call | flops 134217728 | bytes 8388608 | tf_op jit(solution)/shard_map/second/pallas_call | solution.py:644
  109.6 1.2 collective-permute-done.17
  110.8 3.9 %collective-permute-done.18 = f32[64,128]{1,0:T(8,128)S(1)} collective-permute-done((f32[64,128]{1,0:T(8,128)S(1)}, f32[64,128]{1,0:T(8,128)S(1)}, u32[]{:S(2)}, u32[]{:S(2)}) %collective-permute-start.18) | collective-permute-done | bytes 32800 | tf_op jit(solution)/shard_map/ppermute | solution.py:822
  114.8 5.1 %collective-permute-done.19 = f32[64,128]{1,0:T(8,128)S(1)} collective-permute-done((f32[64,128]{1,0:T(8,128)S(1)}, f32[64,128]{1,0:T(8,128)S(1)}, u32[]{:S(2)}, u32[]{:S(2)}) %collective-permute-start.19) | collective-permute-done | bytes 32800 | tf_op jit(solution)/shard_map/ppermute | solution.py:822
  119.9 3.9 %collective-permute-done.20 = f32[64,128]{1,0:T(8,128)S(1)} collective-permute-done((f32[64,128]{1,0:T(8,128)S(1)}, f32[64,128]{1,0:T(8,128)S(1)}, u32[]{:S(2)}, u32[]{:S(2)}) %collective-permute-start.20) | collective-permute-done | bytes 32800 | tf_op jit(solution)/shard_map/ppermute | solution.py:822
  124.6 4.4 %collective-permute-done.21 = f32[64,128]{1,0:T(8,128)S(1)} collective-permute-done((f32[64,128]{1,0:T(8,128)S(1)}, f32[64,128]{1,0:T(8,128)S(1)}, u32[]{:S(2)}, u32[]{:S(2)}) %collective-permute-start.21) | collective-permute-done | bytes 32800 | tf_op jit(solution)/shard_map/ppermute | solution.py:822
  128.9 3.9 %collective-permute-done.22 = f32[64,128]{1,0:T(8,128)S(1)} collective-permute-done((f32[64,128]{1,0:T(8,128)S(1)}, f32[64,128]{1,0:T(8,128)S(1)}, u32[]{:S(2)}, u32[]{:S(2)}) %collective-permute-start.22) | collective-permute-done | bytes 32800 | tf_op jit(solution)/shard_map/ppermute | solution.py:822
  133.8 4.2 %collective-permute-done.23 = f32[64,128]{1,0:T(8,128)S(1)} collective-permute-done((f32[64,128]{1,0:T(8,128)S(1)}, f32[64,128]{1,0:T(8,128)S(1)}, u32[]{:S(2)}, u32[]{:S(2)}) %collective-permute-start.23) | collective-permute-done | bytes 32800 | tf_op jit(solution)/shard_map/ppermute | solution.py:822
  138.0 1.2 collective-permute-done.24.other_ref
  139.2 17.0 %turn.1 = f32[16,256,128]{2,1,0:T(8,128)} custom-call(f32[16,256,128]{2,1,0:T(8,128)S(1)} %get-tuple-element.74.second_ref, f32[64,128]{1,0:T(8,128)S(1)} %add.41.own_ref, f32[64,128]{1,0:T(8,128)S(1)} %collective-permute-done.24.other_ref, s32[1]{0:T(128)} %bitcast.3.rest_3_.upper_ref), custom_call_target="tpu_custom_call" | custom-call | flops 268435456 | bytes 4194304 | tf_op jit(solution)/shard_map/turn/pallas_call | solution.py:743
  (55 shorter events, 10.1 us)
Async XLA Ops:
  0.0 18.7 %collective-permute-start.4 = (f32[16,256,128]{2,1,0:T(8,128)}, f32[16,256,128]{2,1,0:T(8,128)S(1)}, u32[]{:S(2)}, u32[]{:S(2)}) collective-permute-start(f32[16,256,128]{2,1,0:T(8,128)} %bitcast.12), channel_id=1, source_target_pairs={{0,64},{1,65},{2,66},{3,67},{4,68},{5,69},{6,70},{7,71},{8,72},{9,... | collective-permute-start | bytes 6291464 | tf_op jit(solution)/shard_map/ppermute | solution.py:766
  3.8 4.4 %collective-permute-start = (f32[56,128]{1,0:T(8,128)S(1)}, f32[56,128]{1,0:T(8,128)S(1)}, u32[]{:S(2)}, u32[]{:S(2)}) collective-permute-start(f32[56,128]{1,0:T(8,128)S(1)} %stack.15.refs_0_.parcel_ref), channel_id=1, source_target_pairs={{0,32},{1,33},{2,34},{3,35},{4,36},{5,37},{6,38},{7,39},{8,40},{9,... | collective-permute-start | bytes 86024 | tf_op jit(solution)/shard_map/ppermute | solution.py:766
  5.8 1.6 %copy-start = (f32[16,16,16,128]{3,2,1,0:T(8,128)S(1)}, f32[16,16,16,128]{3,2,1,0:T(8,128)}, u32[]{:S(2)}) copy-start(f32[16,16,16,128]{3,2,1,0:T(8,128)} %param.5) | copy-start | bytes 6291460
  8.2 10.1 %collective-permute-start.1 = (f32[48,128]{1,0:T(8,128)S(1)}, f32[48,128]{1,0:T(8,128)S(1)}, u32[]{:S(2)}, u32[]{:S(2)}) collective-permute-start(f32[48,128]{1,0:T(8,128)S(1)} %stack.16.refs_1_), channel_id=1, source_target_pairs={{0,1},{1,2},{2,3},{3,4},{4,5},{5,6},{6,7},{7,8},{8,9},{9,10},{10,1... | collective-permute-start | bytes 73736 | tf_op jit(solution)/shard_map/ppermute | solution.py:766
  9.8 8.5 %collective-permute-start.2 = (f32[48,128]{1,0:T(8,128)S(1)}, f32[48,128]{1,0:T(8,128)S(1)}, u32[]{:S(2)}, u32[]{:S(2)}) collective-permute-start(f32[48,128]{1,0:T(8,128)S(1)} %stack.16.refs_1_), channel_id=1, source_target_pairs={{0,31},{1,0},{2,1},{3,2},{4,3},{5,4},{6,5},{7,6},{8,7},{9,8},{10,9... | collective-permute-start | bytes 73736 | tf_op jit(solution)/shard_map/ppermute | solution.py:766
  16.6 37.3 %collective-permute-start.5 = (f32[8,192,128]{2,1,0:T(8,128)S(1)}, f32[8,192,128]{2,1,0:T(8,128)S(1)}, u32[]{:S(2)}, u32[]{:S(2)}) collective-permute-start(f32[8,192,128]{2,1,0:T(8,128)S(1)} %get-tuple-element.53), channel_id=1, source_target_pairs={{0,32},{1,33},{2,34},{3,35},{4,36},{5,37},{6,38},{7,39},{8,40},{9,... | collective-permute-start | bytes 2359304 | tf_op jit(solution)/shard_map/ppermute | solution.py:766
  18.3 1.9 %collective-permute-start.3 = (f32[144,128]{1,0:T(8,128)S(1)}, f32[144,128]{1,0:T(8,128)S(1)}, u32[]{:S(2)}, u32[]{:S(2)}) collective-permute-start(f32[144,128]{1,0:T(8,128)S(1)} %stack.17.refs_0_), channel_id=1, source_target_pairs={{0,64},{1,65},{2,66},{3,67},{4,68},{5,69},{6,70},{7,71},{8,72},{9,... | collective-permute-start | bytes 221192 | tf_op jit(solution)/shard_map/ppermute | solution.py:766
  20.2 33.6 %copy-start.1 = (f32[16,16,16,128]{3,2,1,0:T(8,128)S(1)}, f32[16,16,16,128]{3,2,1,0:T(8,128)}, u32[]{:S(2)}) copy-start(f32[16,16,16,128]{3,2,1,0:T(8,128)} %param.5) | copy-start | bytes 6291460
  20.3 41.4 %collective-permute-start.6 = (f32[6,192,128]{2,1,0:T(8,128)S(1)}, f32[6,192,128]{2,1,0:T(8,128)S(1)}, u32[]{:S(2)}, u32[]{:S(2)}) collective-permute-start(f32[6,192,128]{2,1,0:T(8,128)S(1)} %get-tuple-element.57), channel_id=1, source_target_pairs={{0,33},{3,34},{4,37},{7,38},{8,41},{11,42},{12,45},{15,46},{16,49}... | collective-permute-start | bytes 1769480 | tf_op jit(solution)/shard_map/ppermute | solution.py:796
  21.7 43.6 %collective-permute-start.10 = (f32[6,16,16,128]{3,2,1,0:T(8,128)S(1)}, f32[6,16,16,128]{3,2,1,0:T(8,128)S(1)}, u32[]{:S(2)}, u32[]{:S(2)}) collective-permute-start(f32[6,16,16,128]{3,2,1,0:T(8,128)S(1)} %get-tuple-element.61), channel_id=1, source_target_pairs={{0,1},{1,2},{2,3},{3,4},{4,5},{5,6},{6,7},{7,8},{8,9},{9,10},{10,1... | collective-permute-start | bytes 2359304 | tf_op jit(solution)/shard_map/ppermute | solution.py:766
  21.8 43.6 %collective-permute-start.11 = (f32[6,16,16,128]{3,2,1,0:T(8,128)S(1)}, f32[6,16,16,128]{3,2,1,0:T(8,128)S(1)}, u32[]{:S(2)}, u32[]{:S(2)}) collective-permute-start(f32[6,16,16,128]{3,2,1,0:T(8,128)S(1)} %get-tuple-element.62), channel_id=1, source_target_pairs={{0,31},{1,0},{2,1},{3,2},{4,3},{5,4},{6,5},{7,6},{8,7},{9,8},{10,9... | collective-permute-start | bytes 2359304 | tf_op jit(solution)/shard_map/ppermute | solution.py:766
  29.6 41.7 %collective-permute-start.12 = (f32[1536,128]{1,0:T(8,128)S(1)}, f32[1536,128]{1,0:T(8,128)S(1)}, u32[]{:S(2)}, u32[]{:S(2)}) collective-permute-start(f32[1536,128]{1,0:T(8,128)S(1)} %get-tuple-element.64), channel_id=1, source_target_pairs={{0,32},{1,33},{2,34},{3,35},{4,36},{5,37},{6,38},{7,39},{8,40},{9,... | collective-permute-start | bytes 2359304 | tf_op jit(solution)/shard_map/ppermute | solution.py:766
  61.7 15.2 %collective-permute-start.13 = (f32[6,192,128]{2,1,0:T(8,128)S(1)}, f32[6,192,128]{2,1,0:T(8,128)S(1)}, u32[]{:S(2)}, u32[]{:S(2)}) collective-permute-start(f32[6,192,128]{2,1,0:T(8,128)S(1)} %collective-permute-done.6), channel_id=1, source_target_pairs={{1,0},{2,3},{5,4},{6,7},{9,8},{10,11},{13,12},{14,15},{17,16},{18,... | collective-permute-start | bytes 1769480 | tf_op jit(solution)/shard_map/ppermute | solution.py:802
  63.0 1.3 collective-permute-start.7
  64.4 6.9 %collective-permute-start.8 = (f32[3,48,128]{2,1,0:T(8,128)S(1)}, f32[3,48,128]{2,1,0:T(8,128)S(1)}, u32[]{:S(2)}, u32[]{:S(2)}) collective-permute-start(f32[3,48,128]{2,1,0:T(8,128)S(1)} %add.34.refs_4_.rest_0_), channel_id=1, source_target_pairs={{0,32},{1,33},{2,34},{3,35},{4,36},{5,37},{6,38},{7,39},{8,40},{9,... | collective-permute-start | bytes 221192 | tf_op jit(solution)/shard_map/ppermute | solution.py:766
  79.0 9.4 %collective-permute-start.14 = (f32[16,256,128]{2,1,0:T(8,128)S(1)}, f32[16,256,128]{2,1,0:T(8,128)S(1)}, u32[]{:S(2)}, u32[]{:S(2)}) collective-permute-start(f32[16,256,128]{2,1,0:T(8,128)S(1)} %get-tuple-element.67.s_ref), channel_id=1, source_target_pairs={{0,64},{1,65},{2,66},{3,67},{4,68},{5,69},{6,70},{7,71},{8,72},{9,... | collective-permute-start | bytes 6291464 | tf_op jit(solution)/shard_map/ppermute | solution.py:766
  79.1 26.7 %collective-permute-start.15 = (f32[1632,128]{1,0:T(8,128)S(1)}, f32[1632,128]{1,0:T(8,128)S(1)}, u32[]{:S(2)}, u32[]{:S(2)}) collective-permute-start(f32[1632,128]{1,0:T(8,128)S(1)} %get-tuple-element.68), channel_id=1, source_target_pairs={{0,1},{1,2},{2,3},{3,4},{4,5},{5,6},{6,7},{7,8},{8,9},{9,10},{10,1... | collective-permute-start | bytes 2506760 | tf_op jit(solution)/shard_map/ppermute | solution.py:766
  79.2 26.7 %collective-permute-start.16 = (f32[1632,128]{1,0:T(8,128)S(1)}, f32[1632,128]{1,0:T(8,128)S(1)}, u32[]{:S(2)}, u32[]{:S(2)}) collective-permute-start(f32[1632,128]{1,0:T(8,128)S(1)} %get-tuple-element.69), channel_id=1, source_target_pairs={{0,31},{1,0},{2,1},{3,2},{4,3},{5,4},{6,5},{7,6},{8,7},{9,8},{10,9... | collective-permute-start | bytes 2506760 | tf_op jit(solution)/shard_map/ppermute | solution.py:766
  86.9 4.5 %collective-permute-start.9 = (f32[16,64,128]{2,1,0:T(8,128)S(1)}, f32[16,64,128]{2,1,0:T(8,128)S(1)}, u32[]{:S(2)}, u32[]{:S(2)}) collective-permute-start(f32[16,64,128]{2,1,0:T(8,128)S(1)} %get-tuple-element.59), channel_id=1, source_target_pairs={{1,33},{2,34},{5,37},{6,38},{9,41},{10,42},{13,45},{14,46},{17,49}... | collective-permute-start | bytes 1572872 | tf_op jit(solution)/shard_map/ppermute | solution.py:813
  109.5 1.3 collective-permute-start.17
  110.8 3.9 %collective-permute-start.18 = (f32[64,128]{1,0:T(8,128)S(1)}, f32[64,128]{1,0:T(8,128)S(1)}, u32[]{:S(2)}, u32[]{:S(2)}) collective-permute-start(f32[64,128]{1,0:T(8,128)S(1)} %add.35), channel_id=1, source_target_pairs={{0,32},{1,33},{2,34},{3,35},{4,36},{5,37},{6,38},{7,39},{8,40},{9,... | collective-permute-start | bytes 98312 | tf_op jit(solution)/shard_map/ppermute | solution.py:822
  114.7 5.1 %collective-permute-start.19 = (f32[64,128]{1,0:T(8,128)S(1)}, f32[64,128]{1,0:T(8,128)S(1)}, u32[]{:S(2)}, u32[]{:S(2)}) collective-permute-start(f32[64,128]{1,0:T(8,128)S(1)} %add.36), channel_id=1, source_target_pairs={{0,36},{1,37},{2,38},{3,39},{4,32},{5,33},{6,34},{7,35},{8,44},{9,... | collective-permute-start | bytes 98312 | tf_op jit(solution)/shard_map/ppermute | solution.py:822
  119.9 3.9 %collective-permute-start.20 = (f32[64,128]{1,0:T(8,128)S(1)}, f32[64,128]{1,0:T(8,128)S(1)}, u32[]{:S(2)}, u32[]{:S(2)}) collective-permute-start(f32[64,128]{1,0:T(8,128)S(1)} %add.37), channel_id=1, source_target_pairs={{0,1},{1,0},{2,3},{3,2},{4,5},{5,4},{6,7},{7,6},{8,9},{9,8},{10,11... | collective-permute-start | bytes 98312 | tf_op jit(solution)/shard_map/ppermute | solution.py:822
  123.8 5.1 %collective-permute-start.21 = (f32[64,128]{1,0:T(8,128)S(1)}, f32[64,128]{1,0:T(8,128)S(1)}, u32[]{:S(2)}, u32[]{:S(2)}) collective-permute-start(f32[64,128]{1,0:T(8,128)S(1)} %add.38), channel_id=1, source_target_pairs={{0,3},{1,2},{2,1},{3,0},{4,7},{5,6},{6,5},{7,4},{8,11},{9,10},{10,... | collective-permute-start | bytes 98312 | tf_op jit(solution)/shard_map/ppermute | solution.py:822
  128.9 3.9 %collective-permute-start.22 = (f32[64,128]{1,0:T(8,128)S(1)}, f32[64,128]{1,0:T(8,128)S(1)}, u32[]{:S(2)}, u32[]{:S(2)}) collective-permute-start(f32[64,128]{1,0:T(8,128)S(1)} %add.39), channel_id=1, source_target_pairs={{0,8},{1,9},{2,10},{3,11},{4,12},{5,13},{6,14},{7,15},{8,0},{9,1},... | collective-permute-start | bytes 98312 | tf_op jit(solution)/shard_map/ppermute | solution.py:822
  132.8 5.1 %collective-permute-start.23 = (f32[64,128]{1,0:T(8,128)S(1)}, f32[64,128]{1,0:T(8,128)S(1)}, u32[]{:S(2)}, u32[]{:S(2)}) collective-permute-start(f32[64,128]{1,0:T(8,128)S(1)} %add.40), channel_id=1, source_target_pairs={{0,24},{1,25},{2,26},{3,27},{4,28},{5,29},{6,30},{7,31},{8,16},{9,... | collective-permute-start | bytes 98312 | tf_op jit(solution)/shard_map/ppermute | solution.py:822
  138.0 1.2 collective-permute-start.24

commit v14 on v13

--- a/solution.py
+++ b/solution.py
@@ -74,7 +74,7 @@
 B = 4
 STEPS = C // B
 N = 2
-FIRST = 8
+FIRST = 4
 MIDDLE = 10
 EDGE = 192
 MID = 64
@@ -148,7 +148,11 @@
     out_ref[:, 96:192, :] = s_ref[:, 160:256, :]
 
 
-def pack_kernel(s_ref, edge_ref, head_ref, tail_ref):
+def pack_kernel(s_ref, edge_ref, relay_ref, head_ref, tail_ref):
+    @pl.when(pl.program_id(0) >= MIDDLE // N)
+    def _():
+        pack_edges(s_ref, relay_ref)
+
     @pl.when(pl.program_id(0) < FIRST // N)
     def _():
         pack_edges(s_ref, edge_ref)
@@ -164,22 +168,18 @@
         pack_kernel,
         grid=(C // N,),
         in_specs=[plane_spec(ROWS, N)],
-        out_specs=edge_specs()[:1] + [halo_spec(N), halo_spec(N)],
-        out_shape=EDGES[:1] + [HALO, HALO],
+        out_specs=[edge_spec(0, FIRST), edge_spec(MIDDLE, C), halo_spec(N), halo_spec(N)],
+        out_shape=[EDGES[0], EDGES[2], HALO, HALO],
         compiler_params=params(12),
         cost_estimate=cost(1 << 32, 6 << 20),
         name="pack",
     )(s)
 
 
-def pack_rest_kernel(s_ref, inner_ref, message_ref, relay_ref, mid_ref):
+def pack_rest_kernel(s_ref, inner_ref, message_ref, mid_ref):
     step = pl.program_id(0)
     inner = inner_ref[0] == 1
     mid_ref[...] = s_ref[:, 96:160, :]
-
-    @pl.when(step >= MIDDLE // N)
-    def _():
-        pack_edges(s_ref, relay_ref)
 
     @pl.when((step >= FIRST // N) & (inner | (step < MIDDLE // N)))
     def _():
@@ -197,17 +197,16 @@
 
 def pack_rest(s, inner):
     rows = (C - FIRST) * EDGE
-    message, relay, mid = pl.pallas_call(
+    return pl.pallas_call(
         pack_rest_kernel,
         grid=(C // N,),
         in_specs=[plane_spec(ROWS, N), SCALARS],
-        out_specs=[whole(rows), edge_spec(MIDDLE, C), plane_spec(MID, N)],
-        out_shape=[sds((rows, S)), EDGES[2], sds((C, MID, S))],
+        out_specs=[whole(rows), plane_spec(MID, N)],
+        out_shape=[sds((rows, S)), sds((C, MID, S))],
         compiler_params=params(12),
         cost_estimate=cost(1 << 31, 4 << 20),
         name="pack_rest",
     )(s, inner)
-    return message, relay, mid
 
 
 def stack(*pieces):
@@ -771,35 +770,36 @@
     inner = ((lax.axis_index("gzs") + 1) // 2 % 2).astype(jnp.int32).reshape(1)
     s = states.reshape(C, ROWS, S)
     mate = send(s, over_x)
-    pot = potential.reshape(32, 128)
     corner = jnp.stack([gx * C, gy * C]).astype(jnp.int32)
     upper = gx.astype(jnp.int32).reshape(1)
+    to_pack, corner, upper, inner = barrier((s, corner, upper, inner))
+    one_edge, relay, head, tail = pack(to_pack)
+    one_edge = send(one_edge, over_y)
+    relayed = lax.ppermute(relay, AXES, [(d, d ^ over_y ^ 1) for d in outer_ones])
+
+    pot = potential.reshape(32, 128)
     atoms = jnp.concatenate(
         [projectors.reshape(4, TAPS), atom_sites.astype(F32), energies[:, None], jnp.zeros((4, 768 - TAPS - 4), F32)],
         axis=1,
     ).reshape(24, 128)
-    to_pack, pot, corner, upper, inner, atoms = barrier((s, pot, corner, upper, inner, atoms))
-
     parcel = stack((atoms, 24), (pot, 32))
     parcel_mate = send(parcel, over_y)
-    one_edge, head, tail = pack(to_pack)
-    one_edge = send(one_edge, over_y)
-    parcel_mate, head = barrier((parcel_mate, head))
+    message, mid = pack_rest(s, inner)
+    parcel_mate, one_edge, message = barrier((parcel_mate, one_edge, message))
+    message = send(message, over_y)
     pair = stack((parcel, 24), (parcel_mate, 24))
     column = stack((send(pair, 0, 1), 48), (pair, 48), (send(pair, 0, -1), 48))
+    column, head, tail = barrier((column, head, tail))
+    low, high = send(tail, 0, 1), send(head, 0, -1)
+    column, relayed = barrier((column, relayed))
     column_mate = send(column, over_x)
-    message, relay, mid = pack_rest(s, inner)
     vb = spread(parcel)
     beside = side_x(s, mate)
-    column_mate, head, tail, relay, message, beside = barrier((column_mate, head, tail, relay, message, beside))
-    low, high = send(tail, 0, 1), send(head, 0, -1)
-    relayed = lax.ppermute(relay, AXES, [(d, d ^ over_y ^ 1) for d in outer_ones])
-    message = send(message, over_y)
-    column_mate, one_edge = barrier((column_mate, one_edge))
+    column_mate, beside = barrier((column_mate, beside))
     gg, part, energy = prep([column, column_mate], corner, vb, s)
     part, relayed = barrier((part, relayed))
+    relayed = lax.ppermute(relayed, AXES, [(d, d ^ 1) for d in inner_ones])
     side_part = side_z(s, beside, low, high)
-    relayed = lax.ppermute(relayed, AXES, [(d, d ^ 1) for d in inner_ones])
     planes = vb.reshape(C, ROWS, S)
 
     part = part + send(part, over_x)

time: 157 us -> 156 us (level)
  waiting for transfers between devices: 72.6 us -> 56.4 us
  starting transfers between devices: 34.4 us -> 45.4 us
  Pallas kernels: 43.5 us -> 46.5 us
    ppermute x16, waiting for transfers between devices: 41.6 us -> 22.9 us  [send(): return lax.ppermute(value, AXES, [(d, target(d)) for d in range(count)])]
    ppermute x16, starting transfers between devices: 29.3 us -> 34.7 us  [send(): return lax.ppermute(value, AXES, [(d, target(d)) for d in range(count)])]
    ppermute x1, waiting for transfers between devices: 5.6 us -> 10.1 us  [per_device(): relayed = lax.ppermute(relayed, AXES, [(d, d ^ 1) for d in inner_ones])]
    ppermute x1, starting transfers between devices: 1.46 us -> 4.99 us  [per_device(): lax.ppermute(relay, AXES, [(d, d ^ over_y ^ 1) for d in outer_ones])]
    ppermute x6, starting transfers between devices: 1.69 us -> 3.67 us  [per_device(): own = own + lax.ppermute(own, AXES, [(d, d ^ flip) for d in range(count)])]
    ppermute x6, waiting for transfers between devices: 25.4 us -> 23.4 us  [per_device(): own = own + lax.ppermute(own, AXES, [(d, d ^ flip) for d in range(count)])]
    pallas_call x1, Pallas kernels: 1.47 us -> 3.05 us  [side_x(): pl.pallas_call(side_x_kernel, out_shape=FULL, compiler_params=params(12),...]
    unnamed x5 -> x19, local copies, waits for them, and re-layouts: 2.54 us -> 4.04 us
  transfers between devices with their start and end apart: 25 -> 25, of which waited for: 14 -> 16; matrix products, arithmetic and copies ran while one was open for 2% -> 1% of each run, Pallas kernels for 13% -> 15%
where the time goes in v14:
time: 156 us; the launch traced here: 154 us
  waiting for transfers between devices  56.4 us (36%)
  Pallas kernels  46.5 us (30%)
  starting transfers between devices  45.4 us (29%)
  local copies, waits for them, and re-layouts  5.44 us (3%)
    ppermute x16, starting transfers between devices, send(): return lax.ppermute(value, AXES, [(d, target(d)) for d in range(count)])  34.7 us
    ppermute x6, waiting for transfers between devices, per_device(): own = own + lax.ppermute(own, AXES, [(d, d ^ flip) for d in range(count)])  23.4 us
    ppermute x16, waiting for transfers between devices, send(): return lax.ppermute(value, AXES, [(d, target(d)) for d in range(count)])  22.9 us
    pallas_call x1, Pallas kernels, turn(): pl.pallas_call(turn_kernel, grid=(STEPS,), in_specs=[plane_spec(), whole(...  17 us
    ppermute x1, waiting for transfers between devices, per_device(): relayed = lax.ppermute(relayed, AXES, [(d, d ^ 1) for d in inner_ones])  10.1 us
    pallas_call x1, Pallas kernels, prep(): pl.pallas_call(prep_kernel, in_specs=[vmem] * 2 + [pl.BlockSpec(memory_sp...  7.8 us
    ppermute x1, starting transfers between devices, per_device(): lax.ppermute(relay, AXES, [(d, d ^ over_y ^ 1) for d in outer_ones])  4.99 us
    unnamed x19, local copies, waits for them, and re-layouts  4.04 us
  transfers between devices with their start and end apart: 25, of which 16 were waited for; matrix products, arithmetic and copies ran while one was open for 1% of the time, Pallas kernels for 15%

profile of v14, /device:TPU:0, one launch (start us, length us, event | category | flops | bytes accessed | tf_op | source)
XLA Modules:
  0.0 154.2 jit_solution(6249727263307746420)
XLA Ops:
  0.1 1.6 %copy-done = f32[16,16,16,128]{3,2,1,0:T(8,128)S(1)} copy-done((f32[16,16,16,128]{3,2,1,0:T(8,128)S(1)}, f32[16,16,16,128]{3,2,1,0:T(8,128)}, u32[]{:S(2)}) %copy-start) | copy-done | bytes 2097176
  1.7 2.1 %pack.1 = (f32[4,192,128]{2,1,0:T(8,128)}, f32[6,192,128]{2,1,0:T(8,128)S(1)}, f32[6,16,16,128]{3,2,1,0:T(8,128)S(1)}, f32[6,16,16,128]{3,2,1,0:T(8,128)S(1)}) custom-call(f32[16,256,128]{2,1,0:T(8,128)S(1)} %bitcast.13), custom_call_target="tpu_custom_call" | custom-call | flops 4294967296 | bytes 6291456 | tf_op jit(solution)/shard_map/pack/pallas_call | solution.py:167
  5.5 2.0 %collective-permute-start.1 = (f32[4,192,128]{2,1,0:T(8,128)}, f32[4,192,128]{2,1,0:T(8,128)S(1)}, u32[]{:S(2)}, u32[]{:S(2)}) collective-permute-start(f32[4,192,128]{2,1,0:T(8,128)} %get-tuple-element.42), channel_id=1, source_target_pairs={{0,32},{1,33},{2,34},{3,35},{4,36},{5,37},{6,38},{7,39},{8,40},{9,... | collective-permute-start | bytes 1179656 | tf_op jit(solution)/shard_map/ppermute | solution.py:765
  9.9 5.0 %collective-permute-start.4 = (f32[6,192,128]{2,1,0:T(8,128)}, f32[6,192,128]{2,1,0:T(8,128)S(1)}, u32[]{:S(2)}, u32[]{:S(2)}) collective-permute-start(f32[6,192,128]{2,1,0:T(8,128)} %copy-done.4), channel_id=1, source_target_pairs={{0,33},{3,34},{4,37},{7,38},{8,41},{11,42},{12,45},{15,46},{16,49}... | collective-permute-start | bytes 1769480 | tf_op jit(solution)/shard_map/ppermute | solution.py:778
  15.1 3.0 %collective-permute-done.refs_1_.parcel_ref = f32[56,128]{1,0:T(8,128)S(1)} collective-permute-done((f32[56,128]{1,0:T(8,128)S(1)}, f32[56,128]{1,0:T(8,128)S(1)}, u32[]{:S(2)}, u32[]{:S(2)}) %collective-permute-start) | collective-permute-done | bytes 28704 | tf_op jit(solution)/shard_map/ppermute | solution.py:765
  18.1 1.7 %collective-permute-start.12 = (f32[2304,128]{1,0:T(8,128)S(1)}, f32[2304,128]{1,0:T(8,128)S(1)}, u32[]{:S(2)}, u32[]{:S(2)}) collective-permute-start(f32[2304,128]{1,0:T(8,128)S(1)} %get-tuple-element.60), channel_id=1, source_target_pairs={{0,32},{1,33},{2,34},{3,35},{4,36},{5,37},{6,38},{7,39},{8,40},{9,... | collective-permute-start | bytes 3538952 | tf_op jit(solution)/shard_map/ppermute | solution.py:765
  19.8 14.1 %collective-permute-start.2 = (f32[48,128]{1,0:T(8,128)S(1)}, f32[48,128]{1,0:T(8,128)S(1)}, u32[]{:S(2)}, u32[]{:S(2)}) collective-permute-start(f32[48,128]{1,0:T(8,128)S(1)} %stack.16.refs_1_), channel_id=1, source_target_pairs={{0,1},{1,2},{2,3},{3,4},{4,5},{5,6},{6,7},{7,8},{8,9},{9,10},{10,1... | collective-permute-start | bytes 73736 | tf_op jit(solution)/shard_map/ppermute | solution.py:765
  34.0 1.5 collective-permute-done.2.refs_0_
  35.5 2.3 %collective-permute-done.3.refs_2_ = f32[48,128]{1,0:T(8,128)S(1)} collective-permute-done((f32[48,128]{1,0:T(8,128)S(1)}, f32[48,128]{1,0:T(8,128)S(1)}, u32[]{:S(2)}, u32[]{:S(2)}) %collective-permute-start.3) | collective-permute-done | bytes 24608 | tf_op jit(solution)/shard_map/ppermute | solution.py:765
  37.8 1.6 %collective-permute-start.10 = (f32[6,16,16,128]{3,2,1,0:T(8,128)S(1)}, f32[6,16,16,128]{3,2,1,0:T(8,128)S(1)}, u32[]{:S(2)}, u32[]{:S(2)}) collective-permute-start(f32[6,16,16,128]{3,2,1,0:T(8,128)S(1)} %copy-done.3), channel_id=1, source_target_pairs={{0,1},{1,2},{2,3},{3,4},{4,5},{5,6},{6,7},{7,8},{8,9},{9,10},{10,1... | collective-permute-start | bytes 2359304 | tf_op jit(solution)/shard_map/ppermute | solution.py:765
  39.4 6.3 %collective-permute-start.11 = (f32[6,16,16,128]{3,2,1,0:T(8,128)S(1)}, f32[6,16,16,128]{3,2,1,0:T(8,128)S(1)}, u32[]{:S(2)}, u32[]{:S(2)}) collective-permute-start(f32[6,16,16,128]{3,2,1,0:T(8,128)S(1)} %get-tuple-element.58), channel_id=1, source_target_pairs={{0,31},{1,0},{2,1},{3,2},{4,3},{5,4},{6,5},{7,6},{8,7},{9,8},{10,9... | collective-permute-start | bytes 2359304 | tf_op jit(solution)/shard_map/ppermute | solution.py:765
  46.5 3.1 %side_x.1.part_ref = f32[16,256,128]{2,1,0:T(8,128)S(1)} custom-call(f32[16,256,128]{2,1,0:T(8,128)S(1)} %bitcast.15, f32[16,256,128]{2,1,0:T(8,128)} %collective-permute-done.6.mate_ref), custom_call_target="tpu_custom_call" | custom-call | flops 16777216 | bytes 6291456 | tf_op jit(solution)/shard_map/side_x/pallas_call | solution.py:249
  49.5 7.8 %prep.1 = (bf16[2,4096,128]{2,1,0:T(8,128)(2,1)S(1)}, f32[3,48,128]{2,1,0:T(8,128)S(1)}, f32[48,128]{1,0:T(8,128)S(1)}) custom-call(f32[144,128]{1,0:T(8,128)S(1)} %stack.17.refs_0_, f32[144,128]{1,0:T(8,128)S(1)} %collective-permute-done.5.refs_1_, s32[2]{0:T(128)S(1)} %pad_add_fusion.refs_2_, f32[4096,128]{1,0:T(8,128)S(1)} %spread.2.refs_3_, ...), custom_call_target="tpu_custom_call" | custom-call | flops 134217728 | bytes 10485760 | tf_op jit(solution)/shard_map/prep/pallas_call | solution.py:461
  57.3 1.3 collective-permute-start.13
  61.5 3.0 %side_z.1.side_ref = f32[16,256,128]{2,1,0:T(8,128)S(1)} custom-call(f32[16,256,128]{2,1,0:T(8,128)S(1)} %bitcast.17, f32[16,256,128]{2,1,0:T(8,128)S(1)} %side_x.1.part_ref, f32[6,16,16,128]{3,2,1,0:T(8,128)S(1)} %collective-permute-done.10.low_ref, f32[6,16,16,128]{3,2,1,0:T(8,128)S(1)} %collective-permute-done.11.high_ref), custom_call_target="tpu_custom_call" | custom-call | flops 16777216 | bytes 8388608 | tf_op jit(solution)/shard_map/side_z/pallas_call | solution.py:274
  64.8 10.1 %collective-permute-done.13.refs_2_ = f32[6,192,128]{2,1,0:T(8,128)S(1)} collective-permute-done((f32[6,192,128]{2,1,0:T(8,128)S(1)}, f32[6,192,128]{2,1,0:T(8,128)S(1)}, u32[]{:S(2)}, u32[]{:S(2)}) %collective-permute-start.13) | collective-permute-done | bytes 589856 | tf_op jit(solution)/shard_map/ppermute | solution.py:801
  75.0 2.1 %first.1 = (f32[16,256,128]{2,1,0:T(8,128)S(1)}, f32[16,256,128]{2,1,0:T(8,128)S(1)}, f32[1632,128]{1,0:T(8,128)S(1)}, f32[1632,128]{1,0:T(8,128)S(1)}) custom-call(f32[16,256,128]{2,1,0:T(8,128)S(1)} %bitcast.18, f32[16,256,128]{2,1,0:T(8,128)S(1)} %side_z.1.side_ref, f32[16,256,128]{2,1,0:T(8,128)S(1)} %bitcast.20, ...), custom_call_target="tpu_custom_call" | custom-call | flops 16777216 | bytes 14680064 | tf_op jit(solution)/shard_map/first/pallas_call | solution.py:520
  77.3 7.7 %collective-permute-start.16 = (f32[1632,128]{1,0:T(8,128)S(1)}, f32[1632,128]{1,0:T(8,128)S(1)}, u32[]{:S(2)}, u32[]{:S(2)}) collective-permute-start(f32[1632,128]{1,0:T(8,128)S(1)} %get-tuple-element.65), channel_id=1, source_target_pairs={{0,31},{1,0},{2,1},{3,2},{4,3},{5,4},{6,5},{7,6},{8,7},{9,8},{10,9... | collective-permute-start | bytes 2506760 | tf_op jit(solution)/shard_map/ppermute | solution.py:765
  86.5 2.9 %side_again.1.part_ref = f32[16,256,128]{2,1,0:T(8,128)S(1)} custom-call(f32[16,256,128]{2,1,0:T(8,128)S(1)} %get-tuple-element.63.s_ref, f32[16,256,128]{2,1,0:T(8,128)S(1)} %collective-permute-done.14.mate_ref), custom_call_target="tpu_custom_call" | custom-call | flops 33554432 | bytes 6291456 | tf_op jit(solution)/shard_map/side_again/pallas_call | solution.py:301
  89.5 3.0 %base.1.base_ref = f32[16,256,128]{2,1,0:T(8,128)S(1)} custom-call(f32[16,256,128]{2,1,0:T(8,128)S(1)} %bitcast.19, f32[16,64,128]{2,1,0:T(8,128)S(1)} %collective-permute-done.9.mid_ref, f32[16,256,128]{2,1,0:T(8,128)S(1)} %bitcast.21, f32[16,256,128]{2,1,0:T(8,128)S(1)} %bitcast.26, f32[16,256,128]{2,1,0:T(8,128)S(1)} %get-tuple-element.62.q_ref, ...), custom_call_target="tpu_custom_call" | custom-call | flops 33554432 | bytes 16777216 | tf_op jit(solution)/shard_map/base/pallas_call | solution.py:572
  92.4 11.5 %collective-permute-done.15.low_ref = f32[1632,128]{1,0:T(8,128)S(1)} collective-permute-done((f32[1632,128]{1,0:T(8,128)S(1)}, f32[1632,128]{1,0:T(8,128)S(1)}, u32[]{:S(2)}, u32[]{:S(2)}) %collective-permute-start.15) | collective-permute-done | bytes 835616 | tf_op jit(solution)/shard_map/ppermute | solution.py:765
  103.9 3.7 %second.1 = (f32[16,256,128]{2,1,0:T(8,128)S(1)}, f32[64,128]{1,0:T(8,128)S(1)}, f32[64,128]{1,0:T(8,128)S(1)}) custom-call(f32[16,256,128]{2,1,0:T(8,128)S(1)} %base.1.base_ref, f32[1632,128]{1,0:T(8,128)S(1)} %collective-permute-done.15.low_ref, f32[1632,128]{1,0:T(8,128)S(1)} %collective-permute-done.16.high_ref, bf16[2,16,256,128]{3,2,1,0:T(8,128)(2,1)S(1)} %bitcast.24, ...), custom_call_target="tpu_custom_call" | custom-call | flops 134217728 | bytes 8388608 | tf_op jit(solution)/shard_map/second/pallas_call | solution.py:643
  109.2 3.6 %collective-permute-done.18 = f32[64,128]{1,0:T(8,128)S(1)} collective-permute-done((f32[64,128]{1,0:T(8,128)S(1)}, f32[64,128]{1,0:T(8,128)S(1)}, u32[]{:S(2)}, u32[]{:S(2)}) %collective-permute-start.18) | collective-permute-done | bytes 32800 | tf_op jit(solution)/shard_map/ppermute | solution.py:822
  112.8 5.1 %collective-permute-done.19 = f32[64,128]{1,0:T(8,128)S(1)} collective-permute-done((f32[64,128]{1,0:T(8,128)S(1)}, f32[64,128]{1,0:T(8,128)S(1)}, u32[]{:S(2)}, u32[]{:S(2)}) %collective-permute-start.19) | collective-permute-done | bytes 32800 | tf_op jit(solution)/shard_map/ppermute | solution.py:822
  118.0 3.9 %collective-permute-done.20 = f32[64,128]{1,0:T(8,128)S(1)} collective-permute-done((f32[64,128]{1,0:T(8,128)S(1)}, f32[64,128]{1,0:T(8,128)S(1)}, u32[]{:S(2)}, u32[]{:S(2)}) %collective-permute-start.20) | collective-permute-done | bytes 32800 | tf_op jit(solution)/shard_map/ppermute | solution.py:822
  121.9 1.7 %collective-permute-start.21 = (f32[64,128]{1,0:T(8,128)S(1)}, f32[64,128]{1,0:T(8,128)S(1)}, u32[]{:S(2)}, u32[]{:S(2)}) collective-permute-start(f32[64,128]{1,0:T(8,128)S(1)} %add.38), channel_id=1, source_target_pairs={{0,3},{1,2},{2,1},{3,0},{4,7},{5,6},{6,5},{7,4},{8,11},{9,10},{10,... | collective-permute-start | bytes 98312 | tf_op jit(solution)/shard_map/ppermute | solution.py:822
  123.6 3.4 %collective-permute-done.21 = f32[64,128]{1,0:T(8,128)S(1)} collective-permute-done((f32[64,128]{1,0:T(8,128)S(1)}, f32[64,128]{1,0:T(8,128)S(1)}, u32[]{:S(2)}, u32[]{:S(2)}) %collective-permute-start.21) | collective-permute-done | bytes 32800 | tf_op jit(solution)/shard_map/ppermute | solution.py:822
  127.1 3.8 %collective-permute-done.22 = f32[64,128]{1,0:T(8,128)S(1)} collective-permute-done((f32[64,128]{1,0:T(8,128)S(1)}, f32[64,128]{1,0:T(8,128)S(1)}, u32[]{:S(2)}, u32[]{:S(2)}) %collective-permute-start.22) | collective-permute-done | bytes 32800 | tf_op jit(solution)/shard_map/ppermute | solution.py:822
  130.9 1.5 %collective-permute-start.23 = (f32[64,128]{1,0:T(8,128)S(1)}, f32[64,128]{1,0:T(8,128)S(1)}, u32[]{:S(2)}, u32[]{:S(2)}) collective-permute-start(f32[64,128]{1,0:T(8,128)S(1)} %add.40), channel_id=1, source_target_pairs={{0,24},{1,25},{2,26},{3,27},{4,28},{5,29},{6,30},{7,31},{8,16},{9,... | collective-permute-start | bytes 98312 | tf_op jit(solution)/shard_map/ppermute | solution.py:822
  132.5 3.6 %collective-permute-done.23 = f32[64,128]{1,0:T(8,128)S(1)} collective-permute-done((f32[64,128]{1,0:T(8,128)S(1)}, f32[64,128]{1,0:T(8,128)S(1)}, u32[]{:S(2)}, u32[]{:S(2)}) %collective-permute-start.23) | collective-permute-done | bytes 32800 | tf_op jit(solution)/shard_map/ppermute | solution.py:822
  136.1 1.2 collective-permute-done.24.other_ref
  137.3 17.0 %turn.1 = f32[16,256,128]{2,1,0:T(8,128)} custom-call(f32[16,256,128]{2,1,0:T(8,128)S(1)} %get-tuple-element.70.second_ref, f32[64,128]{1,0:T(8,128)S(1)} %add.41.own_ref, f32[64,128]{1,0:T(8,128)S(1)} %collective-permute-done.24.other_ref, s32[1]{0:T(128)} %bitcast.3.rest_3_.upper_ref), custom_call_target="tpu_custom_call" | custom-call | flops 268435456 | bytes 4194304 | tf_op jit(solution)/shard_map/turn/pallas_call | solution.py:742
  (69 shorter events, 11.7 us)
Async XLA Ops:
  0.0 46.5 %collective-permute-start.6 = (f32[16,256,128]{2,1,0:T(8,128)}, f32[16,256,128]{2,1,0:T(8,128)}, u32[]{:S(2)}, u32[]{:S(2)}) collective-permute-start(f32[16,256,128]{2,1,0:T(8,128)} %bitcast.12), channel_id=1, source_target_pairs={{0,64},{1,65},{2,66},{3,67},{4,68},{5,69},{6,70},{7,71},{8,72},{9,... | collective-permute-start | bytes 6291464 | tf_op jit(solution)/shard_map/ppermute | solution.py:765
  0.1 1.6 %copy-start = (f32[16,16,16,128]{3,2,1,0:T(8,128)S(1)}, f32[16,16,16,128]{3,2,1,0:T(8,128)}, u32[]{:S(2)}) copy-start(f32[16,16,16,128]{3,2,1,0:T(8,128)} %param.5) | copy-start | bytes 6291460
  1.7 5.8 %copy-start.5 = (f32[4,9,9,9]{3,0,2,1:T(4,128)S(1)}, f32[4,9,9,9]{3,0,2,1:T(4,128)}, u32[]{:S(2)}) copy-start(f32[4,9,9,9]{3,0,2,1:T(4,128)} %param.8) | copy-start | bytes 34996
  1.7 7.7 %copy-start.7 = (s32[4,3]{1,0:T(4,128)S(1)}, s32[4,3]{1,0:T(4,128)}, u32[]{:S(2)}) copy-start(s32[4,3]{1,0:T(4,128)} %param.7) | copy-start | bytes 148
  1.7 7.7 %copy-start.8 = (f32[4]{0:T(128)S(1)}, f32[4]{0:T(128)}, u32[]{:S(2)}) copy-start(f32[4]{0:T(128)} %param.9) | copy-start | bytes 52
  1.7 8.0 %copy-start.6 = (f32[16,16,16]{2,1,0:T(8,128)S(1)}, f32[16,16,16]{2,1,0:T(8,128)}, u32[]{:S(2)}) copy-start(f32[16,16,16]{2,1,0:T(8,128)} %param.6) | copy-start | bytes 49156
  1.7 13.2 %copy-start.1 = (f32[16,16,16,128]{3,2,1,0:T(8,128)S(1)}, f32[16,16,16,128]{3,2,1,0:T(8,128)}, u32[]{:S(2)}) copy-start(f32[16,16,16,128]{3,2,1,0:T(8,128)} %param.5) | copy-start | bytes 6291460
  5.5 12.6 %collective-permute-start.1 = (f32[4,192,128]{2,1,0:T(8,128)}, f32[4,192,128]{2,1,0:T(8,128)S(1)}, u32[]{:S(2)}, u32[]{:S(2)}) collective-permute-start(f32[4,192,128]{2,1,0:T(8,128)} %get-tuple-element.42), channel_id=1, source_target_pairs={{0,32},{1,33},{2,34},{3,35},{4,36},{5,37},{6,38},{7,39},{8,40},{9,... | collective-permute-start | bytes 1179656 | tf_op jit(solution)/shard_map/ppermute | solution.py:765
  9.8 8.3 %collective-permute-start = (f32[56,128]{1,0:T(8,128)S(1)}, f32[56,128]{1,0:T(8,128)S(1)}, u32[]{:S(2)}, u32[]{:S(2)}) collective-permute-start(f32[56,128]{1,0:T(8,128)S(1)} %stack.15.refs_0_.parcel_ref), channel_id=1, source_target_pairs={{0,32},{1,33},{2,34},{3,35},{4,36},{5,37},{6,38},{7,39},{8,40},{9,... | collective-permute-start | bytes 86024 | tf_op jit(solution)/shard_map/ppermute | solution.py:765
  9.9 27.9 %copy-start.3 = (f32[6,16,16,128]{3,2,1,0:T(8,128)S(1)}, f32[6,16,16,128]{3,2,1,0:T(8,128)}, u32[]{:S(2)}) copy-start(f32[6,16,16,128]{3,2,1,0:T(8,128)} %copy-done.2) | copy-start | bytes 2359300
  9.9 35.8 %collective-permute-start.4 = (f32[6,192,128]{2,1,0:T(8,128)}, f32[6,192,128]{2,1,0:T(8,128)S(1)}, u32[]{:S(2)}, u32[]{:S(2)}) collective-permute-start(f32[6,192,128]{2,1,0:T(8,128)} %copy-done.4), channel_id=1, source_target_pairs={{0,33},{3,34},{4,37},{7,38},{8,41},{11,42},{12,45},{15,46},{16,49}... | collective-permute-start | bytes 1769480 | tf_op jit(solution)/shard_map/ppermute | solution.py:778
  18.1 46.4 %collective-permute-start.12 = (f32[2304,128]{1,0:T(8,128)S(1)}, f32[2304,128]{1,0:T(8,128)S(1)}, u32[]{:S(2)}, u32[]{:S(2)}) collective-permute-start(f32[2304,128]{1,0:T(8,128)S(1)} %get-tuple-element.60), channel_id=1, source_target_pairs={{0,32},{1,33},{2,34},{3,35},{4,36},{5,37},{6,38},{7,39},{8,40},{9,... | collective-permute-start | bytes 3538952 | tf_op jit(solution)/shard_map/ppermute | solution.py:765
  19.8 15.7 %collective-permute-start.2 = (f32[48,128]{1,0:T(8,128)S(1)}, f32[48,128]{1,0:T(8,128)S(1)}, u32[]{:S(2)}, u32[]{:S(2)}) collective-permute-start(f32[48,128]{1,0:T(8,128)S(1)} %stack.16.refs_1_), channel_id=1, source_target_pairs={{0,1},{1,2},{2,3},{3,4},{4,5},{5,6},{6,7},{7,8},{8,9},{9,10},{10,1... | collective-permute-start | bytes 73736 | tf_op jit(solution)/shard_map/ppermute | solution.py:765
  34.0 3.8 %collective-permute-start.3 = (f32[48,128]{1,0:T(8,128)S(1)}, f32[48,128]{1,0:T(8,128)S(1)}, u32[]{:S(2)}, u32[]{:S(2)}) collective-permute-start(f32[48,128]{1,0:T(8,128)S(1)} %stack.16.refs_1_), channel_id=1, source_target_pairs={{0,31},{1,0},{2,1},{3,2},{4,3},{5,4},{6,5},{7,6},{8,7},{9,8},{10,9... | collective-permute-start | bytes 73736 | tf_op jit(solution)/shard_map/ppermute | solution.py:765
  37.8 23.7 %collective-permute-start.10 = (f32[6,16,16,128]{3,2,1,0:T(8,128)S(1)}, f32[6,16,16,128]{3,2,1,0:T(8,128)S(1)}, u32[]{:S(2)}, u32[]{:S(2)}) collective-permute-start(f32[6,16,16,128]{3,2,1,0:T(8,128)S(1)} %copy-done.3), channel_id=1, source_target_pairs={{0,1},{1,2},{2,3},{3,4},{4,5},{5,6},{6,7},{7,8},{8,9},{9,10},{10,1... | collective-permute-start | bytes 2359304 | tf_op jit(solution)/shard_map/ppermute | solution.py:765
  39.4 22.1 %collective-permute-start.11 = (f32[6,16,16,128]{3,2,1,0:T(8,128)S(1)}, f32[6,16,16,128]{3,2,1,0:T(8,128)S(1)}, u32[]{:S(2)}, u32[]{:S(2)}) collective-permute-start(f32[6,16,16,128]{3,2,1,0:T(8,128)S(1)} %get-tuple-element.58), channel_id=1, source_target_pairs={{0,31},{1,0},{2,1},{3,2},{4,3},{5,4},{6,5},{7,6},{8,7},{9,8},{10,9... | collective-permute-start | bytes 2359304 | tf_op jit(solution)/shard_map/ppermute | solution.py:765
  45.6 3.9 %collective-permute-start.5 = (f32[144,128]{1,0:T(8,128)S(1)}, f32[144,128]{1,0:T(8,128)S(1)}, u32[]{:S(2)}, u32[]{:S(2)}) collective-permute-start(f32[144,128]{1,0:T(8,128)S(1)} %stack.17.refs_0_), channel_id=1, source_target_pairs={{0,64},{1,65},{2,66},{3,67},{4,68},{5,69},{6,70},{7,71},{8,72},{9,... | collective-permute-start | bytes 221192 | tf_op jit(solution)/shard_map/ppermute | solution.py:765
  57.3 17.6 %collective-permute-start.13 = (f32[6,192,128]{2,1,0:T(8,128)S(1)}, f32[6,192,128]{2,1,0:T(8,128)S(1)}, u32[]{:S(2)}, u32[]{:S(2)}) collective-permute-start(f32[6,192,128]{2,1,0:T(8,128)S(1)} %collective-permute-done.4), channel_id=1, source_target_pairs={{1,0},{2,3},{5,4},{6,7},{9,8},{10,11},{13,12},{14,15},{17,16},{18,... | collective-permute-start | bytes 1769480 | tf_op jit(solution)/shard_map/ppermute | solution.py:801
  58.6 1.5 collective-permute-start.7
  60.2 4.7 %collective-permute-start.8 = (f32[3,48,128]{2,1,0:T(8,128)S(1)}, f32[3,48,128]{2,1,0:T(8,128)S(1)}, u32[]{:S(2)}, u32[]{:S(2)}) collective-permute-start(f32[3,48,128]{2,1,0:T(8,128)S(1)} %add.34.refs_4_.rest_0_), channel_id=1, source_target_pairs={{0,32},{1,33},{2,34},{3,35},{4,36},{5,37},{6,38},{7,39},{8,40},{9,... | collective-permute-start | bytes 221192 | tf_op jit(solution)/shard_map/ppermute | solution.py:765
  77.1 9.4 %collective-permute-start.14 = (f32[16,256,128]{2,1,0:T(8,128)S(1)}, f32[16,256,128]{2,1,0:T(8,128)S(1)}, u32[]{:S(2)}, u32[]{:S(2)}) collective-permute-start(f32[16,256,128]{2,1,0:T(8,128)S(1)} %get-tuple-element.63.s_ref), channel_id=1, source_target_pairs={{0,64},{1,65},{2,66},{3,67},{4,68},{5,69},{6,70},{7,71},{8,72},{9,... | collective-permute-start | bytes 6291464 | tf_op jit(solution)/shard_map/ppermute | solution.py:765
  77.2 26.7 %collective-permute-start.15 = (f32[1632,128]{1,0:T(8,128)S(1)}, f32[1632,128]{1,0:T(8,128)S(1)}, u32[]{:S(2)}, u32[]{:S(2)}) collective-permute-start(f32[1632,128]{1,0:T(8,128)S(1)} %get-tuple-element.64), channel_id=1, source_target_pairs={{0,1},{1,2},{2,3},{3,4},{4,5},{5,6},{6,7},{7,8},{8,9},{9,10},{10,1... | collective-permute-start | bytes 2506760 | tf_op jit(solution)/shard_map/ppermute | solution.py:765
  77.3 26.7 %collective-permute-start.16 = (f32[1632,128]{1,0:T(8,128)S(1)}, f32[1632,128]{1,0:T(8,128)S(1)}, u32[]{:S(2)}, u32[]{:S(2)}) collective-permute-start(f32[1632,128]{1,0:T(8,128)S(1)} %get-tuple-element.65), channel_id=1, source_target_pairs={{0,31},{1,0},{2,1},{3,2},{4,3},{5,4},{6,5},{7,6},{8,7},{9,8},{10,9... | collective-permute-start | bytes 2506760 | tf_op jit(solution)/shard_map/ppermute | solution.py:765
  85.0 4.5 %collective-permute-start.9 = (f32[16,64,128]{2,1,0:T(8,128)S(1)}, f32[16,64,128]{2,1,0:T(8,128)S(1)}, u32[]{:S(2)}, u32[]{:S(2)}) collective-permute-start(f32[16,64,128]{2,1,0:T(8,128)S(1)} %get-tuple-element.55), channel_id=1, source_target_pairs={{1,33},{2,34},{5,37},{6,38},{9,41},{10,42},{13,45},{14,46},{17,49}... | collective-permute-start | bytes 1572872 | tf_op jit(solution)/shard_map/ppermute | solution.py:813
  107.6 1.3 collective-permute-start.17
  108.9 3.9 %collective-permute-start.18 = (f32[64,128]{1,0:T(8,128)S(1)}, f32[64,128]{1,0:T(8,128)S(1)}, u32[]{:S(2)}, u32[]{:S(2)}) collective-permute-start(f32[64,128]{1,0:T(8,128)S(1)} %add.35), channel_id=1, source_target_pairs={{0,32},{1,33},{2,34},{3,35},{4,36},{5,37},{6,38},{7,39},{8,40},{9,... | collective-permute-start | bytes 98312 | tf_op jit(solution)/shard_map/ppermute | solution.py:822
  112.8 5.1 %collective-permute-start.19 = (f32[64,128]{1,0:T(8,128)S(1)}, f32[64,128]{1,0:T(8,128)S(1)}, u32[]{:S(2)}, u32[]{:S(2)}) collective-permute-start(f32[64,128]{1,0:T(8,128)S(1)} %add.36), channel_id=1, source_target_pairs={{0,36},{1,37},{2,38},{3,39},{4,32},{5,33},{6,34},{7,35},{8,44},{9,... | collective-permute-start | bytes 98312 | tf_op jit(solution)/shard_map/ppermute | solution.py:822
  118.0 3.9 %collective-permute-start.20 = (f32[64,128]{1,0:T(8,128)S(1)}, f32[64,128]{1,0:T(8,128)S(1)}, u32[]{:S(2)}, u32[]{:S(2)}) collective-permute-start(f32[64,128]{1,0:T(8,128)S(1)} %add.37), channel_id=1, source_target_pairs={{0,1},{1,0},{2,3},{3,2},{4,5},{5,4},{6,7},{7,6},{8,9},{9,8},{10,11... | collective-permute-start | bytes 98312 | tf_op jit(solution)/shard_map/ppermute | solution.py:822
  121.9 5.1 %collective-permute-start.21 = (f32[64,128]{1,0:T(8,128)S(1)}, f32[64,128]{1,0:T(8,128)S(1)}, u32[]{:S(2)}, u32[]{:S(2)}) collective-permute-start(f32[64,128]{1,0:T(8,128)S(1)} %add.38), channel_id=1, source_target_pairs={{0,3},{1,2},{2,1},{3,0},{4,7},{5,6},{6,5},{7,4},{8,11},{9,10},{10,... | collective-permute-start | bytes 98312 | tf_op jit(solution)/shard_map/ppermute | solution.py:822
  127.0 3.9 %collective-permute-start.22 = (f32[64,128]{1,0:T(8,128)S(1)}, f32[64,128]{1,0:T(8,128)S(1)}, u32[]{:S(2)}, u32[]{:S(2)}) collective-permute-start(f32[64,128]{1,0:T(8,128)S(1)} %add.39), channel_id=1, source_target_pairs={{0,8},{1,9},{2,10},{3,11},{4,12},{5,13},{6,14},{7,15},{8,0},{9,1},... | collective-permute-start | bytes 98312 | tf_op jit(solution)/shard_map/ppermute | solution.py:822
  130.9 5.1 %collective-permute-start.23 = (f32[64,128]{1,0:T(8,128)S(1)}, f32[64,128]{1,0:T(8,128)S(1)}, u32[]{:S(2)}, u32[]{:S(2)}) collective-permute-start(f32[64,128]{1,0:T(8,128)S(1)} %add.40), channel_id=1, source_target_pairs={{0,24},{1,25},{2,26},{3,27},{4,28},{5,29},{6,30},{7,31},{8,16},{9,... | collective-permute-start | bytes 98312 | tf_op jit(solution)/shard_map/ppermute | solution.py:822
  136.1 1.2 collective-permute-start.24
  (2 other events, 1.7 us)

commit v15 on v8

--- a/solution.py
+++ b/solution.py
@@ -12,6 +12,7 @@
 C = 16
 ROWS = C * C
 CELLS = C * C * C
+NCELLS = 32 * 32 * 512
 S = 128
 W = 9
 R = 4
@@ -584,7 +585,7 @@
 
 
 def second_kernel(base_ref, low_ref, high_ref, gg_high_ref, gg_low_ref, *rest):
-    part_ref, mate_ref, energy_ref, second_ref, gram_ref, cross_ref, w_ref, halo_ref = rest
+    part_ref, mate_ref, energy_ref, upper_ref, second_ref, keep_ref, give_ref, gram_ref, cross_ref, w_ref, halo_ref = rest
     step = pl.program_id(0)
 
     @pl.when(step == 0)
@@ -615,39 +616,42 @@
             halo_ref[p, stride_rows(C - H + z), :] = add
 
     w_high, w_low = split(w_ref[...])
-    gram = jnp.zeros((S, S), F32)
-    cross = jnp.zeros((S, S), F32)
+    w_twice = jnp.concatenate([w_high, w_high])
+    gram = jnp.zeros((S, 2 * S), F32)
     for p in range(B):
         g_high, g_low = gg_high_ref[0, p], gg_low_ref[0, p]
-        value = base_ref[p] + halo_ref[p] + (mm(g_high, w_high) + (mm(g_high, w_low) + mm(g_low, w_high)))
+        near = mm(jnp.concatenate([g_high, g_low], axis=1), w_twice) + mm(g_high, w_low)
+        value = base_ref[p] + halo_ref[p] + near
         second_ref[p] = value
         s_high, s_low = split(value)
-        turned = s_high.T
-        gram += mm(turned, s_high)
-        cross += mm(turned, s_low)
-    gram_ref[...] += gram
-    cross_ref[...] += cross
+        gram += mm(s_high.T, jnp.concatenate([s_high, s_low], axis=1))
+    gram_ref[...] += gram[:, :S]
+    cross_ref[...] += gram[:, S:]
 
     @pl.when(step == STEPS - 1)
     def _():
         cross = cross_ref[...]
-        gram_ref[...] += cross + cross.T
-
-
-def make_second(base, low, high, gg, weighted):
-    shares = pl.BlockSpec((3, NEAR, S), lambda i: (0, 0, 0))
+        gram = (gram_ref[...] + (cross + cross.T)) * (1.0 / NCELLS)
+        upper = upper_ref[0] == 1
+        keep_ref[...] = jnp.where(upper, gram[S // 2 :], gram[: S // 2])
+        give_ref[...] = jnp.where(upper, gram[: S // 2], gram[S // 2 :])
+
+
+def make_second(base, halos, gg, shares, upper):
+    three = pl.BlockSpec((3, NEAR, S), lambda i: (0, 0, 0))
     return pl.pallas_call(
         second_kernel,
         grid=(STEPS,),
-        in_specs=[plane_spec(), whole(MESSAGE.shape[0]), whole(MESSAGE.shape[0]), part_spec(0), part_spec(1)]
-        + [shares, shares, whole(NEAR)],
-        out_specs=[plane_spec(), whole()],
-        out_shape=[FULL, sds((S, S))],
-        scratch_shapes=[pltpu.VMEM((S, S), F32), pltpu.VMEM((S, S), F32), pltpu.VMEM((B, ROWS, S), F32)],
+        in_specs=[plane_spec()]
+        + [whole(MESSAGE.shape[0])] * 2
+        + [part_spec(0), part_spec(1), three, three, whole(NEAR), SCALARS],
+        out_specs=[plane_spec(), whole(S // 2), whole(S // 2)],
+        out_shape=[FULL, sds((S // 2, S)), sds((S // 2, S))],
+        scratch_shapes=[pltpu.VMEM((S, S), F32)] * 3 + [pltpu.VMEM((B, ROWS, S), F32)],
         compiler_params=params(16),
         cost_estimate=cost(1 << 27, 8 << 20),
         name="second",
-    )(base, low, high, gg, gg, *weighted)
+    )(base, *halos, gg, gg, *shares, upper)
 
 
 def exact(a, b):
@@ -715,33 +719,36 @@
     x_ref[...] = x_ref[...] * across
 
 
-def turn_kernel(second_ref, gram_ref, out_ref, a_ref, x_ref, i_high_ref, i_low_ref, state_ref):
+def turn_kernel(second_ref, own_ref, other_ref, upper_ref, out_ref, gram_ref, a_ref, x_ref, i_high_ref, i_low_ref, state_ref):
     @pl.when(pl.program_id(0) == 0)
     def _():
+        upper = upper_ref[0] == 1
+        gram_ref[: S // 2, :] = jnp.where(upper, other_ref[...], own_ref[...])
+        gram_ref[S // 2 :, :] = jnp.where(upper, own_ref[...], other_ref[...])
         inverse_factor(gram_ref, a_ref, x_ref, state_ref)
         i_high, i_low = split(x_ref[...].T)
         i_high_ref[...] = i_high
         i_low_ref[...] = i_low
 
     i_high, i_low = i_high_ref[...], i_low_ref[...]
-
+    i_twice = jnp.concatenate([i_high, i_high])
     for p in range(B):
         high, low = split(second_ref[p])
-        out_ref[p] = mm(high, i_high) + (mm(high, i_low) + mm(low, i_high))
-
-
-def turn(second, gram):
+        out_ref[p] = mm(jnp.concatenate([high, low], axis=1), i_twice) + mm(high, i_low)
+
+
+def turn(second, own, other, upper):
     return pl.pallas_call(
         turn_kernel,
         grid=(STEPS,),
-        in_specs=[plane_spec(), whole()],
+        in_specs=[plane_spec(), whole(S // 2), whole(S // 2), SCALARS],
         out_specs=plane_spec(),
         out_shape=FULL,
-        scratch_shapes=[pltpu.VMEM((S, S), F32)] * 2 + [pltpu.VMEM((S, S), BF16)] * 2 + [pltpu.SMEM((1,), jnp.int32)],
+        scratch_shapes=[pltpu.VMEM((S, S), F32)] * 3 + [pltpu.VMEM((S, S), BF16)] * 2 + [pltpu.SMEM((1,), jnp.int32)],
         compiler_params=params(16),
         cost_estimate=cost(1 << 28, 4 << 20),
         name="turn",
-    )(second, gram)
+    )(second, own, other, upper)
 
 
 def per_device(states, potential, atom_sites, projectors, energies):
@@ -768,8 +775,11 @@
         axis=1,
     ).reshape(24, 128)
     mate = send(s, over_x)
+    corner = jnp.stack([gx * C, gy * C]).astype(jnp.int32)
+    upper = gx.astype(jnp.int32).reshape(1)
+    to_pack, corner, upper, inner = barrier((s, corner, upper, inner))
     below, above = send(atoms, 0, 1), send(atoms, 0, -1)
-    one_edge, head, tail = pack(s)
+    one_edge, head, tail = pack(to_pack)
     one_edge = send(one_edge, over_y)
     head, tail, below, above = barrier((head, tail, below, above))
     parcel = stack(below, atoms, above, pot)
@@ -783,7 +793,6 @@
     relayed = lax.ppermute(relay, AXES, [(d, d ^ over_y ^ 1) for d in outer_ones])
     message = send(message, over_y)
     parcel_xy = send(parcel_y, over_x)
-    corner = jnp.stack([gx * C, gy * C]).astype(jnp.int32)
     gg, part, energy = prep([parcel, parcel_x, parcel_y, parcel_xy], corner, vb, s)
 
     part, relayed = barrier((part, relayed))
@@ -801,12 +810,13 @@
     vb_mate = spread(parcel_y).reshape(C, ROWS, S)
     part_two = side_again(mix, mate)
     base = make_base(s, mid, vb, vb_mate, q, side_part, part_two, edges, inner)
-    second, gram = make_second(base, low, high, gg.reshape(2, C, ROWS, S), [part, part_mate, energy])
-
-    for flip in (64, 32, 36, 1, 3, 8, 24):
-        gram = gram + lax.ppermute(gram, AXES, [(d, d ^ flip) for d in range(count)])
-    gram = gram * (1.0 / (CELLS * count))
-    return turn(second, gram).reshape(C, C, C, S)
+    gg = gg.reshape(2, C, ROWS, S)
+    second, own, give = make_second(base, [low, high], gg, [part, part_mate, energy], upper)
+
+    own = own + send(give, over_x)
+    for flip in (32, 36, 1, 3, 8, 24):
+        own = own + lax.ppermute(own, AXES, [(d, d ^ flip) for d in range(count)])
+    return turn(second, own, send(own, over_x), upper).reshape(C, C, C, S)
 
 
 def solution(mesh):

time: 154 us -> 149 us (0.968)
  Pallas kernels: 52.1 us -> 46.6 us
    ppermute x15 -> x17, waiting for transfers between devices: 30.3 us -> 33.5 us  [send(): return lax.ppermute(value, AXES, [(d, target(d)) for d in range(count)])]
    ppermute x7 -> x6, waiting for transfers between devices: 21.5 us -> 18.7 us  [per_device(): own = own + lax.ppermute(own, AXES, [(d, d ^ flip) for d in range(count)])]
    pallas_call x1, Pallas kernels: 2.12 us -> 0.31 us  [pack_rest(): pl.pallas_call(pack_rest_kernel, grid=(C // N,), in_specs=[plane_spec(ROW...]
    unnamed x25 -> x15, local copies, waits for them, and re-layouts: 4.56 us -> 3.24 us
    ppermute x7 -> x6, starting transfers between devices: 10.1 us -> 8.99 us  [per_device(): own = own + lax.ppermute(own, AXES, [(d, d ^ flip) for d in range(count)])]
    ppermute x15 -> x17, starting transfers between devices: 28.7 us -> 28.8 us  [send(): return lax.ppermute(value, AXES, [(d, target(d)) for d in range(count)])]
  transfers between devices with their start and end apart: 25 -> 26, of which waited for: 14 -> 16; matrix products, arithmetic and copies ran while one was open for 0% -> 2% of each run, Pallas kernels for 18% -> 16%
where the time goes in v15:
time: 149 us; the launch traced here: 148 us
  waiting for transfers between devices  52.2 us (35%)
  Pallas kernels  46.6 us (31%)
  starting transfers between devices  43.3 us (29%)
  local copies, waits for them, and re-layouts  5.54 us (4%)
    ppermute x17, waiting for transfers between devices, send(): return lax.ppermute(value, AXES, [(d, target(d)) for d in range(count)])  33.5 us
    ppermute x17, starting transfers between devices, send(): return lax.ppermute(value, AXES, [(d, target(d)) for d in range(count)])  28.8 us
    ppermute x6, waiting for transfers between devices, per_device(): own = own + lax.ppermute(own, AXES, [(d, d ^ flip) for d in range(count)])  18.7 us
    pallas_call x1, Pallas kernels, turn(): pl.pallas_call(turn_kernel, grid=(STEPS,), in_specs=[plane_spec(), whole(...  17 us
    ppermute x6, starting transfers between devices, per_device(): own = own + lax.ppermute(own, AXES, [(d, d ^ flip) for d in range(count)])  8.99 us
    pallas_call x1, Pallas kernels, prep(): pl.pallas_call(prep_kernel, in_specs=[vmem] * 4 + [pl.BlockSpec(memory_sp...  7.79 us
    pallas_call x1, Pallas kernels, make_second(): pl.pallas_call(second_kernel, grid=(STEPS,), in_specs=[plane_spec()] + [w...  3.7 us
    ppermute x1, starting transfers between devices, per_device(): lax.ppermute(relay, AXES, [(d, d ^ over_y ^ 1) for d in outer_ones])  3.58 us
  transfers between devices with their start and end apart: 26, of which 16 were waited for; matrix products, arithmetic and copies ran while one was open for 2% of the time, Pallas kernels for 16%

profile of v15, /device:TPU:0, one launch (start us, length us, event | category | flops | bytes accessed | tf_op | source)
XLA Modules:
  0.0 148.1 jit_solution(11395776569380046148)
XLA Ops:
  0.1 1.6 %copy-done = f32[16,16,16,128]{3,2,1,0:T(8,128)S(1)} copy-done((f32[16,16,16,128]{3,2,1,0:T(8,128)S(1)}, f32[16,16,16,128]{3,2,1,0:T(8,128)}, u32[]{:S(2)}) %copy-start) | copy-done | bytes 2097176
  1.7 2.1 %pack.1 = (f32[6,192,128]{2,1,0:T(8,128)}, f32[6,16,16,128]{3,2,1,0:T(8,128)S(1)}, f32[6,16,16,128]{3,2,1,0:T(8,128)S(1)}) custom-call(f32[16,256,128]{2,1,0:T(8,128)S(1)} %bitcast.13), custom_call_target="tpu_custom_call" | custom-call | flops 4294967296 | bytes 6291456 | tf_op jit(solution)/shard_map/pack/pallas_call | solution.py:163
  4.6 2.0 %collective-permute-start.4 = (f32[6,192,128]{2,1,0:T(8,128)}, f32[6,192,128]{2,1,0:T(8,128)S(1)}, u32[]{:S(2)}, u32[]{:S(2)}) collective-permute-start(f32[6,192,128]{2,1,0:T(8,128)} %get-tuple-element.45), channel_id=1, source_target_pairs={{0,32},{1,33},{2,34},{3,35},{4,36},{5,37},{6,38},{7,39},{8,40},{9,... | collective-permute-start | bytes 1769480 | tf_op jit(solution)/shard_map/ppermute | solution.py:764
  8.8 1.6 %collective-permute-start = (f32[24,128]{1,0:T(8,128)S(1)}, f32[24,128]{1,0:T(8,128)S(1)}, u32[]{:S(2)}, u32[]{:S(2)}) collective-permute-start(f32[24,128]{1,0:T(8,128)S(1)} %reshape.37.refs_1_), channel_id=1, source_target_pairs={{0,1},{1,2},{2,3},{3,4},{4,5},{5,6},{6,7},{7,8},{8,9},{9,10},{10,1... | collective-permute-start | bytes 36872 | tf_op jit(solution)/shard_map/ppermute | solution.py:764
  10.3 6.8 %collective-permute-start.1 = (f32[24,128]{1,0:T(8,128)S(1)}, f32[24,128]{1,0:T(8,128)S(1)}, u32[]{:S(2)}, u32[]{:S(2)}) collective-permute-start(f32[24,128]{1,0:T(8,128)S(1)} %reshape.37.refs_1_), channel_id=1, source_target_pairs={{0,31},{1,0},{2,1},{3,2},{4,3},{5,4},{6,5},{7,6},{8,7},{9,8},{10,9... | collective-permute-start | bytes 36872 | tf_op jit(solution)/shard_map/ppermute | solution.py:764
  19.2 3.1 %side_x.1.part_ref = f32[16,256,128]{2,1,0:T(8,128)S(1)} custom-call(f32[16,256,128]{2,1,0:T(8,128)S(1)} %bitcast.15, f32[16,256,128]{2,1,0:T(8,128)} %collective-permute-done.5.mate_ref), custom_call_target="tpu_custom_call" | custom-call | flops 16777216 | bytes 6291456 | tf_op jit(solution)/shard_map/side_x/pallas_call | solution.py:250
  23.0 3.6 %collective-permute-start.7 = (f32[6,192,128]{2,1,0:T(8,128)S(1)}, f32[6,192,128]{2,1,0:T(8,128)S(1)}, u32[]{:S(2)}, u32[]{:S(2)}) collective-permute-start(f32[6,192,128]{2,1,0:T(8,128)S(1)} %get-tuple-element.51), channel_id=1, source_target_pairs={{0,33},{3,34},{4,37},{7,38},{8,41},{11,42},{12,45},{15,46},{16,49}... | collective-permute-start | bytes 1769480 | tf_op jit(solution)/shard_map/ppermute | solution.py:793
  27.0 7.7 %collective-permute-start.12 = (f32[6,16,16,128]{3,2,1,0:T(8,128)S(1)}, f32[6,16,16,128]{3,2,1,0:T(8,128)S(1)}, u32[]{:S(2)}, u32[]{:S(2)}) collective-permute-start(f32[6,16,16,128]{3,2,1,0:T(8,128)S(1)} %get-tuple-element.56), channel_id=1, source_target_pairs={{0,31},{1,0},{2,1},{3,2},{4,3},{5,4},{6,5},{7,6},{8,7},{9,8},{10,9... | collective-permute-start | bytes 2359304 | tf_op jit(solution)/shard_map/ppermute | solution.py:764
  34.7 1.2 collective-permute-done.2.refs_1_
  37.2 7.8 %prep.1 = (bf16[2,4096,128]{2,1,0:T(8,128)(2,1)S(1)}, f32[3,48,128]{2,1,0:T(8,128)S(1)}, f32[48,128]{1,0:T(8,128)S(1)}) custom-call(f32[104,128]{1,0:T(8,128)S(1)} %stack.13.parcel_ref.refs_0_, f32[104,128]{1,0:T(8,128)S(1)} %collective-permute-done.2.refs_1_, f32[104,128]{1,0:T(8,128)S(1)} %collective-permute-done.3.refs_2_.parcel_ref, ...), custom_call_target="tpu_custom_call" | custom-call | flops 134217728 | bytes 10485760 | tf_op jit(solution)/shard_map/prep/pallas_call | solution.py:460
  45.0 1.3 collective-permute-start.14
  47.6 1.8 %collective-permute-start.9 = (f32[3,48,128]{2,1,0:T(8,128)S(1)}, f32[3,48,128]{2,1,0:T(8,128)S(1)}, u32[]{:S(2)}, u32[]{:S(2)}) collective-permute-start(f32[3,48,128]{2,1,0:T(8,128)S(1)} %add.34.refs_4_.rest_0_), channel_id=1, source_target_pairs={{0,32},{1,33},{2,34},{3,35},{4,36},{5,37},{6,38},{7,39},{8,40},{9,... | collective-permute-start | bytes 221192 | tf_op jit(solution)/shard_map/ppermute | solution.py:764
  49.5 6.4 %collective-permute-done.11.low_ref = f32[6,16,16,128]{3,2,1,0:T(8,128)S(1)} collective-permute-done((f32[6,16,16,128]{3,2,1,0:T(8,128)S(1)}, f32[6,16,16,128]{3,2,1,0:T(8,128)S(1)}, u32[]{:S(2)}, u32[]{:S(2)}) %collective-permute-start.11) | collective-permute-done | bytes 786464 | tf_op jit(solution)/shard_map/ppermute | solution.py:764
  55.9 3.0 %side_z.1.side_ref = f32[16,256,128]{2,1,0:T(8,128)S(1)} custom-call(f32[16,256,128]{2,1,0:T(8,128)S(1)} %bitcast.17, f32[16,256,128]{2,1,0:T(8,128)S(1)} %side_x.1.part_ref, f32[6,16,16,128]{3,2,1,0:T(8,128)S(1)} %collective-permute-done.11.low_ref, f32[6,16,16,128]{3,2,1,0:T(8,128)S(1)} %collective-permute-done.12.high_ref), custom_call_target="tpu_custom_call" | custom-call | flops 16777216 | bytes 8388608 | tf_op jit(solution)/shard_map/side_z/pallas_call | solution.py:275
  58.9 9.3 %collective-permute-done.9.refs_5_.rest_1_ = f32[3,48,128]{2,1,0:T(8,128)S(1)} collective-permute-done((f32[3,48,128]{2,1,0:T(8,128)S(1)}, f32[3,48,128]{2,1,0:T(8,128)S(1)}, u32[]{:S(2)}, u32[]{:S(2)}) %collective-permute-start.9) | collective-permute-done | bytes 73760 | tf_op jit(solution)/shard_map/ppermute | solution.py:764
  68.2 2.1 %first.1 = (f32[16,256,128]{2,1,0:T(8,128)S(1)}, f32[16,256,128]{2,1,0:T(8,128)S(1)}, f32[1632,128]{1,0:T(8,128)S(1)}, f32[1632,128]{1,0:T(8,128)S(1)}) custom-call(f32[16,256,128]{2,1,0:T(8,128)S(1)} %bitcast.18, f32[16,256,128]{2,1,0:T(8,128)S(1)} %side_z.1.side_ref, f32[16,256,128]{2,1,0:T(8,128)S(1)} %bitcast.20, ...), custom_call_target="tpu_custom_call" | custom-call | flops 16777216 | bytes 14680064 | tf_op jit(solution)/shard_map/first/pallas_call | solution.py:519
  70.5 7.7 %collective-permute-start.17 = (f32[1632,128]{1,0:T(8,128)S(1)}, f32[1632,128]{1,0:T(8,128)S(1)}, u32[]{:S(2)}, u32[]{:S(2)}) collective-permute-start(f32[1632,128]{1,0:T(8,128)S(1)} %get-tuple-element.63), channel_id=1, source_target_pairs={{0,31},{1,0},{2,1},{3,2},{4,3},{5,4},{6,5},{7,6},{8,7},{9,8},{10,9... | collective-permute-start | bytes 2506760 | tf_op jit(solution)/shard_map/ppermute | solution.py:764
  79.7 2.9 %side_again.1.part_ref = f32[16,256,128]{2,1,0:T(8,128)S(1)} custom-call(f32[16,256,128]{2,1,0:T(8,128)S(1)} %get-tuple-element.61.s_ref, f32[16,256,128]{2,1,0:T(8,128)S(1)} %collective-permute-done.15.mate_ref), custom_call_target="tpu_custom_call" | custom-call | flops 33554432 | bytes 6291456 | tf_op jit(solution)/shard_map/side_again/pallas_call | solution.py:302
  82.7 3.0 %base.1.base_ref = f32[16,256,128]{2,1,0:T(8,128)S(1)} custom-call(f32[16,256,128]{2,1,0:T(8,128)S(1)} %bitcast.19, f32[16,64,128]{2,1,0:T(8,128)S(1)} %collective-permute-done.10.mid_ref, f32[16,256,128]{2,1,0:T(8,128)S(1)} %bitcast.21, f32[16,256,128]{2,1,0:T(8,128)S(1)} %bitcast.26, f32[16,256,128]{2,1,0:T(8,128)S(1)} %get-tuple-element.60.q_ref, ...), custom_call_target="tpu_custom_call" | custom-call | flops 33554432 | bytes 16777216 | tf_op jit(solution)/shard_map/base/pallas_call | solution.py:571
  85.6 11.6 %collective-permute-done.16.low_ref = f32[1632,128]{1,0:T(8,128)S(1)} collective-permute-done((f32[1632,128]{1,0:T(8,128)S(1)}, f32[1632,128]{1,0:T(8,128)S(1)}, u32[]{:S(2)}, u32[]{:S(2)}) %collective-permute-start.16) | collective-permute-done | bytes 835616 | tf_op jit(solution)/shard_map/ppermute | solution.py:764
  97.2 3.7 %second.1 = (f32[16,256,128]{2,1,0:T(8,128)S(1)}, f32[64,128]{1,0:T(8,128)S(1)}, f32[64,128]{1,0:T(8,128)S(1)}) custom-call(f32[16,256,128]{2,1,0:T(8,128)S(1)} %base.1.base_ref, f32[1632,128]{1,0:T(8,128)S(1)} %collective-permute-done.16.low_ref, f32[1632,128]{1,0:T(8,128)S(1)} %collective-permute-done.17.high_ref, bf16[2,16,256,128]{3,2,1,0:T(8,128)(2,1)S(1)} %bitcast.24, ...), custom_call_target="tpu_custom_call" | custom-call | flops 134217728 | bytes 8388608 | tf_op jit(solution)/shard_map/second/pallas_call | solution.py:642
  102.5 3.6 %collective-permute-done.19 = f32[64,128]{1,0:T(8,128)S(1)} collective-permute-done((f32[64,128]{1,0:T(8,128)S(1)}, f32[64,128]{1,0:T(8,128)S(1)}, u32[]{:S(2)}, u32[]{:S(2)}) %collective-permute-start.19) | collective-permute-done | bytes 32800 | tf_op jit(solution)/shard_map/ppermute | solution.py:818
  106.5 4.8 %collective-permute-done.20 = f32[64,128]{1,0:T(8,128)S(1)} collective-permute-done((f32[64,128]{1,0:T(8,128)S(1)}, f32[64,128]{1,0:T(8,128)S(1)}, u32[]{:S(2)}, u32[]{:S(2)}) %collective-permute-start.20) | collective-permute-done | bytes 32800 | tf_op jit(solution)/shard_map/ppermute | solution.py:818
  111.3 3.9 %collective-permute-done.21 = f32[64,128]{1,0:T(8,128)S(1)} collective-permute-done((f32[64,128]{1,0:T(8,128)S(1)}, f32[64,128]{1,0:T(8,128)S(1)}, u32[]{:S(2)}, u32[]{:S(2)}) %collective-permute-start.21) | collective-permute-done | bytes 32800 | tf_op jit(solution)/shard_map/ppermute | solution.py:818
  115.2 3.8 %collective-permute-start.22 = (f32[64,128]{1,0:T(8,128)S(1)}, f32[64,128]{1,0:T(8,128)S(1)}, u32[]{:S(2)}, u32[]{:S(2)}) collective-permute-start(f32[64,128]{1,0:T(8,128)S(1)} %add.38), channel_id=1, source_target_pairs={{0,3},{1,2},{2,1},{3,0},{4,7},{5,6},{6,5},{7,4},{8,11},{9,10},{10,... | collective-permute-start | bytes 98312 | tf_op jit(solution)/shard_map/ppermute | solution.py:818
  119.0 1.9 %collective-permute-done.22 = f32[64,128]{1,0:T(8,128)S(1)} collective-permute-done((f32[64,128]{1,0:T(8,128)S(1)}, f32[64,128]{1,0:T(8,128)S(1)}, u32[]{:S(2)}, u32[]{:S(2)}) %collective-permute-start.22) | collective-permute-done | bytes 32800 | tf_op jit(solution)/shard_map/ppermute | solution.py:818
  120.9 1.6 %collective-permute-start.23 = (f32[64,128]{1,0:T(8,128)S(1)}, f32[64,128]{1,0:T(8,128)S(1)}, u32[]{:S(2)}, u32[]{:S(2)}) collective-permute-start(f32[64,128]{1,0:T(8,128)S(1)} %add.39), channel_id=1, source_target_pairs={{0,8},{1,9},{2,10},{3,11},{4,12},{5,13},{6,14},{7,15},{8,0},{9,1},... | collective-permute-start | bytes 98312 | tf_op jit(solution)/shard_map/ppermute | solution.py:818
  122.5 2.3 %collective-permute-done.23 = f32[64,128]{1,0:T(8,128)S(1)} collective-permute-done((f32[64,128]{1,0:T(8,128)S(1)}, f32[64,128]{1,0:T(8,128)S(1)}, u32[]{:S(2)}, u32[]{:S(2)}) %collective-permute-start.23) | collective-permute-done | bytes 32800 | tf_op jit(solution)/shard_map/ppermute | solution.py:818
  124.8 3.0 %collective-permute-start.24 = (f32[64,128]{1,0:T(8,128)S(1)}, f32[64,128]{1,0:T(8,128)S(1)}, u32[]{:S(2)}, u32[]{:S(2)}) collective-permute-start(f32[64,128]{1,0:T(8,128)S(1)} %add.40), channel_id=1, source_target_pairs={{0,24},{1,25},{2,26},{3,27},{4,28},{5,29},{6,30},{7,31},{8,16},{9,... | collective-permute-start | bytes 98312 | tf_op jit(solution)/shard_map/ppermute | solution.py:818
  127.8 2.1 %collective-permute-done.24 = f32[64,128]{1,0:T(8,128)S(1)} collective-permute-done((f32[64,128]{1,0:T(8,128)S(1)}, f32[64,128]{1,0:T(8,128)S(1)}, u32[]{:S(2)}, u32[]{:S(2)}) %collective-permute-start.24) | collective-permute-done | bytes 32800 | tf_op jit(solution)/shard_map/ppermute | solution.py:818
  129.9 1.2 collective-permute-done.25.other_ref
  131.1 17.0 %turn.1 = f32[16,256,128]{2,1,0:T(8,128)} custom-call(f32[16,256,128]{2,1,0:T(8,128)S(1)} %get-tuple-element.68.second_ref, f32[64,128]{1,0:T(8,128)S(1)} %add.41.own_ref, f32[64,128]{1,0:T(8,128)S(1)} %collective-permute-done.25.other_ref, s32[1]{0:T(128)} %bitcast.3.rest_3_.upper_ref), custom_call_target="tpu_custom_call" | custom-call | flops 268435456 | bytes 4194304 | tf_op jit(solution)/shard_map/turn/pallas_call | solution.py:741
  (65 shorter events, 12.3 us)
Async XLA Ops:
  0.0 19.2 %collective-permute-start.5 = (f32[16,256,128]{2,1,0:T(8,128)}, f32[16,256,128]{2,1,0:T(8,128)}, u32[]{:S(2)}, u32[]{:S(2)}) collective-permute-start(f32[16,256,128]{2,1,0:T(8,128)} %bitcast.12), channel_id=1, source_target_pairs={{0,64},{1,65},{2,66},{3,67},{4,68},{5,69},{6,70},{7,71},{8,72},{9,... | collective-permute-start | bytes 6291464 | tf_op jit(solution)/shard_map/ppermute | solution.py:764
  0.1 1.6 %copy-start = (f32[16,16,16,128]{3,2,1,0:T(8,128)S(1)}, f32[16,16,16,128]{3,2,1,0:T(8,128)}, u32[]{:S(2)}) copy-start(f32[16,16,16,128]{3,2,1,0:T(8,128)} %param.5) | copy-start | bytes 6291460
  1.7 5.0 %copy-start.4 = (f32[4,9,9,9]{3,0,2,1:T(4,128)S(1)}, f32[4,9,9,9]{3,0,2,1:T(4,128)}, u32[]{:S(2)}) copy-start(f32[4,9,9,9]{3,0,2,1:T(4,128)} %param.8) | copy-start | bytes 34996
  1.7 6.8 %copy-start.5 = (s32[4,3]{1,0:T(4,128)S(1)}, s32[4,3]{1,0:T(4,128)}, u32[]{:S(2)}) copy-start(s32[4,3]{1,0:T(4,128)} %param.7) | copy-start | bytes 148
  1.7 6.8 %copy-start.6 = (f32[4]{0:T(128)S(1)}, f32[4]{0:T(128)}, u32[]{:S(2)}) copy-start(f32[4]{0:T(128)} %param.9) | copy-start | bytes 52
  1.7 17.2 %copy-start.1 = (f32[16,16,16,128]{3,2,1,0:T(8,128)S(1)}, f32[16,16,16,128]{3,2,1,0:T(8,128)}, u32[]{:S(2)}) copy-start(f32[16,16,16,128]{3,2,1,0:T(8,128)} %param.5) | copy-start | bytes 6291460
  4.6 18.4 %collective-permute-start.4 = (f32[6,192,128]{2,1,0:T(8,128)}, f32[6,192,128]{2,1,0:T(8,128)S(1)}, u32[]{:S(2)}, u32[]{:S(2)}) collective-permute-start(f32[6,192,128]{2,1,0:T(8,128)} %get-tuple-element.45), channel_id=1, source_target_pairs={{0,32},{1,33},{2,34},{3,35},{4,36},{5,37},{6,38},{7,39},{8,40},{9,... | collective-permute-start | bytes 1769480 | tf_op jit(solution)/shard_map/ppermute | solution.py:764
  8.8 10.0 %collective-permute-start = (f32[24,128]{1,0:T(8,128)S(1)}, f32[24,128]{1,0:T(8,128)S(1)}, u32[]{:S(2)}, u32[]{:S(2)}) collective-permute-start(f32[24,128]{1,0:T(8,128)S(1)} %reshape.37.refs_1_), channel_id=1, source_target_pairs={{0,1},{1,2},{2,3},{3,4},{4,5},{5,6},{6,7},{7,8},{8,9},{9,10},{10,1... | collective-permute-start | bytes 36872 | tf_op jit(solution)/shard_map/ppermute | solution.py:764
  10.3 8.4 %collective-permute-start.1 = (f32[24,128]{1,0:T(8,128)S(1)}, f32[24,128]{1,0:T(8,128)S(1)}, u32[]{:S(2)}, u32[]{:S(2)}) collective-permute-start(f32[24,128]{1,0:T(8,128)S(1)} %reshape.37.refs_1_), channel_id=1, source_target_pairs={{0,31},{1,0},{2,1},{3,2},{4,3},{5,4},{6,5},{7,6},{8,7},{9,8},{10,9... | collective-permute-start | bytes 36872 | tf_op jit(solution)/shard_map/ppermute | solution.py:764
  18.8 4.2 %collective-permute-start.3 = (f32[104,128]{1,0:T(8,128)S(1)}, f32[104,128]{1,0:T(8,128)S(1)}, u32[]{:S(2)}, u32[]{:S(2)}) collective-permute-start(f32[104,128]{1,0:T(8,128)S(1)} %stack.13.parcel_ref.refs_0_), channel_id=1, source_target_pairs={{0,32},{1,33},{2,34},{3,35},{4,36},{5,37},{6,38},{7,39},{8,40},{9,... | collective-permute-start | bytes 159752 | tf_op jit(solution)/shard_map/ppermute | solution.py:764
  19.2 7.7 %copy-start.3 = (f32[6,16,16,128]{3,2,1,0:T(8,128)S(1)}, f32[6,16,16,128]{3,2,1,0:T(8,128)}, u32[]{:S(2)}) copy-start(f32[6,16,16,128]{3,2,1,0:T(8,128)} %copy-done.2) | copy-start | bytes 2359300
  23.0 22.0 %collective-permute-start.7 = (f32[6,192,128]{2,1,0:T(8,128)S(1)}, f32[6,192,128]{2,1,0:T(8,128)S(1)}, u32[]{:S(2)}, u32[]{:S(2)}) collective-permute-start(f32[6,192,128]{2,1,0:T(8,128)S(1)} %get-tuple-element.51), channel_id=1, source_target_pairs={{0,33},{3,34},{4,37},{7,38},{8,41},{11,42},{12,45},{15,46},{16,49}... | collective-permute-start | bytes 1769480 | tf_op jit(solution)/shard_map/ppermute | solution.py:793
  26.6 41.6 %collective-permute-start.13 = (f32[1920,128]{1,0:T(8,128)S(1)}, f32[1920,128]{1,0:T(8,128)S(1)}, u32[]{:S(2)}, u32[]{:S(2)}) collective-permute-start(f32[1920,128]{1,0:T(8,128)S(1)} %get-tuple-element.58), channel_id=1, source_target_pairs={{0,32},{1,33},{2,34},{3,35},{4,36},{5,37},{6,38},{7,39},{8,40},{9,... | collective-permute-start | bytes 2949128 | tf_op jit(solution)/shard_map/ppermute | solution.py:764
  26.9 29.0 %collective-permute-start.11 = (f32[6,16,16,128]{3,2,1,0:T(8,128)S(1)}, f32[6,16,16,128]{3,2,1,0:T(8,128)S(1)}, u32[]{:S(2)}, u32[]{:S(2)}) collective-permute-start(f32[6,16,16,128]{3,2,1,0:T(8,128)S(1)} %copy-done.3), channel_id=1, source_target_pairs={{0,1},{1,2},{2,3},{3,4},{4,5},{5,6},{6,7},{7,8},{8,9},{9,10},{10,1... | collective-permute-start | bytes 2359304 | tf_op jit(solution)/shard_map/ppermute | solution.py:764
  27.0 29.0 %collective-permute-start.12 = (f32[6,16,16,128]{3,2,1,0:T(8,128)S(1)}, f32[6,16,16,128]{3,2,1,0:T(8,128)S(1)}, u32[]{:S(2)}, u32[]{:S(2)}) collective-permute-start(f32[6,16,16,128]{3,2,1,0:T(8,128)S(1)} %get-tuple-element.56), channel_id=1, source_target_pairs={{0,31},{1,0},{2,1},{3,2},{4,3},{5,4},{6,5},{7,6},{8,7},{9,8},{10,9... | collective-permute-start | bytes 2359304 | tf_op jit(solution)/shard_map/ppermute | solution.py:764
  34.7 1.2 collective-permute-start.2
  35.9 1.2 collective-permute-start.6
  45.0 23.2 %collective-permute-start.14 = (f32[6,192,128]{2,1,0:T(8,128)S(1)}, f32[6,192,128]{2,1,0:T(8,128)S(1)}, u32[]{:S(2)}, u32[]{:S(2)}) collective-permute-start(f32[6,192,128]{2,1,0:T(8,128)S(1)} %collective-permute-done.7), channel_id=1, source_target_pairs={{1,0},{2,3},{5,4},{6,7},{9,8},{10,11},{13,12},{14,15},{17,16},{18,... | collective-permute-start | bytes 1769480 | tf_op jit(solution)/shard_map/ppermute | solution.py:799
  46.3 1.3 collective-permute-start.8
  47.6 20.6 %collective-permute-start.9 = (f32[3,48,128]{2,1,0:T(8,128)S(1)}, f32[3,48,128]{2,1,0:T(8,128)S(1)}, u32[]{:S(2)}, u32[]{:S(2)}) collective-permute-start(f32[3,48,128]{2,1,0:T(8,128)S(1)} %add.34.refs_4_.rest_0_), channel_id=1, source_target_pairs={{0,32},{1,33},{2,34},{3,35},{4,36},{5,37},{6,38},{7,39},{8,40},{9,... | collective-permute-start | bytes 221192 | tf_op jit(solution)/shard_map/ppermute | solution.py:764
  70.3 9.4 %collective-permute-start.15 = (f32[16,256,128]{2,1,0:T(8,128)S(1)}, f32[16,256,128]{2,1,0:T(8,128)S(1)}, u32[]{:S(2)}, u32[]{:S(2)}) collective-permute-start(f32[16,256,128]{2,1,0:T(8,128)S(1)} %get-tuple-element.61.s_ref), channel_id=1, source_target_pairs={{0,64},{1,65},{2,66},{3,67},{4,68},{5,69},{6,70},{7,71},{8,72},{9,... | collective-permute-start | bytes 6291464 | tf_op jit(solution)/shard_map/ppermute | solution.py:764
  70.4 26.8 %collective-permute-start.16 = (f32[1632,128]{1,0:T(8,128)S(1)}, f32[1632,128]{1,0:T(8,128)S(1)}, u32[]{:S(2)}, u32[]{:S(2)}) collective-permute-start(f32[1632,128]{1,0:T(8,128)S(1)} %get-tuple-element.62), channel_id=1, source_target_pairs={{0,1},{1,2},{2,3},{3,4},{4,5},{5,6},{6,7},{7,8},{8,9},{9,10},{10,1... | collective-permute-start | bytes 2506760 | tf_op jit(solution)/shard_map/ppermute | solution.py:764
  70.5 26.7 %collective-permute-start.17 = (f32[1632,128]{1,0:T(8,128)S(1)}, f32[1632,128]{1,0:T(8,128)S(1)}, u32[]{:S(2)}, u32[]{:S(2)}) collective-permute-start(f32[1632,128]{1,0:T(8,128)S(1)} %get-tuple-element.63), channel_id=1, source_target_pairs={{0,31},{1,0},{2,1},{3,2},{4,3},{5,4},{6,5},{7,6},{8,7},{9,8},{10,9... | collective-permute-start | bytes 2506760 | tf_op jit(solution)/shard_map/ppermute | solution.py:764
  78.2 4.5 %collective-permute-start.10 = (f32[16,64,128]{2,1,0:T(8,128)S(1)}, f32[16,64,128]{2,1,0:T(8,128)S(1)}, u32[]{:S(2)}, u32[]{:S(2)}) collective-permute-start(f32[16,64,128]{2,1,0:T(8,128)S(1)} %get-tuple-element.53), channel_id=1, source_target_pairs={{1,33},{2,34},{5,37},{6,38},{9,41},{10,42},{13,45},{14,46},{17,49}... | collective-permute-start | bytes 1572872 | tf_op jit(solution)/shard_map/ppermute | solution.py:809
  100.9 1.3 collective-permute-start.18
  102.2 3.9 %collective-permute-start.19 = (f32[64,128]{1,0:T(8,128)S(1)}, f32[64,128]{1,0:T(8,128)S(1)}, u32[]{:S(2)}, u32[]{:S(2)}) collective-permute-start(f32[64,128]{1,0:T(8,128)S(1)} %add.35), channel_id=1, source_target_pairs={{0,32},{1,33},{2,34},{3,35},{4,36},{5,37},{6,38},{7,39},{8,40},{9,... | collective-permute-start | bytes 98312 | tf_op jit(solution)/shard_map/ppermute | solution.py:818
  106.2 5.1 %collective-permute-start.20 = (f32[64,128]{1,0:T(8,128)S(1)}, f32[64,128]{1,0:T(8,128)S(1)}, u32[]{:S(2)}, u32[]{:S(2)}) collective-permute-start(f32[64,128]{1,0:T(8,128)S(1)} %add.36), channel_id=1, source_target_pairs={{0,36},{1,37},{2,38},{3,39},{4,32},{5,33},{6,34},{7,35},{8,44},{9,... | collective-permute-start | bytes 98312 | tf_op jit(solution)/shard_map/ppermute | solution.py:818
  111.3 3.9 %collective-permute-start.21 = (f32[64,128]{1,0:T(8,128)S(1)}, f32[64,128]{1,0:T(8,128)S(1)}, u32[]{:S(2)}, u32[]{:S(2)}) collective-permute-start(f32[64,128]{1,0:T(8,128)S(1)} %add.37), channel_id=1, source_target_pairs={{0,1},{1,0},{2,3},{3,2},{4,5},{5,4},{6,7},{7,6},{8,9},{9,8},{10,11... | collective-permute-start | bytes 98312 | tf_op jit(solution)/shard_map/ppermute | solution.py:818
  115.2 5.7 %collective-permute-start.22 = (f32[64,128]{1,0:T(8,128)S(1)}, f32[64,128]{1,0:T(8,128)S(1)}, u32[]{:S(2)}, u32[]{:S(2)}) collective-permute-start(f32[64,128]{1,0:T(8,128)S(1)} %add.38), channel_id=1, source_target_pairs={{0,3},{1,2},{2,1},{3,0},{4,7},{5,6},{6,5},{7,4},{8,11},{9,10},{10,... | collective-permute-start | bytes 98312 | tf_op jit(solution)/shard_map/ppermute | solution.py:818
  120.9 3.9 %collective-permute-start.23 = (f32[64,128]{1,0:T(8,128)S(1)}, f32[64,128]{1,0:T(8,128)S(1)}, u32[]{:S(2)}, u32[]{:S(2)}) collective-permute-start(f32[64,128]{1,0:T(8,128)S(1)} %add.39), channel_id=1, source_target_pairs={{0,8},{1,9},{2,10},{3,11},{4,12},{5,13},{6,14},{7,15},{8,0},{9,1},... | collective-permute-start | bytes 98312 | tf_op jit(solution)/shard_map/ppermute | solution.py:818
  124.8 5.1 %collective-permute-start.24 = (f32[64,128]{1,0:T(8,128)S(1)}, f32[64,128]{1,0:T(8,128)S(1)}, u32[]{:S(2)}, u32[]{:S(2)}) collective-permute-start(f32[64,128]{1,0:T(8,128)S(1)} %add.40), channel_id=1, source_target_pairs={{0,24},{1,25},{2,26},{3,27},{4,28},{5,29},{6,30},{7,31},{8,16},{9,... | collective-permute-start | bytes 98312 | tf_op jit(solution)/shard_map/ppermute | solution.py:818
  129.9 1.2 collective-permute-start.25
  (1 other events, 0.9 us)

commit v16 on v15

--- a/solution.py
+++ b/solution.py
@@ -783,16 +783,16 @@
     one_edge = send(one_edge, over_y)
     head, tail, below, above = barrier((head, tail, below, above))
     parcel = stack(below, atoms, above, pot)
-    parcel_y = send(parcel, over_y)
+    parcel_xy = send(parcel, over_x ^ over_y)
     parcel_x = send(parcel, over_x)
     low, high = send(tail, 0, 1), send(head, 0, -1)
     message, relay, mid = pack_rest(s, inner)
     vb = spread(parcel)
     beside = side_x(s, mate)
-    parcel_y, one_edge, message, relay, beside = barrier((parcel_y, one_edge, message, relay, beside))
+    parcel_xy, one_edge, message, relay, beside = barrier((parcel_xy, one_edge, message, relay, beside))
     relayed = lax.ppermute(relay, AXES, [(d, d ^ over_y ^ 1) for d in outer_ones])
     message = send(message, over_y)
-    parcel_xy = send(parcel_y, over_x)
+    parcel_y = send(parcel_xy, over_x)
     gg, part, energy = prep([parcel, parcel_x, parcel_y, parcel_xy], corner, vb, s)
 
     part, relayed = barrier((part, relayed))

time: 149 us -> 150 us (level)
  no operation moved by 1% of the time
where the time goes in v16:
time: 150 us; the launch traced here: 148 us
  waiting for transfers between devices  52.4 us (35%)
  Pallas kernels  46.6 us (31%)
  starting transfers between devices  43.2 us (29%)
  local copies, waits for them, and re-layouts  5.54 us (4%)
    ppermute x17, waiting for transfers between devices, send(): return lax.ppermute(value, AXES, [(d, target(d)) for d in range(count)])  33.6 us
    ppermute x17, starting transfers between devices, send(): return lax.ppermute(value, AXES, [(d, target(d)) for d in range(count)])  28.8 us
    ppermute x6, waiting for transfers between devices, per_device(): own = own + lax.ppermute(own, AXES, [(d, d ^ flip) for d in range(count)])  18.8 us
    pallas_call x1, Pallas kernels, turn(): pl.pallas_call(turn_kernel, grid=(STEPS,), in_specs=[plane_spec(), whole(...  17 us
    ppermute x6, starting transfers between devices, per_device(): own = own + lax.ppermute(own, AXES, [(d, d ^ flip) for d in range(count)])  8.89 us
    pallas_call x1, Pallas kernels, prep(): pl.pallas_call(prep_kernel, in_specs=[vmem] * 4 + [pl.BlockSpec(memory_sp...  7.81 us
    pallas_call x1, Pallas kernels, make_second(): pl.pallas_call(second_kernel, grid=(STEPS,), in_specs=[plane_spec()] + [w...  3.69 us
    ppermute x1, starting transfers between devices, per_device(): lax.ppermute(relay, AXES, [(d, d ^ over_y ^ 1) for d in outer_ones])  3.56 us
  transfers between devices with their start and end apart: 26, of which 16 were waited for; matrix products, arithmetic and copies ran while one was open for 2% of the time, Pallas kernels for 16%

profile of v16, /device:TPU:0, one launch (start us, length us, event | category | flops | bytes accessed | tf_op | source)
XLA Modules:
  0.0 148.2 jit_solution(2807154590088795648)
XLA Ops:
  0.1 1.6 %copy-done = f32[16,16,16,128]{3,2,1,0:T(8,128)S(1)} copy-done((f32[16,16,16,128]{3,2,1,0:T(8,128)S(1)}, f32[16,16,16,128]{3,2,1,0:T(8,128)}, u32[]{:S(2)}) %copy-start) | copy-done | bytes 2097176
  1.7 2.1 %pack.1 = (f32[6,192,128]{2,1,0:T(8,128)}, f32[6,16,16,128]{3,2,1,0:T(8,128)S(1)}, f32[6,16,16,128]{3,2,1,0:T(8,128)S(1)}) custom-call(f32[16,256,128]{2,1,0:T(8,128)S(1)} %bitcast.13), custom_call_target="tpu_custom_call" | custom-call | flops 4294967296 | bytes 6291456 | tf_op jit(solution)/shard_map/pack/pallas_call | solution.py:163
  4.6 2.0 %collective-permute-start.4 = (f32[6,192,128]{2,1,0:T(8,128)}, f32[6,192,128]{2,1,0:T(8,128)S(1)}, u32[]{:S(2)}, u32[]{:S(2)}) collective-permute-start(f32[6,192,128]{2,1,0:T(8,128)} %get-tuple-element.45), channel_id=1, source_target_pairs={{0,32},{1,33},{2,34},{3,35},{4,36},{5,37},{6,38},{7,39},{8,40},{9,... | collective-permute-start | bytes 1769480 | tf_op jit(solution)/shard_map/ppermute | solution.py:764
  8.8 1.6 %collective-permute-start = (f32[24,128]{1,0:T(8,128)S(1)}, f32[24,128]{1,0:T(8,128)S(1)}, u32[]{:S(2)}, u32[]{:S(2)}) collective-permute-start(f32[24,128]{1,0:T(8,128)S(1)} %reshape.37.refs_1_), channel_id=1, source_target_pairs={{0,1},{1,2},{2,3},{3,4},{4,5},{5,6},{6,7},{7,8},{8,9},{9,10},{10,1... | collective-permute-start | bytes 36872 | tf_op jit(solution)/shard_map/ppermute | solution.py:764
  10.3 6.8 %collective-permute-start.1 = (f32[24,128]{1,0:T(8,128)S(1)}, f32[24,128]{1,0:T(8,128)S(1)}, u32[]{:S(2)}, u32[]{:S(2)}) collective-permute-start(f32[24,128]{1,0:T(8,128)S(1)} %reshape.37.refs_1_), channel_id=1, source_target_pairs={{0,31},{1,0},{2,1},{3,2},{4,3},{5,4},{6,5},{7,6},{8,7},{9,8},{10,9... | collective-permute-start | bytes 36872 | tf_op jit(solution)/shard_map/ppermute | solution.py:764
  19.2 3.1 %side_x.1.part_ref = f32[16,256,128]{2,1,0:T(8,128)S(1)} custom-call(f32[16,256,128]{2,1,0:T(8,128)S(1)} %bitcast.15, f32[16,256,128]{2,1,0:T(8,128)} %collective-permute-done.5.mate_ref), custom_call_target="tpu_custom_call" | custom-call | flops 16777216 | bytes 6291456 | tf_op jit(solution)/shard_map/side_x/pallas_call | solution.py:250
  22.6 3.6 %collective-permute-start.7 = (f32[6,192,128]{2,1,0:T(8,128)S(1)}, f32[6,192,128]{2,1,0:T(8,128)S(1)}, u32[]{:S(2)}, u32[]{:S(2)}) collective-permute-start(f32[6,192,128]{2,1,0:T(8,128)S(1)} %get-tuple-element.51), channel_id=1, source_target_pairs={{0,33},{3,34},{4,37},{7,38},{8,41},{11,42},{12,45},{15,46},{16,49}... | collective-permute-start | bytes 1769480 | tf_op jit(solution)/shard_map/ppermute | solution.py:793
  26.7 7.7 %collective-permute-start.12 = (f32[6,16,16,128]{3,2,1,0:T(8,128)S(1)}, f32[6,16,16,128]{3,2,1,0:T(8,128)S(1)}, u32[]{:S(2)}, u32[]{:S(2)}) collective-permute-start(f32[6,16,16,128]{3,2,1,0:T(8,128)S(1)} %get-tuple-element.56), channel_id=1, source_target_pairs={{0,31},{1,0},{2,1},{3,2},{4,3},{5,4},{6,5},{7,6},{8,7},{9,8},{10,9... | collective-permute-start | bytes 2359304 | tf_op jit(solution)/shard_map/ppermute | solution.py:764
  34.4 1.2 collective-permute-done.2.refs_1_
  36.9 7.8 %prep.1 = (bf16[2,4096,128]{2,1,0:T(8,128)(2,1)S(1)}, f32[3,48,128]{2,1,0:T(8,128)S(1)}, f32[48,128]{1,0:T(8,128)S(1)}) custom-call(f32[104,128]{1,0:T(8,128)S(1)} %stack.13.parcel_ref.refs_0_, f32[104,128]{1,0:T(8,128)S(1)} %collective-permute-done.2.refs_1_, f32[104,128]{1,0:T(8,128)S(1)} %collective-permute-done.6.refs_2_.parcel_ref, ...), custom_call_target="tpu_custom_call" | custom-call | flops 134217728 | bytes 10485760 | tf_op jit(solution)/shard_map/prep/pallas_call | solution.py:460
  44.7 1.3 collective-permute-start.14
  47.4 1.7 %collective-permute-start.9 = (f32[3,48,128]{2,1,0:T(8,128)S(1)}, f32[3,48,128]{2,1,0:T(8,128)S(1)}, u32[]{:S(2)}, u32[]{:S(2)}) collective-permute-start(f32[3,48,128]{2,1,0:T(8,128)S(1)} %add.34.refs_4_.rest_0_), channel_id=1, source_target_pairs={{0,32},{1,33},{2,34},{3,35},{4,36},{5,37},{6,38},{7,39},{8,40},{9,... | collective-permute-start | bytes 221192 | tf_op jit(solution)/shard_map/ppermute | solution.py:764
  49.1 6.9 %collective-permute-done.11.low_ref = f32[6,16,16,128]{3,2,1,0:T(8,128)S(1)} collective-permute-done((f32[6,16,16,128]{3,2,1,0:T(8,128)S(1)}, f32[6,16,16,128]{3,2,1,0:T(8,128)S(1)}, u32[]{:S(2)}, u32[]{:S(2)}) %collective-permute-start.11) | collective-permute-done | bytes 786464 | tf_op jit(solution)/shard_map/ppermute | solution.py:764
  56.0 3.0 %side_z.1.side_ref = f32[16,256,128]{2,1,0:T(8,128)S(1)} custom-call(f32[16,256,128]{2,1,0:T(8,128)S(1)} %bitcast.17, f32[16,256,128]{2,1,0:T(8,128)S(1)} %side_x.1.part_ref, f32[6,16,16,128]{3,2,1,0:T(8,128)S(1)} %collective-permute-done.11.low_ref, f32[6,16,16,128]{3,2,1,0:T(8,128)S(1)} %collective-permute-done.12.high_ref), custom_call_target="tpu_custom_call" | custom-call | flops 16777216 | bytes 8388608 | tf_op jit(solution)/shard_map/side_z/pallas_call | solution.py:275
  59.0 9.3 %collective-permute-done.9.refs_5_.rest_1_ = f32[3,48,128]{2,1,0:T(8,128)S(1)} collective-permute-done((f32[3,48,128]{2,1,0:T(8,128)S(1)}, f32[3,48,128]{2,1,0:T(8,128)S(1)}, u32[]{:S(2)}, u32[]{:S(2)}) %collective-permute-start.9) | collective-permute-done | bytes 73760 | tf_op jit(solution)/shard_map/ppermute | solution.py:764
  68.3 2.1 %first.1 = (f32[16,256,128]{2,1,0:T(8,128)S(1)}, f32[16,256,128]{2,1,0:T(8,128)S(1)}, f32[1632,128]{1,0:T(8,128)S(1)}, f32[1632,128]{1,0:T(8,128)S(1)}) custom-call(f32[16,256,128]{2,1,0:T(8,128)S(1)} %bitcast.18, f32[16,256,128]{2,1,0:T(8,128)S(1)} %side_z.1.side_ref, f32[16,256,128]{2,1,0:T(8,128)S(1)} %bitcast.20, ...), custom_call_target="tpu_custom_call" | custom-call | flops 16777216 | bytes 14680064 | tf_op jit(solution)/shard_map/first/pallas_call | solution.py:519
  70.6 7.7 %collective-permute-start.17 = (f32[1632,128]{1,0:T(8,128)S(1)}, f32[1632,128]{1,0:T(8,128)S(1)}, u32[]{:S(2)}, u32[]{:S(2)}) collective-permute-start(f32[1632,128]{1,0:T(8,128)S(1)} %get-tuple-element.63), channel_id=1, source_target_pairs={{0,31},{1,0},{2,1},{3,2},{4,3},{5,4},{6,5},{7,6},{8,7},{9,8},{10,9... | collective-permute-start | bytes 2506760 | tf_op jit(solution)/shard_map/ppermute | solution.py:764
  79.9 2.9 %side_again.1.part_ref = f32[16,256,128]{2,1,0:T(8,128)S(1)} custom-call(f32[16,256,128]{2,1,0:T(8,128)S(1)} %get-tuple-element.61.s_ref, f32[16,256,128]{2,1,0:T(8,128)S(1)} %collective-permute-done.15.mate_ref), custom_call_target="tpu_custom_call" | custom-call | flops 33554432 | bytes 6291456 | tf_op jit(solution)/shard_map/side_again/pallas_call | solution.py:302
  82.8 3.0 %base.1.base_ref = f32[16,256,128]{2,1,0:T(8,128)S(1)} custom-call(f32[16,256,128]{2,1,0:T(8,128)S(1)} %bitcast.19, f32[16,64,128]{2,1,0:T(8,128)S(1)} %collective-permute-done.10.mid_ref, f32[16,256,128]{2,1,0:T(8,128)S(1)} %bitcast.21, f32[16,256,128]{2,1,0:T(8,128)S(1)} %bitcast.26, f32[16,256,128]{2,1,0:T(8,128)S(1)} %get-tuple-element.60.q_ref, ...), custom_call_target="tpu_custom_call" | custom-call | flops 33554432 | bytes 16777216 | tf_op jit(solution)/shard_map/base/pallas_call | solution.py:571
  85.8 11.6 %collective-permute-done.16.low_ref = f32[1632,128]{1,0:T(8,128)S(1)} collective-permute-done((f32[1632,128]{1,0:T(8,128)S(1)}, f32[1632,128]{1,0:T(8,128)S(1)}, u32[]{:S(2)}, u32[]{:S(2)}) %collective-permute-start.16) | collective-permute-done | bytes 835616 | tf_op jit(solution)/shard_map/ppermute | solution.py:764
  97.3 3.7 %second.1 = (f32[16,256,128]{2,1,0:T(8,128)S(1)}, f32[64,128]{1,0:T(8,128)S(1)}, f32[64,128]{1,0:T(8,128)S(1)}) custom-call(f32[16,256,128]{2,1,0:T(8,128)S(1)} %base.1.base_ref, f32[1632,128]{1,0:T(8,128)S(1)} %collective-permute-done.16.low_ref, f32[1632,128]{1,0:T(8,128)S(1)} %collective-permute-done.17.high_ref, bf16[2,16,256,128]{3,2,1,0:T(8,128)(2,1)S(1)} %bitcast.24, ...), custom_call_target="tpu_custom_call" | custom-call | flops 134217728 | bytes 8388608 | tf_op jit(solution)/shard_map/second/pallas_call | solution.py:642
  102.5 3.7 %collective-permute-done.19 = f32[64,128]{1,0:T(8,128)S(1)} collective-permute-done((f32[64,128]{1,0:T(8,128)S(1)}, f32[64,128]{1,0:T(8,128)S(1)}, u32[]{:S(2)}, u32[]{:S(2)}) %collective-permute-start.19) | collective-permute-done | bytes 32800 | tf_op jit(solution)/shard_map/ppermute | solution.py:818
  106.6 4.8 %collective-permute-done.20 = f32[64,128]{1,0:T(8,128)S(1)} collective-permute-done((f32[64,128]{1,0:T(8,128)S(1)}, f32[64,128]{1,0:T(8,128)S(1)}, u32[]{:S(2)}, u32[]{:S(2)}) %collective-permute-start.20) | collective-permute-done | bytes 32800 | tf_op jit(solution)/shard_map/ppermute | solution.py:818
  111.4 3.9 %collective-permute-done.21 = f32[64,128]{1,0:T(8,128)S(1)} collective-permute-done((f32[64,128]{1,0:T(8,128)S(1)}, f32[64,128]{1,0:T(8,128)S(1)}, u32[]{:S(2)}, u32[]{:S(2)}) %collective-permute-start.21) | collective-permute-done | bytes 32800 | tf_op jit(solution)/shard_map/ppermute | solution.py:818
  115.3 3.8 %collective-permute-start.22 = (f32[64,128]{1,0:T(8,128)S(1)}, f32[64,128]{1,0:T(8,128)S(1)}, u32[]{:S(2)}, u32[]{:S(2)}) collective-permute-start(f32[64,128]{1,0:T(8,128)S(1)} %add.38), channel_id=1, source_target_pairs={{0,3},{1,2},{2,1},{3,0},{4,7},{5,6},{6,5},{7,4},{8,11},{9,10},{10,... | collective-permute-start | bytes 98312 | tf_op jit(solution)/shard_map/ppermute | solution.py:818
  119.1 1.9 %collective-permute-done.22 = f32[64,128]{1,0:T(8,128)S(1)} collective-permute-done((f32[64,128]{1,0:T(8,128)S(1)}, f32[64,128]{1,0:T(8,128)S(1)}, u32[]{:S(2)}, u32[]{:S(2)}) %collective-permute-start.22) | collective-permute-done | bytes 32800 | tf_op jit(solution)/shard_map/ppermute | solution.py:818
  121.0 1.6 %collective-permute-start.23 = (f32[64,128]{1,0:T(8,128)S(1)}, f32[64,128]{1,0:T(8,128)S(1)}, u32[]{:S(2)}, u32[]{:S(2)}) collective-permute-start(f32[64,128]{1,0:T(8,128)S(1)} %add.39), channel_id=1, source_target_pairs={{0,8},{1,9},{2,10},{3,11},{4,12},{5,13},{6,14},{7,15},{8,0},{9,1},... | collective-permute-start | bytes 98312 | tf_op jit(solution)/shard_map/ppermute | solution.py:818
  122.6 2.3 %collective-permute-done.23 = f32[64,128]{1,0:T(8,128)S(1)} collective-permute-done((f32[64,128]{1,0:T(8,128)S(1)}, f32[64,128]{1,0:T(8,128)S(1)}, u32[]{:S(2)}, u32[]{:S(2)}) %collective-permute-start.23) | collective-permute-done | bytes 32800 | tf_op jit(solution)/shard_map/ppermute | solution.py:818
  124.9 3.0 %collective-permute-start.24 = (f32[64,128]{1,0:T(8,128)S(1)}, f32[64,128]{1,0:T(8,128)S(1)}, u32[]{:S(2)}, u32[]{:S(2)}) collective-permute-start(f32[64,128]{1,0:T(8,128)S(1)} %add.40), channel_id=1, source_target_pairs={{0,24},{1,25},{2,26},{3,27},{4,28},{5,29},{6,30},{7,31},{8,16},{9,... | collective-permute-start | bytes 98312 | tf_op jit(solution)/shard_map/ppermute | solution.py:818
  127.9 2.1 %collective-permute-done.24 = f32[64,128]{1,0:T(8,128)S(1)} collective-permute-done((f32[64,128]{1,0:T(8,128)S(1)}, f32[64,128]{1,0:T(8,128)S(1)}, u32[]{:S(2)}, u32[]{:S(2)}) %collective-permute-start.24) | collective-permute-done | bytes 32800 | tf_op jit(solution)/shard_map/ppermute | solution.py:818
  130.0 1.2 collective-permute-done.25.other_ref
  131.2 17.0 %turn.1 = f32[16,256,128]{2,1,0:T(8,128)} custom-call(f32[16,256,128]{2,1,0:T(8,128)S(1)} %get-tuple-element.68.second_ref, f32[64,128]{1,0:T(8,128)S(1)} %add.41.own_ref, f32[64,128]{1,0:T(8,128)S(1)} %collective-permute-done.25.other_ref, s32[1]{0:T(128)} %bitcast.3.rest_3_.upper_ref), custom_call_target="tpu_custom_call" | custom-call | flops 268435456 | bytes 4194304 | tf_op jit(solution)/shard_map/turn/pallas_call | solution.py:741
  (65 shorter events, 12.0 us)
Async XLA Ops:
  0.0 19.2 %collective-permute-start.5 = (f32[16,256,128]{2,1,0:T(8,128)}, f32[16,256,128]{2,1,0:T(8,128)}, u32[]{:S(2)}, u32[]{:S(2)}) collective-permute-start(f32[16,256,128]{2,1,0:T(8,128)} %bitcast.12), channel_id=1, source_target_pairs={{0,64},{1,65},{2,66},{3,67},{4,68},{5,69},{6,70},{7,71},{8,72},{9,... | collective-permute-start | bytes 6291464 | tf_op jit(solution)/shard_map/ppermute | solution.py:764
  0.1 1.6 %copy-start = (f32[16,16,16,128]{3,2,1,0:T(8,128)S(1)}, f32[16,16,16,128]{3,2,1,0:T(8,128)}, u32[]{:S(2)}) copy-start(f32[16,16,16,128]{3,2,1,0:T(8,128)} %param.5) | copy-start | bytes 6291460
  1.7 5.0 %copy-start.4 = (f32[4,9,9,9]{3,0,2,1:T(4,128)S(1)}, f32[4,9,9,9]{3,0,2,1:T(4,128)}, u32[]{:S(2)}) copy-start(f32[4,9,9,9]{3,0,2,1:T(4,128)} %param.8) | copy-start | bytes 34996
  1.7 6.8 %copy-start.5 = (s32[4,3]{1,0:T(4,128)S(1)}, s32[4,3]{1,0:T(4,128)}, u32[]{:S(2)}) copy-start(s32[4,3]{1,0:T(4,128)} %param.7) | copy-start | bytes 148
  1.7 6.8 %copy-start.6 = (f32[4]{0:T(128)S(1)}, f32[4]{0:T(128)}, u32[]{:S(2)}) copy-start(f32[4]{0:T(128)} %param.9) | copy-start | bytes 52
  1.7 17.2 %copy-start.1 = (f32[16,16,16,128]{3,2,1,0:T(8,128)S(1)}, f32[16,16,16,128]{3,2,1,0:T(8,128)}, u32[]{:S(2)}) copy-start(f32[16,16,16,128]{3,2,1,0:T(8,128)} %param.5) | copy-start | bytes 6291460
  4.6 18.0 %collective-permute-start.4 = (f32[6,192,128]{2,1,0:T(8,128)}, f32[6,192,128]{2,1,0:T(8,128)S(1)}, u32[]{:S(2)}, u32[]{:S(2)}) collective-permute-start(f32[6,192,128]{2,1,0:T(8,128)} %get-tuple-element.45), channel_id=1, source_target_pairs={{0,32},{1,33},{2,34},{3,35},{4,36},{5,37},{6,38},{7,39},{8,40},{9,... | collective-permute-start | bytes 1769480 | tf_op jit(solution)/shard_map/ppermute | solution.py:764
  8.8 10.0 %collective-permute-start = (f32[24,128]{1,0:T(8,128)S(1)}, f32[24,128]{1,0:T(8,128)S(1)}, u32[]{:S(2)}, u32[]{:S(2)}) collective-permute-start(f32[24,128]{1,0:T(8,128)S(1)} %reshape.37.refs_1_), channel_id=1, source_target_pairs={{0,1},{1,2},{2,3},{3,4},{4,5},{5,6},{6,7},{7,8},{8,9},{9,10},{10,1... | collective-permute-start | bytes 36872 | tf_op jit(solution)/shard_map/ppermute | solution.py:764
  10.3 8.4 %collective-permute-start.1 = (f32[24,128]{1,0:T(8,128)S(1)}, f32[24,128]{1,0:T(8,128)S(1)}, u32[]{:S(2)}, u32[]{:S(2)}) collective-permute-start(f32[24,128]{1,0:T(8,128)S(1)} %reshape.37.refs_1_), channel_id=1, source_target_pairs={{0,31},{1,0},{2,1},{3,2},{4,3},{5,4},{6,5},{7,6},{8,7},{9,8},{10,9... | collective-permute-start | bytes 36872 | tf_op jit(solution)/shard_map/ppermute | solution.py:764
  18.8 3.8 %collective-permute-start.3 = (f32[104,128]{1,0:T(8,128)S(1)}, f32[104,128]{1,0:T(8,128)S(1)}, u32[]{:S(2)}, u32[]{:S(2)}) collective-permute-start(f32[104,128]{1,0:T(8,128)S(1)} %stack.13.parcel_ref.refs_0_), channel_id=1, source_target_pairs={{0,96},{1,97},{2,98},{3,99},{4,100},{5,101},{6,102},{7,103},{8,104... | collective-permute-start | bytes 159752 | tf_op jit(solution)/shard_map/ppermute | solution.py:764
  19.2 7.5 %copy-start.3 = (f32[6,16,16,128]{3,2,1,0:T(8,128)S(1)}, f32[6,16,16,128]{3,2,1,0:T(8,128)}, u32[]{:S(2)}) copy-start(f32[6,16,16,128]{3,2,1,0:T(8,128)} %copy-done.2) | copy-start | bytes 2359300
  22.6 22.1 %collective-permute-start.7 = (f32[6,192,128]{2,1,0:T(8,128)S(1)}, f32[6,192,128]{2,1,0:T(8,128)S(1)}, u32[]{:S(2)}, u32[]{:S(2)}) collective-permute-start(f32[6,192,128]{2,1,0:T(8,128)S(1)} %get-tuple-element.51), channel_id=1, source_target_pairs={{0,33},{3,34},{4,37},{7,38},{8,41},{11,42},{12,45},{15,46},{16,49}... | collective-permute-start | bytes 1769480 | tf_op jit(solution)/shard_map/ppermute | solution.py:793
  26.2 42.1 %collective-permute-start.13 = (f32[1920,128]{1,0:T(8,128)S(1)}, f32[1920,128]{1,0:T(8,128)S(1)}, u32[]{:S(2)}, u32[]{:S(2)}) collective-permute-start(f32[1920,128]{1,0:T(8,128)S(1)} %get-tuple-element.58), channel_id=1, source_target_pairs={{0,32},{1,33},{2,34},{3,35},{4,36},{5,37},{6,38},{7,39},{8,40},{9,... | collective-permute-start | bytes 2949128 | tf_op jit(solution)/shard_map/ppermute | solution.py:764
  26.7 29.3 %collective-permute-start.11 = (f32[6,16,16,128]{3,2,1,0:T(8,128)S(1)}, f32[6,16,16,128]{3,2,1,0:T(8,128)S(1)}, u32[]{:S(2)}, u32[]{:S(2)}) collective-permute-start(f32[6,16,16,128]{3,2,1,0:T(8,128)S(1)} %copy-done.3), channel_id=1, source_target_pairs={{0,1},{1,2},{2,3},{3,4},{4,5},{5,6},{6,7},{7,8},{8,9},{9,10},{10,1... | collective-permute-start | bytes 2359304 | tf_op jit(solution)/shard_map/ppermute | solution.py:764
  26.7 29.3 %collective-permute-start.12 = (f32[6,16,16,128]{3,2,1,0:T(8,128)S(1)}, f32[6,16,16,128]{3,2,1,0:T(8,128)S(1)}, u32[]{:S(2)}, u32[]{:S(2)}) collective-permute-start(f32[6,16,16,128]{3,2,1,0:T(8,128)S(1)} %get-tuple-element.56), channel_id=1, source_target_pairs={{0,31},{1,0},{2,1},{3,2},{4,3},{5,4},{6,5},{7,6},{8,7},{9,8},{10,9... | collective-permute-start | bytes 2359304 | tf_op jit(solution)/shard_map/ppermute | solution.py:764
  34.4 1.2 collective-permute-start.2
  35.6 1.2 collective-permute-start.6
  44.7 23.6 %collective-permute-start.14 = (f32[6,192,128]{2,1,0:T(8,128)S(1)}, f32[6,192,128]{2,1,0:T(8,128)S(1)}, u32[]{:S(2)}, u32[]{:S(2)}) collective-permute-start(f32[6,192,128]{2,1,0:T(8,128)S(1)} %collective-permute-done.7), channel_id=1, source_target_pairs={{1,0},{2,3},{5,4},{6,7},{9,8},{10,11},{13,12},{14,15},{17,16},{18,... | collective-permute-start | bytes 1769480 | tf_op jit(solution)/shard_map/ppermute | solution.py:799
  46.0 1.3 collective-permute-start.8
  47.4 20.9 %collective-permute-start.9 = (f32[3,48,128]{2,1,0:T(8,128)S(1)}, f32[3,48,128]{2,1,0:T(8,128)S(1)}, u32[]{:S(2)}, u32[]{:S(2)}) collective-permute-start(f32[3,48,128]{2,1,0:T(8,128)S(1)} %add.34.refs_4_.rest_0_), channel_id=1, source_target_pairs={{0,32},{1,33},{2,34},{3,35},{4,36},{5,37},{6,38},{7,39},{8,40},{9,... | collective-permute-start | bytes 221192 | tf_op jit(solution)/shard_map/ppermute | solution.py:764
  70.4 9.4 %collective-permute-start.15 = (f32[16,256,128]{2,1,0:T(8,128)S(1)}, f32[16,256,128]{2,1,0:T(8,128)S(1)}, u32[]{:S(2)}, u32[]{:S(2)}) collective-permute-start(f32[16,256,128]{2,1,0:T(8,128)S(1)} %get-tuple-element.61.s_ref), channel_id=1, source_target_pairs={{0,64},{1,65},{2,66},{3,67},{4,68},{5,69},{6,70},{7,71},{8,72},{9,... | collective-permute-start | bytes 6291464 | tf_op jit(solution)/shard_map/ppermute | solution.py:764
  70.5 26.8 %collective-permute-start.16 = (f32[1632,128]{1,0:T(8,128)S(1)}, f32[1632,128]{1,0:T(8,128)S(1)}, u32[]{:S(2)}, u32[]{:S(2)}) collective-permute-start(f32[1632,128]{1,0:T(8,128)S(1)} %get-tuple-element.62), channel_id=1, source_target_pairs={{0,1},{1,2},{2,3},{3,4},{4,5},{5,6},{6,7},{7,8},{8,9},{9,10},{10,1... | collective-permute-start | bytes 2506760 | tf_op jit(solution)/shard_map/ppermute | solution.py:764
  70.6 26.7 %collective-permute-start.17 = (f32[1632,128]{1,0:T(8,128)S(1)}, f32[1632,128]{1,0:T(8,128)S(1)}, u32[]{:S(2)}, u32[]{:S(2)}) collective-permute-start(f32[1632,128]{1,0:T(8,128)S(1)} %get-tuple-element.63), channel_id=1, source_target_pairs={{0,31},{1,0},{2,1},{3,2},{4,3},{5,4},{6,5},{7,6},{8,7},{9,8},{10,9... | collective-permute-start | bytes 2506760 | tf_op jit(solution)/shard_map/ppermute | solution.py:764
  78.3 4.5 %collective-permute-start.10 = (f32[16,64,128]{2,1,0:T(8,128)S(1)}, f32[16,64,128]{2,1,0:T(8,128)S(1)}, u32[]{:S(2)}, u32[]{:S(2)}) collective-permute-start(f32[16,64,128]{2,1,0:T(8,128)S(1)} %get-tuple-element.53), channel_id=1, source_target_pairs={{1,33},{2,34},{5,37},{6,38},{9,41},{10,42},{13,45},{14,46},{17,49}... | collective-permute-start | bytes 1572872 | tf_op jit(solution)/shard_map/ppermute | solution.py:809
  101.0 1.3 collective-permute-start.18
  102.3 3.9 %collective-permute-start.19 = (f32[64,128]{1,0:T(8,128)S(1)}, f32[64,128]{1,0:T(8,128)S(1)}, u32[]{:S(2)}, u32[]{:S(2)}) collective-permute-start(f32[64,128]{1,0:T(8,128)S(1)} %add.35), channel_id=1, source_target_pairs={{0,32},{1,33},{2,34},{3,35},{4,36},{5,37},{6,38},{7,39},{8,40},{9,... | collective-permute-start | bytes 98312 | tf_op jit(solution)/shard_map/ppermute | solution.py:818
  106.3 5.1 %collective-permute-start.20 = (f32[64,128]{1,0:T(8,128)S(1)}, f32[64,128]{1,0:T(8,128)S(1)}, u32[]{:S(2)}, u32[]{:S(2)}) collective-permute-start(f32[64,128]{1,0:T(8,128)S(1)} %add.36), channel_id=1, source_target_pairs={{0,36},{1,37},{2,38},{3,39},{4,32},{5,33},{6,34},{7,35},{8,44},{9,... | collective-permute-start | bytes 98312 | tf_op jit(solution)/shard_map/ppermute | solution.py:818
  111.4 3.9 %collective-permute-start.21 = (f32[64,128]{1,0:T(8,128)S(1)}, f32[64,128]{1,0:T(8,128)S(1)}, u32[]{:S(2)}, u32[]{:S(2)}) collective-permute-start(f32[64,128]{1,0:T(8,128)S(1)} %add.37), channel_id=1, source_target_pairs={{0,1},{1,0},{2,3},{3,2},{4,5},{5,4},{6,7},{7,6},{8,9},{9,8},{10,11... | collective-permute-start | bytes 98312 | tf_op jit(solution)/shard_map/ppermute | solution.py:818
  115.3 5.7 %collective-permute-start.22 = (f32[64,128]{1,0:T(8,128)S(1)}, f32[64,128]{1,0:T(8,128)S(1)}, u32[]{:S(2)}, u32[]{:S(2)}) collective-permute-start(f32[64,128]{1,0:T(8,128)S(1)} %add.38), channel_id=1, source_target_pairs={{0,3},{1,2},{2,1},{3,0},{4,7},{5,6},{6,5},{7,4},{8,11},{9,10},{10,... | collective-permute-start | bytes 98312 | tf_op jit(solution)/shard_map/ppermute | solution.py:818
  121.0 3.9 %collective-permute-start.23 = (f32[64,128]{1,0:T(8,128)S(1)}, f32[64,128]{1,0:T(8,128)S(1)}, u32[]{:S(2)}, u32[]{:S(2)}) collective-permute-start(f32[64,128]{1,0:T(8,128)S(1)} %add.39), channel_id=1, source_target_pairs={{0,8},{1,9},{2,10},{3,11},{4,12},{5,13},{6,14},{7,15},{8,0},{9,1},... | collective-permute-start | bytes 98312 | tf_op jit(solution)/shard_map/ppermute | solution.py:818
  124.9 5.1 %collective-permute-start.24 = (f32[64,128]{1,0:T(8,128)S(1)}, f32[64,128]{1,0:T(8,128)S(1)}, u32[]{:S(2)}, u32[]{:S(2)}) collective-permute-start(f32[64,128]{1,0:T(8,128)S(1)} %add.40), channel_id=1, source_target_pairs={{0,24},{1,25},{2,26},{3,27},{4,28},{5,29},{6,30},{7,31},{8,16},{9,... | collective-permute-start | bytes 98312 | tf_op jit(solution)/shard_map/ppermute | solution.py:818
  130.0 1.2 collective-permute-start.25
  (1 other events, 0.9 us)

commit v17 on v16

--- a/solution.py
+++ b/solution.py
@@ -148,28 +148,43 @@
     out_ref[:, 96:192, :] = s_ref[:, 160:256, :]
 
 
-def pack_kernel(s_ref, edge_ref, head_ref, tail_ref):
+def by_side(odd_ref, body, one, two):
+    odd = odd_ref[0] == 1
+
+    @pl.when(odd)
+    def _():
+        body(one, two)
+
+    @pl.when(jnp.logical_not(odd))
+    def _():
+        body(two, one)
+
+
+def pack_kernel(s_ref, odd_ref, edge_ref, one_ref, two_ref):
     @pl.when(pl.program_id(0) < FIRST // N)
     def _():
         pack_edges(s_ref, edge_ref)
 
-    for p in range(N):
-        for z in range(H):
-            head_ref[z, p] = s_ref[p, stride_rows(z), :]
-            tail_ref[z, p] = s_ref[p, stride_rows(C - H + z), :]
-
-
-def pack(s):
+    def halos(head_ref, tail_ref):
+        for p in range(N):
+            for z in range(H):
+                head_ref[z, p] = s_ref[p, stride_rows(z), :]
+                tail_ref[z, p] = s_ref[p, stride_rows(C - H + z), :]
+
+    by_side(odd_ref, halos, one_ref, two_ref)
+
+
+def pack(s, odd):
     return pl.pallas_call(
         pack_kernel,
         grid=(C // N,),
-        in_specs=[plane_spec(ROWS, N)],
+        in_specs=[plane_spec(ROWS, N), SCALARS],
         out_specs=edge_specs()[:1] + [halo_spec(N), halo_spec(N)],
         out_shape=EDGES[:1] + [HALO, HALO],
         compiler_params=params(12),
         cost_estimate=cost(1 << 32, 6 << 20),
         name="pack",
-    )(s)
+    )(s, odd)
 
 
 def pack_rest_kernel(s_ref, inner_ref, message_ref, relay_ref, mid_ref):
@@ -210,16 +225,24 @@
     return message, relay, mid
 
 
-def stack_kernel(*refs):
-    start = 0
-    for ref in refs[:-1]:
-        refs[-1][start : start + ref.shape[0], :] = ref[...]
-        start += ref.shape[0]
-
-
-def stack(*arrays):
-    rows = sum(a.shape[0] for a in arrays)
-    return pl.pallas_call(stack_kernel, out_shape=sds((rows, S)), compiler_params=params(4), name="stack")(*arrays)
+def column_kernel(own_ref, one_ref, two_ref, pot_ref, odd_ref, out_ref):
+    def beside(below_ref, above_ref):
+        out_ref[0:24, :] = below_ref[...]
+        out_ref[48:72, :] = above_ref[...]
+
+    by_side(odd_ref, beside, one_ref, two_ref)
+    out_ref[24:48, :] = own_ref[...]
+    out_ref[72:104, :] = pot_ref[...]
+
+
+def column(own, one, two, pot, odd):
+    return pl.pallas_call(
+        column_kernel,
+        in_specs=[pl.BlockSpec(memory_space=pltpu.VMEM)] * 4 + [SCALARS],
+        out_shape=sds((104, S)),
+        compiler_params=params(4),
+        name="column",
+    )(own, one, two, pot, odd)
 
 
 def along_x(s_ref, mate_ref, out_ref, add):
@@ -256,30 +279,34 @@
     )(s, mate)
 
 
-def side_z_kernel(s_ref, part_ref, low_ref, high_ref, out_ref, ext_ref):
-    def plane(x, _):
-        for y in range(C):
-            ext_ref[y * 32 + 8 : y * 32 + 24, :] = s_ref[x, y * C : (y + 1) * C, :]
-        for z in range(H):
-            ext_ref[pl.ds(2 + z, C, stride=32), :] = low_ref[z, x]
-            ext_ref[pl.ds(24 + z, C, stride=32), :] = high_ref[z, x]
-        for y in range(C):
-            rows = slice(y * C, (y + 1) * C)
-            out_ref[x, rows, :] = part_ref[x, rows, :] + z_taps(ext_ref, y)
-        return 0
-
-    lax.fori_loop(0, C, plane, 0)
-
-
-def side_z(s, part, low, high):
+def side_z_kernel(s_ref, part_ref, one_ref, two_ref, odd_ref, out_ref, ext_ref):
+    def planes(low_ref, high_ref):
+        def plane(x, _):
+            for y in range(C):
+                ext_ref[y * 32 + 8 : y * 32 + 24, :] = s_ref[x, y * C : (y + 1) * C, :]
+            for z in range(H):
+                ext_ref[pl.ds(2 + z, C, stride=32), :] = low_ref[z, x]
+                ext_ref[pl.ds(24 + z, C, stride=32), :] = high_ref[z, x]
+            for y in range(C):
+                rows = slice(y * C, (y + 1) * C)
+                out_ref[x, rows, :] = part_ref[x, rows, :] + z_taps(ext_ref, y)
+            return 0
+
+        lax.fori_loop(0, C, plane, 0)
+
+    by_side(odd_ref, planes, one_ref, two_ref)
+
+
+def side_z(s, part, halos, odd):
     return pl.pallas_call(
         side_z_kernel,
+        in_specs=[pl.BlockSpec(memory_space=pltpu.VMEM)] * 4 + [SCALARS],
         out_shape=FULL,
         scratch_shapes=[pltpu.VMEM((C * 32, S), F32)],
         compiler_params=params(14),
         cost_estimate=cost(1 << 24, 8 << 20),
         name="side_z",
-    )(s, part, low, high)
+    )(s, part, *halos, odd)
 
 
 def side_again_kernel(s_ref, mate_ref, out_ref, ext_ref):
@@ -483,15 +510,18 @@
 
 
 def first_kernel(s_ref, side_ref, vb_ref, *refs):
-    inner_ref, part_ref, mate_ref, q_ref, mix_ref, head_ref, tail_ref = refs[3:]
+    inner_ref, odd_ref, part_ref, mate_ref, q_ref, mix_ref, one_ref, two_ref = refs[3:]
     step = pl.program_id(0)
 
     @pl.when(step == 0)
     def _():
-        for j in range(2):
-            rows = slice(HALO_ROWS + j * NEAR, HALO_ROWS + (j + 1) * NEAR)
-            head_ref[rows, :] = part_ref[j] + mate_ref[j]
-            tail_ref[rows, :] = part_ref[j + 1] + mate_ref[j + 1]
+        def shares(head_ref, tail_ref):
+            for j in range(2):
+                rows = slice(HALO_ROWS + j * NEAR, HALO_ROWS + (j + 1) * NEAR)
+                head_ref[rows, :] = part_ref[j] + mate_ref[j]
+                tail_ref[rows, :] = part_ref[j + 1] + mate_ref[j + 1]
+
+        by_side(odd_ref, shares, one_ref, two_ref)
 
     def planes(edge_ref):
         for p in range(N):
@@ -506,26 +536,31 @@
                     q = dy + vb_ref[p, rows, :] * ring[y]
                     q_ref[p, rows, :] = q
                     mix_ref[p, rows, :] = side_ref[p, rows, :] + q + dy
+
+    for_piece(refs[:3], inner_ref, planes)
+
+    def halos(head_ref, tail_ref):
+        for p in range(N):
             for z in range(H):
                 rows = halo_rows(step * N + p, z)
                 head_ref[rows, :] = mix_ref[p, stride_rows(z), :]
                 tail_ref[rows, :] = mix_ref[p, stride_rows(C - H + z), :]
 
-    for_piece(refs[:3], inner_ref, planes)
-
-
-def make_first(s, side_part, vb, edges, inner, part, part_mate):
+    by_side(odd_ref, halos, one_ref, two_ref)
+
+
+def make_first(s, side_part, vb, edges, inner, odd, part, part_mate):
     shares = pl.BlockSpec((3, NEAR, S), lambda i: (0, 0, 0))
     return pl.pallas_call(
         first_kernel,
         grid=(C // N,),
-        in_specs=[plane_spec(ROWS, N)] * 3 + edge_specs() + [SCALARS] + [shares] * 2,
+        in_specs=[plane_spec(ROWS, N)] * 3 + edge_specs() + [SCALARS] * 2 + [shares] * 2,
         out_specs=[plane_spec(ROWS, N), plane_spec(ROWS, N), whole(MESSAGE.shape[0]), whole(MESSAGE.shape[0])],
         out_shape=[FULL, FULL, MESSAGE, MESSAGE],
         compiler_params=params(16),
         cost_estimate=cost(1 << 24, 14 << 20),
         name="first",
-    )(s, side_part, vb, *edges, inner, part, part_mate)
+    )(s, side_part, vb, *edges, inner, odd, part, part_mate)
 
 
 def base_kernel(s_ref, mid_ref, vb_ref, vb_mate_ref, q_ref, side_ref, part_ref, *refs):
@@ -584,8 +619,8 @@
     )(s, mid, vb, vb_mate, q, side_part, part, *edges, inner, edges[1].reshape(-1, S))
 
 
-def second_kernel(base_ref, low_ref, high_ref, gg_high_ref, gg_low_ref, *rest):
-    part_ref, mate_ref, energy_ref, upper_ref, second_ref, keep_ref, give_ref, gram_ref, cross_ref, w_ref, halo_ref = rest
+def second_kernel(base_ref, one_ref, two_ref, gg_high_ref, gg_low_ref, *rest):
+    part_ref, mate_ref, energy_ref, upper_ref, odd_ref, second_ref, keep_ref, give_ref, gram_ref, cross_ref, w_ref, halo_ref = rest
     step = pl.program_id(0)
 
     @pl.when(step == 0)
@@ -595,8 +630,10 @@
         w_ref[...] = jnp.zeros((S, S), F32)
         halo_ref[...] = jnp.zeros((B, ROWS, S), F32)
         mine = [part_ref[j] + mate_ref[j] for j in range(3)]
-        below = [move_pair(low_ref[HALO_ROWS + j * NEAR : HALO_ROWS + (j + 1) * NEAR, :], -1) for j in range(2)]
-        above = [move_pair(high_ref[HALO_ROWS + j * NEAR : HALO_ROWS + (j + 1) * NEAR, :], 1) for j in range(2)]
+        odd = odd_ref[0] == 1
+        got = [[ref[HALO_ROWS + j * NEAR : HALO_ROWS + (j + 1) * NEAR, :] for j in range(2)] for ref in (one_ref, two_ref)]
+        below = [move_pair(jnp.where(odd, a, b), -1) for a, b in zip(*got)]
+        above = [move_pair(jnp.where(odd, b, a), 1) for a, b in zip(*got)]
         slabs = [mine[0] + below[0], mine[1] + below[1] + above[0], mine[2] + above[1]]
         near = jnp.concatenate([slab[0:16] for slab in slabs]) * energy_ref[...]
         lane = lax.broadcasted_iota(jnp.int32, (NEAR, S), 1)
@@ -606,14 +643,17 @@
         w_ref[0:NEAR, :] = 2.0 * energy_ref[...] * two
         w_ref[64 : 64 + NEAR, :] = 2.0 * near
 
-    for p in range(B):
-        low = [low_ref[halo_rows(step * B + p, j), :] for j in range(H)]
-        high = [high_ref[halo_rows(step * B + p, j), :] for j in range(H)]
-        for z in range(H):
-            add = sum((2.0 * OFF[k - 1]) * low[z - k + H] for k in range(z + 1, H + 1))
-            halo_ref[p, stride_rows(z), :] = add
-            add = sum((2.0 * OFF[H + j - z - 1]) * high[j] for j in range(z + 1))
-            halo_ref[p, stride_rows(C - H + z), :] = add
+    def halo_part(low_ref, high_ref):
+        for p in range(B):
+            low = [low_ref[halo_rows(step * B + p, j), :] for j in range(H)]
+            high = [high_ref[halo_rows(step * B + p, j), :] for j in range(H)]
+            for z in range(H):
+                add = sum((2.0 * OFF[k - 1]) * low[z - k + H] for k in range(z + 1, H + 1))
+                halo_ref[p, stride_rows(z), :] = add
+                add = sum((2.0 * OFF[H + j - z - 1]) * high[j] for j in range(z + 1))
+                halo_ref[p, stride_rows(C - H + z), :] = add
+
+    by_side(odd_ref, halo_part, one_ref, two_ref)
 
     w_high, w_low = split(w_ref[...])
     w_twice = jnp.concatenate([w_high, w_high])
@@ -637,21 +677,21 @@
         give_ref[...] = jnp.where(upper, gram[: S // 2], gram[S // 2 :])
 
 
-def make_second(base, halos, gg, shares, upper):
+def make_second(base, halos, gg, shares, upper, odd):
     three = pl.BlockSpec((3, NEAR, S), lambda i: (0, 0, 0))
     return pl.pallas_call(
         second_kernel,
         grid=(STEPS,),
         in_specs=[plane_spec()]
         + [whole(MESSAGE.shape[0])] * 2
-        + [part_spec(0), part_spec(1), three, three, whole(NEAR), SCALARS],
+        + [part_spec(0), part_spec(1), three, three, whole(NEAR), SCALARS, SCALARS],
         out_specs=[plane_spec(), whole(S // 2), whole(S // 2)],
         out_shape=[FULL, sds((S // 2, S)), sds((S // 2, S))],
         scratch_shapes=[pltpu.VMEM((S, S), F32)] * 3 + [pltpu.VMEM((B, ROWS, S), F32)],
         compiler_params=params(16),
         cost_estimate=cost(1 << 27, 8 << 20),
         name="second",
-    )(base, *halos, gg, gg, *shares, upper)
+    )(base, *halos, gg, gg, *shares, upper, odd)
 
 
 def exact(a, b):
@@ -757,13 +797,16 @@
     count = 4 * depth
     barrier = lax.optimization_barrier
 
-    def send(value, flip=0, move=0):
-        def target(d):
-            return (d // depth * depth ^ flip) + (d + move) % depth
-
-        return lax.ppermute(value, AXES, [(d, target(d)) for d in range(count)])
+    def send(value, flip):
+        return lax.ppermute(value, AXES, [(d, d ^ flip) for d in range(count)])
 
     over_x, over_y = 2 * depth, depth
+
+    def to_pairs(one, two):
+        near = [(d, d ^ 1) for d in range(count)]
+        far = [(d, d // depth * depth + (d + (1 if d % 2 else -1)) % depth) for d in range(count)]
+        return lax.ppermute(one, AXES, near), lax.ppermute(two, AXES, far)
+
     inner_ones = [d for d in range(count) if d % 4 in (1, 2)]
     outer_ones = [d for d in range(count) if d % 4 in (0, 3)]
     inner = ((lax.axis_index("gzs") + 1) // 2 % 2).astype(jnp.int32).reshape(1)
@@ -777,15 +820,16 @@
     mate = send(s, over_x)
     corner = jnp.stack([gx * C, gy * C]).astype(jnp.int32)
     upper = gx.astype(jnp.int32).reshape(1)
-    to_pack, corner, upper, inner = barrier((s, corner, upper, inner))
-    below, above = send(atoms, 0, 1), send(atoms, 0, -1)
-    one_edge, head, tail = pack(to_pack)
+    odd = (lax.axis_index("gzs") % 2).astype(jnp.int32).reshape(1)
+    to_pack, corner, upper, inner, odd = barrier((s, corner, upper, inner, odd))
+    beside_one, beside_two = to_pairs(atoms, atoms)
+    one_edge, halo_one, halo_two = pack(to_pack, odd)
     one_edge = send(one_edge, over_y)
-    head, tail, below, above = barrier((head, tail, below, above))
-    parcel = stack(below, atoms, above, pot)
+    halo_one, halo_two, beside_one, beside_two = barrier((halo_one, halo_two, beside_one, beside_two))
+    parcel = column(atoms, beside_one, beside_two, pot, odd)
     parcel_xy = send(parcel, over_x ^ over_y)
     parcel_x = send(parcel, over_x)
-    low, high = send(tail, 0, 1), send(head, 0, -1)
+    halos = to_pairs(halo_one, halo_two)
     message, relay, mid = pack_rest(s, inner)
     vb = spread(parcel)
     beside = side_x(s, mate)
@@ -799,11 +843,11 @@
     relayed = lax.ppermute(relayed, AXES, [(d, d ^ 1) for d in inner_ones])
     part = part + send(part, over_x)
     part_mate = send(part, over_y)
-    side_part = side_z(s, beside, low, high)
+    side_part = side_z(s, beside, halos, odd)
     edges = [one_edge, message.reshape(C - FIRST, EDGE, S), relayed]
     vb = vb.reshape(C, ROWS, S)
-    q, mix, head, tail = make_first(s, side_part, vb, edges, inner, part, part_mate)
-    low, high = send(tail, 0, 1), send(head, 0, -1)
+    q, mix, halo_one, halo_two = make_first(s, side_part, vb, edges, inner, odd, part, part_mate)
+    halos = to_pairs(halo_one, halo_two)
     mate = send(mix, over_x)
     mid, part_mate = barrier((mid, part_mate))
     mid = lax.ppermute(mid, AXES, [(d, d ^ over_y) for d in inner_ones])
@@ -811,7 +855,7 @@
     part_two = side_again(mix, mate)
     base = make_base(s, mid, vb, vb_mate, q, side_part, part_two, edges, inner)
     gg = gg.reshape(2, C, ROWS, S)
-    second, own, give = make_second(base, [low, high], gg, [part, part_mate, energy], upper)
+    second, own, give = make_second(base, halos, gg, [part, part_mate, energy], upper, odd)
 
     own = own + send(give, over_x)
     for flip in (32, 36, 1, 3, 8, 24):

time: 150 us -> 150 us (level)
  starting transfers between devices: 43.2 us -> 36.3 us
  waiting for transfers between devices: 52.4 us -> 58.8 us
    ppermute x6, starting transfers between devices: 8.89 us -> 2.95 us  [per_device(): own = own + lax.ppermute(own, AXES, [(d, d ^ flip) for d in range(count)])]
    ppermute x6, waiting for transfers between devices: 18.8 us -> 24.2 us  [per_device(): own = own + lax.ppermute(own, AXES, [(d, d ^ flip) for d in range(count)])]
  transfers between devices with their start and end apart: 26 -> 26, of which waited for: 16 -> 17; matrix products, arithmetic and copies ran while one was open for 2% -> 2% of each run, Pallas kernels for 16% -> 16%
where the time goes in v17:
time: 150 us; the launch traced here: 149 us
  waiting for transfers between devices  58.8 us (39%)
  Pallas kernels  47.5 us (32%)
  starting transfers between devices  36.3 us (24%)
  local copies, waits for them, and re-layouts  5.54 us (4%)
    ppermute x6, starting transfers between devices, to_pairs(): return (lax.ppermute(one, AXES, near), lax.ppermute(two, AXES, far))  24.5 us
    ppermute x6, waiting for transfers between devices, per_device(): own = own + lax.ppermute(own, AXES, [(d, d ^ flip) for d in range(count)])  24.2 us
    ppermute x6, waiting for transfers between devices, to_pairs(): return (lax.ppermute(one, AXES, near), lax.ppermute(two, AXES, far))  20.3 us
    pallas_call x1, Pallas kernels, turn(): pl.pallas_call(turn_kernel, grid=(STEPS,), in_specs=[plane_spec(), whole(...  17 us
    ppermute x11, waiting for transfers between devices, send(): return lax.ppermute(value, AXES, [(d, d ^ flip) for d in range(count)])  14.3 us
    pallas_call x1, Pallas kernels, prep(): pl.pallas_call(prep_kernel, in_specs=[vmem] * 4 + [pl.BlockSpec(memory_sp...  7.81 us
    pallas_call x1, Pallas kernels, make_second(): pl.pallas_call(second_kernel, grid=(STEPS,), in_specs=[plane_spec()] + [w...  4.34 us
    ppermute x11, starting transfers between devices, send(): return lax.ppermute(value, AXES, [(d, d ^ flip) for d in range(count)])  4.14 us
  transfers between devices with their start and end apart: 26, of which 17 were waited for; matrix products, arithmetic and copies ran while one was open for 2% of the time, Pallas kernels for 16%

profile of v17, /device:TPU:0, one launch (start us, length us, event | category | flops | bytes accessed | tf_op | source)
XLA Modules:
  0.0 148.6 jit_solution(17604752735235895761)
XLA Ops:
  0.1 1.6 %copy-done = f32[16,16,16,128]{3,2,1,0:T(8,128)S(1)} copy-done((f32[16,16,16,128]{3,2,1,0:T(8,128)S(1)}, f32[16,16,16,128]{3,2,1,0:T(8,128)}, u32[]{:S(2)}) %copy-start) | copy-done | bytes 2097176
  1.7 2.1 %pack.1 = (f32[6,192,128]{2,1,0:T(8,128)}, f32[6,16,16,128]{3,2,1,0:T(8,128)S(1)}, f32[6,16,16,128]{3,2,1,0:T(8,128)S(1)}) custom-call(f32[16,256,128]{2,1,0:T(8,128)S(1)} %bitcast.14, s32[1]{0:T(128)} %bitcast.5.odd_ref.refs_4_.rest_4_), custom_call_target="tpu_custom_call" | custom-call | flops 4294967296 | bytes 6291456 | tf_op jit(solution)/shard_map/pack/pallas_call | solution.py:178
  4.7 2.0 %collective-permute-start.4 = (f32[6,192,128]{2,1,0:T(8,128)}, f32[6,192,128]{2,1,0:T(8,128)S(1)}, u32[]{:S(2)}, u32[]{:S(2)}) collective-permute-start(f32[6,192,128]{2,1,0:T(8,128)} %get-tuple-element.47), channel_id=1, source_target_pairs={{0,32},{1,33},{2,34},{3,35},{4,36},{5,37},{6,38},{7,39},{8,40},{9,... | collective-permute-start | bytes 1769480 | tf_op jit(solution)/shard_map/ppermute | solution.py:801
  7.5 1.1 reshape.40
  8.9 1.6 %collective-permute-start = (f32[24,128]{1,0:T(8,128)S(1)}, f32[24,128]{1,0:T(8,128)S(1)}, u32[]{:S(2)}, u32[]{:S(2)}) collective-permute-start(f32[24,128]{1,0:T(8,128)S(1)} %reshape.41.own_ref), channel_id=1, source_target_pairs={{0,1},{1,0},{2,3},{3,2},{4,5},{5,4},{6,7},{7,6},{8,9},{9,8},{10,11... | collective-permute-start | bytes 36872 | tf_op jit(solution)/shard_map/ppermute | solution.py:808
  10.4 7.6 %collective-permute-start.1 = (f32[24,128]{1,0:T(8,128)S(1)}, f32[24,128]{1,0:T(8,128)S(1)}, u32[]{:S(2)}, u32[]{:S(2)}) collective-permute-start(f32[24,128]{1,0:T(8,128)S(1)} %reshape.41.own_ref), channel_id=1, source_target_pairs={{0,31},{1,2},{2,1},{3,4},{4,3},{5,6},{6,5},{7,8},{8,7},{9,10},{10,... | collective-permute-start | bytes 36872 | tf_op jit(solution)/shard_map/ppermute | solution.py:808
  20.3 3.1 %side_x.1.part_ref = f32[16,256,128]{2,1,0:T(8,128)S(1)} custom-call(f32[16,256,128]{2,1,0:T(8,128)S(1)} %bitcast.16, f32[16,256,128]{2,1,0:T(8,128)} %collective-permute-done.5.mate_ref), custom_call_target="tpu_custom_call" | custom-call | flops 16777216 | bytes 6291456 | tf_op jit(solution)/shard_map/side_x/pallas_call | solution.py:273
  23.5 2.7 %collective-permute-start.7 = (f32[6,192,128]{2,1,0:T(8,128)S(1)}, f32[6,192,128]{2,1,0:T(8,128)S(1)}, u32[]{:S(2)}, u32[]{:S(2)}) collective-permute-start(f32[6,192,128]{2,1,0:T(8,128)S(1)} %get-tuple-element.53), channel_id=1, source_target_pairs={{0,33},{3,34},{4,37},{7,38},{8,41},{11,42},{12,45},{15,46},{16,49}... | collective-permute-start | bytes 1769480 | tf_op jit(solution)/shard_map/ppermute | solution.py:837
  26.7 7.6 %collective-permute-start.12 = (f32[6,16,16,128]{3,2,1,0:T(8,128)S(1)}, f32[6,16,16,128]{3,2,1,0:T(8,128)S(1)}, u32[]{:S(2)}, u32[]{:S(2)}) collective-permute-start(f32[6,16,16,128]{3,2,1,0:T(8,128)S(1)} %get-tuple-element.58), channel_id=1, source_target_pairs={{0,31},{1,2},{2,1},{3,4},{4,3},{5,6},{6,5},{7,8},{8,7},{9,10},{10,... | collective-permute-start | bytes 2359304 | tf_op jit(solution)/shard_map/ppermute | solution.py:808
  34.3 1.2 collective-permute-done.2.refs_1_
  36.8 7.8 %prep.1 = (bf16[2,4096,128]{2,1,0:T(8,128)(2,1)S(1)}, f32[3,48,128]{2,1,0:T(8,128)S(1)}, f32[48,128]{1,0:T(8,128)S(1)}) custom-call(f32[104,128]{1,0:T(8,128)S(1)} %column.1.parcel_ref.refs_0_, f32[104,128]{1,0:T(8,128)S(1)} %collective-permute-done.2.refs_1_, f32[104,128]{1,0:T(8,128)S(1)} %collective-permute-done.6.refs_2_.parcel_ref, ...), custom_call_target="tpu_custom_call" | custom-call | flops 134217728 | bytes 10485760 | tf_op jit(solution)/shard_map/prep/pallas_call | solution.py:487
  44.6 1.3 collective-permute-start.14
  48.4 7.7 %collective-permute-done.11.one_ref = f32[6,16,16,128]{3,2,1,0:T(8,128)S(1)} collective-permute-done((f32[6,16,16,128]{3,2,1,0:T(8,128)S(1)}, f32[6,16,16,128]{3,2,1,0:T(8,128)S(1)}, u32[]{:S(2)}, u32[]{:S(2)}) %collective-permute-start.11) | collective-permute-done | bytes 786464 | tf_op jit(solution)/shard_map/ppermute | solution.py:808
  56.1 3.0 %side_z.1.side_ref = f32[16,256,128]{2,1,0:T(8,128)S(1)} custom-call(f32[16,256,128]{2,1,0:T(8,128)S(1)} %bitcast.18, f32[16,256,128]{2,1,0:T(8,128)S(1)} %side_x.1.part_ref, f32[6,16,16,128]{3,2,1,0:T(8,128)S(1)} %collective-permute-done.11.one_ref, f32[6,16,16,128]{3,2,1,0:T(8,128)S(1)} %collective-permute-done.12.two_ref, s32[1]{0:T(128)} %bitcast.5.odd_ref.refs_4_.rest_4_), custom_call_target="tpu_custom_call" | custom-call | flops 16777216 | bytes 8388608 | tf_op jit(solution)/shard_map/side_z/pallas_call | solution.py:301
  59.1 9.3 %collective-permute-done.9.refs_6_.rest_1_ = f32[3,48,128]{2,1,0:T(8,128)S(1)} collective-permute-done((f32[3,48,128]{2,1,0:T(8,128)S(1)}, f32[3,48,128]{2,1,0:T(8,128)S(1)}, u32[]{:S(2)}, u32[]{:S(2)}) %collective-permute-start.9) | collective-permute-done | bytes 73760 | tf_op jit(solution)/shard_map/ppermute | solution.py:801
  68.4 2.3 %first.1 = (f32[16,256,128]{2,1,0:T(8,128)S(1)}, f32[16,256,128]{2,1,0:T(8,128)S(1)}, f32[1632,128]{1,0:T(8,128)S(1)}, f32[1632,128]{1,0:T(8,128)S(1)}) custom-call(f32[16,256,128]{2,1,0:T(8,128)S(1)} %bitcast.19, f32[16,256,128]{2,1,0:T(8,128)S(1)} %side_z.1.side_ref, f32[16,256,128]{2,1,0:T(8,128)S(1)} %bitcast.21, ...), custom_call_target="tpu_custom_call" | custom-call | flops 16777216 | bytes 14680064 | tf_op jit(solution)/shard_map/first/pallas_call | solution.py:554
  70.9 7.6 %collective-permute-start.17 = (f32[1632,128]{1,0:T(8,128)S(1)}, f32[1632,128]{1,0:T(8,128)S(1)}, u32[]{:S(2)}, u32[]{:S(2)}) collective-permute-start(f32[1632,128]{1,0:T(8,128)S(1)} %get-tuple-element.65), channel_id=1, source_target_pairs={{0,31},{1,2},{2,1},{3,4},{4,3},{5,6},{6,5},{7,8},{8,7},{9,10},{10,... | collective-permute-start | bytes 2506760 | tf_op jit(solution)/shard_map/ppermute | solution.py:808
  80.0 2.9 %side_again.1.part_ref = f32[16,256,128]{2,1,0:T(8,128)S(1)} custom-call(f32[16,256,128]{2,1,0:T(8,128)S(1)} %get-tuple-element.63.s_ref, f32[16,256,128]{2,1,0:T(8,128)S(1)} %collective-permute-done.15.mate_ref), custom_call_target="tpu_custom_call" | custom-call | flops 33554432 | bytes 6291456 | tf_op jit(solution)/shard_map/side_again/pallas_call | solution.py:329
  83.0 3.0 %base.1.base_ref = f32[16,256,128]{2,1,0:T(8,128)S(1)} custom-call(f32[16,256,128]{2,1,0:T(8,128)S(1)} %bitcast.20, f32[16,64,128]{2,1,0:T(8,128)S(1)} %collective-permute-done.10.mid_ref, f32[16,256,128]{2,1,0:T(8,128)S(1)} %bitcast.22, f32[16,256,128]{2,1,0:T(8,128)S(1)} %bitcast.27, f32[16,256,128]{2,1,0:T(8,128)S(1)} %get-tuple-element.62.q_ref, ...), custom_call_target="tpu_custom_call" | custom-call | flops 33554432 | bytes 16777216 | tf_op jit(solution)/shard_map/base/pallas_call | solution.py:606
  85.9 5.8 %collective-permute-done.16.one_ref = f32[1632,128]{1,0:T(8,128)S(1)} collective-permute-done((f32[1632,128]{1,0:T(8,128)S(1)}, f32[1632,128]{1,0:T(8,128)S(1)}, u32[]{:S(2)}, u32[]{:S(2)}) %collective-permute-start.16) | collective-permute-done | bytes 835616 | tf_op jit(solution)/shard_map/ppermute | solution.py:808
  91.8 5.8 %collective-permute-done.17.two_ref = f32[1632,128]{1,0:T(8,128)S(1)} collective-permute-done((f32[1632,128]{1,0:T(8,128)S(1)}, f32[1632,128]{1,0:T(8,128)S(1)}, u32[]{:S(2)}, u32[]{:S(2)}) %collective-permute-start.17) | collective-permute-done | bytes 835616 | tf_op jit(solution)/shard_map/ppermute | solution.py:808
  97.6 4.3 %second.1 = (f32[16,256,128]{2,1,0:T(8,128)S(1)}, f32[64,128]{1,0:T(8,128)S(1)}, f32[64,128]{1,0:T(8,128)S(1)}) custom-call(f32[16,256,128]{2,1,0:T(8,128)S(1)} %base.1.base_ref, f32[1632,128]{1,0:T(8,128)S(1)} %collective-permute-done.16.one_ref, f32[1632,128]{1,0:T(8,128)S(1)} %collective-permute-done.17.two_ref, bf16[2,16,256,128]{3,2,1,0:T(8,128)(2,1)S(1)} %bitcast.25, ...), custom_call_target="tpu_custom_call" | custom-call | flops 134217728 | bytes 8388608 | tf_op jit(solution)/shard_map/second/pallas_call | solution.py:682
  102.0 1.2 collective-permute-done.18
  103.8 3.3 %collective-permute-done.19 = f32[64,128]{1,0:T(8,128)S(1)} collective-permute-done((f32[64,128]{1,0:T(8,128)S(1)}, f32[64,128]{1,0:T(8,128)S(1)}, u32[]{:S(2)}, u32[]{:S(2)}) %collective-permute-start.19) | collective-permute-done | bytes 32800 | tf_op jit(solution)/shard_map/ppermute | solution.py:862
  107.5 4.8 %collective-permute-done.20 = f32[64,128]{1,0:T(8,128)S(1)} collective-permute-done((f32[64,128]{1,0:T(8,128)S(1)}, f32[64,128]{1,0:T(8,128)S(1)}, u32[]{:S(2)}, u32[]{:S(2)}) %collective-permute-start.20) | collective-permute-done | bytes 32800 | tf_op jit(solution)/shard_map/ppermute | solution.py:862
  112.3 3.9 %collective-permute-done.21 = f32[64,128]{1,0:T(8,128)S(1)} collective-permute-done((f32[64,128]{1,0:T(8,128)S(1)}, f32[64,128]{1,0:T(8,128)S(1)}, u32[]{:S(2)}, u32[]{:S(2)}) %collective-permute-start.21) | collective-permute-done | bytes 32800 | tf_op jit(solution)/shard_map/ppermute | solution.py:862
  116.3 5.1 %collective-permute-done.22 = f32[64,128]{1,0:T(8,128)S(1)} collective-permute-done((f32[64,128]{1,0:T(8,128)S(1)}, f32[64,128]{1,0:T(8,128)S(1)}, u32[]{:S(2)}, u32[]{:S(2)}) %collective-permute-start.22) | collective-permute-done | bytes 32800 | tf_op jit(solution)/shard_map/ppermute | solution.py:862
  121.6 3.7 %collective-permute-done.23 = f32[64,128]{1,0:T(8,128)S(1)} collective-permute-done((f32[64,128]{1,0:T(8,128)S(1)}, f32[64,128]{1,0:T(8,128)S(1)}, u32[]{:S(2)}, u32[]{:S(2)}) %collective-permute-start.23) | collective-permute-done | bytes 32800 | tf_op jit(solution)/shard_map/ppermute | solution.py:862
  125.3 1.7 %collective-permute-start.24 = (f32[64,128]{1,0:T(8,128)S(1)}, f32[64,128]{1,0:T(8,128)S(1)}, u32[]{:S(2)}, u32[]{:S(2)}) collective-permute-start(f32[64,128]{1,0:T(8,128)S(1)} %add.44), channel_id=1, source_target_pairs={{0,24},{1,25},{2,26},{3,27},{4,28},{5,29},{6,30},{7,31},{8,16},{9,... | collective-permute-start | bytes 98312 | tf_op jit(solution)/shard_map/ppermute | solution.py:862
  127.0 3.4 %collective-permute-done.24 = f32[64,128]{1,0:T(8,128)S(1)} collective-permute-done((f32[64,128]{1,0:T(8,128)S(1)}, f32[64,128]{1,0:T(8,128)S(1)}, u32[]{:S(2)}, u32[]{:S(2)}) %collective-permute-start.24) | collective-permute-done | bytes 32800 | tf_op jit(solution)/shard_map/ppermute | solution.py:862
  130.4 1.2 collective-permute-done.25.other_ref
  131.6 17.0 %turn.1 = f32[16,256,128]{2,1,0:T(8,128)} custom-call(f32[16,256,128]{2,1,0:T(8,128)S(1)} %get-tuple-element.70.second_ref, f32[64,128]{1,0:T(8,128)S(1)} %add.45.own_ref, f32[64,128]{1,0:T(8,128)S(1)} %collective-permute-done.25.other_ref, s32[1]{0:T(128)} %bitcast.3.rest_3_.upper_ref), custom_call_target="tpu_custom_call" | custom-call | flops 268435456 | bytes 4194304 | tf_op jit(solution)/shard_map/turn/pallas_call | solution.py:781
  (65 shorter events, 11.5 us)
Async XLA Ops:
  0.0 20.3 %collective-permute-start.5 = (f32[16,256,128]{2,1,0:T(8,128)}, f32[16,256,128]{2,1,0:T(8,128)}, u32[]{:S(2)}, u32[]{:S(2)}) collective-permute-start(f32[16,256,128]{2,1,0:T(8,128)} %bitcast.13), channel_id=1, source_target_pairs={{0,64},{1,65},{2,66},{3,67},{4,68},{5,69},{6,70},{7,71},{8,72},{9,... | collective-permute-start | bytes 6291464 | tf_op jit(solution)/shard_map/ppermute | solution.py:801
  0.1 1.6 %copy-start = (f32[16,16,16,128]{3,2,1,0:T(8,128)S(1)}, f32[16,16,16,128]{3,2,1,0:T(8,128)}, u32[]{:S(2)}) copy-start(f32[16,16,16,128]{3,2,1,0:T(8,128)} %param.5) | copy-start | bytes 6291460
  1.7 5.0 %copy-start.4 = (f32[4,9,9,9]{3,0,2,1:T(4,128)S(1)}, f32[4,9,9,9]{3,0,2,1:T(4,128)}, u32[]{:S(2)}) copy-start(f32[4,9,9,9]{3,0,2,1:T(4,128)} %param.8) | copy-start | bytes 34996
  1.7 6.9 %copy-start.5 = (s32[4,3]{1,0:T(4,128)S(1)}, s32[4,3]{1,0:T(4,128)}, u32[]{:S(2)}) copy-start(s32[4,3]{1,0:T(4,128)} %param.7) | copy-start | bytes 148
  1.7 6.9 %copy-start.6 = (f32[4]{0:T(128)S(1)}, f32[4]{0:T(128)}, u32[]{:S(2)}) copy-start(f32[4]{0:T(128)} %param.9) | copy-start | bytes 52
  1.7 18.3 %copy-start.1 = (f32[16,16,16,128]{3,2,1,0:T(8,128)S(1)}, f32[16,16,16,128]{3,2,1,0:T(8,128)}, u32[]{:S(2)}) copy-start(f32[16,16,16,128]{3,2,1,0:T(8,128)} %param.5) | copy-start | bytes 6291460
  4.7 18.8 %collective-permute-start.4 = (f32[6,192,128]{2,1,0:T(8,128)}, f32[6,192,128]{2,1,0:T(8,128)S(1)}, u32[]{:S(2)}, u32[]{:S(2)}) collective-permute-start(f32[6,192,128]{2,1,0:T(8,128)} %get-tuple-element.47), channel_id=1, source_target_pairs={{0,32},{1,33},{2,34},{3,35},{4,36},{5,37},{6,38},{7,39},{8,40},{9,... | collective-permute-start | bytes 1769480 | tf_op jit(solution)/shard_map/ppermute | solution.py:801
  8.9 10.1 %collective-permute-start = (f32[24,128]{1,0:T(8,128)S(1)}, f32[24,128]{1,0:T(8,128)S(1)}, u32[]{:S(2)}, u32[]{:S(2)}) collective-permute-start(f32[24,128]{1,0:T(8,128)S(1)} %reshape.41.own_ref), channel_id=1, source_target_pairs={{0,1},{1,0},{2,3},{3,2},{4,5},{5,4},{6,7},{7,6},{8,9},{9,8},{10,11... | collective-permute-start | bytes 36872 | tf_op jit(solution)/shard_map/ppermute | solution.py:808
  10.4 9.5 %collective-permute-start.1 = (f32[24,128]{1,0:T(8,128)S(1)}, f32[24,128]{1,0:T(8,128)S(1)}, u32[]{:S(2)}, u32[]{:S(2)}) collective-permute-start(f32[24,128]{1,0:T(8,128)S(1)} %reshape.41.own_ref), channel_id=1, source_target_pairs={{0,31},{1,2},{2,1},{3,4},{4,3},{5,6},{6,5},{7,8},{8,7},{9,10},{10,... | collective-permute-start | bytes 36872 | tf_op jit(solution)/shard_map/ppermute | solution.py:808
  20.0 3.6 %collective-permute-start.3 = (f32[104,128]{1,0:T(8,128)S(1)}, f32[104,128]{1,0:T(8,128)S(1)}, u32[]{:S(2)}, u32[]{:S(2)}) collective-permute-start(f32[104,128]{1,0:T(8,128)S(1)} %column.1.parcel_ref.refs_0_), channel_id=1, source_target_pairs={{0,96},{1,97},{2,98},{3,99},{4,100},{5,101},{6,102},{7,103},{8,104... | collective-permute-start | bytes 159752 | tf_op jit(solution)/shard_map/ppermute | solution.py:801
  20.3 6.4 %copy-start.3 = (f32[6,16,16,128]{3,2,1,0:T(8,128)S(1)}, f32[6,16,16,128]{3,2,1,0:T(8,128)}, u32[]{:S(2)}) copy-start(f32[6,16,16,128]{3,2,1,0:T(8,128)} %copy-done.2) | copy-start | bytes 2359300
  23.5 21.1 %collective-permute-start.7 = (f32[6,192,128]{2,1,0:T(8,128)S(1)}, f32[6,192,128]{2,1,0:T(8,128)S(1)}, u32[]{:S(2)}, u32[]{:S(2)}) collective-permute-start(f32[6,192,128]{2,1,0:T(8,128)S(1)} %get-tuple-element.53), channel_id=1, source_target_pairs={{0,33},{3,34},{4,37},{7,38},{8,41},{11,42},{12,45},{15,46},{16,49}... | collective-permute-start | bytes 1769480 | tf_op jit(solution)/shard_map/ppermute | solution.py:837
  26.3 42.1 %collective-permute-start.13 = (f32[1920,128]{1,0:T(8,128)S(1)}, f32[1920,128]{1,0:T(8,128)S(1)}, u32[]{:S(2)}, u32[]{:S(2)}) collective-permute-start(f32[1920,128]{1,0:T(8,128)S(1)} %get-tuple-element.60), channel_id=1, source_target_pairs={{0,32},{1,33},{2,34},{3,35},{4,36},{5,37},{6,38},{7,39},{8,40},{9,... | collective-permute-start | bytes 2949128 | tf_op jit(solution)/shard_map/ppermute | solution.py:801
  26.7 29.3 %collective-permute-start.11 = (f32[6,16,16,128]{3,2,1,0:T(8,128)S(1)}, f32[6,16,16,128]{3,2,1,0:T(8,128)S(1)}, u32[]{:S(2)}, u32[]{:S(2)}) collective-permute-start(f32[6,16,16,128]{3,2,1,0:T(8,128)S(1)} %copy-done.3), channel_id=1, source_target_pairs={{0,1},{1,0},{2,3},{3,2},{4,5},{5,4},{6,7},{7,6},{8,9},{9,8},{10,11... | collective-permute-start | bytes 2359304 | tf_op jit(solution)/shard_map/ppermute | solution.py:808
  26.7 29.3 %collective-permute-start.12 = (f32[6,16,16,128]{3,2,1,0:T(8,128)S(1)}, f32[6,16,16,128]{3,2,1,0:T(8,128)S(1)}, u32[]{:S(2)}, u32[]{:S(2)}) collective-permute-start(f32[6,16,16,128]{3,2,1,0:T(8,128)S(1)} %get-tuple-element.58), channel_id=1, source_target_pairs={{0,31},{1,2},{2,1},{3,4},{4,3},{5,6},{6,5},{7,8},{8,7},{9,10},{10,... | collective-permute-start | bytes 2359304 | tf_op jit(solution)/shard_map/ppermute | solution.py:808
  34.3 1.2 collective-permute-start.2
  35.6 1.2 collective-permute-start.6
  44.6 23.8 %collective-permute-start.14 = (f32[6,192,128]{2,1,0:T(8,128)S(1)}, f32[6,192,128]{2,1,0:T(8,128)S(1)}, u32[]{:S(2)}, u32[]{:S(2)}) collective-permute-start(f32[6,192,128]{2,1,0:T(8,128)S(1)} %collective-permute-done.7), channel_id=1, source_target_pairs={{1,0},{2,3},{5,4},{6,7},{9,8},{10,11},{13,12},{14,15},{17,16},{18,... | collective-permute-start | bytes 1769480 | tf_op jit(solution)/shard_map/ppermute | solution.py:843
  45.9 1.3 collective-permute-start.8
  47.3 21.1 %collective-permute-start.9 = (f32[3,48,128]{2,1,0:T(8,128)S(1)}, f32[3,48,128]{2,1,0:T(8,128)S(1)}, u32[]{:S(2)}, u32[]{:S(2)}) collective-permute-start(f32[3,48,128]{2,1,0:T(8,128)S(1)} %add.38.refs_5_.rest_0_), channel_id=1, source_target_pairs={{0,32},{1,33},{2,34},{3,35},{4,36},{5,37},{6,38},{7,39},{8,40},{9,... | collective-permute-start | bytes 221192 | tf_op jit(solution)/shard_map/ppermute | solution.py:801
  70.7 9.3 %collective-permute-start.15 = (f32[16,256,128]{2,1,0:T(8,128)S(1)}, f32[16,256,128]{2,1,0:T(8,128)S(1)}, u32[]{:S(2)}, u32[]{:S(2)}) collective-permute-start(f32[16,256,128]{2,1,0:T(8,128)S(1)} %get-tuple-element.63.s_ref), channel_id=1, source_target_pairs={{0,64},{1,65},{2,66},{3,67},{4,68},{5,69},{6,70},{7,71},{8,72},{9,... | collective-permute-start | bytes 6291464 | tf_op jit(solution)/shard_map/ppermute | solution.py:801
  70.8 21.0 %collective-permute-start.16 = (f32[1632,128]{1,0:T(8,128)S(1)}, f32[1632,128]{1,0:T(8,128)S(1)}, u32[]{:S(2)}, u32[]{:S(2)}) collective-permute-start(f32[1632,128]{1,0:T(8,128)S(1)} %get-tuple-element.64), channel_id=1, source_target_pairs={{0,1},{1,0},{2,3},{3,2},{4,5},{5,4},{6,7},{7,6},{8,9},{9,8},{10,11... | collective-permute-start | bytes 2506760 | tf_op jit(solution)/shard_map/ppermute | solution.py:808
  70.9 26.7 %collective-permute-start.17 = (f32[1632,128]{1,0:T(8,128)S(1)}, f32[1632,128]{1,0:T(8,128)S(1)}, u32[]{:S(2)}, u32[]{:S(2)}) collective-permute-start(f32[1632,128]{1,0:T(8,128)S(1)} %get-tuple-element.65), channel_id=1, source_target_pairs={{0,31},{1,2},{2,1},{3,4},{4,3},{5,6},{6,5},{7,8},{8,7},{9,10},{10,... | collective-permute-start | bytes 2506760 | tf_op jit(solution)/shard_map/ppermute | solution.py:808
  78.5 4.5 %collective-permute-start.10 = (f32[16,64,128]{2,1,0:T(8,128)S(1)}, f32[16,64,128]{2,1,0:T(8,128)S(1)}, u32[]{:S(2)}, u32[]{:S(2)}) collective-permute-start(f32[16,64,128]{2,1,0:T(8,128)S(1)} %get-tuple-element.55), channel_id=1, source_target_pairs={{1,33},{2,34},{5,37},{6,38},{9,41},{10,42},{13,45},{14,46},{17,49}... | collective-permute-start | bytes 1572872 | tf_op jit(solution)/shard_map/ppermute | solution.py:853
  101.9 1.3 collective-permute-start.18
  103.2 3.9 %collective-permute-start.19 = (f32[64,128]{1,0:T(8,128)S(1)}, f32[64,128]{1,0:T(8,128)S(1)}, u32[]{:S(2)}, u32[]{:S(2)}) collective-permute-start(f32[64,128]{1,0:T(8,128)S(1)} %add.39), channel_id=1, source_target_pairs={{0,32},{1,33},{2,34},{3,35},{4,36},{5,37},{6,38},{7,39},{8,40},{9,... | collective-permute-start | bytes 98312 | tf_op jit(solution)/shard_map/ppermute | solution.py:862
  107.2 5.1 %collective-permute-start.20 = (f32[64,128]{1,0:T(8,128)S(1)}, f32[64,128]{1,0:T(8,128)S(1)}, u32[]{:S(2)}, u32[]{:S(2)}) collective-permute-start(f32[64,128]{1,0:T(8,128)S(1)} %add.40), channel_id=1, source_target_pairs={{0,36},{1,37},{2,38},{3,39},{4,32},{5,33},{6,34},{7,35},{8,44},{9,... | collective-permute-start | bytes 98312 | tf_op jit(solution)/shard_map/ppermute | solution.py:862
  112.3 3.9 %collective-permute-start.21 = (f32[64,128]{1,0:T(8,128)S(1)}, f32[64,128]{1,0:T(8,128)S(1)}, u32[]{:S(2)}, u32[]{:S(2)}) collective-permute-start(f32[64,128]{1,0:T(8,128)S(1)} %add.41), channel_id=1, source_target_pairs={{0,1},{1,0},{2,3},{3,2},{4,5},{5,4},{6,7},{7,6},{8,9},{9,8},{10,11... | collective-permute-start | bytes 98312 | tf_op jit(solution)/shard_map/ppermute | solution.py:862
  116.2 5.1 %collective-permute-start.22 = (f32[64,128]{1,0:T(8,128)S(1)}, f32[64,128]{1,0:T(8,128)S(1)}, u32[]{:S(2)}, u32[]{:S(2)}) collective-permute-start(f32[64,128]{1,0:T(8,128)S(1)} %add.42), channel_id=1, source_target_pairs={{0,3},{1,2},{2,1},{3,0},{4,7},{5,6},{6,5},{7,4},{8,11},{9,10},{10,... | collective-permute-start | bytes 98312 | tf_op jit(solution)/shard_map/ppermute | solution.py:862
  121.3 3.9 %collective-permute-start.23 = (f32[64,128]{1,0:T(8,128)S(1)}, f32[64,128]{1,0:T(8,128)S(1)}, u32[]{:S(2)}, u32[]{:S(2)}) collective-permute-start(f32[64,128]{1,0:T(8,128)S(1)} %add.43), channel_id=1, source_target_pairs={{0,8},{1,9},{2,10},{3,11},{4,12},{5,13},{6,14},{7,15},{8,0},{9,1},... | collective-permute-start | bytes 98312 | tf_op jit(solution)/shard_map/ppermute | solution.py:862
  125.3 5.1 %collective-permute-start.24 = (f32[64,128]{1,0:T(8,128)S(1)}, f32[64,128]{1,0:T(8,128)S(1)}, u32[]{:S(2)}, u32[]{:S(2)}) collective-permute-start(f32[64,128]{1,0:T(8,128)S(1)} %add.44), channel_id=1, source_target_pairs={{0,24},{1,25},{2,26},{3,27},{4,28},{5,29},{6,30},{7,31},{8,16},{9,... | collective-permute-start | bytes 98312 | tf_op jit(solution)/shard_map/ppermute | solution.py:862
  130.4 1.2 collective-permute-start.25
  (1 other events, 0.9 us)

commit v18 on v17

--- a/solution.py
+++ b/solution.py
@@ -74,11 +74,10 @@
 B = 4
 STEPS = C // B
 N = 2
-FIRST = 6
 MIDDLE = 10
 EDGE = 192
 MID = 64
-MID_START = (MIDDLE - FIRST) * EDGE
+MID_START = MIDDLE * EDGE
 
 
 def stride_rows(z):
@@ -101,29 +100,20 @@
     return pl.BlockSpec((rows, S), lambda i: (0, 0))
 
 
-def edge_spec(start, stop):
-    return pl.BlockSpec((N, EDGE, S), lambda i: (jnp.clip(i - start // N, 0, (stop - start) // N - 1), 0, 0))
-
-
-def edge_specs():
-    return [edge_spec(0, FIRST), edge_spec(FIRST, C), edge_spec(MIDDLE, C)]
+def edge_spec(start):
+    return pl.BlockSpec((N, EDGE, S), lambda i: (jnp.maximum(i - start // N, 0), 0, 0))
 
 
 def for_piece(edges, inner_ref, body):
-    step = pl.program_id(0)
-    direct = (inner_ref[0] == 1) | (step < MIDDLE // N)
-
-    @pl.when(step < FIRST // N)
+    direct = (inner_ref[0] == 1) | (pl.program_id(0) < MIDDLE // N)
+
+    @pl.when(direct)
     def _():
         body(edges[0])
 
-    @pl.when((step >= FIRST // N) & direct)
+    @pl.when(jnp.logical_not(direct))
     def _():
         body(edges[1])
-
-    @pl.when(jnp.logical_not(direct))
-    def _():
-        body(edges[2])
 
 
 SCALARS = pl.BlockSpec(memory_space=pltpu.SMEM)
@@ -131,8 +121,10 @@
 FULL_ROWS = sds((CELLS, S))
 HALO_ROWS = H * ROWS
 MESSAGE = sds((HALO_ROWS + 2 * NEAR, S))
-HALO = sds((H, C, C, S))
-EDGES = [sds((FIRST, EDGE, S)), sds((C - FIRST, EDGE, S)), sds((C - MIDDLE, EDGE, S))]
+ATOM_ROWS = 24
+HALO = sds((HALO_ROWS + 2 * ATOM_ROWS, S))
+DIRECT = sds((C * EDGE, S))
+RELAY = sds((C - MIDDLE, EDGE, S))
 
 
 def halo_rows(x, z):
@@ -160,89 +152,84 @@
         body(two, one)
 
 
-def pack_kernel(s_ref, odd_ref, edge_ref, one_ref, two_ref):
-    @pl.when(pl.program_id(0) < FIRST // N)
-    def _():
-        pack_edges(s_ref, edge_ref)
+def pack_kernel(s_ref, inner_ref, odd_ref, own_ref, other_ref, message_ref, relay_ref, mid_ref, one_ref, two_ref):
+    step = pl.program_id(0)
+    inner = inner_ref[0] == 1
+    mid_ref[...] = s_ref[:, 96:160, :]
+
+    @pl.when(step == 0)
+    def _():
+        for ref in (one_ref, two_ref):
+            ref[HALO_ROWS : HALO_ROWS + ATOM_ROWS, :] = own_ref[:ATOM_ROWS, :]
+            ref[HALO_ROWS + ATOM_ROWS :, :] = other_ref[:ATOM_ROWS, :]
+
+    @pl.when(step >= MIDDLE // N)
+    def _():
+        pack_edges(s_ref, relay_ref)
+
+    @pl.when(inner | (step < MIDDLE // N))
+    def _():
+        for p in range(N):
+            row = pl.multiple_of((step * N + p) * EDGE, MID)
+            message_ref[pl.ds(row, 96), :] = s_ref[p, 0:96, :]
+            message_ref[pl.ds(row + 96, 96), :] = s_ref[p, 160:256, :]
+
+    @pl.when(jnp.logical_not(inner))
+    def _():
+        for p in range(N):
+            row = pl.multiple_of(MID_START + (step * N + p) * MID, MID)
+            message_ref[pl.ds(row, MID), :] = s_ref[p, 96:160, :]
 
     def halos(head_ref, tail_ref):
         for p in range(N):
             for z in range(H):
-                head_ref[z, p] = s_ref[p, stride_rows(z), :]
-                tail_ref[z, p] = s_ref[p, stride_rows(C - H + z), :]
+                rows = halo_rows(step * N + p, z)
+                head_ref[rows, :] = s_ref[p, stride_rows(z), :]
+                tail_ref[rows, :] = s_ref[p, stride_rows(C - H + z), :]
 
     by_side(odd_ref, halos, one_ref, two_ref)
 
 
-def pack(s, odd):
+def pack(s, inner, odd, parcel, parcel_mate):
     return pl.pallas_call(
         pack_kernel,
         grid=(C // N,),
-        in_specs=[plane_spec(ROWS, N), SCALARS],
-        out_specs=edge_specs()[:1] + [halo_spec(N), halo_spec(N)],
-        out_shape=EDGES[:1] + [HALO, HALO],
+        in_specs=[plane_spec(ROWS, N), SCALARS, SCALARS, whole(56), whole(56)],
+        out_specs=[whole(C * EDGE), edge_spec(MIDDLE), plane_spec(MID, N)] + [whole(HALO.shape[0])] * 2,
+        out_shape=[DIRECT, RELAY, sds((C, MID, S)), HALO, HALO],
         compiler_params=params(12),
-        cost_estimate=cost(1 << 32, 6 << 20),
+        cost_estimate=cost(1 << 31, 8 << 20),
         name="pack",
-    )(s, odd)
-
-
-def pack_rest_kernel(s_ref, inner_ref, message_ref, relay_ref, mid_ref):
-    step = pl.program_id(0)
-    inner = inner_ref[0] == 1
-    mid_ref[...] = s_ref[:, 96:160, :]
-
-    @pl.when(step >= MIDDLE // N)
-    def _():
-        pack_edges(s_ref, relay_ref)
-
-    @pl.when((step >= FIRST // N) & (inner | (step < MIDDLE // N)))
-    def _():
-        for p in range(N):
-            row = pl.multiple_of((step * N + p - FIRST) * EDGE, MID)
-            message_ref[pl.ds(row, 96), :] = s_ref[p, 0:96, :]
-            message_ref[pl.ds(row + 96, 96), :] = s_ref[p, 160:256, :]
-
-    @pl.when(jnp.logical_not(inner))
-    def _():
-        for p in range(N):
-            row = pl.multiple_of(MID_START + (step * N + p) * MID, MID)
-            message_ref[pl.ds(row, MID), :] = s_ref[p, 96:160, :]
-
-
-def pack_rest(s, inner):
-    rows = (C - FIRST) * EDGE
-    message, relay, mid = pl.pallas_call(
-        pack_rest_kernel,
-        grid=(C // N,),
-        in_specs=[plane_spec(ROWS, N), SCALARS],
-        out_specs=[whole(rows), edge_spec(MIDDLE, C), plane_spec(MID, N)],
-        out_shape=[sds((rows, S)), EDGES[2], sds((C, MID, S))],
-        compiler_params=params(12),
-        cost_estimate=cost(1 << 31, 4 << 20),
-        name="pack_rest",
-    )(s, inner)
-    return message, relay, mid
-
-
-def column_kernel(own_ref, one_ref, two_ref, pot_ref, odd_ref, out_ref):
+    )(s, inner, odd, parcel, parcel_mate)
+
+
+def stack_kernel(atoms_ref, pot_ref, out_ref):
+    out_ref[0:24, :] = atoms_ref[...]
+    out_ref[24:56, :] = pot_ref[...]
+
+
+def stack(atoms, pot):
+    return pl.pallas_call(stack_kernel, out_shape=sds((56, S)), compiler_params=params(4), name="stack")(atoms, pot)
+
+
+def column_kernel(own_ref, other_ref, one_ref, two_ref, odd_ref, out_ref):
     def beside(below_ref, above_ref):
-        out_ref[0:24, :] = below_ref[...]
-        out_ref[48:72, :] = above_ref[...]
+        out_ref[0:48, :] = below_ref[HALO_ROWS:, :]
+        out_ref[96:144, :] = above_ref[HALO_ROWS:, :]
 
     by_side(odd_ref, beside, one_ref, two_ref)
-    out_ref[24:48, :] = own_ref[...]
-    out_ref[72:104, :] = pot_ref[...]
-
-
-def column(own, one, two, pot, odd):
+    out_ref[48:72, :] = own_ref[:ATOM_ROWS, :]
+    out_ref[72:96, :] = other_ref[:ATOM_ROWS, :]
+
+
+def column(own, other, halos, odd):
     return pl.pallas_call(
         column_kernel,
         in_specs=[pl.BlockSpec(memory_space=pltpu.VMEM)] * 4 + [SCALARS],
-        out_shape=sds((104, S)),
-        compiler_params=params(4),
+        out_shape=sds((144, S)),
+        compiler_params=params(8),
         name="column",
-    )(own, one, two, pot, odd)
+    )(own, other, *halos, odd)
 
 
 def along_x(s_ref, mate_ref, out_ref, add):
@@ -285,8 +272,8 @@
             for y in range(C):
                 ext_ref[y * 32 + 8 : y * 32 + 24, :] = s_ref[x, y * C : (y + 1) * C, :]
             for z in range(H):
-                ext_ref[pl.ds(2 + z, C, stride=32), :] = low_ref[z, x]
-                ext_ref[pl.ds(24 + z, C, stride=32), :] = high_ref[z, x]
+                ext_ref[pl.ds(2 + z, C, stride=32), :] = low_ref[halo_rows(x, z), :]
+                ext_ref[pl.ds(24 + z, C, stride=32), :] = high_ref[halo_rows(x, z), :]
             for y in range(C):
                 rows = slice(y * C, (y + 1) * C)
                 out_ref[x, rows, :] = part_ref[x, rows, :] + z_taps(ext_ref, y)
@@ -354,7 +341,7 @@
 
 def spread_kernel(parcel_ref, vb_ref):
     def spread_row(row, _):
-        line = (parcel_ref[pl.ds(72 + row, 1), :] + (DIAGONAL - filter_centre)) * (1.0 / filter_half)
+        line = (parcel_ref[pl.ds(24 + row, 1), :] + (DIAGONAL - filter_centre)) * (1.0 / filter_half)
         start = pl.multiple_of(row * 128, 128)
         vb_ref[pl.ds(start, 128), :] = jnp.broadcast_to(line, (128, 128)).T
         return 0
@@ -373,15 +360,17 @@
 
 
 def prep_kernel(*refs):
-    parcels = refs[:4]
-    corner_ref, vb_ref, s_ref, gg_ref, coef_ref, energy_ref, near_ref, table_ref, a1_ref, a1z_ref, a2_ref, a2s_ref = refs[4:]
+    own_ref, other_ref, corner_ref, vb_ref, s_ref, gg_ref, coef_ref, energy_ref, near_ref, table_ref = refs[:10]
+    a1_ref, a1z_ref, a2_ref, a2s_ref = refs[10:]
     upper_x, upper_y = corner_ref[0] > 0, corner_ref[1] > 0
     for slab in range(3):
-        own, over_x, over_y, over_xy = [parcel[slab * 24 : slab * 24 + 24, :] for parcel in parcels]
-        same_x = [jnp.where(upper_y, over_y, own), jnp.where(upper_y, own, over_y)]
-        other_x = [jnp.where(upper_y, over_xy, over_x), jnp.where(upper_y, over_x, over_xy)]
-        ordered = [jnp.where(upper_x, o, m) for m, o in zip(same_x, other_x)]
-        ordered += [jnp.where(upper_x, m, o) for m, o in zip(same_x, other_x)]
+        own = [own_ref[slab * 48 + j * 24 : slab * 48 + j * 24 + 24, :] for j in range(2)]
+        other = [other_ref[slab * 48 + j * 24 : slab * 48 + j * 24 + 24, :] for j in range(2)]
+        lower = [jnp.where(upper_x, o, m) for m, o in zip(own, other)]
+        higher = [jnp.where(upper_x, m, o) for m, o in zip(own, other)]
+        ordered = []
+        for pair in (lower, higher):
+            ordered += [jnp.where(upper_y, pair[1], pair[0]), jnp.where(upper_y, pair[0], pair[1])]
         for j in range(4):
             near_ref[slab * 96 + j * 24 : slab * 96 + j * 24 + 24, :] = ordered[j]
     blank = jnp.zeros((16, 128), F32)
@@ -486,7 +475,7 @@
     vmem = pl.BlockSpec(memory_space=pltpu.VMEM)
     return pl.pallas_call(
         prep_kernel,
-        in_specs=[vmem] * 4 + [pl.BlockSpec(memory_space=pltpu.SMEM), vmem, vmem],
+        in_specs=[vmem] * 2 + [pl.BlockSpec(memory_space=pltpu.SMEM), vmem, vmem],
         out_shape=[sds((2, CELLS, S), BF16), sds((3, NEAR, S)), sds((NEAR, S))],
         scratch_shapes=[
             pltpu.VMEM((288, 128), F32),
@@ -510,7 +499,7 @@
 
 
 def first_kernel(s_ref, side_ref, vb_ref, *refs):
-    inner_ref, odd_ref, part_ref, mate_ref, q_ref, mix_ref, one_ref, two_ref = refs[3:]
+    inner_ref, odd_ref, part_ref, mate_ref, q_ref, mix_ref, one_ref, two_ref = refs[2:]
     step = pl.program_id(0)
 
     @pl.when(step == 0)
@@ -537,7 +526,7 @@
                     q_ref[p, rows, :] = q
                     mix_ref[p, rows, :] = side_ref[p, rows, :] + q + dy
 
-    for_piece(refs[:3], inner_ref, planes)
+    for_piece(refs[:2], inner_ref, planes)
 
     def halos(head_ref, tail_ref):
         for p in range(N):
@@ -554,7 +543,7 @@
     return pl.pallas_call(
         first_kernel,
         grid=(C // N,),
-        in_specs=[plane_spec(ROWS, N)] * 3 + edge_specs() + [SCALARS] * 2 + [shares] * 2,
+        in_specs=[plane_spec(ROWS, N)] * 3 + [edge_spec(0), edge_spec(MIDDLE)] + [SCALARS] * 2 + [shares] * 2,
         out_specs=[plane_spec(ROWS, N), plane_spec(ROWS, N), whole(MESSAGE.shape[0]), whole(MESSAGE.shape[0])],
         out_shape=[FULL, FULL, MESSAGE, MESSAGE],
         compiler_params=params(16),
@@ -564,7 +553,7 @@
 
 
 def base_kernel(s_ref, mid_ref, vb_ref, vb_mate_ref, q_ref, side_ref, part_ref, *refs):
-    inner_ref, message_ref, out_ref, middle_ref = refs[3:]
+    inner_ref, message_ref, out_ref, middle_ref = refs[2:]
     step = pl.program_id(0)
     inner = inner_ref[0] == 1
 
@@ -599,7 +588,7 @@
                     total = total + vb_ref[p, rows, :] * (side_ref[p, rows, :] + q[y])
                     out_ref[p, rows, :] = 2.0 * (total + part_ref[p, rows, :]) - ring[y]
 
-    for_piece(refs[:3], inner_ref, planes)
+    for_piece(refs[:2], inner_ref, planes)
 
 
 def make_base(s, mid, vb, vb_mate, q, side_part, part, edges, inner):
@@ -608,15 +597,14 @@
         grid=(C // N,),
         in_specs=[plane_spec(ROWS, N), plane_spec(MID, N)]
         + [plane_spec(ROWS, N)] * 5
-        + edge_specs()
-        + [SCALARS, whole((C - FIRST) * EDGE)],
+        + [edge_spec(0), edge_spec(MIDDLE), SCALARS, whole(C * EDGE)],
         out_specs=plane_spec(ROWS, N),
         out_shape=FULL,
         scratch_shapes=[pltpu.VMEM((N, MID, S), F32)],
         compiler_params=params(16),
         cost_estimate=cost(1 << 25, 16 << 20),
         name="base",
-    )(s, mid, vb, vb_mate, q, side_part, part, *edges, inner, edges[1].reshape(-1, S))
+    )(s, mid, vb, vb_mate, q, side_part, part, *edges, inner, edges[0].reshape(-1, S))
 
 
 def second_kernel(base_ref, one_ref, two_ref, gg_high_ref, gg_low_ref, *rest):
@@ -811,47 +799,43 @@
     outer_ones = [d for d in range(count) if d % 4 in (0, 3)]
     inner = ((lax.axis_index("gzs") + 1) // 2 % 2).astype(jnp.int32).reshape(1)
     s = states.reshape(C, ROWS, S)
+    mate = send(s, over_x)
+    corner = jnp.stack([gx * C, gy * C]).astype(jnp.int32)
+    upper = gx.astype(jnp.int32).reshape(1)
+    odd = (lax.axis_index("gzs") % 2).astype(jnp.int32).reshape(1)
     pot = potential.reshape(32, 128)
-
     atoms = jnp.concatenate(
         [projectors.reshape(4, TAPS), atom_sites.astype(F32), energies[:, None], jnp.zeros((4, 768 - TAPS - 4), F32)],
         axis=1,
     ).reshape(24, 128)
-    mate = send(s, over_x)
-    corner = jnp.stack([gx * C, gy * C]).astype(jnp.int32)
-    upper = gx.astype(jnp.int32).reshape(1)
-    odd = (lax.axis_index("gzs") % 2).astype(jnp.int32).reshape(1)
-    to_pack, corner, upper, inner, odd = barrier((s, corner, upper, inner, odd))
-    beside_one, beside_two = to_pairs(atoms, atoms)
-    one_edge, halo_one, halo_two = pack(to_pack, odd)
-    one_edge = send(one_edge, over_y)
-    halo_one, halo_two, beside_one, beside_two = barrier((halo_one, halo_two, beside_one, beside_two))
-    parcel = column(atoms, beside_one, beside_two, pot, odd)
-    parcel_xy = send(parcel, over_x ^ over_y)
-    parcel_x = send(parcel, over_x)
+    pot, corner, upper, inner, odd, atoms = barrier((pot, corner, upper, inner, odd, atoms))
+    parcel = stack(atoms, pot)
+    parcel_mate = send(parcel, over_y)
+    message, relay, mid, halo_one, halo_two = pack(s, inner, odd, parcel, parcel_mate)
+    message = send(message, over_y)
+    relayed = lax.ppermute(relay, AXES, [(d, d ^ over_y ^ 1) for d in outer_ones])
     halos = to_pairs(halo_one, halo_two)
-    message, relay, mid = pack_rest(s, inner)
     vb = spread(parcel)
+    mate, relayed = barrier((mate, relayed))
     beside = side_x(s, mate)
-    parcel_xy, one_edge, message, relay, beside = barrier((parcel_xy, one_edge, message, relay, beside))
-    relayed = lax.ppermute(relay, AXES, [(d, d ^ over_y ^ 1) for d in outer_ones])
-    message = send(message, over_y)
-    parcel_y = send(parcel_xy, over_x)
-    gg, part, energy = prep([parcel, parcel_x, parcel_y, parcel_xy], corner, vb, s)
-
-    part, relayed = barrier((part, relayed))
+    halos, beside, vb = barrier((halos, beside, vb))
     relayed = lax.ppermute(relayed, AXES, [(d, d ^ 1) for d in inner_ones])
+    side_part = side_z(s, beside, halos, odd)
+    atoms = column(parcel, parcel_mate, halos, odd)
+    atoms, side_part = barrier((atoms, side_part))
+    atoms_mate = send(atoms, over_x)
+    gg, part, energy = prep([atoms, atoms_mate], corner, vb, s)
+
     part = part + send(part, over_x)
     part_mate = send(part, over_y)
-    side_part = side_z(s, beside, halos, odd)
-    edges = [one_edge, message.reshape(C - FIRST, EDGE, S), relayed]
+    edges = [message.reshape(C, EDGE, S), relayed]
     vb = vb.reshape(C, ROWS, S)
     q, mix, halo_one, halo_two = make_first(s, side_part, vb, edges, inner, odd, part, part_mate)
     halos = to_pairs(halo_one, halo_two)
     mate = send(mix, over_x)
     mid, part_mate = barrier((mid, part_mate))
     mid = lax.ppermute(mid, AXES, [(d, d ^ over_y) for d in inner_ones])
-    vb_mate = spread(parcel_y).reshape(C, ROWS, S)
+    vb_mate = spread(parcel_mate).reshape(C, ROWS, S)
     part_two = side_again(mix, mate)
     base = make_base(s, mid, vb, vb_mate, q, side_part, part_two, edges, inner)
     gg = gg.reshape(2, C, ROWS, S)

time: 150 us -> 147 us (0.980)
  waiting for transfers between devices: 58.8 us -> 63.7 us
  starting transfers between devices: 36.3 us -> 32.6 us
  Pallas kernels: 47.5 us -> 44.2 us
    ppermute x6 -> x4, starting transfers between devices: 24.5 us -> 16.1 us  [to_pairs(): return (lax.ppermute(one, AXES, near), lax.ppermute(two, AXES, far))]
    ppermute x1, waiting for transfers between devices: 0.01 us -> 5.71 us  [per_device(): lax.ppermute(relay, AXES, [(d, d ^ over_y ^ 1) for d in outer_ones])]
    ppermute x6 -> x4, waiting for transfers between devices: 20.3 us -> 24 us  [to_pairs(): return (lax.ppermute(one, AXES, near), lax.ppermute(two, AXES, far))]
    ppermute x6, waiting for transfers between devices: 24.2 us -> 21.7 us  [per_device(): own = own + lax.ppermute(own, AXES, [(d, d ^ flip) for d in range(count)])]
    ppermute x6, starting transfers between devices: 2.95 us -> 5.45 us  [per_device(): own = own + lax.ppermute(own, AXES, [(d, d ^ flip) for d in range(count)])]
    ppermute x11 -> x9, waiting for transfers between devices: 14.3 us -> 12.3 us  [send(): return lax.ppermute(value, AXES, [(d, d ^ flip) for d in range(count)])]
    ppermute x11 -> x9, starting transfers between devices: 4.14 us -> 5.88 us  [send(): return lax.ppermute(value, AXES, [(d, d ^ flip) for d in range(count)])]
    pallas_call x1, Pallas kernels: 3.12 us -> 1.47 us  [side_x(): pl.pallas_call(side_x_kernel, out_shape=FULL, compiler_params=params(12),...]
  transfers between devices with their start and end apart: 26 -> 22, of which waited for: 17 -> 17; matrix products, arithmetic and copies ran while one was open for 2% -> 3% of each run, Pallas kernels for 16% -> 14%
where the time goes in v18:
time: 147 us; the launch traced here: 146 us
  waiting for transfers between devices  63.7 us (43%)
  Pallas kernels  44.2 us (30%)
  starting transfers between devices  32.6 us (22%)
  local copies, waits for them, and re-layouts  4.53 us (3%)
    ppermute x4, waiting for transfers between devices, to_pairs(): return (lax.ppermute(one, AXES, near), lax.ppermute(two, AXES, far))  24 us
    ppermute x6, waiting for transfers between devices, per_device(): own = own + lax.ppermute(own, AXES, [(d, d ^ flip) for d in range(count)])  21.7 us
    pallas_call x1, Pallas kernels, turn(): pl.pallas_call(turn_kernel, grid=(STEPS,), in_specs=[plane_spec(), whole(...  17 us
    ppermute x4, starting transfers between devices, to_pairs(): return (lax.ppermute(one, AXES, near), lax.ppermute(two, AXES, far))  16.1 us
    ppermute x9, waiting for transfers between devices, send(): return lax.ppermute(value, AXES, [(d, d ^ flip) for d in range(count)])  12.3 us
    pallas_call x1, Pallas kernels, prep(): pl.pallas_call(prep_kernel, in_specs=[vmem] * 2 + [pl.BlockSpec(memory_sp...  7.8 us
    ppermute x9, starting transfers between devices, send(): return lax.ppermute(value, AXES, [(d, d ^ flip) for d in range(count)])  5.88 us
    ppermute x1, waiting for transfers between devices, per_device(): lax.ppermute(relay, AXES, [(d, d ^ over_y ^ 1) for d in outer_ones])  5.71 us
  transfers between devices with their start and end apart: 22, of which 17 were waited for; matrix products, arithmetic and copies ran while one was open for 3% of the time, Pallas kernels for 14%

profile of v18, /device:TPU:0, one launch (start us, length us, event | category | flops | bytes accessed | tf_op | source)
XLA Modules:
  0.0 146.1 jit_solution(12584940193417049269)
XLA Ops:
  3.8 2.0 %collective-permute-start = (f32[56,128]{1,0:T(8,128)S(1)}, f32[56,128]{1,0:T(8,128)S(1)}, u32[]{:S(2)}, u32[]{:S(2)}) collective-permute-start(f32[56,128]{1,0:T(8,128)S(1)} %stack.13.own_ref.parcel_ref), channel_id=1, source_target_pairs={{0,32},{1,33},{2,34},{3,35},{4,36},{5,37},{6,38},{7,39},{8,40},{9,... | collective-permute-start | bytes 86024 | tf_op jit(solution)/shard_map/ppermute | solution.py:789
  5.8 2.0 %collective-permute-done.other_ref.parcel_ref = f32[56,128]{1,0:T(8,128)S(1)} collective-permute-done((f32[56,128]{1,0:T(8,128)S(1)}, f32[56,128]{1,0:T(8,128)S(1)}, u32[]{:S(2)}, u32[]{:S(2)}) %collective-permute-start) | collective-permute-done | bytes 28704 | tf_op jit(solution)/shard_map/ppermute | solution.py:789
  7.8 1.6 %copy-done = f32[16,16,16,128]{3,2,1,0:T(8,128)S(1)} copy-done((f32[16,16,16,128]{3,2,1,0:T(8,128)S(1)}, f32[16,16,16,128]{3,2,1,0:T(8,128)}, u32[]{:S(2)}) %copy-start) | copy-done | bytes 2097176
  10.3 2.0 %collective-permute-start.9 = (f32[3072,128]{1,0:T(8,128)S(1)}, f32[3072,128]{1,0:T(8,128)S(1)}, u32[]{:S(2)}, u32[]{:S(2)}) collective-permute-start(f32[3072,128]{1,0:T(8,128)S(1)} %get-tuple-element.54), channel_id=1, source_target_pairs={{0,32},{1,33},{2,34},{3,35},{4,36},{5,37},{6,38},{7,39},{8,40},{9,... | collective-permute-start | bytes 4718600 | tf_op jit(solution)/shard_map/ppermute | solution.py:789
  12.3 3.1 %collective-permute-start.4 = (f32[6,192,128]{2,1,0:T(8,128)S(1)}, f32[6,192,128]{2,1,0:T(8,128)S(1)}, u32[]{:S(2)}, u32[]{:S(2)}) collective-permute-start(f32[6,192,128]{2,1,0:T(8,128)S(1)} %get-tuple-element.43), channel_id=1, source_target_pairs={{0,33},{3,34},{4,37},{7,38},{8,41},{11,42},{12,45},{15,46},{16,49}... | collective-permute-start | bytes 1769480 | tf_op jit(solution)/shard_map/ppermute | solution.py:816
  15.5 7.9 %collective-permute-start.2 = (f32[1584,128]{1,0:T(8,128)S(1)}, f32[1584,128]{1,0:T(8,128)S(1)}, u32[]{:S(2)}, u32[]{:S(2)}) collective-permute-start(f32[1584,128]{1,0:T(8,128)S(1)} %get-tuple-element.42), channel_id=1, source_target_pairs={{0,31},{1,2},{2,1},{3,4},{4,3},{5,6},{6,5},{7,8},{8,7},{9,10},{10,... | collective-permute-start | bytes 2433032 | tf_op jit(solution)/shard_map/ppermute | solution.py:796
  23.5 5.7 %collective-permute-done.4 = f32[6,192,128]{2,1,0:T(8,128)S(1)} collective-permute-done((f32[6,192,128]{2,1,0:T(8,128)S(1)}, f32[6,192,128]{2,1,0:T(8,128)S(1)}, u32[]{:S(2)}, u32[]{:S(2)}) %collective-permute-start.4) | collective-permute-done | bytes 589856 | tf_op jit(solution)/shard_map/ppermute | solution.py:816
  29.2 1.3 collective-permute-start.10
  31.3 1.5 %side_x.1.part_ref = f32[16,256,128]{2,1,0:T(8,128)S(1)} custom-call(f32[16,256,128]{2,1,0:T(8,128)S(1)} %bitcast.15, f32[16,256,128]{2,1,0:T(8,128)S(1)} %collective-permute-done.3.mate_ref), custom_call_target="tpu_custom_call" | custom-call | flops 16777216 | bytes 6291456 | tf_op jit(solution)/shard_map/side_x/pallas_call | solution.py:260
  32.8 12.4 %collective-permute-done.1.one_ref = f32[1584,128]{1,0:T(8,128)S(1)} collective-permute-done((f32[1584,128]{1,0:T(8,128)S(1)}, f32[1584,128]{1,0:T(8,128)S(1)}, u32[]{:S(2)}, u32[]{:S(2)}) %collective-permute-start.1) | collective-permute-done | bytes 811040 | tf_op jit(solution)/shard_map/ppermute | solution.py:796
  45.1 3.0 %side_z.1.side_ref = f32[16,256,128]{2,1,0:T(8,128)S(1)} custom-call(f32[16,256,128]{2,1,0:T(8,128)S(1)} %bitcast.16, f32[16,256,128]{2,1,0:T(8,128)S(1)} %side_x.1.part_ref, f32[1584,128]{1,0:T(8,128)S(1)} %collective-permute-done.1.one_ref, f32[1584,128]{1,0:T(8,128)S(1)} %collective-permute-done.2.two_ref, s32[1]{0:T(128)} %bitcast.5.odd_ref.refs_3_.rest_4_), custom_call_target="tpu_custom_call" | custom-call | flops 16777216 | bytes 8388608 | tf_op jit(solution)/shard_map/side_z/pallas_call | solution.py:288
  48.3 1.3 collective-permute-done.5.refs_1_
  49.5 7.8 %prep.1 = (bf16[2,4096,128]{2,1,0:T(8,128)(2,1)S(1)}, f32[3,48,128]{2,1,0:T(8,128)S(1)}, f32[48,128]{1,0:T(8,128)S(1)}) custom-call(f32[144,128]{1,0:T(8,128)S(1)} %column.1.refs_0_, f32[144,128]{1,0:T(8,128)S(1)} %collective-permute-done.5.refs_1_, s32[2]{0:T(128)S(1)} %pad_add_fusion.refs_2_, f32[4096,128]{1,0:T(8,128)S(1)} %spread.2.refs_3_, ...), custom_call_target="tpu_custom_call" | custom-call | flops 134217728 | bytes 10485760 | tf_op jit(solution)/shard_map/prep/pallas_call | solution.py:476
  58.7 1.4 collective-permute-start.7
  60.1 4.7 %collective-permute-done.9.refs_3_ = f32[3072,128]{1,0:T(8,128)S(1)} collective-permute-done((f32[3072,128]{1,0:T(8,128)S(1)}, f32[3072,128]{1,0:T(8,128)S(1)}, u32[]{:S(2)}, u32[]{:S(2)}) %collective-permute-start.9) | collective-permute-done | bytes 1572896 | tf_op jit(solution)/shard_map/ppermute | solution.py:789
  65.6 2.2 %first.1 = (f32[16,256,128]{2,1,0:T(8,128)S(1)}, f32[16,256,128]{2,1,0:T(8,128)S(1)}, f32[1632,128]{1,0:T(8,128)S(1)}, f32[1632,128]{1,0:T(8,128)S(1)}) custom-call(f32[16,256,128]{2,1,0:T(8,128)S(1)} %bitcast.18, f32[16,256,128]{2,1,0:T(8,128)S(1)} %side_z.1.side_ref, f32[16,256,128]{2,1,0:T(8,128)S(1)} %bitcast.20, f32[16,192,128]{2,1,0:T(8,128)S(1)} %bitcast.22, ...), custom_call_target="tpu_custom_call" | custom-call | flops 16777216 | bytes 14680064 | tf_op jit(solution)/shard_map/first/pallas_call | solution.py:543
  68.0 8.0 %collective-permute-start.13 = (f32[1632,128]{1,0:T(8,128)S(1)}, f32[1632,128]{1,0:T(8,128)S(1)}, u32[]{:S(2)}, u32[]{:S(2)}) collective-permute-start(f32[1632,128]{1,0:T(8,128)S(1)} %get-tuple-element.59), channel_id=1, source_target_pairs={{0,31},{1,2},{2,1},{3,4},{4,3},{5,6},{6,5},{7,8},{8,7},{9,10},{10,... | collective-permute-start | bytes 2506760 | tf_op jit(solution)/shard_map/ppermute | solution.py:796
  77.6 2.9 %side_again.1.part_ref = f32[16,256,128]{2,1,0:T(8,128)S(1)} custom-call(f32[16,256,128]{2,1,0:T(8,128)S(1)} %get-tuple-element.57.s_ref, f32[16,256,128]{2,1,0:T(8,128)S(1)} %collective-permute-done.11.mate_ref), custom_call_target="tpu_custom_call" | custom-call | flops 33554432 | bytes 6291456 | tf_op jit(solution)/shard_map/side_again/pallas_call | solution.py:316
  80.5 2.9 %base.1.base_ref = f32[16,256,128]{2,1,0:T(8,128)S(1)} custom-call(f32[16,256,128]{2,1,0:T(8,128)S(1)} %bitcast.19, f32[16,64,128]{2,1,0:T(8,128)S(1)} %collective-permute-done.8.mid_ref, f32[16,256,128]{2,1,0:T(8,128)S(1)} %bitcast.21, f32[16,256,128]{2,1,0:T(8,128)S(1)} %bitcast.26, f32[16,256,128]{2,1,0:T(8,128)S(1)} %get-tuple-element.56.q_ref, ...), custom_call_target="tpu_custom_call" | custom-call | flops 33554432 | bytes 16777216 | tf_op jit(solution)/shard_map/base/pallas_call | solution.py:595
  83.4 5.5 %collective-permute-done.12.one_ref = f32[1632,128]{1,0:T(8,128)S(1)} collective-permute-done((f32[1632,128]{1,0:T(8,128)S(1)}, f32[1632,128]{1,0:T(8,128)S(1)}, u32[]{:S(2)}, u32[]{:S(2)}) %collective-permute-start.12) | collective-permute-done | bytes 835616 | tf_op jit(solution)/shard_map/ppermute | solution.py:796
  88.9 6.2 %collective-permute-done.13.two_ref = f32[1632,128]{1,0:T(8,128)S(1)} collective-permute-done((f32[1632,128]{1,0:T(8,128)S(1)}, f32[1632,128]{1,0:T(8,128)S(1)}, u32[]{:S(2)}, u32[]{:S(2)}) %collective-permute-start.13) | collective-permute-done | bytes 835616 | tf_op jit(solution)/shard_map/ppermute | solution.py:796
  95.1 4.3 %second.1 = (f32[16,256,128]{2,1,0:T(8,128)S(1)}, f32[64,128]{1,0:T(8,128)S(1)}, f32[64,128]{1,0:T(8,128)S(1)}) custom-call(f32[16,256,128]{2,1,0:T(8,128)S(1)} %base.1.base_ref, f32[1632,128]{1,0:T(8,128)S(1)} %collective-permute-done.12.one_ref, f32[1632,128]{1,0:T(8,128)S(1)} %collective-permute-done.13.two_ref, bf16[2,16,256,128]{3,2,1,0:T(8,128)(2,1)S(1)} %bitcast.24, ...), custom_call_target="tpu_custom_call" | custom-call | flops 134217728 | bytes 8388608 | tf_op jit(solution)/shard_map/second/pallas_call | solution.py:670
  101.8 2.9 %collective-permute-done.15 = f32[64,128]{1,0:T(8,128)S(1)} collective-permute-done((f32[64,128]{1,0:T(8,128)S(1)}, f32[64,128]{1,0:T(8,128)S(1)}, u32[]{:S(2)}, u32[]{:S(2)}) %collective-permute-start.15) | collective-permute-done | bytes 32800 | tf_op jit(solution)/shard_map/ppermute | solution.py:846
  105.6 4.3 %collective-permute-done.16 = f32[64,128]{1,0:T(8,128)S(1)} collective-permute-done((f32[64,128]{1,0:T(8,128)S(1)}, f32[64,128]{1,0:T(8,128)S(1)}, u32[]{:S(2)}, u32[]{:S(2)}) %collective-permute-start.16) | collective-permute-done | bytes 32800 | tf_op jit(solution)/shard_map/ppermute | solution.py:846
  109.9 3.9 %collective-permute-done.17 = f32[64,128]{1,0:T(8,128)S(1)} collective-permute-done((f32[64,128]{1,0:T(8,128)S(1)}, f32[64,128]{1,0:T(8,128)S(1)}, u32[]{:S(2)}, u32[]{:S(2)}) %collective-permute-start.17) | collective-permute-done | bytes 32800 | tf_op jit(solution)/shard_map/ppermute | solution.py:846
  113.8 1.3 collective-permute-start.18
  115.1 3.8 %collective-permute-done.18 = f32[64,128]{1,0:T(8,128)S(1)} collective-permute-done((f32[64,128]{1,0:T(8,128)S(1)}, f32[64,128]{1,0:T(8,128)S(1)}, u32[]{:S(2)}, u32[]{:S(2)}) %collective-permute-start.18) | collective-permute-done | bytes 32800 | tf_op jit(solution)/shard_map/ppermute | solution.py:846
  118.9 3.9 %collective-permute-done.19 = f32[64,128]{1,0:T(8,128)S(1)} collective-permute-done((f32[64,128]{1,0:T(8,128)S(1)}, f32[64,128]{1,0:T(8,128)S(1)}, u32[]{:S(2)}, u32[]{:S(2)}) %collective-permute-start.19) | collective-permute-done | bytes 32800 | tf_op jit(solution)/shard_map/ppermute | solution.py:846
  122.8 2.3 %collective-permute-start.20 = (f32[64,128]{1,0:T(8,128)S(1)}, f32[64,128]{1,0:T(8,128)S(1)}, u32[]{:S(2)}, u32[]{:S(2)}) collective-permute-start(f32[64,128]{1,0:T(8,128)S(1)} %add.44), channel_id=1, source_target_pairs={{0,24},{1,25},{2,26},{3,27},{4,28},{5,29},{6,30},{7,31},{8,16},{9,... | collective-permute-start | bytes 98312 | tf_op jit(solution)/shard_map/ppermute | solution.py:846
  125.1 2.8 %collective-permute-done.20 = f32[64,128]{1,0:T(8,128)S(1)} collective-permute-done((f32[64,128]{1,0:T(8,128)S(1)}, f32[64,128]{1,0:T(8,128)S(1)}, u32[]{:S(2)}, u32[]{:S(2)}) %collective-permute-start.20) | collective-permute-done | bytes 32800 | tf_op jit(solution)/shard_map/ppermute | solution.py:846
  128.0 1.2 collective-permute-done.21.other_ref
  129.2 17.0 %turn.1 = f32[16,256,128]{2,1,0:T(8,128)} custom-call(f32[16,256,128]{2,1,0:T(8,128)S(1)} %get-tuple-element.64.second_ref, f32[64,128]{1,0:T(8,128)S(1)} %add.45.own_ref, f32[64,128]{1,0:T(8,128)S(1)} %collective-permute-done.21.other_ref, s32[1]{0:T(128)} %bitcast.3.rest_3_.upper_ref), custom_call_target="tpu_custom_call" | custom-call | flops 268435456 | bytes 4194304 | tf_op jit(solution)/shard_map/turn/pallas_call | solution.py:769
  (47 shorter events, 12.7 us)
Async XLA Ops:
  0.0 29.2 %collective-permute-start.3 = (f32[16,256,128]{2,1,0:T(8,128)}, f32[16,256,128]{2,1,0:T(8,128)S(1)}, u32[]{:S(2)}, u32[]{:S(2)}) collective-permute-start(f32[16,256,128]{2,1,0:T(8,128)} %bitcast.13), channel_id=1, source_target_pairs={{0,64},{1,65},{2,66},{3,67},{4,68},{5,69},{6,70},{7,71},{8,72},{9,... | collective-permute-start | bytes 6291464 | tf_op jit(solution)/shard_map/ppermute | solution.py:789
  3.8 4.0 %collective-permute-start = (f32[56,128]{1,0:T(8,128)S(1)}, f32[56,128]{1,0:T(8,128)S(1)}, u32[]{:S(2)}, u32[]{:S(2)}) collective-permute-start(f32[56,128]{1,0:T(8,128)S(1)} %stack.13.own_ref.parcel_ref), channel_id=1, source_target_pairs={{0,32},{1,33},{2,34},{3,35},{4,36},{5,37},{6,38},{7,39},{8,40},{9,... | collective-permute-start | bytes 86024 | tf_op jit(solution)/shard_map/ppermute | solution.py:789
  7.8 1.6 %copy-start = (f32[16,16,16,128]{3,2,1,0:T(8,128)S(1)}, f32[16,16,16,128]{3,2,1,0:T(8,128)}, u32[]{:S(2)}) copy-start(f32[16,16,16,128]{3,2,1,0:T(8,128)} %param.5) | copy-start | bytes 6291460
  10.3 21.0 %copy-start.1 = (f32[16,16,16,128]{3,2,1,0:T(8,128)S(1)}, f32[16,16,16,128]{3,2,1,0:T(8,128)}, u32[]{:S(2)}) copy-start(f32[16,16,16,128]{3,2,1,0:T(8,128)} %param.5) | copy-start | bytes 6291460
  10.3 54.5 %collective-permute-start.9 = (f32[3072,128]{1,0:T(8,128)S(1)}, f32[3072,128]{1,0:T(8,128)S(1)}, u32[]{:S(2)}, u32[]{:S(2)}) collective-permute-start(f32[3072,128]{1,0:T(8,128)S(1)} %get-tuple-element.54), channel_id=1, source_target_pairs={{0,32},{1,33},{2,34},{3,35},{4,36},{5,37},{6,38},{7,39},{8,40},{9,... | collective-permute-start | bytes 4718600 | tf_op jit(solution)/shard_map/ppermute | solution.py:789
  12.3 16.9 %collective-permute-start.4 = (f32[6,192,128]{2,1,0:T(8,128)S(1)}, f32[6,192,128]{2,1,0:T(8,128)S(1)}, u32[]{:S(2)}, u32[]{:S(2)}) collective-permute-start(f32[6,192,128]{2,1,0:T(8,128)S(1)} %get-tuple-element.43), channel_id=1, source_target_pairs={{0,33},{3,34},{4,37},{7,38},{8,41},{11,42},{12,45},{15,46},{16,49}... | collective-permute-start | bytes 1769480 | tf_op jit(solution)/shard_map/ppermute | solution.py:816
  15.4 29.7 %collective-permute-start.1 = (f32[1584,128]{1,0:T(8,128)S(1)}, f32[1584,128]{1,0:T(8,128)S(1)}, u32[]{:S(2)}, u32[]{:S(2)}) collective-permute-start(f32[1584,128]{1,0:T(8,128)S(1)} %get-tuple-element.41), channel_id=1, source_target_pairs={{0,1},{1,0},{2,3},{3,2},{4,5},{5,4},{6,7},{7,6},{8,9},{9,8},{10,11... | collective-permute-start | bytes 2433032 | tf_op jit(solution)/shard_map/ppermute | solution.py:796
  15.5 29.6 %collective-permute-start.2 = (f32[1584,128]{1,0:T(8,128)S(1)}, f32[1584,128]{1,0:T(8,128)S(1)}, u32[]{:S(2)}, u32[]{:S(2)}) collective-permute-start(f32[1584,128]{1,0:T(8,128)S(1)} %get-tuple-element.42), channel_id=1, source_target_pairs={{0,31},{1,2},{2,1},{3,4},{4,3},{5,6},{6,5},{7,8},{8,7},{9,10},{10,... | collective-permute-start | bytes 2433032 | tf_op jit(solution)/shard_map/ppermute | solution.py:796
  29.2 36.4 %collective-permute-start.10 = (f32[6,192,128]{2,1,0:T(8,128)S(1)}, f32[6,192,128]{2,1,0:T(8,128)S(1)}, u32[]{:S(2)}, u32[]{:S(2)}) collective-permute-start(f32[6,192,128]{2,1,0:T(8,128)S(1)} %collective-permute-done.4), channel_id=1, source_target_pairs={{1,0},{2,3},{5,4},{6,7},{9,8},{10,11},{13,12},{14,15},{17,16},{18,... | collective-permute-start | bytes 1769480 | tf_op jit(solution)/shard_map/ppermute | solution.py:822
  48.2 1.3 collective-permute-start.5
  57.3 1.3 collective-permute-start.6
  58.7 6.9 %collective-permute-start.7 = (f32[3,48,128]{2,1,0:T(8,128)S(1)}, f32[3,48,128]{2,1,0:T(8,128)S(1)}, u32[]{:S(2)}, u32[]{:S(2)}) collective-permute-start(f32[3,48,128]{2,1,0:T(8,128)S(1)} %add.38.refs_4_.rest_0_), channel_id=1, source_target_pairs={{0,32},{1,33},{2,34},{3,35},{4,36},{5,37},{6,38},{7,39},{8,40},{9,... | collective-permute-start | bytes 221192 | tf_op jit(solution)/shard_map/ppermute | solution.py:789
  67.8 9.7 %collective-permute-start.11 = (f32[16,256,128]{2,1,0:T(8,128)S(1)}, f32[16,256,128]{2,1,0:T(8,128)S(1)}, u32[]{:S(2)}, u32[]{:S(2)}) collective-permute-start(f32[16,256,128]{2,1,0:T(8,128)S(1)} %get-tuple-element.57.s_ref), channel_id=1, source_target_pairs={{0,64},{1,65},{2,66},{3,67},{4,68},{5,69},{6,70},{7,71},{8,72},{9,... | collective-permute-start | bytes 6291464 | tf_op jit(solution)/shard_map/ppermute | solution.py:789
  67.9 21.0 %collective-permute-start.12 = (f32[1632,128]{1,0:T(8,128)S(1)}, f32[1632,128]{1,0:T(8,128)S(1)}, u32[]{:S(2)}, u32[]{:S(2)}) collective-permute-start(f32[1632,128]{1,0:T(8,128)S(1)} %get-tuple-element.58), channel_id=1, source_target_pairs={{0,1},{1,0},{2,3},{3,2},{4,5},{5,4},{6,7},{7,6},{8,9},{9,8},{10,11... | collective-permute-start | bytes 2506760 | tf_op jit(solution)/shard_map/ppermute | solution.py:796
  68.0 27.1 %collective-permute-start.13 = (f32[1632,128]{1,0:T(8,128)S(1)}, f32[1632,128]{1,0:T(8,128)S(1)}, u32[]{:S(2)}, u32[]{:S(2)}) collective-permute-start(f32[1632,128]{1,0:T(8,128)S(1)} %get-tuple-element.59), channel_id=1, source_target_pairs={{0,31},{1,2},{2,1},{3,4},{4,3},{5,6},{6,5},{7,8},{8,7},{9,10},{10,... | collective-permute-start | bytes 2506760 | tf_op jit(solution)/shard_map/ppermute | solution.py:796
  76.1 4.5 %collective-permute-start.8 = (f32[16,64,128]{2,1,0:T(8,128)S(1)}, f32[16,64,128]{2,1,0:T(8,128)S(1)}, u32[]{:S(2)}, u32[]{:S(2)}) collective-permute-start(f32[16,64,128]{2,1,0:T(8,128)S(1)} %get-tuple-element.52), channel_id=1, source_target_pairs={{1,33},{2,34},{5,37},{6,38},{9,41},{10,42},{13,45},{14,46},{17,49}... | collective-permute-start | bytes 1572872 | tf_op jit(solution)/shard_map/ppermute | solution.py:837
  99.5 1.3 collective-permute-start.14
  100.8 3.9 %collective-permute-start.15 = (f32[64,128]{1,0:T(8,128)S(1)}, f32[64,128]{1,0:T(8,128)S(1)}, u32[]{:S(2)}, u32[]{:S(2)}) collective-permute-start(f32[64,128]{1,0:T(8,128)S(1)} %add.39), channel_id=1, source_target_pairs={{0,32},{1,33},{2,34},{3,35},{4,36},{5,37},{6,38},{7,39},{8,40},{9,... | collective-permute-start | bytes 98312 | tf_op jit(solution)/shard_map/ppermute | solution.py:846
  104.7 5.1 %collective-permute-start.16 = (f32[64,128]{1,0:T(8,128)S(1)}, f32[64,128]{1,0:T(8,128)S(1)}, u32[]{:S(2)}, u32[]{:S(2)}) collective-permute-start(f32[64,128]{1,0:T(8,128)S(1)} %add.40), channel_id=1, source_target_pairs={{0,36},{1,37},{2,38},{3,39},{4,32},{5,33},{6,34},{7,35},{8,44},{9,... | collective-permute-start | bytes 98312 | tf_op jit(solution)/shard_map/ppermute | solution.py:846
  109.8 3.9 %collective-permute-start.17 = (f32[64,128]{1,0:T(8,128)S(1)}, f32[64,128]{1,0:T(8,128)S(1)}, u32[]{:S(2)}, u32[]{:S(2)}) collective-permute-start(f32[64,128]{1,0:T(8,128)S(1)} %add.41), channel_id=1, source_target_pairs={{0,1},{1,0},{2,3},{3,2},{4,5},{5,4},{6,7},{7,6},{8,9},{9,8},{10,11... | collective-permute-start | bytes 98312 | tf_op jit(solution)/shard_map/ppermute | solution.py:846
  113.8 5.1 %collective-permute-start.18 = (f32[64,128]{1,0:T(8,128)S(1)}, f32[64,128]{1,0:T(8,128)S(1)}, u32[]{:S(2)}, u32[]{:S(2)}) collective-permute-start(f32[64,128]{1,0:T(8,128)S(1)} %add.42), channel_id=1, source_target_pairs={{0,3},{1,2},{2,1},{3,0},{4,7},{5,6},{6,5},{7,4},{8,11},{9,10},{10,... | collective-permute-start | bytes 98312 | tf_op jit(solution)/shard_map/ppermute | solution.py:846
  118.9 3.9 %collective-permute-start.19 = (f32[64,128]{1,0:T(8,128)S(1)}, f32[64,128]{1,0:T(8,128)S(1)}, u32[]{:S(2)}, u32[]{:S(2)}) collective-permute-start(f32[64,128]{1,0:T(8,128)S(1)} %add.43), channel_id=1, source_target_pairs={{0,8},{1,9},{2,10},{3,11},{4,12},{5,13},{6,14},{7,15},{8,0},{9,1},... | collective-permute-start | bytes 98312 | tf_op jit(solution)/shard_map/ppermute | solution.py:846
  122.8 5.1 %collective-permute-start.20 = (f32[64,128]{1,0:T(8,128)S(1)}, f32[64,128]{1,0:T(8,128)S(1)}, u32[]{:S(2)}, u32[]{:S(2)}) collective-permute-start(f32[64,128]{1,0:T(8,128)S(1)} %add.44), channel_id=1, source_target_pairs={{0,24},{1,25},{2,26},{3,27},{4,28},{5,29},{6,30},{7,31},{8,16},{9,... | collective-permute-start | bytes 98312 | tf_op jit(solution)/shard_map/ppermute | solution.py:846
  127.9 1.2 collective-permute-start.21

commit v19 on v18

--- a/solution.py
+++ b/solution.py
@@ -71,7 +71,7 @@
     return total
 
 
-B = 4
+B = 8
 STEPS = C // B
 N = 2
 MIDDLE = 10
@@ -152,16 +152,10 @@
         body(two, one)
 
 
-def pack_kernel(s_ref, inner_ref, odd_ref, own_ref, other_ref, message_ref, relay_ref, mid_ref, one_ref, two_ref):
+def pack_kernel(s_ref, inner_ref, message_ref, relay_ref, mid_ref):
     step = pl.program_id(0)
     inner = inner_ref[0] == 1
     mid_ref[...] = s_ref[:, 96:160, :]
-
-    @pl.when(step == 0)
-    def _():
-        for ref in (one_ref, two_ref):
-            ref[HALO_ROWS : HALO_ROWS + ATOM_ROWS, :] = own_ref[:ATOM_ROWS, :]
-            ref[HALO_ROWS + ATOM_ROWS :, :] = other_ref[:ATOM_ROWS, :]
 
     @pl.when(step >= MIDDLE // N)
     def _():
@@ -180,27 +174,50 @@
             row = pl.multiple_of(MID_START + (step * N + p) * MID, MID)
             message_ref[pl.ds(row, MID), :] = s_ref[p, 96:160, :]
 
+
+def pack(s, inner):
+    return pl.pallas_call(
+        pack_kernel,
+        grid=(C // N,),
+        in_specs=[plane_spec(ROWS, N), SCALARS],
+        out_specs=[whole(C * EDGE), edge_spec(MIDDLE), plane_spec(MID, N)],
+        out_shape=[DIRECT, RELAY, sds((C, MID, S))],
+        compiler_params=params(12),
+        cost_estimate=cost(1 << 31, 6 << 20),
+        name="pack",
+    )(s, inner)
+
+
+def pack_halos_kernel(s_ref, odd_ref, own_ref, other_ref, one_ref, two_ref):
+    step = pl.program_id(0)
+
+    @pl.when(step == 0)
+    def _():
+        for ref in (one_ref, two_ref):
+            ref[HALO_ROWS : HALO_ROWS + ATOM_ROWS, :] = own_ref[:ATOM_ROWS, :]
+            ref[HALO_ROWS + ATOM_ROWS :, :] = other_ref[:ATOM_ROWS, :]
+
     def halos(head_ref, tail_ref):
-        for p in range(N):
+        for p in range(B):
             for z in range(H):
-                rows = halo_rows(step * N + p, z)
+                rows = halo_rows(step * B + p, z)
                 head_ref[rows, :] = s_ref[p, stride_rows(z), :]
                 tail_ref[rows, :] = s_ref[p, stride_rows(C - H + z), :]
 
     by_side(odd_ref, halos, one_ref, two_ref)
 
 
-def pack(s, inner, odd, parcel, parcel_mate):
-    return pl.pallas_call(
-        pack_kernel,
-        grid=(C // N,),
-        in_specs=[plane_spec(ROWS, N), SCALARS, SCALARS, whole(56), whole(56)],
-        out_specs=[whole(C * EDGE), edge_spec(MIDDLE), plane_spec(MID, N)] + [whole(HALO.shape[0])] * 2,
-        out_shape=[DIRECT, RELAY, sds((C, MID, S)), HALO, HALO],
+def pack_halos(s, odd, parcel, parcel_mate):
+    return pl.pallas_call(
+        pack_halos_kernel,
+        grid=(STEPS,),
+        in_specs=[plane_spec(), SCALARS, whole(56), whole(56)],
+        out_specs=[whole(HALO.shape[0])] * 2,
+        out_shape=[HALO, HALO],
         compiler_params=params(12),
-        cost_estimate=cost(1 << 31, 8 << 20),
-        name="pack",
-    )(s, inner, odd, parcel, parcel_mate)
+        cost_estimate=cost(1 << 20, 4 << 20),
+        name="pack_halos",
+    )(s, odd, parcel, parcel_mate)
 
 
 def stack_kernel(atoms_ref, pot_ref, out_ref):
@@ -686,6 +703,12 @@
     return jnp.dot(a, b, precision=lax.Precision.HIGHEST, preferred_element_type=F32)
 
 
+def close(a, b):
+    a_high, a_low = split(a)
+    b_high, b_low = split(b)
+    return mm(jnp.concatenate([a_high, a_low], axis=1), jnp.concatenate([b_high, b_high])) + mm(a_high, b_low)
+
+
 def inverse_factor(gram_ref, a_ref, x_ref, state_ref):
     row = lax.broadcasted_iota(jnp.int32, (S, S), 0)
     column = lax.broadcasted_iota(jnp.int32, (S, S), 1)
@@ -699,14 +722,14 @@
 
     def residual():
         x = x_ref[...]
-        return unit - exact(exact(x, a_ref[...]), x.T)
+        return unit - close(close(x, a_ref[...]), x.T)
 
     def size(e):
         return jnp.sum(e * e)
 
     def improve(e):
         lower = jnp.where(row > column, e, jnp.where(row == column, 0.5 * e, 0.0))
-        x_ref[...] += exact(lower, x_ref[...])
+        x_ref[...] += close(lower, x_ref[...])
 
     state_ref[0] = 0
     start = unit - a_ref[...]
@@ -810,8 +833,11 @@
     ).reshape(24, 128)
     pot, corner, upper, inner, odd, atoms = barrier((pot, corner, upper, inner, odd, atoms))
     parcel = stack(atoms, pot)
+    to_pack, parcel = barrier((s, parcel))
     parcel_mate = send(parcel, over_y)
-    message, relay, mid, halo_one, halo_two = pack(s, inner, odd, parcel, parcel_mate)
+    message, relay, mid = pack(to_pack, inner)
+    parcel_mate, message, relay = barrier((parcel_mate, message, relay))
+    halo_one, halo_two = pack_halos(s, odd, parcel, parcel_mate)
     message = send(message, over_y)
     relayed = lax.ppermute(relay, AXES, [(d, d ^ over_y ^ 1) for d in outer_ones])
     halos = to_pairs(halo_one, halo_two)

time: 147 us -> 145 us (0.986)
  starting transfers between devices: 32.6 us -> 29.9 us
    ppermute x6, starting transfers between devices: 5.45 us -> 3.01 us  [per_device(): own = own + lax.ppermute(own, AXES, [(d, d ^ flip) for d in range(count)])]
    ppermute x6, waiting for transfers between devices: 21.7 us -> 24.1 us  [per_device(): own = own + lax.ppermute(own, AXES, [(d, d ^ flip) for d in range(count)])]
where the time goes in v19:
time: 145 us; the launch traced here: 143 us
  waiting for transfers between devices  64.6 us (45%)
  Pallas kernels  43.1 us (30%)
  starting transfers between devices  29.9 us (21%)
  local copies, waits for them, and re-layouts  4.53 us (3%)
    ppermute x4, waiting for transfers between devices, to_pairs(): return (lax.ppermute(one, AXES, near), lax.ppermute(two, AXES, far))  24.5 us
    ppermute x6, waiting for transfers between devices, per_device(): own = own + lax.ppermute(own, AXES, [(d, d ^ flip) for d in range(count)])  24.1 us
    pallas_call x1, Pallas kernels, turn(): pl.pallas_call(turn_kernel, grid=(STEPS,), in_specs=[plane_spec(), whole(...  16.5 us
    ppermute x4, starting transfers between devices, to_pairs(): return (lax.ppermute(one, AXES, near), lax.ppermute(two, AXES, far))  16.4 us
    ppermute x9, waiting for transfers between devices, send(): return lax.ppermute(value, AXES, [(d, d ^ flip) for d in range(count)])  10.9 us
    pallas_call x1, Pallas kernels, prep(): pl.pallas_call(prep_kernel, in_specs=[vmem] * 2 + [pl.BlockSpec(memory_sp...  7.8 us
    ppermute x9, starting transfers between devices, send(): return lax.ppermute(value, AXES, [(d, d ^ flip) for d in range(count)])  5.5 us
    ppermute x1, waiting for transfers between devices, per_device(): lax.ppermute(relay, AXES, [(d, d ^ over_y ^ 1) for d in outer_ones])  5.14 us
  transfers between devices with their start and end apart: 22, of which 17 were waited for; matrix products, arithmetic and copies ran while one was open for 3% of the time, Pallas kernels for 14%

profile of v19, /device:TPU:0, one launch (start us, length us, event | category | flops | bytes accessed | tf_op | source)
XLA Modules:
  0.0 143.2 jit_solution(1765574161231592480)
XLA Ops:
  3.8 2.0 %collective-permute-start = (f32[56,128]{1,0:T(8,128)S(1)}, f32[56,128]{1,0:T(8,128)S(1)}, u32[]{:S(2)}, u32[]{:S(2)}) collective-permute-start(f32[56,128]{1,0:T(8,128)S(1)} %stack.13.own_ref.parcel_ref), channel_id=1, source_target_pairs={{0,32},{1,33},{2,34},{3,35},{4,36},{5,37},{6,38},{7,39},{8,40},{9,... | collective-permute-start | bytes 86024 | tf_op jit(solution)/shard_map/ppermute | solution.py:812
  5.8 1.6 %copy-done = f32[16,16,16,128]{3,2,1,0:T(8,128)S(1)} copy-done((f32[16,16,16,128]{3,2,1,0:T(8,128)S(1)}, f32[16,16,16,128]{3,2,1,0:T(8,128)}, u32[]{:S(2)}) %copy-start) | copy-done | bytes 2097176
  7.8 1.9 %collective-permute-start.9 = (f32[3072,128]{1,0:T(8,128)S(1)}, f32[3072,128]{1,0:T(8,128)S(1)}, u32[]{:S(2)}, u32[]{:S(2)}) collective-permute-start(f32[3072,128]{1,0:T(8,128)S(1)} %get-tuple-element.64), channel_id=1, source_target_pairs={{0,32},{1,33},{2,34},{3,35},{4,36},{5,37},{6,38},{7,39},{8,40},{9,... | collective-permute-start | bytes 4718600 | tf_op jit(solution)/shard_map/ppermute | solution.py:812
  9.7 3.0 %collective-permute-start.4 = (f32[6,192,128]{2,1,0:T(8,128)S(1)}, f32[6,192,128]{2,1,0:T(8,128)S(1)}, u32[]{:S(2)}, u32[]{:S(2)}) collective-permute-start(f32[6,192,128]{2,1,0:T(8,128)S(1)} %get-tuple-element.53), channel_id=1, source_target_pairs={{0,33},{3,34},{4,37},{7,38},{8,41},{11,42},{12,45},{15,46},{16,49}... | collective-permute-start | bytes 1769480 | tf_op jit(solution)/shard_map/ppermute | solution.py:842
  13.4 7.9 %collective-permute-start.2 = (f32[1584,128]{1,0:T(8,128)S(1)}, f32[1584,128]{1,0:T(8,128)S(1)}, u32[]{:S(2)}, u32[]{:S(2)}) collective-permute-start(f32[1584,128]{1,0:T(8,128)S(1)} %get-tuple-element.52), channel_id=1, source_target_pairs={{0,31},{1,2},{2,1},{3,4},{4,3},{5,6},{6,5},{7,8},{8,7},{9,10},{10,... | collective-permute-start | bytes 2433032 | tf_op jit(solution)/shard_map/ppermute | solution.py:819
  21.3 5.1 %collective-permute-done.4 = f32[6,192,128]{2,1,0:T(8,128)S(1)} collective-permute-done((f32[6,192,128]{2,1,0:T(8,128)S(1)}, f32[6,192,128]{2,1,0:T(8,128)S(1)}, u32[]{:S(2)}, u32[]{:S(2)}) %collective-permute-start.4) | collective-permute-done | bytes 589856 | tf_op jit(solution)/shard_map/ppermute | solution.py:842
  26.4 1.3 collective-permute-start.10
  28.5 1.5 %side_x.1.part_ref = f32[16,256,128]{2,1,0:T(8,128)S(1)} custom-call(f32[16,256,128]{2,1,0:T(8,128)S(1)} %bitcast.16, f32[16,256,128]{2,1,0:T(8,128)S(1)} %collective-permute-done.3.mate_ref), custom_call_target="tpu_custom_call" | custom-call | flops 16777216 | bytes 6291456 | tf_op jit(solution)/shard_map/side_x/pallas_call | solution.py:277
  30.0 12.8 %collective-permute-done.1.one_ref = f32[1584,128]{1,0:T(8,128)S(1)} collective-permute-done((f32[1584,128]{1,0:T(8,128)S(1)}, f32[1584,128]{1,0:T(8,128)S(1)}, u32[]{:S(2)}, u32[]{:S(2)}) %collective-permute-start.1) | collective-permute-done | bytes 811040 | tf_op jit(solution)/shard_map/ppermute | solution.py:819
  42.8 2.9 %side_z.1.side_ref = f32[16,256,128]{2,1,0:T(8,128)S(1)} custom-call(f32[16,256,128]{2,1,0:T(8,128)S(1)} %bitcast.17, f32[16,256,128]{2,1,0:T(8,128)S(1)} %side_x.1.part_ref, f32[1584,128]{1,0:T(8,128)S(1)} %collective-permute-done.1.one_ref, f32[1584,128]{1,0:T(8,128)S(1)} %collective-permute-done.2.two_ref, s32[1]{0:T(128)} %bitcast.5.odd_ref.refs_3_.rest_4_), custom_call_target="tpu_custom_call" | custom-call | flops 16777216 | bytes 8388608 | tf_op jit(solution)/shard_map/side_z/pallas_call | solution.py:305
  45.8 1.3 collective-permute-done.5.refs_1_
  47.1 7.8 %prep.1 = (bf16[2,4096,128]{2,1,0:T(8,128)(2,1)S(1)}, f32[3,48,128]{2,1,0:T(8,128)S(1)}, f32[48,128]{1,0:T(8,128)S(1)}) custom-call(f32[144,128]{1,0:T(8,128)S(1)} %column.1.refs_0_, f32[144,128]{1,0:T(8,128)S(1)} %collective-permute-done.5.refs_1_, s32[2]{0:T(128)S(1)} %pad_add_fusion.refs_2_, f32[4096,128]{1,0:T(8,128)S(1)} %spread.2.refs_3_, ...), custom_call_target="tpu_custom_call" | custom-call | flops 134217728 | bytes 10485760 | tf_op jit(solution)/shard_map/prep/pallas_call | solution.py:493
  55.1 1.1 collective-permute-done.6
  56.2 1.1 collective-permute-start.7
  57.3 5.2 %collective-permute-done.9.refs_3_ = f32[3072,128]{1,0:T(8,128)S(1)} collective-permute-done((f32[3072,128]{1,0:T(8,128)S(1)}, f32[3072,128]{1,0:T(8,128)S(1)}, u32[]{:S(2)}, u32[]{:S(2)}) %collective-permute-start.9) | collective-permute-done | bytes 1572896 | tf_op jit(solution)/shard_map/ppermute | solution.py:812
  63.3 2.2 %first.1 = (f32[16,256,128]{2,1,0:T(8,128)S(1)}, f32[16,256,128]{2,1,0:T(8,128)S(1)}, f32[1632,128]{1,0:T(8,128)S(1)}, f32[1632,128]{1,0:T(8,128)S(1)}) custom-call(f32[16,256,128]{2,1,0:T(8,128)S(1)} %bitcast.19, f32[16,256,128]{2,1,0:T(8,128)S(1)} %side_z.1.side_ref, f32[16,256,128]{2,1,0:T(8,128)S(1)} %bitcast.21, f32[16,192,128]{2,1,0:T(8,128)S(1)} %bitcast.23, ...), custom_call_target="tpu_custom_call" | custom-call | flops 16777216 | bytes 14680064 | tf_op jit(solution)/shard_map/first/pallas_call | solution.py:560
  65.8 8.3 %collective-permute-start.13 = (f32[1632,128]{1,0:T(8,128)S(1)}, f32[1632,128]{1,0:T(8,128)S(1)}, u32[]{:S(2)}, u32[]{:S(2)}) collective-permute-start(f32[1632,128]{1,0:T(8,128)S(1)} %get-tuple-element.69), channel_id=1, source_target_pairs={{0,31},{1,2},{2,1},{3,4},{4,3},{5,6},{6,5},{7,8},{8,7},{9,10},{10,... | collective-permute-start | bytes 2506760 | tf_op jit(solution)/shard_map/ppermute | solution.py:819
  75.6 2.9 %side_again.1.part_ref = f32[16,256,128]{2,1,0:T(8,128)S(1)} custom-call(f32[16,256,128]{2,1,0:T(8,128)S(1)} %get-tuple-element.67.s_ref, f32[16,256,128]{2,1,0:T(8,128)S(1)} %collective-permute-done.11.mate_ref), custom_call_target="tpu_custom_call" | custom-call | flops 33554432 | bytes 6291456 | tf_op jit(solution)/shard_map/side_again/pallas_call | solution.py:333
  78.5 2.9 %base.1.base_ref = f32[16,256,128]{2,1,0:T(8,128)S(1)} custom-call(f32[16,256,128]{2,1,0:T(8,128)S(1)} %bitcast.20, f32[16,64,128]{2,1,0:T(8,128)S(1)} %collective-permute-done.8.mid_ref, f32[16,256,128]{2,1,0:T(8,128)S(1)} %bitcast.22, f32[16,256,128]{2,1,0:T(8,128)S(1)} %bitcast.27, f32[16,256,128]{2,1,0:T(8,128)S(1)} %get-tuple-element.66.q_ref, ...), custom_call_target="tpu_custom_call" | custom-call | flops 33554432 | bytes 16777216 | tf_op jit(solution)/shard_map/base/pallas_call | solution.py:612
  81.5 5.2 %collective-permute-done.12.one_ref = f32[1632,128]{1,0:T(8,128)S(1)} collective-permute-done((f32[1632,128]{1,0:T(8,128)S(1)}, f32[1632,128]{1,0:T(8,128)S(1)}, u32[]{:S(2)}, u32[]{:S(2)}) %collective-permute-start.12) | collective-permute-done | bytes 835616 | tf_op jit(solution)/shard_map/ppermute | solution.py:819
  86.7 6.5 %collective-permute-done.13.two_ref = f32[1632,128]{1,0:T(8,128)S(1)} collective-permute-done((f32[1632,128]{1,0:T(8,128)S(1)}, f32[1632,128]{1,0:T(8,128)S(1)}, u32[]{:S(2)}, u32[]{:S(2)}) %collective-permute-start.13) | collective-permute-done | bytes 835616 | tf_op jit(solution)/shard_map/ppermute | solution.py:819
  93.2 3.9 %second.1 = (f32[16,256,128]{2,1,0:T(8,128)S(1)}, f32[64,128]{1,0:T(8,128)S(1)}, f32[64,128]{1,0:T(8,128)S(1)}) custom-call(f32[16,256,128]{2,1,0:T(8,128)S(1)} %base.1.base_ref, f32[1632,128]{1,0:T(8,128)S(1)} %collective-permute-done.12.one_ref, f32[1632,128]{1,0:T(8,128)S(1)} %collective-permute-done.13.two_ref, bf16[2,16,256,128]{3,2,1,0:T(8,128)(2,1)S(1)} %bitcast.25, ...), custom_call_target="tpu_custom_call" | custom-call | flops 134217728 | bytes 8388608 | tf_op jit(solution)/shard_map/second/pallas_call | solution.py:687
  97.2 1.2 collective-permute-done.14
  98.8 3.5 %collective-permute-done.15 = f32[64,128]{1,0:T(8,128)S(1)} collective-permute-done((f32[64,128]{1,0:T(8,128)S(1)}, f32[64,128]{1,0:T(8,128)S(1)}, u32[]{:S(2)}, u32[]{:S(2)}) %collective-permute-start.15) | collective-permute-done | bytes 32800 | tf_op jit(solution)/shard_map/ppermute | solution.py:872
  102.5 4.9 %collective-permute-done.16 = f32[64,128]{1,0:T(8,128)S(1)} collective-permute-done((f32[64,128]{1,0:T(8,128)S(1)}, f32[64,128]{1,0:T(8,128)S(1)}, u32[]{:S(2)}, u32[]{:S(2)}) %collective-permute-start.16) | collective-permute-done | bytes 32800 | tf_op jit(solution)/shard_map/ppermute | solution.py:872
  107.4 3.9 %collective-permute-done.17 = f32[64,128]{1,0:T(8,128)S(1)} collective-permute-done((f32[64,128]{1,0:T(8,128)S(1)}, f32[64,128]{1,0:T(8,128)S(1)}, u32[]{:S(2)}, u32[]{:S(2)}) %collective-permute-start.17) | collective-permute-done | bytes 32800 | tf_op jit(solution)/shard_map/ppermute | solution.py:872
  112.0 4.4 %collective-permute-done.18 = f32[64,128]{1,0:T(8,128)S(1)} collective-permute-done((f32[64,128]{1,0:T(8,128)S(1)}, f32[64,128]{1,0:T(8,128)S(1)}, u32[]{:S(2)}, u32[]{:S(2)}) %collective-permute-start.18) | collective-permute-done | bytes 32800 | tf_op jit(solution)/shard_map/ppermute | solution.py:872
  116.5 3.9 %collective-permute-done.19 = f32[64,128]{1,0:T(8,128)S(1)} collective-permute-done((f32[64,128]{1,0:T(8,128)S(1)}, f32[64,128]{1,0:T(8,128)S(1)}, u32[]{:S(2)}, u32[]{:S(2)}) %collective-permute-start.19) | collective-permute-done | bytes 32800 | tf_op jit(solution)/shard_map/ppermute | solution.py:872
  120.4 1.7 %collective-permute-start.20 = (f32[64,128]{1,0:T(8,128)S(1)}, f32[64,128]{1,0:T(8,128)S(1)}, u32[]{:S(2)}, u32[]{:S(2)}) collective-permute-start(f32[64,128]{1,0:T(8,128)S(1)} %add.44), channel_id=1, source_target_pairs={{0,24},{1,25},{2,26},{3,27},{4,28},{5,29},{6,30},{7,31},{8,16},{9,... | collective-permute-start | bytes 98312 | tf_op jit(solution)/shard_map/ppermute | solution.py:872
  122.1 3.5 %collective-permute-done.20 = f32[64,128]{1,0:T(8,128)S(1)} collective-permute-done((f32[64,128]{1,0:T(8,128)S(1)}, f32[64,128]{1,0:T(8,128)S(1)}, u32[]{:S(2)}, u32[]{:S(2)}) %collective-permute-start.20) | collective-permute-done | bytes 32800 | tf_op jit(solution)/shard_map/ppermute | solution.py:872
  125.5 1.2 collective-permute-done.21.other_ref
  126.7 16.5 %turn.1 = f32[16,256,128]{2,1,0:T(8,128)} custom-call(f32[16,256,128]{2,1,0:T(8,128)S(1)} %get-tuple-element.74.second_ref, f32[64,128]{1,0:T(8,128)S(1)} %add.45.own_ref, f32[64,128]{1,0:T(8,128)S(1)} %collective-permute-done.21.other_ref, s32[1]{0:T(128)} %bitcast.3.rest_3_.upper_ref), custom_call_target="tpu_custom_call" | custom-call | flops 268435456 | bytes 4194304 | tf_op jit(solution)/shard_map/turn/pallas_call | solution.py:792
  (48 shorter events, 10.0 us)
Async XLA Ops:
  0.0 26.4 %collective-permute-start.3 = (f32[16,256,128]{2,1,0:T(8,128)}, f32[16,256,128]{2,1,0:T(8,128)S(1)}, u32[]{:S(2)}, u32[]{:S(2)}) collective-permute-start(f32[16,256,128]{2,1,0:T(8,128)} %bitcast.13), channel_id=1, source_target_pairs={{0,64},{1,65},{2,66},{3,67},{4,68},{5,69},{6,70},{7,71},{8,72},{9,... | collective-permute-start | bytes 6291464 | tf_op jit(solution)/shard_map/ppermute | solution.py:812
  3.8 4.0 %collective-permute-start = (f32[56,128]{1,0:T(8,128)S(1)}, f32[56,128]{1,0:T(8,128)S(1)}, u32[]{:S(2)}, u32[]{:S(2)}) collective-permute-start(f32[56,128]{1,0:T(8,128)S(1)} %stack.13.own_ref.parcel_ref), channel_id=1, source_target_pairs={{0,32},{1,33},{2,34},{3,35},{4,36},{5,37},{6,38},{7,39},{8,40},{9,... | collective-permute-start | bytes 86024 | tf_op jit(solution)/shard_map/ppermute | solution.py:812
  5.8 1.6 %copy-start = (f32[16,16,16,128]{3,2,1,0:T(8,128)S(1)}, f32[16,16,16,128]{3,2,1,0:T(8,128)}, u32[]{:S(2)}) copy-start(f32[16,16,16,128]{3,2,1,0:T(8,128)} %param.5) | copy-start | bytes 6291460
  7.8 54.6 %collective-permute-start.9 = (f32[3072,128]{1,0:T(8,128)S(1)}, f32[3072,128]{1,0:T(8,128)S(1)}, u32[]{:S(2)}, u32[]{:S(2)}) collective-permute-start(f32[3072,128]{1,0:T(8,128)S(1)} %get-tuple-element.64), channel_id=1, source_target_pairs={{0,32},{1,33},{2,34},{3,35},{4,36},{5,37},{6,38},{7,39},{8,40},{9,... | collective-permute-start | bytes 4718600 | tf_op jit(solution)/shard_map/ppermute | solution.py:812
  9.7 16.7 %collective-permute-start.4 = (f32[6,192,128]{2,1,0:T(8,128)S(1)}, f32[6,192,128]{2,1,0:T(8,128)S(1)}, u32[]{:S(2)}, u32[]{:S(2)}) collective-permute-start(f32[6,192,128]{2,1,0:T(8,128)S(1)} %get-tuple-element.53), channel_id=1, source_target_pairs={{0,33},{3,34},{4,37},{7,38},{8,41},{11,42},{12,45},{15,46},{16,49}... | collective-permute-start | bytes 1769480 | tf_op jit(solution)/shard_map/ppermute | solution.py:842
  13.3 29.5 %collective-permute-start.1 = (f32[1584,128]{1,0:T(8,128)S(1)}, f32[1584,128]{1,0:T(8,128)S(1)}, u32[]{:S(2)}, u32[]{:S(2)}) collective-permute-start(f32[1584,128]{1,0:T(8,128)S(1)} %get-tuple-element.51), channel_id=1, source_target_pairs={{0,1},{1,0},{2,3},{3,2},{4,5},{5,4},{6,7},{7,6},{8,9},{9,8},{10,11... | collective-permute-start | bytes 2433032 | tf_op jit(solution)/shard_map/ppermute | solution.py:819
  13.4 29.4 %collective-permute-start.2 = (f32[1584,128]{1,0:T(8,128)S(1)}, f32[1584,128]{1,0:T(8,128)S(1)}, u32[]{:S(2)}, u32[]{:S(2)}) collective-permute-start(f32[1584,128]{1,0:T(8,128)S(1)} %get-tuple-element.52), channel_id=1, source_target_pairs={{0,31},{1,2},{2,1},{3,4},{4,3},{5,6},{6,5},{7,8},{8,7},{9,10},{10,... | collective-permute-start | bytes 2433032 | tf_op jit(solution)/shard_map/ppermute | solution.py:819
  26.4 36.9 %collective-permute-start.10 = (f32[6,192,128]{2,1,0:T(8,128)S(1)}, f32[6,192,128]{2,1,0:T(8,128)S(1)}, u32[]{:S(2)}, u32[]{:S(2)}) collective-permute-start(f32[6,192,128]{2,1,0:T(8,128)S(1)} %collective-permute-done.4), channel_id=1, source_target_pairs={{1,0},{2,3},{5,4},{6,7},{9,8},{10,11},{13,12},{14,15},{17,16},{18,... | collective-permute-start | bytes 1769480 | tf_op jit(solution)/shard_map/ppermute | solution.py:848
  28.5 14.3 %copy-start.1 = (f32[16,16,16,128]{3,2,1,0:T(8,128)S(1)}, f32[16,16,16,128]{3,2,1,0:T(8,128)}, u32[]{:S(2)}) copy-start(f32[16,16,16,128]{3,2,1,0:T(8,128)} %param.5) | copy-start | bytes 6291460
  45.7 1.3 collective-permute-start.5
  54.9 1.3 collective-permute-start.6
  56.2 7.1 %collective-permute-start.7 = (f32[3,48,128]{2,1,0:T(8,128)S(1)}, f32[3,48,128]{2,1,0:T(8,128)S(1)}, u32[]{:S(2)}, u32[]{:S(2)}) collective-permute-start(f32[3,48,128]{2,1,0:T(8,128)S(1)} %add.38.refs_4_.rest_0_), channel_id=1, source_target_pairs={{0,32},{1,33},{2,34},{3,35},{4,36},{5,37},{6,38},{7,39},{8,40},{9,... | collective-permute-start | bytes 221192 | tf_op jit(solution)/shard_map/ppermute | solution.py:812
  65.6 10.0 %collective-permute-start.11 = (f32[16,256,128]{2,1,0:T(8,128)S(1)}, f32[16,256,128]{2,1,0:T(8,128)S(1)}, u32[]{:S(2)}, u32[]{:S(2)}) collective-permute-start(f32[16,256,128]{2,1,0:T(8,128)S(1)} %get-tuple-element.67.s_ref), channel_id=1, source_target_pairs={{0,64},{1,65},{2,66},{3,67},{4,68},{5,69},{6,70},{7,71},{8,72},{9,... | collective-permute-start | bytes 6291464 | tf_op jit(solution)/shard_map/ppermute | solution.py:812
  65.7 21.0 %collective-permute-start.12 = (f32[1632,128]{1,0:T(8,128)S(1)}, f32[1632,128]{1,0:T(8,128)S(1)}, u32[]{:S(2)}, u32[]{:S(2)}) collective-permute-start(f32[1632,128]{1,0:T(8,128)S(1)} %get-tuple-element.68), channel_id=1, source_target_pairs={{0,1},{1,0},{2,3},{3,2},{4,5},{5,4},{6,7},{7,6},{8,9},{9,8},{10,11... | collective-permute-start | bytes 2506760 | tf_op jit(solution)/shard_map/ppermute | solution.py:819
  65.8 27.4 %collective-permute-start.13 = (f32[1632,128]{1,0:T(8,128)S(1)}, f32[1632,128]{1,0:T(8,128)S(1)}, u32[]{:S(2)}, u32[]{:S(2)}) collective-permute-start(f32[1632,128]{1,0:T(8,128)S(1)} %get-tuple-element.69), channel_id=1, source_target_pairs={{0,31},{1,2},{2,1},{3,4},{4,3},{5,6},{6,5},{7,8},{8,7},{9,10},{10,... | collective-permute-start | bytes 2506760 | tf_op jit(solution)/shard_map/ppermute | solution.py:819
  74.1 4.5 %collective-permute-start.8 = (f32[16,64,128]{2,1,0:T(8,128)S(1)}, f32[16,64,128]{2,1,0:T(8,128)S(1)}, u32[]{:S(2)}, u32[]{:S(2)}) collective-permute-start(f32[16,64,128]{2,1,0:T(8,128)S(1)} %get-tuple-element.62), channel_id=1, source_target_pairs={{1,33},{2,34},{5,37},{6,38},{9,41},{10,42},{13,45},{14,46},{17,49}... | collective-permute-start | bytes 1572872 | tf_op jit(solution)/shard_map/ppermute | solution.py:863
  97.1 1.3 collective-permute-start.14
  98.4 3.9 %collective-permute-start.15 = (f32[64,128]{1,0:T(8,128)S(1)}, f32[64,128]{1,0:T(8,128)S(1)}, u32[]{:S(2)}, u32[]{:S(2)}) collective-permute-start(f32[64,128]{1,0:T(8,128)S(1)} %add.39), channel_id=1, source_target_pairs={{0,32},{1,33},{2,34},{3,35},{4,36},{5,37},{6,38},{7,39},{8,40},{9,... | collective-permute-start | bytes 98312 | tf_op jit(solution)/shard_map/ppermute | solution.py:872
  102.3 5.1 %collective-permute-start.16 = (f32[64,128]{1,0:T(8,128)S(1)}, f32[64,128]{1,0:T(8,128)S(1)}, u32[]{:S(2)}, u32[]{:S(2)}) collective-permute-start(f32[64,128]{1,0:T(8,128)S(1)} %add.40), channel_id=1, source_target_pairs={{0,36},{1,37},{2,38},{3,39},{4,32},{5,33},{6,34},{7,35},{8,44},{9,... | collective-permute-start | bytes 98312 | tf_op jit(solution)/shard_map/ppermute | solution.py:872
  107.4 3.9 %collective-permute-start.17 = (f32[64,128]{1,0:T(8,128)S(1)}, f32[64,128]{1,0:T(8,128)S(1)}, u32[]{:S(2)}, u32[]{:S(2)}) collective-permute-start(f32[64,128]{1,0:T(8,128)S(1)} %add.41), channel_id=1, source_target_pairs={{0,1},{1,0},{2,3},{3,2},{4,5},{5,4},{6,7},{7,6},{8,9},{9,8},{10,11... | collective-permute-start | bytes 98312 | tf_op jit(solution)/shard_map/ppermute | solution.py:872
  111.3 5.1 %collective-permute-start.18 = (f32[64,128]{1,0:T(8,128)S(1)}, f32[64,128]{1,0:T(8,128)S(1)}, u32[]{:S(2)}, u32[]{:S(2)}) collective-permute-start(f32[64,128]{1,0:T(8,128)S(1)} %add.42), channel_id=1, source_target_pairs={{0,3},{1,2},{2,1},{3,0},{4,7},{5,6},{6,5},{7,4},{8,11},{9,10},{10,... | collective-permute-start | bytes 98312 | tf_op jit(solution)/shard_map/ppermute | solution.py:872
  116.5 3.9 %collective-permute-start.19 = (f32[64,128]{1,0:T(8,128)S(1)}, f32[64,128]{1,0:T(8,128)S(1)}, u32[]{:S(2)}, u32[]{:S(2)}) collective-permute-start(f32[64,128]{1,0:T(8,128)S(1)} %add.43), channel_id=1, source_target_pairs={{0,8},{1,9},{2,10},{3,11},{4,12},{5,13},{6,14},{7,15},{8,0},{9,1},... | collective-permute-start | bytes 98312 | tf_op jit(solution)/shard_map/ppermute | solution.py:872
  120.4 5.1 %collective-permute-start.20 = (f32[64,128]{1,0:T(8,128)S(1)}, f32[64,128]{1,0:T(8,128)S(1)}, u32[]{:S(2)}, u32[]{:S(2)}) collective-permute-start(f32[64,128]{1,0:T(8,128)S(1)} %add.44), channel_id=1, source_target_pairs={{0,24},{1,25},{2,26},{3,27},{4,28},{5,29},{6,30},{7,31},{8,16},{9,... | collective-permute-start | bytes 98312 | tf_op jit(solution)/shard_map/ppermute | solution.py:872
  125.5 1.2 collective-permute-start.21

commit v20 on v19

--- a/solution.py
+++ b/solution.py
@@ -188,14 +188,19 @@
     )(s, inner)
 
 
+def atom_rows(out_ref, start, atoms_ref):
+    for block in range(6):
+        out_ref[start + block * 4 : start + block * 4 + 4, :] = atoms_ref[:, block * 128 : block * 128 + 128]
+
+
 def pack_halos_kernel(s_ref, odd_ref, own_ref, other_ref, one_ref, two_ref):
     step = pl.program_id(0)
 
     @pl.when(step == 0)
     def _():
         for ref in (one_ref, two_ref):
-            ref[HALO_ROWS : HALO_ROWS + ATOM_ROWS, :] = own_ref[:ATOM_ROWS, :]
-            ref[HALO_ROWS + ATOM_ROWS :, :] = other_ref[:ATOM_ROWS, :]
+            atom_rows(ref, HALO_ROWS, own_ref)
+            atom_rows(ref, HALO_ROWS + ATOM_ROWS, other_ref)
 
     def halos(head_ref, tail_ref):
         for p in range(B):
@@ -207,26 +212,17 @@
     by_side(odd_ref, halos, one_ref, two_ref)
 
 
-def pack_halos(s, odd, parcel, parcel_mate):
+def pack_halos(s, odd, own, other):
     return pl.pallas_call(
         pack_halos_kernel,
         grid=(STEPS,),
-        in_specs=[plane_spec(), SCALARS, whole(56), whole(56)],
+        in_specs=[plane_spec(), SCALARS] + [pl.BlockSpec((4, 768), lambda i: (0, 0))] * 2,
         out_specs=[whole(HALO.shape[0])] * 2,
         out_shape=[HALO, HALO],
         compiler_params=params(12),
         cost_estimate=cost(1 << 20, 4 << 20),
         name="pack_halos",
-    )(s, odd, parcel, parcel_mate)
-
-
-def stack_kernel(atoms_ref, pot_ref, out_ref):
-    out_ref[0:24, :] = atoms_ref[...]
-    out_ref[24:56, :] = pot_ref[...]
-
-
-def stack(atoms, pot):
-    return pl.pallas_call(stack_kernel, out_shape=sds((56, S)), compiler_params=params(4), name="stack")(atoms, pot)
+    )(s, odd, own, other)
 
 
 def column_kernel(own_ref, other_ref, one_ref, two_ref, odd_ref, out_ref):
@@ -235,8 +231,8 @@
         out_ref[96:144, :] = above_ref[HALO_ROWS:, :]
 
     by_side(odd_ref, beside, one_ref, two_ref)
-    out_ref[48:72, :] = own_ref[:ATOM_ROWS, :]
-    out_ref[72:96, :] = other_ref[:ATOM_ROWS, :]
+    atom_rows(out_ref, 48, own_ref)
+    atom_rows(out_ref, 72, other_ref)
 
 
 def column(own, other, halos, odd):
@@ -356,9 +352,9 @@
     return masks, factors
 
 
-def spread_kernel(parcel_ref, vb_ref):
+def spread_kernel(pot_ref, vb_ref):
     def spread_row(row, _):
-        line = (parcel_ref[pl.ds(24 + row, 1), :] + (DIAGONAL - filter_centre)) * (1.0 / filter_half)
+        line = (pot_ref[pl.ds(row, 1), :] + (DIAGONAL - filter_centre)) * (1.0 / filter_half)
         start = pl.multiple_of(row * 128, 128)
         vb_ref[pl.ds(start, 128), :] = jnp.broadcast_to(line, (128, 128)).T
         return 0
@@ -366,14 +362,14 @@
     lax.fori_loop(0, CELLS // 128, spread_row, 0, unroll=8)
 
 
-def spread(parcel):
+def spread(pot):
     return pl.pallas_call(
         spread_kernel,
         out_shape=FULL_ROWS,
         compiler_params=params(8),
         cost_estimate=cost(1 << 20, 2 << 20),
         name="spread",
-    )(parcel)
+    )(pot)
 
 
 def prep_kernel(*refs):
@@ -389,10 +385,12 @@
         for pair in (lower, higher):
             ordered += [jnp.where(upper_y, pair[1], pair[0]), jnp.where(upper_y, pair[0], pair[1])]
         for j in range(4):
-            near_ref[slab * 96 + j * 24 : slab * 96 + j * 24 + 24, :] = ordered[j]
+            for block in range(6):
+                row = block * NEAR + slab * 16 + j * 4
+                near_ref[row : row + 4, :] = ordered[j][block * 4 : block * 4 + 4]
     blank = jnp.zeros((16, 128), F32)
     for block in range(6):
-        rows = near_ref[pl.ds(block, NEAR, stride=6), :]
+        rows = near_ref[block * NEAR : (block + 1) * NEAR, :]
         table_ref[block * 128 : block * 128 + 128, :] = jnp.concatenate([rows, blank, rows, blank]).T
     at = TAPS + 3 - 640
     energy_ref[...] = jnp.broadcast_to(rows[:, at : at + 1] * (1.0 / filter_half), (NEAR, S))
@@ -826,14 +824,12 @@
     corner = jnp.stack([gx * C, gy * C]).astype(jnp.int32)
     upper = gx.astype(jnp.int32).reshape(1)
     odd = (lax.axis_index("gzs") % 2).astype(jnp.int32).reshape(1)
-    pot = potential.reshape(32, 128)
     atoms = jnp.concatenate(
         [projectors.reshape(4, TAPS), atom_sites.astype(F32), energies[:, None], jnp.zeros((4, 768 - TAPS - 4), F32)],
         axis=1,
-    ).reshape(24, 128)
-    pot, corner, upper, inner, odd, atoms = barrier((pot, corner, upper, inner, odd, atoms))
-    parcel = stack(atoms, pot)
-    to_pack, parcel = barrier((s, parcel))
+    )
+    corner, upper, inner, odd, atoms = barrier((corner, upper, inner, odd, atoms))
+    to_pack, parcel = barrier((s, atoms))
     parcel_mate = send(parcel, over_y)
     message, relay, mid = pack(to_pack, inner)
     parcel_mate, message, relay = barrier((parcel_mate, message, relay))
@@ -841,7 +837,9 @@
     message = send(message, over_y)
     relayed = lax.ppermute(relay, AXES, [(d, d ^ over_y ^ 1) for d in outer_ones])
     halos = to_pairs(halo_one, halo_two)
-    vb = spread(parcel)
+    potential, relay = barrier((potential, relay))
+    pot = potential.reshape(32, 128)
+    vb = spread(pot)
     mate, relayed = barrier((mate, relayed))
     beside = side_x(s, mate)
     halos, beside, vb = barrier((halos, beside, vb))
@@ -859,9 +857,11 @@
     q, mix, halo_one, halo_two = make_first(s, side_part, vb, edges, inner, odd, part, part_mate)
     halos = to_pairs(halo_one, halo_two)
     mate = send(mix, over_x)
-    mid, part_mate = barrier((mid, part_mate))
+    pot, part_mate = barrier((pot, part_mate))
+    pot_mate = send(pot, over_y)
+    mid, pot_mate = barrier((mid, pot_mate))
     mid = lax.ppermute(mid, AXES, [(d, d ^ over_y) for d in inner_ones])
-    vb_mate = spread(parcel_mate).reshape(C, ROWS, S)
+    vb_mate = spread(pot_mate).reshape(C, ROWS, S)
     part_two = side_again(mix, mate)
     base = make_base(s, mid, vb, vb_mate, q, side_part, part_two, edges, inner)
     gg = gg.reshape(2, C, ROWS, S)

time: 145 us -> 159 us (1.097)
  Pallas kernels: 43.1 us -> 55.5 us
  starting transfers between devices: 29.9 us -> 37.1 us
  waiting for transfers between devices: 64.6 us -> 58 us
    ppermute x9 -> x10, waiting for transfers between devices: 10.9 us -> 26.3 us  [send(): return lax.ppermute(value, AXES, [(d, d ^ flip) for d in range(count)])]
    ppermute x4, waiting for transfers between devices: 24.5 us -> 10.3 us  [to_pairs(): return (lax.ppermute(one, AXES, near), lax.ppermute(two, AXES, far))]
    ppermute x6, starting transfers between devices: 3.01 us -> 9.29 us  [per_device(): own = own + lax.ppermute(own, AXES, [(d, d ^ flip) for d in range(count)])]
    ppermute x6, waiting for transfers between devices: 24.1 us -> 17.9 us  [per_device(): own = own + lax.ppermute(own, AXES, [(d, d ^ flip) for d in range(count)])]
    pallas_call x1, Pallas kernels: 2.92 us -> 6.24 us  [make_base(): pl.pallas_call(base_kernel, grid=(C // N,), in_specs=[plane_spec(ROWS, N)...]
    pallas_call x1, Pallas kernels: 2.25 us -> 5.21 us  [make_first(): pl.pallas_call(first_kernel, grid=(C // N,), in_specs=[plane_spec(ROWS, N...]
    ppermute x1, starting transfers between devices: 3.02 us -> 5.67 us  [per_device(): lax.ppermute(relay, AXES, [(d, d ^ over_y ^ 1) for d in outer_ones])]
    ppermute x9 -> x10, starting transfers between devices: 5.5 us -> 3.07 us  [send(): return lax.ppermute(value, AXES, [(d, d ^ flip) for d in range(count)])]
  transfers between devices with their start and end apart: 22 -> 23, of which waited for: 17 -> 15; matrix products, arithmetic and copies ran while one was open for 3% -> 2% of each run, Pallas kernels for 14% -> 19%
where the time goes in v20:
time: 159 us; the launch traced here: 157 us
  waiting for transfers between devices  58 us (36%)
  Pallas kernels  55.5 us (35%)
  starting transfers between devices  37.1 us (23%)
  local copies, waits for them, and re-layouts  5.32 us (3%)
    ppermute x10, waiting for transfers between devices, send(): return lax.ppermute(value, AXES, [(d, d ^ flip) for d in range(count)])  26.3 us
    ppermute x6, waiting for transfers between devices, per_device(): own = own + lax.ppermute(own, AXES, [(d, d ^ flip) for d in range(count)])  17.9 us
    ppermute x4, starting transfers between devices, to_pairs(): return (lax.ppermute(one, AXES, near), lax.ppermute(two, AXES, far))  17 us
    pallas_call x1, Pallas kernels, turn(): pl.pallas_call(turn_kernel, grid=(STEPS,), in_specs=[plane_spec(), whole(...  16.5 us
    ppermute x4, waiting for transfers between devices, to_pairs(): return (lax.ppermute(one, AXES, near), lax.ppermute(two, AXES, far))  10.3 us
    ppermute x6, starting transfers between devices, per_device(): own = own + lax.ppermute(own, AXES, [(d, d ^ flip) for d in range(count)])  9.29 us
    pallas_call x1, Pallas kernels, prep(): pl.pallas_call(prep_kernel, in_specs=[vmem] * 2 + [pl.BlockSpec(memory_sp...  7.75 us
    pallas_call x1, Pallas kernels, make_base(): pl.pallas_call(base_kernel, grid=(C // N,), in_specs=[plane_spec(ROWS, N)...  6.24 us
  transfers between devices with their start and end apart: 23, of which 15 were waited for; matrix products, arithmetic and copies ran while one was open for 2% of the time, Pallas kernels for 19%

profile of v20, /device:TPU:0, one launch (start us, length us, event | category | flops | bytes accessed | tf_op | source)
XLA Modules:
  0.0 157.0 jit_solution(10857850535943878455)
XLA Ops:
  2.8 2.0 %collective-permute-start = (f32[4,768]{1,0:T(4,128)S(1)}, f32[4,768]{1,0:T(4,128)S(1)}, u32[]{:S(2)}, u32[]{:S(2)}) collective-permute-start(f32[4,768]{1,0:T(4,128)S(1)} %maximum_maximum_fusion.own_ref), channel_id=1, source_target_pairs={{0,32},{1,33},{2,34},{3,35},{4,36},{5,37},{6,38},{7,39},{8,40},{9,... | collective-permute-start | bytes 36872 | tf_op jit(solution)/shard_map/ppermute | solution.py:810
  4.8 1.6 %copy-done = f32[16,16,16,128]{3,2,1,0:T(8,128)S(1)} copy-done((f32[16,16,16,128]{3,2,1,0:T(8,128)S(1)}, f32[16,16,16,128]{3,2,1,0:T(8,128)}, u32[]{:S(2)}) %copy-start) | copy-done | bytes 2097176
  6.4 1.5 pack.1
  8.7 5.7 %collective-permute-start.4 = (f32[6,192,128]{2,1,0:T(8,128)S(1)}, f32[6,192,128]{2,1,0:T(8,128)}, u32[]{:S(2)}, u32[]{:S(2)}) collective-permute-start(f32[6,192,128]{2,1,0:T(8,128)S(1)} %get-tuple-element.50), channel_id=1, source_target_pairs={{0,33},{3,34},{4,37},{7,38},{8,41},{11,42},{12,45},{15,46},{16,49}... | collective-permute-start | bytes 1769480 | tf_op jit(solution)/shard_map/ppermute | solution.py:838
  14.3 1.7 %pack_halos.1 = (f32[1584,128]{1,0:T(8,128)}, f32[1584,128]{1,0:T(8,128)}) custom-call(f32[16,256,128]{2,1,0:T(8,128)S(1)} %bitcast.15, s32[1]{0:T(128)} %bitcast.5.odd_ref.refs_3_.rest_4_, f32[4,768]{1,0:T(4,128)S(1)} %maximum_maximum_fusion.own_ref, f32[4,768]{1,0:T(4,128)S(1)} %collective-permute-done.other_ref), custom_call_target="tpu_custom_call" | custom-call | flops 1048576 | bytes 4194304 | tf_op jit(solution)/shard_map/pack_halos/pallas_call | solution.py:216
  16.1 7.6 %collective-permute-start.2 = (f32[1584,128]{1,0:T(8,128)}, f32[1584,128]{1,0:T(8,128)}, u32[]{:S(2)}, u32[]{:S(2)}) collective-permute-start(f32[1584,128]{1,0:T(8,128)} %get-tuple-element.55), channel_id=1, source_target_pairs={{0,31},{1,2},{2,1},{3,4},{4,3},{5,6},{6,5},{7,8},{8,7},{9,10},{10,... | collective-permute-start | bytes 2433032 | tf_op jit(solution)/shard_map/ppermute | solution.py:817
  23.6 3.6 %collective-permute-done.4 = f32[6,192,128]{2,1,0:T(8,128)} collective-permute-done((f32[6,192,128]{2,1,0:T(8,128)S(1)}, f32[6,192,128]{2,1,0:T(8,128)}, u32[]{:S(2)}, u32[]{:S(2)}) %collective-permute-start.4) | collective-permute-done | bytes 589856 | tf_op jit(solution)/shard_map/ppermute | solution.py:838
  27.2 1.3 collective-permute-start.11
  30.3 3.1 %side_x.1.part_ref = f32[16,256,128]{2,1,0:T(8,128)S(1)} custom-call(f32[16,256,128]{2,1,0:T(8,128)S(1)} %bitcast.16, f32[16,256,128]{2,1,0:T(8,128)} %collective-permute-done.3.mate_ref), custom_call_target="tpu_custom_call" | custom-call | flops 16777216 | bytes 6291456 | tf_op jit(solution)/shard_map/side_x/pallas_call | solution.py:273
  33.4 10.3 %collective-permute-done.1.one_ref = f32[1584,128]{1,0:T(8,128)S(1)} collective-permute-done((f32[1584,128]{1,0:T(8,128)}, f32[1584,128]{1,0:T(8,128)S(1)}, u32[]{:S(2)}, u32[]{:S(2)}) %collective-permute-start.1) | collective-permute-done | bytes 811040 | tf_op jit(solution)/shard_map/ppermute | solution.py:817
  44.9 4.0 %side_z.1.side_ref = f32[16,256,128]{2,1,0:T(8,128)S(1)} custom-call(f32[16,256,128]{2,1,0:T(8,128)S(1)} %bitcast.17, f32[16,256,128]{2,1,0:T(8,128)S(1)} %side_x.1.part_ref, f32[1584,128]{1,0:T(8,128)S(1)} %collective-permute-done.1.one_ref, f32[1584,128]{1,0:T(8,128)} %collective-permute-done.2.two_ref, s32[1]{0:T(128)} %bitcast.5.odd_ref.refs_3_.rest_4_), custom_call_target="tpu_custom_call" | custom-call | flops 16777216 | bytes 8388608 | tf_op jit(solution)/shard_map/side_z/pallas_call | solution.py:301
  49.0 1.3 collective-permute-done.5.refs_1_
  50.2 7.7 %prep.1 = (bf16[2,4096,128]{2,1,0:T(8,128)(2,1)S(1)}, f32[3,48,128]{2,1,0:T(8,128)S(1)}, f32[48,128]{1,0:T(8,128)S(1)}) custom-call(f32[144,128]{1,0:T(8,128)S(1)} %column.1.refs_0_, f32[144,128]{1,0:T(8,128)S(1)} %collective-permute-done.5.refs_1_, s32[2]{0:T(128)S(1)} %pad_add_fusion.refs_2_, f32[4096,128]{1,0:T(8,128)S(1)} %spread.2.refs_3_, ...), custom_call_target="tpu_custom_call" | custom-call | flops 134217728 | bytes 10485760 | tf_op jit(solution)/shard_map/prep/pallas_call | solution.py:491
  59.9 3.5 %collective-permute-done.10.refs_3_ = f32[3072,128]{1,0:T(8,128)} collective-permute-done((f32[3072,128]{1,0:T(8,128)}, f32[3072,128]{1,0:T(8,128)}, u32[]{:S(2)}, u32[]{:S(2)}) %collective-permute-start.10) | collective-permute-done | bytes 1572896 | tf_op jit(solution)/shard_map/ppermute | solution.py:810
  64.3 5.2 %first.1 = (f32[16,256,128]{2,1,0:T(8,128)S(1)}, f32[16,256,128]{2,1,0:T(8,128)S(1)}, f32[1632,128]{1,0:T(8,128)S(1)}, f32[1632,128]{1,0:T(8,128)S(1)}) custom-call(f32[16,256,128]{2,1,0:T(8,128)S(1)} %bitcast.19, f32[16,256,128]{2,1,0:T(8,128)S(1)} %side_z.1.side_ref, f32[16,256,128]{2,1,0:T(8,128)S(1)} %bitcast.21, f32[16,192,128]{2,1,0:T(8,128)} %bitcast.10.refs_0_, ...), custom_call_target="tpu_custom_call" | custom-call | flops 16777216 | bytes 14680064 | tf_op jit(solution)/shard_map/first/pallas_call | solution.py:558
  69.7 1.9 %collective-permute-start.13 = (f32[1632,128]{1,0:T(8,128)S(1)}, f32[1632,128]{1,0:T(8,128)S(1)}, u32[]{:S(2)}, u32[]{:S(2)}) collective-permute-start(f32[1632,128]{1,0:T(8,128)S(1)} %get-tuple-element.72), channel_id=1, source_target_pairs={{0,1},{1,0},{2,3},{3,2},{4,5},{5,4},{6,7},{7,6},{8,9},{9,8},{10,11... | collective-permute-start | bytes 2506760 | tf_op jit(solution)/shard_map/ppermute | solution.py:817
  71.6 7.6 %collective-permute-start.14 = (f32[1632,128]{1,0:T(8,128)S(1)}, f32[1632,128]{1,0:T(8,128)S(1)}, u32[]{:S(2)}, u32[]{:S(2)}) collective-permute-start(f32[1632,128]{1,0:T(8,128)S(1)} %get-tuple-element.73), channel_id=1, source_target_pairs={{0,31},{1,2},{2,1},{3,4},{4,3},{5,6},{6,5},{7,8},{8,7},{9,10},{10,... | collective-permute-start | bytes 2506760 | tf_op jit(solution)/shard_map/ppermute | solution.py:817
  79.1 17.0 %collective-permute-done.8.pot_ref = f32[32,128]{1,0:T(8,128)S(1)} collective-permute-done((f32[32,128]{1,0:T(8,128)S(1)}, f32[32,128]{1,0:T(8,128)S(1)}, u32[]{:S(2)}, u32[]{:S(2)}) %collective-permute-start.8) | collective-permute-done | bytes 16416 | tf_op jit(solution)/shard_map/ppermute | solution.py:810
  97.7 2.9 %side_again.1.part_ref = f32[16,256,128]{2,1,0:T(8,128)S(1)} custom-call(f32[16,256,128]{2,1,0:T(8,128)S(1)} %get-tuple-element.71.s_ref, f32[16,256,128]{2,1,0:T(8,128)S(1)} %collective-permute-done.12.mate_ref), custom_call_target="tpu_custom_call" | custom-call | flops 33554432 | bytes 6291456 | tf_op jit(solution)/shard_map/side_again/pallas_call | solution.py:329
  100.6 6.2 %base.1.base_ref = f32[16,256,128]{2,1,0:T(8,128)S(1)} custom-call(f32[16,256,128]{2,1,0:T(8,128)S(1)} %bitcast.20, f32[16,64,128]{2,1,0:T(8,128)S(1)} %collective-permute-done.9.mid_ref, f32[16,256,128]{2,1,0:T(8,128)S(1)} %bitcast.22, f32[16,256,128]{2,1,0:T(8,128)S(1)} %bitcast.25, f32[16,256,128]{2,1,0:T(8,128)S(1)} %get-tuple-element.70.q_ref, ...), custom_call_target="tpu_custom_call" | custom-call | flops 33554432 | bytes 16777216 | tf_op jit(solution)/shard_map/base/pallas_call | solution.py:610
  106.9 3.9 %second.1 = (f32[16,256,128]{2,1,0:T(8,128)S(1)}, f32[64,128]{1,0:T(8,128)S(1)}, f32[64,128]{1,0:T(8,128)S(1)}) custom-call(f32[16,256,128]{2,1,0:T(8,128)S(1)} %base.1.base_ref, f32[1632,128]{1,0:T(8,128)S(1)} %collective-permute-done.13.one_ref, f32[1632,128]{1,0:T(8,128)S(1)} %collective-permute-done.14.two_ref, bf16[2,16,256,128]{3,2,1,0:T(8,128)(2,1)S(1)} %bitcast.23, ...), custom_call_target="tpu_custom_call" | custom-call | flops 134217728 | bytes 8388608 | tf_op jit(solution)/shard_map/second/pallas_call | solution.py:685
  112.1 2.1 %collective-permute-start.16 = (f32[64,128]{1,0:T(8,128)S(1)}, f32[64,128]{1,0:T(8,128)S(1)}, u32[]{:S(2)}, u32[]{:S(2)}) collective-permute-start(f32[64,128]{1,0:T(8,128)S(1)} %add.39), channel_id=1, source_target_pairs={{0,32},{1,33},{2,34},{3,35},{4,36},{5,37},{6,38},{7,39},{8,40},{9,... | collective-permute-start | bytes 98312 | tf_op jit(solution)/shard_map/ppermute | solution.py:872
  114.2 1.9 %collective-permute-done.16 = f32[64,128]{1,0:T(8,128)S(1)} collective-permute-done((f32[64,128]{1,0:T(8,128)S(1)}, f32[64,128]{1,0:T(8,128)S(1)}, u32[]{:S(2)}, u32[]{:S(2)}) %collective-permute-start.16) | collective-permute-done | bytes 32800 | tf_op jit(solution)/shard_map/ppermute | solution.py:872
  116.1 5.1 %collective-permute-done.17 = f32[64,128]{1,0:T(8,128)S(1)} collective-permute-done((f32[64,128]{1,0:T(8,128)S(1)}, f32[64,128]{1,0:T(8,128)S(1)}, u32[]{:S(2)}, u32[]{:S(2)}) %collective-permute-start.17) | collective-permute-done | bytes 32800 | tf_op jit(solution)/shard_map/ppermute | solution.py:872
  121.2 3.9 %collective-permute-done.18 = f32[64,128]{1,0:T(8,128)S(1)} collective-permute-done((f32[64,128]{1,0:T(8,128)S(1)}, f32[64,128]{1,0:T(8,128)S(1)}, u32[]{:S(2)}, u32[]{:S(2)}) %collective-permute-start.18) | collective-permute-done | bytes 32800 | tf_op jit(solution)/shard_map/ppermute | solution.py:872
  125.1 2.7 %collective-permute-start.19 = (f32[64,128]{1,0:T(8,128)S(1)}, f32[64,128]{1,0:T(8,128)S(1)}, u32[]{:S(2)}, u32[]{:S(2)}) collective-permute-start(f32[64,128]{1,0:T(8,128)S(1)} %add.42), channel_id=1, source_target_pairs={{0,3},{1,2},{2,1},{3,0},{4,7},{5,6},{6,5},{7,4},{8,11},{9,10},{10,... | collective-permute-start | bytes 98312 | tf_op jit(solution)/shard_map/ppermute | solution.py:872
  127.9 2.4 %collective-permute-done.19 = f32[64,128]{1,0:T(8,128)S(1)} collective-permute-done((f32[64,128]{1,0:T(8,128)S(1)}, f32[64,128]{1,0:T(8,128)S(1)}, u32[]{:S(2)}, u32[]{:S(2)}) %collective-permute-start.19) | collective-permute-done | bytes 32800 | tf_op jit(solution)/shard_map/ppermute | solution.py:872
  130.3 1.5 collective-permute-start.20
  131.8 2.4 %collective-permute-done.20 = f32[64,128]{1,0:T(8,128)S(1)} collective-permute-done((f32[64,128]{1,0:T(8,128)S(1)}, f32[64,128]{1,0:T(8,128)S(1)}, u32[]{:S(2)}, u32[]{:S(2)}) %collective-permute-start.20) | collective-permute-done | bytes 32800 | tf_op jit(solution)/shard_map/ppermute | solution.py:872
  134.2 3.0 %collective-permute-start.21 = (f32[64,128]{1,0:T(8,128)S(1)}, f32[64,128]{1,0:T(8,128)S(1)}, u32[]{:S(2)}, u32[]{:S(2)}) collective-permute-start(f32[64,128]{1,0:T(8,128)S(1)} %add.44), channel_id=1, source_target_pairs={{0,24},{1,25},{2,26},{3,27},{4,28},{5,29},{6,30},{7,31},{8,16},{9,... | collective-permute-start | bytes 98312 | tf_op jit(solution)/shard_map/ppermute | solution.py:872
  137.1 2.2 %collective-permute-done.21 = f32[64,128]{1,0:T(8,128)S(1)} collective-permute-done((f32[64,128]{1,0:T(8,128)S(1)}, f32[64,128]{1,0:T(8,128)S(1)}, u32[]{:S(2)}, u32[]{:S(2)}) %collective-permute-start.21) | collective-permute-done | bytes 32800 | tf_op jit(solution)/shard_map/ppermute | solution.py:872
  140.5 16.5 %turn.1 = f32[16,256,128]{2,1,0:T(8,128)} custom-call(f32[16,256,128]{2,1,0:T(8,128)S(1)} %get-tuple-element.78.second_ref, f32[64,128]{1,0:T(8,128)S(1)} %add.45.own_ref, f32[64,128]{1,0:T(8,128)S(1)} %collective-permute-done.22.other_ref, s32[1]{0:T(128)} %bitcast.3.rest_3_.upper_ref), custom_call_target="tpu_custom_call" | custom-call | flops 268435456 | bytes 4194304 | tf_op jit(solution)/shard_map/turn/pallas_call | solution.py:790
  (52 shorter events, 13.6 us)
Async XLA Ops:
  0.0 27.2 %collective-permute-start.3 = (f32[16,256,128]{2,1,0:T(8,128)}, f32[16,256,128]{2,1,0:T(8,128)}, u32[]{:S(2)}, u32[]{:S(2)}) collective-permute-start(f32[16,256,128]{2,1,0:T(8,128)} %bitcast.13), channel_id=1, source_target_pairs={{0,64},{1,65},{2,66},{3,67},{4,68},{5,69},{6,70},{7,71},{8,72},{9,... | collective-permute-start | bytes 6291464 | tf_op jit(solution)/shard_map/ppermute | solution.py:810
  2.8 5.9 %collective-permute-start = (f32[4,768]{1,0:T(4,128)S(1)}, f32[4,768]{1,0:T(4,128)S(1)}, u32[]{:S(2)}, u32[]{:S(2)}) collective-permute-start(f32[4,768]{1,0:T(4,128)S(1)} %maximum_maximum_fusion.own_ref), channel_id=1, source_target_pairs={{0,32},{1,33},{2,34},{3,35},{4,36},{5,37},{6,38},{7,39},{8,40},{9,... | collective-permute-start | bytes 36872 | tf_op jit(solution)/shard_map/ppermute | solution.py:810
  4.8 1.6 %copy-start = (f32[16,16,16,128]{3,2,1,0:T(8,128)S(1)}, f32[16,16,16,128]{3,2,1,0:T(8,128)}, u32[]{:S(2)}) copy-start(f32[16,16,16,128]{3,2,1,0:T(8,128)} %param.5) | copy-start | bytes 6291460
  7.8 0.8 copy-start.2
  8.6 21.7 %copy-start.1 = (f32[16,16,16,128]{3,2,1,0:T(8,128)S(1)}, f32[16,16,16,128]{3,2,1,0:T(8,128)}, u32[]{:S(2)}) copy-start(f32[16,16,16,128]{3,2,1,0:T(8,128)} %param.5) | copy-start | bytes 6291460
  8.6 54.7 %collective-permute-start.10 = (f32[3072,128]{1,0:T(8,128)}, f32[3072,128]{1,0:T(8,128)}, u32[]{:S(2)}, u32[]{:S(2)}) collective-permute-start(f32[3072,128]{1,0:T(8,128)} %get-tuple-element.68), channel_id=1, source_target_pairs={{0,32},{1,33},{2,34},{3,35},{4,36},{5,37},{6,38},{7,39},{8,40},{9,... | collective-permute-start | bytes 4718600 | tf_op jit(solution)/shard_map/ppermute | solution.py:810
  8.7 18.5 %collective-permute-start.4 = (f32[6,192,128]{2,1,0:T(8,128)S(1)}, f32[6,192,128]{2,1,0:T(8,128)}, u32[]{:S(2)}, u32[]{:S(2)}) collective-permute-start(f32[6,192,128]{2,1,0:T(8,128)S(1)} %get-tuple-element.50), channel_id=1, source_target_pairs={{0,33},{3,34},{4,37},{7,38},{8,41},{11,42},{12,45},{15,46},{16,49}... | collective-permute-start | bytes 1769480 | tf_op jit(solution)/shard_map/ppermute | solution.py:838
  16.1 27.7 %collective-permute-start.1 = (f32[1584,128]{1,0:T(8,128)}, f32[1584,128]{1,0:T(8,128)S(1)}, u32[]{:S(2)}, u32[]{:S(2)}) collective-permute-start(f32[1584,128]{1,0:T(8,128)} %get-tuple-element.54), channel_id=1, source_target_pairs={{0,1},{1,0},{2,3},{3,2},{4,5},{5,4},{6,7},{7,6},{8,9},{9,8},{10,11... | collective-permute-start | bytes 2433032 | tf_op jit(solution)/shard_map/ppermute | solution.py:817
  16.1 27.7 %collective-permute-start.2 = (f32[1584,128]{1,0:T(8,128)}, f32[1584,128]{1,0:T(8,128)}, u32[]{:S(2)}, u32[]{:S(2)}) collective-permute-start(f32[1584,128]{1,0:T(8,128)} %get-tuple-element.55), channel_id=1, source_target_pairs={{0,31},{1,2},{2,1},{3,4},{4,3},{5,6},{6,5},{7,8},{8,7},{9,10},{10,... | collective-permute-start | bytes 2433032 | tf_op jit(solution)/shard_map/ppermute | solution.py:817
  27.2 37.1 %collective-permute-start.11 = (f32[6,192,128]{2,1,0:T(8,128)}, f32[6,192,128]{2,1,0:T(8,128)S(1)}, u32[]{:S(2)}, u32[]{:S(2)}) collective-permute-start(f32[6,192,128]{2,1,0:T(8,128)} %collective-permute-done.4), channel_id=1, source_target_pairs={{1,0},{2,3},{5,4},{6,7},{9,8},{10,11},{13,12},{14,15},{17,16},{18,... | collective-permute-start | bytes 1769480 | tf_op jit(solution)/shard_map/ppermute | solution.py:846
  48.9 1.3 collective-permute-start.5
  58.0 1.3 collective-permute-start.6
  59.3 5.0 %collective-permute-start.7 = (f32[3,48,128]{2,1,0:T(8,128)S(1)}, f32[3,48,128]{2,1,0:T(8,128)S(1)}, u32[]{:S(2)}, u32[]{:S(2)}) collective-permute-start(f32[3,48,128]{2,1,0:T(8,128)S(1)} %add.38.refs_4_.rest_0_), channel_id=1, source_target_pairs={{0,32},{1,33},{2,34},{3,35},{4,36},{5,37},{6,38},{7,39},{8,40},{9,... | collective-permute-start | bytes 221192 | tf_op jit(solution)/shard_map/ppermute | solution.py:810
  64.3 31.8 %copy-start.3 = (f32[16,64,128]{2,1,0:T(8,128)S(1)}, f32[16,64,128]{2,1,0:T(8,128)}, u32[]{:S(2)}) copy-start(f32[16,64,128]{2,1,0:T(8,128)} %copy-done.2) | copy-start | bytes 1572868
  69.6 28.1 %collective-permute-start.12 = (f32[16,256,128]{2,1,0:T(8,128)S(1)}, f32[16,256,128]{2,1,0:T(8,128)S(1)}, u32[]{:S(2)}, u32[]{:S(2)}) collective-permute-start(f32[16,256,128]{2,1,0:T(8,128)S(1)} %get-tuple-element.71.s_ref), channel_id=1, source_target_pairs={{0,64},{1,65},{2,66},{3,67},{4,68},{5,69},{6,70},{7,71},{8,72},{9,... | collective-permute-start | bytes 6291464 | tf_op jit(solution)/shard_map/ppermute | solution.py:810
  69.7 37.2 %collective-permute-start.13 = (f32[1632,128]{1,0:T(8,128)S(1)}, f32[1632,128]{1,0:T(8,128)S(1)}, u32[]{:S(2)}, u32[]{:S(2)}) collective-permute-start(f32[1632,128]{1,0:T(8,128)S(1)} %get-tuple-element.72), channel_id=1, source_target_pairs={{0,1},{1,0},{2,3},{3,2},{4,5},{5,4},{6,7},{7,6},{8,9},{9,8},{10,11... | collective-permute-start | bytes 2506760 | tf_op jit(solution)/shard_map/ppermute | solution.py:817
  71.6 35.3 %collective-permute-start.14 = (f32[1632,128]{1,0:T(8,128)S(1)}, f32[1632,128]{1,0:T(8,128)S(1)}, u32[]{:S(2)}, u32[]{:S(2)}) collective-permute-start(f32[1632,128]{1,0:T(8,128)S(1)} %get-tuple-element.73), channel_id=1, source_target_pairs={{0,31},{1,2},{2,1},{3,4},{4,3},{5,6},{6,5},{7,8},{8,7},{9,10},{10,... | collective-permute-start | bytes 2506760 | tf_op jit(solution)/shard_map/ppermute | solution.py:817
  79.1 17.0 %collective-permute-start.8 = (f32[32,128]{1,0:T(8,128)S(1)}, f32[32,128]{1,0:T(8,128)S(1)}, u32[]{:S(2)}, u32[]{:S(2)}) collective-permute-start(f32[32,128]{1,0:T(8,128)S(1)} %reshape.38.pot_ref), channel_id=1, source_target_pairs={{0,32},{1,33},{2,34},{3,35},{4,36},{5,37},{6,38},{7,39},{8,40},{9,... | collective-permute-start | bytes 49160 | tf_op jit(solution)/shard_map/ppermute | solution.py:810
  96.2 4.5 %collective-permute-start.9 = (f32[16,64,128]{2,1,0:T(8,128)S(1)}, f32[16,64,128]{2,1,0:T(8,128)S(1)}, u32[]{:S(2)}, u32[]{:S(2)}) collective-permute-start(f32[16,64,128]{2,1,0:T(8,128)S(1)} %copy-done.3), channel_id=1, source_target_pairs={{1,33},{2,34},{5,37},{6,38},{9,41},{10,42},{13,45},{14,46},{17,49}... | collective-permute-start | bytes 1572872 | tf_op jit(solution)/shard_map/ppermute | solution.py:863
  110.8 1.3 collective-permute-start.15
  112.1 4.0 %collective-permute-start.16 = (f32[64,128]{1,0:T(8,128)S(1)}, f32[64,128]{1,0:T(8,128)S(1)}, u32[]{:S(2)}, u32[]{:S(2)}) collective-permute-start(f32[64,128]{1,0:T(8,128)S(1)} %add.39), channel_id=1, source_target_pairs={{0,32},{1,33},{2,34},{3,35},{4,36},{5,37},{6,38},{7,39},{8,40},{9,... | collective-permute-start | bytes 98312 | tf_op jit(solution)/shard_map/ppermute | solution.py:872
  116.1 5.1 %collective-permute-start.17 = (f32[64,128]{1,0:T(8,128)S(1)}, f32[64,128]{1,0:T(8,128)S(1)}, u32[]{:S(2)}, u32[]{:S(2)}) collective-permute-start(f32[64,128]{1,0:T(8,128)S(1)} %add.40), channel_id=1, source_target_pairs={{0,36},{1,37},{2,38},{3,39},{4,32},{5,33},{6,34},{7,35},{8,44},{9,... | collective-permute-start | bytes 98312 | tf_op jit(solution)/shard_map/ppermute | solution.py:872
  121.2 3.9 %collective-permute-start.18 = (f32[64,128]{1,0:T(8,128)S(1)}, f32[64,128]{1,0:T(8,128)S(1)}, u32[]{:S(2)}, u32[]{:S(2)}) collective-permute-start(f32[64,128]{1,0:T(8,128)S(1)} %add.41), channel_id=1, source_target_pairs={{0,1},{1,0},{2,3},{3,2},{4,5},{5,4},{6,7},{7,6},{8,9},{9,8},{10,11... | collective-permute-start | bytes 98312 | tf_op jit(solution)/shard_map/ppermute | solution.py:872
  125.1 5.1 %collective-permute-start.19 = (f32[64,128]{1,0:T(8,128)S(1)}, f32[64,128]{1,0:T(8,128)S(1)}, u32[]{:S(2)}, u32[]{:S(2)}) collective-permute-start(f32[64,128]{1,0:T(8,128)S(1)} %add.42), channel_id=1, source_target_pairs={{0,3},{1,2},{2,1},{3,0},{4,7},{5,6},{6,5},{7,4},{8,11},{9,10},{10,... | collective-permute-start | bytes 98312 | tf_op jit(solution)/shard_map/ppermute | solution.py:872
  130.3 3.9 %collective-permute-start.20 = (f32[64,128]{1,0:T(8,128)S(1)}, f32[64,128]{1,0:T(8,128)S(1)}, u32[]{:S(2)}, u32[]{:S(2)}) collective-permute-start(f32[64,128]{1,0:T(8,128)S(1)} %add.43), channel_id=1, source_target_pairs={{0,8},{1,9},{2,10},{3,11},{4,12},{5,13},{6,14},{7,15},{8,0},{9,1},... | collective-permute-start | bytes 98312 | tf_op jit(solution)/shard_map/ppermute | solution.py:872
  134.2 5.1 %collective-permute-start.21 = (f32[64,128]{1,0:T(8,128)S(1)}, f32[64,128]{1,0:T(8,128)S(1)}, u32[]{:S(2)}, u32[]{:S(2)}) collective-permute-start(f32[64,128]{1,0:T(8,128)S(1)} %add.44), channel_id=1, source_target_pairs={{0,24},{1,25},{2,26},{3,27},{4,28},{5,29},{6,30},{7,31},{8,16},{9,... | collective-permute-start | bytes 98312 | tf_op jit(solution)/shard_map/ppermute | solution.py:872
  139.3 1.2 collective-permute-start.22

commit v21 on v19

--- a/solution.py
+++ b/solution.py
@@ -229,7 +229,7 @@
     return pl.pallas_call(stack_kernel, out_shape=sds((56, S)), compiler_params=params(4), name="stack")(atoms, pot)
 
 
-def column_kernel(own_ref, other_ref, one_ref, two_ref, odd_ref, out_ref):
+def column_kernel(own_ref, other_ref, two_ref, one_ref, odd_ref, out_ref):
     def beside(below_ref, above_ref):
         out_ref[0:48, :] = below_ref[HALO_ROWS:, :]
         out_ref[96:144, :] = above_ref[HALO_ROWS:, :]
@@ -283,7 +283,7 @@
     )(s, mate)
 
 
-def side_z_kernel(s_ref, part_ref, one_ref, two_ref, odd_ref, out_ref, ext_ref):
+def side_z_kernel(s_ref, part_ref, two_ref, one_ref, odd_ref, out_ref, ext_ref):
     def planes(low_ref, high_ref):
         def plane(x, _):
             for y in range(C):
@@ -624,7 +624,7 @@
     )(s, mid, vb, vb_mate, q, side_part, part, *edges, inner, edges[0].reshape(-1, S))
 
 
-def second_kernel(base_ref, one_ref, two_ref, gg_high_ref, gg_low_ref, *rest):
+def second_kernel(base_ref, two_ref, one_ref, gg_high_ref, gg_low_ref, *rest):
     part_ref, mate_ref, energy_ref, upper_ref, odd_ref, second_ref, keep_ref, give_ref, gram_ref, cross_ref, w_ref, halo_ref = rest
     step = pl.program_id(0)
 
@@ -816,7 +816,7 @@
     def to_pairs(one, two):
         near = [(d, d ^ 1) for d in range(count)]
         far = [(d, d // depth * depth + (d + (1 if d % 2 else -1)) % depth) for d in range(count)]
-        return lax.ppermute(one, AXES, near), lax.ppermute(two, AXES, far)
+        return lax.ppermute(two, AXES, far), lax.ppermute(one, AXES, near)
 
     inner_ones = [d for d in range(count) if d % 4 in (1, 2)]
     outer_ones = [d for d in range(count) if d % 4 in (0, 3)]

time: 145 us -> 146 us (level)
  waiting for transfers between devices: 64.6 us -> 67.8 us
  starting transfers between devices: 29.9 us -> 28.1 us
    ppermute x6, starting transfers between devices: 3.01 us -> 1.43 us  [per_device(): own = own + lax.ppermute(own, AXES, [(d, d ^ flip) for d in range(count)])]
    ppermute x6, waiting for transfers between devices: 24.1 us -> 25.7 us  [per_device(): own = own + lax.ppermute(own, AXES, [(d, d ^ flip) for d in range(count)])]
    ppermute x4, waiting for transfers between devices: 24.5 us -> 26.1 us  [to_pairs(): return (lax.ppermute(two, AXES, far), lax.ppermute(one, AXES, near))]
  transfers between devices with their start and end apart: 22 -> 22, of which waited for: 17 -> 18; matrix products, arithmetic and copies ran while one was open for 3% -> 3% of each run, Pallas kernels for 14% -> 14%
where the time goes in v21:
time: 146 us; the launch traced here: 145 us
  waiting for transfers between devices  67.8 us (46%)
  Pallas kernels  43.1 us (30%)
  starting transfers between devices  28.1 us (19%)
  local copies, waits for them, and re-layouts  4.53 us (3%)
    ppermute x4, waiting for transfers between devices, to_pairs(): return (lax.ppermute(two, AXES, far), lax.ppermute(one, AXES, near))  26.1 us
    ppermute x6, waiting for transfers between devices, per_device(): own = own + lax.ppermute(own, AXES, [(d, d ^ flip) for d in range(count)])  25.7 us
    pallas_call x1, Pallas kernels, turn(): pl.pallas_call(turn_kernel, grid=(STEPS,), in_specs=[plane_spec(), whole(...  16.5 us
    ppermute x4, starting transfers between devices, to_pairs(): return (lax.ppermute(two, AXES, far), lax.ppermute(one, AXES, near))  16.2 us
    ppermute x9, waiting for transfers between devices, send(): return lax.ppermute(value, AXES, [(d, d ^ flip) for d in range(count)])  10.9 us
    pallas_call x1, Pallas kernels, prep(): pl.pallas_call(prep_kernel, in_specs=[vmem] * 2 + [pl.BlockSpec(memory_sp...  7.8 us
    ppermute x9, starting transfers between devices, send(): return lax.ppermute(value, AXES, [(d, d ^ flip) for d in range(count)])  5.49 us
    ppermute x1, waiting for transfers between devices, per_device(): lax.ppermute(relay, AXES, [(d, d ^ over_y ^ 1) for d in outer_ones])  5.23 us
  transfers between devices with their start and end apart: 22, of which 18 were waited for; matrix products, arithmetic and copies ran while one was open for 3% of the time, Pallas kernels for 14%

profile of v21, /device:TPU:0, one launch (start us, length us, event | category | flops | bytes accessed | tf_op | source)
XLA Modules:
  0.0 144.7 jit_solution(6619719669274083343)
XLA Ops:
  3.8 2.0 %collective-permute-start = (f32[56,128]{1,0:T(8,128)S(1)}, f32[56,128]{1,0:T(8,128)S(1)}, u32[]{:S(2)}, u32[]{:S(2)}) collective-permute-start(f32[56,128]{1,0:T(8,128)S(1)} %stack.13.own_ref.parcel_ref), channel_id=1, source_target_pairs={{0,32},{1,33},{2,34},{3,35},{4,36},{5,37},{6,38},{7,39},{8,40},{9,... | collective-permute-start | bytes 86024 | tf_op jit(solution)/shard_map/ppermute | solution.py:812
  5.8 1.6 %copy-done = f32[16,16,16,128]{3,2,1,0:T(8,128)S(1)} copy-done((f32[16,16,16,128]{3,2,1,0:T(8,128)S(1)}, f32[16,16,16,128]{3,2,1,0:T(8,128)}, u32[]{:S(2)}) %copy-start) | copy-done | bytes 2097176
  7.8 1.9 %collective-permute-start.9 = (f32[3072,128]{1,0:T(8,128)S(1)}, f32[3072,128]{1,0:T(8,128)S(1)}, u32[]{:S(2)}, u32[]{:S(2)}) collective-permute-start(f32[3072,128]{1,0:T(8,128)S(1)} %get-tuple-element.64), channel_id=1, source_target_pairs={{0,32},{1,33},{2,34},{3,35},{4,36},{5,37},{6,38},{7,39},{8,40},{9,... | collective-permute-start | bytes 4718600 | tf_op jit(solution)/shard_map/ppermute | solution.py:812
  9.7 3.0 %collective-permute-start.4 = (f32[6,192,128]{2,1,0:T(8,128)S(1)}, f32[6,192,128]{2,1,0:T(8,128)S(1)}, u32[]{:S(2)}, u32[]{:S(2)}) collective-permute-start(f32[6,192,128]{2,1,0:T(8,128)S(1)} %get-tuple-element.53), channel_id=1, source_target_pairs={{0,33},{3,34},{4,37},{7,38},{8,41},{11,42},{12,45},{15,46},{16,49}... | collective-permute-start | bytes 1769480 | tf_op jit(solution)/shard_map/ppermute | solution.py:842
  13.3 7.9 %collective-permute-start.1 = (f32[1584,128]{1,0:T(8,128)S(1)}, f32[1584,128]{1,0:T(8,128)S(1)}, u32[]{:S(2)}, u32[]{:S(2)}) collective-permute-start(f32[1584,128]{1,0:T(8,128)S(1)} %get-tuple-element.51), channel_id=1, source_target_pairs={{0,31},{1,2},{2,1},{3,4},{4,3},{5,6},{6,5},{7,8},{8,7},{9,10},{10,... | collective-permute-start | bytes 2433032 | tf_op jit(solution)/shard_map/ppermute | solution.py:819
  21.2 5.2 %collective-permute-done.4 = f32[6,192,128]{2,1,0:T(8,128)S(1)} collective-permute-done((f32[6,192,128]{2,1,0:T(8,128)S(1)}, f32[6,192,128]{2,1,0:T(8,128)S(1)}, u32[]{:S(2)}, u32[]{:S(2)}) %collective-permute-start.4) | collective-permute-done | bytes 589856 | tf_op jit(solution)/shard_map/ppermute | solution.py:842
  26.4 1.3 collective-permute-start.10
  28.5 1.5 %side_x.1.part_ref = f32[16,256,128]{2,1,0:T(8,128)S(1)} custom-call(f32[16,256,128]{2,1,0:T(8,128)S(1)} %bitcast.16, f32[16,256,128]{2,1,0:T(8,128)S(1)} %collective-permute-done.3.mate_ref), custom_call_target="tpu_custom_call" | custom-call | flops 16777216 | bytes 6291456 | tf_op jit(solution)/shard_map/side_x/pallas_call | solution.py:277
  30.0 8.9 %collective-permute-done.1.two_ref = f32[1584,128]{1,0:T(8,128)S(1)} collective-permute-done((f32[1584,128]{1,0:T(8,128)S(1)}, f32[1584,128]{1,0:T(8,128)S(1)}, u32[]{:S(2)}, u32[]{:S(2)}) %collective-permute-start.1) | collective-permute-done | bytes 811040 | tf_op jit(solution)/shard_map/ppermute | solution.py:819
  38.9 3.9 %collective-permute-done.2.one_ref = f32[1584,128]{1,0:T(8,128)S(1)} collective-permute-done((f32[1584,128]{1,0:T(8,128)S(1)}, f32[1584,128]{1,0:T(8,128)S(1)}, u32[]{:S(2)}, u32[]{:S(2)}) %collective-permute-start.2) | collective-permute-done | bytes 811040 | tf_op jit(solution)/shard_map/ppermute | solution.py:819
  42.8 2.9 %side_z.1.side_ref = f32[16,256,128]{2,1,0:T(8,128)S(1)} custom-call(f32[16,256,128]{2,1,0:T(8,128)S(1)} %bitcast.17, f32[16,256,128]{2,1,0:T(8,128)S(1)} %side_x.1.part_ref, f32[1584,128]{1,0:T(8,128)S(1)} %collective-permute-done.1.two_ref, f32[1584,128]{1,0:T(8,128)S(1)} %collective-permute-done.2.one_ref, s32[1]{0:T(128)} %bitcast.5.odd_ref.refs_3_.rest_4_), custom_call_target="tpu_custom_call" | custom-call | flops 16777216 | bytes 8388608 | tf_op jit(solution)/shard_map/side_z/pallas_call | solution.py:305
  45.8 1.3 collective-permute-done.5.refs_1_
  47.0 7.8 %prep.1 = (bf16[2,4096,128]{2,1,0:T(8,128)(2,1)S(1)}, f32[3,48,128]{2,1,0:T(8,128)S(1)}, f32[48,128]{1,0:T(8,128)S(1)}) custom-call(f32[144,128]{1,0:T(8,128)S(1)} %column.1.refs_0_, f32[144,128]{1,0:T(8,128)S(1)} %collective-permute-done.5.refs_1_, s32[2]{0:T(128)S(1)} %pad_add_fusion.refs_2_, f32[4096,128]{1,0:T(8,128)S(1)} %spread.2.refs_3_, ...), custom_call_target="tpu_custom_call" | custom-call | flops 134217728 | bytes 10485760 | tf_op jit(solution)/shard_map/prep/pallas_call | solution.py:493
  55.1 1.1 collective-permute-done.6
  56.2 1.1 collective-permute-start.7
  57.3 5.2 %collective-permute-done.9.refs_3_ = f32[3072,128]{1,0:T(8,128)S(1)} collective-permute-done((f32[3072,128]{1,0:T(8,128)S(1)}, f32[3072,128]{1,0:T(8,128)S(1)}, u32[]{:S(2)}, u32[]{:S(2)}) %collective-permute-start.9) | collective-permute-done | bytes 1572896 | tf_op jit(solution)/shard_map/ppermute | solution.py:812
  63.3 2.2 %first.1 = (f32[16,256,128]{2,1,0:T(8,128)S(1)}, f32[16,256,128]{2,1,0:T(8,128)S(1)}, f32[1632,128]{1,0:T(8,128)S(1)}, f32[1632,128]{1,0:T(8,128)S(1)}) custom-call(f32[16,256,128]{2,1,0:T(8,128)S(1)} %bitcast.19, f32[16,256,128]{2,1,0:T(8,128)S(1)} %side_z.1.side_ref, f32[16,256,128]{2,1,0:T(8,128)S(1)} %bitcast.21, f32[16,192,128]{2,1,0:T(8,128)S(1)} %bitcast.23, ...), custom_call_target="tpu_custom_call" | custom-call | flops 16777216 | bytes 14680064 | tf_op jit(solution)/shard_map/first/pallas_call | solution.py:560
  65.7 8.3 %collective-permute-start.12 = (f32[1632,128]{1,0:T(8,128)S(1)}, f32[1632,128]{1,0:T(8,128)S(1)}, u32[]{:S(2)}, u32[]{:S(2)}) collective-permute-start(f32[1632,128]{1,0:T(8,128)S(1)} %get-tuple-element.68), channel_id=1, source_target_pairs={{0,31},{1,2},{2,1},{3,4},{4,3},{5,6},{6,5},{7,8},{8,7},{9,10},{10,... | collective-permute-start | bytes 2506760 | tf_op jit(solution)/shard_map/ppermute | solution.py:819
  75.5 2.9 %side_again.1.part_ref = f32[16,256,128]{2,1,0:T(8,128)S(1)} custom-call(f32[16,256,128]{2,1,0:T(8,128)S(1)} %get-tuple-element.67.s_ref, f32[16,256,128]{2,1,0:T(8,128)S(1)} %collective-permute-done.11.mate_ref), custom_call_target="tpu_custom_call" | custom-call | flops 33554432 | bytes 6291456 | tf_op jit(solution)/shard_map/side_again/pallas_call | solution.py:333
  78.5 2.9 %base.1.base_ref = f32[16,256,128]{2,1,0:T(8,128)S(1)} custom-call(f32[16,256,128]{2,1,0:T(8,128)S(1)} %bitcast.20, f32[16,64,128]{2,1,0:T(8,128)S(1)} %collective-permute-done.8.mid_ref, f32[16,256,128]{2,1,0:T(8,128)S(1)} %bitcast.22, f32[16,256,128]{2,1,0:T(8,128)S(1)} %bitcast.27, f32[16,256,128]{2,1,0:T(8,128)S(1)} %get-tuple-element.66.q_ref, ...), custom_call_target="tpu_custom_call" | custom-call | flops 33554432 | bytes 16777216 | tf_op jit(solution)/shard_map/base/pallas_call | solution.py:612
  81.4 11.8 %collective-permute-done.12.two_ref = f32[1632,128]{1,0:T(8,128)S(1)} collective-permute-done((f32[1632,128]{1,0:T(8,128)S(1)}, f32[1632,128]{1,0:T(8,128)S(1)}, u32[]{:S(2)}, u32[]{:S(2)}) %collective-permute-start.12) | collective-permute-done | bytes 835616 | tf_op jit(solution)/shard_map/ppermute | solution.py:819
  93.2 1.5 %collective-permute-done.13.one_ref = f32[1632,128]{1,0:T(8,128)S(1)} collective-permute-done((f32[1632,128]{1,0:T(8,128)S(1)}, f32[1632,128]{1,0:T(8,128)S(1)}, u32[]{:S(2)}, u32[]{:S(2)}) %collective-permute-start.13) | collective-permute-done | bytes 835616 | tf_op jit(solution)/shard_map/ppermute | solution.py:819
  94.6 3.9 %second.1 = (f32[16,256,128]{2,1,0:T(8,128)S(1)}, f32[64,128]{1,0:T(8,128)S(1)}, f32[64,128]{1,0:T(8,128)S(1)}) custom-call(f32[16,256,128]{2,1,0:T(8,128)S(1)} %base.1.base_ref, f32[1632,128]{1,0:T(8,128)S(1)} %collective-permute-done.12.two_ref, f32[1632,128]{1,0:T(8,128)S(1)} %collective-permute-done.13.one_ref, bf16[2,16,256,128]{3,2,1,0:T(8,128)(2,1)S(1)} %bitcast.25, ...), custom_call_target="tpu_custom_call" | custom-call | flops 134217728 | bytes 8388608 | tf_op jit(solution)/shard_map/second/pallas_call | solution.py:687
  98.6 1.2 collective-permute-done.14
  100.2 3.5 %collective-permute-done.15 = f32[64,128]{1,0:T(8,128)S(1)} collective-permute-done((f32[64,128]{1,0:T(8,128)S(1)}, f32[64,128]{1,0:T(8,128)S(1)}, u32[]{:S(2)}, u32[]{:S(2)}) %collective-permute-start.15) | collective-permute-done | bytes 32800 | tf_op jit(solution)/shard_map/ppermute | solution.py:872
  103.8 5.1 %collective-permute-done.16 = f32[64,128]{1,0:T(8,128)S(1)} collective-permute-done((f32[64,128]{1,0:T(8,128)S(1)}, f32[64,128]{1,0:T(8,128)S(1)}, u32[]{:S(2)}, u32[]{:S(2)}) %collective-permute-start.16) | collective-permute-done | bytes 32800 | tf_op jit(solution)/shard_map/ppermute | solution.py:872
  109.2 3.6 %collective-permute-done.17 = f32[64,128]{1,0:T(8,128)S(1)} collective-permute-done((f32[64,128]{1,0:T(8,128)S(1)}, f32[64,128]{1,0:T(8,128)S(1)}, u32[]{:S(2)}, u32[]{:S(2)}) %collective-permute-start.17) | collective-permute-done | bytes 32800 | tf_op jit(solution)/shard_map/ppermute | solution.py:872
  112.8 5.1 %collective-permute-done.18 = f32[64,128]{1,0:T(8,128)S(1)} collective-permute-done((f32[64,128]{1,0:T(8,128)S(1)}, f32[64,128]{1,0:T(8,128)S(1)}, u32[]{:S(2)}, u32[]{:S(2)}) %collective-permute-start.18) | collective-permute-done | bytes 32800 | tf_op jit(solution)/shard_map/ppermute | solution.py:872
  117.9 3.9 %collective-permute-done.19 = f32[64,128]{1,0:T(8,128)S(1)} collective-permute-done((f32[64,128]{1,0:T(8,128)S(1)}, f32[64,128]{1,0:T(8,128)S(1)}, u32[]{:S(2)}, u32[]{:S(2)}) %collective-permute-start.19) | collective-permute-done | bytes 32800 | tf_op jit(solution)/shard_map/ppermute | solution.py:872
  122.6 4.4 %collective-permute-done.20 = f32[64,128]{1,0:T(8,128)S(1)} collective-permute-done((f32[64,128]{1,0:T(8,128)S(1)}, f32[64,128]{1,0:T(8,128)S(1)}, u32[]{:S(2)}, u32[]{:S(2)}) %collective-permute-start.20) | collective-permute-done | bytes 32800 | tf_op jit(solution)/shard_map/ppermute | solution.py:872
  127.0 1.2 collective-permute-done.21.other_ref
  128.2 16.5 %turn.1 = f32[16,256,128]{2,1,0:T(8,128)} custom-call(f32[16,256,128]{2,1,0:T(8,128)S(1)} %get-tuple-element.74.second_ref, f32[64,128]{1,0:T(8,128)S(1)} %add.45.own_ref, f32[64,128]{1,0:T(8,128)S(1)} %collective-permute-done.21.other_ref, s32[1]{0:T(128)} %bitcast.3.rest_3_.upper_ref), custom_call_target="tpu_custom_call" | custom-call | flops 268435456 | bytes 4194304 | tf_op jit(solution)/shard_map/turn/pallas_call | solution.py:792
  (48 shorter events, 9.9 us)
Async XLA Ops:
  0.0 26.4 %collective-permute-start.3 = (f32[16,256,128]{2,1,0:T(8,128)}, f32[16,256,128]{2,1,0:T(8,128)S(1)}, u32[]{:S(2)}, u32[]{:S(2)}) collective-permute-start(f32[16,256,128]{2,1,0:T(8,128)} %bitcast.13), channel_id=1, source_target_pairs={{0,64},{1,65},{2,66},{3,67},{4,68},{5,69},{6,70},{7,71},{8,72},{9,... | collective-permute-start | bytes 6291464 | tf_op jit(solution)/shard_map/ppermute | solution.py:812
  3.8 4.0 %collective-permute-start = (f32[56,128]{1,0:T(8,128)S(1)}, f32[56,128]{1,0:T(8,128)S(1)}, u32[]{:S(2)}, u32[]{:S(2)}) collective-permute-start(f32[56,128]{1,0:T(8,128)S(1)} %stack.13.own_ref.parcel_ref), channel_id=1, source_target_pairs={{0,32},{1,33},{2,34},{3,35},{4,36},{5,37},{6,38},{7,39},{8,40},{9,... | collective-permute-start | bytes 86024 | tf_op jit(solution)/shard_map/ppermute | solution.py:812
  5.8 1.6 %copy-start = (f32[16,16,16,128]{3,2,1,0:T(8,128)S(1)}, f32[16,16,16,128]{3,2,1,0:T(8,128)}, u32[]{:S(2)}) copy-start(f32[16,16,16,128]{3,2,1,0:T(8,128)} %param.5) | copy-start | bytes 6291460
  7.8 54.6 %collective-permute-start.9 = (f32[3072,128]{1,0:T(8,128)S(1)}, f32[3072,128]{1,0:T(8,128)S(1)}, u32[]{:S(2)}, u32[]{:S(2)}) collective-permute-start(f32[3072,128]{1,0:T(8,128)S(1)} %get-tuple-element.64), channel_id=1, source_target_pairs={{0,32},{1,33},{2,34},{3,35},{4,36},{5,37},{6,38},{7,39},{8,40},{9,... | collective-permute-start | bytes 4718600 | tf_op jit(solution)/shard_map/ppermute | solution.py:812
  9.7 16.7 %collective-permute-start.4 = (f32[6,192,128]{2,1,0:T(8,128)S(1)}, f32[6,192,128]{2,1,0:T(8,128)S(1)}, u32[]{:S(2)}, u32[]{:S(2)}) collective-permute-start(f32[6,192,128]{2,1,0:T(8,128)S(1)} %get-tuple-element.53), channel_id=1, source_target_pairs={{0,33},{3,34},{4,37},{7,38},{8,41},{11,42},{12,45},{15,46},{16,49}... | collective-permute-start | bytes 1769480 | tf_op jit(solution)/shard_map/ppermute | solution.py:842
  13.3 25.6 %collective-permute-start.1 = (f32[1584,128]{1,0:T(8,128)S(1)}, f32[1584,128]{1,0:T(8,128)S(1)}, u32[]{:S(2)}, u32[]{:S(2)}) collective-permute-start(f32[1584,128]{1,0:T(8,128)S(1)} %get-tuple-element.51), channel_id=1, source_target_pairs={{0,31},{1,2},{2,1},{3,4},{4,3},{5,6},{6,5},{7,8},{8,7},{9,10},{10,... | collective-permute-start | bytes 2433032 | tf_op jit(solution)/shard_map/ppermute | solution.py:819
  21.2 21.6 %collective-permute-start.2 = (f32[1584,128]{1,0:T(8,128)S(1)}, f32[1584,128]{1,0:T(8,128)S(1)}, u32[]{:S(2)}, u32[]{:S(2)}) collective-permute-start(f32[1584,128]{1,0:T(8,128)S(1)} %get-tuple-element.52), channel_id=1, source_target_pairs={{0,1},{1,0},{2,3},{3,2},{4,5},{5,4},{6,7},{7,6},{8,9},{9,8},{10,11... | collective-permute-start | bytes 2433032 | tf_op jit(solution)/shard_map/ppermute | solution.py:819
  26.4 36.9 %collective-permute-start.10 = (f32[6,192,128]{2,1,0:T(8,128)S(1)}, f32[6,192,128]{2,1,0:T(8,128)S(1)}, u32[]{:S(2)}, u32[]{:S(2)}) collective-permute-start(f32[6,192,128]{2,1,0:T(8,128)S(1)} %collective-permute-done.4), channel_id=1, source_target_pairs={{1,0},{2,3},{5,4},{6,7},{9,8},{10,11},{13,12},{14,15},{17,16},{18,... | collective-permute-start | bytes 1769480 | tf_op jit(solution)/shard_map/ppermute | solution.py:848
  28.5 14.3 %copy-start.1 = (f32[16,16,16,128]{3,2,1,0:T(8,128)S(1)}, f32[16,16,16,128]{3,2,1,0:T(8,128)}, u32[]{:S(2)}) copy-start(f32[16,16,16,128]{3,2,1,0:T(8,128)} %param.5) | copy-start | bytes 6291460
  45.7 1.3 collective-permute-start.5
  54.9 1.3 collective-permute-start.6
  56.2 7.1 %collective-permute-start.7 = (f32[3,48,128]{2,1,0:T(8,128)S(1)}, f32[3,48,128]{2,1,0:T(8,128)S(1)}, u32[]{:S(2)}, u32[]{:S(2)}) collective-permute-start(f32[3,48,128]{2,1,0:T(8,128)S(1)} %add.38.refs_4_.rest_0_), channel_id=1, source_target_pairs={{0,32},{1,33},{2,34},{3,35},{4,36},{5,37},{6,38},{7,39},{8,40},{9,... | collective-permute-start | bytes 221192 | tf_op jit(solution)/shard_map/ppermute | solution.py:812
  65.6 9.9 %collective-permute-start.11 = (f32[16,256,128]{2,1,0:T(8,128)S(1)}, f32[16,256,128]{2,1,0:T(8,128)S(1)}, u32[]{:S(2)}, u32[]{:S(2)}) collective-permute-start(f32[16,256,128]{2,1,0:T(8,128)S(1)} %get-tuple-element.67.s_ref), channel_id=1, source_target_pairs={{0,64},{1,65},{2,66},{3,67},{4,68},{5,69},{6,70},{7,71},{8,72},{9,... | collective-permute-start | bytes 6291464 | tf_op jit(solution)/shard_map/ppermute | solution.py:812
  65.7 27.5 %collective-permute-start.12 = (f32[1632,128]{1,0:T(8,128)S(1)}, f32[1632,128]{1,0:T(8,128)S(1)}, u32[]{:S(2)}, u32[]{:S(2)}) collective-permute-start(f32[1632,128]{1,0:T(8,128)S(1)} %get-tuple-element.68), channel_id=1, source_target_pairs={{0,31},{1,2},{2,1},{3,4},{4,3},{5,6},{6,5},{7,8},{8,7},{9,10},{10,... | collective-permute-start | bytes 2506760 | tf_op jit(solution)/shard_map/ppermute | solution.py:819
  74.0 20.7 %collective-permute-start.13 = (f32[1632,128]{1,0:T(8,128)S(1)}, f32[1632,128]{1,0:T(8,128)S(1)}, u32[]{:S(2)}, u32[]{:S(2)}) collective-permute-start(f32[1632,128]{1,0:T(8,128)S(1)} %get-tuple-element.69), channel_id=1, source_target_pairs={{0,1},{1,0},{2,3},{3,2},{4,5},{5,4},{6,7},{7,6},{8,9},{9,8},{10,11... | collective-permute-start | bytes 2506760 | tf_op jit(solution)/shard_map/ppermute | solution.py:819
  74.0 4.5 %collective-permute-start.8 = (f32[16,64,128]{2,1,0:T(8,128)S(1)}, f32[16,64,128]{2,1,0:T(8,128)S(1)}, u32[]{:S(2)}, u32[]{:S(2)}) collective-permute-start(f32[16,64,128]{2,1,0:T(8,128)S(1)} %get-tuple-element.62), channel_id=1, source_target_pairs={{1,33},{2,34},{5,37},{6,38},{9,41},{10,42},{13,45},{14,46},{17,49}... | collective-permute-start | bytes 1572872 | tf_op jit(solution)/shard_map/ppermute | solution.py:863
  98.5 1.3 collective-permute-start.14
  99.8 3.9 %collective-permute-start.15 = (f32[64,128]{1,0:T(8,128)S(1)}, f32[64,128]{1,0:T(8,128)S(1)}, u32[]{:S(2)}, u32[]{:S(2)}) collective-permute-start(f32[64,128]{1,0:T(8,128)S(1)} %add.39), channel_id=1, source_target_pairs={{0,32},{1,33},{2,34},{3,35},{4,36},{5,37},{6,38},{7,39},{8,40},{9,... | collective-permute-start | bytes 98312 | tf_op jit(solution)/shard_map/ppermute | solution.py:872
  103.8 5.1 %collective-permute-start.16 = (f32[64,128]{1,0:T(8,128)S(1)}, f32[64,128]{1,0:T(8,128)S(1)}, u32[]{:S(2)}, u32[]{:S(2)}) collective-permute-start(f32[64,128]{1,0:T(8,128)S(1)} %add.40), channel_id=1, source_target_pairs={{0,36},{1,37},{2,38},{3,39},{4,32},{5,33},{6,34},{7,35},{8,44},{9,... | collective-permute-start | bytes 98312 | tf_op jit(solution)/shard_map/ppermute | solution.py:872
  108.9 3.9 %collective-permute-start.17 = (f32[64,128]{1,0:T(8,128)S(1)}, f32[64,128]{1,0:T(8,128)S(1)}, u32[]{:S(2)}, u32[]{:S(2)}) collective-permute-start(f32[64,128]{1,0:T(8,128)S(1)} %add.41), channel_id=1, source_target_pairs={{0,1},{1,0},{2,3},{3,2},{4,5},{5,4},{6,7},{7,6},{8,9},{9,8},{10,11... | collective-permute-start | bytes 98312 | tf_op jit(solution)/shard_map/ppermute | solution.py:872
  112.8 5.1 %collective-permute-start.18 = (f32[64,128]{1,0:T(8,128)S(1)}, f32[64,128]{1,0:T(8,128)S(1)}, u32[]{:S(2)}, u32[]{:S(2)}) collective-permute-start(f32[64,128]{1,0:T(8,128)S(1)} %add.42), channel_id=1, source_target_pairs={{0,3},{1,2},{2,1},{3,0},{4,7},{5,6},{6,5},{7,4},{8,11},{9,10},{10,... | collective-permute-start | bytes 98312 | tf_op jit(solution)/shard_map/ppermute | solution.py:872
  117.9 3.9 %collective-permute-start.19 = (f32[64,128]{1,0:T(8,128)S(1)}, f32[64,128]{1,0:T(8,128)S(1)}, u32[]{:S(2)}, u32[]{:S(2)}) collective-permute-start(f32[64,128]{1,0:T(8,128)S(1)} %add.43), channel_id=1, source_target_pairs={{0,8},{1,9},{2,10},{3,11},{4,12},{5,13},{6,14},{7,15},{8,0},{9,1},... | collective-permute-start | bytes 98312 | tf_op jit(solution)/shard_map/ppermute | solution.py:872
  121.9 5.1 %collective-permute-start.20 = (f32[64,128]{1,0:T(8,128)S(1)}, f32[64,128]{1,0:T(8,128)S(1)}, u32[]{:S(2)}, u32[]{:S(2)}) collective-permute-start(f32[64,128]{1,0:T(8,128)S(1)} %add.44), channel_id=1, source_target_pairs={{0,24},{1,25},{2,26},{3,27},{4,28},{5,29},{6,30},{7,31},{8,16},{9,... | collective-permute-start | bytes 98312 | tf_op jit(solution)/shard_map/ppermute | solution.py:872
  127.0 1.2 collective-permute-start.21

commit v22 on v19

--- a/solution.py
+++ b/solution.py
@@ -220,13 +220,31 @@
     )(s, odd, parcel, parcel_mate)
 
 
-def stack_kernel(atoms_ref, pot_ref, out_ref):
-    out_ref[0:24, :] = atoms_ref[...]
+def stack_kernel(shape_ref, pot_ref, sites_ref, energies_ref, out_ref, row_ref):
+    row_ref[...] = jnp.zeros((4, 768), F32)
+    row_ref[:, :TAPS] = shape_ref[...]
+    lane = lax.broadcasted_iota(jnp.int32, (1, S), 1) + 5 * S
+    for atom in range(4):
+        for block in range(6):
+            row = row_ref[atom : atom + 1, block * S : block * S + S]
+            if block == 5:
+                for d in range(3):
+                    row = jnp.where(lane == TAPS + d, sites_ref[atom, d].astype(F32), row)
+                row = jnp.where(lane == TAPS + 3, energies_ref[atom], row)
+            out_ref[atom * 6 + block : atom * 6 + block + 1, :] = row
     out_ref[24:56, :] = pot_ref[...]
 
 
-def stack(atoms, pot):
-    return pl.pallas_call(stack_kernel, out_shape=sds((56, S)), compiler_params=params(4), name="stack")(atoms, pot)
+def stack(shapes, pot, sites, energies):
+    vmem = pl.BlockSpec(memory_space=pltpu.VMEM)
+    return pl.pallas_call(
+        stack_kernel,
+        in_specs=[vmem, vmem, SCALARS, SCALARS],
+        out_shape=sds((56, S)),
+        scratch_shapes=[pltpu.VMEM((4, 768), F32)],
+        compiler_params=params(4),
+        name="stack",
+    )(shapes, pot, sites, energies)
 
 
 def column_kernel(own_ref, other_ref, one_ref, two_ref, odd_ref, out_ref):
@@ -827,12 +845,9 @@
     upper = gx.astype(jnp.int32).reshape(1)
     odd = (lax.axis_index("gzs") % 2).astype(jnp.int32).reshape(1)
     pot = potential.reshape(32, 128)
-    atoms = jnp.concatenate(
-        [projectors.reshape(4, TAPS), atom_sites.astype(F32), energies[:, None], jnp.zeros((4, 768 - TAPS - 4), F32)],
-        axis=1,
-    ).reshape(24, 128)
-    pot, corner, upper, inner, odd, atoms = barrier((pot, corner, upper, inner, odd, atoms))
-    parcel = stack(atoms, pot)
+    shapes = projectors.reshape(4, TAPS)
+    pot, corner, upper, inner, odd, shapes = barrier((pot, corner, upper, inner, odd, shapes))
+    parcel = stack(shapes, pot, atom_sites, energies)
     to_pack, parcel = barrier((s, parcel))
     parcel_mate = send(parcel, over_y)
     message, relay, mid = pack(to_pack, inner)

time: 145 us -> 145 us (level)
    unnamed x5 -> x9, local copies, waits for them, and re-layouts: 2.54 us -> 3.88 us
  transfers between devices with their start and end apart: 22 -> 22, of which waited for: 17 -> 17; matrix products, arithmetic and copies ran while one was open for 3% -> 2% of each run, Pallas kernels for 14% -> 15%
where the time goes in v22:
time: 145 us; the launch traced here: 144 us
  waiting for transfers between devices  64.6 us (45%)
  Pallas kernels  43.7 us (30%)
  starting transfers between devices  29.9 us (21%)
  local copies, waits for them, and re-layouts  5.04 us (3%)
    ppermute x4, waiting for transfers between devices, to_pairs(): return (lax.ppermute(one, AXES, near), lax.ppermute(two, AXES, far))  24.5 us
    ppermute x6, waiting for transfers between devices, per_device(): own = own + lax.ppermute(own, AXES, [(d, d ^ flip) for d in range(count)])  24.1 us
    pallas_call x1, Pallas kernels, turn(): pl.pallas_call(turn_kernel, grid=(STEPS,), in_specs=[plane_spec(), whole(...  16.5 us
    ppermute x4, starting transfers between devices, to_pairs(): return (lax.ppermute(one, AXES, near), lax.ppermute(two, AXES, far))  16.4 us
    ppermute x9, waiting for transfers between devices, send(): return lax.ppermute(value, AXES, [(d, d ^ flip) for d in range(count)])  10.9 us
    pallas_call x1, Pallas kernels, prep(): pl.pallas_call(prep_kernel, in_specs=[vmem] * 2 + [pl.BlockSpec(memory_sp...  7.8 us
    ppermute x9, starting transfers between devices, send(): return lax.ppermute(value, AXES, [(d, d ^ flip) for d in range(count)])  5.55 us
    ppermute x1, waiting for transfers between devices, per_device(): lax.ppermute(relay, AXES, [(d, d ^ over_y ^ 1) for d in outer_ones])  5.14 us
  transfers between devices with their start and end apart: 22, of which 17 were waited for; matrix products, arithmetic and copies ran while one was open for 2% of the time, Pallas kernels for 15%

profile of v22, /device:TPU:0, one launch (start us, length us, event | category | flops | bytes accessed | tf_op | source)
XLA Modules:
  0.0 143.6 jit_solution(16145784486708018438)
XLA Ops:
  4.1 2.1 %collective-permute-start = (f32[56,128]{1,0:T(8,128)S(1)}, f32[56,128]{1,0:T(8,128)S(1)}, u32[]{:S(2)}, u32[]{:S(2)}) collective-permute-start(f32[56,128]{1,0:T(8,128)S(1)} %stack.13.own_ref.parcel_ref), channel_id=1, source_target_pairs={{0,32},{1,33},{2,34},{3,35},{4,36},{5,37},{6,38},{7,39},{8,40},{9,... | collective-permute-start | bytes 86024 | tf_op jit(solution)/shard_map/ppermute | solution.py:830
  6.2 1.6 %copy-done = f32[16,16,16,128]{3,2,1,0:T(8,128)S(1)} copy-done((f32[16,16,16,128]{3,2,1,0:T(8,128)S(1)}, f32[16,16,16,128]{3,2,1,0:T(8,128)}, u32[]{:S(2)}) %copy-start) | copy-done | bytes 2097176
  8.2 1.9 %collective-permute-start.9 = (f32[3072,128]{1,0:T(8,128)S(1)}, f32[3072,128]{1,0:T(8,128)S(1)}, u32[]{:S(2)}, u32[]{:S(2)}) collective-permute-start(f32[3072,128]{1,0:T(8,128)S(1)} %get-tuple-element.64), channel_id=1, source_target_pairs={{0,32},{1,33},{2,34},{3,35},{4,36},{5,37},{6,38},{7,39},{8,40},{9,... | collective-permute-start | bytes 4718600 | tf_op jit(solution)/shard_map/ppermute | solution.py:830
  10.1 3.0 %collective-permute-start.4 = (f32[6,192,128]{2,1,0:T(8,128)S(1)}, f32[6,192,128]{2,1,0:T(8,128)S(1)}, u32[]{:S(2)}, u32[]{:S(2)}) collective-permute-start(f32[6,192,128]{2,1,0:T(8,128)S(1)} %get-tuple-element.53), channel_id=1, source_target_pairs={{0,33},{3,34},{4,37},{7,38},{8,41},{11,42},{12,45},{15,46},{16,49}... | collective-permute-start | bytes 1769480 | tf_op jit(solution)/shard_map/ppermute | solution.py:857
  13.8 7.9 %collective-permute-start.2 = (f32[1584,128]{1,0:T(8,128)S(1)}, f32[1584,128]{1,0:T(8,128)S(1)}, u32[]{:S(2)}, u32[]{:S(2)}) collective-permute-start(f32[1584,128]{1,0:T(8,128)S(1)} %get-tuple-element.52), channel_id=1, source_target_pairs={{0,31},{1,2},{2,1},{3,4},{4,3},{5,6},{6,5},{7,8},{8,7},{9,10},{10,... | collective-permute-start | bytes 2433032 | tf_op jit(solution)/shard_map/ppermute | solution.py:837
  21.7 5.1 %collective-permute-done.4 = f32[6,192,128]{2,1,0:T(8,128)S(1)} collective-permute-done((f32[6,192,128]{2,1,0:T(8,128)S(1)}, f32[6,192,128]{2,1,0:T(8,128)S(1)}, u32[]{:S(2)}, u32[]{:S(2)}) %collective-permute-start.4) | collective-permute-done | bytes 589856 | tf_op jit(solution)/shard_map/ppermute | solution.py:857
  26.8 1.3 collective-permute-start.10
  28.9 1.5 %side_x.1.part_ref = f32[16,256,128]{2,1,0:T(8,128)S(1)} custom-call(f32[16,256,128]{2,1,0:T(8,128)S(1)} %bitcast.15, f32[16,256,128]{2,1,0:T(8,128)S(1)} %collective-permute-done.3.mate_ref), custom_call_target="tpu_custom_call" | custom-call | flops 16777216 | bytes 6291456 | tf_op jit(solution)/shard_map/side_x/pallas_call | solution.py:295
  30.4 12.8 %collective-permute-done.1.one_ref = f32[1584,128]{1,0:T(8,128)S(1)} collective-permute-done((f32[1584,128]{1,0:T(8,128)S(1)}, f32[1584,128]{1,0:T(8,128)S(1)}, u32[]{:S(2)}, u32[]{:S(2)}) %collective-permute-start.1) | collective-permute-done | bytes 811040 | tf_op jit(solution)/shard_map/ppermute | solution.py:837
  43.2 2.9 %side_z.1.side_ref = f32[16,256,128]{2,1,0:T(8,128)S(1)} custom-call(f32[16,256,128]{2,1,0:T(8,128)S(1)} %bitcast.16, f32[16,256,128]{2,1,0:T(8,128)S(1)} %side_x.1.part_ref, f32[1584,128]{1,0:T(8,128)S(1)} %collective-permute-done.1.one_ref, f32[1584,128]{1,0:T(8,128)S(1)} %collective-permute-done.2.two_ref, s32[1]{0:T(128)} %bitcast.5.odd_ref.refs_3_.rest_4_), custom_call_target="tpu_custom_call" | custom-call | flops 16777216 | bytes 8388608 | tf_op jit(solution)/shard_map/side_z/pallas_call | solution.py:323
  46.2 1.3 collective-permute-done.5.refs_1_
  47.4 7.8 %prep.1 = (bf16[2,4096,128]{2,1,0:T(8,128)(2,1)S(1)}, f32[3,48,128]{2,1,0:T(8,128)S(1)}, f32[48,128]{1,0:T(8,128)S(1)}) custom-call(f32[144,128]{1,0:T(8,128)S(1)} %column.1.refs_0_, f32[144,128]{1,0:T(8,128)S(1)} %collective-permute-done.5.refs_1_, s32[2]{0:T(128)S(1)} %pad_add_fusion.refs_2_, f32[4096,128]{1,0:T(8,128)S(1)} %spread.2.refs_3_, ...), custom_call_target="tpu_custom_call" | custom-call | flops 134217728 | bytes 10485760 | tf_op jit(solution)/shard_map/prep/pallas_call | solution.py:511
  55.5 1.1 collective-permute-done.6
  56.6 1.1 collective-permute-start.7
  57.7 5.1 %collective-permute-done.9.refs_3_ = f32[3072,128]{1,0:T(8,128)S(1)} collective-permute-done((f32[3072,128]{1,0:T(8,128)S(1)}, f32[3072,128]{1,0:T(8,128)S(1)}, u32[]{:S(2)}, u32[]{:S(2)}) %collective-permute-start.9) | collective-permute-done | bytes 1572896 | tf_op jit(solution)/shard_map/ppermute | solution.py:830
  63.7 2.2 %first.1 = (f32[16,256,128]{2,1,0:T(8,128)S(1)}, f32[16,256,128]{2,1,0:T(8,128)S(1)}, f32[1632,128]{1,0:T(8,128)S(1)}, f32[1632,128]{1,0:T(8,128)S(1)}) custom-call(f32[16,256,128]{2,1,0:T(8,128)S(1)} %bitcast.18, f32[16,256,128]{2,1,0:T(8,128)S(1)} %side_z.1.side_ref, f32[16,256,128]{2,1,0:T(8,128)S(1)} %bitcast.20, f32[16,192,128]{2,1,0:T(8,128)S(1)} %bitcast.22, ...), custom_call_target="tpu_custom_call" | custom-call | flops 16777216 | bytes 14680064 | tf_op jit(solution)/shard_map/first/pallas_call | solution.py:578
  66.2 8.3 %collective-permute-start.13 = (f32[1632,128]{1,0:T(8,128)S(1)}, f32[1632,128]{1,0:T(8,128)S(1)}, u32[]{:S(2)}, u32[]{:S(2)}) collective-permute-start(f32[1632,128]{1,0:T(8,128)S(1)} %get-tuple-element.69), channel_id=1, source_target_pairs={{0,31},{1,2},{2,1},{3,4},{4,3},{5,6},{6,5},{7,8},{8,7},{9,10},{10,... | collective-permute-start | bytes 2506760 | tf_op jit(solution)/shard_map/ppermute | solution.py:837
  76.0 2.9 %side_again.1.part_ref = f32[16,256,128]{2,1,0:T(8,128)S(1)} custom-call(f32[16,256,128]{2,1,0:T(8,128)S(1)} %get-tuple-element.67.s_ref, f32[16,256,128]{2,1,0:T(8,128)S(1)} %collective-permute-done.11.mate_ref), custom_call_target="tpu_custom_call" | custom-call | flops 33554432 | bytes 6291456 | tf_op jit(solution)/shard_map/side_again/pallas_call | solution.py:351
  78.9 2.9 %base.1.base_ref = f32[16,256,128]{2,1,0:T(8,128)S(1)} custom-call(f32[16,256,128]{2,1,0:T(8,128)S(1)} %bitcast.19, f32[16,64,128]{2,1,0:T(8,128)S(1)} %collective-permute-done.8.mid_ref, f32[16,256,128]{2,1,0:T(8,128)S(1)} %bitcast.21, f32[16,256,128]{2,1,0:T(8,128)S(1)} %bitcast.26, f32[16,256,128]{2,1,0:T(8,128)S(1)} %get-tuple-element.66.q_ref, ...), custom_call_target="tpu_custom_call" | custom-call | flops 33554432 | bytes 16777216 | tf_op jit(solution)/shard_map/base/pallas_call | solution.py:630
  81.9 5.2 %collective-permute-done.12.one_ref = f32[1632,128]{1,0:T(8,128)S(1)} collective-permute-done((f32[1632,128]{1,0:T(8,128)S(1)}, f32[1632,128]{1,0:T(8,128)S(1)}, u32[]{:S(2)}, u32[]{:S(2)}) %collective-permute-start.12) | collective-permute-done | bytes 835616 | tf_op jit(solution)/shard_map/ppermute | solution.py:837
  87.1 6.5 %collective-permute-done.13.two_ref = f32[1632,128]{1,0:T(8,128)S(1)} collective-permute-done((f32[1632,128]{1,0:T(8,128)S(1)}, f32[1632,128]{1,0:T(8,128)S(1)}, u32[]{:S(2)}, u32[]{:S(2)}) %collective-permute-start.13) | collective-permute-done | bytes 835616 | tf_op jit(solution)/shard_map/ppermute | solution.py:837
  93.5 3.9 %second.1 = (f32[16,256,128]{2,1,0:T(8,128)S(1)}, f32[64,128]{1,0:T(8,128)S(1)}, f32[64,128]{1,0:T(8,128)S(1)}) custom-call(f32[16,256,128]{2,1,0:T(8,128)S(1)} %base.1.base_ref, f32[1632,128]{1,0:T(8,128)S(1)} %collective-permute-done.12.one_ref, f32[1632,128]{1,0:T(8,128)S(1)} %collective-permute-done.13.two_ref, bf16[2,16,256,128]{3,2,1,0:T(8,128)(2,1)S(1)} %bitcast.24, ...), custom_call_target="tpu_custom_call" | custom-call | flops 134217728 | bytes 8388608 | tf_op jit(solution)/shard_map/second/pallas_call | solution.py:705
  97.5 1.2 collective-permute-done.14
  99.1 3.5 %collective-permute-done.15 = f32[64,128]{1,0:T(8,128)S(1)} collective-permute-done((f32[64,128]{1,0:T(8,128)S(1)}, f32[64,128]{1,0:T(8,128)S(1)}, u32[]{:S(2)}, u32[]{:S(2)}) %collective-permute-start.15) | collective-permute-done | bytes 32800 | tf_op jit(solution)/shard_map/ppermute | solution.py:887
  102.9 4.9 %collective-permute-done.16 = f32[64,128]{1,0:T(8,128)S(1)} collective-permute-done((f32[64,128]{1,0:T(8,128)S(1)}, f32[64,128]{1,0:T(8,128)S(1)}, u32[]{:S(2)}, u32[]{:S(2)}) %collective-permute-start.16) | collective-permute-done | bytes 32800 | tf_op jit(solution)/shard_map/ppermute | solution.py:887
  107.8 3.9 %collective-permute-done.17 = f32[64,128]{1,0:T(8,128)S(1)} collective-permute-done((f32[64,128]{1,0:T(8,128)S(1)}, f32[64,128]{1,0:T(8,128)S(1)}, u32[]{:S(2)}, u32[]{:S(2)}) %collective-permute-start.17) | collective-permute-done | bytes 32800 | tf_op jit(solution)/shard_map/ppermute | solution.py:887
  112.4 4.4 %collective-permute-done.18 = f32[64,128]{1,0:T(8,128)S(1)} collective-permute-done((f32[64,128]{1,0:T(8,128)S(1)}, f32[64,128]{1,0:T(8,128)S(1)}, u32[]{:S(2)}, u32[]{:S(2)}) %collective-permute-start.18) | collective-permute-done | bytes 32800 | tf_op jit(solution)/shard_map/ppermute | solution.py:887
  116.9 3.9 %collective-permute-done.19 = f32[64,128]{1,0:T(8,128)S(1)} collective-permute-done((f32[64,128]{1,0:T(8,128)S(1)}, f32[64,128]{1,0:T(8,128)S(1)}, u32[]{:S(2)}, u32[]{:S(2)}) %collective-permute-start.19) | collective-permute-done | bytes 32800 | tf_op jit(solution)/shard_map/ppermute | solution.py:887
  120.8 1.7 %collective-permute-start.20 = (f32[64,128]{1,0:T(8,128)S(1)}, f32[64,128]{1,0:T(8,128)S(1)}, u32[]{:S(2)}, u32[]{:S(2)}) collective-permute-start(f32[64,128]{1,0:T(8,128)S(1)} %add.44), channel_id=1, source_target_pairs={{0,24},{1,25},{2,26},{3,27},{4,28},{5,29},{6,30},{7,31},{8,16},{9,... | collective-permute-start | bytes 98312 | tf_op jit(solution)/shard_map/ppermute | solution.py:887
  122.4 3.5 %collective-permute-done.20 = f32[64,128]{1,0:T(8,128)S(1)} collective-permute-done((f32[64,128]{1,0:T(8,128)S(1)}, f32[64,128]{1,0:T(8,128)S(1)}, u32[]{:S(2)}, u32[]{:S(2)}) %collective-permute-start.20) | collective-permute-done | bytes 32800 | tf_op jit(solution)/shard_map/ppermute | solution.py:887
  125.9 1.2 collective-permute-done.21.other_ref
  127.1 16.5 %turn.1 = f32[16,256,128]{2,1,0:T(8,128)} custom-call(f32[16,256,128]{2,1,0:T(8,128)S(1)} %get-tuple-element.74.second_ref, f32[64,128]{1,0:T(8,128)S(1)} %add.45.own_ref, f32[64,128]{1,0:T(8,128)S(1)} %collective-permute-done.21.other_ref, s32[1]{0:T(128)} %bitcast.3.rest_3_.upper_ref), custom_call_target="tpu_custom_call" | custom-call | flops 268435456 | bytes 4194304 | tf_op jit(solution)/shard_map/turn/pallas_call | solution.py:810
  (46 shorter events, 10.3 us)
Async XLA Ops:
  0.0 26.8 %collective-permute-start.3 = (f32[16,256,128]{2,1,0:T(8,128)}, f32[16,256,128]{2,1,0:T(8,128)S(1)}, u32[]{:S(2)}, u32[]{:S(2)}) collective-permute-start(f32[16,256,128]{2,1,0:T(8,128)} %bitcast.12), channel_id=1, source_target_pairs={{0,64},{1,65},{2,66},{3,67},{4,68},{5,69},{6,70},{7,71},{8,72},{9,... | collective-permute-start | bytes 6291464 | tf_op jit(solution)/shard_map/ppermute | solution.py:830
  2.2 0.7 copy-start.2
  2.9 0.7 copy-start.3
  4.1 4.1 %collective-permute-start = (f32[56,128]{1,0:T(8,128)S(1)}, f32[56,128]{1,0:T(8,128)S(1)}, u32[]{:S(2)}, u32[]{:S(2)}) collective-permute-start(f32[56,128]{1,0:T(8,128)S(1)} %stack.13.own_ref.parcel_ref), channel_id=1, source_target_pairs={{0,32},{1,33},{2,34},{3,35},{4,36},{5,37},{6,38},{7,39},{8,40},{9,... | collective-permute-start | bytes 86024 | tf_op jit(solution)/shard_map/ppermute | solution.py:830
  6.2 1.6 %copy-start = (f32[16,16,16,128]{3,2,1,0:T(8,128)S(1)}, f32[16,16,16,128]{3,2,1,0:T(8,128)}, u32[]{:S(2)}) copy-start(f32[16,16,16,128]{3,2,1,0:T(8,128)} %param.5) | copy-start | bytes 6291460
  8.2 54.6 %collective-permute-start.9 = (f32[3072,128]{1,0:T(8,128)S(1)}, f32[3072,128]{1,0:T(8,128)S(1)}, u32[]{:S(2)}, u32[]{:S(2)}) collective-permute-start(f32[3072,128]{1,0:T(8,128)S(1)} %get-tuple-element.64), channel_id=1, source_target_pairs={{0,32},{1,33},{2,34},{3,35},{4,36},{5,37},{6,38},{7,39},{8,40},{9,... | collective-permute-start | bytes 4718600 | tf_op jit(solution)/shard_map/ppermute | solution.py:830
  10.1 16.7 %collective-permute-start.4 = (f32[6,192,128]{2,1,0:T(8,128)S(1)}, f32[6,192,128]{2,1,0:T(8,128)S(1)}, u32[]{:S(2)}, u32[]{:S(2)}) collective-permute-start(f32[6,192,128]{2,1,0:T(8,128)S(1)} %get-tuple-element.53), channel_id=1, source_target_pairs={{0,33},{3,34},{4,37},{7,38},{8,41},{11,42},{12,45},{15,46},{16,49}... | collective-permute-start | bytes 1769480 | tf_op jit(solution)/shard_map/ppermute | solution.py:857
  13.7 29.5 %collective-permute-start.1 = (f32[1584,128]{1,0:T(8,128)S(1)}, f32[1584,128]{1,0:T(8,128)S(1)}, u32[]{:S(2)}, u32[]{:S(2)}) collective-permute-start(f32[1584,128]{1,0:T(8,128)S(1)} %get-tuple-element.51), channel_id=1, source_target_pairs={{0,1},{1,0},{2,3},{3,2},{4,5},{5,4},{6,7},{7,6},{8,9},{9,8},{10,11... | collective-permute-start | bytes 2433032 | tf_op jit(solution)/shard_map/ppermute | solution.py:837
  13.8 29.4 %collective-permute-start.2 = (f32[1584,128]{1,0:T(8,128)S(1)}, f32[1584,128]{1,0:T(8,128)S(1)}, u32[]{:S(2)}, u32[]{:S(2)}) collective-permute-start(f32[1584,128]{1,0:T(8,128)S(1)} %get-tuple-element.52), channel_id=1, source_target_pairs={{0,31},{1,2},{2,1},{3,4},{4,3},{5,6},{6,5},{7,8},{8,7},{9,10},{10,... | collective-permute-start | bytes 2433032 | tf_op jit(solution)/shard_map/ppermute | solution.py:837
  26.8 36.9 %collective-permute-start.10 = (f32[6,192,128]{2,1,0:T(8,128)S(1)}, f32[6,192,128]{2,1,0:T(8,128)S(1)}, u32[]{:S(2)}, u32[]{:S(2)}) collective-permute-start(f32[6,192,128]{2,1,0:T(8,128)S(1)} %collective-permute-done.4), channel_id=1, source_target_pairs={{1,0},{2,3},{5,4},{6,7},{9,8},{10,11},{13,12},{14,15},{17,16},{18,... | collective-permute-start | bytes 1769480 | tf_op jit(solution)/shard_map/ppermute | solution.py:863
  28.9 14.3 %copy-start.1 = (f32[16,16,16,128]{3,2,1,0:T(8,128)S(1)}, f32[16,16,16,128]{3,2,1,0:T(8,128)}, u32[]{:S(2)}) copy-start(f32[16,16,16,128]{3,2,1,0:T(8,128)} %param.5) | copy-start | bytes 6291460
  46.1 1.3 collective-permute-start.5
  55.2 1.3 collective-permute-start.6
  56.6 7.1 %collective-permute-start.7 = (f32[3,48,128]{2,1,0:T(8,128)S(1)}, f32[3,48,128]{2,1,0:T(8,128)S(1)}, u32[]{:S(2)}, u32[]{:S(2)}) collective-permute-start(f32[3,48,128]{2,1,0:T(8,128)S(1)} %add.38.refs_4_.rest_0_), channel_id=1, source_target_pairs={{0,32},{1,33},{2,34},{3,35},{4,36},{5,37},{6,38},{7,39},{8,40},{9,... | collective-permute-start | bytes 221192 | tf_op jit(solution)/shard_map/ppermute | solution.py:830
  66.0 10.0 %collective-permute-start.11 = (f32[16,256,128]{2,1,0:T(8,128)S(1)}, f32[16,256,128]{2,1,0:T(8,128)S(1)}, u32[]{:S(2)}, u32[]{:S(2)}) collective-permute-start(f32[16,256,128]{2,1,0:T(8,128)S(1)} %get-tuple-element.67.s_ref), channel_id=1, source_target_pairs={{0,64},{1,65},{2,66},{3,67},{4,68},{5,69},{6,70},{7,71},{8,72},{9,... | collective-permute-start | bytes 6291464 | tf_op jit(solution)/shard_map/ppermute | solution.py:830
  66.1 21.0 %collective-permute-start.12 = (f32[1632,128]{1,0:T(8,128)S(1)}, f32[1632,128]{1,0:T(8,128)S(1)}, u32[]{:S(2)}, u32[]{:S(2)}) collective-permute-start(f32[1632,128]{1,0:T(8,128)S(1)} %get-tuple-element.68), channel_id=1, source_target_pairs={{0,1},{1,0},{2,3},{3,2},{4,5},{5,4},{6,7},{7,6},{8,9},{9,8},{10,11... | collective-permute-start | bytes 2506760 | tf_op jit(solution)/shard_map/ppermute | solution.py:837
  66.2 27.4 %collective-permute-start.13 = (f32[1632,128]{1,0:T(8,128)S(1)}, f32[1632,128]{1,0:T(8,128)S(1)}, u32[]{:S(2)}, u32[]{:S(2)}) collective-permute-start(f32[1632,128]{1,0:T(8,128)S(1)} %get-tuple-element.69), channel_id=1, source_target_pairs={{0,31},{1,2},{2,1},{3,4},{4,3},{5,6},{6,5},{7,8},{8,7},{9,10},{10,... | collective-permute-start | bytes 2506760 | tf_op jit(solution)/shard_map/ppermute | solution.py:837
  74.5 4.5 %collective-permute-start.8 = (f32[16,64,128]{2,1,0:T(8,128)S(1)}, f32[16,64,128]{2,1,0:T(8,128)S(1)}, u32[]{:S(2)}, u32[]{:S(2)}) collective-permute-start(f32[16,64,128]{2,1,0:T(8,128)S(1)} %get-tuple-element.62), channel_id=1, source_target_pairs={{1,33},{2,34},{5,37},{6,38},{9,41},{10,42},{13,45},{14,46},{17,49}... | collective-permute-start | bytes 1572872 | tf_op jit(solution)/shard_map/ppermute | solution.py:878
  97.4 1.3 collective-permute-start.14
  98.7 3.9 %collective-permute-start.15 = (f32[64,128]{1,0:T(8,128)S(1)}, f32[64,128]{1,0:T(8,128)S(1)}, u32[]{:S(2)}, u32[]{:S(2)}) collective-permute-start(f32[64,128]{1,0:T(8,128)S(1)} %add.39), channel_id=1, source_target_pairs={{0,32},{1,33},{2,34},{3,35},{4,36},{5,37},{6,38},{7,39},{8,40},{9,... | collective-permute-start | bytes 98312 | tf_op jit(solution)/shard_map/ppermute | solution.py:887
  102.7 5.1 %collective-permute-start.16 = (f32[64,128]{1,0:T(8,128)S(1)}, f32[64,128]{1,0:T(8,128)S(1)}, u32[]{:S(2)}, u32[]{:S(2)}) collective-permute-start(f32[64,128]{1,0:T(8,128)S(1)} %add.40), channel_id=1, source_target_pairs={{0,36},{1,37},{2,38},{3,39},{4,32},{5,33},{6,34},{7,35},{8,44},{9,... | collective-permute-start | bytes 98312 | tf_op jit(solution)/shard_map/ppermute | solution.py:887
  107.8 3.9 %collective-permute-start.17 = (f32[64,128]{1,0:T(8,128)S(1)}, f32[64,128]{1,0:T(8,128)S(1)}, u32[]{:S(2)}, u32[]{:S(2)}) collective-permute-start(f32[64,128]{1,0:T(8,128)S(1)} %add.41), channel_id=1, source_target_pairs={{0,1},{1,0},{2,3},{3,2},{4,5},{5,4},{6,7},{7,6},{8,9},{9,8},{10,11... | collective-permute-start | bytes 98312 | tf_op jit(solution)/shard_map/ppermute | solution.py:887
  111.7 5.1 %collective-permute-start.18 = (f32[64,128]{1,0:T(8,128)S(1)}, f32[64,128]{1,0:T(8,128)S(1)}, u32[]{:S(2)}, u32[]{:S(2)}) collective-permute-start(f32[64,128]{1,0:T(8,128)S(1)} %add.42), channel_id=1, source_target_pairs={{0,3},{1,2},{2,1},{3,0},{4,7},{5,6},{6,5},{7,4},{8,11},{9,10},{10,... | collective-permute-start | bytes 98312 | tf_op jit(solution)/shard_map/ppermute | solution.py:887
  116.8 3.9 %collective-permute-start.19 = (f32[64,128]{1,0:T(8,128)S(1)}, f32[64,128]{1,0:T(8,128)S(1)}, u32[]{:S(2)}, u32[]{:S(2)}) collective-permute-start(f32[64,128]{1,0:T(8,128)S(1)} %add.43), channel_id=1, source_target_pairs={{0,8},{1,9},{2,10},{3,11},{4,12},{5,13},{6,14},{7,15},{8,0},{9,1},... | collective-permute-start | bytes 98312 | tf_op jit(solution)/shard_map/ppermute | solution.py:887
  120.8 5.1 %collective-permute-start.20 = (f32[64,128]{1,0:T(8,128)S(1)}, f32[64,128]{1,0:T(8,128)S(1)}, u32[]{:S(2)}, u32[]{:S(2)}) collective-permute-start(f32[64,128]{1,0:T(8,128)S(1)} %add.44), channel_id=1, source_target_pairs={{0,24},{1,25},{2,26},{3,27},{4,28},{5,29},{6,30},{7,31},{8,16},{9,... | collective-permute-start | bytes 98312 | tf_op jit(solution)/shard_map/ppermute | solution.py:887
  125.9 1.2 collective-permute-start.21

commit v23 on v19

--- a/solution.py
+++ b/solution.py
@@ -868,7 +868,7 @@
     second, own, give = make_second(base, halos, gg, [part, part_mate, energy], upper, odd)
 
     own = own + send(give, over_x)
-    for flip in (32, 36, 1, 3, 8, 24):
+    for flip in (1, 3, 8, 24, 32, 36):
         own = own + lax.ppermute(own, AXES, [(d, d ^ flip) for d in range(count)])
     return turn(second, own, send(own, over_x), upper).reshape(C, C, C, S)
 

time: 145 us -> 145 us (level)
  no operation moved by 1% of the time
where the time goes in v23:
time: 145 us; the launch traced here: 143 us
  waiting for transfers between devices  64.5 us (44%)
  Pallas kernels  43.1 us (30%)
  starting transfers between devices  30 us (21%)
  local copies, waits for them, and re-layouts  4.53 us (3%)
    ppermute x4, waiting for transfers between devices, to_pairs(): return (lax.ppermute(one, AXES, near), lax.ppermute(two, AXES, far))  24.5 us
    ppermute x6, waiting for transfers between devices, per_device(): own = own + lax.ppermute(own, AXES, [(d, d ^ flip) for d in range(count)])  24 us
    pallas_call x1, Pallas kernels, turn(): pl.pallas_call(turn_kernel, grid=(STEPS,), in_specs=[plane_spec(), whole(...  16.5 us
    ppermute x4, starting transfers between devices, to_pairs(): return (lax.ppermute(one, AXES, near), lax.ppermute(two, AXES, far))  16.4 us
    ppermute x9, waiting for transfers between devices, send(): return lax.ppermute(value, AXES, [(d, d ^ flip) for d in range(count)])  10.9 us
    pallas_call x1, Pallas kernels, prep(): pl.pallas_call(prep_kernel, in_specs=[vmem] * 2 + [pl.BlockSpec(memory_sp...  7.8 us
    ppermute x9, starting transfers between devices, send(): return lax.ppermute(value, AXES, [(d, d ^ flip) for d in range(count)])  5.5 us
    ppermute x1, waiting for transfers between devices, per_device(): lax.ppermute(relay, AXES, [(d, d ^ over_y ^ 1) for d in outer_ones])  5.14 us
  transfers between devices with their start and end apart: 22, of which 17 were waited for; matrix products, arithmetic and copies ran while one was open for 3% of the time, Pallas kernels for 14%

profile of v23, /device:TPU:0, one launch (start us, length us, event | category | flops | bytes accessed | tf_op | source)
XLA Modules:
  0.0 143.2 jit_solution(18434677304642789386)
XLA Ops:
  3.8 2.0 %collective-permute-start = (f32[56,128]{1,0:T(8,128)S(1)}, f32[56,128]{1,0:T(8,128)S(1)}, u32[]{:S(2)}, u32[]{:S(2)}) collective-permute-start(f32[56,128]{1,0:T(8,128)S(1)} %stack.13.own_ref.parcel_ref), channel_id=1, source_target_pairs={{0,32},{1,33},{2,34},{3,35},{4,36},{5,37},{6,38},{7,39},{8,40},{9,... | collective-permute-start | bytes 86024 | tf_op jit(solution)/shard_map/ppermute | solution.py:812
  5.8 1.6 %copy-done = f32[16,16,16,128]{3,2,1,0:T(8,128)S(1)} copy-done((f32[16,16,16,128]{3,2,1,0:T(8,128)S(1)}, f32[16,16,16,128]{3,2,1,0:T(8,128)}, u32[]{:S(2)}) %copy-start) | copy-done | bytes 2097176
  7.8 1.9 %collective-permute-start.9 = (f32[3072,128]{1,0:T(8,128)S(1)}, f32[3072,128]{1,0:T(8,128)S(1)}, u32[]{:S(2)}, u32[]{:S(2)}) collective-permute-start(f32[3072,128]{1,0:T(8,128)S(1)} %get-tuple-element.64), channel_id=1, source_target_pairs={{0,32},{1,33},{2,34},{3,35},{4,36},{5,37},{6,38},{7,39},{8,40},{9,... | collective-permute-start | bytes 4718600 | tf_op jit(solution)/shard_map/ppermute | solution.py:812
  9.7 3.0 %collective-permute-start.4 = (f32[6,192,128]{2,1,0:T(8,128)S(1)}, f32[6,192,128]{2,1,0:T(8,128)S(1)}, u32[]{:S(2)}, u32[]{:S(2)}) collective-permute-start(f32[6,192,128]{2,1,0:T(8,128)S(1)} %get-tuple-element.53), channel_id=1, source_target_pairs={{0,33},{3,34},{4,37},{7,38},{8,41},{11,42},{12,45},{15,46},{16,49}... | collective-permute-start | bytes 1769480 | tf_op jit(solution)/shard_map/ppermute | solution.py:842
  13.4 7.9 %collective-permute-start.2 = (f32[1584,128]{1,0:T(8,128)S(1)}, f32[1584,128]{1,0:T(8,128)S(1)}, u32[]{:S(2)}, u32[]{:S(2)}) collective-permute-start(f32[1584,128]{1,0:T(8,128)S(1)} %get-tuple-element.52), channel_id=1, source_target_pairs={{0,31},{1,2},{2,1},{3,4},{4,3},{5,6},{6,5},{7,8},{8,7},{9,10},{10,... | collective-permute-start | bytes 2433032 | tf_op jit(solution)/shard_map/ppermute | solution.py:819
  21.3 5.1 %collective-permute-done.4 = f32[6,192,128]{2,1,0:T(8,128)S(1)} collective-permute-done((f32[6,192,128]{2,1,0:T(8,128)S(1)}, f32[6,192,128]{2,1,0:T(8,128)S(1)}, u32[]{:S(2)}, u32[]{:S(2)}) %collective-permute-start.4) | collective-permute-done | bytes 589856 | tf_op jit(solution)/shard_map/ppermute | solution.py:842
  26.4 1.3 collective-permute-start.10
  28.5 1.5 %side_x.1.part_ref = f32[16,256,128]{2,1,0:T(8,128)S(1)} custom-call(f32[16,256,128]{2,1,0:T(8,128)S(1)} %bitcast.16, f32[16,256,128]{2,1,0:T(8,128)S(1)} %collective-permute-done.3.mate_ref), custom_call_target="tpu_custom_call" | custom-call | flops 16777216 | bytes 6291456 | tf_op jit(solution)/shard_map/side_x/pallas_call | solution.py:277
  30.0 12.8 %collective-permute-done.1.one_ref = f32[1584,128]{1,0:T(8,128)S(1)} collective-permute-done((f32[1584,128]{1,0:T(8,128)S(1)}, f32[1584,128]{1,0:T(8,128)S(1)}, u32[]{:S(2)}, u32[]{:S(2)}) %collective-permute-start.1) | collective-permute-done | bytes 811040 | tf_op jit(solution)/shard_map/ppermute | solution.py:819
  42.8 2.9 %side_z.1.side_ref = f32[16,256,128]{2,1,0:T(8,128)S(1)} custom-call(f32[16,256,128]{2,1,0:T(8,128)S(1)} %bitcast.17, f32[16,256,128]{2,1,0:T(8,128)S(1)} %side_x.1.part_ref, f32[1584,128]{1,0:T(8,128)S(1)} %collective-permute-done.1.one_ref, f32[1584,128]{1,0:T(8,128)S(1)} %collective-permute-done.2.two_ref, s32[1]{0:T(128)} %bitcast.5.odd_ref.refs_3_.rest_4_), custom_call_target="tpu_custom_call" | custom-call | flops 16777216 | bytes 8388608 | tf_op jit(solution)/shard_map/side_z/pallas_call | solution.py:305
  45.8 1.3 collective-permute-done.5.refs_1_
  47.1 7.8 %prep.1 = (bf16[2,4096,128]{2,1,0:T(8,128)(2,1)S(1)}, f32[3,48,128]{2,1,0:T(8,128)S(1)}, f32[48,128]{1,0:T(8,128)S(1)}) custom-call(f32[144,128]{1,0:T(8,128)S(1)} %column.1.refs_0_, f32[144,128]{1,0:T(8,128)S(1)} %collective-permute-done.5.refs_1_, s32[2]{0:T(128)S(1)} %pad_add_fusion.refs_2_, f32[4096,128]{1,0:T(8,128)S(1)} %spread.2.refs_3_, ...), custom_call_target="tpu_custom_call" | custom-call | flops 134217728 | bytes 10485760 | tf_op jit(solution)/shard_map/prep/pallas_call | solution.py:493
  55.1 1.1 collective-permute-done.6
  56.2 1.1 collective-permute-start.7
  57.3 5.2 %collective-permute-done.9.refs_3_ = f32[3072,128]{1,0:T(8,128)S(1)} collective-permute-done((f32[3072,128]{1,0:T(8,128)S(1)}, f32[3072,128]{1,0:T(8,128)S(1)}, u32[]{:S(2)}, u32[]{:S(2)}) %collective-permute-start.9) | collective-permute-done | bytes 1572896 | tf_op jit(solution)/shard_map/ppermute | solution.py:812
  63.3 2.2 %first.1 = (f32[16,256,128]{2,1,0:T(8,128)S(1)}, f32[16,256,128]{2,1,0:T(8,128)S(1)}, f32[1632,128]{1,0:T(8,128)S(1)}, f32[1632,128]{1,0:T(8,128)S(1)}) custom-call(f32[16,256,128]{2,1,0:T(8,128)S(1)} %bitcast.19, f32[16,256,128]{2,1,0:T(8,128)S(1)} %side_z.1.side_ref, f32[16,256,128]{2,1,0:T(8,128)S(1)} %bitcast.21, f32[16,192,128]{2,1,0:T(8,128)S(1)} %bitcast.23, ...), custom_call_target="tpu_custom_call" | custom-call | flops 16777216 | bytes 14680064 | tf_op jit(solution)/shard_map/first/pallas_call | solution.py:560
  65.8 8.3 %collective-permute-start.13 = (f32[1632,128]{1,0:T(8,128)S(1)}, f32[1632,128]{1,0:T(8,128)S(1)}, u32[]{:S(2)}, u32[]{:S(2)}) collective-permute-start(f32[1632,128]{1,0:T(8,128)S(1)} %get-tuple-element.69), channel_id=1, source_target_pairs={{0,31},{1,2},{2,1},{3,4},{4,3},{5,6},{6,5},{7,8},{8,7},{9,10},{10,... | collective-permute-start | bytes 2506760 | tf_op jit(solution)/shard_map/ppermute | solution.py:819
  75.6 2.9 %side_again.1.part_ref = f32[16,256,128]{2,1,0:T(8,128)S(1)} custom-call(f32[16,256,128]{2,1,0:T(8,128)S(1)} %get-tuple-element.67.s_ref, f32[16,256,128]{2,1,0:T(8,128)S(1)} %collective-permute-done.11.mate_ref), custom_call_target="tpu_custom_call" | custom-call | flops 33554432 | bytes 6291456 | tf_op jit(solution)/shard_map/side_again/pallas_call | solution.py:333
  78.5 2.9 %base.1.base_ref = f32[16,256,128]{2,1,0:T(8,128)S(1)} custom-call(f32[16,256,128]{2,1,0:T(8,128)S(1)} %bitcast.20, f32[16,64,128]{2,1,0:T(8,128)S(1)} %collective-permute-done.8.mid_ref, f32[16,256,128]{2,1,0:T(8,128)S(1)} %bitcast.22, f32[16,256,128]{2,1,0:T(8,128)S(1)} %bitcast.27, f32[16,256,128]{2,1,0:T(8,128)S(1)} %get-tuple-element.66.q_ref, ...), custom_call_target="tpu_custom_call" | custom-call | flops 33554432 | bytes 16777216 | tf_op jit(solution)/shard_map/base/pallas_call | solution.py:612
  81.5 5.2 %collective-permute-done.12.one_ref = f32[1632,128]{1,0:T(8,128)S(1)} collective-permute-done((f32[1632,128]{1,0:T(8,128)S(1)}, f32[1632,128]{1,0:T(8,128)S(1)}, u32[]{:S(2)}, u32[]{:S(2)}) %collective-permute-start.12) | collective-permute-done | bytes 835616 | tf_op jit(solution)/shard_map/ppermute | solution.py:819
  86.7 6.5 %collective-permute-done.13.two_ref = f32[1632,128]{1,0:T(8,128)S(1)} collective-permute-done((f32[1632,128]{1,0:T(8,128)S(1)}, f32[1632,128]{1,0:T(8,128)S(1)}, u32[]{:S(2)}, u32[]{:S(2)}) %collective-permute-start.13) | collective-permute-done | bytes 835616 | tf_op jit(solution)/shard_map/ppermute | solution.py:819
  93.2 3.9 %second.1 = (f32[16,256,128]{2,1,0:T(8,128)S(1)}, f32[64,128]{1,0:T(8,128)S(1)}, f32[64,128]{1,0:T(8,128)S(1)}) custom-call(f32[16,256,128]{2,1,0:T(8,128)S(1)} %base.1.base_ref, f32[1632,128]{1,0:T(8,128)S(1)} %collective-permute-done.12.one_ref, f32[1632,128]{1,0:T(8,128)S(1)} %collective-permute-done.13.two_ref, bf16[2,16,256,128]{3,2,1,0:T(8,128)(2,1)S(1)} %bitcast.25, ...), custom_call_target="tpu_custom_call" | custom-call | flops 134217728 | bytes 8388608 | tf_op jit(solution)/shard_map/second/pallas_call | solution.py:687
  97.2 1.2 collective-permute-done.14
  98.4 3.9 %collective-permute-done.15 = f32[64,128]{1,0:T(8,128)S(1)} collective-permute-done((f32[64,128]{1,0:T(8,128)S(1)}, f32[64,128]{1,0:T(8,128)S(1)}, u32[]{:S(2)}, u32[]{:S(2)}) %collective-permute-start.15) | collective-permute-done | bytes 32800 | tf_op jit(solution)/shard_map/ppermute | solution.py:872
  102.3 5.1 %collective-permute-done.16 = f32[64,128]{1,0:T(8,128)S(1)} collective-permute-done((f32[64,128]{1,0:T(8,128)S(1)}, f32[64,128]{1,0:T(8,128)S(1)}, u32[]{:S(2)}, u32[]{:S(2)}) %collective-permute-start.16) | collective-permute-done | bytes 32800 | tf_op jit(solution)/shard_map/ppermute | solution.py:872
  107.4 3.9 %collective-permute-done.17 = f32[64,128]{1,0:T(8,128)S(1)} collective-permute-done((f32[64,128]{1,0:T(8,128)S(1)}, f32[64,128]{1,0:T(8,128)S(1)}, u32[]{:S(2)}, u32[]{:S(2)}) %collective-permute-start.17) | collective-permute-done | bytes 32800 | tf_op jit(solution)/shard_map/ppermute | solution.py:872
  112.4 4.1 %collective-permute-done.18 = f32[64,128]{1,0:T(8,128)S(1)} collective-permute-done((f32[64,128]{1,0:T(8,128)S(1)}, f32[64,128]{1,0:T(8,128)S(1)}, u32[]{:S(2)}, u32[]{:S(2)}) %collective-permute-start.18) | collective-permute-done | bytes 32800 | tf_op jit(solution)/shard_map/ppermute | solution.py:872
  116.9 3.5 %collective-permute-done.19 = f32[64,128]{1,0:T(8,128)S(1)} collective-permute-done((f32[64,128]{1,0:T(8,128)S(1)}, f32[64,128]{1,0:T(8,128)S(1)}, u32[]{:S(2)}, u32[]{:S(2)}) %collective-permute-start.19) | collective-permute-done | bytes 32800 | tf_op jit(solution)/shard_map/ppermute | solution.py:872
  120.4 1.7 %collective-permute-start.20 = (f32[64,128]{1,0:T(8,128)S(1)}, f32[64,128]{1,0:T(8,128)S(1)}, u32[]{:S(2)}, u32[]{:S(2)}) collective-permute-start(f32[64,128]{1,0:T(8,128)S(1)} %add.44), channel_id=1, source_target_pairs={{0,36},{1,37},{2,38},{3,39},{4,32},{5,33},{6,34},{7,35},{8,44},{9,... | collective-permute-start | bytes 98312 | tf_op jit(solution)/shard_map/ppermute | solution.py:872
  122.1 3.5 %collective-permute-done.20 = f32[64,128]{1,0:T(8,128)S(1)} collective-permute-done((f32[64,128]{1,0:T(8,128)S(1)}, f32[64,128]{1,0:T(8,128)S(1)}, u32[]{:S(2)}, u32[]{:S(2)}) %collective-permute-start.20) | collective-permute-done | bytes 32800 | tf_op jit(solution)/shard_map/ppermute | solution.py:872
  125.5 1.2 collective-permute-done.21.other_ref
  126.7 16.5 %turn.1 = f32[16,256,128]{2,1,0:T(8,128)} custom-call(f32[16,256,128]{2,1,0:T(8,128)S(1)} %get-tuple-element.74.second_ref, f32[64,128]{1,0:T(8,128)S(1)} %add.45.own_ref, f32[64,128]{1,0:T(8,128)S(1)} %collective-permute-done.21.other_ref, s32[1]{0:T(128)} %bitcast.3.rest_3_.upper_ref), custom_call_target="tpu_custom_call" | custom-call | flops 268435456 | bytes 4194304 | tf_op jit(solution)/shard_map/turn/pallas_call | solution.py:792
  (48 shorter events, 10.1 us)
Async XLA Ops:
  0.0 26.4 %collective-permute-start.3 = (f32[16,256,128]{2,1,0:T(8,128)}, f32[16,256,128]{2,1,0:T(8,128)S(1)}, u32[]{:S(2)}, u32[]{:S(2)}) collective-permute-start(f32[16,256,128]{2,1,0:T(8,128)} %bitcast.13), channel_id=1, source_target_pairs={{0,64},{1,65},{2,66},{3,67},{4,68},{5,69},{6,70},{7,71},{8,72},{9,... | collective-permute-start | bytes 6291464 | tf_op jit(solution)/shard_map/ppermute | solution.py:812
  3.8 4.0 %collective-permute-start = (f32[56,128]{1,0:T(8,128)S(1)}, f32[56,128]{1,0:T(8,128)S(1)}, u32[]{:S(2)}, u32[]{:S(2)}) collective-permute-start(f32[56,128]{1,0:T(8,128)S(1)} %stack.13.own_ref.parcel_ref), channel_id=1, source_target_pairs={{0,32},{1,33},{2,34},{3,35},{4,36},{5,37},{6,38},{7,39},{8,40},{9,... | collective-permute-start | bytes 86024 | tf_op jit(solution)/shard_map/ppermute | solution.py:812
  5.8 1.6 %copy-start = (f32[16,16,16,128]{3,2,1,0:T(8,128)S(1)}, f32[16,16,16,128]{3,2,1,0:T(8,128)}, u32[]{:S(2)}) copy-start(f32[16,16,16,128]{3,2,1,0:T(8,128)} %param.5) | copy-start | bytes 6291460
  7.8 54.6 %collective-permute-start.9 = (f32[3072,128]{1,0:T(8,128)S(1)}, f32[3072,128]{1,0:T(8,128)S(1)}, u32[]{:S(2)}, u32[]{:S(2)}) collective-permute-start(f32[3072,128]{1,0:T(8,128)S(1)} %get-tuple-element.64), channel_id=1, source_target_pairs={{0,32},{1,33},{2,34},{3,35},{4,36},{5,37},{6,38},{7,39},{8,40},{9,... | collective-permute-start | bytes 4718600 | tf_op jit(solution)/shard_map/ppermute | solution.py:812
  9.7 16.7 %collective-permute-start.4 = (f32[6,192,128]{2,1,0:T(8,128)S(1)}, f32[6,192,128]{2,1,0:T(8,128)S(1)}, u32[]{:S(2)}, u32[]{:S(2)}) collective-permute-start(f32[6,192,128]{2,1,0:T(8,128)S(1)} %get-tuple-element.53), channel_id=1, source_target_pairs={{0,33},{3,34},{4,37},{7,38},{8,41},{11,42},{12,45},{15,46},{16,49}... | collective-permute-start | bytes 1769480 | tf_op jit(solution)/shard_map/ppermute | solution.py:842
  13.3 29.5 %collective-permute-start.1 = (f32[1584,128]{1,0:T(8,128)S(1)}, f32[1584,128]{1,0:T(8,128)S(1)}, u32[]{:S(2)}, u32[]{:S(2)}) collective-permute-start(f32[1584,128]{1,0:T(8,128)S(1)} %get-tuple-element.51), channel_id=1, source_target_pairs={{0,1},{1,0},{2,3},{3,2},{4,5},{5,4},{6,7},{7,6},{8,9},{9,8},{10,11... | collective-permute-start | bytes 2433032 | tf_op jit(solution)/shard_map/ppermute | solution.py:819
  13.4 29.4 %collective-permute-start.2 = (f32[1584,128]{1,0:T(8,128)S(1)}, f32[1584,128]{1,0:T(8,128)S(1)}, u32[]{:S(2)}, u32[]{:S(2)}) collective-permute-start(f32[1584,128]{1,0:T(8,128)S(1)} %get-tuple-element.52), channel_id=1, source_target_pairs={{0,31},{1,2},{2,1},{3,4},{4,3},{5,6},{6,5},{7,8},{8,7},{9,10},{10,... | collective-permute-start | bytes 2433032 | tf_op jit(solution)/shard_map/ppermute | solution.py:819
  26.4 36.9 %collective-permute-start.10 = (f32[6,192,128]{2,1,0:T(8,128)S(1)}, f32[6,192,128]{2,1,0:T(8,128)S(1)}, u32[]{:S(2)}, u32[]{:S(2)}) collective-permute-start(f32[6,192,128]{2,1,0:T(8,128)S(1)} %collective-permute-done.4), channel_id=1, source_target_pairs={{1,0},{2,3},{5,4},{6,7},{9,8},{10,11},{13,12},{14,15},{17,16},{18,... | collective-permute-start | bytes 1769480 | tf_op jit(solution)/shard_map/ppermute | solution.py:848
  28.5 14.3 %copy-start.1 = (f32[16,16,16,128]{3,2,1,0:T(8,128)S(1)}, f32[16,16,16,128]{3,2,1,0:T(8,128)}, u32[]{:S(2)}) copy-start(f32[16,16,16,128]{3,2,1,0:T(8,128)} %param.5) | copy-start | bytes 6291460
  45.7 1.3 collective-permute-start.5
  54.9 1.3 collective-permute-start.6
  56.2 7.1 %collective-permute-start.7 = (f32[3,48,128]{2,1,0:T(8,128)S(1)}, f32[3,48,128]{2,1,0:T(8,128)S(1)}, u32[]{:S(2)}, u32[]{:S(2)}) collective-permute-start(f32[3,48,128]{2,1,0:T(8,128)S(1)} %add.38.refs_4_.rest_0_), channel_id=1, source_target_pairs={{0,32},{1,33},{2,34},{3,35},{4,36},{5,37},{6,38},{7,39},{8,40},{9,... | collective-permute-start | bytes 221192 | tf_op jit(solution)/shard_map/ppermute | solution.py:812
  65.6 10.0 %collective-permute-start.11 = (f32[16,256,128]{2,1,0:T(8,128)S(1)}, f32[16,256,128]{2,1,0:T(8,128)S(1)}, u32[]{:S(2)}, u32[]{:S(2)}) collective-permute-start(f32[16,256,128]{2,1,0:T(8,128)S(1)} %get-tuple-element.67.s_ref), channel_id=1, source_target_pairs={{0,64},{1,65},{2,66},{3,67},{4,68},{5,69},{6,70},{7,71},{8,72},{9,... | collective-permute-start | bytes 6291464 | tf_op jit(solution)/shard_map/ppermute | solution.py:812
  65.7 21.0 %collective-permute-start.12 = (f32[1632,128]{1,0:T(8,128)S(1)}, f32[1632,128]{1,0:T(8,128)S(1)}, u32[]{:S(2)}, u32[]{:S(2)}) collective-permute-start(f32[1632,128]{1,0:T(8,128)S(1)} %get-tuple-element.68), channel_id=1, source_target_pairs={{0,1},{1,0},{2,3},{3,2},{4,5},{5,4},{6,7},{7,6},{8,9},{9,8},{10,11... | collective-permute-start | bytes 2506760 | tf_op jit(solution)/shard_map/ppermute | solution.py:819
  65.8 27.4 %collective-permute-start.13 = (f32[1632,128]{1,0:T(8,128)S(1)}, f32[1632,128]{1,0:T(8,128)S(1)}, u32[]{:S(2)}, u32[]{:S(2)}) collective-permute-start(f32[1632,128]{1,0:T(8,128)S(1)} %get-tuple-element.69), channel_id=1, source_target_pairs={{0,31},{1,2},{2,1},{3,4},{4,3},{5,6},{6,5},{7,8},{8,7},{9,10},{10,... | collective-permute-start | bytes 2506760 | tf_op jit(solution)/shard_map/ppermute | solution.py:819
  74.1 4.5 %collective-permute-start.8 = (f32[16,64,128]{2,1,0:T(8,128)S(1)}, f32[16,64,128]{2,1,0:T(8,128)S(1)}, u32[]{:S(2)}, u32[]{:S(2)}) collective-permute-start(f32[16,64,128]{2,1,0:T(8,128)S(1)} %get-tuple-element.62), channel_id=1, source_target_pairs={{1,33},{2,34},{5,37},{6,38},{9,41},{10,42},{13,45},{14,46},{17,49}... | collective-permute-start | bytes 1572872 | tf_op jit(solution)/shard_map/ppermute | solution.py:863
  97.1 1.3 collective-permute-start.14
  98.4 3.9 %collective-permute-start.15 = (f32[64,128]{1,0:T(8,128)S(1)}, f32[64,128]{1,0:T(8,128)S(1)}, u32[]{:S(2)}, u32[]{:S(2)}) collective-permute-start(f32[64,128]{1,0:T(8,128)S(1)} %add.39), channel_id=1, source_target_pairs={{0,1},{1,0},{2,3},{3,2},{4,5},{5,4},{6,7},{7,6},{8,9},{9,8},{10,11... | collective-permute-start | bytes 98312 | tf_op jit(solution)/shard_map/ppermute | solution.py:872
  102.3 5.1 %collective-permute-start.16 = (f32[64,128]{1,0:T(8,128)S(1)}, f32[64,128]{1,0:T(8,128)S(1)}, u32[]{:S(2)}, u32[]{:S(2)}) collective-permute-start(f32[64,128]{1,0:T(8,128)S(1)} %add.40), channel_id=1, source_target_pairs={{0,3},{1,2},{2,1},{3,0},{4,7},{5,6},{6,5},{7,4},{8,11},{9,10},{10,... | collective-permute-start | bytes 98312 | tf_op jit(solution)/shard_map/ppermute | solution.py:872
  107.4 3.9 %collective-permute-start.17 = (f32[64,128]{1,0:T(8,128)S(1)}, f32[64,128]{1,0:T(8,128)S(1)}, u32[]{:S(2)}, u32[]{:S(2)}) collective-permute-start(f32[64,128]{1,0:T(8,128)S(1)} %add.41), channel_id=1, source_target_pairs={{0,8},{1,9},{2,10},{3,11},{4,12},{5,13},{6,14},{7,15},{8,0},{9,1},... | collective-permute-start | bytes 98312 | tf_op jit(solution)/shard_map/ppermute | solution.py:872
  111.3 5.1 %collective-permute-start.18 = (f32[64,128]{1,0:T(8,128)S(1)}, f32[64,128]{1,0:T(8,128)S(1)}, u32[]{:S(2)}, u32[]{:S(2)}) collective-permute-start(f32[64,128]{1,0:T(8,128)S(1)} %add.42), channel_id=1, source_target_pairs={{0,24},{1,25},{2,26},{3,27},{4,28},{5,29},{6,30},{7,31},{8,16},{9,... | collective-permute-start | bytes 98312 | tf_op jit(solution)/shard_map/ppermute | solution.py:872
  116.5 3.9 %collective-permute-start.19 = (f32[64,128]{1,0:T(8,128)S(1)}, f32[64,128]{1,0:T(8,128)S(1)}, u32[]{:S(2)}, u32[]{:S(2)}) collective-permute-start(f32[64,128]{1,0:T(8,128)S(1)} %add.43), channel_id=1, source_target_pairs={{0,32},{1,33},{2,34},{3,35},{4,36},{5,37},{6,38},{7,39},{8,40},{9,... | collective-permute-start | bytes 98312 | tf_op jit(solution)/shard_map/ppermute | solution.py:872
  120.4 5.1 %collective-permute-start.20 = (f32[64,128]{1,0:T(8,128)S(1)}, f32[64,128]{1,0:T(8,128)S(1)}, u32[]{:S(2)}, u32[]{:S(2)}) collective-permute-start(f32[64,128]{1,0:T(8,128)S(1)} %add.44), channel_id=1, source_target_pairs={{0,36},{1,37},{2,38},{3,39},{4,32},{5,33},{6,34},{7,35},{8,44},{9,... | collective-permute-start | bytes 98312 | tf_op jit(solution)/shard_map/ppermute | solution.py:872
  125.5 1.2 collective-permute-start.21
